TPU v7x, 32 devices: a whole 2x2x4 slice. The times are simulated.
32 devices in a mesh: seq: 8 (over y, x, core), tp: 4 (over z).
Axes of the slice: x: 2, y: 2, z: 4, core: 2. Of those that a mesh axis runs over, the one named last changes fastest.
Arguments:
- tokens: bfloat16 [3584, 768], P('seq'), may hold values from -6 to 6
- gain_one: float32 [768], replicated, may hold values from 0.5 to 1.5
- w_qkv: bfloat16 [768, 3, 768], P(None, None, 'tp'), may hold values from -0.21875 to 0.21875
- w_out: bfloat16 [768, 768], P('tp'), may hold values from -4 to 4
- gain_two: float32 [768], replicated, may hold values from 0.5 to 1.5
- w_in: bfloat16 [768, 2, 1152], P(None, None, 'tp'), may hold values from -0.21875 to 0.21875
- w_down: bfloat16 [1152, 768], P('tp'), may hold values from -0.1875 to 0.1875
- cotangent: bfloat16 [3584, 768], P('seq'), may hold values from -6 to 6
- doc_lengths: int32 [4], replicated, may hold values from 1 to 1792, as said below
- roster: int32 [8], replicated, may hold values from 0 to 7, as said below
Outputs:
- layer_out: bfloat16 [3584, 768], P('seq')
- input_grad: bfloat16 [3584, 768], P('seq')
- grad_gain_one: float32 [768], replicated
- grad_qkv: float32 [768, 3, 768], P(None, None, 'tp')
- grad_out: float32 [768, 768], P('tp')
- grad_gain_two: float32 [768], replicated
- grad_in: float32 [768, 2, 1152], P(None, None, 'tp')
- grad_down: float32 [1152, 768], P('tp')
Inputs may be any that keep to these rules, and one draw needn't show every extreme that they name: `doc_lengths`: 4 positive lengths that sum to 3584; the largest is exactly 1792. A permutation; rows i * 448 to (i + 1) * 448 - 1 of tokens and cotangent hold the packed positions from roster[i] * 448 on.
All inputs are finite; a program needn't handle non-finite values.
Results may differ from a plain program's by a relative error of at most 0.024.
Values may be sent and summed in bfloat16 or wider, within the bound.
No kernel may reach another device: no remote copies, remote signals or barrier semaphores. Data moves between devices by JAX's collectives and lax.ppermute only.
A program may use at most 192 MiB of HBM per device.

v0:
```python
import jax
import jax.numpy as jnp
from jax import lax
from jax.sharding import PartitionSpec as P

HDIM = 64


EPSILON = 1e-05
ROPE_THETA = 160000.0
MASKED = -1e30
BLOCK_ROWS = 1024


def layer_norm(values, gain):
    centre = jnp.mean(values, axis=-1, keepdims=True)
    shifted = values - centre
    spread = jnp.mean(shifted * shifted, axis=-1, keepdims=True)
    return shifted * lax.rsqrt(spread + EPSILON) * gain


def exact_gelu(values):
    return jax.nn.gelu(values, approximate=False)


def token_layout(doc_lengths, roster, first_row, row_total, tok_dev):
    row_ids = first_row + jnp.arange(row_total)
    owners = row_ids // tok_dev
    picked = owners[:, None] == jnp.arange(roster.shape[0])[None, :]
    blocks = jnp.sum(jnp.where(picked, roster[None, :], 0), axis=1)
    packed = blocks * tok_dev + row_ids % tok_dev
    doc_ends = jnp.cumsum(doc_lengths)
    starts = doc_ends - doc_lengths
    segment = jnp.sum((packed[:, None] >= doc_ends[None, :]).astype(jnp.int32), axis=1)
    within = segment[:, None] == jnp.arange(doc_lengths.shape[0])[None, :]
    in_doc = packed - jnp.sum(jnp.where(within, starts[None, :], 0), axis=1)
    return (segment, in_doc)


def rotary_tables(in_doc, head_dim):
    half_dim = head_dim // 2
    frequency = ROPE_THETA ** (-(jnp.arange(half_dim).astype(jnp.float32) * (2.0 / head_dim)))
    angles = in_doc.astype(jnp.float32)[:, None] * frequency[None, :]
    cos_table = jnp.cos(angles)
    sin_table = jnp.sin(angles)
    return (
        jnp.concatenate([cos_table, cos_table], axis=1),
        jnp.concatenate([sin_table, sin_table], axis=1),
    )


def rotate(vectors, cos_table, sin_table):
    half_dim = vectors.shape[-1] // 2
    turned = jnp.concatenate([-vectors[..., half_dim:], vectors[..., :half_dim]], axis=-1)
    return vectors * cos_table[:, None, :] + turned * sin_table[:, None, :]


def rotate_back(gradients, cos_table, sin_table):
    half_dim = gradients.shape[-1] // 2
    turned = gradients * sin_table[:, None, :]
    return gradients * cos_table[:, None, :] + jnp.concatenate(
        [turned[..., half_dim:], -turned[..., :half_dim]], axis=-1
    )


def split_count(total_rows, target_rows):
    block_count = max(1, total_rows // target_rows)
    while total_rows % block_count:
        block_count = block_count - 1
    return block_count


def fold_blocks(update, running, portion, target_rows):
    total_rows = portion[0].shape[0]
    block_count = split_count(total_rows, target_rows)
    size_rows = total_rows // block_count
    stacked = tuple(
        (member.reshape((block_count, size_rows) + member.shape[1:]) for member in portion)
    )
    offsets = size_rows * jnp.arange(block_count, dtype=jnp.int32)

    def advance(carried, inputs):
        return (update(carried, inputs[0], inputs[1]), None)

    running, unused = lax.scan(advance, running, (stacked, offsets))
    return running


def block_scores(queries, key_rows, same_doc):
    raw_scores = jnp.einsum("qhd,khd->hqk", queries, key_rows, preferred_element_type=jnp.float32)
    return jnp.where(same_doc[None], raw_scores * HDIM ** (-0.5), MASKED)


def block_probs(queries, key_rows, same_doc, log_total):
    scores = block_scores(queries, key_rows, same_doc)
    return jnp.where(same_doc[None], jnp.exp(scores - log_total[:, :, None]), 0.0)


def block_grads(queries, grad_rows, log_total, row_delta, key_rows, value_rows, same_doc):
    attn_probs = block_probs(queries, key_rows, same_doc, log_total)
    prob_grads = jnp.einsum(
        "qhd,khd->hqk", grad_rows, value_rows, preferred_element_type=jnp.float32
    )
    score_grad = (attn_probs * (prob_grads - row_delta[:, :, None]) * HDIM ** (-0.5)).astype(
        jnp.bfloat16
    )
    return (attn_probs.astype(jnp.bfloat16), score_grad)


def body(tokens, gain_one, w_qkv, w_out, gain_two, w_in, w_down, cotangent, doc_lengths, roster):
    tok_dev = tokens.shape[0]
    local_width = w_qkv.shape[2]
    heads_here = local_width // HDIM
    own_start = lax.axis_index("seq") * tok_dev
    seg_own, place_own = token_layout(doc_lengths, roster, own_start, tok_dev, tok_dev)
    cos_table, sin_table = rotary_tables(place_own, HDIM)

    def remote_segments(offset, amount):
        seg_remote, unused = token_layout(doc_lengths, roster, offset, amount, tok_dev)
        return seg_remote

    inputs = tokens.astype(jnp.float32)
    h_one = layer_norm(inputs, gain_one).astype(jnp.bfloat16)
    projected = jnp.einsum("td,dkc->tkc", h_one, w_qkv, preferred_element_type=jnp.float32)
    query_own = rotate(
        projected[:, 0].reshape(tok_dev, heads_here, HDIM), cos_table, sin_table
    ).astype(jnp.bfloat16)
    key_own = rotate(
        projected[:, 1].reshape(tok_dev, heads_here, HDIM), cos_table, sin_table
    ).astype(jnp.bfloat16)
    value_own = projected[:, 2].reshape(tok_dev, heads_here, HDIM).astype(jnp.bfloat16)
    key_flat = key_own.reshape(tok_dev, local_width)
    key_value = jnp.concatenate([key_flat, value_own.reshape(tok_dev, local_width)], axis=1)

    def maxima_update(running, portion, offset):
        amount = portion[0].shape[0]
        same_doc = seg_own[:, None] == remote_segments(offset, amount)[None, :]

        def maxima_compute():
            scores = block_scores(query_own, portion[0].reshape(amount, heads_here, HDIM), same_doc)
            run_max, run_sum = running
            new_max = jnp.maximum(run_max, jnp.max(scores, axis=2))
            weights = jnp.where(same_doc[None], jnp.exp(scores - new_max[:, :, None]), 0.0)
            return (new_max, run_sum * jnp.exp(run_max - new_max) + jnp.sum(weights, axis=2))

        return lax.cond(jnp.any(same_doc), maxima_compute, lambda: running)

    start_state = (
        jnp.full((heads_here, tok_dev), MASKED, jnp.float32),
        jnp.zeros((heads_here, tok_dev), jnp.float32),
    )
    run_max, run_sum = fold_blocks(
        maxima_update,
        start_state,
        (lax.all_gather(key_flat, "seq", axis=0, tiled=True),),
        BLOCK_ROWS,
    )
    log_total = run_max + jnp.log(run_sum)

    def values_update(attended, portion, offset):
        amount = portion[0].shape[0]
        same_doc = seg_own[:, None] == remote_segments(offset, amount)[None, :]

        def values_compute():
            key_rows = portion[0][:, :local_width].reshape(amount, heads_here, HDIM)
            value_rows = portion[0][:, local_width:].reshape(amount, heads_here, HDIM)
            attn_probs = block_probs(query_own, key_rows, same_doc, log_total).astype(jnp.bfloat16)
            return attended + jnp.einsum(
                "hqk,khd->qhd", attn_probs, value_rows, preferred_element_type=jnp.float32
            )

        return lax.cond(jnp.any(same_doc), values_compute, lambda: attended)

    attended = fold_blocks(
        values_update,
        jnp.zeros((tok_dev, heads_here, HDIM), jnp.float32),
        (lax.all_gather(key_value, "seq", axis=0, tiled=True),),
        BLOCK_ROWS,
    )
    out_b = attended.reshape(tok_dev, local_width).astype(jnp.bfloat16)
    branch_one = lax.psum(
        jnp.dot(out_b, w_out, preferred_element_type=jnp.float32).astype(jnp.bfloat16), "tp"
    ).astype(jnp.float32)
    middle = inputs + branch_one
    h_two = layer_norm(middle, gain_two).astype(jnp.bfloat16)
    gate_up = jnp.einsum("td,dkf->tkf", h_two, w_in, preferred_element_type=jnp.float32)
    activated, gelu_back = jax.vjp(exact_gelu, gate_up[:, 0])
    mixed = (activated * gate_up[:, 1]).astype(jnp.bfloat16)
    branch_two = lax.psum(
        jnp.dot(mixed, w_down, preferred_element_type=jnp.float32).astype(jnp.bfloat16), "tp"
    ).astype(jnp.float32)
    layer_out = (middle + branch_two).astype(jnp.bfloat16)
    out_grad_f = cotangent.astype(jnp.float32)
    grad_down = jnp.einsum("tf,td->fd", mixed, cotangent, preferred_element_type=jnp.float32)
    mixed_grad = jnp.einsum("td,fd->tf", cotangent, w_down, preferred_element_type=jnp.float32)
    gelu_grad = gelu_back(mixed_grad * gate_up[:, 1])[0]
    gate_grad = jnp.stack([gelu_grad, mixed_grad * activated], axis=1).astype(jnp.bfloat16)
    grad_in = jnp.einsum("td,tkf->dkf", h_two, gate_grad, preferred_element_type=jnp.float32)
    h_two_grad = lax.psum(
        jnp.einsum("tkf,dkf->td", gate_grad, w_in, preferred_element_type=jnp.float32).astype(
            jnp.bfloat16
        ),
        "tp",
    ).astype(jnp.float32)
    unused_two, norm_two_back = jax.vjp(layer_norm, middle, gain_two)
    middle_norm_grad, grad_gain_two = norm_two_back(h_two_grad)
    middle_grad = out_grad_f + middle_norm_grad
    branch_grad = middle_grad.astype(jnp.bfloat16)
    grad_out = jnp.einsum("tc,td->cd", out_b, branch_grad, preferred_element_type=jnp.float32)
    grad_flat = jnp.einsum(
        "td,cd->tc", branch_grad, w_out, preferred_element_type=jnp.float32
    ).astype(jnp.bfloat16)
    grad_own = grad_flat.reshape(tok_dev, heads_here, HDIM)
    row_delta = jnp.einsum(
        "thd,thd->ht",
        grad_own,
        out_b.reshape(tok_dev, heads_here, HDIM),
        preferred_element_type=jnp.float32,
    )
    every_pair = lax.all_gather(key_value, "seq", axis=0, tiled=True)
    total_rows = every_pair.shape[0]
    block_count = split_count(total_rows, BLOCK_ROWS)
    size_rows = total_rows // block_count
    stacked = every_pair.reshape(block_count, size_rows, 2 * local_width)
    offsets = size_rows * jnp.arange(block_count, dtype=jnp.int32)

    def backward_block(query_sum, inputs):
        block_rows, offset = inputs
        same_doc = seg_own[:, None] == remote_segments(offset, size_rows)[None, :]

        def backward_compute():
            key_rows = block_rows[:, :local_width].reshape(size_rows, heads_here, HDIM)
            value_rows = block_rows[:, local_width:].reshape(size_rows, heads_here, HDIM)
            probs_b, score_grad = block_grads(
                query_own, grad_own, log_total, row_delta, key_rows, value_rows, same_doc
            )
            new_sum = query_sum + jnp.einsum(
                "hqk,khd->qhd", score_grad, key_rows, preferred_element_type=jnp.float32
            )
            key_part = jnp.einsum(
                "hqk,qhd->khd", score_grad, query_own, preferred_element_type=jnp.float32
            )
            value_part = jnp.einsum(
                "hqk,qhd->khd", probs_b, grad_own, preferred_element_type=jnp.float32
            )
            terms = jnp.concatenate(
                [
                    key_part.reshape(size_rows, local_width),
                    value_part.reshape(size_rows, local_width),
                ],
                axis=1,
            )
            return (new_sum, terms)

        def nothing():
            return (query_sum, jnp.zeros((size_rows, 2 * local_width), jnp.float32))

        return lax.cond(jnp.any(same_doc), backward_compute, nothing)

    query_sum, terms = lax.scan(
        backward_block, jnp.zeros((tok_dev, heads_here, HDIM), jnp.float32), (stacked, offsets)
    )
    key_terms = lax.psum_scatter(
        terms.reshape(total_rows, 2 * local_width), "seq", scatter_dimension=0, tiled=True
    )
    query_grad = rotate_back(query_sum, cos_table, sin_table).reshape(tok_dev, local_width)
    key_grad = rotate_back(
        key_terms[:, :local_width].reshape(tok_dev, heads_here, HDIM), cos_table, sin_table
    ).reshape(tok_dev, local_width)
    proj_grad = jnp.stack([query_grad, key_grad, key_terms[:, local_width:]], axis=1).astype(
        jnp.bfloat16
    )
    grad_qkv = jnp.einsum("td,tkc->dkc", h_one, proj_grad, preferred_element_type=jnp.float32)
    h_one_grad = lax.psum(
        jnp.einsum("tkc,dkc->td", proj_grad, w_qkv, preferred_element_type=jnp.float32).astype(
            jnp.bfloat16
        ),
        "tp",
    ).astype(jnp.float32)
    unused_one, norm_one_back = jax.vjp(layer_norm, inputs, gain_one)
    inputs_norm_grad, grad_gain_one = norm_one_back(h_one_grad)
    input_grad = (middle_grad + inputs_norm_grad).astype(jnp.bfloat16)
    summed = lax.psum((grad_gain_one, grad_qkv, grad_out, grad_gain_two, grad_in, grad_down), "seq")
    return (layer_out, input_grad, summed[0], summed[1], summed[2], summed[3], summed[4], summed[5])


def solution(mesh):
    placed = (
        P("seq", None),
        P(),
        P(None, None, "tp"),
        P("tp", None),
        P(),
        P(None, None, "tp"),
        P("tp", None),
        P("seq", None),
        P(),
        P(),
    )
    return jax.shard_map(
        body,
        mesh=mesh,
        in_specs=placed,
        out_specs=(
            P("seq", None),
            P("seq", None),
            P(),
            P(None, None, "tp"),
            P("tp", None),
            P(),
            P(None, None, "tp"),
            P("tp", None),
        ),
        check_vma=False,
    )
```

profile of v0, /device:TPU:0, one launch (start us, length us, event | category | flops | bytes accessed | tf_op | source)
XLA Modules:
  0.0 497.9 jit_solution(5916104062220520118)
XLA Ops:
  17.6 26.3 %all-gather.6.cloned.1.call-done = bf16[8,448,192]{1,2,0:T(8,128)(2,1)} async-done(((bf16[1,448,192]{1,2,0:T(8,128)(2,1)}), bf16[8,448,192]{1,2,0:T(8,128)(2,1)}) %all-gather.6.cloned.1.call-update) | async-done | bytes 1376272 | tf_op jit(solution)/shard_map/all_gather | solution.py:155
  51.3 23.2 %while.46 = (s32[]{:T(128)}, f32[3,448]{1,0:T(4,128)S(1)}, f32[3,448]{1,0:T(4,128)S(1)}, s32[448]{0:T(512)S(1)}, s32[2]{0:T(128)S(1)}, /*index=5*/s32[8]{0:T(128...) while((s32[]{:T(128)}, f32[3,448]{1,0:T(4,128)S(1)}, ...), condition=%wide.region_15.16_spmd, body=%wide.region_7.15_spmd.sunk | while | flops 329250432 | bytes 24041748 | solution.py:85
  56.2 6.6 %conditional.6 = ((f32[3,448]{1,0:T(4,128)S(1)}, f32[3,448]{1,0:T(4,128)S(1)})) conditional(s32[]{:T(128)} %convert_element_type.314, (f32[3,448]{1,0:T(4,128)S(1)}, f32[3,448]{1,0:T(4,128)S(1)}) %tuple.147, (pred[448,1792]{1,0:T(8,128)(4,1)S(1)}, bf16[2,1792,192]{1,2,0:T(8,128)(2,1)}, s32[]{:T(128)}, bf16[448,3,64]{0,2,1:T(8,128)(2,1)S(1)}, ...), branch_computations={%region_11.11_spmd, %region_12.14_spmd} | conditional | flops 327551616 | bytes 23179548 | solution.py:146
  59.6 3.2 select_reduce_fusion
  67.8 6.6 %conditional.6 = ((f32[3,448]{1,0:T(4,128)S(1)}, f32[3,448]{1,0:T(4,128)S(1)})) conditional(s32[]{:T(128)} %convert_element_type.314, (f32[3,448]{1,0:T(4,128)S(1)}, f32[3,448]{1,0:T(4,128)S(1)}) %tuple.147, (pred[448,1792]{1,0:T(8,128)(4,1)S(1)}, bf16[2,1792,192]{1,2,0:T(8,128)(2,1)}, s32[]{:T(128)}, bf16[448,3,64]{0,2,1:T(8,128)(2,1)S(1)}, ...), branch_computations={%region_11.11_spmd, %region_12.14_spmd} | conditional | flops 327551616 | bytes 23179548 | solution.py:146
  71.2 3.2 select_reduce_fusion
  77.1 4.6 copy.37
  82.6 30.4 %while.47 = (s32[]{:T(128)}, f32[448,3,64]{0,2,1:T(8,128)}, s32[448]{0:T(512)}, s32[2]{0:T(128)}, s32[8]{0:T(128)}, /*index=5*/s32[1,4]{1,0:T(1,128)}, bf16[2,17...) while((s32[]{:T(128)}, f32[448,3,64]{0,2,1:T(8,128)}, ...), condition=%wide.region_22.23_spmd, body=%wide.region_16.22_spmd.sunk | while | flops 630389760 | bytes 9411827 | solution.py:85
  89.6 8.3 %conditional.7 = (f32[448,3,64]{0,2,1:T(8,128)}) conditional(s32[]{:T(128)} %convert_element_type.316, f32[448,3,64]{0,2,1:T(8,128)} %get-tuple-element.1014, (pred[448,1792]{1,0:T(8,128)(4,1)S(1)}, bf16[2,1792,384]{1,2,0:T(8,128)(2,1)}, s32[]{:T(128)}, bf16[448,3,64]{0,2,1:T(8,128)(2,1)S(1)}, f32[3,448]{1,0:T(4,128)}, ...), branch_computations={%region_20.20_spmd, %region_21.21_spmd} | conditional | flops 628690944 | bytes 8549644 | solution.py:172
  92.0 5.9 %fusion.14 = f32[448,3,64]{0,2,1:T(8,128)} fusion(f32[448,3,64]{0,2,1:T(8,128)} %get-tuple-element.482, bf16[1792,3,64]{0,2,1:T(8,128)(2,1)} %bitcast.272, bf16[1792,3,64]{0,2,1:T(8,128)(2,1)S(1)} %bitcast.271, bf16[448,3,64]{0,2,1:T(8,128)(2,1)S(1)} %get-tuple-element.486, f32[3,448]{1,0:T(4,128)} %get-tuple-element.487, ...), kind=kOutput, calls=%fused_computation.28 | convolution fusion | flops 628690944 | bytes 3044608 | tf_op jit(solution)/shard_map/while/body/eval_jaxpr/cond/branch_1_fun/hqk,khd->qhd/dot_general | solution.py:168
  104.7 8.3 %conditional.7 = (f32[448,3,64]{0,2,1:T(8,128)}) conditional(s32[]{:T(128)} %convert_element_type.316, f32[448,3,64]{0,2,1:T(8,128)} %get-tuple-element.1014, (pred[448,1792]{1,0:T(8,128)(4,1)S(1)}, bf16[2,1792,384]{1,2,0:T(8,128)(2,1)}, s32[]{:T(128)}, bf16[448,3,64]{0,2,1:T(8,128)(2,1)S(1)}, f32[3,448]{1,0:T(4,128)}, ...), branch_computations={%region_20.20_spmd, %region_21.21_spmd} | conditional | flops 628690944 | bytes 8549644 | solution.py:172
  107.1 5.9 %fusion.14 = f32[448,3,64]{0,2,1:T(8,128)} fusion(f32[448,3,64]{0,2,1:T(8,128)} %get-tuple-element.482, bf16[1792,3,64]{0,2,1:T(8,128)(2,1)} %bitcast.272, bf16[1792,3,64]{0,2,1:T(8,128)(2,1)S(1)} %bitcast.271, bf16[448,3,64]{0,2,1:T(8,128)(2,1)S(1)} %get-tuple-element.486, f32[3,448]{1,0:T(4,128)} %get-tuple-element.487, ...), kind=kOutput, calls=%fused_computation.28 | convolution fusion | flops 628690944 | bytes 3044608 | tf_op jit(solution)/shard_map/while/body/eval_jaxpr/cond/branch_1_fun/hqk,khd->qhd/dot_general | solution.py:168
  116.7 40.2 %all-reduce.8.cloned.1.call-done = bf16[448,768]{1,0:T(8,128)(2,1)} async-done(((bf16[448,768]{1,0:T(8,128)(2,1)}), bf16[448,768]{1,0:T(8,128)(2,1)}) %all-reduce.8.cloned.1.call-update) | async-done | bytes 688144 | tf_op jit(solution)/shard_map/psum | solution.py:181
  164.0 40.7 %all-reduce.10.cloned.1.call-done = bf16[448,768]{1,0:T(8,128)(2,1)} async-done(((bf16[448,768]{1,0:T(8,128)(2,1)}), bf16[448,768]{1,0:T(8,128)(2,1)}) %all-reduce.10.cloned.1.call-update) | async-done | bytes 688144 | tf_op jit(solution)/shard_map/psum | solution.py:199
  210.2 53.2 %while.48 = (s32[]{:T(128)}, f32[448,3,64]{0,2,1:T(8,128)S(1)}, f32[2,1792,384]{2,1,0:T(8,128)}, s32[448]{0:T(512)S(1)}, s32[2]{0:T(128)S(1)}, /*index=5*/s32[8]...) while((s32[]{:T(128)}, f32[448,3,64]{0,2,1:T(8,128)S(1)}, ...), condition=%wide.region_36.37_spmd, body=%wide.region_30.36_spmd.sunk | while | flops 1575189504 | bytes 74737984 | solution.py:260
  215.3 14.7 %conditional.8 = (f32[448,3,64]{0,2,1:T(8,128)S(1)}, f32[1,1792,384]{1,2,0:T(8,128)}) conditional(s32[]{:T(128)} %convert_element_type.318, f32[448,3,64]{0,2,1:T(8,128)S(1)} %get-tuple-element.1047, (pred[448,1792]{1,0:T(8,128)(4,1)S(1)}, bf16[2,1792,384]{1,2,0:T(8,128)(2,1)}, s32[]{:T(128)}, bf16[448,3,64]{0,2,1:T(8,128)(2,1)S(1)}, ...), branch_computations={%region_34.34_spmd, %region_35.35_spmd} | conditional | flops 1573490688 | bytes 62865200 | solution.py:258
  218.4 4.4 fusion.26
  224.2 3.0 fusion.31
  230.0 3.4 copy.66
  233.4 3.5 constant_dynamic-update-slice_fusion.2
  241.8 14.7 %conditional.8 = (f32[448,3,64]{0,2,1:T(8,128)S(1)}, f32[1,1792,384]{1,2,0:T(8,128)}) conditional(s32[]{:T(128)} %convert_element_type.318, f32[448,3,64]{0,2,1:T(8,128)S(1)} %get-tuple-element.1047, (pred[448,1792]{1,0:T(8,128)(4,1)S(1)}, bf16[2,1792,384]{1,2,0:T(8,128)(2,1)}, s32[]{:T(128)}, bf16[448,3,64]{0,2,1:T(8,128)(2,1)S(1)}, ...), branch_computations={%region_34.34_spmd, %region_35.35_spmd} | conditional | flops 1573490688 | bytes 62865200 | solution.py:258
  244.8 4.4 fusion.26
  250.7 3.0 fusion.31
  256.5 3.4 copy.66
  259.9 3.5 constant_dynamic-update-slice_fusion.2
  265.8 54.8 %reduce-scatter.4.cloned.1.call-done = f32[448,384]{1,0:T(8,128)} async-done(((f32[3584,384]{1,0:T(8,128)}), f32[448,384]{1,0:T(8,128)}) %reduce-scatter.4.cloned.1.call-update) | async-done | bytes 688144
  328.7 3.1 fusion.94
  335.2 53.7 %all-reduce.14.cloned.1.call-done = (bf16[448,768]{1,0:T(8,128)(2,1)}, bf16[448,768]{1,0:T(8,128)(2,1)}) async-done(((bf16[448,768]{1,0:T(8,128)(2,1)}, bf16[448,768]{1,0:T(8,128)(2,1)}), (bf16[448,768]{1,0:T(8,128)(2,1)}, bf16[448,768]{1,0:T(8,128)(2,1)})) %all-reduce.14.cloned.1.call-update) | async-done | bytes 1376272 | tf_op jit(solution)/shard_map/psum | solution.py:189
  391.4 14.6 %all-reduce = (f32[768]{0:T(1024)}, f32[768]{0:T(1024)}) all-reduce(f32[768]{0:T(1024)S(1)} %get-tuple-element.652, f32[768]{0:T(1024)S(1)} %get-tuple-element.650), channel_id=1, replica_groups=mesh['seq'=8,'tp'=4] {'seq'}, use_global_device_ids=true, to_apply=%region_42.43 | all-reduce | flops 1536 | bytes 12288 | tf_op jit(solution)/shard_map/psum | solution.py:283
  406.0 3.6 add_convert_fusion
  409.5 74.6 %all-reduce.12.cloned.1.call-done = (f32[768,3,192]{0,2,1:T(8,128)}, f32[192,768]{1,0:T(8,128)}, f32[768,2,288]{0,2,1:T(8,128)}, f32[288,768]{1,0:T(8,128)}) async-done(((f32[768,3,192]{0,2,1:T(8,128)}, f32[192,768]{1,0:T(8,128)}, f32[768,2,288]{0,2,1:T(8,128)}, f32[288,768]{1,0:T(8,128)}), (f32[768,3,192]{0,2,1:T(8,128)}, f32[192,768]{1,0:T(8,128)}, f32[768,2,288]{0,2,1:T(8,128)}, ...) | async-done | bytes 5013520 | tf_op jit(solution)/shard_map/psum | solution.py:283
  484.1 2.9 copy.112
  (261 shorter events, 112.2 us)
Async XLA Ops:
  7.2 3.8 copy-start
  7.2 3.8 copy-start.1
  7.2 3.8 copy-start.41
  7.2 36.7 %all-gather.6.cloned.1.call-start = ((), (), s32[]{:S(2)}) async-start(), calls=%async_computation.4 | async-start | bytes 1769472 | tf_op jit(solution)/shard_map/all_gather | solution.py:155
  9.4 2.3 copy-start.39
  15.4 61.7 %all-gather.4.cloned.1.call-start = ((), (), s32[]{:S(2)}) async-start(), calls=%async_computation.1 | async-start | bytes 3096576 | tf_op jit(solution)/shard_map/all_gather | solution.py:177
  17.4 139.5 %all-reduce.8.cloned.1.call-start = ((), (), s32[]{:S(2)}) async-start(), calls=%async_computation.2 | async-start | bytes 1376256 | tf_op jit(solution)/shard_map/psum | solution.py:181
  74.4 7.3 %copy-start.32 = (s32[448]{0:T(512)}, s32[448]{0:T(512)S(1)}, u32[]{:S(2)}) copy-start(s32[448]{0:T(512)S(1)} %get-tuple-element.1133) | copy-start | bytes 5380
  74.4 7.3 %copy-start.37 = (s32[1,4]{1,0:T(1,128)}, s32[1,4]{1,0:T(1,128)S(1)}, u32[]{:S(2)}) copy-start(s32[1,4]{1,0:T(1,128)S(1)} %get-tuple-element.1137) | copy-start | bytes 52
  74.5 7.3 %copy-start.51 = (s32[2]{0:T(128)}, s32[2]{0:T(128)S(1)}, u32[]{:S(2)}) copy-start(s32[2]{0:T(128)S(1)} %get-tuple-element.1140) | copy-start | bytes 28
  82.6 31.5 %copy-start.21 = (bf16[192,768]{1,0:T(8,128)(2,1)S(1)}, bf16[192,768]{1,0:T(8,128)(2,1)}, u32[]{:S(2)}) copy-start(bf16[192,768]{1,0:T(8,128)(2,1)} %param.25) | copy-start | bytes 884740
  112.9 2.5 copy-start.5
  112.9 2.5 copy-start.15
  114.1 2.6 copy-start.17
  115.3 89.3 %all-reduce.10.cloned.1.call-start = ((), (), s32[]{:S(2)}) async-start(), calls=%async_computation.3 | async-start | bytes 1376256 | tf_op jit(solution)/shard_map/psum | solution.py:199
  116.6 42.1 %copy-start.47 = (f32[768]{0:T(1024)S(1)}, f32[768]{0:T(1024)}, u32[]{:S(2)}) copy-start(f32[768]{0:T(1024)} %param.26) | copy-start | bytes 9220
  156.9 1.9 copy-start.49
  163.9 156.7 %reduce-scatter.4.cloned.1.call-start = ((), (), s32[]{:S(2)}) async-start(), calls=%async_computation.5 | async-start | bytes 6193152
  204.6 1.9 copy-start.13
  208.5 1.6 copy-start.52
  263.4 125.5 %all-reduce.14.cloned.1.call-start = ((), (), s32[]{:S(2)}) async-start(), calls=%async_computation.7 | async-start | bytes 2752512 | tf_op jit(solution)/shard_map/psum | solution.py:189
  265.8 57.0 %copy-start.20 = (f32[448,64]{0,1:T(8,128)S(1)}, f32[448,64]{0,1:T(8,128)}, u32[]{:S(2)}) copy-start(f32[448,64]{0,1:T(8,128)} %copy-done.19) | copy-start | bytes 344068
  320.6 2.0 slice-start
  326.3 2.4 copy-start.3
  326.3 157.8 %all-reduce.12.cloned.1.call-start = ((), (), s32[]{:S(2)}) async-start(), calls=%async_computation.6 | async-start | bytes 10027008 | tf_op jit(solution)/shard_map/psum | solution.py:283
  328.7 3.1 copy-start.9
  328.7 3.1 copy-start.18
  335.2 55.4 %copy-start.46 = (f32[448]{0:T(512)S(1)}, f32[448]{0:T(512)}, u32[]{:S(2)}) copy-start(f32[448]{0:T(512)} %copy-done.45) | copy-start | bytes 5380
  388.9 1.7 copy-start.7
  484.1 3.0 copy-start.34
  484.1 3.8 copy-start.14
  487.9 1.8 copy-start.23
  (30 other events, 34.0 us)
Sparse Core Ops, SparseCore 0:
  15.5 28.3 all-gather.5
  46.4 30.6 all-gather.3
  115.5 41.3 all-reduce.7
  164.0 40.5 all-reduce.9
  263.6 57.0 reduce-scatter.3
  326.4 62.4 all-reduce.13
  393.3 90.8 all-reduce.11
where the time goes:
time: 507 us; the launch traced here: 498 us
  waiting for transfers between devices  293 us (58%)
  other arithmetic  58.1 us (11%)
  local copies, waits for them, and re-layouts  57 us (11%)
  matrix products  55.3 us (11%)
  between operations  15.3 us (3%)
  blocking collectives  14.6 us (3%)
    psum x1, waiting for transfers between devices, body(): lax.psum((grad_gain_one, grad_qkv, grad_out, grad_gain_two, grad_in, grad...  74.6 us
    unnamed x8, waiting for transfers between devices  54.9 us
    psum x1, waiting for transfers between devices, body(): lax.psum(jnp.dot(mixed, w_down, preferred_element_type=jnp.float32).astyp...  53.7 us
    psum x1, waiting for transfers between devices, body(): lax.psum(jnp.einsum('tkf,dkf->td', gate_grad, w_in, preferred_element_typ...  40.7 us
    psum x1, waiting for transfers between devices, body(): lax.psum(jnp.dot(out_b, w_out, preferred_element_type=jnp.float32).astype...  40.2 us
    all_gather x1, waiting for transfers between devices, body(): lax.all_gather(key_flat, 'seq', axis=0, tiled=True)  26.3 us
    psum x1, blocking collectives, body(): lax.psum((grad_gain_one, grad_qkv, grad_out, grad_gain_two, grad_in, grad...  14.6 us
    dynamic_update_slice x4, local copies, waits for them, and re-layouts, body(): lax.scan(backward_block, jnp.zeros((tok_dev, heads_here, HDIM), jnp.float...  13.8 us
  transfers between devices with their start and end apart: 7, of which 7 were waited for; matrix products, arithmetic and copies ran while one was open for 10% of the time, Pallas kernels for 0%

commit v1 on v0

v1 whole, which is shorter than its diff:
```python
import functools

import jax
import jax.numpy as jnp
from jax import lax
from jax.experimental import pallas as pl
from jax.experimental.pallas import tpu as pltpu
from jax.sharding import PartitionSpec as P

HDIM = 64
HALF = HDIM // 2
EPSILON = 1e-05
ROPE_THETA = 160000.0
MASKED = -1e30
AUG = 80
F32 = jnp.float32
BF16 = jnp.bfloat16
ANY = pl.BlockSpec(memory_space=pl.ANY)
VMEM = pl.BlockSpec(memory_space=pltpu.VMEM)
SMEM = pl.BlockSpec(memory_space=pltpu.SMEM)

NN = (((1,), (0,)), ((), ()))
NT = (((1,), (1,)), ((), ()))
TN = (((0,), (0,)), ((), ()))


def mm(a, b, dims):
    return lax.dot_general(a, b, dims, preferred_element_type=F32)


def swap(x, axis, hop, count):
    return lax.ppermute(x, axis, [(i, i ^ hop) for i in range(count)])


def doc_bounds(len_ref):
    ends, total = [], jnp.int32(0)
    for d in range(len_ref.shape[0]):
        total = total + len_ref[d]
        ends.append(total)
    return ends


def doc_of(ends, position):
    found = jnp.int32(0)
    for end in ends:
        found = found + (end <= position).astype(jnp.int32)
    return found


def meet(ends, base_a, base_b, rows):
    low = jnp.maximum(doc_of(ends, base_a), doc_of(ends, base_b))
    high = jnp.minimum(doc_of(ends, base_a + rows - 1), doc_of(ends, base_b + rows - 1))
    return low <= high


def doc_rows(ends, base, rows):
    spot = base + lax.broadcasted_iota(jnp.int32, (16, rows), 1)
    line = lax.broadcasted_iota(jnp.int32, (16, rows), 0)
    held = jnp.zeros((16, rows), F32)
    start = jnp.int32(0)
    for d, end in enumerate(ends):
        inside = (line == d) & (spot >= start) & (spot < end)
        held = jnp.where(inside, 1.0, held)
        start = end
    return held


def ban_rows(ends, base, rows):
    line = lax.broadcasted_iota(jnp.int32, (16, rows), 0)
    held = doc_rows(ends, base, rows)
    return jnp.where((held > 0.5) | (line >= len(ends)), 0.0, MASKED)


def key_row(block, seq_index):
    return seq_index ^ (2 * block)


def forward_kernel(count, heads, len_ref, roster_ref, q_own, q_pair, *refs):
    kv_refs = refs[:count]
    own_out, pair_out = refs[count : count + 2]
    kv, q_aug, state, sems = refs[count + 2 :]
    rows = q_own.shape[1]
    width = heads * HDIM
    me = lax.axis_index("seq")
    copies = [pltpu.make_async_copy(kv_refs[j], kv.at[j], sems.at[j]) for j in range(count)]
    for copy in copies:
        copy.start()
    ends = doc_bounds(len_ref)
    bases = (roster_ref[me] * rows, roster_ref[me ^ 1] * rows)
    for g, q_ref in enumerate((q_own, q_pair)):
        mark = doc_rows(ends, bases[g], rows).astype(BF16)
        for h in range(heads):
            q_aug[g * heads + h, :HDIM, :] = q_ref[h * HDIM : (h + 1) * HDIM, :]
            q_aug[g * heads + h, HDIM:, :] = mark
    line = lax.broadcasted_iota(jnp.int32, (2 * heads, AUG, rows), 1)
    state[...] = jnp.where(line >= 72, MASKED, 0.0)
    for copy in copies:
        copy.wait()

    first = lax.broadcasted_iota(jnp.int32, (16, rows), 0) == 0
    ones = jnp.where(first, 1.0, 0.0).astype(BF16)

    def block(j, carry):
        key_base = roster_ref[key_row(j, me)] * rows
        ban = ban_rows(ends, key_base, rows).astype(BF16)
        for g in range(2):

            @pl.when(meet(ends, bases[g], key_base, rows))
            def _():
                for h in range(heads):
                    at = g * heads + h
                    keys = jnp.concatenate([kv[j, h * HDIM : (h + 1) * HDIM, :], ban], axis=0)
                    vals = jnp.concatenate(
                        [kv[j, width + h * HDIM : width + (h + 1) * HDIM, :], ones], axis=0
                    )
                    scores = mm(keys, q_aug[at], TN)
                    old = state[at, 72:73, :]
                    new = jnp.maximum(old, jnp.max(scores, axis=0, keepdims=True))
                    probs = jnp.exp(scores - new).astype(BF16)
                    part = mm(vals, probs, NN)
                    fade = jnp.exp(old - new)
                    state[at, :72, :] = state[at, :72, :] * fade + part[:72]
                    state[at, 72:, :] = jnp.broadcast_to(new, (8, rows))

        return carry

    lax.fori_loop(0, count, block, 0)
    own_out[...] = state[:heads]
    pair_out[...] = state[heads:]


def attention_forward(doc_lengths, roster, q_own, q_pair, blocks):
    width, rows = q_own.shape
    heads = width // HDIM
    count = len(blocks)
    shape = jax.ShapeDtypeStruct((heads, AUG, rows), F32)
    return pl.pallas_call(
        functools.partial(forward_kernel, count, heads),
        out_shape=(shape, shape),
        in_specs=[SMEM, SMEM, VMEM, VMEM] + [ANY] * count,
        out_specs=(VMEM, VMEM),
        scratch_shapes=[
            pltpu.VMEM((count, 2 * width, rows), BF16),
            pltpu.VMEM((2 * heads, AUG, rows), BF16),
            pltpu.VMEM((2 * heads, AUG, rows), F32),
            pltpu.SemaphoreType.DMA((count,)),
        ],
        compiler_params=pltpu.CompilerParams(vmem_limit_bytes=56 * 2**20),
    )(doc_lengths, roster, q_own, q_pair, *blocks)


def backward_kernel(count, heads, len_ref, roster_ref, *refs):
    q_own, q_pair, g_own, g_pair, o_own, o_pair, t_own, t_pair = refs[:8]
    kv_refs = refs[8 : 8 + count]
    dq_own, dq_pair = refs[8 + count : 10 + count]
    dkv_refs = refs[10 + count : 10 + 2 * count]
    kv, q_aug, delta, dq, dkv, sems = refs[10 + 2 * count :]
    rows = q_own.shape[1]
    width = heads * HDIM
    me = lax.axis_index("seq")
    copies = [pltpu.make_async_copy(kv_refs[j], kv.at[j], sems.at[j]) for j in range(count)]
    for copy in copies:
        copy.start()
    ends = doc_bounds(len_ref)
    bases = (roster_ref[me] * rows, roster_ref[me ^ 1] * rows)
    for g, (q_ref, g_ref, o_ref) in enumerate(((q_own, g_own, o_own), (q_pair, g_pair, o_pair))):
        mark = doc_rows(ends, bases[g], rows).astype(BF16)
        for h in range(heads):
            part = slice(h * HDIM, (h + 1) * HDIM)
            q_aug[g * heads + h, :HDIM, :] = q_ref[part, :]
            q_aug[g * heads + h, HDIM:, :] = mark
            product = g_ref[part, :].astype(F32) * o_ref[part, :].astype(F32)
            delta[g * heads + h] = jnp.broadcast_to(
                jnp.sum(product, axis=0, keepdims=True), (8, rows)
            )
    dq[...] = jnp.zeros_like(dq)
    for copy in copies:
        copy.wait()

    def block(j, carry):
        key_base = roster_ref[key_row(j, me)] * rows
        ban = ban_rows(ends, key_base, rows).astype(BF16)
        dkv[j] = jnp.zeros((2 * width, rows), F32)
        for g, (g_ref, t_ref) in enumerate(((g_own, t_own), (g_pair, t_pair))):

            @pl.when(meet(ends, bases[g], key_base, rows))
            def _():
                for h in range(heads):
                    at = g * heads + h
                    part = slice(h * HDIM, (h + 1) * HDIM)
                    late = slice(width + h * HDIM, width + (h + 1) * HDIM)
                    keys = kv[j, part, :]
                    scores = mm(jnp.concatenate([keys, ban], axis=0), q_aug[at], TN)
                    probs = jnp.exp(scores - t_ref[h, 0:1, :])
                    prob_grads = mm(kv[j, late, :], g_ref[part, :], TN)
                    score_grad = (probs * (prob_grads - delta[at, 0:1, :])).astype(BF16)
                    dkv[j, late, :] += mm(g_ref[part, :], probs.astype(BF16), NT)
                    dkv[j, part, :] += mm(q_aug[at, :HDIM, :], score_grad, NT)
                    dq[at] += mm(keys, score_grad, NN)

        return carry

    lax.fori_loop(0, count, block, 0)
    for h in range(heads):
        part = slice(h * HDIM, (h + 1) * HDIM)
        dq_own[part, :] = (dq[h] * HDIM**-0.5).astype(dq_own.dtype)
        dq_pair[part, :] = (dq[heads + h] * HDIM**-0.5).astype(dq_pair.dtype)
    for j in range(count):
        dkv_refs[j][...] = dkv[j].astype(dkv_refs[j].dtype)


def attention_backward(doc_lengths, roster, queries, grads, outs, totals, blocks):
    width, rows = queries[0].shape
    heads = width // HDIM
    count = len(blocks)
    grad_shape = jax.ShapeDtypeStruct((width, rows), F32)
    pair_shape = jax.ShapeDtypeStruct((width, rows), BF16)
    first = jax.ShapeDtypeStruct((2 * width, rows), F32)
    other = jax.ShapeDtypeStruct((2 * width, rows), BF16)
    return pl.pallas_call(
        functools.partial(backward_kernel, count, heads),
        out_shape=(grad_shape, pair_shape, first) + (other,) * (count - 1),
        in_specs=[SMEM, SMEM] + [VMEM] * 8 + [ANY] * count,
        out_specs=(VMEM,) * (2 + count),
        scratch_shapes=[
            pltpu.VMEM((count, 2 * width, rows), BF16),
            pltpu.VMEM((2 * heads, AUG, rows), BF16),
            pltpu.VMEM((2 * heads, 8, rows), F32),
            pltpu.VMEM((2 * heads, HDIM, rows), F32),
            pltpu.VMEM((count, 2 * width, rows), F32),
            pltpu.SemaphoreType.DMA((count,)),
        ],
        compiler_params=pltpu.CompilerParams(vmem_limit_bytes=60 * 2**20),
    )(doc_lengths, roster, *queries, *grads, *outs, *totals, *blocks)


def normed(values):
    centre = jnp.mean(values, axis=-1, keepdims=True)
    shifted = values - centre
    spread = jnp.mean(shifted * shifted, axis=-1, keepdims=True)
    scale = lax.rsqrt(spread + EPSILON)
    return shifted * scale, scale


def norm_back(unit, scale, grad, gain):
    u = grad * gain
    mean_u = jnp.mean(u, axis=-1, keepdims=True)
    mean_un = jnp.mean(u * unit, axis=-1, keepdims=True)
    return scale * (u - mean_u - unit * mean_un)


def own_tables(doc_lengths, roster, me, rows):
    base = jnp.sum(jnp.where(jnp.arange(roster.shape[0]) == me, roster, 0)) * rows
    packed = base + jnp.arange(rows, dtype=jnp.int32)
    doc_ends = jnp.cumsum(doc_lengths)
    passed = packed[None, :] >= doc_ends[:, None]
    start = jnp.max(jnp.where(passed, doc_ends[:, None], 0), axis=0)
    place = packed - start
    frequency = ROPE_THETA ** (-(jnp.arange(HALF).astype(F32) * (2.0 / HDIM)))
    angles = place.astype(F32)[None, :] * frequency[:, None]
    return jnp.cos(angles), jnp.sin(angles)


def rotate(vectors, cos_table, sin_table):
    width, rows = vectors.shape
    split = vectors.reshape(width // HDIM, 2, HALF, rows)
    low, high = split[:, 0], split[:, 1]
    return jnp.stack(
        [low * cos_table - high * sin_table, high * cos_table + low * sin_table], axis=1
    ).reshape(width, rows)


def rotate_back(vectors, cos_table, sin_table):
    width, rows = vectors.shape
    split = vectors.reshape(width // HDIM, 2, HALF, rows)
    low, high = split[:, 0], split[:, 1]
    return jnp.stack(
        [low * cos_table + high * sin_table, high * cos_table - low * sin_table], axis=1
    ).reshape(width, rows)


def body(
    n_seq,
    n_tp,
    tokens,
    gain_one,
    w_qkv,
    w_out,
    gain_two,
    w_in,
    w_down,
    cotangent,
    doc_lengths,
    roster,
):
    rows, model = tokens.shape
    width = w_qkv.shape[2]
    heads = width // HDIM
    units = w_in.shape[2]
    part_rows = rows // n_tp
    count = n_seq // 2
    me = lax.axis_index("seq")
    tp = lax.axis_index("tp")
    qkv_t = w_qkv.transpose(1, 2, 0).reshape(3 * width, model)
    in_t = w_in.transpose(1, 2, 0).reshape(2 * units, model)

    def own_part(x, hop=0):
        return lax.dynamic_slice_in_dim(x, (tp ^ hop) * part_rows, part_rows, 0)

    cos_table, sin_table = own_tables(doc_lengths, roster, me, rows)
    inputs = tokens.astype(F32)
    unit_one, scale_one = normed(inputs)
    h_one = (unit_one * gain_one).astype(BF16)
    projected = mm(qkv_t, h_one, NT)
    queries = rotate(projected[:width], cos_table, sin_table).astype(BF16)
    queries = queries * jnp.asarray(HDIM**-0.5, BF16)
    keys = rotate(projected[width : 2 * width], cos_table, sin_table).astype(BF16)
    kv = jnp.concatenate([keys, projected[2 * width :].astype(BF16)], axis=0)
    blocks = [kv] + [swap(kv, "seq", 2 * j, n_seq) for j in range(1, count)]
    q_pair = swap(queries, "seq", 1, n_seq)
    w_outs = [w_out] + [swap(w_out, "tp", k, n_tp) for k in range(1, n_tp)]

    state_own, state_pair = attention_forward(doc_lengths, roster, queries, q_pair, blocks)
    state_back = swap(state_pair, "seq", 1, n_seq)
    top = jnp.maximum(state_own[:, 72:73], state_back[:, 72:73])
    fade_own = jnp.exp(state_own[:, 72:73] - top)
    fade_back = jnp.exp(state_back[:, 72:73] - top)
    mixed_state = state_own[:, :72] * fade_own + state_back[:, :72] * fade_back
    total = mixed_state[:, 64:65]
    log_total = top + jnp.log(total)
    out_b = (mixed_state[:, :64] / total).astype(BF16).reshape(width, rows)
    outs = [out_b] + [swap(out_b, "tp", k, n_tp) for k in range(1, n_tp)]
    out_pair = swap(out_b, "seq", 1, n_seq)
    totals = jnp.broadcast_to(log_total, (heads, 8, rows))
    totals_pair = swap(totals, "seq", 1, n_seq)

    middle = inputs
    for out, weight in zip(outs, w_outs):
        middle = middle + mm(out, weight, TN)
    unit_two, scale_two = normed(middle)
    h_two = (unit_two * gain_two).astype(BF16)
    gate_up = mm(in_t, h_two, NT)
    gate, up = gate_up[:units], gate_up[units:]
    erf_part = 0.5 * (1.0 + lax.erf(gate * (2.0**-0.5)))
    activated = gate * erf_part
    slope = erf_part + gate * jnp.exp(-0.5 * gate * gate) * ((2.0 * jnp.pi) ** -0.5)
    mixed = (activated * up).astype(BF16)
    mixed_grad = mm(w_down, cotangent, NT)
    gate_grad = jnp.concatenate(
        [mixed_grad * up * slope, mixed_grad * activated], axis=0
    ).astype(BF16)
    h_two_grad = mm(gate_grad, in_t, TN)
    gain_two_part = jnp.sum(h_two_grad * unit_two, axis=0, keepdims=True)
    h_two_low = h_two_grad.astype(BF16)
    arrived = own_part(h_two_grad)
    for k in range(1, n_tp):
        arrived = arrived + swap(own_part(h_two_low, k), "tp", k, n_tp).astype(F32)

    branch_two = mm(mixed, w_down, TN).astype(BF16)
    grad_down = mm(mixed, cotangent, NN)
    grad_in = mm(gate_grad, h_two, NN)

    middle_part = own_part(middle)
    unit_part, scale_part = normed(middle_part)
    middle_grad = own_part(cotangent).astype(F32) + norm_back(
        unit_part, scale_part, arrived, gain_two
    )
    branch_grad = middle_grad.astype(BF16)
    pieces = [mm(branch_grad, w_outs[0], NT).astype(BF16)] + [
        swap(mm(branch_grad, w_outs[k], NT).astype(BF16), "tp", k, n_tp) for k in range(1, n_tp)
    ]
    out_grad = jnp.zeros((rows, width), BF16)
    for k in range(n_tp):
        out_grad = lax.dynamic_update_slice_in_dim(out_grad, pieces[k], (tp ^ k) * part_rows, 0)
    out_grad = out_grad.T
    grad_pair = swap(out_grad, "seq", 1, n_seq)

    results = attention_backward(
        doc_lengths,
        roster,
        (queries, q_pair),
        (out_grad, grad_pair),
        (out_b, out_pair),
        (totals, totals_pair),
        blocks,
    )
    dq_own, dq_pair = results[:2]
    dkv = results[2]
    for j in range(1, count):
        dkv = dkv + swap(results[2 + j], "seq", 2 * j, n_seq).astype(F32)
    dq = dq_own + swap(dq_pair, "seq", 1, n_seq).astype(F32)

    branch_full = jnp.zeros((rows, model), BF16)
    for k in range(n_tp):
        piece = swap(branch_grad, "tp", k, n_tp) if k else branch_grad
        branch_full = lax.dynamic_update_slice_in_dim(branch_full, piece, (tp ^ k) * part_rows, 0)
    grad_out = mm(out_b, branch_full, NN)

    proj_grad = jnp.concatenate(
        [
            rotate_back(dq, cos_table, sin_table),
            rotate_back(dkv[:width], cos_table, sin_table),
            dkv[width:],
        ],
        axis=0,
    ).astype(BF16)
    h_one_grad = mm(proj_grad, qkv_t, TN)
    gain_one_part = jnp.sum(h_one_grad * unit_one, axis=0, keepdims=True)
    h_one_low = h_one_grad.astype(BF16)
    arrived = own_part(h_one_grad)
    for k in range(1, n_tp):
        arrived = arrived + swap(own_part(h_one_low, k), "tp", k, n_tp).astype(F32)
    unit_part, scale_part = normed(own_part(tokens).astype(F32))
    input_part = (middle_grad + norm_back(unit_part, scale_part, arrived, gain_one)).astype(BF16)
    input_grad = jnp.zeros((rows, model), BF16)
    for k in range(n_tp):
        piece = swap(input_part, "tp", k, n_tp) if k else input_part
        input_grad = lax.dynamic_update_slice_in_dim(input_grad, piece, (tp ^ k) * part_rows, 0)
    grad_qkv = mm(proj_grad, h_one, NN)

    layer_out = (middle + lax.psum(branch_two, "tp").astype(F32)).astype(BF16)
    low = lambda x: x.astype(BF16)
    gains = jnp.concatenate([gain_one_part, gain_two_part], axis=0)
    early = lax.psum((low(grad_down), low(grad_in)), "seq")
    late = lax.psum((low(grad_out), low(grad_qkv)), "seq")
    gains = lax.psum(gains, ("seq", "tp"))
    f = lambda x: x.astype(F32)
    back = lambda x, n: f(x).reshape(-1, n, model).transpose(2, 0, 1)
    return (
        layer_out,
        input_grad,
        gains[0],
        back(late[1], width),
        f(late[0]),
        gains[1],
        back(early[1], units),
        f(early[0]),
    )


def solution(mesh):
    placed = (
        P("seq", None),
        P(),
        P(None, None, "tp"),
        P("tp", None),
        P(),
        P(None, None, "tp"),
        P("tp", None),
        P("seq", None),
        P(),
        P(),
    )
    return jax.shard_map(
        functools.partial(body, mesh.shape["seq"], mesh.shape["tp"]),
        mesh=mesh,
        in_specs=placed,
        out_specs=(
            P("seq", None),
            P("seq", None),
            P(),
            P(None, None, "tp"),
            P("tp", None),
            P(),
            P(None, None, "tp"),
            P("tp", None),
        ),
        check_vma=False,
    )
```

time: 507 us -> 304 us (0.60); the launches traced: 498 us -> 303 us
  waiting for transfers between devices: 293 us -> 111 us
  starting transfers between devices: 0.54 us -> 63.4 us
  local copies, waits for them, and re-layouts: 57 us -> 13.7 us
  other arithmetic: 58.1 us -> 18.4 us
  matrix products: 55.3 us -> 28.3 us
  blocking collectives: 14.6 us -> 37.9 us
  Pallas kernels: 0 us -> 14.6 us
    psum x4 -> x2, waiting for transfers between devices: 209 us -> 37.3 us  [the longest x1 37.3 us: body(): layer_out = (middle + lax.psum(branch_two, 'tp').astype(F32)).astype(BF16)]
    ppermute x0 -> x33, waiting for transfers between devices: none -> 73.5 us  [swap(): return lax.ppermute(x, axis, [(i, i ^ hop) for i in range(count)])]
    ppermute x0 -> x33, starting transfers between devices: none -> 63.1 us  [swap(): return lax.ppermute(x, axis, [(i, i ^ hop) for i in range(count)])]
    unnamed x8 -> x2, waiting for transfers between devices: 54.9 us -> 0.03 us
    all_gather x2 -> x0, waiting for transfers between devices: 28.4 us -> none  [the longest x1 26.3 us: body(): lax.all_gather(key_flat, 'seq', axis=0, tiled=True)]
    dot_general x24 -> x18, matrix products: 52.5 us -> 28.3 us  [mm(): return lax.dot_general(a, b, dims, preferred_element_type=F32)]
    psum x1, blocking collectives: 14.6 us -> 37.9 us  [body(): gains = lax.psum(gains, ('seq', 'tp'))]
    reduce_sum x25 -> x10, other arithmetic: 23.2 us -> 5.88 us  [the longest x4 2.14 us: normed(): spread = jnp.mean(shifted * shifted, axis=-1, keepdims=True)]
  transfers between devices with their start and end apart: 7 -> 35, of which waited for: 7 -> 15; matrix products, arithmetic and copies ran while one was open for 10% -> 9% of each run, Pallas kernels for 0% -> 2%
where the time goes in v1:
time: 304 us; the launch traced here: 303 us
  waiting for transfers between devices  111 us (37%)
  starting transfers between devices  63.4 us (21%)
  blocking collectives  37.9 us (12%)
  matrix products  28.3 us (9%)
  other arithmetic  18.4 us (6%)
  between operations  15.6 us (5%)
  Pallas kernels  14.6 us (5%)
  local copies, waits for them, and re-layouts  13.7 us (5%)
    ppermute x33, waiting for transfers between devices, swap(): return lax.ppermute(x, axis, [(i, i ^ hop) for i in range(count)])  73.5 us
    ppermute x33, starting transfers between devices, swap(): return lax.ppermute(x, axis, [(i, i ^ hop) for i in range(count)])  63.1 us
    psum x1, blocking collectives, body(): gains = lax.psum(gains, ('seq', 'tp'))  37.9 us
    psum x1, waiting for transfers between devices, body(): layer_out = (middle + lax.psum(branch_two, 'tp').astype(F32)).astype(BF16)  37.3 us
    dot_general x18, matrix products, mm(): return lax.dot_general(a, b, dims, preferred_element_type=F32)  28.3 us
    pallas_call x1, Pallas kernels, attention_backward(): pl.pallas_call(functools.partial(backward_kernel, count, heads), out_shap...  8.11 us
    unnamed x87, local copies, waits for them, and re-layouts  7.47 us
    pallas_call x1, Pallas kernels, attention_forward(): pl.pallas_call(functools.partial(forward_kernel, count, heads), out_shape...  6.45 us
  transfers between devices with their start and end apart: 35, of which 15 were waited for; matrix products, arithmetic and copies ran while one was open for 9% of the time, Pallas kernels for 2%

profile of v1, /device:TPU:0, one launch (start us, length us, event | category | flops | bytes accessed | tf_op | source)
XLA Modules:
  0.0 302.7 jit_solution(11522890994653834572)
XLA Ops:
  14.9 3.0 collective-permute-start.1
  19.6 3.1 %collective-permute-start.8 = (bf16[192,768]{1,0:T(8,128)(2,1)}, bf16[192,768]{1,0:T(8,128)(2,1)}, u32[]{:S(2)}, u32[]{:S(2)}) collective-permute-start(bf16[192,768]{1,0:T(8,128)(2,1)} %param.13), channel_id=1, source_target_pairs={{0,2},{1,3},{2,0},{3,1},{4,6},{5,7},{6,4},{7,5},{8,10},{9,11},{10,... | collective-permute-start | bytes 884744 | tf_op jit(solution)/shard_map/ppermute | solution.py:32
  22.8 2.4 collective-permute-start.10
  25.2 2.7 collective-permute-done.1.refs_1_.refs_9_
  27.9 2.1 collective-permute-start.6
  30.0 6.9 %collective-permute-done.2.refs_2_.refs_10_ = bf16[384,448]{1,0:T(8,128)(2,1)S(1)} collective-permute-done((bf16[384,448]{1,0:T(8,128)(2,1)S(1)}, bf16[384,448]{1,0:T(8,128)(2,1)S(1)}, u32[]{:S(2)}, u32[]{:S(2)}) %collective-permute-start.2) | collective-permute-done | bytes 344096 | tf_op jit(solution)/shard_map/ppermute | solution.py:32
  38.5 6.4 %shard_map.161 = (f32[3,80,448]{2,1,0:T(8,128)}, f32[3,80,448]{2,1,0:T(8,128)}) custom-call(s32[4]{0:T(128)} %len_ref.3, s32[8]{0:T(128)} %roster_ref.3, bf16[192,448]{1,0:T(8,128)(2,1)} %bitcast.76, bf16[192,448]{1,0:T(8,128)(2,1)} %collective-permute-done.q_pair.refs_1_, bf16[384,448]{1,0:T(8,128)(2,1)} %copy-done.2, bf16[384,448]{1,0:T(8,128)(2,1)} %copy-done.8, ...), custom_call_target="tpu_custom_call" | custom-call | tf_op jit(solution)/shard_map/pallas_call | solution.py:137
  44.9 6.8 %collective-permute-start.4 = (f32[3,80,448]{2,1,0:T(8,128)}, f32[3,80,448]{2,1,0:T(8,128)S(1)}, u32[]{:S(2)}, u32[]{:S(2)}) collective-permute-start(f32[3,80,448]{2,1,0:T(8,128)} %get-tuple-element.17), channel_id=1, source_target_pairs={{0,4},{4,0},{8,12},{12,8},{16,20},{20,16},{24,28},{28,24},{1,5},{5... | collective-permute-start | bytes 1290248 | tf_op jit(solution)/shard_map/ppermute | solution.py:32
  56.3 2.6 collective-permute-start.7
  62.0 11.5 %collective-permute-done.7 = bf16[192,448]{1,0:T(8,128)(2,1)S(1)} collective-permute-done((bf16[192,448]{1,0:T(8,128)(2,1)S(1)}, bf16[192,448]{1,0:T(8,128)(2,1)S(1)}, u32[]{:S(2)}, u32[]{:S(2)}) %collective-permute-start.7) | collective-permute-done | bytes 172064 | tf_op jit(solution)/shard_map/ppermute | solution.py:32
  83.6 2.4 convolution_convert_fusion.3
  87.9 37.3 %all-reduce.4.cloned.1.call-done = bf16[448,768]{1,0:T(8,128)(2,1)} async-done(((bf16[448,768]{1,0:T(8,128)(2,1)}), bf16[448,768]{1,0:T(8,128)(2,1)}) %all-reduce.4.cloned.1.call-update) | async-done | bytes 688144 | tf_op jit(solution)/shard_map/psum | solution.py:421
  125.2 2.9 multiply_reduce_fusion
  130.4 2.2 collective-permute-start.13
  133.2 3.7 %collective-permute-done.11 = bf16[112,768]{1,0:T(8,128)(2,1)S(1)} collective-permute-done((bf16[112,768]{1,0:T(8,128)(2,1)S(1)}, bf16[112,768]{1,0:T(8,128)(2,1)S(1)}, u32[]{:S(2)}, u32[]{:S(2)}) %collective-permute-start.11) | collective-permute-done | bytes 172064 | tf_op jit(solution)/shard_map/ppermute | solution.py:32
  136.9 7.5 %collective-permute-done.12 = bf16[112,768]{1,0:T(8,128)(2,1)S(1)} collective-permute-done((bf16[112,768]{1,0:T(8,128)(2,1)S(1)}, bf16[112,768]{1,0:T(8,128)(2,1)S(1)}, u32[]{:S(2)}, u32[]{:S(2)}) %collective-permute-start.12) | collective-permute-done | bytes 172064 | tf_op jit(solution)/shard_map/ppermute | solution.py:32
  147.4 2.5 collective-permute-start.30
  151.7 2.1 collective-permute-start.14
  168.3 2.9 collective-permute-done.32
  173.6 8.1 %shard_map.162 = (f32[192,448]{1,0:T(8,128)}, bf16[192,448]{1,0:T(8,128)(2,1)}, f32[384,448]{1,0:T(8,128)}, bf16[384,448]{1,0:T(8,128)(2,1)}, bf16[384,448]{1,0:T(8,128)(2,1)}, /*index=5*/bf16[384,448]{1,0:T(8,128)(2,1)}) custom-call(s32[4]{0:T(128)} %len_ref.3, s32[8]{0:T(128)} %roster_ref.3, bf16[192,448]{1,0:T(8,128)(2,1)} %bitcast.77, ...), custom_call_target="tpu_custom_call" | custom-call | tf_op jit(solution)/shard_map/pallas_call | solution.py:220
  181.7 9.6 %collective-permute-start.20 = (bf16[192,448]{1,0:T(8,128)(2,1)}, bf16[192,448]{1,0:T(8,128)(2,1)S(1)}, u32[]{:S(2)}, u32[]{:S(2)}) collective-permute-start(bf16[192,448]{1,0:T(8,128)(2,1)} %get-tuple-element.19), channel_id=1, source_target_pairs={{0,4},{4,0},{8,12},{12,8},{16,20},{20,16},{24,28},{28,24},{1,5},{5... | collective-permute-start | bytes 516104 | tf_op jit(solution)/shard_map/ppermute | solution.py:32
  191.4 3.5 %collective-permute-start.23 = (bf16[384,448]{1,0:T(8,128)(2,1)}, bf16[384,448]{1,0:T(8,128)(2,1)S(1)}, u32[]{:S(2)}, u32[]{:S(2)}) collective-permute-start(bf16[384,448]{1,0:T(8,128)(2,1)} %get-tuple-element.23), channel_id=1, source_target_pairs={{0,24},{4,28},{8,16},{12,20},{16,8},{20,12},{24,0},{28,4},{1,25},{... | collective-permute-start | bytes 1032200 | tf_op jit(solution)/shard_map/ppermute | solution.py:32
  196.0 7.6 %collective-permute-done.21 = bf16[384,448]{1,0:T(8,128)(2,1)S(1)} collective-permute-done((bf16[384,448]{1,0:T(8,128)(2,1)}, bf16[384,448]{1,0:T(8,128)(2,1)S(1)}, u32[]{:S(2)}, u32[]{:S(2)}) %collective-permute-start.21) | collective-permute-done | bytes 344096 | tf_op jit(solution)/shard_map/ppermute | solution.py:32
  203.5 7.6 %collective-permute-done.22 = bf16[384,448]{1,0:T(8,128)(2,1)S(1)} collective-permute-done((bf16[384,448]{1,0:T(8,128)(2,1)}, bf16[384,448]{1,0:T(8,128)(2,1)S(1)}, u32[]{:S(2)}, u32[]{:S(2)}) %collective-permute-start.22) | collective-permute-done | bytes 344096 | tf_op jit(solution)/shard_map/ppermute | solution.py:32
  214.5 2.6 collective-permute-start.24
  222.7 9.2 %collective-permute-done.25 = bf16[112,768]{1,0:T(8,128)(2,1)S(1)} collective-permute-done((bf16[112,768]{1,0:T(8,128)(2,1)S(1)}, bf16[112,768]{1,0:T(8,128)(2,1)S(1)}, u32[]{:S(2)}, u32[]{:S(2)}) %collective-permute-start.25) | collective-permute-done | bytes 172064 | tf_op jit(solution)/shard_map/ppermute | solution.py:32
  233.5 3.1 %collective-permute-start.27 = (bf16[112,768]{1,0:T(8,128)(2,1)S(1)}, bf16[112,768]{1,0:T(8,128)(2,1)S(1)}, u32[]{:S(2)}, u32[]{:S(2)}) collective-permute-start(bf16[112,768]{1,0:T(8,128)(2,1)S(1)} %get-tuple-element.38), channel_id=1, source_target_pairs={{0,1},{1,0},{2,3},{3,2},{4,5},{5,4},{6,7},{7,6},{8,9},{9,8},{10,11... | collective-permute-start | bytes 516104 | tf_op jit(solution)/shard_map/ppermute | solution.py:32
  236.6 37.9 %psum.43 = f32[2,768]{1,0:T(2,128)S(1)} all-reduce(f32[2,768]{1,0:T(2,128)S(1)} %pad_maximum_fusion.10), channel_id=1, replica_groups=mesh['seq'=8,'tp'=4] {'seq','tp'}, use_global_device_ids=true, to_apply=%region_18.19 | all-reduce | flops 1536 | bytes 12288 | tf_op jit(solution)/shard_map/psum | solution.py:426
  274.5 2.2 collective-permute-start.28
  277.3 2.3 collective-permute-start.29
  279.6 10.2 %collective-permute-done.28 = bf16[112,768]{1,0:T(8,128)(2,1)S(1)} collective-permute-done((bf16[112,768]{1,0:T(8,128)(2,1)S(1)}, bf16[112,768]{1,0:T(8,128)(2,1)S(1)}, u32[]{:S(2)}, u32[]{:S(2)}) %collective-permute-start.28) | collective-permute-done | bytes 172064 | tf_op jit(solution)/shard_map/ppermute | solution.py:32
  289.9 2.8 transpose.51
  (219 shorter events, 69.4 us)
Async XLA Ops:
  7.2 118.0 %all-reduce.4.cloned.1.call-start = ((), (), s32[]{:S(2)}) async-start(), calls=%async_computation | async-start | bytes 1376256 | tf_op jit(solution)/shard_map/psum | solution.py:421
  14.9 12.9 %collective-permute-start.1 = (bf16[384,448]{1,0:T(8,128)(2,1)S(1)}, bf16[384,448]{1,0:T(8,128)(2,1)S(1)}, u32[]{:S(2)}, u32[]{:S(2)}) collective-permute-start(bf16[384,448]{1,0:T(8,128)(2,1)S(1)} %pad_maximum_fusion.2.refs_0_.refs_8_), channel_id=1, source_target_pairs={{0,8},{4,12},{8,0},{12,4},{16,24},{20,28},{24,16},{28,20},{1,9},{5... | collective-permute-start | bytes 1032200 | tf_op jit(solution)/shard_map/ppermute | solution.py:32
  17.9 19.0 %collective-permute-start.2 = (bf16[384,448]{1,0:T(8,128)(2,1)S(1)}, bf16[384,448]{1,0:T(8,128)(2,1)S(1)}, u32[]{:S(2)}, u32[]{:S(2)}) collective-permute-start(bf16[384,448]{1,0:T(8,128)(2,1)S(1)} %pad_maximum_fusion.2.refs_0_.refs_8_), channel_id=1, source_target_pairs={{0,16},{4,20},{8,24},{12,28},{16,0},{20,4},{24,8},{28,12},{1,17},{... | collective-permute-start | bytes 1032200 | tf_op jit(solution)/shard_map/ppermute | solution.py:32
  19.4 17.5 %collective-permute-start.3 = (bf16[384,448]{1,0:T(8,128)(2,1)S(1)}, bf16[384,448]{1,0:T(8,128)(2,1)S(1)}, u32[]{:S(2)}, u32[]{:S(2)}) collective-permute-start(bf16[384,448]{1,0:T(8,128)(2,1)S(1)} %pad_maximum_fusion.2.refs_0_.refs_8_), channel_id=1, source_target_pairs={{0,24},{4,28},{8,16},{12,20},{16,8},{20,12},{24,0},{28,4},{1,25},{... | collective-permute-start | bytes 1032200 | tf_op jit(solution)/shard_map/ppermute | solution.py:32
  19.6 42.0 %collective-permute-start.8 = (bf16[192,768]{1,0:T(8,128)(2,1)}, bf16[192,768]{1,0:T(8,128)(2,1)}, u32[]{:S(2)}, u32[]{:S(2)}) collective-permute-start(bf16[192,768]{1,0:T(8,128)(2,1)} %param.13), channel_id=1, source_target_pairs={{0,2},{1,3},{2,0},{3,1},{4,6},{5,7},{6,4},{7,5},{8,10},{9,11},{10,... | collective-permute-start | bytes 884744 | tf_op jit(solution)/shard_map/ppermute | solution.py:32
  22.8 52.0 %collective-permute-start.10 = (bf16[192,768]{1,0:T(8,128)(2,1)}, bf16[192,768]{1,0:T(8,128)(2,1)}, u32[]{:S(2)}, u32[]{:S(2)}) collective-permute-start(bf16[192,768]{1,0:T(8,128)(2,1)} %param.13), channel_id=1, source_target_pairs={{0,3},{1,2},{2,1},{3,0},{4,7},{5,6},{6,5},{7,4},{8,11},{9,10},{10,... | collective-permute-start | bytes 884744 | tf_op jit(solution)/shard_map/ppermute | solution.py:32
  27.9 48.3 %collective-permute-start.6 = (bf16[192,768]{1,0:T(8,128)(2,1)}, bf16[192,768]{1,0:T(8,128)(2,1)}, u32[]{:S(2)}, u32[]{:S(2)}) collective-permute-start(bf16[192,768]{1,0:T(8,128)(2,1)} %param.13), channel_id=1, source_target_pairs={{0,1},{1,0},{2,3},{3,2},{4,5},{5,4},{6,7},{7,6},{8,9},{9,8},{10,11... | collective-permute-start | bytes 884744 | tf_op jit(solution)/shard_map/ppermute | solution.py:32
  44.9 8.5 %collective-permute-start.4 = (f32[3,80,448]{2,1,0:T(8,128)}, f32[3,80,448]{2,1,0:T(8,128)S(1)}, u32[]{:S(2)}, u32[]{:S(2)}) collective-permute-start(f32[3,80,448]{2,1,0:T(8,128)} %get-tuple-element.17), channel_id=1, source_target_pairs={{0,4},{4,0},{8,12},{12,8},{16,20},{20,16},{24,28},{28,24},{1,5},{5... | collective-permute-start | bytes 1290248 | tf_op jit(solution)/shard_map/ppermute | solution.py:32
  56.3 17.2 %collective-permute-start.7 = (bf16[192,448]{1,0:T(8,128)(2,1)S(1)}, bf16[192,448]{1,0:T(8,128)(2,1)S(1)}, u32[]{:S(2)}, u32[]{:S(2)}) collective-permute-start(bf16[192,448]{1,0:T(8,128)(2,1)S(1)} %bitcast.68), channel_id=1, source_target_pairs={{0,2},{1,3},{2,0},{3,1},{4,6},{5,7},{6,4},{7,5},{8,10},{9,11},{10,... | collective-permute-start | bytes 516104 | tf_op jit(solution)/shard_map/ppermute | solution.py:32
  58.8 16.0 %collective-permute-start.9 = (bf16[192,448]{1,0:T(8,128)(2,1)S(1)}, bf16[192,448]{1,0:T(8,128)(2,1)S(1)}, u32[]{:S(2)}, u32[]{:S(2)}) collective-permute-start(bf16[192,448]{1,0:T(8,128)(2,1)S(1)} %bitcast.69), channel_id=1, source_target_pairs={{0,3},{1,2},{2,1},{3,0},{4,7},{5,6},{6,5},{7,4},{8,11},{9,10},{10,... | collective-permute-start | bytes 516104 | tf_op jit(solution)/shard_map/ppermute | solution.py:32
  61.6 14.6 %collective-permute-start.5 = (bf16[192,448]{1,0:T(8,128)(2,1)S(1)}, bf16[192,448]{1,0:T(8,128)(2,1)S(1)}, u32[]{:S(2)}, u32[]{:S(2)}) collective-permute-start(bf16[192,448]{1,0:T(8,128)(2,1)S(1)} %bitcast.71), channel_id=1, source_target_pairs={{0,1},{1,0},{2,3},{3,2},{4,5},{5,4},{6,7},{7,6},{8,9},{9,8},{10,11... | collective-permute-start | bytes 516104 | tf_op jit(solution)/shard_map/ppermute | solution.py:32
  83.2 206.7 %all-reduce.6.cloned.1.call-start = ((), (), s32[]{:S(2)}) async-start(), calls=%async_computation.1 | async-start | bytes 5013504 | tf_op jit(solution)/shard_map/psum | solution.py:425
  128.2 8.7 %collective-permute-start.11 = (bf16[112,768]{1,0:T(8,128)(2,1)S(1)}, bf16[112,768]{1,0:T(8,128)(2,1)S(1)}, u32[]{:S(2)}, u32[]{:S(2)}) collective-permute-start(bf16[112,768]{1,0:T(8,128)(2,1)S(1)} %get-tuple-element.56), channel_id=1, source_target_pairs={{0,1},{1,0},{2,3},{3,2},{4,5},{5,4},{6,7},{7,6},{8,9},{9,8},{10,11... | collective-permute-start | bytes 516104 | tf_op jit(solution)/shard_map/ppermute | solution.py:32
  129.2 15.3 %collective-permute-start.12 = (bf16[112,768]{1,0:T(8,128)(2,1)S(1)}, bf16[112,768]{1,0:T(8,128)(2,1)S(1)}, u32[]{:S(2)}, u32[]{:S(2)}) collective-permute-start(bf16[112,768]{1,0:T(8,128)(2,1)S(1)} %get-tuple-element.58), channel_id=1, source_target_pairs={{0,2},{1,3},{2,0},{3,1},{4,6},{5,7},{6,4},{7,5},{8,10},{9,11},{10,... | collective-permute-start | bytes 516104 | tf_op jit(solution)/shard_map/ppermute | solution.py:32
  130.4 14.0 %collective-permute-start.13 = (bf16[112,768]{1,0:T(8,128)(2,1)S(1)}, bf16[112,768]{1,0:T(8,128)(2,1)S(1)}, u32[]{:S(2)}, u32[]{:S(2)}) collective-permute-start(bf16[112,768]{1,0:T(8,128)(2,1)S(1)} %get-tuple-element.57), channel_id=1, source_target_pairs={{0,3},{1,2},{2,1},{3,0},{4,7},{5,6},{6,5},{7,4},{8,11},{9,10},{10,... | collective-permute-start | bytes 516104 | tf_op jit(solution)/shard_map/ppermute | solution.py:32
  147.4 18.3 %collective-permute-start.30 = (bf16[112,768]{1,0:T(8,128)(2,1)S(1)}, bf16[112,768]{1,0:T(8,128)(2,1)S(1)}, u32[]{:S(2)}, u32[]{:S(2)}) collective-permute-start(bf16[112,768]{1,0:T(8,128)(2,1)S(1)} %get-tuple-element.35), channel_id=1, source_target_pairs={{0,1},{1,0},{2,3},{3,2},{4,5},{5,4},{6,7},{7,6},{8,9},{9,8},{10,11... | collective-permute-start | bytes 516104 | tf_op jit(solution)/shard_map/ppermute | solution.py:32
  150.0 17.4 %collective-permute-start.31 = (bf16[112,768]{1,0:T(8,128)(2,1)S(1)}, bf16[112,768]{1,0:T(8,128)(2,1)}, u32[]{:S(2)}, u32[]{:S(2)}) collective-permute-start(bf16[112,768]{1,0:T(8,128)(2,1)S(1)} %get-tuple-element.35), channel_id=1, source_target_pairs={{0,2},{1,3},{2,0},{3,1},{4,6},{5,7},{6,4},{7,5},{8,10},{9,11},{10,... | collective-permute-start | bytes 516104 | tf_op jit(solution)/shard_map/ppermute | solution.py:32
  151.7 9.1 %collective-permute-start.14 = (bf16[112,192]{0,1:T(8,128)(2,1)S(1)}, bf16[112,192]{0,1:T(8,128)(2,1)S(1)}, u32[]{:S(2)}, u32[]{:S(2)}) collective-permute-start(bf16[112,192]{0,1:T(8,128)(2,1)S(1)} %convolution_convert_fusion.7), channel_id=1, source_target_pairs={{0,1},{1,0},{2,3},{3,2},{4,5},{5,4},{6,7},{7,6},{8,9},{9,8},{10,11... | collective-permute-start | bytes 129032 | tf_op jit(solution)/shard_map/ppermute | solution.py:32
  155.6 6.3 %collective-permute-start.15 = (bf16[112,192]{0,1:T(8,128)(2,1)}, bf16[112,192]{0,1:T(8,128)(2,1)S(1)}, u32[]{:S(2)}, u32[]{:S(2)}) collective-permute-start(bf16[112,192]{0,1:T(8,128)(2,1)} %convolution_convert_fusion.6), channel_id=1, source_target_pairs={{0,2},{1,3},{2,0},{3,1},{4,6},{5,7},{6,4},{7,5},{8,10},{9,11},{10,... | collective-permute-start | bytes 129032 | tf_op jit(solution)/shard_map/ppermute | solution.py:32
  160.7 11.5 %collective-permute-start.18 = (bf16[192,448]{1,0:T(8,128)(2,1)S(1)}, bf16[192,448]{1,0:T(8,128)(2,1)S(1)}, u32[]{:S(2)}, u32[]{:S(2)}) collective-permute-start(bf16[192,448]{1,0:T(8,128)(2,1)S(1)} %bitcast.72), channel_id=1, source_target_pairs={{0,4},{4,0},{8,12},{12,8},{16,20},{20,16},{24,28},{28,24},{1,5},{5... | collective-permute-start | bytes 516104 | tf_op jit(solution)/shard_map/ppermute | solution.py:32
  161.9 10.3 %collective-permute-start.19 = (f32[3,8,448]{2,1,0:T(8,128)S(1)}, f32[3,8,448]{2,1,0:T(8,128)}, u32[]{:S(2)}, u32[]{:S(2)}) collective-permute-start(f32[3,8,448]{2,1,0:T(8,128)S(1)} %broadcast_in_dim.28.refs_6_), channel_id=1, source_target_pairs={{0,4},{4,0},{8,12},{12,8},{16,20},{20,16},{24,28},{28,24},{1,5},{5... | collective-permute-start | bytes 129032 | tf_op jit(solution)/shard_map/ppermute | solution.py:32
  163.2 8.0 %collective-permute-start.32 = (bf16[112,768]{1,0:T(8,128)(2,1)S(1)}, bf16[112,768]{1,0:T(8,128)(2,1)}, u32[]{:S(2)}, u32[]{:S(2)}) collective-permute-start(bf16[112,768]{1,0:T(8,128)(2,1)S(1)} %get-tuple-element.35), channel_id=1, source_target_pairs={{0,3},{1,2},{2,1},{3,0},{4,7},{5,6},{6,5},{7,4},{8,11},{9,10},{10,... | collective-permute-start | bytes 516104 | tf_op jit(solution)/shard_map/ppermute | solution.py:32
  181.7 14.2 %collective-permute-start.20 = (bf16[192,448]{1,0:T(8,128)(2,1)}, bf16[192,448]{1,0:T(8,128)(2,1)S(1)}, u32[]{:S(2)}, u32[]{:S(2)}) collective-permute-start(bf16[192,448]{1,0:T(8,128)(2,1)} %get-tuple-element.19), channel_id=1, source_target_pairs={{0,4},{4,0},{8,12},{12,8},{16,20},{20,16},{24,28},{28,24},{1,5},{5... | collective-permute-start | bytes 516104 | tf_op jit(solution)/shard_map/ppermute | solution.py:32
  191.4 12.2 %collective-permute-start.21 = (bf16[384,448]{1,0:T(8,128)(2,1)}, bf16[384,448]{1,0:T(8,128)(2,1)S(1)}, u32[]{:S(2)}, u32[]{:S(2)}) collective-permute-start(bf16[384,448]{1,0:T(8,128)(2,1)} %get-tuple-element.21), channel_id=1, source_target_pairs={{0,8},{4,12},{8,0},{12,4},{16,24},{20,28},{24,16},{28,20},{1,9},{5... | collective-permute-start | bytes 1032200 | tf_op jit(solution)/shard_map/ppermute | solution.py:32
  191.4 19.8 %collective-permute-start.22 = (bf16[384,448]{1,0:T(8,128)(2,1)}, bf16[384,448]{1,0:T(8,128)(2,1)S(1)}, u32[]{:S(2)}, u32[]{:S(2)}) collective-permute-start(bf16[384,448]{1,0:T(8,128)(2,1)} %get-tuple-element.22), channel_id=1, source_target_pairs={{0,16},{4,20},{8,24},{12,28},{16,0},{20,4},{24,8},{28,12},{1,17},{... | collective-permute-start | bytes 1032200 | tf_op jit(solution)/shard_map/ppermute | solution.py:32
  191.4 19.8 %collective-permute-start.23 = (bf16[384,448]{1,0:T(8,128)(2,1)}, bf16[384,448]{1,0:T(8,128)(2,1)S(1)}, u32[]{:S(2)}, u32[]{:S(2)}) collective-permute-start(bf16[384,448]{1,0:T(8,128)(2,1)} %get-tuple-element.23), channel_id=1, source_target_pairs={{0,24},{4,28},{8,16},{12,20},{16,8},{20,12},{24,0},{28,4},{1,25},{... | collective-permute-start | bytes 1032200 | tf_op jit(solution)/shard_map/ppermute | solution.py:32
  214.5 8.3 %collective-permute-start.24 = (bf16[112,768]{1,0:T(8,128)(2,1)S(1)}, bf16[112,768]{1,0:T(8,128)(2,1)S(1)}, u32[]{:S(2)}, u32[]{:S(2)}) collective-permute-start(bf16[112,768]{1,0:T(8,128)(2,1)S(1)} %get-tuple-element.53), channel_id=1, source_target_pairs={{0,1},{1,0},{2,3},{3,2},{4,5},{5,4},{6,7},{7,6},{8,9},{9,8},{10,11... | collective-permute-start | bytes 516104 | tf_op jit(solution)/shard_map/ppermute | solution.py:32
  217.1 14.8 %collective-permute-start.25 = (bf16[112,768]{1,0:T(8,128)(2,1)S(1)}, bf16[112,768]{1,0:T(8,128)(2,1)S(1)}, u32[]{:S(2)}, u32[]{:S(2)}) collective-permute-start(bf16[112,768]{1,0:T(8,128)(2,1)S(1)} %get-tuple-element.55), channel_id=1, source_target_pairs={{0,2},{1,3},{2,0},{3,1},{4,6},{5,7},{6,4},{7,5},{8,10},{9,11},{10,... | collective-permute-start | bytes 516104 | tf_op jit(solution)/shard_map/ppermute | solution.py:32
  218.2 13.8 %collective-permute-start.26 = (bf16[112,768]{1,0:T(8,128)(2,1)S(1)}, bf16[112,768]{1,0:T(8,128)(2,1)S(1)}, u32[]{:S(2)}, u32[]{:S(2)}) collective-permute-start(bf16[112,768]{1,0:T(8,128)(2,1)S(1)} %get-tuple-element.54), channel_id=1, source_target_pairs={{0,3},{1,2},{2,1},{3,0},{4,7},{5,6},{6,5},{7,4},{8,11},{9,10},{10,... | collective-permute-start | bytes 516104 | tf_op jit(solution)/shard_map/ppermute | solution.py:32
  233.5 46.1 %collective-permute-start.27 = (bf16[112,768]{1,0:T(8,128)(2,1)S(1)}, bf16[112,768]{1,0:T(8,128)(2,1)S(1)}, u32[]{:S(2)}, u32[]{:S(2)}) collective-permute-start(bf16[112,768]{1,0:T(8,128)(2,1)S(1)} %get-tuple-element.38), channel_id=1, source_target_pairs={{0,1},{1,0},{2,3},{3,2},{4,5},{5,4},{6,7},{7,6},{8,9},{9,8},{10,11... | collective-permute-start | bytes 516104 | tf_op jit(solution)/shard_map/ppermute | solution.py:32
  274.5 15.3 %collective-permute-start.28 = (bf16[112,768]{1,0:T(8,128)(2,1)S(1)}, bf16[112,768]{1,0:T(8,128)(2,1)S(1)}, u32[]{:S(2)}, u32[]{:S(2)}) collective-permute-start(bf16[112,768]{1,0:T(8,128)(2,1)S(1)} %get-tuple-element.38), channel_id=1, source_target_pairs={{0,2},{1,3},{2,0},{3,1},{4,6},{5,7},{6,4},{7,5},{8,10},{9,11},{10,... | collective-permute-start | bytes 516104 | tf_op jit(solution)/shard_map/ppermute | solution.py:32
  277.3 12.5 %collective-permute-start.29 = (bf16[112,768]{1,0:T(8,128)(2,1)S(1)}, bf16[112,768]{1,0:T(8,128)(2,1)S(1)}, u32[]{:S(2)}, u32[]{:S(2)}) collective-permute-start(bf16[112,768]{1,0:T(8,128)(2,1)S(1)} %get-tuple-element.38), channel_id=1, source_target_pairs={{0,3},{1,2},{2,1},{3,0},{4,7},{5,6},{6,5},{7,4},{8,11},{9,10},{10,... | collective-permute-start | bytes 516104 | tf_op jit(solution)/shard_map/ppermute | solution.py:32
  (45 other events, 426.9 us)
Sparse Core Ops, SparseCore 0:
  83.3 41.8 all-reduce.3
  221.4 64.1 all-reduce.5

commit v2 on v1

--- a/solution.py
+++ b/solution.py
@@ -13,6 +13,7 @@
 ROPE_THETA = 160000.0
 MASKED = -1e30
 AUG = 80
+STRIP = 64
 F32 = jnp.float32
 BF16 = jnp.bfloat16
 ANY = pl.BlockSpec(memory_space=pl.ANY)
@@ -22,6 +23,14 @@
 NN = (((1,), (0,)), ((), ()))
 NT = (((1,), (1,)), ((), ()))
 TN = (((0,), (0,)), ((), ()))
+
+
+def params(mib):
+    return pltpu.CompilerParams(vmem_limit_bytes=mib * 2**20)
+
+
+def shaped(shape, dtype):
+    return jax.ShapeDtypeStruct(shape, dtype)
 
 
 def mm(a, b, dims):
@@ -73,6 +82,83 @@
 
 def key_row(block, seq_index):
     return seq_index ^ (2 * block)
+
+
+def place_row(ends, base, rows):
+    spot = base + lax.broadcasted_iota(jnp.int32, (1, rows), 1)
+    start = jnp.zeros((1, rows), jnp.int32)
+    for end in ends:
+        start = jnp.where(spot >= end, end, start)
+    return (spot - start).astype(F32)
+
+
+def normed(values):
+    centre = jnp.mean(values, axis=-1, keepdims=True)
+    shifted = values - centre
+    spread = jnp.mean(shifted * shifted, axis=-1, keepdims=True)
+    scale = lax.rsqrt(spread + EPSILON)
+    return shifted * scale, scale
+
+
+def norm_back(unit, scale, grad, gain):
+    u = grad * gain
+    mean_u = jnp.mean(u, axis=-1, keepdims=True)
+    mean_un = jnp.mean(u * unit, axis=-1, keepdims=True)
+    return scale * (u - mean_u - unit * mean_un)
+
+
+def project_kernel(width, len_ref, roster_ref, x_ref, gain_ref, w_ref, freq_ref, *refs):
+    q_out, kv_out, h_out, cos_out, sin_out, proj = refs
+    rows = x_ref.shape[0]
+
+    def strip(i, carry):
+        at = pl.ds(i * STRIP, STRIP)
+        unit, unused = normed(x_ref[at, :].astype(F32))
+        h_out[at, :] = (unit * gain_ref[...]).astype(BF16)
+        return carry
+
+    lax.fori_loop(0, rows // STRIP, strip, 0)
+    proj[...] = mm(w_ref[...], h_out[...], NT)
+    ends = doc_bounds(len_ref)
+    place = place_row(ends, roster_ref[lax.axis_index("seq")] * rows, rows)
+    angles = place * freq_ref[...]
+    cos_table = jnp.cos(angles)
+    sin_table = jnp.sin(angles)
+    cos_out[...] = cos_table
+    sin_out[...] = sin_table
+    for at in range(0, 2 * width, HDIM):
+        low = proj[at : at + HALF, :]
+        high = proj[at + HALF : at + HDIM, :]
+        turned_low = (low * cos_table - high * sin_table).astype(BF16)
+        turned_high = (high * cos_table + low * sin_table).astype(BF16)
+        if at < width:
+            q_out[at : at + HALF, :] = (turned_low.astype(F32) * HDIM**-0.5).astype(BF16)
+            q_out[at + HALF : at + HDIM, :] = (turned_high.astype(F32) * HDIM**-0.5).astype(BF16)
+        else:
+            kv_out[at - width : at - width + HALF, :] = turned_low
+            kv_out[at - width + HALF : at - width + HDIM, :] = turned_high
+    kv_out[width:, :] = proj[2 * width :, :].astype(BF16)
+
+
+def project(doc_lengths, roster, tokens, gain, qkv_t):
+    rows, model = tokens.shape
+    width = qkv_t.shape[0] // 3
+    freq = ROPE_THETA ** (-(jnp.arange(HALF).astype(F32) * (2.0 / HDIM)))
+    table = shaped((HALF, rows), F32)
+    return pl.pallas_call(
+        functools.partial(project_kernel, width),
+        out_shape=(
+            shaped((width, rows), BF16),
+            shaped((2 * width, rows), BF16),
+            shaped((rows, model), BF16),
+            table,
+            table,
+        ),
+        in_specs=[SMEM, SMEM] + [VMEM] * 4,
+        out_specs=(VMEM,) * 5,
+        scratch_shapes=[pltpu.VMEM((3 * width, rows), F32)],
+        compiler_params=params(24),
+    )(doc_lengths, roster, tokens, gain, qkv_t, freq[:, None])
 
 
 def forward_kernel(count, heads, len_ref, roster_ref, q_own, q_pair, *refs):
@@ -234,49 +320,317 @@
     )(doc_lengths, roster, *queries, *grads, *outs, *totals, *blocks)
 
 
-def normed(values):
-    centre = jnp.mean(values, axis=-1, keepdims=True)
-    shifted = values - centre
-    spread = jnp.mean(shifted * shifted, axis=-1, keepdims=True)
-    scale = lax.rsqrt(spread + EPSILON)
-    return shifted * scale, scale
-
-
-def norm_back(unit, scale, grad, gain):
-    u = grad * gain
-    mean_u = jnp.mean(u, axis=-1, keepdims=True)
-    mean_un = jnp.mean(u * unit, axis=-1, keepdims=True)
-    return scale * (u - mean_u - unit * mean_un)
-
-
-def own_tables(doc_lengths, roster, me, rows):
-    base = jnp.sum(jnp.where(jnp.arange(roster.shape[0]) == me, roster, 0)) * rows
-    packed = base + jnp.arange(rows, dtype=jnp.int32)
-    doc_ends = jnp.cumsum(doc_lengths)
-    passed = packed[None, :] >= doc_ends[:, None]
-    start = jnp.max(jnp.where(passed, doc_ends[:, None], 0), axis=0)
-    place = packed - start
-    frequency = ROPE_THETA ** (-(jnp.arange(HALF).astype(F32) * (2.0 / HDIM)))
-    angles = place.astype(F32)[None, :] * frequency[:, None]
-    return jnp.cos(angles), jnp.sin(angles)
-
-
-def rotate(vectors, cos_table, sin_table):
-    width, rows = vectors.shape
-    split = vectors.reshape(width // HDIM, 2, HALF, rows)
-    low, high = split[:, 0], split[:, 1]
-    return jnp.stack(
-        [low * cos_table - high * sin_table, high * cos_table + low * sin_table], axis=1
-    ).reshape(width, rows)
-
-
-def rotate_back(vectors, cos_table, sin_table):
-    width, rows = vectors.shape
-    split = vectors.reshape(width // HDIM, 2, HALF, rows)
-    low, high = split[:, 0], split[:, 1]
-    return jnp.stack(
-        [low * cos_table + high * sin_table, high * cos_table - low * sin_table], axis=1
-    ).reshape(width, rows)
+def join_kernel(heads, own_ref, back_ref, out_ref, total_ref):
+    rows = own_ref.shape[2]
+    for h in range(heads):
+        top_own = own_ref[h, 72:73, :]
+        top_back = back_ref[h, 72:73, :]
+        top = jnp.maximum(top_own, top_back)
+        fade_own = jnp.exp(top_own - top)
+        fade_back = jnp.exp(top_back - top)
+        total = own_ref[h, 64:65, :] * fade_own + back_ref[h, 64:65, :] * fade_back
+        share_own = fade_own / total
+        share_back = fade_back / total
+        value = own_ref[h, :HDIM, :] * share_own + back_ref[h, :HDIM, :] * share_back
+        out_ref[h * HDIM : (h + 1) * HDIM, :] = value.astype(BF16)
+        total_ref[h] = jnp.broadcast_to(top + jnp.log(total), (8, rows))
+
+
+def join(own, back):
+    heads, unused, rows = own.shape
+    return pl.pallas_call(
+        functools.partial(join_kernel, heads),
+        out_shape=(shaped((heads * HDIM, rows), BF16), shaped((heads, 8, rows), F32)),
+        in_specs=[VMEM, VMEM],
+        out_specs=(VMEM, VMEM),
+        compiler_params=params(16),
+    )(own, back)
+
+
+def feed_kernel(n_tp, x_ref, cot_ref, gain_ref, in_ref, down_ref, *refs):
+    out_refs = refs[:n_tp]
+    w_refs = refs[n_tp : 2 * n_tp]
+    middle_out, h_out, mixed_out, gate_out, gain_out = refs[2 * n_tp : 2 * n_tp + 5]
+    part_refs = refs[2 * n_tp + 5 : 3 * n_tp + 5]
+    outs, weights, unit, gate_up, mixed_grad, grad = refs[3 * n_tp + 5 :]
+    rows = x_ref.shape[0]
+    part = rows // n_tp
+    units = down_ref.shape[0]
+    width = out_refs[0].shape[0]
+    tp = lax.axis_index("tp")
+    for k in range(n_tp):
+        outs[k * width : (k + 1) * width, :] = out_refs[k][...]
+        weights[k * width : (k + 1) * width, :] = w_refs[k][...]
+    middle_out[...] = mm(outs[...], weights[...], TN)
+    mixed_grad[...] = mm(down_ref[...], cot_ref[...], NT)
+
+    def strip(i, carry):
+        at = pl.ds(i * STRIP, STRIP)
+        middle = middle_out[at, :] + x_ref[at, :].astype(F32)
+        middle_out[at, :] = middle
+        held, unused = normed(middle)
+        unit[at, :] = held
+        h_out[at, :] = (held * gain_ref[...]).astype(BF16)
+        return carry
+
+    lax.fori_loop(0, rows // STRIP, strip, 0)
+    gate_up[...] = mm(in_ref[...], h_out[...], NT)
+
+    def wave(i, carry):
+        at = pl.ds(i * 32, 32)
+        late = pl.ds(units + i * 32, 32)
+        gate = gate_up[at, :]
+        up = gate_up[late, :]
+        back = mixed_grad[at, :]
+        bell = 0.5 * (1.0 + lax.erf(gate * (2.0**-0.5)))
+        active = gate * bell
+        slope = bell + gate * jnp.exp(-0.5 * gate * gate) * ((2.0 * jnp.pi) ** -0.5)
+        mixed_out[at, :] = (active * up).astype(BF16)
+        gate_out[at, :] = (back * up * slope).astype(BF16)
+        gate_out[late, :] = (back * active).astype(BF16)
+        return carry
+
+    lax.fori_loop(0, units // 32, wave, 0)
+    grad[...] = mm(gate_out[...], in_ref[...], TN)
+
+    def gains(i, carry):
+        at = pl.ds(i * STRIP, STRIP)
+        product = grad[at, :] * unit[at, :]
+        return carry + jnp.sum(product.reshape(STRIP // 8, 8, -1), axis=0)
+
+    gain_out[...] = lax.fori_loop(0, rows // STRIP, gains, jnp.zeros(gain_out.shape, F32))
+    for k in range(n_tp):
+        at = pl.ds(pl.multiple_of((tp ^ k) * part, part), part)
+        part_refs[k][...] = grad[at, :].astype(part_refs[k].dtype)
+
+
+def feed(tokens, cotangent, gain, in_t, w_down, outs, w_outs):
+    rows, model = tokens.shape
+    n_tp = len(outs)
+    units = w_down.shape[0]
+    part = rows // n_tp
+    return pl.pallas_call(
+        functools.partial(feed_kernel, n_tp),
+        out_shape=(
+            shaped((rows, model), F32),
+            shaped((rows, model), BF16),
+            shaped((units, rows), BF16),
+            shaped((2 * units, rows), BF16),
+            shaped((8, model), F32),
+            shaped((part, model), F32),
+        )
+        + (shaped((part, model), BF16),) * (n_tp - 1),
+        in_specs=[VMEM] * (5 + 2 * n_tp),
+        out_specs=(VMEM,) * (5 + n_tp),
+        scratch_shapes=[
+            pltpu.VMEM((n_tp * outs[0].shape[0], rows), BF16),
+            pltpu.VMEM((n_tp * outs[0].shape[0], model), BF16),
+            pltpu.VMEM((rows, model), F32),
+            pltpu.VMEM((2 * units, rows), F32),
+            pltpu.VMEM((units, rows), F32),
+            pltpu.VMEM((rows, model), F32),
+        ],
+        compiler_params=params(32),
+    )(tokens, cotangent, gain, in_t, w_down, *outs, *w_outs)
+
+
+def branch_kernel(n_tp, middle_ref, cot_ref, gain_ref, *refs):
+    arrived = refs[:n_tp]
+    w_refs = refs[n_tp : 2 * n_tp]
+    grad_out, branch_out = refs[2 * n_tp : 2 * n_tp + 2]
+    piece_refs = refs[2 * n_tp + 2 :]
+    part = arrived[0].shape[0]
+    tp = lax.axis_index("tp")
+    at = pl.ds(pl.multiple_of(tp * part, part), part)
+    total = arrived[0][...]
+    for ref in arrived[1:]:
+        total = total + ref[...].astype(F32)
+    unit, scale = normed(middle_ref[at, :])
+    value = cot_ref[at, :].astype(F32) + norm_back(unit, scale, total, gain_ref[...])
+    grad_out[...] = value
+    branch_out[...] = value.astype(BF16)
+    for k in range(n_tp):
+        piece_refs[k][...] = mm(branch_out[...], w_refs[k][...], NT).astype(BF16)
+
+
+def branch(middle, cotangent, gain, arrived, w_outs):
+    part, model = arrived[0].shape
+    n_tp = len(arrived)
+    width = w_outs[0].shape[0]
+    return pl.pallas_call(
+        functools.partial(branch_kernel, n_tp),
+        out_shape=(shaped((part, model), F32), shaped((part, model), BF16))
+        + (shaped((part, width), BF16),) * n_tp,
+        in_specs=[VMEM] * (3 + 2 * n_tp),
+        out_specs=(VMEM,) * (2 + n_tp),
+        compiler_params=params(24),
+    )(middle, cotangent, gain, *arrived, *w_outs)
+
+
+def lay_kernel(n_tp, *refs):
+    out_ref, held = refs[n_tp:]
+    part = refs[0].shape[0]
+    tp = lax.axis_index("tp")
+    for k in range(n_tp):
+        at = pl.ds(pl.multiple_of((tp ^ k) * part, part), part)
+        held[at, :] = refs[k][...].astype(F32)
+    out_ref[...] = held[...].T.astype(BF16)
+
+
+def lay_turned(pieces):
+    part, width = pieces[0].shape
+    rows = part * len(pieces)
+    return pl.pallas_call(
+        functools.partial(lay_kernel, len(pieces)),
+        out_shape=shaped((width, rows), BF16),
+        in_specs=[VMEM] * len(pieces),
+        out_specs=VMEM,
+        scratch_shapes=[pltpu.VMEM((rows, width), F32)],
+        compiler_params=params(16),
+    )(*pieces)
+
+
+def stack_kernel(n_tp, *refs):
+    out_ref = refs[n_tp]
+    part = refs[0].shape[0]
+    tp = lax.axis_index("tp")
+    for k in range(n_tp):
+        at = pl.ds(pl.multiple_of((tp ^ k) * part, part), part)
+        out_ref[at, :] = refs[k][...]
+
+
+def stack_parts(pieces):
+    part, model = pieces[0].shape
+    return pl.pallas_call(
+        functools.partial(stack_kernel, len(pieces)),
+        out_shape=shaped((part * len(pieces), model), pieces[0].dtype),
+        in_specs=[VMEM] * len(pieces),
+        out_specs=VMEM,
+        compiler_params=params(16),
+    )(*pieces)
+
+
+def turn_back(out_ref, first, value, cos_table, sin_table):
+    for at in range(0, value.shape[0], HDIM):
+        low = value[at : at + HALF]
+        high = value[at + HALF : at + HDIM]
+        spot = first + at
+        out_ref[spot : spot + HALF, :] = (low * cos_table + high * sin_table).astype(BF16)
+        out_ref[spot + HALF : spot + HDIM, :] = (high * cos_table - low * sin_table).astype(BF16)
+
+
+def unproject_kernel(count, n_tp, x_ref, w_ref, cos_ref, sin_ref, dq_ref, dq_back, *refs):
+    dkv_refs = refs[:count]
+    proj_out = refs[count]
+    part_refs = refs[count + 1 : count + 1 + n_tp]
+    grad, dkv = refs[count + 1 + n_tp :]
+    rows, model = x_ref.shape
+    part = rows // n_tp
+    width = dq_ref.shape[0]
+    tp = lax.axis_index("tp")
+    cos_table = cos_ref[...]
+    sin_table = sin_ref[...]
+    turn_back(proj_out, 0, dq_ref[...] + dq_back[...].astype(F32), cos_table, sin_table)
+    total = dkv_refs[0][...]
+    for ref in dkv_refs[1:]:
+        total = total + ref[...].astype(F32)
+    dkv[...] = total
+    turn_back(proj_out, width, dkv[:width, :], cos_table, sin_table)
+    proj_out[2 * width :, :] = dkv[width:, :].astype(BF16)
+    grad[...] = mm(proj_out[...], w_ref[...], TN)
+
+    def gains(i, carry):
+        at = pl.ds(i * STRIP, STRIP)
+        unit, unused = normed(x_ref[at, :].astype(F32))
+        product = grad[at, :] * unit
+        return carry + jnp.sum(product.reshape(STRIP // 8, 8, -1), axis=0)
+
+    gain = lax.fori_loop(0, rows // STRIP, gains, jnp.zeros((8, model), F32))
+    first = lax.broadcasted_iota(jnp.int32, (16, model), 0) == 0
+    gain = jnp.where(first, jnp.sum(gain, axis=0, keepdims=True), 0.0)
+    for k in range(n_tp):
+        at = pl.ds(pl.multiple_of((tp ^ k) * part, part), part)
+        part_refs[k][:part, :] = grad[at, :].astype(part_refs[k].dtype)
+        part_refs[k][part:, :] = gain.astype(part_refs[k].dtype)
+
+
+def unproject(n_tp, tokens, qkv_t, cos_table, sin_table, dq, dq_back, dkvs):
+    rows, model = tokens.shape
+    part = rows // n_tp
+    count = len(dkvs)
+    return pl.pallas_call(
+        functools.partial(unproject_kernel, count, n_tp),
+        out_shape=(shaped((qkv_t.shape[0], rows), BF16), shaped((part + 16, model), F32))
+        + (shaped((part + 16, model), BF16),) * (n_tp - 1),
+        in_specs=[VMEM] * (6 + count),
+        out_specs=(VMEM,) * (1 + n_tp),
+        scratch_shapes=[pltpu.VMEM((rows, model), F32), pltpu.VMEM(dkvs[0].shape, F32)],
+        compiler_params=params(40),
+    )(tokens, qkv_t, cos_table, sin_table, dq, dq_back, *dkvs)
+
+
+def input_kernel(n_tp, x_ref, gain_ref, grad_ref, gain_two_ref, *refs):
+    arrived = refs[:n_tp]
+    out_ref, gain_out = refs[n_tp:]
+    part, model = grad_ref.shape
+    tp = lax.axis_index("tp")
+    at = pl.ds(pl.multiple_of(tp * part, part), part)
+    total = arrived[0][...]
+    for ref in arrived[1:]:
+        total = total + ref[...].astype(F32)
+    unit, scale = normed(x_ref[at, :].astype(F32))
+    value = grad_ref[...] + norm_back(unit, scale, total[:part], gain_ref[...])
+    out_ref[...] = value.astype(BF16)
+    line = lax.broadcasted_iota(jnp.int32, (8, model), 0)
+    gain_two = jnp.sum(gain_two_ref[...], axis=0, keepdims=True)
+    gain_out[...] = jnp.where(
+        line == 0, total[part : part + 8], jnp.where(line == 1, gain_two, 0.0)
+    )
+
+
+def input_side(tokens, gain, middle_grad, gain_two_part, arrived):
+    part, model = middle_grad.shape
+    return pl.pallas_call(
+        functools.partial(input_kernel, len(arrived)),
+        out_shape=(shaped((part, model), BF16), shaped((8, model), F32)),
+        in_specs=[VMEM] * (4 + len(arrived)),
+        out_specs=(VMEM, VMEM),
+        compiler_params=params(16),
+    )(tokens, gain, middle_grad, gain_two_part, *arrived)
+
+
+def sum_over_seq(value, n_seq, me):
+    rows, columns = value.shape
+    count = n_seq // 2
+    half = columns // 2
+    core = me % 2
+    chip = me // 2
+    low = value.astype(BF16)
+    pick = lambda x, c: lax.dynamic_slice_in_dim(x, c * half, half, 1)
+    mine = pick(value, core) + swap(pick(low, 1 - core), "seq", 1, n_seq).astype(F32)
+    if rows % count:
+        total = mine
+        for k in range(1, count):
+            total = total + swap(mine.astype(BF16), "seq", 2 * k, n_seq).astype(F32)
+        held = total.astype(BF16)
+    else:
+        piece = rows // count
+        parts = mine.reshape(count, piece, half)
+        low = mine.astype(BF16).reshape(count, piece, half)
+        total = lax.dynamic_index_in_dim(parts, chip, 0, keepdims=False)
+        for k in range(1, count):
+            sent = lax.dynamic_index_in_dim(low, chip ^ k, 0, keepdims=False)
+            total = total + swap(sent, "seq", 2 * k, n_seq).astype(F32)
+        total = total.astype(BF16)
+        held = jnp.zeros((count, piece, half), BF16)
+        for k in range(count):
+            sent = swap(total, "seq", 2 * k, n_seq) if k else total
+            held = lax.dynamic_update_slice_in_dim(held, sent[None], chip ^ k, 0)
+        held = held.reshape(rows, half)
+    other = swap(held, "seq", 1, n_seq)
+    left = jnp.where(core == 0, held, other)
+    right = jnp.where(core == 0, other, held)
+    return jnp.concatenate([left, right], axis=1).astype(F32)
 
 
 def body(
@@ -295,87 +649,45 @@
 ):
     rows, model = tokens.shape
     width = w_qkv.shape[2]
-    heads = width // HDIM
     units = w_in.shape[2]
-    part_rows = rows // n_tp
     count = n_seq // 2
     me = lax.axis_index("seq")
-    tp = lax.axis_index("tp")
     qkv_t = w_qkv.transpose(1, 2, 0).reshape(3 * width, model)
     in_t = w_in.transpose(1, 2, 0).reshape(2 * units, model)
-
-    def own_part(x, hop=0):
-        return lax.dynamic_slice_in_dim(x, (tp ^ hop) * part_rows, part_rows, 0)
-
-    cos_table, sin_table = own_tables(doc_lengths, roster, me, rows)
-    inputs = tokens.astype(F32)
-    unit_one, scale_one = normed(inputs)
-    h_one = (unit_one * gain_one).astype(BF16)
-    projected = mm(qkv_t, h_one, NT)
-    queries = rotate(projected[:width], cos_table, sin_table).astype(BF16)
-    queries = queries * jnp.asarray(HDIM**-0.5, BF16)
-    keys = rotate(projected[width : 2 * width], cos_table, sin_table).astype(BF16)
-    kv = jnp.concatenate([keys, projected[2 * width :].astype(BF16)], axis=0)
-    blocks = [kv] + [swap(kv, "seq", 2 * j, n_seq) for j in range(1, count)]
-    q_pair = swap(queries, "seq", 1, n_seq)
-    w_outs = [w_out] + [swap(w_out, "tp", k, n_tp) for k in range(1, n_tp)]
+    gain_one = gain_one[None]
+    gain_two = gain_two[None]
+    over_tp = lambda x, k: swap(x, "tp", k, n_tp)
+    over_chips = lambda x, k: swap(x, "seq", 2 * k, n_seq)
+    over_cores = lambda x: swap(x, "seq", 1, n_seq)
+
+    queries, kv, h_one, cos_table, sin_table = project(
+        doc_lengths, roster, tokens, gain_one, qkv_t
+    )
+    blocks = [kv] + [over_chips(kv, j) for j in range(1, count)]
+    q_pair = over_cores(queries)
+    w_outs = [w_out] + [over_tp(w_out, k) for k in range(1, n_tp)]
 
     state_own, state_pair = attention_forward(doc_lengths, roster, queries, q_pair, blocks)
-    state_back = swap(state_pair, "seq", 1, n_seq)
-    top = jnp.maximum(state_own[:, 72:73], state_back[:, 72:73])
-    fade_own = jnp.exp(state_own[:, 72:73] - top)
-    fade_back = jnp.exp(state_back[:, 72:73] - top)
-    mixed_state = state_own[:, :72] * fade_own + state_back[:, :72] * fade_back
-    total = mixed_state[:, 64:65]
-    log_total = top + jnp.log(total)
-    out_b = (mixed_state[:, :64] / total).astype(BF16).reshape(width, rows)
-    outs = [out_b] + [swap(out_b, "tp", k, n_tp) for k in range(1, n_tp)]
-    out_pair = swap(out_b, "seq", 1, n_seq)
-    totals = jnp.broadcast_to(log_total, (heads, 8, rows))
-    totals_pair = swap(totals, "seq", 1, n_seq)
-
-    middle = inputs
-    for out, weight in zip(outs, w_outs):
-        middle = middle + mm(out, weight, TN)
-    unit_two, scale_two = normed(middle)
-    h_two = (unit_two * gain_two).astype(BF16)
-    gate_up = mm(in_t, h_two, NT)
-    gate, up = gate_up[:units], gate_up[units:]
-    erf_part = 0.5 * (1.0 + lax.erf(gate * (2.0**-0.5)))
-    activated = gate * erf_part
-    slope = erf_part + gate * jnp.exp(-0.5 * gate * gate) * ((2.0 * jnp.pi) ** -0.5)
-    mixed = (activated * up).astype(BF16)
-    mixed_grad = mm(w_down, cotangent, NT)
-    gate_grad = jnp.concatenate(
-        [mixed_grad * up * slope, mixed_grad * activated], axis=0
-    ).astype(BF16)
-    h_two_grad = mm(gate_grad, in_t, TN)
-    gain_two_part = jnp.sum(h_two_grad * unit_two, axis=0, keepdims=True)
-    h_two_low = h_two_grad.astype(BF16)
-    arrived = own_part(h_two_grad)
-    for k in range(1, n_tp):
-        arrived = arrived + swap(own_part(h_two_low, k), "tp", k, n_tp).astype(F32)
-
-    branch_two = mm(mixed, w_down, TN).astype(BF16)
-    grad_down = mm(mixed, cotangent, NN)
-    grad_in = mm(gate_grad, h_two, NN)
-
-    middle_part = own_part(middle)
-    unit_part, scale_part = normed(middle_part)
-    middle_grad = own_part(cotangent).astype(F32) + norm_back(
-        unit_part, scale_part, arrived, gain_two
+    out_b, totals = join(state_own, over_cores(state_pair))
+    outs = [out_b] + [over_tp(out_b, k) for k in range(1, n_tp)]
+    out_pair = over_cores(out_b)
+    totals_pair = over_cores(totals)
+
+    middle, h_two, mixed, gate_grad, gain_two_part, *parts = feed(
+        tokens, cotangent, gain_two, in_t, w_down, outs, w_outs
     )
-    branch_grad = middle_grad.astype(BF16)
-    pieces = [mm(branch_grad, w_outs[0], NT).astype(BF16)] + [
-        swap(mm(branch_grad, w_outs[k], NT).astype(BF16), "tp", k, n_tp) for k in range(1, n_tp)
-    ]
-    out_grad = jnp.zeros((rows, width), BF16)
-    for k in range(n_tp):
-        out_grad = lax.dynamic_update_slice_in_dim(out_grad, pieces[k], (tp ^ k) * part_rows, 0)
-    out_grad = out_grad.T
-    grad_pair = swap(out_grad, "seq", 1, n_seq)
-
-    results = attention_backward(
+    arrived = [parts[0]] + [over_tp(parts[k], k) for k in range(1, n_tp)]
+    middle_grad, branch_grad, *pieces = branch(middle, cotangent, gain_two, arrived, w_outs)
+    out_grad = lay_turned([pieces[0]] + [over_tp(pieces[k], k) for k in range(1, n_tp)])
+    grad_pair = over_cores(out_grad)
+
+    grad_down = mm(mixed, cotangent, NN).astype(BF16)
+    grad_in = mm(gate_grad, h_two, NN).astype(BF16)
+    branch_full = stack_parts([branch_grad] + [over_tp(branch_grad, k) for k in range(1, n_tp)])
+    grad_out = mm(out_b, branch_full, NN).astype(BF16)
+    early = lax.psum((grad_down, grad_in, grad_out), "seq")
+
+    dq_own, dq_pair, *dkvs = attention_backward(
         doc_lengths,
         roster,
         (queries, q_pair),
@@ -384,57 +696,45 @@
         (totals, totals_pair),
         blocks,
     )
-    dq_own, dq_pair = results[:2]
-    dkv = results[2]
-    for j in range(1, count):
-        dkv = dkv + swap(results[2 + j], "seq", 2 * j, n_seq).astype(F32)
-    dq = dq_own + swap(dq_pair, "seq", 1, n_seq).astype(F32)
-
-    branch_full = jnp.zeros((rows, model), BF16)
-    for k in range(n_tp):
-        piece = swap(branch_grad, "tp", k, n_tp) if k else branch_grad
-        branch_full = lax.dynamic_update_slice_in_dim(branch_full, piece, (tp ^ k) * part_rows, 0)
-    grad_out = mm(out_b, branch_full, NN)
-
-    proj_grad = jnp.concatenate(
-        [
-            rotate_back(dq, cos_table, sin_table),
-            rotate_back(dkv[:width], cos_table, sin_table),
-            dkv[width:],
-        ],
-        axis=0,
-    ).astype(BF16)
-    h_one_grad = mm(proj_grad, qkv_t, TN)
-    gain_one_part = jnp.sum(h_one_grad * unit_one, axis=0, keepdims=True)
-    h_one_low = h_one_grad.astype(BF16)
-    arrived = own_part(h_one_grad)
+    dkvs = [dkvs[0]] + [over_chips(dkvs[j], j) for j in range(1, count)]
+
+    mixed_late, unused = lax.optimization_barrier((mixed, dq_pair))
+    branch_two = mm(mixed_late, w_down, TN)
+    tp = lax.axis_index("tp")
+    part = rows // n_tp
+    own = lambda x, k: lax.dynamic_slice_in_dim(x, (tp ^ k) * part, part, 0)
+    total = own(middle, 0) + own(branch_two, 0)
+    low = branch_two.astype(BF16)
     for k in range(1, n_tp):
-        arrived = arrived + swap(own_part(h_one_low, k), "tp", k, n_tp).astype(F32)
-    unit_part, scale_part = normed(own_part(tokens).astype(F32))
-    input_part = (middle_grad + norm_back(unit_part, scale_part, arrived, gain_one)).astype(BF16)
-    input_grad = jnp.zeros((rows, model), BF16)
-    for k in range(n_tp):
-        piece = swap(input_part, "tp", k, n_tp) if k else input_part
-        input_grad = lax.dynamic_update_slice_in_dim(input_grad, piece, (tp ^ k) * part_rows, 0)
-    grad_qkv = mm(proj_grad, h_one, NN)
-
-    layer_out = (middle + lax.psum(branch_two, "tp").astype(F32)).astype(BF16)
-    low = lambda x: x.astype(BF16)
-    gains = jnp.concatenate([gain_one_part, gain_two_part], axis=0)
-    early = lax.psum((low(grad_down), low(grad_in)), "seq")
-    late = lax.psum((low(grad_out), low(grad_qkv)), "seq")
-    gains = lax.psum(gains, ("seq", "tp"))
-    f = lambda x: x.astype(F32)
-    back = lambda x, n: f(x).reshape(-1, n, model).transpose(2, 0, 1)
+        total = total + over_tp(own(low, k), k).astype(F32)
+    total = total.astype(BF16)
+    layer_out = stack_parts([total] + [over_tp(total, k) for k in range(1, n_tp)])
+
+    proj_grad, *parts = unproject(
+        n_tp, tokens, qkv_t, cos_table, sin_table, dq_own, over_cores(dq_pair), dkvs
+    )
+    arrived = [parts[0]] + [over_tp(parts[k], k) for k in range(1, n_tp)]
+    input_part, gains = input_side(tokens, gain_one, middle_grad, gain_two_part, arrived)
+    input_grad = stack_parts([input_part] + [over_tp(input_part, k) for k in range(1, n_tp)])
+    grad_qkv = sum_over_seq(mm(proj_grad, h_one, NN), n_seq, me)
+    chip_gains = gains + over_cores(gains)
+    gains = chip_gains
+    for k in range(1, count):
+        gains = gains + over_chips(chip_gains, k)
+    gain_two_sum = gains[1]
+    for k in range(1, n_tp):
+        gain_two_sum = gain_two_sum + over_tp(gains[1], k)
+
+    back = lambda x, n: x.reshape(-1, n, model).transpose(2, 0, 1)
     return (
         layer_out,
         input_grad,
         gains[0],
-        back(late[1], width),
-        f(late[0]),
-        gains[1],
-        back(early[1], units),
-        f(early[0]),
+        back(grad_qkv, width),
+        early[2].astype(F32),
+        gain_two_sum,
+        back(early[1].astype(F32), units),
+        early[0].astype(F32),
     )
 
 

time: 304 us -> 265 us (0.87)
  blocking collectives: 37.9 us -> 0 us
  matrix products: 28.3 us -> 6.18 us
  Pallas kernels: 14.6 us -> 35.9 us
  starting transfers between devices: 63.4 us -> 81.7 us
  other arithmetic: 18.4 us -> 8.78 us
  waiting for transfers between devices: 111 us -> 107 us
    psum x1 -> x0, blocking collectives: 37.9 us -> none  [body(): gains = lax.psum(gains, ('seq', 'tp'))]
    psum x2 -> x1, waiting for transfers between devices: 37.3 us -> 0.01 us  [body(): early = lax.psum((grad_down, grad_in, grad_out), 'seq')]
    ppermute x33 -> x54, waiting for transfers between devices: 73.5 us -> 107 us  [swap(): return lax.ppermute(x, axis, [(i, i ^ hop) for i in range(count)])]
    dot_general x18 -> x5, matrix products: 28.3 us -> 6.18 us  [mm(): return lax.dot_general(a, b, dims, preferred_element_type=F32)]
    ppermute x33 -> x54, starting transfers between devices: 63.1 us -> 81.6 us  [swap(): return lax.ppermute(x, axis, [(i, i ^ hop) for i in range(count)])]
    pallas_call x0 -> x10, Pallas kernels: none -> 14.5 us  [the longest x1 4.72 us: feed(): pl.pallas_call(functools.partial(feed_kernel, n_tp), out_shape=(shaped((r...]
    reduce_sum x10 -> x0, other arithmetic: 5.88 us -> none  [the longest x4 2.14 us: normed(): spread = jnp.mean(shifted * shifted, axis=-1, keepdims=True)]
    dynamic_update_slice x10 -> x3, local copies, waits for them, and re-layouts: 4.67 us -> 0.06 us  [sum_over_seq(): held = lax.dynamic_update_slice_in_dim(held, sent[None], chip ^ k, 0)]
  transfers between devices with their start and end apart: 35 -> 55, of which waited for: 15 -> 21; matrix products, arithmetic and copies ran while one was open for 9% -> 5% of each run, Pallas kernels for 2% -> 6%
where the time goes in v2:
time: 265 us
  waiting for transfers between devices  107 us (40%)
  starting transfers between devices  81.7 us (31%)
  Pallas kernels  35.9 us (14%)
  between operations  14.6 us (6%)
  local copies, waits for them, and re-layouts  10.7 us (4%)
  other arithmetic  8.78 us (3%)
  matrix products  6.18 us (2%)
    ppermute x54, waiting for transfers between devices, swap(): return lax.ppermute(x, axis, [(i, i ^ hop) for i in range(count)])  107 us
    ppermute x54, starting transfers between devices, swap(): return lax.ppermute(x, axis, [(i, i ^ hop) for i in range(count)])  81.6 us
    pallas_call x1, Pallas kernels, attention_backward(): pl.pallas_call(functools.partial(backward_kernel, count, heads), out_shap...  12 us
    pallas_call x1, Pallas kernels, attention_forward(): pl.pallas_call(functools.partial(forward_kernel, count, heads), out_shape...  9.41 us
    unnamed x78, local copies, waits for them, and re-layouts  8.43 us
    dot_general x5, matrix products, mm(): return lax.dot_general(a, b, dims, preferred_element_type=F32)  6.18 us
  transfers between devices with their start and end apart: 55, of which 21 were waited for; matrix products, arithmetic and copies ran while one was open for 5% of the time, Pallas kernels for 6%

profile of v2, /device:TPU:0, one launch (start us, length us, event | category | flops | bytes accessed | tf_op | source)
XLA Modules:
  0.0 264.8 jit_solution(16387677997941943522)
XLA Ops:
  11.5 2.7 %shard_map.161 = (bf16[192,448]{1,0:T(8,128)(2,1)S(1)}, bf16[384,448]{1,0:T(8,128)(2,1)S(1)}, bf16[448,768]{1,0:T(8,128)(2,1)S(1)}, f32[32,448]{1,0:T(8,128)S(1)}, f32[32,448]{1,0:T(8,128)S(1)}) custom-call(s32[4]{0:T(128)S(1)} %copy-done.26, s32[8]{0:T(128)S(1)} %copy-done.27, bf16[448,768]{1,0:T(8,128)(2,1)S(1)} %copy-done, ...), custom_call_target="tpu_custom_call" | custom-call | tf_op jit(solution)/shard_map/pallas_call | solution.py:148
  15.1 3.0 %collective-permute-start.1 = (bf16[384,448]{1,0:T(8,128)(2,1)S(1)}, bf16[384,448]{1,0:T(8,128)(2,1)S(1)}, u32[]{:S(2)}, u32[]{:S(2)}) collective-permute-start(bf16[384,448]{1,0:T(8,128)(2,1)S(1)} %get-tuple-element.47.refs_0_.refs_8_), channel_id=1, source_target_pairs={{0,8},{4,12},{8,0},{12,4},{16,24},{20,28},{24,16},{28,20},{1,9},{5... | collective-permute-start | bytes 1032200 | tf_op jit(solution)/shard_map/ppermute | solution.py:41
  21.1 7.0 %collective-permute-done.1.refs_1_.refs_9_ = bf16[384,448]{1,0:T(8,128)(2,1)S(1)} collective-permute-done((bf16[384,448]{1,0:T(8,128)(2,1)S(1)}, bf16[384,448]{1,0:T(8,128)(2,1)S(1)}, u32[]{:S(2)}, u32[]{:S(2)}) %collective-permute-start.1) | collective-permute-done | bytes 344096 | tf_op jit(solution)/shard_map/ppermute | solution.py:41
  28.1 9.1 %collective-permute-done.2.refs_2_.refs_10_ = bf16[384,448]{1,0:T(8,128)(2,1)S(1)} collective-permute-done((bf16[384,448]{1,0:T(8,128)(2,1)S(1)}, bf16[384,448]{1,0:T(8,128)(2,1)S(1)}, u32[]{:S(2)}, u32[]{:S(2)}) %collective-permute-start.2) | collective-permute-done | bytes 344096 | tf_op jit(solution)/shard_map/ppermute | solution.py:41
  38.6 9.4 %shard_map.162 = (f32[3,80,448]{2,1,0:T(8,128)}, f32[3,80,448]{2,1,0:T(8,128)}) custom-call(s32[4]{0:T(128)} %len_ref.5, s32[8]{0:T(128)} %roster_ref.5, bf16[192,448]{1,0:T(8,128)(2,1)} %copy-done.15, bf16[192,448]{1,0:T(8,128)(2,1)} %copy-done.35, bf16[384,448]{1,0:T(8,128)(2,1)} %copy-done.8, bf16[384,448]{1,0:T(8,128)(2,1)} %copy-done.32, ...), custom_call_target="tpu_custom_call" | custom-call | tf_op jit(solution)/shard_map/pallas_call | solution.py:223
  49.8 2.6 collective-permute-start.9
  54.9 3.5 %collective-permute-start.6 = (bf16[192,448]{1,0:T(8,128)(2,1)S(1)}, bf16[192,448]{1,0:T(8,128)(2,1)S(1)}, u32[]{:S(2)}, u32[]{:S(2)}) collective-permute-start(bf16[192,448]{1,0:T(8,128)(2,1)S(1)} %get-tuple-element.50.refs_0_.refs_4_), channel_id=1, source_target_pairs={{0,2},{1,3},{2,0},{3,1},{4,6},{5,7},{6,4},{7,5},{8,10},{9,11},{10,... | collective-permute-start | bytes 516104 | tf_op jit(solution)/shard_map/ppermute | solution.py:41
  58.4 5.4 %collective-permute-done.8.refs_5_ = bf16[192,768]{1,0:T(8,128)(2,1)S(1)} collective-permute-done((bf16[192,768]{1,0:T(8,128)(2,1)S(1)}, bf16[192,768]{1,0:T(8,128)(2,1)S(1)}, u32[]{:S(2)}, u32[]{:S(2)}) %collective-permute-start.8) | collective-permute-done | bytes 294944 | tf_op jit(solution)/shard_map/ppermute | solution.py:41
  63.9 2.8 %collective-permute-start.7 = (bf16[192,448]{1,0:T(8,128)(2,1)S(1)}, bf16[192,448]{1,0:T(8,128)(2,1)S(1)}, u32[]{:S(2)}, u32[]{:S(2)}) collective-permute-start(bf16[192,448]{1,0:T(8,128)(2,1)S(1)} %get-tuple-element.50.refs_0_.refs_4_), channel_id=1, source_target_pairs={{0,3},{1,2},{2,1},{3,0},{4,7},{5,6},{6,5},{7,4},{8,11},{9,10},{10,... | collective-permute-start | bytes 516104 | tf_op jit(solution)/shard_map/ppermute | solution.py:41
  66.7 6.6 %collective-permute-done.9.refs_6_ = bf16[192,768]{1,0:T(8,128)(2,1)S(1)} collective-permute-done((bf16[192,768]{1,0:T(8,128)(2,1)S(1)}, bf16[192,768]{1,0:T(8,128)(2,1)S(1)}, u32[]{:S(2)}, u32[]{:S(2)}) %collective-permute-start.9) | collective-permute-done | bytes 294944 | tf_op jit(solution)/shard_map/ppermute | solution.py:41
  74.4 17.8 %collective-permute-done.6.refs_2_ = bf16[192,448]{1,0:T(8,128)(2,1)S(1)} collective-permute-done((bf16[192,448]{1,0:T(8,128)(2,1)S(1)}, bf16[192,448]{1,0:T(8,128)(2,1)S(1)}, u32[]{:S(2)}, u32[]{:S(2)}) %collective-permute-start.6) | collective-permute-done | bytes 172064 | tf_op jit(solution)/shard_map/ppermute | solution.py:41
  92.2 4.7 %shard_map.164 = (f32[448,768]{1,0:T(8,128)S(1)}, bf16[448,768]{1,0:T(8,128)(2,1)S(1)}, bf16[288,448]{1,0:T(8,128)(2,1)S(1)}, bf16[576,448]{1,0:T(8,128)(2,1)S(1...) custom-call(bf16[448,768]{1,0:T(8,128)(2,1)S(1)} %copy-done.1, ...), custom_call_target="tpu_custom_call" | custom-call | tf_op jit(solution)/shard_map/pallas_call | solution.py:412
  97.0 4.1 %collective-permute-start.11 = (bf16[112,768]{1,0:T(8,128)(2,1)S(1)}, bf16[112,768]{1,0:T(8,128)(2,1)S(1)}, u32[]{:S(2)}, u32[]{:S(2)}) collective-permute-start(bf16[112,768]{1,0:T(8,128)(2,1)S(1)} %get-tuple-element.54), channel_id=1, source_target_pairs={{0,1},{1,0},{2,3},{3,2},{4,5},{5,4},{6,7},{7,6},{8,9},{9,8},{10,11... | collective-permute-start | bytes 516104 | tf_op jit(solution)/shard_map/ppermute | solution.py:41
  103.5 3.6 %collective-permute-done.11.refs_1_ = bf16[112,768]{1,0:T(8,128)(2,1)S(1)} collective-permute-done((bf16[112,768]{1,0:T(8,128)(2,1)S(1)}, bf16[112,768]{1,0:T(8,128)(2,1)S(1)}, u32[]{:S(2)}, u32[]{:S(2)}) %collective-permute-start.11) | collective-permute-done | bytes 172064 | tf_op jit(solution)/shard_map/ppermute | solution.py:41
  107.1 9.4 %collective-permute-done.12.refs_2_ = bf16[112,768]{1,0:T(8,128)(2,1)S(1)} collective-permute-done((bf16[112,768]{1,0:T(8,128)(2,1)S(1)}, bf16[112,768]{1,0:T(8,128)(2,1)S(1)}, u32[]{:S(2)}, u32[]{:S(2)}) %collective-permute-start.12) | collective-permute-done | bytes 172064 | tf_op jit(solution)/shard_map/ppermute | solution.py:41
  123.6 3.5 %collective-permute-done.15.refs_2_ = bf16[112,192]{1,0:T(8,128)(2,1)S(1)} collective-permute-done((bf16[112,192]{1,0:T(8,128)(2,1)S(1)}, bf16[112,192]{1,0:T(8,128)(2,1)S(1)}, u32[]{:S(2)}, u32[]{:S(2)}) %collective-permute-start.15) | collective-permute-done | bytes 43040 | tf_op jit(solution)/shard_map/ppermute | solution.py:41
  131.7 12.0 %shard_map.167 = (f32[192,448]{1,0:T(8,128)}, bf16[192,448]{1,0:T(8,128)(2,1)}, f32[384,448]{1,0:T(8,128)}, bf16[384,448]{1,0:T(8,128)(2,1)}, bf16[384,448]{1,0:T(8,128)(2,1)}, /*index=5*/bf16[384,448]{1,0:T(8,128)(2,1)}) custom-call(s32[4]{0:T(128)} %len_ref.5, s32[8]{0:T(128)} %roster_ref.5, bf16[192,448]{1,0:T(8,128)(2,1)} %copy-done.15, ...), custom_call_target="tpu_custom_call" | custom-call | tf_op jit(solution)/shard_map/pallas_call | solution.py:306
  143.7 3.9 %collective-permute-start.27 = (bf16[384,448]{1,0:T(8,128)(2,1)}, bf16[384,448]{1,0:T(8,128)(2,1)S(1)}, u32[]{:S(2)}, u32[]{:S(2)}) collective-permute-start(bf16[384,448]{1,0:T(8,128)(2,1)} %get-tuple-element.70), channel_id=1, source_target_pairs={{0,8},{4,12},{8,0},{12,4},{16,24},{20,28},{24,16},{28,20},{1,9},{5... | collective-permute-start | bytes 1032200 | tf_op jit(solution)/shard_map/ppermute | solution.py:41
  147.5 4.8 %collective-permute-start.28 = (bf16[384,448]{1,0:T(8,128)(2,1)}, bf16[384,448]{1,0:T(8,128)(2,1)S(1)}, u32[]{:S(2)}, u32[]{:S(2)}) collective-permute-start(bf16[384,448]{1,0:T(8,128)(2,1)} %get-tuple-element.71), channel_id=1, source_target_pairs={{0,16},{4,20},{8,24},{12,28},{16,0},{20,4},{24,8},{28,12},{1,17},{... | collective-permute-start | bytes 1032200 | tf_op jit(solution)/shard_map/ppermute | solution.py:41
  152.3 2.8 %convolution_convert_fusion = bf16[576,768]{1,0:T(8,128)(2,1)} fusion(bf16[576,448]{1,0:T(8,128)(2,1)} %copy-done.29, bf16[448,768]{1,0:T(8,128)(2,1)} %copy-done.28), kind=kOutput, calls=%fused_computation.1 | convolution fusion | flops 396804096 | bytes 2088960 | tf_op jit(solution)/shard_map/dot_general | solution.py:37
  158.8 3.8 %collective-permute-done.50.refs_3_ = bf16[112,768]{1,0:T(8,128)(2,1)S(1)} collective-permute-done((bf16[112,768]{1,0:T(8,128)(2,1)S(1)}, bf16[112,768]{1,0:T(8,128)(2,1)S(1)}, u32[]{:S(2)}, u32[]{:S(2)}) %collective-permute-start.50) | collective-permute-done | bytes 172064 | tf_op jit(solution)/shard_map/ppermute | solution.py:41
  162.6 3.2 %collective-permute-done.28.refs_2_ = bf16[384,448]{1,0:T(8,128)(2,1)S(1)} collective-permute-done((bf16[384,448]{1,0:T(8,128)(2,1)}, bf16[384,448]{1,0:T(8,128)(2,1)S(1)}, u32[]{:S(2)}, u32[]{:S(2)}) %collective-permute-start.28) | collective-permute-done | bytes 344096 | tf_op jit(solution)/shard_map/ppermute | solution.py:41
  184.0 5.7 %collective-permute-done.31.refs_2_ = bf16[128,768]{1,0:T(8,128)(2,1)S(1)} collective-permute-done((bf16[128,768]{1,0:T(8,128)(2,1)S(1)}, bf16[128,768]{1,0:T(8,128)(2,1)S(1)}, u32[]{:S(2)}, u32[]{:S(2)}) %collective-permute-start.31) | collective-permute-done | bytes 196640 | tf_op jit(solution)/shard_map/ppermute | solution.py:41
  191.7 8.8 %collective-permute-start.21 = (bf16[112,768]{1,0:T(8,128)(2,1)S(1)}, bf16[112,768]{1,0:T(8,128)(2,1)S(1)}, u32[]{:S(2)}, u32[]{:S(2)}) collective-permute-start(bf16[112,768]{1,0:T(8,128)(2,1)S(1)} %get-tuple-element.97), channel_id=1, source_target_pairs={{0,2},{1,3},{2,0},{3,1},{4,6},{5,7},{6,4},{7,5},{8,10},{9,11},{10,... | collective-permute-start | bytes 516104 | tf_op jit(solution)/shard_map/ppermute | solution.py:41
  202.8 5.2 %collective-permute-done.21 = bf16[112,768]{1,0:T(8,128)(2,1)S(1)} collective-permute-done((bf16[112,768]{1,0:T(8,128)(2,1)S(1)}, bf16[112,768]{1,0:T(8,128)(2,1)S(1)}, u32[]{:S(2)}, u32[]{:S(2)}) %collective-permute-start.21) | collective-permute-done | bytes 172064 | tf_op jit(solution)/shard_map/ppermute | solution.py:41
  214.4 4.1 %collective-permute-done.45 = bf16[144,384]{1,0:T(8,128)(2,1)S(1)} collective-permute-done((bf16[144,384]{1,0:T(8,128)(2,1)S(1)}, bf16[144,384]{1,0:T(8,128)(2,1)S(1)}, u32[]{:S(2)}, u32[]{:S(2)}) %collective-permute-start.45) | collective-permute-done | bytes 110624 | tf_op jit(solution)/shard_map/ppermute | solution.py:41
  220.2 4.2 %collective-permute-done.46 = bf16[144,384]{1,0:T(8,128)(2,1)S(1)} collective-permute-done((bf16[144,384]{1,0:T(8,128)(2,1)S(1)}, bf16[144,384]{1,0:T(8,128)(2,1)S(1)}, u32[]{:S(2)}, u32[]{:S(2)}) %collective-permute-start.46) | collective-permute-done | bytes 110624 | tf_op jit(solution)/shard_map/ppermute | solution.py:41
  224.7 3.8 %collective-permute-start.25 = (bf16[112,768]{1,0:T(8,128)(2,1)S(1)}, bf16[112,768]{1,0:T(8,128)(2,1)S(1)}, u32[]{:S(2)}, u32[]{:S(2)}) collective-permute-start(bf16[112,768]{1,0:T(8,128)(2,1)S(1)} %add_convert_fusion.refs_0_), channel_id=1, source_target_pairs={{0,3},{1,2},{2,1},{3,0},{4,7},{5,6},{6,5},{7,4},{8,11},{9,10},{10,... | collective-permute-start | bytes 516104 | tf_op jit(solution)/shard_map/ppermute | solution.py:41
  229.2 3.2 %collective-permute-start.53 = (f32[768]{0:T(1024)S(1)}, f32[768]{0:T(1024)S(1)}, u32[]{:S(2)}, u32[]{:S(2)}) collective-permute-start(f32[768]{0:T(1024)S(1)} %get-tuple-element.84), channel_id=1, source_target_pairs={{0,3},{1,2},{2,1},{3,0},{4,7},{5,6},{6,5},{7,4},{8,11},{9,10},{10,... | collective-permute-start | bytes 9224 | tf_op jit(solution)/shard_map/ppermute | solution.py:41
  235.4 2.9 %collective-permute-start.34 = (bf16[112,768]{1,0:T(8,128)(2,1)S(1)}, bf16[112,768]{1,0:T(8,128)(2,1)S(1)}, u32[]{:S(2)}, u32[]{:S(2)}) collective-permute-start(bf16[112,768]{1,0:T(8,128)(2,1)S(1)} %get-tuple-element.77.refs_0_), channel_id=1, source_target_pairs={{0,2},{1,3},{2,0},{3,1},{4,6},{5,7},{6,4},{7,5},{8,10},{9,11},{10,... | collective-permute-start | bytes 516104 | tf_op jit(solution)/shard_map/ppermute | solution.py:41
  239.5 4.3 %collective-permute-done.33.refs_1_ = bf16[112,768]{1,0:T(8,128)(2,1)S(1)} collective-permute-done((bf16[112,768]{1,0:T(8,128)(2,1)S(1)}, bf16[112,768]{1,0:T(8,128)(2,1)S(1)}, u32[]{:S(2)}, u32[]{:S(2)}) %collective-permute-start.33) | collective-permute-done | bytes 172064 | tf_op jit(solution)/shard_map/ppermute | solution.py:41
  243.8 6.4 %collective-permute-done.34.refs_2_ = bf16[112,768]{1,0:T(8,128)(2,1)S(1)} collective-permute-done((bf16[112,768]{1,0:T(8,128)(2,1)S(1)}, bf16[112,768]{1,0:T(8,128)(2,1)S(1)}, u32[]{:S(2)}, u32[]{:S(2)}) %collective-permute-start.34) | collective-permute-done | bytes 172064 | tf_op jit(solution)/shard_map/ppermute | solution.py:41
  (196 shorter events, 76.0 us)
Async XLA Ops:
  7.2 244.0 %all-reduce.3.cloned.1.call-start = ((), (), s32[]{:S(2)}) async-start(), calls=%async_computation | async-start | bytes 3244032 | tf_op jit(solution)/shard_map/psum | solution.py:688
  15.1 12.9 %collective-permute-start.1 = (bf16[384,448]{1,0:T(8,128)(2,1)S(1)}, bf16[384,448]{1,0:T(8,128)(2,1)S(1)}, u32[]{:S(2)}, u32[]{:S(2)}) collective-permute-start(bf16[384,448]{1,0:T(8,128)(2,1)S(1)} %get-tuple-element.47.refs_0_.refs_8_), channel_id=1, source_target_pairs={{0,8},{4,12},{8,0},{12,4},{16,24},{20,28},{24,16},{28,20},{1,9},{5... | collective-permute-start | bytes 1032200 | tf_op jit(solution)/shard_map/ppermute | solution.py:41
  18.1 19.0 %collective-permute-start.2 = (bf16[384,448]{1,0:T(8,128)(2,1)S(1)}, bf16[384,448]{1,0:T(8,128)(2,1)S(1)}, u32[]{:S(2)}, u32[]{:S(2)}) collective-permute-start(bf16[384,448]{1,0:T(8,128)(2,1)S(1)} %get-tuple-element.47.refs_0_.refs_8_), channel_id=1, source_target_pairs={{0,16},{4,20},{8,24},{12,28},{16,0},{20,4},{24,8},{28,12},{1,17},{... | collective-permute-start | bytes 1032200 | tf_op jit(solution)/shard_map/ppermute | solution.py:41
  19.6 17.5 %collective-permute-start.3 = (bf16[384,448]{1,0:T(8,128)(2,1)S(1)}, bf16[384,448]{1,0:T(8,128)(2,1)S(1)}, u32[]{:S(2)}, u32[]{:S(2)}) collective-permute-start(bf16[384,448]{1,0:T(8,128)(2,1)S(1)} %get-tuple-element.47.refs_0_.refs_8_), channel_id=1, source_target_pairs={{0,24},{4,28},{8,16},{12,20},{16,8},{20,12},{24,0},{28,4},{1,25},{... | collective-permute-start | bytes 1032200 | tf_op jit(solution)/shard_map/ppermute | solution.py:41
  48.1 15.7 %collective-permute-start.8 = (bf16[192,768]{1,0:T(8,128)(2,1)S(1)}, bf16[192,768]{1,0:T(8,128)(2,1)S(1)}, u32[]{:S(2)}, u32[]{:S(2)}) collective-permute-start(bf16[192,768]{1,0:T(8,128)(2,1)S(1)} %copy-done.9), channel_id=1, source_target_pairs={{0,1},{1,0},{2,3},{3,2},{4,5},{5,4},{6,7},{7,6},{8,9},{9,8},{10,11... | collective-permute-start | bytes 884744 | tf_op jit(solution)/shard_map/ppermute | solution.py:41
  49.8 23.5 %collective-permute-start.9 = (bf16[192,768]{1,0:T(8,128)(2,1)S(1)}, bf16[192,768]{1,0:T(8,128)(2,1)S(1)}, u32[]{:S(2)}, u32[]{:S(2)}) collective-permute-start(bf16[192,768]{1,0:T(8,128)(2,1)S(1)} %copy-done.9), channel_id=1, source_target_pairs={{0,2},{1,3},{2,0},{3,1},{4,6},{5,7},{6,4},{7,5},{8,10},{9,11},{10,... | collective-permute-start | bytes 884744 | tf_op jit(solution)/shard_map/ppermute | solution.py:41
  52.4 20.9 %collective-permute-start.10 = (bf16[192,768]{1,0:T(8,128)(2,1)S(1)}, bf16[192,768]{1,0:T(8,128)(2,1)S(1)}, u32[]{:S(2)}, u32[]{:S(2)}) collective-permute-start(bf16[192,768]{1,0:T(8,128)(2,1)S(1)} %copy-done.9), channel_id=1, source_target_pairs={{0,3},{1,2},{2,1},{3,0},{4,7},{5,6},{6,5},{7,4},{8,11},{9,10},{10,... | collective-permute-start | bytes 884744 | tf_op jit(solution)/shard_map/ppermute | solution.py:41
  54.3 20.1 %collective-permute-start.5 = (bf16[192,448]{1,0:T(8,128)(2,1)S(1)}, bf16[192,448]{1,0:T(8,128)(2,1)S(1)}, u32[]{:S(2)}, u32[]{:S(2)}) collective-permute-start(bf16[192,448]{1,0:T(8,128)(2,1)S(1)} %get-tuple-element.50.refs_0_.refs_4_), channel_id=1, source_target_pairs={{0,1},{1,0},{2,3},{3,2},{4,5},{5,4},{6,7},{7,6},{8,9},{9,8},{10,11... | collective-permute-start | bytes 516104 | tf_op jit(solution)/shard_map/ppermute | solution.py:41
  54.9 37.3 %collective-permute-start.6 = (bf16[192,448]{1,0:T(8,128)(2,1)S(1)}, bf16[192,448]{1,0:T(8,128)(2,1)S(1)}, u32[]{:S(2)}, u32[]{:S(2)}) collective-permute-start(bf16[192,448]{1,0:T(8,128)(2,1)S(1)} %get-tuple-element.50.refs_0_.refs_4_), channel_id=1, source_target_pairs={{0,2},{1,3},{2,0},{3,1},{4,6},{5,7},{6,4},{7,5},{8,10},{9,11},{10,... | collective-permute-start | bytes 516104 | tf_op jit(solution)/shard_map/ppermute | solution.py:41
  63.9 28.3 %collective-permute-start.7 = (bf16[192,448]{1,0:T(8,128)(2,1)S(1)}, bf16[192,448]{1,0:T(8,128)(2,1)S(1)}, u32[]{:S(2)}, u32[]{:S(2)}) collective-permute-start(bf16[192,448]{1,0:T(8,128)(2,1)S(1)} %get-tuple-element.50.refs_0_.refs_4_), channel_id=1, source_target_pairs={{0,3},{1,2},{2,1},{3,0},{4,7},{5,6},{6,5},{7,4},{8,11},{9,10},{10,... | collective-permute-start | bytes 516104 | tf_op jit(solution)/shard_map/ppermute | solution.py:41
  101.1 15.5 %collective-permute-start.12 = (bf16[112,768]{1,0:T(8,128)(2,1)S(1)}, bf16[112,768]{1,0:T(8,128)(2,1)S(1)}, u32[]{:S(2)}, u32[]{:S(2)}) collective-permute-start(bf16[112,768]{1,0:T(8,128)(2,1)S(1)} %get-tuple-element.55), channel_id=1, source_target_pairs={{0,2},{1,3},{2,0},{3,1},{4,6},{5,7},{6,4},{7,5},{8,10},{9,11},{10,... | collective-permute-start | bytes 516104 | tf_op jit(solution)/shard_map/ppermute | solution.py:41
  102.1 14.4 %collective-permute-start.13 = (bf16[112,768]{1,0:T(8,128)(2,1)S(1)}, bf16[112,768]{1,0:T(8,128)(2,1)S(1)}, u32[]{:S(2)}, u32[]{:S(2)}) collective-permute-start(bf16[112,768]{1,0:T(8,128)(2,1)S(1)} %get-tuple-element.56), channel_id=1, source_target_pairs={{0,3},{1,2},{2,1},{3,0},{4,7},{5,6},{6,5},{7,4},{8,11},{9,10},{10,... | collective-permute-start | bytes 516104 | tf_op jit(solution)/shard_map/ppermute | solution.py:41
  129.6 25.6 %collective-permute-start.48 = (bf16[112,768]{1,0:T(8,128)(2,1)}, bf16[112,768]{1,0:T(8,128)(2,1)S(1)}, u32[]{:S(2)}, u32[]{:S(2)}) collective-permute-start(bf16[112,768]{1,0:T(8,128)(2,1)} %copy-done.24), channel_id=1, source_target_pairs={{0,1},{1,0},{2,3},{3,2},{4,5},{5,4},{6,7},{7,6},{8,9},{9,8},{10,11... | collective-permute-start | bytes 516104 | tf_op jit(solution)/shard_map/ppermute | solution.py:41
  130.4 27.3 %collective-permute-start.49 = (bf16[112,768]{1,0:T(8,128)(2,1)}, bf16[112,768]{1,0:T(8,128)(2,1)S(1)}, u32[]{:S(2)}, u32[]{:S(2)}) collective-permute-start(bf16[112,768]{1,0:T(8,128)(2,1)} %copy-done.24), channel_id=1, source_target_pairs={{0,2},{1,3},{2,0},{3,1},{4,6},{5,7},{6,4},{7,5},{8,10},{9,11},{10,... | collective-permute-start | bytes 516104 | tf_op jit(solution)/shard_map/ppermute | solution.py:41
  143.7 19.0 %collective-permute-start.27 = (bf16[384,448]{1,0:T(8,128)(2,1)}, bf16[384,448]{1,0:T(8,128)(2,1)S(1)}, u32[]{:S(2)}, u32[]{:S(2)}) collective-permute-start(bf16[384,448]{1,0:T(8,128)(2,1)} %get-tuple-element.70), channel_id=1, source_target_pairs={{0,8},{4,12},{8,0},{12,4},{16,24},{20,28},{24,16},{28,20},{1,9},{5... | collective-permute-start | bytes 1032200 | tf_op jit(solution)/shard_map/ppermute | solution.py:41
  147.5 18.3 %collective-permute-start.28 = (bf16[384,448]{1,0:T(8,128)(2,1)}, bf16[384,448]{1,0:T(8,128)(2,1)S(1)}, u32[]{:S(2)}, u32[]{:S(2)}) collective-permute-start(bf16[384,448]{1,0:T(8,128)(2,1)} %get-tuple-element.71), channel_id=1, source_target_pairs={{0,16},{4,20},{8,24},{12,28},{16,0},{20,4},{24,8},{28,12},{1,17},{... | collective-permute-start | bytes 1032200 | tf_op jit(solution)/shard_map/ppermute | solution.py:41
  152.3 13.5 %collective-permute-start.29 = (bf16[384,448]{1,0:T(8,128)(2,1)}, bf16[384,448]{1,0:T(8,128)(2,1)S(1)}, u32[]{:S(2)}, u32[]{:S(2)}) collective-permute-start(bf16[384,448]{1,0:T(8,128)(2,1)} %get-tuple-element.72), channel_id=1, source_target_pairs={{0,24},{4,28},{8,16},{12,20},{16,8},{20,12},{24,0},{28,4},{1,25},{... | collective-permute-start | bytes 1032200 | tf_op jit(solution)/shard_map/ppermute | solution.py:41
  172.6 17.1 %collective-permute-start.31 = (bf16[128,768]{1,0:T(8,128)(2,1)S(1)}, bf16[128,768]{1,0:T(8,128)(2,1)S(1)}, u32[]{:S(2)}, u32[]{:S(2)}) collective-permute-start(bf16[128,768]{1,0:T(8,128)(2,1)S(1)} %get-tuple-element.75), channel_id=1, source_target_pairs={{0,2},{1,3},{2,0},{3,1},{4,6},{5,7},{6,4},{7,5},{8,10},{9,11},{10,... | collective-permute-start | bytes 589832 | tf_op jit(solution)/shard_map/ppermute | solution.py:41
  174.4 17.3 %collective-permute-start.32 = (bf16[128,768]{1,0:T(8,128)(2,1)S(1)}, bf16[128,768]{1,0:T(8,128)(2,1)S(1)}, u32[]{:S(2)}, u32[]{:S(2)}) collective-permute-start(bf16[128,768]{1,0:T(8,128)(2,1)S(1)} %get-tuple-element.76), channel_id=1, source_target_pairs={{0,3},{1,2},{2,1},{3,0},{4,7},{5,6},{6,5},{7,4},{8,11},{9,10},{10,... | collective-permute-start | bytes 589832 | tf_op jit(solution)/shard_map/ppermute | solution.py:41
  177.2 23.7 %collective-permute-start.43 = (bf16[144,384]{1,0:T(8,128)(2,1)S(1)}, bf16[144,384]{1,0:T(8,128)(2,1)S(1)}, u32[]{:S(2)}, u32[]{:S(2)}) collective-permute-start(bf16[144,384]{1,0:T(8,128)(2,1)S(1)} %get-tuple-element.99), channel_id=1, source_target_pairs={{0,24},{4,28},{8,16},{12,20},{16,8},{20,12},{24,0},{28,4},{1,25},{... | collective-permute-start | bytes 331784 | tf_op jit(solution)/shard_map/ppermute | solution.py:41
  178.8 22.2 %collective-permute-start.42 = (bf16[144,384]{1,0:T(8,128)(2,1)S(1)}, bf16[144,384]{1,0:T(8,128)(2,1)S(1)}, u32[]{:S(2)}, u32[]{:S(2)}) collective-permute-start(bf16[144,384]{1,0:T(8,128)(2,1)S(1)} %get-tuple-element.100), channel_id=1, source_target_pairs={{0,16},{4,20},{8,24},{12,28},{16,0},{20,4},{24,8},{28,12},{1,17},{... | collective-permute-start | bytes 331784 | tf_op jit(solution)/shard_map/ppermute | solution.py:41
  182.5 18.6 %collective-permute-start.41 = (bf16[144,384]{1,0:T(8,128)(2,1)S(1)}, bf16[144,384]{1,0:T(8,128)(2,1)S(1)}, u32[]{:S(2)}, u32[]{:S(2)}) collective-permute-start(bf16[144,384]{1,0:T(8,128)(2,1)S(1)} %get-tuple-element.98), channel_id=1, source_target_pairs={{0,8},{4,12},{8,0},{12,4},{16,24},{20,28},{24,16},{28,20},{1,9},{5... | collective-permute-start | bytes 331784 | tf_op jit(solution)/shard_map/ppermute | solution.py:41
  189.7 13.1 %collective-permute-start.22 = (bf16[112,768]{1,0:T(8,128)(2,1)S(1)}, bf16[112,768]{1,0:T(8,128)(2,1)S(1)}, u32[]{:S(2)}, u32[]{:S(2)}) collective-permute-start(bf16[112,768]{1,0:T(8,128)(2,1)S(1)} %get-tuple-element.96), channel_id=1, source_target_pairs={{0,3},{1,2},{2,1},{3,0},{4,7},{5,6},{6,5},{7,4},{8,11},{9,10},{10,... | collective-permute-start | bytes 516104 | tf_op jit(solution)/shard_map/ppermute | solution.py:41
  191.7 16.3 %collective-permute-start.21 = (bf16[112,768]{1,0:T(8,128)(2,1)S(1)}, bf16[112,768]{1,0:T(8,128)(2,1)S(1)}, u32[]{:S(2)}, u32[]{:S(2)}) collective-permute-start(bf16[112,768]{1,0:T(8,128)(2,1)S(1)} %get-tuple-element.97), channel_id=1, source_target_pairs={{0,2},{1,3},{2,0},{3,1},{4,6},{5,7},{6,4},{7,5},{8,10},{9,11},{10,... | collective-permute-start | bytes 516104 | tf_op jit(solution)/shard_map/ppermute | solution.py:41
  201.3 12.5 %collective-permute-start.44 = (bf16[144,384]{1,0:T(8,128)(2,1)S(1)}, bf16[144,384]{1,0:T(8,128)(2,1)S(1)}, u32[]{:S(2)}, u32[]{:S(2)}) collective-permute-start(bf16[144,384]{1,0:T(8,128)(2,1)S(1)} %get-tuple-element.90), channel_id=1, source_target_pairs={{0,8},{4,12},{8,0},{12,4},{16,24},{20,28},{24,16},{28,20},{1,9},{5... | collective-permute-start | bytes 331784 | tf_op jit(solution)/shard_map/ppermute | solution.py:41
  209.7 22.6 %collective-permute-start.23 = (bf16[112,768]{1,0:T(8,128)(2,1)S(1)}, bf16[112,768]{1,0:T(8,128)(2,1)S(1)}, u32[]{:S(2)}, u32[]{:S(2)}) collective-permute-start(bf16[112,768]{1,0:T(8,128)(2,1)S(1)} %add_convert_fusion.refs_0_), channel_id=1, source_target_pairs={{0,1},{1,0},{2,3},{3,2},{4,5},{5,4},{6,7},{7,6},{8,9},{9,8},{10,11... | collective-permute-start | bytes 516104 | tf_op jit(solution)/shard_map/ppermute | solution.py:41
  209.8 22.6 %collective-permute-start.24 = (bf16[112,768]{1,0:T(8,128)(2,1)S(1)}, bf16[112,768]{1,0:T(8,128)(2,1)S(1)}, u32[]{:S(2)}, u32[]{:S(2)}) collective-permute-start(bf16[112,768]{1,0:T(8,128)(2,1)S(1)} %add_convert_fusion.refs_0_), channel_id=1, source_target_pairs={{0,2},{1,3},{2,0},{3,1},{4,6},{5,7},{6,4},{7,5},{8,10},{9,11},{10,... | collective-permute-start | bytes 516104 | tf_op jit(solution)/shard_map/ppermute | solution.py:41
  210.7 14.0 %collective-permute-start.39 = (f32[8,768]{1,0:T(8,128)S(1)}, f32[8,768]{1,0:T(8,128)S(1)}, u32[]{:S(2)}, u32[]{:S(2)}) collective-permute-start(f32[8,768]{1,0:T(8,128)S(1)} %add.101), channel_id=1, source_target_pairs={{0,24},{4,28},{8,16},{12,20},{16,8},{20,12},{24,0},{28,4},{1,25},{... | collective-permute-start | bytes 73736 | tf_op jit(solution)/shard_map/ppermute | solution.py:41
  212.3 16.2 %collective-permute-start.38 = (f32[8,768]{1,0:T(8,128)S(1)}, f32[8,768]{1,0:T(8,128)S(1)}, u32[]{:S(2)}, u32[]{:S(2)}) collective-permute-start(f32[8,768]{1,0:T(8,128)S(1)} %add.101), channel_id=1, source_target_pairs={{0,16},{4,20},{8,24},{12,28},{16,0},{20,4},{24,8},{28,12},{1,17},{... | collective-permute-start | bytes 73736 | tf_op jit(solution)/shard_map/ppermute | solution.py:41
  228.5 28.0 %collective-permute-start.47 = (bf16[576,384]{1,0:T(8,128)(2,1)S(1)}, bf16[576,384]{1,0:T(8,128)(2,1)S(1)}, u32[]{:S(2)}, u32[]{:S(2)}) collective-permute-start(bf16[576,384]{1,0:T(8,128)(2,1)S(1)} %bitcast.54), channel_id=1, source_target_pairs={{0,4},{4,0},{8,12},{12,8},{16,20},{20,16},{24,28},{28,24},{1,5},{5... | collective-permute-start | bytes 1327112 | tf_op jit(solution)/shard_map/ppermute | solution.py:41
  235.4 14.9 %collective-permute-start.34 = (bf16[112,768]{1,0:T(8,128)(2,1)S(1)}, bf16[112,768]{1,0:T(8,128)(2,1)S(1)}, u32[]{:S(2)}, u32[]{:S(2)}) collective-permute-start(bf16[112,768]{1,0:T(8,128)(2,1)S(1)} %get-tuple-element.77.refs_0_), channel_id=1, source_target_pairs={{0,2},{1,3},{2,0},{3,1},{4,6},{5,7},{6,4},{7,5},{8,10},{9,11},{10,... | collective-permute-start | bytes 516104 | tf_op jit(solution)/shard_map/ppermute | solution.py:41
  238.2 12.0 %collective-permute-start.35 = (bf16[112,768]{1,0:T(8,128)(2,1)S(1)}, bf16[112,768]{1,0:T(8,128)(2,1)S(1)}, u32[]{:S(2)}, u32[]{:S(2)}) collective-permute-start(bf16[112,768]{1,0:T(8,128)(2,1)S(1)} %get-tuple-element.77.refs_0_), channel_id=1, source_target_pairs={{0,3},{1,2},{2,1},{3,0},{4,7},{5,6},{6,5},{7,4},{8,11},{9,10},{10,... | collective-permute-start | bytes 516104 | tf_op jit(solution)/shard_map/ppermute | solution.py:41
  (62 other events, 896.4 us)
Sparse Core Ops, SparseCore 0:
  171.1 63.3 all-reduce.2

commit v3 on v2

v3 whole, which is shorter than its diff:
```python
import functools

import jax
import jax.numpy as jnp
from jax import lax
from jax.experimental import pallas as pl
from jax.experimental.pallas import tpu as pltpu
from jax.sharding import PartitionSpec as P

HDIM = 64
HALF = HDIM // 2
EPSILON = 1e-05
ROPE_THETA = 160000.0
MASKED = -1e30
AUG = 80
STRIP = 64
F32 = jnp.float32
BF16 = jnp.bfloat16
ANY = pl.BlockSpec(memory_space=pl.ANY)
VMEM = pl.BlockSpec(memory_space=pltpu.VMEM)
SMEM = pl.BlockSpec(memory_space=pltpu.SMEM)

NN = (((1,), (0,)), ((), ()))
NT = (((1,), (1,)), ((), ()))
TN = (((0,), (0,)), ((), ()))


def params(mib):
    return pltpu.CompilerParams(vmem_limit_bytes=mib * 2**20)


def shaped(shape, dtype):
    return jax.ShapeDtypeStruct(shape, dtype)


def mm(a, b, dims):
    return lax.dot_general(a, b, dims, preferred_element_type=F32)


def waiting(kernel, given, ready):
    def inner(*refs):
        kernel(*refs[:given], *refs[given + len(ready) :])

    return inner


def swap(x, axis, hop, count):
    return lax.ppermute(x, axis, [(i, i ^ hop) for i in range(count)])


def doc_scratch(doc_lengths, roster):
    return [pltpu.SMEM(doc_lengths.shape, jnp.int32), pltpu.SMEM(roster.shape, jnp.int32)]


def fetch_docs(len_any, roster_any, len_ref, roster_ref, len_sem, roster_sem):
    one = pltpu.make_async_copy(len_any, len_ref, len_sem)
    two = pltpu.make_async_copy(roster_any, roster_ref, roster_sem)
    one.start()
    two.start()
    one.wait()
    two.wait()


def doc_bounds(len_ref):
    ends, total = [], jnp.int32(0)
    for d in range(len_ref.shape[0]):
        total = total + len_ref[d]
        ends.append(total)
    return ends


def doc_of(ends, position):
    found = jnp.int32(0)
    for end in ends:
        found = found + (end <= position).astype(jnp.int32)
    return found


def meet(ends, base_a, base_b, rows):
    low = jnp.maximum(doc_of(ends, base_a), doc_of(ends, base_b))
    high = jnp.minimum(doc_of(ends, base_a + rows - 1), doc_of(ends, base_b + rows - 1))
    return low <= high


def doc_rows(ends, base, rows):
    spot = base + lax.broadcasted_iota(jnp.int32, (16, rows), 1)
    line = lax.broadcasted_iota(jnp.int32, (16, rows), 0)
    held = jnp.zeros((16, rows), F32)
    start = jnp.int32(0)
    for d, end in enumerate(ends):
        inside = (line == d) & (spot >= start) & (spot < end)
        held = jnp.where(inside, 1.0, held)
        start = end
    return held


def ban_rows(ends, base, rows):
    line = lax.broadcasted_iota(jnp.int32, (16, rows), 0)
    held = doc_rows(ends, base, rows)
    return jnp.where((held > 0.5) | (line >= len(ends)), 0.0, MASKED)


def key_row(block, seq_index):
    return seq_index ^ (2 * block)


def place_row(ends, base, rows):
    spot = base + lax.broadcasted_iota(jnp.int32, (1, rows), 1)
    start = jnp.zeros((1, rows), jnp.int32)
    for end in ends:
        start = jnp.where(spot >= end, end, start)
    return (spot - start).astype(F32)


def normed(values):
    centre = jnp.mean(values, axis=-1, keepdims=True)
    shifted = values - centre
    spread = jnp.mean(shifted * shifted, axis=-1, keepdims=True)
    scale = lax.rsqrt(spread + EPSILON)
    return shifted * scale, scale


def norm_back(unit, scale, grad, gain):
    u = grad * gain
    mean_u = jnp.mean(u, axis=-1, keepdims=True)
    mean_un = jnp.mean(u * unit, axis=-1, keepdims=True)
    return scale * (u - mean_u - unit * mean_un)


def project_kernel(width, len_any, roster_any, x_any, w_any, gain_ref, freq_ref, *refs):
    q_out, kv_out, h_out, cos_out, sin_out = refs[:5]
    x_ref, w_ref, proj, len_ref, roster_ref, sems = refs[5:]
    rows = x_ref.shape[0]
    x_copy = pltpu.make_async_copy(x_any, x_ref, sems.at[0])
    w_copy = pltpu.make_async_copy(w_any, w_ref, sems.at[1])
    x_copy.start()
    w_copy.start()
    fetch_docs(len_any, roster_any, len_ref, roster_ref, sems.at[2], sems.at[3])
    ends = doc_bounds(len_ref)
    place = place_row(ends, roster_ref[lax.axis_index("seq")] * rows, rows)
    angles = place * freq_ref[...]
    cos_table = jnp.cos(angles)
    sin_table = jnp.sin(angles)
    cos_out[...] = cos_table
    sin_out[...] = sin_table
    x_copy.wait()

    def strip(i, carry):
        at = pl.ds(i * STRIP, STRIP)
        unit, unused = normed(x_ref[at, :].astype(F32))
        h_out[at, :] = (unit * gain_ref[...]).astype(BF16)
        return carry

    lax.fori_loop(0, rows // STRIP, strip, 0)
    w_copy.wait()
    proj[...] = mm(w_ref[...], h_out[...], NT)
    for at in range(0, 2 * width, HDIM):
        low = proj[at : at + HALF, :]
        high = proj[at + HALF : at + HDIM, :]
        turned_low = (low * cos_out[...] - high * sin_out[...]).astype(BF16)
        turned_high = (high * cos_out[...] + low * sin_out[...]).astype(BF16)
        if at < width:
            q_out[at : at + HALF, :] = (turned_low.astype(F32) * HDIM**-0.5).astype(BF16)
            q_out[at + HALF : at + HDIM, :] = (turned_high.astype(F32) * HDIM**-0.5).astype(BF16)
        else:
            kv_out[at - width : at - width + HALF, :] = turned_low
            kv_out[at - width + HALF : at - width + HDIM, :] = turned_high
    kv_out[width:, :] = proj[2 * width :, :].astype(BF16)


def project(doc_lengths, roster, tokens, gain, qkv_t):
    rows, model = tokens.shape
    width = qkv_t.shape[0] // 3
    freq = ROPE_THETA ** (-(jnp.arange(HALF).astype(F32) * (2.0 / HDIM)))
    table = shaped((HALF, rows), F32)
    return pl.pallas_call(
        functools.partial(project_kernel, width),
        out_shape=(
            shaped((width, rows), BF16),
            shaped((2 * width, rows), BF16),
            shaped((rows, model), BF16),
            table,
            table,
        ),
        in_specs=[ANY] * 4 + [VMEM] * 2,
        out_specs=(VMEM,) * 5,
        scratch_shapes=[
            pltpu.VMEM((rows, model), BF16),
            pltpu.VMEM(qkv_t.shape, BF16),
            pltpu.VMEM((3 * width, rows), F32),
        ]
        + doc_scratch(doc_lengths, roster)
        + [pltpu.SemaphoreType.DMA((4,))],
        name="project",
        compiler_params=params(24),
    )(doc_lengths, roster, tokens, qkv_t, gain, freq[:, None])


def forward_kernel(first, count, heads, last, len_any, roster_any, q_own, q_pair, *refs):
    kv_refs = refs[:count]
    refs = refs[count:]
    if first:
        state_in, refs = refs[0], refs[1:]
    outs = refs[: 2 if last else 1]
    kv, q_aug, state, len_ref, roster_ref, sems = refs[len(outs) :]
    rows = q_own.shape[1]
    width = heads * HDIM
    me = lax.axis_index("seq")
    copies = [pltpu.make_async_copy(kv_refs[j], kv.at[j], sems.at[j]) for j in range(count)]
    for copy in copies:
        copy.start()
    fetch_docs(len_any, roster_any, len_ref, roster_ref, sems.at[count], sems.at[count + 1])
    ends = doc_bounds(len_ref)
    bases = (roster_ref[me] * rows, roster_ref[me ^ 1] * rows)
    for g, q_ref in enumerate((q_own, q_pair)):
        mark = doc_rows(ends, bases[g], rows).astype(BF16)
        for h in range(heads):
            q_aug[g * heads + h, :HDIM, :] = q_ref[h * HDIM : (h + 1) * HDIM, :]
            q_aug[g * heads + h, HDIM:, :] = mark
    if first:
        state[...] = state_in[...]
    else:
        line = lax.broadcasted_iota(jnp.int32, (2 * heads, AUG, rows), 1)
        state[...] = jnp.where(line >= 72, MASKED, 0.0)
    for copy in copies:
        copy.wait()

    top = lax.broadcasted_iota(jnp.int32, (16, rows), 0) == 0
    ones = jnp.where(top, 1.0, 0.0).astype(BF16)

    def block(j, carry):
        key_base = roster_ref[key_row(j + first, me)] * rows
        ban = ban_rows(ends, key_base, rows).astype(BF16)
        for g in range(2):

            @pl.when(meet(ends, bases[g], key_base, rows))
            def _():
                for h in range(heads):
                    at = g * heads + h
                    keys = jnp.concatenate([kv[j, h * HDIM : (h + 1) * HDIM, :], ban], axis=0)
                    vals = jnp.concatenate(
                        [kv[j, width + h * HDIM : width + (h + 1) * HDIM, :], ones], axis=0
                    )
                    scores = mm(keys, q_aug[at], TN)
                    old = state[at, 72:73, :]
                    new = jnp.maximum(old, jnp.max(scores, axis=0, keepdims=True))
                    probs = jnp.exp(scores - new).astype(BF16)
                    part = mm(vals, probs, NN)
                    fade = jnp.exp(old - new)
                    state[at, :72, :] = state[at, :72, :] * fade + part[:72]
                    state[at, 72:, :] = jnp.broadcast_to(new, (8, rows))

        return carry

    lax.fori_loop(0, count, block, 0)
    if last:
        outs[0][...] = state[:heads]
        outs[1][...] = state[heads:]
    else:
        outs[0][...] = state[...]


def attention_forward(first, last, doc_lengths, roster, q_own, q_pair, blocks, state=None):
    width, rows = q_own.shape
    heads = width // HDIM
    count = len(blocks)
    half = shaped((heads, AUG, rows), F32)
    whole = shaped((2 * heads, AUG, rows), F32)
    given = () if state is None else (state,)
    return pl.pallas_call(
        functools.partial(forward_kernel, first, count, heads, last),
        out_shape=(half, half) if last else (whole,),
        in_specs=[ANY, ANY, VMEM, VMEM] + [ANY] * count + [VMEM] * len(given),
        out_specs=(VMEM, VMEM) if last else (VMEM,),
        scratch_shapes=[
            pltpu.VMEM((count, 2 * width, rows), BF16),
            pltpu.VMEM((2 * heads, AUG, rows), BF16),
            pltpu.VMEM((2 * heads, AUG, rows), F32),
        ]
        + doc_scratch(doc_lengths, roster)
        + [pltpu.SemaphoreType.DMA((count + 2,))],
        name="attention_forward",
        compiler_params=params(24 if count < 8 else 48),
    )(doc_lengths, roster, q_own, q_pair, *blocks, *given)


def backward_kernel(index, heads, more, last, len_any, roster_any, *refs):
    q_own, q_pair, g_own, g_pair, o_own, o_pair, t_own, t_pair, kv_ref = refs[:9]
    refs = refs[9:]
    if more:
        dq_in, refs = refs[0], refs[1:]
    outs = refs[: 3 if last else 2]
    kv, q_aug, delta, dq, dkv, len_ref, roster_ref, sems = refs[len(outs) :]
    rows = q_own.shape[1]
    width = heads * HDIM
    me = lax.axis_index("seq")
    copy = pltpu.make_async_copy(kv_ref, kv, sems.at[0])
    copy.start()
    fetch_docs(len_any, roster_any, len_ref, roster_ref, sems.at[1], sems.at[2])
    ends = doc_bounds(len_ref)
    bases = (roster_ref[me] * rows, roster_ref[me ^ 1] * rows)
    for g, (q_ref, g_ref, o_ref) in enumerate(((q_own, g_own, o_own), (q_pair, g_pair, o_pair))):
        mark = doc_rows(ends, bases[g], rows).astype(BF16)
        for h in range(heads):
            part = slice(h * HDIM, (h + 1) * HDIM)
            q_aug[g * heads + h, :HDIM, :] = q_ref[part, :]
            q_aug[g * heads + h, HDIM:, :] = mark
            product = g_ref[part, :].astype(F32) * o_ref[part, :].astype(F32)
            delta[g * heads + h] = jnp.broadcast_to(
                jnp.sum(product, axis=0, keepdims=True), (8, rows)
            )
    if more:
        dq[...] = dq_in[...]
    else:
        dq[...] = jnp.zeros_like(dq)
    dkv[...] = jnp.zeros_like(dkv)
    key_base = roster_ref[key_row(index, me)] * rows
    ban = ban_rows(ends, key_base, rows).astype(BF16)
    copy.wait()

    for g, (g_ref, t_ref) in enumerate(((g_own, t_own), (g_pair, t_pair))):

        @pl.when(meet(ends, bases[g], key_base, rows))
        def _():
            for h in range(heads):
                at = g * heads + h
                part = slice(h * HDIM, (h + 1) * HDIM)
                late = slice(width + h * HDIM, width + (h + 1) * HDIM)
                keys = kv[part, :]
                scores = mm(jnp.concatenate([keys, ban], axis=0), q_aug[at], TN)
                probs = jnp.exp(scores - t_ref[h, 0:1, :])
                prob_grads = mm(kv[late, :], g_ref[part, :], TN)
                score_grad = (probs * (prob_grads - delta[at, 0:1, :])).astype(BF16)
                dkv[late, :] += mm(g_ref[part, :], probs.astype(BF16), NT)
                dkv[part, :] += mm(q_aug[at, :HDIM, :], score_grad, NT)
                dq[at] += mm(keys, score_grad, NN)

    outs[0][...] = dkv[...].astype(outs[0].dtype)
    if last:
        for h in range(heads):
            part = slice(h * HDIM, (h + 1) * HDIM)
            outs[1][part, :] = dq[h] * HDIM**-0.5
            outs[2][part, :] = (dq[heads + h] * HDIM**-0.5).astype(BF16)
    else:
        outs[1][...] = dq[...]


def attention_backward(index, last, doc_lengths, roster, held, block, dq=None, ready=()):
    width, rows = held[0].shape
    heads = width // HDIM
    given = () if dq is None else (dq,)
    total = shaped((2 * heads, HDIM, rows), F32)
    if last:
        queries = (shaped((width, rows), F32), shaped((width, rows), BF16))
    else:
        queries = (total,)
    return pl.pallas_call(
        waiting(
            functools.partial(backward_kernel, index, heads, bool(given), last),
            11 + len(given),
            ready,
        ),
        out_shape=(shaped((2 * width, rows), BF16 if index else F32),) + queries,
        in_specs=[ANY, ANY] + [VMEM] * 8 + [ANY] + [VMEM] * len(given) + [ANY] * len(ready),
        out_specs=(VMEM,) * (1 + len(queries)),
        scratch_shapes=[
            pltpu.VMEM((2 * width, rows), BF16),
            pltpu.VMEM((2 * heads, AUG, rows), BF16),
            pltpu.VMEM((2 * heads, 8, rows), F32),
            pltpu.VMEM((2 * heads, HDIM, rows), F32),
            pltpu.VMEM((2 * width, rows), F32),
        ]
        + doc_scratch(doc_lengths, roster)
        + [pltpu.SemaphoreType.DMA((3,))],
        name="attention_backward",
        compiler_params=params(24),
    )(doc_lengths, roster, *held, block, *given, *ready)


def join_kernel(heads, own_ref, back_ref, out_ref, total_ref):
    rows = own_ref.shape[2]
    for h in range(heads):
        top_own = own_ref[h, 72:73, :]
        top_back = back_ref[h, 72:73, :]
        top = jnp.maximum(top_own, top_back)
        fade_own = jnp.exp(top_own - top)
        fade_back = jnp.exp(top_back - top)
        total = own_ref[h, 64:65, :] * fade_own + back_ref[h, 64:65, :] * fade_back
        share_own = fade_own / total
        share_back = fade_back / total
        value = own_ref[h, :HDIM, :] * share_own + back_ref[h, :HDIM, :] * share_back
        out_ref[h * HDIM : (h + 1) * HDIM, :] = value.astype(BF16)
        total_ref[h] = jnp.broadcast_to(top + jnp.log(total), (8, rows))


def join(own, back):
    heads, unused, rows = own.shape
    return pl.pallas_call(
        functools.partial(join_kernel, heads),
        out_shape=(shaped((heads * HDIM, rows), BF16), shaped((heads, 8, rows), F32)),
        in_specs=[VMEM, VMEM],
        out_specs=(VMEM, VMEM),
        name="join",
        compiler_params=params(16),
    )(own, back)


def feed_kernel(n_tp, x_ref, cot_ref, gain_ref, in_ref, down_ref, w_ref, *refs):
    out_refs = refs[:n_tp]
    middle_out, h_out, mixed_out, gate_out, gain_out = refs[n_tp : n_tp + 5]
    part_refs = refs[n_tp + 5 : 2 * n_tp + 5]
    outs, unit, gate_up, mixed_grad, grad = refs[2 * n_tp + 5 :]
    rows = x_ref.shape[0]
    part = rows // n_tp
    units = down_ref.shape[0]
    width = out_refs[0].shape[0]
    tp = lax.axis_index("tp")
    for k in range(n_tp):
        at = pl.ds(pl.multiple_of((tp ^ k) * width, width), width)
        outs[at, :] = out_refs[k][...]
    middle_out[...] = mm(outs[...], w_ref[...], TN)
    mixed_grad[...] = mm(down_ref[...], cot_ref[...], NT)

    def strip(i, carry):
        at = pl.ds(i * STRIP, STRIP)
        middle = middle_out[at, :] + x_ref[at, :].astype(F32)
        middle_out[at, :] = middle
        held, unused = normed(middle)
        unit[at, :] = held
        h_out[at, :] = (held * gain_ref[...]).astype(BF16)
        return carry

    lax.fori_loop(0, rows // STRIP, strip, 0)
    gate_up[...] = mm(in_ref[...], h_out[...], NT)

    def wave(i, carry):
        at = pl.ds(i * 32, 32)
        late = pl.ds(units + i * 32, 32)
        gate = gate_up[at, :]
        up = gate_up[late, :]
        back = mixed_grad[at, :]
        bell = 0.5 * (1.0 + lax.erf(gate * (2.0**-0.5)))
        active = gate * bell
        slope = bell + gate * jnp.exp(-0.5 * gate * gate) * ((2.0 * jnp.pi) ** -0.5)
        mixed_out[at, :] = (active * up).astype(BF16)
        gate_out[at, :] = (back * up * slope).astype(BF16)
        gate_out[late, :] = (back * active).astype(BF16)
        return carry

    lax.fori_loop(0, units // 32, wave, 0)
    grad[...] = mm(gate_out[...], in_ref[...], TN)

    def gains(i, carry):
        at = pl.ds(i * STRIP, STRIP)
        product = grad[at, :] * unit[at, :]
        return carry + jnp.sum(product.reshape(STRIP // 8, 8, -1), axis=0)

    gain_out[...] = lax.fori_loop(0, rows // STRIP, gains, jnp.zeros(gain_out.shape, F32))
    for k in range(n_tp):
        at = pl.ds(pl.multiple_of((tp ^ k) * part, part), part)
        part_refs[k][...] = grad[at, :].astype(part_refs[k].dtype)


def feed(tokens, cotangent, gain, in_t, w_down, w_full, outs):
    rows, model = tokens.shape
    n_tp = len(outs)
    units = w_down.shape[0]
    part = rows // n_tp
    return pl.pallas_call(
        functools.partial(feed_kernel, n_tp),
        out_shape=(
            shaped((rows, model), F32),
            shaped((rows, model), BF16),
            shaped((units, rows), BF16),
            shaped((2 * units, rows), BF16),
            shaped((8, model), F32),
            shaped((part, model), F32),
        )
        + (shaped((part, model), BF16),) * (n_tp - 1),
        in_specs=[VMEM] * (6 + n_tp),
        out_specs=(VMEM,) * (5 + n_tp),
        scratch_shapes=[
            pltpu.VMEM((n_tp * outs[0].shape[0], rows), BF16),
            pltpu.VMEM((rows, model), F32),
            pltpu.VMEM((2 * units, rows), F32),
            pltpu.VMEM((units, rows), F32),
            pltpu.VMEM((rows, model), F32),
        ],
        name="feed",
        compiler_params=params(32),
    )(tokens, cotangent, gain, in_t, w_down, w_full, *outs)


def branch_kernel(n_tp, middle_ref, cot_ref, gain_ref, w_ref, *refs):
    arrived = refs[:n_tp]
    grad_out, branch_out = refs[n_tp : n_tp + 2]
    piece_refs = refs[n_tp + 2 :]
    width = piece_refs[0].shape[1]
    part = arrived[0].shape[0]
    tp = lax.axis_index("tp")
    at = pl.ds(pl.multiple_of(tp * part, part), part)
    total = arrived[0][...]
    for ref in arrived[1:]:
        total = total + ref[...].astype(F32)
    unit, scale = normed(middle_ref[at, :])
    value = cot_ref[at, :].astype(F32) + norm_back(unit, scale, total, gain_ref[...])
    grad_out[...] = value
    branch_out[...] = value.astype(BF16)
    for k in range(n_tp):
        at = pl.ds(pl.multiple_of((tp ^ k) * width, width), width)
        piece_refs[k][...] = mm(branch_out[...], w_ref[at, :], NT).astype(BF16)


def branch(middle, cotangent, gain, w_full, arrived, ready):
    part, model = arrived[0].shape
    n_tp = len(arrived)
    width = w_full.shape[0] // n_tp
    return pl.pallas_call(
        waiting(functools.partial(branch_kernel, n_tp), 4 + n_tp, ready),
        out_shape=(shaped((part, model), F32), shaped((part, model), BF16))
        + (shaped((part, width), BF16),) * n_tp,
        in_specs=[VMEM] * (4 + n_tp) + [ANY] * len(ready),
        out_specs=(VMEM,) * (2 + n_tp),
        name="branch",
        compiler_params=params(24),
    )(middle, cotangent, gain, w_full, *arrived, *ready)


def lay_kernel(n_tp, *refs):
    out_ref, held = refs[n_tp:]
    part = refs[0].shape[0]
    tp = lax.axis_index("tp")
    for k in range(n_tp):
        at = pl.ds(pl.multiple_of((tp ^ k) * part, part), part)
        held[at, :] = refs[k][...].astype(F32)
    out_ref[...] = held[...].T.astype(BF16)


def lay_turned(pieces):
    part, width = pieces[0].shape
    rows = part * len(pieces)
    return pl.pallas_call(
        functools.partial(lay_kernel, len(pieces)),
        out_shape=shaped((width, rows), BF16),
        in_specs=[VMEM] * len(pieces),
        out_specs=VMEM,
        scratch_shapes=[pltpu.VMEM((rows, width), F32)],
        name="lay_turned",
        compiler_params=params(16),
    )(*pieces)


def stack_kernel(n_tp, *refs):
    out_ref = refs[n_tp]
    part = refs[0].shape[0]
    tp = lax.axis_index("tp")
    for k in range(n_tp):
        at = pl.ds(pl.multiple_of((tp ^ k) * part, part), part)
        out_ref[at, :] = refs[k][...]


def stack_parts(pieces):
    part, model = pieces[0].shape
    return pl.pallas_call(
        functools.partial(stack_kernel, len(pieces)),
        out_shape=shaped((part * len(pieces), model), pieces[0].dtype),
        in_specs=[VMEM] * len(pieces),
        out_specs=VMEM,
        name="stack_parts",
        compiler_params=params(16),
    )(*pieces)


def turn_back(out_ref, first, value, cos_table, sin_table):
    for at in range(0, value.shape[0], HDIM):
        low = value[at : at + HALF]
        high = value[at + HALF : at + HDIM]
        spot = first + at
        out_ref[spot : spot + HALF, :] = (low * cos_table + high * sin_table).astype(BF16)
        out_ref[spot + HALF : spot + HDIM, :] = (high * cos_table - low * sin_table).astype(BF16)


def unproject_kernel(count, n_tp, x_ref, w_ref, cos_ref, sin_ref, two_ref, dq_ref, dq_back, *refs):
    dkv_refs = refs[:count]
    proj_out = refs[count]
    part_refs = refs[count + 1 : count + 1 + n_tp]
    grad, dkv = refs[count + 1 + n_tp :]
    rows, model = x_ref.shape
    part = rows // n_tp
    width = dq_ref.shape[0]
    tp = lax.axis_index("tp")
    cos_table = cos_ref[...]
    sin_table = sin_ref[...]
    turn_back(proj_out, 0, dq_ref[...] + dq_back[...].astype(F32), cos_table, sin_table)
    total = dkv_refs[0][...]
    for ref in dkv_refs[1:]:
        total = total + ref[...].astype(F32)
    dkv[...] = total
    turn_back(proj_out, width, dkv[:width, :], cos_table, sin_table)
    proj_out[2 * width :, :] = dkv[width:, :].astype(BF16)
    grad[...] = mm(proj_out[...], w_ref[...], TN)

    def gains(i, carry):
        at = pl.ds(i * STRIP, STRIP)
        unit, unused = normed(x_ref[at, :].astype(F32))
        product = grad[at, :] * unit
        return carry + jnp.sum(product.reshape(STRIP // 8, 8, -1), axis=0)

    gain = lax.fori_loop(0, rows // STRIP, gains, jnp.zeros((8, model), F32))
    line = lax.broadcasted_iota(jnp.int32, (16, model), 0)
    gain_two = jnp.sum(two_ref[...], axis=0, keepdims=True)
    gain = jnp.sum(gain, axis=0, keepdims=True)
    gain = jnp.where(line == 0, gain, jnp.where(line == 1, gain_two, 0.0))
    for k in range(n_tp):
        at = pl.ds(pl.multiple_of((tp ^ k) * part, part), part)
        part_refs[k][:part, :] = grad[at, :].astype(part_refs[k].dtype)
        part_refs[k][part:, :] = gain.astype(part_refs[k].dtype)


def unproject(
    n_tp, tokens, qkv_t, cos_table, sin_table, gain_two_part, dq, dq_back, dkvs, ready
):
    rows, model = tokens.shape
    part = rows // n_tp
    count = len(dkvs)
    return pl.pallas_call(
        waiting(functools.partial(unproject_kernel, count, n_tp), 7 + count, ready),
        out_shape=(shaped((qkv_t.shape[0], rows), BF16), shaped((part + 16, model), F32))
        + (shaped((part + 16, model), BF16),) * (n_tp - 1),
        in_specs=[VMEM] * (7 + count) + [ANY] * len(ready),
        out_specs=(VMEM,) * (1 + n_tp),
        scratch_shapes=[pltpu.VMEM((rows, model), F32), pltpu.VMEM(dkvs[0].shape, F32)],
        name="unproject",
        compiler_params=params(40),
    )(tokens, qkv_t, cos_table, sin_table, gain_two_part, dq, dq_back, *dkvs, *ready)


def input_kernel(n_tp, x_ref, gain_ref, grad_ref, *refs):
    arrived = refs[:n_tp]
    out_ref, gain_out = refs[n_tp:]
    part, model = grad_ref.shape
    tp = lax.axis_index("tp")
    at = pl.ds(pl.multiple_of(tp * part, part), part)
    total = arrived[0][...]
    for ref in arrived[1:]:
        total = total + ref[...].astype(F32)
    unit, scale = normed(x_ref[at, :].astype(F32))
    value = grad_ref[...] + norm_back(unit, scale, total[:part], gain_ref[...])
    out_ref[...] = value.astype(BF16)
    gain_out[...] = total[part : part + 8]


def input_side(tokens, gain, middle_grad, arrived, ready):
    part, model = middle_grad.shape
    return pl.pallas_call(
        waiting(functools.partial(input_kernel, len(arrived)), 3 + len(arrived), ready),
        out_shape=(shaped((part, model), BF16), shaped((8, model), F32)),
        in_specs=[VMEM] * (3 + len(arrived)) + [ANY] * len(ready),
        out_specs=(VMEM, VMEM),
        name="input_side",
        compiler_params=params(16),
    )(tokens, gain, middle_grad, *arrived, *ready)


def early_kernel(mixed_ref, gate_ref, cot_ref, h_ref, out_ref):
    units = mixed_ref.shape[0]
    out_ref[:units, :] = mm(mixed_ref[...], cot_ref[...], NN)
    out_ref[units : 3 * units, :] = mm(gate_ref[...], h_ref[...], NN)
    out_ref[3 * units :, :] = jnp.zeros((out_ref.shape[0] - 3 * units, out_ref.shape[1]), F32)


def early_grads(mixed, gate_grad, cotangent, h_two):
    model = cotangent.shape[1]
    return pl.pallas_call(
        early_kernel,
        out_shape=shaped((4 * mixed.shape[0], model), F32),
        in_specs=[VMEM] * 4,
        out_specs=VMEM,
        name="early_grads",
        compiler_params=params(24),
    )(mixed, gate_grad, cotangent, h_two)


def widen_kernel(in_ref, *out_refs):
    at = 0
    for ref in out_refs:
        ref[...] = in_ref[at : at + ref.shape[0], :].astype(F32)
        at += ref.shape[0]


def widen(value, sizes):
    return pl.pallas_call(
        widen_kernel,
        out_shape=tuple(shaped((size, value.shape[1]), F32) for size in sizes),
        in_specs=[VMEM],
        out_specs=(VMEM,) * len(sizes),
        name="widen",
        compiler_params=params(24),
    )(value)


def late_kernel(n_tp, proj_ref, h_ref, out_ref, *refs):
    branch_refs = refs[:n_tp]
    keep_ref, send_ref, branch_full = refs[n_tp:]
    part = branch_refs[0].shape[0]
    half = keep_ref.shape[1]
    wide = proj_ref.shape[0]
    tp = lax.axis_index("tp")
    core = lax.axis_index("seq") % 2
    for k in range(n_tp):
        at = pl.ds(pl.multiple_of((tp ^ k) * part, part), part)
        branch_full[at, :] = branch_refs[k][...]
    for ref, side in ((send_ref, 1 - core), (keep_ref, core)):
        columns = pl.ds(pl.multiple_of(side * half, half), half)
        ref[:wide, :] = mm(proj_ref[...], h_ref[:, columns], NN).astype(ref.dtype)
        ref[wide:, :] = mm(out_ref[...], branch_full[:, columns], NN).astype(ref.dtype)


def late_grads(proj_grad, h_one, out_b, branches, ready):
    rows, model = h_one.shape
    wide = proj_grad.shape[0] + out_b.shape[0]
    return pl.pallas_call(
        waiting(functools.partial(late_kernel, len(branches)), 3 + len(branches), ready),
        out_shape=(shaped((wide, model // 2), F32), shaped((wide, model // 2), BF16)),
        in_specs=[VMEM] * (3 + len(branches)) + [ANY] * len(ready),
        out_specs=(VMEM, VMEM),
        scratch_shapes=[pltpu.VMEM((rows, model), BF16)],
        name="late_grads",
        compiler_params=params(24),
    )(proj_grad, h_one, out_b, *branches, *ready)


def spread_kernel(count, keep_ref, back_ref, *refs):
    held = refs[count]
    piece = refs[0].shape[0]
    chip = lax.axis_index("seq") // 2
    held[...] = keep_ref[...] + back_ref[...].astype(F32)
    for k in range(count):
        at = pl.ds(pl.multiple_of((chip ^ k) * piece, piece), piece)
        refs[k][...] = held[at, :].astype(refs[k].dtype)


def spread(count, keep, back):
    wide, half = keep.shape
    piece = wide // count
    return pl.pallas_call(
        functools.partial(spread_kernel, count),
        out_shape=(shaped((piece, half), F32),) + (shaped((piece, half), BF16),) * (count - 1),
        in_specs=[VMEM, VMEM],
        out_specs=(VMEM,) * count,
        scratch_shapes=[pltpu.VMEM((wide, half), F32)],
        name="spread",
        compiler_params=params(16),
    )(keep, back)


def piece_kernel(count, gain_ref, *refs):
    out_ref = refs[count]
    half = out_ref.shape[1]
    total = refs[0][...]
    for ref in refs[1:count]:
        total = total + ref[...].astype(F32)
    line = lax.broadcasted_iota(jnp.int32, (16, half), 0)
    gains = jnp.zeros((16, half), F32)
    for at in range(4):
        row = gain_ref[at // 2 : at // 2 + 1, at % 2 * half : (at % 2 + 1) * half]
        gains = jnp.where(line == at, row, gains)
    out_ref[...] = jnp.concatenate([total, gains], axis=0).astype(BF16)


def sum_piece(gains, pieces, ready):
    piece, half = pieces[0].shape
    return pl.pallas_call(
        waiting(functools.partial(piece_kernel, len(pieces)), 1 + len(pieces), ready),
        out_shape=shaped((piece + 16, half), BF16),
        in_specs=[VMEM] * (1 + len(pieces)) + [ANY] * len(ready),
        out_specs=VMEM,
        name="sum_piece",
        compiler_params=params(16),
    )(gains, *pieces, *ready)


def collect_kernel(count, *refs):
    out_ref, held = refs[count:]
    piece = refs[0].shape[0] - 16
    wide = count * piece
    chip = lax.axis_index("seq") // 2
    gains = jnp.zeros((16, out_ref.shape[1]), F32)
    for k in range(count):
        at = pl.ds(pl.multiple_of((chip ^ k) * piece, piece), piece)
        whole = refs[k][...].astype(F32)
        held[at, :] = whole[:piece]
        gains = gains + whole[piece:]
    held[wide:, :] = gains
    out_ref[...] = held[...].astype(BF16)


def collect(pieces, ready=()):
    piece, half = pieces[0].shape
    wide = (piece - 16) * len(pieces) + 16
    return pl.pallas_call(
        waiting(functools.partial(collect_kernel, len(pieces)), len(pieces), ready),
        out_shape=shaped((wide, half), BF16),
        in_specs=[VMEM] * len(pieces) + [ANY] * len(ready),
        out_specs=VMEM,
        scratch_shapes=[pltpu.VMEM((wide, half), F32)],
        name="collect",
        compiler_params=params(16),
    )(*pieces, *ready)


def finish_kernel(own_ref, pair_ref, qkv_ref, out_ref, one_ref, two_ref):
    half = own_ref.shape[1]
    wide, tall = qkv_ref.shape[0], out_ref.shape[0]
    core = lax.axis_index("seq") % 2
    for ref, side in ((own_ref, core), (pair_ref, 1 - core)):
        columns = pl.ds(pl.multiple_of(side * half, half), half)
        qkv_ref[:, columns] = ref[:wide, :].astype(F32)
        out_ref[:, columns] = ref[wide : wide + tall, :].astype(F32)
    gains = own_ref[wide + tall :, :].astype(F32) + pair_ref[wide + tall :, :].astype(F32)
    for at, ref in ((0, one_ref), (2, two_ref)):
        ref[:, :half] = gains[at : at + 1]
        ref[:, half:] = gains[at + 1 : at + 2]


def finish(own, pair, wide):
    half = own.shape[1]
    tall = own.shape[0] - 16 - wide
    model = 2 * half
    return pl.pallas_call(
        finish_kernel,
        out_shape=(
            shaped((wide, model), F32),
            shaped((tall, model), F32),
            shaped((1, model), F32),
            shaped((1, model), F32),
        ),
        in_specs=[VMEM, VMEM],
        out_specs=(VMEM,) * 4,
        name="finish",
        compiler_params=params(16),
    )(own, pair)


def down_kernel(n_tp, mixed_ref, w_ref, middle_ref, keep_ref, send_ref, total):
    part = keep_ref.shape[0] * 2 // n_tp
    tp = lax.axis_index("tp")
    total[...] = mm(mixed_ref[...], w_ref[...], TN)
    for k in range(n_tp):
        at = pl.ds(pl.multiple_of((tp ^ k) * part, part), part)
        spot = k // 2 * part
        if k % 2:
            send_ref[spot : spot + part, :] = total[at, :].astype(BF16)
        else:
            value = total[at, :] + middle_ref[at, :] if k == 0 else total[at, :]
            keep_ref[spot : spot + part, :] = value


def down(n_tp, mixed, w_down, middle, ready):
    rows, model = middle.shape
    return pl.pallas_call(
        waiting(functools.partial(down_kernel, n_tp), 3, ready),
        out_shape=(shaped((rows // 2, model), F32), shaped((rows // 2, model), BF16)),
        in_specs=[VMEM] * 3 + [ANY] * len(ready),
        out_specs=(VMEM, VMEM),
        scratch_shapes=[pltpu.VMEM((rows, model), F32)],
        name="down",
        compiler_params=params(16),
    )(mixed, w_down, middle, *ready)


def pair_kernel(keep_ref, back_ref, own_ref, *send_refs):
    part = own_ref.shape[0]
    own_ref[...] = keep_ref[:part, :] + back_ref[:part, :].astype(F32)
    for k, ref in enumerate(send_refs):
        at = (k + 1) * part
        total = keep_ref[at : at + part, :] + back_ref[at : at + part, :].astype(F32)
        ref[...] = total.astype(BF16)


def pair_sum(n_tp, keep, back):
    part = keep.shape[0] * 2 // n_tp
    model = keep.shape[1]
    return pl.pallas_call(
        pair_kernel,
        out_shape=(shaped((part, model), F32),)
        + (shaped((part, model), BF16),) * (n_tp // 2 - 1),
        in_specs=[VMEM, VMEM],
        out_specs=(VMEM,) * (n_tp // 2),
        name="pair_sum",
        compiler_params=params(16),
    )(keep, back)


def total_kernel(count, *refs):
    total = refs[0][...]
    for ref in refs[1:count]:
        total = total + ref[...].astype(F32)
    refs[count][...] = total.astype(refs[count].dtype)


def total_of(parts, dtype=BF16):
    return pl.pallas_call(
        functools.partial(total_kernel, len(parts)),
        out_shape=shaped(parts[0].shape, dtype),
        in_specs=[VMEM] * len(parts),
        out_specs=VMEM,
        name="total_of",
        compiler_params=params(16),
    )(*parts)


def body(
    n_seq,
    n_tp,
    tokens,
    gain_one,
    w_qkv,
    w_out,
    gain_two,
    w_in,
    w_down,
    cotangent,
    doc_lengths,
    roster,
):
    rows, model = tokens.shape
    width = w_qkv.shape[2]
    units = w_in.shape[2]
    count = n_seq // 2
    qkv_t = w_qkv.transpose(1, 2, 0).reshape(3 * width, model)
    in_t = w_in.transpose(1, 2, 0).reshape(2 * units, model)
    gain_one = gain_one[None]
    gain_two = gain_two[None]
    over_tp = lambda x, k: swap(x, "tp", k, n_tp)
    over_chips = lambda x, k: swap(x, "seq", 2 * k, n_seq)
    over_cores = lambda x: swap(x, "seq", 1, n_seq)
    everywhere = lambda xs: [xs[0]] + [over_tp(xs[k], k) for k in range(1, n_tp)]

    def by_steps(part):
        parts = {0: part}
        hop = n_tp // 2
        while hop:
            parts.update({k ^ hop: over_tp(x, hop) for k, x in parts.items()})
            hop //= 2
        return [parts[k] for k in range(n_tp)]

    docs = (doc_lengths, roster)

    queries, kv, h_one, cos_table, sin_table = project(*docs, tokens, gain_one, qkv_t)
    blocks = [kv] + [over_chips(kv, j) for j in range(1, count)]
    q_pair = over_cores(queries)
    w_full = lax.all_gather(w_out, "tp", axis=0, tiled=True)

    (state,) = attention_forward(0, False, *docs, queries, q_pair, blocks[:-1])
    state_own, state_pair = attention_forward(
        count - 1, True, *docs, queries, q_pair, blocks[-1:], state
    )
    out_b, totals = join(state_own, over_cores(state_pair))
    outs = everywhere([out_b] * n_tp)
    out_pair = over_cores(out_b)
    totals_pair = over_cores(totals)

    middle, h_two, mixed, gate_grad, gain_two_part, *parts = feed(
        tokens, cotangent, gain_two, in_t, w_down, w_full, outs
    )
    early = early_grads(mixed, gate_grad, cotangent, h_two)
    keep, send = down(n_tp, mixed, w_down, middle, (early,))
    middle_grad, branch_grad, *pieces = branch(
        middle, cotangent, gain_two, w_full, everywhere(parts), (keep,)
    )
    early = lax.psum(early, "seq")
    out_grad = lay_turned(everywhere(pieces))
    grad_pair = over_cores(out_grad)
    branches = by_steps(branch_grad)

    own, *others = pair_sum(n_tp, keep, over_tp(send, 1))
    total = total_of([own] + [over_tp(others[k], 2 * k + 2) for k in range(n_tp // 2 - 1)])
    totals_all = by_steps(total)

    held = (queries, q_pair, out_grad, grad_pair, out_b, out_pair, totals, totals_pair)
    dkvs = [None] * count
    dq = None
    for j in range(count - 1, 0, -1):
        ready = (own,) if dq is None else ()
        terms, dq = attention_backward(j, False, *docs, held, blocks[j], dq, ready)
        dkvs[j] = over_chips(terms, j)
    dkv, dq_own, dq_pair = attention_backward(0, True, *docs, held, blocks[0], dq, (total,))
    for j in range(count - 1, 1, -1):
        dkv = total_of([dkv, dkvs[j]], F32)

    proj_grad, *parts = unproject(
        n_tp,
        tokens,
        qkv_t,
        cos_table,
        sin_table,
        gain_two_part,
        dq_own,
        over_cores(dq_pair),
        [dkv, dkvs[1]],
        branches[1:],
    )
    arrived = everywhere(parts)
    input_part, gains = input_side(tokens, gain_one, middle_grad, arrived, ())
    inputs_all = everywhere([input_part] * n_tp)

    keep, send = late_grads(proj_grad, h_one, out_b, branches, ())
    own, *others = spread(count, keep, over_cores(send))
    arrived = [own] + [over_chips(others[k - 1], k) for k in range(1, count)]
    grad_down, grad_in = widen(early, (units, 2 * units))
    layer_out = stack_parts(totals_all)
    piece = sum_piece(gains, arrived, (layer_out, grad_down))
    input_grad = stack_parts(inputs_all)
    collected = collect([piece] + [over_chips(piece, k) for k in range(1, count)], (input_grad,))
    grad_qkv, grad_out, grad_one, grad_two = finish(collected, over_cores(collected), 3 * width)

    back = lambda x, n: x.reshape(-1, n, model).transpose(2, 0, 1)
    return (
        layer_out,
        input_grad,
        grad_one[0],
        back(grad_qkv, width),
        grad_out,
        grad_two[0],
        back(grad_in, units),
        grad_down,
    )


def solution(mesh):
    placed = (
        P("seq", None),
        P(),
        P(None, None, "tp"),
        P("tp", None),
        P(),
        P(None, None, "tp"),
        P("tp", None),
        P("seq", None),
        P(),
        P(),
    )
    return jax.shard_map(
        functools.partial(body, mesh.shape["seq"], mesh.shape["tp"]),
        mesh=mesh,
        in_specs=placed,
        out_specs=(
            P("seq", None),
            P("seq", None),
            P(),
            P(None, None, "tp"),
            P("tp", None),
            P(),
            P(None, None, "tp"),
            P("tp", None),
        ),
        check_vma=False,
    )
```

time: 265 us -> 224 us (0.85)
  starting transfers between devices: 81.7 us -> 51.9 us
  local copies, waits for them, and re-layouts: 10.7 us -> 28 us
  waiting for transfers between devices: 107 us -> 90 us
  other arithmetic: 8.78 us -> 1.22 us
  matrix products: 6.18 us -> 0 us
    ppermute x54 -> x43, starting transfers between devices: 81.6 us -> 51.9 us  [swap(): return lax.ppermute(x, axis, [(i, i ^ hop) for i in range(count)])]
    unnamed x78 -> x92, local copies, waits for them, and re-layouts: 8.43 us -> 27.3 us
    ppermute x54 -> x43, waiting for transfers between devices: 107 us -> 88.6 us  [swap(): return lax.ppermute(x, axis, [(i, i ^ hop) for i in range(count)])]
    dot_general x5 -> x0, matrix products: 6.18 us -> none  [mm(): return lax.dot_general(a, b, dims, preferred_element_type=F32)]
    convert_element_type x4 -> x0, other arithmetic: 4.1 us -> none  [the longest x1 1.87 us: body(): early[2].astype(F32)]
    transpose x2 -> x0, other arithmetic: 3.85 us -> none  [body(): back = lambda x, n: x.reshape(-1, n, model).transpose(2, 0, 1)]
    pallas_call x5 -> x21, Pallas kernels: 25 us -> 25.8 us  [the longest x4 8.58 us: attention_backward(): pl.pallas_call(waiting(functools.partial(backward_kernel, index, heads, b...]
  transfers between devices with their start and end apart: 55 -> 45, of which waited for: 21 -> 23; matrix products, arithmetic and copies ran while one was open for 5% -> 0% of each run, Pallas kernels for 6% -> 12%
where the time goes in v3:
time: 224 us; the launch traced here: 222 us
  waiting for transfers between devices  90 us (40%)
  starting transfers between devices  51.9 us (23%)
  Pallas kernels  36.1 us (16%)
  local copies, waits for them, and re-layouts  28 us (12%)
  between operations  14.5 us (6%)
    ppermute x43, waiting for transfers between devices, swap(): return lax.ppermute(x, axis, [(i, i ^ hop) for i in range(count)])  88.6 us
    ppermute x43, starting transfers between devices, swap(): return lax.ppermute(x, axis, [(i, i ^ hop) for i in range(count)])  51.9 us
    unnamed x92, local copies, waits for them, and re-layouts  27.3 us
    pallas_call x4, Pallas kernels, attention_backward(): pl.pallas_call(waiting(functools.partial(backward_kernel, index, heads, b...  8.58 us
    pallas_call x2, Pallas kernels, attention_forward(): pl.pallas_call(functools.partial(forward_kernel, first, count, heads, las...  5.36 us
    pallas_call x1, Pallas kernels, feed(): pl.pallas_call(functools.partial(feed_kernel, n_tp), out_shape=(shaped((r...  4.77 us
  transfers between devices with their start and end apart: 45, of which 23 were waited for; matrix products, arithmetic and copies ran while one was open for 0% of the time, Pallas kernels for 12%

profile of v3, /device:TPU:0, one launch (start us, length us, event | category | flops | bytes accessed | tf_op | source)
XLA Modules:
  0.0 221.7 jit_solution(7041273493123626587)
XLA Ops:
  12.2 3.4 %project.1 = (bf16[192,448]{1,0:T(8,128)(2,1)S(1)}, bf16[384,448]{1,0:T(8,128)(2,1)S(1)}, bf16[448,768]{1,0:T(8,128)(2,1)S(1)}, f32[32,448]{1,0:T(8,128)S(1)}, f32[32,448]{1,0:T(8,128)S(1)}) custom-call(s32[4]{0:T(128)S(1)} %copy-done.37, s32[8]{0:T(128)S(1)} %copy-done.39, bf16[448,768]{1,0:T(8,128)(2,1)S(1)} %copy-done, bf16[576,768]{1,0:T(8,128)(2,1)S(1)} %bitcast.12, ...), custom_call_target="tpu_custom_call" | custom-call | tf_op jit(solution)/shard_map/project/pallas_call | solution.py:176
  15.6 3.0 %collective-permute-start.2 = (bf16[384,448]{1,0:T(8,128)(2,1)S(1)}, bf16[384,448]{1,0:T(8,128)(2,1)S(1)}, u32[]{:S(2)}, u32[]{:S(2)}) collective-permute-start(bf16[384,448]{1,0:T(8,128)(2,1)S(1)} %get-tuple-element.65.refs_0_.refs_10_), channel_id=1, source_target_pairs={{0,8},{4,12},{8,0},{12,4},{16,24},{20,28},{24,16},{28,20},{1,9},{5... | collective-permute-start | bytes 1032200 | tf_op jit(solution)/shard_map/ppermute | solution.py:48
  21.6 7.0 %collective-permute-done.2.refs_1_.refs_10_ = bf16[384,448]{1,0:T(8,128)(2,1)S(1)} collective-permute-done((bf16[384,448]{1,0:T(8,128)(2,1)S(1)}, bf16[384,448]{1,0:T(8,128)(2,1)S(1)}, u32[]{:S(2)}, u32[]{:S(2)}) %collective-permute-start.2) | collective-permute-done | bytes 344096 | tf_op jit(solution)/shard_map/ppermute | solution.py:48
  28.5 9.1 %collective-permute-done.3.refs_2_.refs_10_ = bf16[384,448]{1,0:T(8,128)(2,1)S(1)} collective-permute-done((bf16[384,448]{1,0:T(8,128)(2,1)S(1)}, bf16[384,448]{1,0:T(8,128)(2,1)S(1)}, u32[]{:S(2)}, u32[]{:S(2)}) %collective-permute-start.3) | collective-permute-done | bytes 344096 | tf_op jit(solution)/shard_map/ppermute | solution.py:48
  37.6 4.4 %attention_forward.2.refs_1_ = f32[6,80,448]{2,1,0:T(8,128)S(1)} custom-call(s32[4]{0:T(128)S(1)} %copy-done.37, s32[8]{0:T(128)S(1)} %copy-done.39, bf16[192,448]{1,0:T(8,128)(2,1)S(1)} %get-tuple-element.64.q_own.refs_2_, bf16[192,448]{1,0:T(8,128)(2,1)S(1)} %collective-permute-done.q_pair.refs_3_, ...), custom_call_target="tpu_custom_call" | custom-call | tf_op jit(solution)/shard_map/attention_forward/pallas_call | solution.py:270
  43.8 1.9 collective-permute-done.4.back_ref
  47.4 2.6 %collective-permute-start.6 = (bf16[192,448]{1,0:T(8,128)(2,1)S(1)}, bf16[192,448]{1,0:T(8,128)(2,1)S(1)}, u32[]{:S(2)}, u32[]{:S(2)}) collective-permute-start(bf16[192,448]{1,0:T(8,128)(2,1)S(1)} %get-tuple-element.68.refs_0_.refs_6_.refs_2_), channel_id=1, source_target_pairs={{0,2},{1,3},{2,0},{3,1},{4,6},{5,7},{6,4},{7,5},{8,10},{9,11},{10,... | collective-permute-start | bytes 516104 | tf_op jit(solution)/shard_map/ppermute | solution.py:48
  50.2 6.2 %collective-permute-done.5.refs_1_ = bf16[192,448]{1,0:T(8,128)(2,1)S(1)} collective-permute-done((bf16[192,448]{1,0:T(8,128)(2,1)S(1)}, bf16[192,448]{1,0:T(8,128)(2,1)S(1)}, u32[]{:S(2)}, u32[]{:S(2)}) %collective-permute-start.5) | collective-permute-done | bytes 172064 | tf_op jit(solution)/shard_map/ppermute | solution.py:48
  57.1 7.4 %collective-permute-done.6.refs_2_ = bf16[192,448]{1,0:T(8,128)(2,1)S(1)} collective-permute-done((bf16[192,448]{1,0:T(8,128)(2,1)S(1)}, bf16[192,448]{1,0:T(8,128)(2,1)S(1)}, u32[]{:S(2)}, u32[]{:S(2)}) %collective-permute-start.6) | collective-permute-done | bytes 172064 | tf_op jit(solution)/shard_map/ppermute | solution.py:48
  72.2 4.8 %feed.1 = (f32[448,768]{1,0:T(8,128)S(1)}, bf16[448,768]{1,0:T(8,128)(2,1)S(1)}, bf16[288,448]{1,0:T(8,128)(2,1)S(1)}, bf16[576,448]{1,0:T(8,128)(2,1)S(1)}, f32...) custom-call(bf16[448,768]{1,0:T(8,128)(2,1)S(1)} %copy-done.1, ...), custom_call_target="tpu_custom_call" | custom-call | tf_op jit(solution)/shard_map/feed/pallas_call | solution.py:469
  79.7 2.7 %early_grads.1.refs_3_ = f32[1152,768]{1,0:T(8,128)} custom-call(bf16[288,448]{1,0:T(8,128)(2,1)S(1)} %get-tuple-element.69.mixed_ref.refs_0_, bf16[576,448]{1,0:T(8,128)(2,1)S(1)} %get-tuple-element.71.gate_ref, bf16[448,768]{1,0:T(8,128)(2,1)S(1)} %copy-done.2, bf16[448,768]{1,0:T(8,128)(2,1)S(1)} %get-tuple-element.72.h_ref), custom_call_target="tpu_custom_call" | custom-call | tf_op jit(solution)/shard_map/early_grads/pallas_call | solution.py:674
  88.1 3.1 %collective-permute-start.13 = (bf16[112,768]{1,0:T(8,128)(2,1)}, bf16[112,768]{1,0:T(8,128)(2,1)S(1)}, u32[]{:S(2)}, u32[]{:S(2)}) collective-permute-start(bf16[112,768]{1,0:T(8,128)(2,1)} %copy-done.44), channel_id=1, source_target_pairs={{0,1},{1,0},{2,3},{3,2},{4,5},{5,4},{6,7},{7,6},{8,9},{9,8},{10,11... | collective-permute-start | bytes 516104 | tf_op jit(solution)/shard_map/ppermute | solution.py:48
  94.6 4.0 %collective-permute-done.13.refs_5_ = bf16[112,768]{1,0:T(8,128)(2,1)S(1)} collective-permute-done((bf16[112,768]{1,0:T(8,128)(2,1)}, bf16[112,768]{1,0:T(8,128)(2,1)S(1)}, u32[]{:S(2)}, u32[]{:S(2)}) %collective-permute-start.13) | collective-permute-done | bytes 172064 | tf_op jit(solution)/shard_map/ppermute | solution.py:48
  98.6 8.0 %collective-permute-done.14.refs_6_ = bf16[112,768]{1,0:T(8,128)(2,1)S(1)} collective-permute-done((bf16[112,768]{1,0:T(8,128)(2,1)}, bf16[112,768]{1,0:T(8,128)(2,1)S(1)}, u32[]{:S(2)}, u32[]{:S(2)}) %collective-permute-start.14) | collective-permute-done | bytes 172064 | tf_op jit(solution)/shard_map/ppermute | solution.py:48
  110.8 2.5 %collective-permute-start.16 = (bf16[112,192]{1,0:T(8,128)(2,1)S(1)}, bf16[112,192]{1,0:T(8,128)(2,1)S(1)}, u32[]{:S(2)}, u32[]{:S(2)}) collective-permute-start(bf16[112,192]{1,0:T(8,128)(2,1)S(1)} %get-tuple-element.86), channel_id=1, source_target_pairs={{0,1},{1,0},{2,3},{3,2},{4,5},{5,4},{6,7},{7,6},{8,9},{9,8},{10,11... | collective-permute-start | bytes 129032 | tf_op jit(solution)/shard_map/ppermute | solution.py:48
  116.0 3.3 %collective-permute-done.17.refs_2_ = bf16[112,192]{1,0:T(8,128)(2,1)S(1)} collective-permute-done((bf16[112,192]{1,0:T(8,128)(2,1)S(1)}, bf16[112,192]{1,0:T(8,128)(2,1)S(1)}, u32[]{:S(2)}, u32[]{:S(2)}) %collective-permute-start.17) | collective-permute-done | bytes 43040 | tf_op jit(solution)/shard_map/ppermute | solution.py:48
  123.5 4.8 %collective-permute-start.23 = (bf16[384,448]{1,0:T(8,128)(2,1)S(1)}, bf16[384,448]{1,0:T(8,128)(2,1)S(1)}, u32[]{:S(2)}, u32[]{:S(2)}) collective-permute-start(bf16[384,448]{1,0:T(8,128)(2,1)S(1)} %get-tuple-element.96), channel_id=1, source_target_pairs={{0,24},{4,28},{8,16},{12,20},{16,8},{20,12},{24,0},{28,4},{1,25},{... | collective-permute-start | bytes 1032200 | tf_op jit(solution)/shard_map/ppermute | solution.py:48
  132.4 2.9 %collective-permute-start.24 = (bf16[384,448]{1,0:T(8,128)(2,1)S(1)}, bf16[384,448]{1,0:T(8,128)(2,1)S(1)}, u32[]{:S(2)}, u32[]{:S(2)}) collective-permute-start(bf16[384,448]{1,0:T(8,128)(2,1)S(1)} %get-tuple-element.97), channel_id=1, source_target_pairs={{0,16},{4,20},{8,24},{12,28},{16,0},{20,4},{24,8},{28,12},{1,17},{... | collective-permute-start | bytes 1032200 | tf_op jit(solution)/shard_map/ppermute | solution.py:48
  136.5 6.6 %collective-permute-done.27.refs_10_.refs_5_ = bf16[112,768]{1,0:T(8,128)(2,1)S(1)} collective-permute-done((bf16[112,768]{1,0:T(8,128)(2,1)S(1)}, bf16[112,768]{1,0:T(8,128)(2,1)S(1)}, u32[]{:S(2)}, u32[]{:S(2)}) %collective-permute-start.27) | collective-permute-done | bytes 172064 | tf_op jit(solution)/shard_map/ppermute | solution.py:48
  143.1 3.5 %collective-permute-done.9.refs_1_ = bf16[112,768]{1,0:T(8,128)(2,1)S(1)} collective-permute-done((bf16[112,768]{1,0:T(8,128)(2,1)S(1)}, bf16[112,768]{1,0:T(8,128)(2,1)S(1)}, u32[]{:S(2)}, u32[]{:S(2)}) %collective-permute-start.9) | collective-permute-done | bytes 172064 | tf_op jit(solution)/shard_map/ppermute | solution.py:48
  146.7 5.0 %attention_backward.7 = (f32[384,448]{1,0:T(8,128)S(1)}, f32[192,448]{1,0:T(8,128)S(1)}, bf16[192,448]{1,0:T(8,128)(2,1)S(1)}) custom-call(s32[4]{0:T(128)S(1)} %copy-done.38, s32[8]{0:T(128)S(1)} %copy-done.40, bf16[192,448]{1,0:T(8,128)(2,1)S(1)} %get-tuple-element.64.q_own.refs_2_, bf16[192,448]{1,0:T(8,128)(2,1)S(1)} %collective-permute-done.q_pair.refs_3_, ...), custom_call_target="tpu_custom_call" | custom-call | tf_op jit(solution)/shard_map/attention_backward/pallas_call | solution.py:357
  152.0 1.9 collective-permute-done.28.refs_11_.refs_6_
  153.9 2.4 %unproject.1 = (bf16[576,448]{1,0:T(8,128)(2,1)S(1)}, f32[128,768]{1,0:T(8,128)S(1)}, bf16[128,768]{1,0:T(8,128)(2,1)S(1)}, bf16[128,768]{1,0:T(8,128)(2,1)S(1)}, bf16[128,768]{1,0:T(8,128)(2,1)S(1)}) custom-call(bf16[448,768]{1,0:T(8,128)(2,1)S(1)} %copy-done.1, bf16[576,768]{1,0:T(8,128)(2,1)S(1)} %bitcast.13, f32[32,448]{1,0:T(8,128)S(1)} %get-tuple-element.82.refs_2_, ...), custom_call_target="tpu_custom_call" | custom-call | tf_op jit(solution)/shard_map/unproject/pallas_call | solution.py:626
  159.5 2.3 %collective-permute-start.30 = (bf16[128,768]{1,0:T(8,128)(2,1)S(1)}, bf16[128,768]{1,0:T(8,128)(2,1)S(1)}, u32[]{:S(2)}, u32[]{:S(2)}) collective-permute-start(bf16[128,768]{1,0:T(8,128)(2,1)S(1)} %get-tuple-element.102), channel_id=1, source_target_pairs={{0,2},{1,3},{2,0},{3,1},{4,6},{5,7},{6,4},{7,5},{8,10},{9,11},{10,... | collective-permute-start | bytes 589832 | tf_op jit(solution)/shard_map/ppermute | solution.py:48
  163.3 6.0 %collective-permute-done.11.refs_2_ = bf16[112,768]{1,0:T(8,128)(2,1)S(1)} collective-permute-done((bf16[112,768]{1,0:T(8,128)(2,1)S(1)}, bf16[112,768]{1,0:T(8,128)(2,1)S(1)}, u32[]{:S(2)}, u32[]{:S(2)}) %collective-permute-start.11) | collective-permute-done | bytes 172064 | tf_op jit(solution)/shard_map/ppermute | solution.py:48
  171.4 10.6 %collective-permute-done.30.refs_5_ = bf16[128,768]{1,0:T(8,128)(2,1)S(1)} collective-permute-done((bf16[128,768]{1,0:T(8,128)(2,1)S(1)}, bf16[128,768]{1,0:T(8,128)(2,1)S(1)}, u32[]{:S(2)}, u32[]{:S(2)}) %collective-permute-start.30) | collective-permute-done | bytes 196640 | tf_op jit(solution)/shard_map/ppermute | solution.py:48
  182.4 4.4 %collective-permute-start.32 = (bf16[112,768]{1,0:T(8,128)(2,1)S(1)}, bf16[112,768]{1,0:T(8,128)(2,1)S(1)}, u32[]{:S(2)}, u32[]{:S(2)}) collective-permute-start(bf16[112,768]{1,0:T(8,128)(2,1)S(1)} %get-tuple-element.104.refs_0_), channel_id=1, source_target_pairs={{0,1},{1,0},{2,3},{3,2},{4,5},{5,4},{6,7},{7,6},{8,9},{9,8},{10,11... | collective-permute-start | bytes 516104 | tf_op jit(solution)/shard_map/ppermute | solution.py:48
  187.7 2.8 %collective-permute-start.38 = (bf16[192,384]{1,0:T(8,128)(2,1)S(1)}, bf16[192,384]{1,0:T(8,128)(2,1)S(1)}, u32[]{:S(2)}, u32[]{:S(2)}) collective-permute-start(bf16[192,384]{1,0:T(8,128)(2,1)S(1)} %get-tuple-element.113), channel_id=1, source_target_pairs={{0,24},{4,28},{8,16},{12,20},{16,8},{20,12},{24,0},{28,4},{1,25},{... | collective-permute-start | bytes 442376 | tf_op jit(solution)/shard_map/ppermute | solution.py:48
  190.6 3.2 %collective-permute-done.36.refs_2_ = bf16[192,384]{1,0:T(8,128)(2,1)S(1)} collective-permute-done((bf16[192,384]{1,0:T(8,128)(2,1)S(1)}, bf16[192,384]{1,0:T(8,128)(2,1)S(1)}, u32[]{:S(2)}, u32[]{:S(2)}) %collective-permute-start.36) | collective-permute-done | bytes 147488 | tf_op jit(solution)/shard_map/ppermute | solution.py:48
  196.1 2.0 copy-done.5
  202.5 2.1 collective-permute-start.41
  210.1 2.0 collective-permute-done.42.pair_ref
  (184 shorter events, 71.6 us)
Async XLA Ops:
  7.2 58.7 %all-gather.2.cloned.1.call-start = ((), (), s32[]{:S(2)}) async-start(), calls=%async_computation | async-start | bytes 1474560 | tf_op jit(solution)/shard_map/all_gather | solution.py:953
  15.6 12.9 %collective-permute-start.2 = (bf16[384,448]{1,0:T(8,128)(2,1)S(1)}, bf16[384,448]{1,0:T(8,128)(2,1)S(1)}, u32[]{:S(2)}, u32[]{:S(2)}) collective-permute-start(bf16[384,448]{1,0:T(8,128)(2,1)S(1)} %get-tuple-element.65.refs_0_.refs_10_), channel_id=1, source_target_pairs={{0,8},{4,12},{8,0},{12,4},{16,24},{20,28},{24,16},{28,20},{1,9},{5... | collective-permute-start | bytes 1032200 | tf_op jit(solution)/shard_map/ppermute | solution.py:48
  18.6 19.0 %collective-permute-start.3 = (bf16[384,448]{1,0:T(8,128)(2,1)S(1)}, bf16[384,448]{1,0:T(8,128)(2,1)S(1)}, u32[]{:S(2)}, u32[]{:S(2)}) collective-permute-start(bf16[384,448]{1,0:T(8,128)(2,1)S(1)} %get-tuple-element.65.refs_0_.refs_10_), channel_id=1, source_target_pairs={{0,16},{4,20},{8,24},{12,28},{16,0},{20,4},{24,8},{28,12},{1,17},{... | collective-permute-start | bytes 1032200 | tf_op jit(solution)/shard_map/ppermute | solution.py:48
  20.1 22.6 %collective-permute-start.1 = (bf16[384,448]{1,0:T(8,128)(2,1)S(1)}, bf16[384,448]{1,0:T(8,128)(2,1)S(1)}, u32[]{:S(2)}, u32[]{:S(2)}) collective-permute-start(bf16[384,448]{1,0:T(8,128)(2,1)S(1)} %get-tuple-element.65.refs_0_.refs_10_), channel_id=1, source_target_pairs={{0,24},{4,28},{8,16},{12,20},{16,8},{20,12},{24,0},{28,4},{1,25},{... | collective-permute-start | bytes 1032200 | tf_op jit(solution)/shard_map/ppermute | solution.py:48
  45.8 10.6 %collective-permute-start.5 = (bf16[192,448]{1,0:T(8,128)(2,1)S(1)}, bf16[192,448]{1,0:T(8,128)(2,1)S(1)}, u32[]{:S(2)}, u32[]{:S(2)}) collective-permute-start(bf16[192,448]{1,0:T(8,128)(2,1)S(1)} %get-tuple-element.68.refs_0_.refs_6_.refs_2_), channel_id=1, source_target_pairs={{0,1},{1,0},{2,3},{3,2},{4,5},{5,4},{6,7},{7,6},{8,9},{9,8},{10,11... | collective-permute-start | bytes 516104 | tf_op jit(solution)/shard_map/ppermute | solution.py:48
  47.4 17.1 %collective-permute-start.6 = (bf16[192,448]{1,0:T(8,128)(2,1)S(1)}, bf16[192,448]{1,0:T(8,128)(2,1)S(1)}, u32[]{:S(2)}, u32[]{:S(2)}) collective-permute-start(bf16[192,448]{1,0:T(8,128)(2,1)S(1)} %get-tuple-element.68.refs_0_.refs_6_.refs_2_), channel_id=1, source_target_pairs={{0,2},{1,3},{2,0},{3,1},{4,6},{5,7},{6,4},{7,5},{8,10},{9,11},{10,... | collective-permute-start | bytes 516104 | tf_op jit(solution)/shard_map/ppermute | solution.py:48
  50.0 15.2 %collective-permute-start.7 = (bf16[192,448]{1,0:T(8,128)(2,1)S(1)}, bf16[192,448]{1,0:T(8,128)(2,1)S(1)}, u32[]{:S(2)}, u32[]{:S(2)}) collective-permute-start(bf16[192,448]{1,0:T(8,128)(2,1)S(1)} %get-tuple-element.68.refs_0_.refs_6_.refs_2_), channel_id=1, source_target_pairs={{0,3},{1,2},{2,1},{3,0},{4,7},{5,6},{6,5},{7,4},{8,11},{9,10},{10,... | collective-permute-start | bytes 516104 | tf_op jit(solution)/shard_map/ppermute | solution.py:48
  87.3 108.8 %all-reduce.2.cloned.1.call-start = ((), (), s32[]{:S(2)}) async-start(), calls=%async_computation.1 | async-start | bytes 7077888 | tf_op jit(solution)/shard_map/psum | solution.py:972
  88.1 10.5 %collective-permute-start.13 = (bf16[112,768]{1,0:T(8,128)(2,1)}, bf16[112,768]{1,0:T(8,128)(2,1)S(1)}, u32[]{:S(2)}, u32[]{:S(2)}) collective-permute-start(bf16[112,768]{1,0:T(8,128)(2,1)} %copy-done.44), channel_id=1, source_target_pairs={{0,1},{1,0},{2,3},{3,2},{4,5},{5,4},{6,7},{7,6},{8,9},{9,8},{10,11... | collective-permute-start | bytes 516104 | tf_op jit(solution)/shard_map/ppermute | solution.py:48
  91.1 15.4 %collective-permute-start.14 = (bf16[112,768]{1,0:T(8,128)(2,1)}, bf16[112,768]{1,0:T(8,128)(2,1)S(1)}, u32[]{:S(2)}, u32[]{:S(2)}) collective-permute-start(bf16[112,768]{1,0:T(8,128)(2,1)} %copy-done.43), channel_id=1, source_target_pairs={{0,2},{1,3},{2,0},{3,1},{4,6},{5,7},{6,4},{7,5},{8,10},{9,11},{10,... | collective-permute-start | bytes 516104 | tf_op jit(solution)/shard_map/ppermute | solution.py:48
  92.2 14.3 %collective-permute-start.15 = (bf16[112,768]{1,0:T(8,128)(2,1)}, bf16[112,768]{1,0:T(8,128)(2,1)S(1)}, u32[]{:S(2)}, u32[]{:S(2)}) collective-permute-start(bf16[112,768]{1,0:T(8,128)(2,1)} %copy-done.42), channel_id=1, source_target_pairs={{0,3},{1,2},{2,1},{3,0},{4,7},{5,6},{6,5},{7,4},{8,11},{9,10},{10,... | collective-permute-start | bytes 516104 | tf_op jit(solution)/shard_map/ppermute | solution.py:48
  93.6 27.5 %collective-permute-start.8 = (bf16[224,768]{1,0:T(8,128)(2,1)}, bf16[224,768]{1,0:T(8,128)(2,1)S(1)}, u32[]{:S(2)}, u32[]{:S(2)}) collective-permute-start(bf16[224,768]{1,0:T(8,128)(2,1)} %copy-done.41), channel_id=1, source_target_pairs={{0,1},{1,0},{2,3},{3,2},{4,5},{5,4},{6,7},{7,6},{8,9},{9,8},{10,11... | collective-permute-start | bytes 1032200 | tf_op jit(solution)/shard_map/ppermute | solution.py:48
  123.5 28.1 %collective-permute-start.23 = (bf16[384,448]{1,0:T(8,128)(2,1)S(1)}, bf16[384,448]{1,0:T(8,128)(2,1)S(1)}, u32[]{:S(2)}, u32[]{:S(2)}) collective-permute-start(bf16[384,448]{1,0:T(8,128)(2,1)S(1)} %get-tuple-element.96), channel_id=1, source_target_pairs={{0,24},{4,28},{8,16},{12,20},{16,8},{20,12},{24,0},{28,4},{1,25},{... | collective-permute-start | bytes 1032200 | tf_op jit(solution)/shard_map/ppermute | solution.py:48
  128.3 14.8 %collective-permute-start.27 = (bf16[112,768]{1,0:T(8,128)(2,1)S(1)}, bf16[112,768]{1,0:T(8,128)(2,1)S(1)}, u32[]{:S(2)}, u32[]{:S(2)}) collective-permute-start(bf16[112,768]{1,0:T(8,128)(2,1)S(1)} %get-tuple-element.99.refs_3_), channel_id=1, source_target_pairs={{0,2},{1,3},{2,0},{3,1},{4,6},{5,7},{6,4},{7,5},{8,10},{9,11},{10,... | collective-permute-start | bytes 516104 | tf_op jit(solution)/shard_map/ppermute | solution.py:48
  129.5 17.1 %collective-permute-start.9 = (bf16[112,768]{1,0:T(8,128)(2,1)S(1)}, bf16[112,768]{1,0:T(8,128)(2,1)S(1)}, u32[]{:S(2)}, u32[]{:S(2)}) collective-permute-start(bf16[112,768]{1,0:T(8,128)(2,1)S(1)} %get-tuple-element.76), channel_id=1, source_target_pairs={{0,2},{1,3},{2,0},{3,1},{4,6},{5,7},{6,4},{7,5},{8,10},{9,11},{10,... | collective-permute-start | bytes 516104 | tf_op jit(solution)/shard_map/ppermute | solution.py:48
  132.4 19.4 %collective-permute-start.24 = (bf16[384,448]{1,0:T(8,128)(2,1)S(1)}, bf16[384,448]{1,0:T(8,128)(2,1)S(1)}, u32[]{:S(2)}, u32[]{:S(2)}) collective-permute-start(bf16[384,448]{1,0:T(8,128)(2,1)S(1)} %get-tuple-element.97), channel_id=1, source_target_pairs={{0,16},{4,20},{8,24},{12,28},{16,0},{20,4},{24,8},{28,12},{1,17},{... | collective-permute-start | bytes 1032200 | tf_op jit(solution)/shard_map/ppermute | solution.py:48
  136.4 17.5 %collective-permute-start.25 = (bf16[384,448]{1,0:T(8,128)(2,1)S(1)}, bf16[384,448]{1,0:T(8,128)(2,1)S(1)}, u32[]{:S(2)}, u32[]{:S(2)}) collective-permute-start(bf16[384,448]{1,0:T(8,128)(2,1)S(1)} %get-tuple-element.98), channel_id=1, source_target_pairs={{0,8},{4,12},{8,0},{12,4},{16,24},{20,28},{24,16},{28,20},{1,9},{5... | collective-permute-start | bytes 1032200 | tf_op jit(solution)/shard_map/ppermute | solution.py:48
  143.1 8.8 %collective-permute-start.26 = (bf16[112,768]{1,0:T(8,128)(2,1)S(1)}, bf16[112,768]{1,0:T(8,128)(2,1)S(1)}, u32[]{:S(2)}, u32[]{:S(2)}) collective-permute-start(bf16[112,768]{1,0:T(8,128)(2,1)S(1)} %get-tuple-element.99.refs_3_), channel_id=1, source_target_pairs={{0,1},{1,0},{2,3},{3,2},{4,5},{5,4},{6,7},{7,6},{8,9},{9,8},{10,11... | collective-permute-start | bytes 516104 | tf_op jit(solution)/shard_map/ppermute | solution.py:48
  146.6 7.3 %collective-permute-start.28 = (bf16[112,768]{1,0:T(8,128)(2,1)S(1)}, bf16[112,768]{1,0:T(8,128)(2,1)S(1)}, u32[]{:S(2)}, u32[]{:S(2)}) collective-permute-start(bf16[112,768]{1,0:T(8,128)(2,1)S(1)} %collective-permute-done.27.refs_10_.refs_5_), channel_id=1, source_target_pairs={{0,1},{1,0},{2,3},{3,2},{4,5},{5,4},{6,7},{7,6},{8,9},{9,8},{10,11... | collective-permute-start | bytes 516104 | tf_op jit(solution)/shard_map/ppermute | solution.py:48
  157.3 29.4 %collective-permute-start.35 = (bf16[768,384]{1,0:T(8,128)(2,1)S(1)}, bf16[768,384]{1,0:T(8,128)(2,1)S(1)}, u32[]{:S(2)}, u32[]{:S(2)}) collective-permute-start(bf16[768,384]{1,0:T(8,128)(2,1)S(1)} %get-tuple-element.109), channel_id=1, source_target_pairs={{0,4},{4,0},{8,12},{12,8},{16,20},{20,16},{24,28},{28,24},{1,5},{5... | collective-permute-start | bytes 1769480 | tf_op jit(solution)/shard_map/ppermute | solution.py:48
  157.4 11.9 %collective-permute-start.11 = (bf16[112,768]{1,0:T(8,128)(2,1)S(1)}, bf16[112,768]{1,0:T(8,128)(2,1)S(1)}, u32[]{:S(2)}, u32[]{:S(2)}) collective-permute-start(bf16[112,768]{1,0:T(8,128)(2,1)S(1)} %total_of.3.refs_0_.refs_12_), channel_id=1, source_target_pairs={{0,2},{1,3},{2,0},{3,1},{4,6},{5,7},{6,4},{7,5},{8,10},{9,11},{10,... | collective-permute-start | bytes 516104 | tf_op jit(solution)/shard_map/ppermute | solution.py:48
  158.9 11.5 %collective-permute-start.29 = (bf16[128,768]{1,0:T(8,128)(2,1)S(1)}, bf16[128,768]{1,0:T(8,128)(2,1)S(1)}, u32[]{:S(2)}, u32[]{:S(2)}) collective-permute-start(bf16[128,768]{1,0:T(8,128)(2,1)S(1)} %get-tuple-element.101), channel_id=1, source_target_pairs={{0,1},{1,0},{2,3},{3,2},{4,5},{5,4},{6,7},{7,6},{8,9},{9,8},{10,11... | collective-permute-start | bytes 589832 | tf_op jit(solution)/shard_map/ppermute | solution.py:48
  159.5 22.5 %collective-permute-start.30 = (bf16[128,768]{1,0:T(8,128)(2,1)S(1)}, bf16[128,768]{1,0:T(8,128)(2,1)S(1)}, u32[]{:S(2)}, u32[]{:S(2)}) collective-permute-start(bf16[128,768]{1,0:T(8,128)(2,1)S(1)} %get-tuple-element.102), channel_id=1, source_target_pairs={{0,2},{1,3},{2,0},{3,1},{4,6},{5,7},{6,4},{7,5},{8,10},{9,11},{10,... | collective-permute-start | bytes 589832 | tf_op jit(solution)/shard_map/ppermute | solution.py:48
  161.9 20.1 %collective-permute-start.31 = (bf16[128,768]{1,0:T(8,128)(2,1)S(1)}, bf16[128,768]{1,0:T(8,128)(2,1)S(1)}, u32[]{:S(2)}, u32[]{:S(2)}) collective-permute-start(bf16[128,768]{1,0:T(8,128)(2,1)S(1)} %get-tuple-element.103), channel_id=1, source_target_pairs={{0,3},{1,2},{2,1},{3,0},{4,7},{5,6},{6,5},{7,4},{8,11},{9,10},{10,... | collective-permute-start | bytes 589832 | tf_op jit(solution)/shard_map/ppermute | solution.py:48
  169.4 18.4 %collective-permute-start.10 = (bf16[112,768]{1,0:T(8,128)(2,1)S(1)}, bf16[112,768]{1,0:T(8,128)(2,1)S(1)}, u32[]{:S(2)}, u32[]{:S(2)}) collective-permute-start(bf16[112,768]{1,0:T(8,128)(2,1)S(1)} %total_of.3.refs_0_.refs_12_), channel_id=1, source_target_pairs={{0,1},{1,0},{2,3},{3,2},{4,5},{5,4},{6,7},{7,6},{8,9},{9,8},{10,11... | collective-permute-start | bytes 516104 | tf_op jit(solution)/shard_map/ppermute | solution.py:48
  170.4 20.1 %collective-permute-start.12 = (bf16[112,768]{1,0:T(8,128)(2,1)S(1)}, bf16[112,768]{1,0:T(8,128)(2,1)S(1)}, u32[]{:S(2)}, u32[]{:S(2)}) collective-permute-start(bf16[112,768]{1,0:T(8,128)(2,1)S(1)} %collective-permute-done.11.refs_2_), channel_id=1, source_target_pairs={{0,1},{1,0},{2,3},{3,2},{4,5},{5,4},{6,7},{7,6},{8,9},{9,8},{10,11... | collective-permute-start | bytes 516104 | tf_op jit(solution)/shard_map/ppermute | solution.py:48
  182.4 20.2 %collective-permute-start.32 = (bf16[112,768]{1,0:T(8,128)(2,1)S(1)}, bf16[112,768]{1,0:T(8,128)(2,1)S(1)}, u32[]{:S(2)}, u32[]{:S(2)}) collective-permute-start(bf16[112,768]{1,0:T(8,128)(2,1)S(1)} %get-tuple-element.104.refs_0_), channel_id=1, source_target_pairs={{0,1},{1,0},{2,3},{3,2},{4,5},{5,4},{6,7},{7,6},{8,9},{9,8},{10,11... | collective-permute-start | bytes 516104 | tf_op jit(solution)/shard_map/ppermute | solution.py:48
  187.0 6.8 %collective-permute-start.36 = (bf16[192,384]{1,0:T(8,128)(2,1)S(1)}, bf16[192,384]{1,0:T(8,128)(2,1)S(1)}, u32[]{:S(2)}, u32[]{:S(2)}) collective-permute-start(bf16[192,384]{1,0:T(8,128)(2,1)S(1)} %get-tuple-element.111), channel_id=1, source_target_pairs={{0,8},{4,12},{8,0},{12,4},{16,24},{20,28},{24,16},{28,20},{1,9},{5... | collective-permute-start | bytes 442376 | tf_op jit(solution)/shard_map/ppermute | solution.py:48
  187.1 12.7 %collective-permute-start.37 = (bf16[192,384]{1,0:T(8,128)(2,1)S(1)}, bf16[192,384]{1,0:T(8,128)(2,1)S(1)}, u32[]{:S(2)}, u32[]{:S(2)}) collective-permute-start(bf16[192,384]{1,0:T(8,128)(2,1)S(1)} %get-tuple-element.112), channel_id=1, source_target_pairs={{0,16},{4,20},{8,24},{12,28},{16,0},{20,4},{24,8},{28,12},{1,17},{... | collective-permute-start | bytes 442376 | tf_op jit(solution)/shard_map/ppermute | solution.py:48
  187.7 12.1 %collective-permute-start.38 = (bf16[192,384]{1,0:T(8,128)(2,1)S(1)}, bf16[192,384]{1,0:T(8,128)(2,1)S(1)}, u32[]{:S(2)}, u32[]{:S(2)}) collective-permute-start(bf16[192,384]{1,0:T(8,128)(2,1)S(1)} %get-tuple-element.113), channel_id=1, source_target_pairs={{0,24},{4,28},{8,16},{12,20},{16,8},{20,12},{24,0},{28,4},{1,25},{... | collective-permute-start | bytes 442376 | tf_op jit(solution)/shard_map/ppermute | solution.py:48
  190.5 14.1 %collective-permute-start.33 = (bf16[112,768]{1,0:T(8,128)(2,1)S(1)}, bf16[112,768]{1,0:T(8,128)(2,1)S(1)}, u32[]{:S(2)}, u32[]{:S(2)}) collective-permute-start(bf16[112,768]{1,0:T(8,128)(2,1)S(1)} %get-tuple-element.104.refs_0_), channel_id=1, source_target_pairs={{0,2},{1,3},{2,0},{3,1},{4,6},{5,7},{6,4},{7,5},{8,10},{9,11},{10,... | collective-permute-start | bytes 516104 | tf_op jit(solution)/shard_map/ppermute | solution.py:48
  193.8 10.9 %collective-permute-start.34 = (bf16[112,768]{1,0:T(8,128)(2,1)S(1)}, bf16[112,768]{1,0:T(8,128)(2,1)S(1)}, u32[]{:S(2)}, u32[]{:S(2)}) collective-permute-start(bf16[112,768]{1,0:T(8,128)(2,1)S(1)} %get-tuple-element.104.refs_0_), channel_id=1, source_target_pairs={{0,3},{1,2},{2,1},{3,0},{4,7},{5,6},{6,5},{7,4},{8,11},{9,10},{10,... | collective-permute-start | bytes 516104 | tf_op jit(solution)/shard_map/ppermute | solution.py:48
  (59 other events, 304.7 us)
Sparse Core Ops, SparseCore 0:
  9.6 33.1 all-gather.1
  91.5 82.2 all-reduce.1

commit v4 on v3

--- a/solution.py
+++ b/solution.py
@@ -16,9 +16,8 @@
 STRIP = 64
 F32 = jnp.float32
 BF16 = jnp.bfloat16
-ANY = pl.BlockSpec(memory_space=pl.ANY)
+HBM = pl.BlockSpec(memory_space=pltpu.HBM)
 VMEM = pl.BlockSpec(memory_space=pltpu.VMEM)
-SMEM = pl.BlockSpec(memory_space=pltpu.SMEM)
 
 NN = (((1,), (0,)), ((), ()))
 NT = (((1,), (1,)), ((), ()))
@@ -29,19 +28,80 @@
     return pltpu.CompilerParams(vmem_limit_bytes=mib * 2**20)
 
 
+def mm(a, b, dims):
+    return lax.dot_general(a, b, dims, preferred_element_type=F32)
+
+
 def shaped(shape, dtype):
     return jax.ShapeDtypeStruct(shape, dtype)
 
 
-def mm(a, b, dims):
-    return lax.dot_general(a, b, dims, preferred_element_type=F32)
-
-
-def waiting(kernel, given, ready):
-    def inner(*refs):
-        kernel(*refs[:given], *refs[given + len(ready) :])
-
-    return inner
+def kinds(arrays, kind):
+    return [(array, kind) for array in arrays]
+
+
+def pin(array, kind):
+    return array if kind in ("v", "free") else pltpu.with_memory_space_constraint(array, pltpu.HBM)
+
+
+def call(name, kernel, ins, outs, scratch=(), mib=16, after=()):
+    fetched = [i for i, given in enumerate(ins) if given[1] not in ("v", "raw", "free")]
+    left = [i for i, out in enumerate(outs) if out[2] == "h"]
+
+    def held(array, kind):
+        rows = array.shape[0] if kind == "h" else kind
+        return pltpu.VMEM((rows,) + array.shape[1:], array.dtype)
+
+    def run(*refs):
+        in_refs = list(refs[: len(ins)])
+        at = len(ins) + len(after)
+        out_refs = list(refs[at : at + len(outs)])
+        at += len(outs)
+        own = refs[at : at + len(scratch)]
+        at += len(scratch)
+        buffers = refs[at : at + len(fetched) + len(left)]
+        sems = refs[-1]
+        copies = []
+        for n, i in enumerate(fetched):
+            source = in_refs[i]
+            if ins[i][1] != "h":
+                rows = ins[i][1]
+                at = pl.multiple_of(lax.axis_index("tp") * rows, rows)
+                source = source.at[pl.ds(at, rows)]
+            copies.append(pltpu.make_async_copy(source, buffers[n], sems.at[n]))
+            in_refs[i] = buffers[n]
+        for copy in copies:
+            copy.start()
+        for copy in copies:
+            copy.wait()
+        copies = []
+        for n, i in enumerate(left):
+            spot = len(fetched) + n
+            copies.append(pltpu.make_async_copy(buffers[spot], out_refs[i], sems.at[spot]))
+            out_refs[i] = buffers[spot]
+        kernel(*in_refs, *out_refs, *own)
+        for copy in copies:
+            copy.start()
+        for copy in copies:
+            copy.wait()
+
+    spec = lambda kind: VMEM if kind == "v" else HBM
+    count = len(fetched) + len(left)
+    return pl.pallas_call(
+        run,
+        out_shape=tuple(
+            shaped(shape, dtype) if kind == "v" else pltpu.HBM(shape, dtype)
+            for shape, dtype, kind in outs
+        ),
+        in_specs=[spec(kind) for unused, kind in ins] + [spec(kind) for unused, kind in after],
+        out_specs=tuple(spec(kind) for unused, unused, kind in outs),
+        scratch_shapes=list(scratch)
+        + [held(*ins[i]) for i in fetched]
+        + [pltpu.VMEM(outs[i][0], outs[i][1]) for i in left]
+        + [pltpu.SemaphoreType.DMA((max(count, 1),))],
+        name=name,
+        compiler_params=params(mib),
+    )(*[pin(*given) for given in ins], *[pin(*given) for given in after])
 
 
 def swap(x, axis, hop, count):
@@ -172,28 +232,26 @@
     rows, model = tokens.shape
     width = qkv_t.shape[0] // 3
     freq = ROPE_THETA ** (-(jnp.arange(HALF).astype(F32) * (2.0 / HDIM)))
-    table = shaped((HALF, rows), F32)
-    return pl.pallas_call(
+    return call(
+        "project",
         functools.partial(project_kernel, width),
-        out_shape=(
-            shaped((width, rows), BF16),
-            shaped((2 * width, rows), BF16),
-            shaped((rows, model), BF16),
-            table,
-            table,
-        ),
-        in_specs=[ANY] * 4 + [VMEM] * 2,
-        out_specs=(VMEM,) * 5,
-        scratch_shapes=[
+        [(x, "raw") for x in (doc_lengths, roster, tokens, qkv_t)]
+        + [(gain, "h"), (freq[:, None], "h")],
+        [
+            ((width, rows), BF16, "v"),
+            ((2 * width, rows), BF16, "v"),
+            ((rows, model), BF16, "h"),
+            ((HALF, rows), F32, "h"),
+            ((HALF, rows), F32, "h"),
+        ],
+        [
             pltpu.VMEM((rows, model), BF16),
             pltpu.VMEM(qkv_t.shape, BF16),
             pltpu.VMEM((3 * width, rows), F32),
         ]
         + doc_scratch(doc_lengths, roster)
         + [pltpu.SemaphoreType.DMA((4,))],
-        name="project",
-        compiler_params=params(24),
-    )(doc_lengths, roster, tokens, qkv_t, gain, freq[:, None])
+    )
 
 
 def forward_kernel(first, count, heads, last, len_any, roster_any, q_own, q_pair, *refs):
@@ -264,24 +322,25 @@
     width, rows = q_own.shape
     heads = width // HDIM
     count = len(blocks)
-    half = shaped((heads, AUG, rows), F32)
-    whole = shaped((2 * heads, AUG, rows), F32)
-    given = () if state is None else (state,)
-    return pl.pallas_call(
+    half = ((heads, AUG, rows), F32, "v")
+    whole = ((2 * heads, AUG, rows), F32, "v")
+    given = [] if state is None else [(state, "v")]
+    return call(
+        "attention_forward",
         functools.partial(forward_kernel, first, count, heads, last),
-        out_shape=(half, half) if last else (whole,),
-        in_specs=[ANY, ANY, VMEM, VMEM] + [ANY] * count + [VMEM] * len(given),
-        out_specs=(VMEM, VMEM) if last else (VMEM,),
-        scratch_shapes=[
+        [(doc_lengths, "raw"), (roster, "raw"), (q_own, "v"), (q_pair, "v")]
+        + kinds(blocks, "free")
+        + given,
+        [half, half] if last else [whole],
+        [
             pltpu.VMEM((count, 2 * width, rows), BF16),
             pltpu.VMEM((2 * heads, AUG, rows), BF16),
             pltpu.VMEM((2 * heads, AUG, rows), F32),
         ]
         + doc_scratch(doc_lengths, roster)
         + [pltpu.SemaphoreType.DMA((count + 2,))],
-        name="attention_forward",
-        compiler_params=params(24 if count < 8 else 48),
-    )(doc_lengths, roster, q_own, q_pair, *blocks, *given)
+        16 if count < 8 else 40,
+    )
 
 
 def backward_kernel(index, heads, more, last, len_any, roster_any, *refs):
@@ -345,25 +404,20 @@
         outs[1][...] = dq[...]
 
 
-def attention_backward(index, last, doc_lengths, roster, held, block, dq=None, ready=()):
+def attention_backward(index, last, doc_lengths, roster, held, block, dq=None, after=()):
     width, rows = held[0].shape
     heads = width // HDIM
-    given = () if dq is None else (dq,)
-    total = shaped((2 * heads, HDIM, rows), F32)
+    given = [] if dq is None else [(dq, "v")]
     if last:
-        queries = (shaped((width, rows), F32), shaped((width, rows), BF16))
+        queries = [((width, rows), F32, "v"), ((width, rows), BF16, "v")]
     else:
-        queries = (total,)
-    return pl.pallas_call(
-        waiting(
-            functools.partial(backward_kernel, index, heads, bool(given), last),
-            11 + len(given),
-            ready,
-        ),
-        out_shape=(shaped((2 * width, rows), BF16 if index else F32),) + queries,
-        in_specs=[ANY, ANY] + [VMEM] * 8 + [ANY] + [VMEM] * len(given) + [ANY] * len(ready),
-        out_specs=(VMEM,) * (1 + len(queries)),
-        scratch_shapes=[
+        queries = [((2 * heads, HDIM, rows), F32, "v")]
+    return call(
+        "attention_backward",
+        functools.partial(backward_kernel, index, heads, bool(given), last),
+        [(doc_lengths, "raw"), (roster, "raw")] + kinds(held, "v") + [(block, "free")] + given,
+        [((2 * width, rows), BF16 if index else F32, "v")] + queries,
+        [
             pltpu.VMEM((2 * width, rows), BF16),
             pltpu.VMEM((2 * heads, AUG, rows), BF16),
             pltpu.VMEM((2 * heads, 8, rows), F32),
@@ -372,9 +426,9 @@
         ]
         + doc_scratch(doc_lengths, roster)
         + [pltpu.SemaphoreType.DMA((3,))],
-        name="attention_backward",
-        compiler_params=params(24),
-    )(doc_lengths, roster, *held, block, *given, *ready)
+        16,
+        after,
+    )
 
 
 def join_kernel(heads, own_ref, back_ref, out_ref, total_ref):
@@ -395,14 +449,12 @@
 
 def join(own, back):
     heads, unused, rows = own.shape
-    return pl.pallas_call(
+    return call(
+        "join",
         functools.partial(join_kernel, heads),
-        out_shape=(shaped((heads * HDIM, rows), BF16), shaped((heads, 8, rows), F32)),
-        in_specs=[VMEM, VMEM],
-        out_specs=(VMEM, VMEM),
-        name="join",
-        compiler_params=params(16),
-    )(own, back)
+        [(own, "v"), (back, "v")],
+        [((heads * HDIM, rows), BF16, "v"), ((heads, 8, rows), F32, "v")],
+    )
 
 
 def feed_kernel(n_tp, x_ref, cot_ref, gain_ref, in_ref, down_ref, w_ref, *refs):
@@ -466,29 +518,28 @@
     n_tp = len(outs)
     units = w_down.shape[0]
     part = rows // n_tp
-    return pl.pallas_call(
+    return call(
+        "feed",
         functools.partial(feed_kernel, n_tp),
-        out_shape=(
-            shaped((rows, model), F32),
-            shaped((rows, model), BF16),
-            shaped((units, rows), BF16),
-            shaped((2 * units, rows), BF16),
-            shaped((8, model), F32),
-            shaped((part, model), F32),
-        )
-        + (shaped((part, model), BF16),) * (n_tp - 1),
-        in_specs=[VMEM] * (6 + n_tp),
-        out_specs=(VMEM,) * (5 + n_tp),
-        scratch_shapes=[
+        kinds((tokens, cotangent, gain, in_t, w_down, w_full), "h") + kinds(outs, "v"),
+        [
+            ((rows, model), F32, "h"),
+            ((rows, model), BF16, "h"),
+            ((units, rows), BF16, "h"),
+            ((2 * units, rows), BF16, "h"),
+            ((8, model), F32, "h"),
+            ((part, model), F32, "h"),
+        ]
+        + [((part, model), BF16, "h")] * (n_tp - 1),
+        [
             pltpu.VMEM((n_tp * outs[0].shape[0], rows), BF16),
             pltpu.VMEM((rows, model), F32),
             pltpu.VMEM((2 * units, rows), F32),
             pltpu.VMEM((units, rows), F32),
             pltpu.VMEM((rows, model), F32),
         ],
-        name="feed",
-        compiler_params=params(32),
-    )(tokens, cotangent, gain, in_t, w_down, w_full, *outs)
+        32,
+    )
 
 
 def branch_kernel(n_tp, middle_ref, cot_ref, gain_ref, w_ref, *refs):
@@ -496,14 +547,12 @@
     grad_out, branch_out = refs[n_tp : n_tp + 2]
     piece_refs = refs[n_tp + 2 :]
     width = piece_refs[0].shape[1]
-    part = arrived[0].shape[0]
     tp = lax.axis_index("tp")
-    at = pl.ds(pl.multiple_of(tp * part, part), part)
     total = arrived[0][...]
     for ref in arrived[1:]:
         total = total + ref[...].astype(F32)
-    unit, scale = normed(middle_ref[at, :])
-    value = cot_ref[at, :].astype(F32) + norm_back(unit, scale, total, gain_ref[...])
+    unit, scale = normed(middle_ref[...])
+    value = cot_ref[...].astype(F32) + norm_back(unit, scale, total, gain_ref[...])
     grad_out[...] = value
     branch_out[...] = value.astype(BF16)
     for k in range(n_tp):
@@ -511,19 +560,20 @@
         piece_refs[k][...] = mm(branch_out[...], w_ref[at, :], NT).astype(BF16)
 
 
-def branch(middle, cotangent, gain, w_full, arrived, ready):
+def branch(middle, cotangent, gain, w_full, arrived, after):
     part, model = arrived[0].shape
     n_tp = len(arrived)
     width = w_full.shape[0] // n_tp
-    return pl.pallas_call(
-        waiting(functools.partial(branch_kernel, n_tp), 4 + n_tp, ready),
-        out_shape=(shaped((part, model), F32), shaped((part, model), BF16))
-        + (shaped((part, width), BF16),) * n_tp,
-        in_specs=[VMEM] * (4 + n_tp) + [ANY] * len(ready),
-        out_specs=(VMEM,) * (2 + n_tp),
-        name="branch",
-        compiler_params=params(24),
-    )(middle, cotangent, gain, w_full, *arrived, *ready)
+    return call(
+        "branch",
+        functools.partial(branch_kernel, n_tp),
+        [(middle, part), (cotangent, part)] + kinds((gain, w_full, arrived[0]), "h") + kinds(arrived[1:], "v"),
+        [((part, model), F32, "h"), ((part, model), BF16, "h")]
+        + [((part, width), BF16, "v")] * n_tp,
+        (),
+        16,
+        after,
+    )
 
 
 def lay_kernel(n_tp, *refs):
@@ -539,15 +589,14 @@
 def lay_turned(pieces):
     part, width = pieces[0].shape
     rows = part * len(pieces)
-    return pl.pallas_call(
+    (out,) = call(
+        "lay_turned",
         functools.partial(lay_kernel, len(pieces)),
-        out_shape=shaped((width, rows), BF16),
-        in_specs=[VMEM] * len(pieces),
-        out_specs=VMEM,
-        scratch_shapes=[pltpu.VMEM((rows, width), F32)],
-        name="lay_turned",
-        compiler_params=params(16),
-    )(*pieces)
+        kinds(pieces, "v"),
+        [((width, rows), BF16, "v")],
+        [pltpu.VMEM((rows, width), F32)],
+    )
+    return out
 
 
 def stack_kernel(n_tp, *refs):
@@ -559,16 +608,18 @@
         out_ref[at, :] = refs[k][...]
 
 
-def stack_parts(pieces):
+def stack_parts(pieces, after=()):
     part, model = pieces[0].shape
-    return pl.pallas_call(
+    (out,) = call(
+        "stack_parts",
         functools.partial(stack_kernel, len(pieces)),
-        out_shape=shaped((part * len(pieces), model), pieces[0].dtype),
-        in_specs=[VMEM] * len(pieces),
-        out_specs=VMEM,
-        name="stack_parts",
-        compiler_params=params(16),
-    )(*pieces)
+        kinds(pieces, "v"),
+        [((part * len(pieces), model), pieces[0].dtype, "h")],
+        (),
+        16,
+        after,
+    )
+    return out
 
 
 def turn_back(out_ref, first, value, cos_table, sin_table):
@@ -617,86 +668,90 @@
         part_refs[k][part:, :] = gain.astype(part_refs[k].dtype)
 
 
-def unproject(
-    n_tp, tokens, qkv_t, cos_table, sin_table, gain_two_part, dq, dq_back, dkvs, ready
-):
+def unproject(n_tp, tokens, qkv_t, cos_table, sin_table, gain_two_part, dq, dq_back, dkvs, after):
     rows, model = tokens.shape
     part = rows // n_tp
-    count = len(dkvs)
-    return pl.pallas_call(
-        waiting(functools.partial(unproject_kernel, count, n_tp), 7 + count, ready),
-        out_shape=(shaped((qkv_t.shape[0], rows), BF16), shaped((part + 16, model), F32))
-        + (shaped((part + 16, model), BF16),) * (n_tp - 1),
-        in_specs=[VMEM] * (7 + count) + [ANY] * len(ready),
-        out_specs=(VMEM,) * (1 + n_tp),
-        scratch_shapes=[pltpu.VMEM((rows, model), F32), pltpu.VMEM(dkvs[0].shape, F32)],
-        name="unproject",
-        compiler_params=params(40),
-    )(tokens, qkv_t, cos_table, sin_table, gain_two_part, dq, dq_back, *dkvs, *ready)
+    return call(
+        "unproject",
+        functools.partial(unproject_kernel, len(dkvs), n_tp),
+        kinds((tokens, qkv_t, cos_table, sin_table, gain_two_part), "h")
+        + kinds((dq, dq_back, *dkvs), "v"),
+        [((qkv_t.shape[0], rows), BF16, "v"), ((part + 16, model), F32, "v")]
+        + [((part + 16, model), BF16, "v")] * (n_tp - 1),
+        [pltpu.VMEM((rows, model), F32), pltpu.VMEM(dkvs[0].shape, F32)],
+        16,
+        after,
+    )
 
 
 def input_kernel(n_tp, x_ref, gain_ref, grad_ref, *refs):
     arrived = refs[:n_tp]
     out_ref, gain_out = refs[n_tp:]
     part, model = grad_ref.shape
-    tp = lax.axis_index("tp")
-    at = pl.ds(pl.multiple_of(tp * part, part), part)
     total = arrived[0][...]
     for ref in arrived[1:]:
         total = total + ref[...].astype(F32)
-    unit, scale = normed(x_ref[at, :].astype(F32))
+    unit, scale = normed(x_ref[...].astype(F32))
     value = grad_ref[...] + norm_back(unit, scale, total[:part], gain_ref[...])
     out_ref[...] = value.astype(BF16)
     gain_out[...] = total[part : part + 8]
 
 
-def input_side(tokens, gain, middle_grad, arrived, ready):
+def input_side(tokens, gain, middle_grad, arrived, after):
     part, model = middle_grad.shape
-    return pl.pallas_call(
-        waiting(functools.partial(input_kernel, len(arrived)), 3 + len(arrived), ready),
-        out_shape=(shaped((part, model), BF16), shaped((8, model), F32)),
-        in_specs=[VMEM] * (3 + len(arrived)) + [ANY] * len(ready),
-        out_specs=(VMEM, VMEM),
-        name="input_side",
-        compiler_params=params(16),
-    )(tokens, gain, middle_grad, *arrived, *ready)
+    return call(
+        "input_side",
+        functools.partial(input_kernel, len(arrived)),
+        [(tokens, part), (gain, "h"), (middle_grad, "h")] + kinds(arrived, "v"),
+        [((part, model), BF16, "v"), ((8, model), F32, "v")],
+        (),
+        16,
+        after,
+    )
 
 
 def early_kernel(mixed_ref, gate_ref, cot_ref, h_ref, out_ref):
     units = mixed_ref.shape[0]
     out_ref[:units, :] = mm(mixed_ref[...], cot_ref[...], NN)
     out_ref[units : 3 * units, :] = mm(gate_ref[...], h_ref[...], NN)
-    out_ref[3 * units :, :] = jnp.zeros((out_ref.shape[0] - 3 * units, out_ref.shape[1]), F32)
+    if out_ref.shape[0] > 3 * units:
+        out_ref[3 * units :, :] = jnp.zeros((out_ref.shape[0] - 3 * units, out_ref.shape[1]), F32)
 
 
 def early_grads(mixed, gate_grad, cotangent, h_two):
     model = cotangent.shape[1]
+    (out,) = call(
+        "early_grads",
+        early_kernel,
+        kinds((mixed, gate_grad, cotangent, h_two), "h"),
+        [((4 * mixed.shape[0], model), F32, "h")],
+    )
+    return out
+
+
+def part_kernel(in_ref, *refs):
+    out_refs, sems = refs[:-1], refs[-1]
+    copies = []
+    at = 0
+    for n, ref in enumerate(out_refs):
+        source = in_ref.at[pl.ds(at, ref.shape[0])]
+        copies.append(pltpu.make_async_copy(source, ref, sems.at[n]))
+        at += ref.shape[0]
+    for copy in copies:
+        copy.start()
+    for copy in copies:
+        copy.wait()
+
+
+def parted(value, sizes):
     return pl.pallas_call(
-        early_kernel,
-        out_shape=shaped((4 * mixed.shape[0], model), F32),
-        in_specs=[VMEM] * 4,
-        out_specs=VMEM,
-        name="early_grads",
-        compiler_params=params(24),
-    )(mixed, gate_grad, cotangent, h_two)
-
-
-def widen_kernel(in_ref, *out_refs):
-    at = 0
-    for ref in out_refs:
-        ref[...] = in_ref[at : at + ref.shape[0], :].astype(F32)
-        at += ref.shape[0]
-
-
-def widen(value, sizes):
-    return pl.pallas_call(
-        widen_kernel,
-        out_shape=tuple(shaped((size, value.shape[1]), F32) for size in sizes),
-        in_specs=[VMEM],
-        out_specs=(VMEM,) * len(sizes),
-        name="widen",
-        compiler_params=params(24),
-    )(value)
+        part_kernel,
+        out_shape=tuple(shaped((size, value.shape[1]), value.dtype) for size in sizes),
+        in_specs=[HBM],
+        out_specs=(HBM,) * len(sizes),
+        scratch_shapes=[pltpu.SemaphoreType.DMA((len(sizes),))],
+        name="parted",
+    )(pin(value, "h"))
 
 
 def late_kernel(n_tp, proj_ref, h_ref, out_ref, *refs):
@@ -716,18 +771,17 @@
         ref[wide:, :] = mm(out_ref[...], branch_full[:, columns], NN).astype(ref.dtype)
 
 
-def late_grads(proj_grad, h_one, out_b, branches, ready):
+def late_grads(proj_grad, h_one, out_b, branches):
     rows, model = h_one.shape
     wide = proj_grad.shape[0] + out_b.shape[0]
-    return pl.pallas_call(
-        waiting(functools.partial(late_kernel, len(branches)), 3 + len(branches), ready),
-        out_shape=(shaped((wide, model // 2), F32), shaped((wide, model // 2), BF16)),
-        in_specs=[VMEM] * (3 + len(branches)) + [ANY] * len(ready),
-        out_specs=(VMEM, VMEM),
-        scratch_shapes=[pltpu.VMEM((rows, model), BF16)],
-        name="late_grads",
-        compiler_params=params(24),
-    )(proj_grad, h_one, out_b, *branches, *ready)
+    return call(
+        "late_grads",
+        functools.partial(late_kernel, len(branches)),
+        [(proj_grad, "v"), (h_one, "h"), (out_b, "v"), (branches[0], "h")]
+        + kinds(branches[1:], "v"),
+        [((wide, model // 2), F32, "v"), ((wide, model // 2), BF16, "v")],
+        [pltpu.VMEM((rows, model), BF16)],
+    )
 
 
 def spread_kernel(count, keep_ref, back_ref, *refs):
@@ -743,15 +797,13 @@
 def spread(count, keep, back):
     wide, half = keep.shape
     piece = wide // count
-    return pl.pallas_call(
+    return call(
+        "spread",
         functools.partial(spread_kernel, count),
-        out_shape=(shaped((piece, half), F32),) + (shaped((piece, half), BF16),) * (count - 1),
-        in_specs=[VMEM, VMEM],
-        out_specs=(VMEM,) * count,
-        scratch_shapes=[pltpu.VMEM((wide, half), F32)],
-        name="spread",
-        compiler_params=params(16),
-    )(keep, back)
+        [(keep, "v"), (back, "v")],
+        [((piece, half), F32, "v")] + [((piece, half), BF16, "v")] * (count - 1),
+        [pltpu.VMEM((wide, half), F32)],
+    )
 
 
 def piece_kernel(count, gain_ref, *refs):
@@ -768,16 +820,18 @@
     out_ref[...] = jnp.concatenate([total, gains], axis=0).astype(BF16)
 
 
-def sum_piece(gains, pieces, ready):
+def sum_piece(gains, pieces, after=()):
     piece, half = pieces[0].shape
-    return pl.pallas_call(
-        waiting(functools.partial(piece_kernel, len(pieces)), 1 + len(pieces), ready),
-        out_shape=shaped((piece + 16, half), BF16),
-        in_specs=[VMEM] * (1 + len(pieces)) + [ANY] * len(ready),
-        out_specs=VMEM,
-        name="sum_piece",
-        compiler_params=params(16),
-    )(gains, *pieces, *ready)
+    (out,) = call(
+        "sum_piece",
+        functools.partial(piece_kernel, len(pieces)),
+        [(gains, "v")] + kinds(pieces, "v"),
+        [((piece + 16, half), BF16, "v")],
+        (),
+        16,
+        after,
+    )
+    return out
 
 
 def collect_kernel(count, *refs):
@@ -795,18 +849,19 @@
     out_ref[...] = held[...].astype(BF16)
 
 
-def collect(pieces, ready=()):
+def collect(pieces, after=()):
     piece, half = pieces[0].shape
     wide = (piece - 16) * len(pieces) + 16
-    return pl.pallas_call(
-        waiting(functools.partial(collect_kernel, len(pieces)), len(pieces), ready),
-        out_shape=shaped((wide, half), BF16),
-        in_specs=[VMEM] * len(pieces) + [ANY] * len(ready),
-        out_specs=VMEM,
-        scratch_shapes=[pltpu.VMEM((wide, half), F32)],
-        name="collect",
-        compiler_params=params(16),
-    )(*pieces, *ready)
+    (out,) = call(
+        "collect",
+        functools.partial(collect_kernel, len(pieces)),
+        kinds(pieces, "v"),
+        [((wide, half), BF16, "v")],
+        [pltpu.VMEM((wide, half), F32)],
+        16,
+        after,
+    )
+    return out
 
 
 def finish_kernel(own_ref, pair_ref, qkv_ref, out_ref, one_ref, two_ref):
@@ -823,23 +878,24 @@
         ref[:, half:] = gains[at + 1 : at + 2]
 
 
-def finish(own, pair, wide):
+def finish(own, pair, wide, after=()):
     half = own.shape[1]
     tall = own.shape[0] - 16 - wide
     model = 2 * half
-    return pl.pallas_call(
+    return call(
+        "finish",
         finish_kernel,
-        out_shape=(
-            shaped((wide, model), F32),
-            shaped((tall, model), F32),
-            shaped((1, model), F32),
-            shaped((1, model), F32),
-        ),
-        in_specs=[VMEM, VMEM],
-        out_specs=(VMEM,) * 4,
-        name="finish",
-        compiler_params=params(16),
-    )(own, pair)
+        [(own, "v"), (pair, "v")],
+        [
+            ((wide, model), F32, "h"),
+            ((tall, model), F32, "h"),
+            ((1, model), F32, "h"),
+            ((1, model), F32, "h"),
+        ],
+        (),
+        16,
+        after,
+    )
 
 
 def down_kernel(n_tp, mixed_ref, w_ref, middle_ref, keep_ref, send_ref, total):
@@ -856,17 +912,17 @@
             keep_ref[spot : spot + part, :] = value
 
 
-def down(n_tp, mixed, w_down, middle, ready):
+def down(n_tp, mixed, w_down, middle, after):
     rows, model = middle.shape
-    return pl.pallas_call(
-        waiting(functools.partial(down_kernel, n_tp), 3, ready),
-        out_shape=(shaped((rows // 2, model), F32), shaped((rows // 2, model), BF16)),
-        in_specs=[VMEM] * 3 + [ANY] * len(ready),
-        out_specs=(VMEM, VMEM),
-        scratch_shapes=[pltpu.VMEM((rows, model), F32)],
-        name="down",
-        compiler_params=params(16),
-    )(mixed, w_down, middle, *ready)
+    return call(
+        "down",
+        functools.partial(down_kernel, n_tp),
+        kinds((mixed, w_down, middle), "h"),
+        [((rows // 2, model), F32, "h"), ((rows // 2, model), BF16, "h")],
+        [pltpu.VMEM((rows, model), F32)],
+        16,
+        after,
+    )
 
 
 def pair_kernel(keep_ref, back_ref, own_ref, *send_refs):
@@ -878,18 +934,18 @@
         ref[...] = total.astype(BF16)
 
 
-def pair_sum(n_tp, keep, back):
+def pair_sum(n_tp, keep, back, after=()):
     part = keep.shape[0] * 2 // n_tp
     model = keep.shape[1]
-    return pl.pallas_call(
+    return call(
+        "pair_sum",
         pair_kernel,
-        out_shape=(shaped((part, model), F32),)
-        + (shaped((part, model), BF16),) * (n_tp // 2 - 1),
-        in_specs=[VMEM, VMEM],
-        out_specs=(VMEM,) * (n_tp // 2),
-        name="pair_sum",
-        compiler_params=params(16),
-    )(keep, back)
+        [(keep, "h"), (back, "v")],
+        [((part, model), F32, "v")] + [((part, model), BF16, "v")] * (n_tp // 2 - 1),
+        (),
+        16,
+        after,
+    )
 
 
 def total_kernel(count, *refs):
@@ -899,15 +955,17 @@
     refs[count][...] = total.astype(refs[count].dtype)
 
 
-def total_of(parts, dtype=BF16):
-    return pl.pallas_call(
+def total_of(parts, dtype=BF16, kind="v", after=()):
+    (out,) = call(
+        "total_of",
         functools.partial(total_kernel, len(parts)),
-        out_shape=shaped(parts[0].shape, dtype),
-        in_specs=[VMEM] * len(parts),
-        out_specs=VMEM,
-        name="total_of",
-        compiler_params=params(16),
-    )(*parts)
+        kinds(parts, kind),
+        [(parts[0].shape, dtype, kind)],
+        (),
+        16,
+        after,
+    )
+    return out
 
 
 def body(
@@ -952,9 +1010,10 @@
     q_pair = over_cores(queries)
     w_full = lax.all_gather(w_out, "tp", axis=0, tiled=True)
 
-    (state,) = attention_forward(0, False, *docs, queries, q_pair, blocks[:-1])
+    split = (count + 1) // 2
+    (state,) = attention_forward(0, False, *docs, queries, q_pair, blocks[:split])
     state_own, state_pair = attention_forward(
-        count - 1, True, *docs, queries, q_pair, blocks[-1:], state
+        split, True, *docs, queries, q_pair, blocks[split:], state
     )
     out_b, totals = join(state_own, over_cores(state_pair))
     outs = everywhere([out_b] * n_tp)
@@ -965,27 +1024,31 @@
         tokens, cotangent, gain_two, in_t, w_down, w_full, outs
     )
     early = early_grads(mixed, gate_grad, cotangent, h_two)
-    keep, send = down(n_tp, mixed, w_down, middle, (early,))
+    keep, send = down(n_tp, mixed, w_down, middle, [(early, "h")])
     middle_grad, branch_grad, *pieces = branch(
-        middle, cotangent, gain_two, w_full, everywhere(parts), (keep,)
+        middle, cotangent, gain_two, w_full, everywhere(parts), [(keep, "h")]
     )
     early = lax.psum(early, "seq")
+    grad_down, grad_in = parted(early, (units, 2 * units))
     out_grad = lay_turned(everywhere(pieces))
     grad_pair = over_cores(out_grad)
     branches = by_steps(branch_grad)
 
-    own, *others = pair_sum(n_tp, keep, over_tp(send, 1))
-    total = total_of([own] + [over_tp(others[k], 2 * k + 2) for k in range(n_tp // 2 - 1)])
+    own, *others = pair_sum(n_tp, keep, over_tp(send, 1), [(out_grad, "v")])
+    total = total_of(
+        [own] + [over_tp(others[k], 2 * k + 2) for k in range(n_tp // 2 - 1)], BF16
+    )
     totals_all = by_steps(total)
 
     held = (queries, q_pair, out_grad, grad_pair, out_b, out_pair, totals, totals_pair)
     dkvs = [None] * count
     dq = None
+    after = [(own, "v")]
     for j in range(count - 1, 0, -1):
-        ready = (own,) if dq is None else ()
-        terms, dq = attention_backward(j, False, *docs, held, blocks[j], dq, ready)
+        terms, dq = attention_backward(j, False, *docs, held, blocks[j], dq, after)
+        after = ()
         dkvs[j] = over_chips(terms, j)
-    dkv, dq_own, dq_pair = attention_backward(0, True, *docs, held, blocks[0], dq, (total,))
+    dkv, dq_own, dq_pair = attention_backward(0, True, *docs, held, blocks[0], dq)
     for j in range(count - 1, 1, -1):
         dkv = total_of([dkv, dkvs[j]], F32)
 
@@ -999,21 +1062,24 @@
         dq_own,
         over_cores(dq_pair),
         [dkv, dkvs[1]],
-        branches[1:],
-    )
-    arrived = everywhere(parts)
-    input_part, gains = input_side(tokens, gain_one, middle_grad, arrived, ())
+        kinds([*branches[1:], totals_all[n_tp // 2]], "v"),
+    )
+    keep, send = late_grads(proj_grad, h_one, out_b, branches)
+    own, *others = spread(count, keep, over_cores(send))
+    chip_sum = total_of([own] + [over_chips(others[k - 1], k) for k in range(1, count)], F32)
+    input_part, gains = input_side(
+        tokens, gain_one, middle_grad, everywhere(parts), [(own, "v")]
+    )
     inputs_all = everywhere([input_part] * n_tp)
-
-    keep, send = late_grads(proj_grad, h_one, out_b, branches, ())
-    own, *others = spread(count, keep, over_cores(send))
-    arrived = [own] + [over_chips(others[k - 1], k) for k in range(1, count)]
-    grad_down, grad_in = widen(early, (units, 2 * units))
-    layer_out = stack_parts(totals_all)
-    piece = sum_piece(gains, arrived, (layer_out, grad_down))
+    piece = sum_piece(gains, [chip_sum], ())
     input_grad = stack_parts(inputs_all)
-    collected = collect([piece] + [over_chips(piece, k) for k in range(1, count)], (input_grad,))
-    grad_qkv, grad_out, grad_one, grad_two = finish(collected, over_cores(collected), 3 * width)
+    collected = collect(
+        [piece] + [over_chips(piece, k) for k in range(1, count)], [(input_grad, "h"), (grad_down, "h")]
+    )
+    layer_out = stack_parts(totals_all, [(input_part, "v")])
+    grad_qkv, grad_out, grad_one, grad_two = finish(
+        collected, over_cores(collected), 3 * width, [(layer_out, "h")]
+    )
 
     back = lambda x, n: x.reshape(-1, n, model).transpose(2, 0, 1)
     return (

time: 224 us -> 297 us (1.33)
  Pallas kernels: 36.1 us -> 136 us
  local copies, waits for them, and re-layouts: 28 us -> 1.86 us
  waiting for transfers between devices: 90 us -> 85.4 us
    pallas_call x27 -> x28, Pallas kernels: 36.1 us -> 136 us  [the longest x1 81.5 us: parted(): pl.pallas_call(part_kernel, out_shape=tuple((shaped((size, value.shape[1]...]
    unnamed x92 -> x4, local copies, waits for them, and re-layouts: 27.3 us -> 0.01 us
    ppermute x43, waiting for transfers between devices: 88.6 us -> 84.6 us  [swap(): return lax.ppermute(x, axis, [(i, i ^ hop) for i in range(count)])]
  transfers between devices with their start and end apart: 45 -> 45, of which waited for: 23 -> 22; matrix products, arithmetic and copies ran while one was open for 0% -> 1% of each run, Pallas kernels for 12% -> 43%
where the time goes in v4:
time: 297 us; the launch traced here: 296 us
  Pallas kernels  136 us (46%)
  waiting for transfers between devices  85.4 us (29%)
  starting transfers between devices  54.6 us (18%)
  between operations  14.4 us (5%)
  other arithmetic  3.19 us (1%)
    ppermute x43, waiting for transfers between devices, swap(): return lax.ppermute(x, axis, [(i, i ^ hop) for i in range(count)])  84.6 us
    pallas_call x1, Pallas kernels, parted(): pl.pallas_call(part_kernel, out_shape=tuple((shaped((size, value.shape[1]...  81.5 us
    pallas_call x27, Pallas kernels, call(): pl.pallas_call(run, out_shape=tuple((shaped(shape, dtype) if kind == 'v'...  55 us
    ppermute x43, starting transfers between devices, swap(): return lax.ppermute(x, axis, [(i, i ^ hop) for i in range(count)])  54.5 us
  transfers between devices with their start and end apart: 45, of which 22 were waited for; matrix products, arithmetic and copies ran while one was open for 1% of the time, Pallas kernels for 43%

profile of v4, /device:TPU:0, one launch (start us, length us, event | category | flops | bytes accessed | tf_op | source)
XLA Modules:
  0.0 296.0 jit_solution(4462756045137815987)
XLA Ops:
  9.8 4.8 %project.1 = (bf16[192,448]{1,0:T(8,128)(2,1)S(1)}, bf16[384,448]{1,0:T(8,128)(2,1)S(1)}, bf16[448,768]{1,0:T(8,128)(2,1)}, f32[32,448]{1,0:T(8,128)}, f32[32,448]{1,0:T(8,128)}) custom-call(s32[4]{0:T(128)} %refs_0_.17, s32[8]{0:T(128)} %refs_1_.19, bf16[448,768]{1,0:T(8,128)(2,1)} %refs_0_.19, bf16[576,768]{1,0:T(8,128)(2,1)} %bitcast.12, ...), custom_call_target="tpu_custom_call" | custom-call | tf_op jit(solution)/shard_map/project/pallas_call | solution.py:90
  14.6 3.0 %collective-permute-start.3 = (bf16[384,448]{1,0:T(8,128)(2,1)S(1)}, bf16[384,448]{1,0:T(8,128)(2,1)S(1)}, u32[]{:S(2)}, u32[]{:S(2)}) collective-permute-start(bf16[384,448]{1,0:T(8,128)(2,1)S(1)} %get-tuple-element.65.refs_4_.refs_10_), channel_id=1, source_target_pairs={{0,8},{4,12},{8,0},{12,4},{16,24},{20,28},{24,16},{28,20},{1,9},{5... | collective-permute-start | bytes 1032200 | tf_op jit(solution)/shard_map/ppermute | solution.py:108
  20.5 7.0 %collective-permute-done.3.refs_5_.refs_10_ = bf16[384,448]{1,0:T(8,128)(2,1)S(1)} collective-permute-done((bf16[384,448]{1,0:T(8,128)(2,1)S(1)}, bf16[384,448]{1,0:T(8,128)(2,1)S(1)}, u32[]{:S(2)}, u32[]{:S(2)}) %collective-permute-start.3) | collective-permute-done | bytes 344096 | tf_op jit(solution)/shard_map/ppermute | solution.py:108
  27.5 2.8 attention_forward.2.refs_6_
  30.3 6.2 %collective-permute-done.1.refs_4_.refs_10_ = bf16[384,448]{1,0:T(8,128)(2,1)S(1)} collective-permute-done((bf16[384,448]{1,0:T(8,128)(2,1)S(1)}, bf16[384,448]{1,0:T(8,128)(2,1)S(1)}, u32[]{:S(2)}, u32[]{:S(2)}) %collective-permute-start.1) | collective-permute-done | bytes 344096 | tf_op jit(solution)/shard_map/ppermute | solution.py:108
  36.6 4.2 %attention_forward.3 = (f32[3,80,448]{2,1,0:T(8,128)S(1)}, f32[3,80,448]{2,1,0:T(8,128)S(1)}) custom-call(s32[4]{0:T(128)} %refs_0_.17, s32[8]{0:T(128)} %refs_1_.19, bf16[192,448]{1,0:T(8,128)(2,1)S(1)} %get-tuple-element.64.refs_2_, bf16[192,448]{1,0:T(8,128)(2,1)S(1)} %collective-permute-done.refs_3_, ...), custom_call_target="tpu_custom_call" | custom-call | tf_op jit(solution)/shard_map/attention_forward/pallas_call | solution.py:90
  47.9 5.8 %collective-permute-done.5.refs_7_ = bf16[192,448]{1,0:T(8,128)(2,1)S(1)} collective-permute-done((bf16[192,448]{1,0:T(8,128)(2,1)S(1)}, bf16[192,448]{1,0:T(8,128)(2,1)S(1)}, u32[]{:S(2)}, u32[]{:S(2)}) %collective-permute-start.5) | collective-permute-done | bytes 172064 | tf_op jit(solution)/shard_map/ppermute | solution.py:108
  53.6 8.0 %collective-permute-done.6.refs_8_ = bf16[192,448]{1,0:T(8,128)(2,1)S(1)} collective-permute-done((bf16[192,448]{1,0:T(8,128)(2,1)S(1)}, bf16[192,448]{1,0:T(8,128)(2,1)S(1)}, u32[]{:S(2)}, u32[]{:S(2)}) %collective-permute-start.6) | collective-permute-done | bytes 172064 | tf_op jit(solution)/shard_map/ppermute | solution.py:108
  61.6 8.8 %feed.1 = (f32[448,768]{1,0:T(8,128)}, bf16[448,768]{1,0:T(8,128)(2,1)}, bf16[288,448]{1,0:T(8,128)(2,1)}, bf16[576,448]{1,0:T(8,128)(2,1)}, f32[8,768]{1,0:T(8,...) custom-call(bf16[448,768]{1,0:T(8,128)(2,1)} %refs_0_.19, ...), custom_call_target="tpu_custom_call" | custom-call | tf_op jit(solution)/shard_map/feed/pallas_call | solution.py:90
  70.4 3.9 %collective-permute-start.9 = (bf16[112,768]{1,0:T(8,128)(2,1)}, bf16[112,768]{1,0:T(8,128)(2,1)S(1)}, u32[]{:S(2)}, u32[]{:S(2)}) collective-permute-start(bf16[112,768]{1,0:T(8,128)(2,1)} %get-tuple-element.76), channel_id=1, source_target_pairs={{0,1},{1,0},{2,3},{3,2},{4,5},{5,4},{6,7},{7,6},{8,9},{9,8},{10,11... | collective-permute-start | bytes 516104 | tf_op jit(solution)/shard_map/ppermute | solution.py:108
  76.7 4.2 %early_grads.1.refs_3_ = f32[1152,768]{1,0:T(8,128)} custom-call(bf16[288,448]{1,0:T(8,128)(2,1)} %get-tuple-element.69.refs_0_, bf16[576,448]{1,0:T(8,128)(2,1)} %get-tuple-element.71.refs_1_, bf16[448,768]{1,0:T(8,128)(2,1)} %refs_1_.15, bf16[448,768]{1,0:T(8,128)(2,1)} %get-tuple-element.72.refs_3_), custom_call_target="tpu_custom_call" | custom-call | tf_op jit(solution)/shard_map/early_grads/pallas_call | solution.py:90
  81.0 3.2 %down.1 = (f32[224,768]{1,0:T(8,128)}, bf16[224,768]{1,0:T(8,128)(2,1)}) custom-call(bf16[288,448]{1,0:T(8,128)(2,1)} %get-tuple-element.69.refs_0_, bf16[288,768]{1,0:T(8,128)(2,1)} %refs_1_.14, f32[448,768]{1,0:T(8,128)} %get-tuple-element.70.refs_2_.refs_0_, f32[1152,768]{1,0:T(8,128)} %early_grads.1.refs_3_), custom_call_target="tpu_custom_call" | custom-call | tf_op jit(solution)/shard_map/down/pallas_call | solution.py:90
  85.5 4.3 %collective-permute-done.10.refs_6_ = bf16[112,768]{1,0:T(8,128)(2,1)S(1)} collective-permute-done((bf16[112,768]{1,0:T(8,128)(2,1)}, bf16[112,768]{1,0:T(8,128)(2,1)S(1)}, u32[]{:S(2)}, u32[]{:S(2)}) %collective-permute-start.10) | collective-permute-done | bytes 172064 | tf_op jit(solution)/shard_map/ppermute | solution.py:108
  89.8 3.0 %branch.1 = (f32[112,768]{1,0:T(8,128)}, bf16[112,768]{1,0:T(8,128)(2,1)}, bf16[112,192]{1,0:T(8,128)(2,1)S(1)}, bf16[112,192]{1,0:T(8,128)(2,1)S(1)}, bf16[112,...) custom-call(f32[448,768]{1,0:T(8,128)} %get-tuple-element.70.refs_2_.refs_0_, bf16[448,768]{1,0:T(8,128)(2,1)} %refs_1_.15, ...), custom_call_target="tpu_custom_call" | custom-call | tf_op jit(solution)/shard_map/branch/pallas_call | solution.py:90
  98.1 3.1 %collective-permute-done.13.refs_2_ = bf16[112,192]{1,0:T(8,128)(2,1)S(1)} collective-permute-done((bf16[112,192]{1,0:T(8,128)(2,1)S(1)}, bf16[112,192]{1,0:T(8,128)(2,1)S(1)}, u32[]{:S(2)}, u32[]{:S(2)}) %collective-permute-start.13) | collective-permute-done | bytes 43040 | tf_op jit(solution)/shard_map/ppermute | solution.py:108
  104.3 3.2 %attention_backward.4 = (bf16[384,448]{1,0:T(8,128)(2,1)S(1)}, f32[6,64,448]{2,1,0:T(8,128)S(1)}) custom-call(s32[4]{0:T(128)} %refs_0_.17, s32[8]{0:T(128)} %refs_1_.19, bf16[192,448]{1,0:T(8,128)(2,1)S(1)} %get-tuple-element.64.refs_2_, bf16[192,448]{1,0:T(8,128)(2,1)S(1)} %collective-permute-done.refs_3_, bf16[192,448]{1,0:T(8,128)(2,1)S(1)} %lay_turned.1.refs_2_.refs_4_, ...), custom_call_target="tpu_custom_call" | custom-call | tf_op jit(solution)/shard_map/attention_backward/pallas_call | solution.py:90
  107.6 3.2 %collective-permute-start.23 = (bf16[384,448]{1,0:T(8,128)(2,1)S(1)}, bf16[384,448]{1,0:T(8,128)(2,1)S(1)}, u32[]{:S(2)}, u32[]{:S(2)}) collective-permute-start(bf16[384,448]{1,0:T(8,128)(2,1)S(1)} %get-tuple-element.96), channel_id=1, source_target_pairs={{0,24},{4,28},{8,16},{12,20},{16,8},{20,12},{24,0},{28,4},{1,25},{... | collective-permute-start | bytes 1032200 | tf_op jit(solution)/shard_map/ppermute | solution.py:108
  110.8 3.0 %attention_backward.5 = (bf16[384,448]{1,0:T(8,128)(2,1)S(1)}, f32[6,64,448]{2,1,0:T(8,128)S(1)}) custom-call(s32[4]{0:T(128)} %refs_0_.17, s32[8]{0:T(128)} %refs_1_.19, bf16[192,448]{1,0:T(8,128)(2,1)S(1)} %get-tuple-element.64.refs_2_, bf16[192,448]{1,0:T(8,128)(2,1)S(1)} %collective-permute-done.refs_3_, bf16[192,448]{1,0:T(8,128)(2,1)S(1)} %lay_turned.1.refs_2_.refs_4_, ...), custom_call_target="tpu_custom_call" | custom-call | tf_op jit(solution)/shard_map/attention_backward/pallas_call | solution.py:90
  119.6 3.3 %attention_backward.7 = (f32[384,448]{1,0:T(8,128)S(1)}, f32[192,448]{1,0:T(8,128)S(1)}, bf16[192,448]{1,0:T(8,128)(2,1)S(1)}) custom-call(s32[4]{0:T(128)} %refs_0_.17, s32[8]{0:T(128)} %refs_1_.19, bf16[192,448]{1,0:T(8,128)(2,1)S(1)} %get-tuple-element.64.refs_2_, bf16[192,448]{1,0:T(8,128)(2,1)S(1)} %collective-permute-done.refs_3_, ...), custom_call_target="tpu_custom_call" | custom-call | tf_op jit(solution)/shard_map/attention_backward/pallas_call | solution.py:90
  122.9 4.6 %collective-permute-done.27.refs_10_.refs_5_ = bf16[112,768]{1,0:T(8,128)(2,1)S(1)} collective-permute-done((bf16[112,768]{1,0:T(8,128)(2,1)S(1)}, bf16[112,768]{1,0:T(8,128)(2,1)S(1)}, u32[]{:S(2)}, u32[]{:S(2)}) %collective-permute-start.27) | collective-permute-done | bytes 172064 | tf_op jit(solution)/shard_map/ppermute | solution.py:108
  127.5 3.6 %collective-permute-done.15.refs_1_ = bf16[112,768]{1,0:T(8,128)(2,1)S(1)} collective-permute-done((bf16[112,768]{1,0:T(8,128)(2,1)S(1)}, bf16[112,768]{1,0:T(8,128)(2,1)S(1)}, u32[]{:S(2)}, u32[]{:S(2)}) %collective-permute-start.15) | collective-permute-done | bytes 172064 | tf_op jit(solution)/shard_map/ppermute | solution.py:108
  134.8 5.2 %collective-permute-done.28.refs_11_.refs_6_ = bf16[112,768]{1,0:T(8,128)(2,1)S(1)} collective-permute-done((bf16[112,768]{1,0:T(8,128)(2,1)S(1)}, bf16[112,768]{1,0:T(8,128)(2,1)S(1)}, u32[]{:S(2)}, u32[]{:S(2)}) %collective-permute-start.28) | collective-permute-done | bytes 172064 | tf_op jit(solution)/shard_map/ppermute | solution.py:108
  142.7 3.8 %unproject.1 = (bf16[576,448]{1,0:T(8,128)(2,1)S(1)}, f32[128,768]{1,0:T(8,128)S(1)}, bf16[128,768]{1,0:T(8,128)(2,1)S(1)}, bf16[128,768]{1,0:T(8,128)(2,1)S(1)}, bf16[128,768]{1,0:T(8,128)(2,1)S(1)}) custom-call(bf16[448,768]{1,0:T(8,128)(2,1)} %refs_0_.19, bf16[576,768]{1,0:T(8,128)(2,1)} %bitcast.13, f32[32,448]{1,0:T(8,128)} %get-tuple-element.86.refs_2_, ...), custom_call_target="tpu_custom_call" | custom-call | tf_op jit(solution)/shard_map/unproject/pallas_call | solution.py:90
  153.4 6.0 %collective-permute-done.29.refs_4_ = bf16[128,768]{1,0:T(8,128)(2,1)S(1)} collective-permute-done((bf16[128,768]{1,0:T(8,128)(2,1)S(1)}, bf16[128,768]{1,0:T(8,128)(2,1)S(1)}, u32[]{:S(2)}, u32[]{:S(2)}) %collective-permute-start.29) | collective-permute-done | bytes 196640 | tf_op jit(solution)/shard_map/ppermute | solution.py:108
  159.4 6.6 %collective-permute-done.30.refs_5_ = bf16[128,768]{1,0:T(8,128)(2,1)S(1)} collective-permute-done((bf16[128,768]{1,0:T(8,128)(2,1)S(1)}, bf16[128,768]{1,0:T(8,128)(2,1)S(1)}, u32[]{:S(2)}, u32[]{:S(2)}) %collective-permute-start.30) | collective-permute-done | bytes 196640 | tf_op jit(solution)/shard_map/ppermute | solution.py:108
  167.5 4.3 %collective-permute-start.33 = (bf16[112,768]{1,0:T(8,128)(2,1)S(1)}, bf16[112,768]{1,0:T(8,128)(2,1)S(1)}, u32[]{:S(2)}, u32[]{:S(2)}) collective-permute-start(bf16[112,768]{1,0:T(8,128)(2,1)S(1)} %get-tuple-element.109.refs_4_.refs_0_), channel_id=1, source_target_pairs={{0,1},{1,0},{2,3},{3,2},{4,5},{5,4},{6,7},{7,6},{8,9},{9,8},{10,11... | collective-permute-start | bytes 516104 | tf_op jit(solution)/shard_map/ppermute | solution.py:108
  175.5 2.9 collective-permute-done.36.refs_1_
  184.8 3.8 %collective-permute-done.34.refs_2_ = bf16[112,768]{1,0:T(8,128)(2,1)S(1)} collective-permute-done((bf16[112,768]{1,0:T(8,128)(2,1)S(1)}, bf16[112,768]{1,0:T(8,128)(2,1)S(1)}, u32[]{:S(2)}, u32[]{:S(2)}) %collective-permute-start.34) | collective-permute-done | bytes 172064 | tf_op jit(solution)/shard_map/ppermute | solution.py:108
  189.5 81.5 %parted.1 = (f32[288,768]{1,0:T(8,128)}, f32[576,768]{1,0:T(8,128)}) custom-call(f32[1152,768]{1,0:T(8,128)} %all-reduce.2.cloned.1.call-done.in_ref), custom_call_target="tpu_custom_call" | custom-call | tf_op jit(solution)/shard_map/parted/pallas_call | solution.py:747
  271.3 4.0 %collective-permute-start.16 = (bf16[112,768]{1,0:T(8,128)(2,1)S(1)}, bf16[112,768]{1,0:T(8,128)(2,1)S(1)}, u32[]{:S(2)}, u32[]{:S(2)}) collective-permute-start(bf16[112,768]{1,0:T(8,128)(2,1)S(1)} %total_of.4.refs_0_), channel_id=1, source_target_pairs={{0,1},{1,0},{2,3},{3,2},{4,5},{5,4},{6,7},{7,6},{8,9},{9,8},{10,11... | collective-permute-start | bytes 516104 | tf_op jit(solution)/shard_map/ppermute | solution.py:108
  275.4 5.1 %collective-permute-done.16.refs_1_ = bf16[112,768]{1,0:T(8,128)(2,1)S(1)} collective-permute-done((bf16[112,768]{1,0:T(8,128)(2,1)S(1)}, bf16[112,768]{1,0:T(8,128)(2,1)S(1)}, u32[]{:S(2)}, u32[]{:S(2)}) %collective-permute-start.16) | collective-permute-done | bytes 172064 | tf_op jit(solution)/shard_map/ppermute | solution.py:108
  280.5 3.4 %collective-permute-done.18.refs_3_ = bf16[112,768]{1,0:T(8,128)(2,1)S(1)} collective-permute-done((bf16[112,768]{1,0:T(8,128)(2,1)S(1)}, bf16[112,768]{1,0:T(8,128)(2,1)S(1)}, u32[]{:S(2)}, u32[]{:S(2)}) %collective-permute-start.18) | collective-permute-done | bytes 172064 | tf_op jit(solution)/shard_map/ppermute | solution.py:108
  (97 shorter events, 61.7 us)
Async XLA Ops:
  7.2 54.4 %all-gather.2.cloned.1.call-start = ((), (), s32[]{:S(2)}) async-start(), calls=%async_computation | async-start | bytes 1474560 | tf_op jit(solution)/shard_map/all_gather | solution.py:1011
  14.6 12.9 %collective-permute-start.3 = (bf16[384,448]{1,0:T(8,128)(2,1)S(1)}, bf16[384,448]{1,0:T(8,128)(2,1)S(1)}, u32[]{:S(2)}, u32[]{:S(2)}) collective-permute-start(bf16[384,448]{1,0:T(8,128)(2,1)S(1)} %get-tuple-element.65.refs_4_.refs_10_), channel_id=1, source_target_pairs={{0,8},{4,12},{8,0},{12,4},{16,24},{20,28},{24,16},{28,20},{1,9},{5... | collective-permute-start | bytes 1032200 | tf_op jit(solution)/shard_map/ppermute | solution.py:108
  17.6 19.0 %collective-permute-start.1 = (bf16[384,448]{1,0:T(8,128)(2,1)S(1)}, bf16[384,448]{1,0:T(8,128)(2,1)S(1)}, u32[]{:S(2)}, u32[]{:S(2)}) collective-permute-start(bf16[384,448]{1,0:T(8,128)(2,1)S(1)} %get-tuple-element.65.refs_4_.refs_10_), channel_id=1, source_target_pairs={{0,16},{4,20},{8,24},{12,28},{16,0},{20,4},{24,8},{28,12},{1,17},{... | collective-permute-start | bytes 1032200 | tf_op jit(solution)/shard_map/ppermute | solution.py:108
  19.1 17.5 %collective-permute-start.2 = (bf16[384,448]{1,0:T(8,128)(2,1)S(1)}, bf16[384,448]{1,0:T(8,128)(2,1)S(1)}, u32[]{:S(2)}, u32[]{:S(2)}) collective-permute-start(bf16[384,448]{1,0:T(8,128)(2,1)S(1)} %get-tuple-element.65.refs_4_.refs_10_), channel_id=1, source_target_pairs={{0,24},{4,28},{8,16},{12,20},{16,8},{20,12},{24,0},{28,4},{1,25},{... | collective-permute-start | bytes 1032200 | tf_op jit(solution)/shard_map/ppermute | solution.py:108
  42.8 10.8 %collective-permute-start.5 = (bf16[192,448]{1,0:T(8,128)(2,1)S(1)}, bf16[192,448]{1,0:T(8,128)(2,1)S(1)}, u32[]{:S(2)}, u32[]{:S(2)}) collective-permute-start(bf16[192,448]{1,0:T(8,128)(2,1)S(1)} %get-tuple-element.68.refs_6_.refs_2_), channel_id=1, source_target_pairs={{0,1},{1,0},{2,3},{3,2},{4,5},{5,4},{6,7},{7,6},{8,9},{9,8},{10,11... | collective-permute-start | bytes 516104 | tf_op jit(solution)/shard_map/ppermute | solution.py:108
  44.5 17.1 %collective-permute-start.6 = (bf16[192,448]{1,0:T(8,128)(2,1)S(1)}, bf16[192,448]{1,0:T(8,128)(2,1)S(1)}, u32[]{:S(2)}, u32[]{:S(2)}) collective-permute-start(bf16[192,448]{1,0:T(8,128)(2,1)S(1)} %get-tuple-element.68.refs_6_.refs_2_), channel_id=1, source_target_pairs={{0,2},{1,3},{2,0},{3,1},{4,6},{5,7},{6,4},{7,5},{8,10},{9,11},{10,... | collective-permute-start | bytes 516104 | tf_op jit(solution)/shard_map/ppermute | solution.py:108
  47.1 14.5 %collective-permute-start.7 = (bf16[192,448]{1,0:T(8,128)(2,1)S(1)}, bf16[192,448]{1,0:T(8,128)(2,1)S(1)}, u32[]{:S(2)}, u32[]{:S(2)}) collective-permute-start(bf16[192,448]{1,0:T(8,128)(2,1)S(1)} %get-tuple-element.68.refs_6_.refs_2_), channel_id=1, source_target_pairs={{0,3},{1,2},{2,1},{3,0},{4,7},{5,6},{6,5},{7,4},{8,11},{9,10},{10,... | collective-permute-start | bytes 516104 | tf_op jit(solution)/shard_map/ppermute | solution.py:108
  70.4 15.1 %collective-permute-start.9 = (bf16[112,768]{1,0:T(8,128)(2,1)}, bf16[112,768]{1,0:T(8,128)(2,1)S(1)}, u32[]{:S(2)}, u32[]{:S(2)}) collective-permute-start(bf16[112,768]{1,0:T(8,128)(2,1)} %get-tuple-element.76), channel_id=1, source_target_pairs={{0,1},{1,0},{2,3},{3,2},{4,5},{5,4},{6,7},{7,6},{8,9},{9,8},{10,11... | collective-permute-start | bytes 516104 | tf_op jit(solution)/shard_map/ppermute | solution.py:108
  74.3 15.5 %collective-permute-start.10 = (bf16[112,768]{1,0:T(8,128)(2,1)}, bf16[112,768]{1,0:T(8,128)(2,1)S(1)}, u32[]{:S(2)}, u32[]{:S(2)}) collective-permute-start(bf16[112,768]{1,0:T(8,128)(2,1)} %get-tuple-element.77), channel_id=1, source_target_pairs={{0,2},{1,3},{2,0},{3,1},{4,6},{5,7},{6,4},{7,5},{8,10},{9,11},{10,... | collective-permute-start | bytes 516104 | tf_op jit(solution)/shard_map/ppermute | solution.py:108
  75.3 14.5 %collective-permute-start.11 = (bf16[112,768]{1,0:T(8,128)(2,1)}, bf16[112,768]{1,0:T(8,128)(2,1)S(1)}, u32[]{:S(2)}, u32[]{:S(2)}) collective-permute-start(bf16[112,768]{1,0:T(8,128)(2,1)} %get-tuple-element.78), channel_id=1, source_target_pairs={{0,3},{1,2},{2,1},{3,0},{4,7},{5,6},{6,5},{7,4},{8,11},{9,10},{10,... | collective-permute-start | bytes 516104 | tf_op jit(solution)/shard_map/ppermute | solution.py:108
  84.3 105.2 %all-reduce.2.cloned.1.call-start = ((), (), s32[]{:S(2)}) async-start(), calls=%async_computation.1 | async-start | bytes 7077888 | tf_op jit(solution)/shard_map/psum | solution.py:1031
  84.3 18.8 %collective-permute-start.8 = (bf16[224,768]{1,0:T(8,128)(2,1)}, bf16[224,768]{1,0:T(8,128)(2,1)S(1)}, u32[]{:S(2)}, u32[]{:S(2)}) collective-permute-start(bf16[224,768]{1,0:T(8,128)(2,1)} %get-tuple-element.74), channel_id=1, source_target_pairs={{0,1},{1,0},{2,3},{3,2},{4,5},{5,4},{6,7},{7,6},{8,9},{9,8},{10,11... | collective-permute-start | bytes 1032200 | tf_op jit(solution)/shard_map/ppermute | solution.py:108
  107.6 23.5 %collective-permute-start.23 = (bf16[384,448]{1,0:T(8,128)(2,1)S(1)}, bf16[384,448]{1,0:T(8,128)(2,1)S(1)}, u32[]{:S(2)}, u32[]{:S(2)}) collective-permute-start(bf16[384,448]{1,0:T(8,128)(2,1)S(1)} %get-tuple-element.96), channel_id=1, source_target_pairs={{0,24},{4,28},{8,16},{12,20},{16,8},{20,12},{24,0},{28,4},{1,25},{... | collective-permute-start | bytes 1032200 | tf_op jit(solution)/shard_map/ppermute | solution.py:108
  113.9 17.4 %collective-permute-start.24 = (bf16[384,448]{1,0:T(8,128)(2,1)S(1)}, bf16[384,448]{1,0:T(8,128)(2,1)S(1)}, u32[]{:S(2)}, u32[]{:S(2)}) collective-permute-start(bf16[384,448]{1,0:T(8,128)(2,1)S(1)} %get-tuple-element.97), channel_id=1, source_target_pairs={{0,16},{4,20},{8,24},{12,28},{16,0},{20,4},{24,8},{28,12},{1,17},{... | collective-permute-start | bytes 1032200 | tf_op jit(solution)/shard_map/ppermute | solution.py:108
  115.4 12.1 %collective-permute-start.27 = (bf16[112,768]{1,0:T(8,128)(2,1)S(1)}, bf16[112,768]{1,0:T(8,128)(2,1)S(1)}, u32[]{:S(2)}, u32[]{:S(2)}) collective-permute-start(bf16[112,768]{1,0:T(8,128)(2,1)S(1)} %copy-done), channel_id=1, source_target_pairs={{0,2},{1,3},{2,0},{3,1},{4,6},{5,7},{6,4},{7,5},{8,10},{9,11},{10,... | collective-permute-start | bytes 516104 | tf_op jit(solution)/shard_map/ppermute | solution.py:108
  116.5 14.6 %collective-permute-start.15 = (bf16[112,768]{1,0:T(8,128)(2,1)S(1)}, bf16[112,768]{1,0:T(8,128)(2,1)S(1)}, u32[]{:S(2)}, u32[]{:S(2)}) collective-permute-start(bf16[112,768]{1,0:T(8,128)(2,1)S(1)} %get-tuple-element.84), channel_id=1, source_target_pairs={{0,2},{1,3},{2,0},{3,1},{4,6},{5,7},{6,4},{7,5},{8,10},{9,11},{10,... | collective-permute-start | bytes 516104 | tf_op jit(solution)/shard_map/ppermute | solution.py:108
  119.6 23.1 %collective-permute-start.25 = (bf16[384,448]{1,0:T(8,128)(2,1)S(1)}, bf16[384,448]{1,0:T(8,128)(2,1)S(1)}, u32[]{:S(2)}, u32[]{:S(2)}) collective-permute-start(bf16[384,448]{1,0:T(8,128)(2,1)S(1)} %get-tuple-element.98), channel_id=1, source_target_pairs={{0,8},{4,12},{8,0},{12,4},{16,24},{20,28},{24,16},{28,20},{1,9},{5... | collective-permute-start | bytes 1032200 | tf_op jit(solution)/shard_map/ppermute | solution.py:108
  131.1 8.9 %collective-permute-start.28 = (bf16[112,768]{1,0:T(8,128)(2,1)S(1)}, bf16[112,768]{1,0:T(8,128)(2,1)S(1)}, u32[]{:S(2)}, u32[]{:S(2)}) collective-permute-start(bf16[112,768]{1,0:T(8,128)(2,1)S(1)} %collective-permute-done.27.refs_10_.refs_5_), channel_id=1, source_target_pairs={{0,1},{1,0},{2,3},{3,2},{4,5},{5,4},{6,7},{7,6},{8,9},{9,8},{10,11... | collective-permute-start | bytes 516104 | tf_op jit(solution)/shard_map/ppermute | solution.py:108
  131.2 8.8 %collective-permute-start.22 = (bf16[192,448]{1,0:T(8,128)(2,1)S(1)}, bf16[192,448]{1,0:T(8,128)(2,1)S(1)}, u32[]{:S(2)}, u32[]{:S(2)}) collective-permute-start(bf16[192,448]{1,0:T(8,128)(2,1)S(1)} %get-tuple-element.94), channel_id=1, source_target_pairs={{0,4},{4,0},{8,12},{12,8},{16,20},{20,16},{24,28},{28,24},{1,5},{5... | collective-permute-start | bytes 516104 | tf_op jit(solution)/shard_map/ppermute | solution.py:108
  131.2 11.4 %collective-permute-start.17 = (bf16[112,768]{1,0:T(8,128)(2,1)S(1)}, bf16[112,768]{1,0:T(8,128)(2,1)S(1)}, u32[]{:S(2)}, u32[]{:S(2)}) collective-permute-start(bf16[112,768]{1,0:T(8,128)(2,1)S(1)} %total_of.4.refs_0_), channel_id=1, source_target_pairs={{0,2},{1,3},{2,0},{3,1},{4,6},{5,7},{6,4},{7,5},{8,10},{9,11},{10,... | collective-permute-start | bytes 516104 | tf_op jit(solution)/shard_map/ppermute | solution.py:108
  148.7 10.6 %collective-permute-start.29 = (bf16[128,768]{1,0:T(8,128)(2,1)S(1)}, bf16[128,768]{1,0:T(8,128)(2,1)S(1)}, u32[]{:S(2)}, u32[]{:S(2)}) collective-permute-start(bf16[128,768]{1,0:T(8,128)(2,1)S(1)} %get-tuple-element.101), channel_id=1, source_target_pairs={{0,1},{1,0},{2,3},{3,2},{4,5},{5,4},{6,7},{7,6},{8,9},{9,8},{10,11... | collective-permute-start | bytes 589832 | tf_op jit(solution)/shard_map/ppermute | solution.py:108
  148.8 17.2 %collective-permute-start.30 = (bf16[128,768]{1,0:T(8,128)(2,1)S(1)}, bf16[128,768]{1,0:T(8,128)(2,1)S(1)}, u32[]{:S(2)}, u32[]{:S(2)}) collective-permute-start(bf16[128,768]{1,0:T(8,128)(2,1)S(1)} %get-tuple-element.102), channel_id=1, source_target_pairs={{0,2},{1,3},{2,0},{3,1},{4,6},{5,7},{6,4},{7,5},{8,10},{9,11},{10,... | collective-permute-start | bytes 589832 | tf_op jit(solution)/shard_map/ppermute | solution.py:108
  151.1 14.9 %collective-permute-start.31 = (bf16[128,768]{1,0:T(8,128)(2,1)S(1)}, bf16[128,768]{1,0:T(8,128)(2,1)S(1)}, u32[]{:S(2)}, u32[]{:S(2)}) collective-permute-start(bf16[128,768]{1,0:T(8,128)(2,1)S(1)} %get-tuple-element.103), channel_id=1, source_target_pairs={{0,3},{1,2},{2,1},{3,0},{4,7},{5,6},{6,5},{7,4},{8,11},{9,10},{10,... | collective-permute-start | bytes 589832 | tf_op jit(solution)/shard_map/ppermute | solution.py:108
  167.5 16.1 %collective-permute-start.33 = (bf16[112,768]{1,0:T(8,128)(2,1)S(1)}, bf16[112,768]{1,0:T(8,128)(2,1)S(1)}, u32[]{:S(2)}, u32[]{:S(2)}) collective-permute-start(bf16[112,768]{1,0:T(8,128)(2,1)S(1)} %get-tuple-element.109.refs_4_.refs_0_), channel_id=1, source_target_pairs={{0,1},{1,0},{2,3},{3,2},{4,5},{5,4},{6,7},{7,6},{8,9},{9,8},{10,11... | collective-permute-start | bytes 516104 | tf_op jit(solution)/shard_map/ppermute | solution.py:108
  175.2 13.3 %collective-permute-start.34 = (bf16[112,768]{1,0:T(8,128)(2,1)S(1)}, bf16[112,768]{1,0:T(8,128)(2,1)S(1)}, u32[]{:S(2)}, u32[]{:S(2)}) collective-permute-start(bf16[112,768]{1,0:T(8,128)(2,1)S(1)} %get-tuple-element.109.refs_4_.refs_0_), channel_id=1, source_target_pairs={{0,2},{1,3},{2,0},{3,1},{4,6},{5,7},{6,4},{7,5},{8,10},{9,11},{10,... | collective-permute-start | bytes 516104 | tf_op jit(solution)/shard_map/ppermute | solution.py:108
  178.4 10.1 %collective-permute-start.35 = (bf16[112,768]{1,0:T(8,128)(2,1)S(1)}, bf16[112,768]{1,0:T(8,128)(2,1)S(1)}, u32[]{:S(2)}, u32[]{:S(2)}) collective-permute-start(bf16[112,768]{1,0:T(8,128)(2,1)S(1)} %get-tuple-element.109.refs_4_.refs_0_), channel_id=1, source_target_pairs={{0,3},{1,2},{2,1},{3,0},{4,7},{5,6},{6,5},{7,4},{8,11},{9,10},{10,... | collective-permute-start | bytes 516104 | tf_op jit(solution)/shard_map/ppermute | solution.py:108
  181.2 89.8 %collective-permute-start.39 = (bf16[208,384]{1,0:T(8,128)(2,1)S(1)}, bf16[208,384]{1,0:T(8,128)(2,1)S(1)}, u32[]{:S(2)}, u32[]{:S(2)}) collective-permute-start(bf16[208,384]{1,0:T(8,128)(2,1)S(1)} %sum_piece.1.refs_0_), channel_id=1, source_target_pairs={{0,8},{4,12},{8,0},{12,4},{16,24},{20,28},{24,16},{28,20},{1,9},{5... | collective-permute-start | bytes 479240 | tf_op jit(solution)/shard_map/ppermute | solution.py:108
  182.2 88.8 %collective-permute-start.40 = (bf16[208,384]{1,0:T(8,128)(2,1)S(1)}, bf16[208,384]{1,0:T(8,128)(2,1)S(1)}, u32[]{:S(2)}, u32[]{:S(2)}) collective-permute-start(bf16[208,384]{1,0:T(8,128)(2,1)S(1)} %sum_piece.1.refs_0_), channel_id=1, source_target_pairs={{0,16},{4,20},{8,24},{12,28},{16,0},{20,4},{24,8},{28,12},{1,17},{... | collective-permute-start | bytes 479240 | tf_op jit(solution)/shard_map/ppermute | solution.py:108
  183.6 87.4 %collective-permute-start.41 = (bf16[208,384]{1,0:T(8,128)(2,1)S(1)}, bf16[208,384]{1,0:T(8,128)(2,1)S(1)}, u32[]{:S(2)}, u32[]{:S(2)}) collective-permute-start(bf16[208,384]{1,0:T(8,128)(2,1)S(1)} %sum_piece.1.refs_0_), channel_id=1, source_target_pairs={{0,24},{4,28},{8,16},{12,20},{16,8},{20,12},{24,0},{28,4},{1,25},{... | collective-permute-start | bytes 479240 | tf_op jit(solution)/shard_map/ppermute | solution.py:108
  271.2 13.7 %collective-permute-start.42 = (bf16[784,384]{1,0:T(8,128)(2,1)S(1)}, bf16[784,384]{1,0:T(8,128)(2,1)S(1)}, u32[]{:S(2)}, u32[]{:S(2)}) collective-permute-start(bf16[784,384]{1,0:T(8,128)(2,1)S(1)} %collect.1.refs_0_), channel_id=1, source_target_pairs={{0,4},{4,0},{8,12},{12,8},{16,20},{20,16},{24,28},{28,24},{1,5},{5... | collective-permute-start | bytes 1806344 | tf_op jit(solution)/shard_map/ppermute | solution.py:108
  271.3 9.2 %collective-permute-start.16 = (bf16[112,768]{1,0:T(8,128)(2,1)S(1)}, bf16[112,768]{1,0:T(8,128)(2,1)S(1)}, u32[]{:S(2)}, u32[]{:S(2)}) collective-permute-start(bf16[112,768]{1,0:T(8,128)(2,1)S(1)} %total_of.4.refs_0_), channel_id=1, source_target_pairs={{0,1},{1,0},{2,3},{3,2},{4,5},{5,4},{6,7},{7,6},{8,9},{9,8},{10,11... | collective-permute-start | bytes 516104 | tf_op jit(solution)/shard_map/ppermute | solution.py:108
  275.3 8.7 %collective-permute-start.18 = (bf16[112,768]{1,0:T(8,128)(2,1)S(1)}, bf16[112,768]{1,0:T(8,128)(2,1)S(1)}, u32[]{:S(2)}, u32[]{:S(2)}) collective-permute-start(bf16[112,768]{1,0:T(8,128)(2,1)S(1)} %collective-permute-done.17.refs_12_.refs_2_), channel_id=1, source_target_pairs={{0,1},{1,0},{2,3},{3,2},{4,5},{5,4},{6,7},{7,6},{8,9},{9,8},{10,11... | collective-permute-start | bytes 516104 | tf_op jit(solution)/shard_map/ppermute | solution.py:108
  (15 other events, 93.1 us)
Sparse Core Ops, SparseCore 0:
  9.6 33.1 all-gather.1
  88.5 84.3 all-reduce.1

commit v5 on v4

--- a/solution.py
+++ b/solution.py
@@ -2,6 +2,7 @@
 
 import jax
 import jax.numpy as jnp
+import numpy as np
 from jax import lax
 from jax.experimental import pallas as pl
 from jax.experimental.pallas import tpu as pltpu
@@ -44,7 +45,7 @@
     return array if kind in ("v", "free") else pltpu.with_memory_space_constraint(array, pltpu.HBM)
 
 
-def call(name, kernel, ins, outs, scratch=(), mib=16, after=()):
+def call(name, kernel, ins, outs, scratch=(), mib=16, after=(), lazy=False):
     fetched = [i for i, given in enumerate(ins) if given[1] not in ("v", "raw", "free")]
     left = [i for i, out in enumerate(outs) if out[2] == "h"]
 
@@ -72,17 +73,33 @@
             in_refs[i] = buffers[n]
         for copy in copies:
             copy.start()
-        for copy in copies:
-            copy.wait()
-        copies = []
+        coming = dict(zip(fetched, copies))
+        going = {}
         for n, i in enumerate(left):
             spot = len(fetched) + n
-            copies.append(pltpu.make_async_copy(buffers[spot], out_refs[i], sems.at[spot]))
+            going[i] = pltpu.make_async_copy(buffers[spot], out_refs[i], sems.at[spot])
             out_refs[i] = buffers[spot]
-        kernel(*in_refs, *out_refs, *own)
-        for copy in copies:
-            copy.start()
-        for copy in copies:
+        gone = []
+
+        def need(*which):
+            for i in which:
+                if i in coming:
+                    coming.pop(i).wait()
+
+        def give(*which):
+            for i in which:
+                if i in going:
+                    gone.append(going.pop(i))
+                    gone[-1].start()
+
+        if lazy:
+            kernel(need, give, *in_refs, *out_refs, *own)
+        else:
+            need(*fetched)
+            kernel(*in_refs, *out_refs, *own)
+        need(*fetched)
+        give(*left)
+        for copy in gone:
             copy.wait()
 
     spec = lambda kind: VMEM if kind == "v" else HBM
@@ -187,15 +204,14 @@
     return scale * (u - mean_u - unit * mean_un)
 
 
-def project_kernel(width, len_any, roster_any, x_any, w_any, gain_ref, freq_ref, *refs):
+def project_kernel(
+    width, need, give, len_any, roster_any, x_ref, w_ref, gain_ref, freq_ref, *refs
+):
     q_out, kv_out, h_out, cos_out, sin_out = refs[:5]
-    x_ref, w_ref, proj, len_ref, roster_ref, sems = refs[5:]
+    proj, len_ref, roster_ref, sems = refs[5:]
     rows = x_ref.shape[0]
-    x_copy = pltpu.make_async_copy(x_any, x_ref, sems.at[0])
-    w_copy = pltpu.make_async_copy(w_any, w_ref, sems.at[1])
-    x_copy.start()
-    w_copy.start()
-    fetch_docs(len_any, roster_any, len_ref, roster_ref, sems.at[2], sems.at[3])
+    fetch_docs(len_any, roster_any, len_ref, roster_ref, sems.at[0], sems.at[1])
+    need(5)
     ends = doc_bounds(len_ref)
     place = place_row(ends, roster_ref[lax.axis_index("seq")] * rows, rows)
     angles = place * freq_ref[...]
@@ -203,16 +219,19 @@
     sin_table = jnp.sin(angles)
     cos_out[...] = cos_table
     sin_out[...] = sin_table
-    x_copy.wait()
+    give(3, 4)
+    need(2, 4)
+    gain = gain_ref[...].reshape(1, -1)
 
     def strip(i, carry):
         at = pl.ds(i * STRIP, STRIP)
         unit, unused = normed(x_ref[at, :].astype(F32))
-        h_out[at, :] = (unit * gain_ref[...]).astype(BF16)
+        h_out[at, :] = (unit * gain).astype(BF16)
         return carry
 
     lax.fori_loop(0, rows // STRIP, strip, 0)
-    w_copy.wait()
+    give(2)
+    need(3)
     proj[...] = mm(w_ref[...], h_out[...], NT)
     for at in range(0, 2 * width, HDIM):
         low = proj[at : at + HALF, :]
@@ -231,12 +250,11 @@
 def project(doc_lengths, roster, tokens, gain, qkv_t):
     rows, model = tokens.shape
     width = qkv_t.shape[0] // 3
-    freq = ROPE_THETA ** (-(jnp.arange(HALF).astype(F32) * (2.0 / HDIM)))
+    freq = (ROPE_THETA ** -(np.arange(HALF) * (2.0 / HDIM))).astype(np.float32)[:, None]
     return call(
         "project",
         functools.partial(project_kernel, width),
-        [(x, "raw") for x in (doc_lengths, roster, tokens, qkv_t)]
-        + [(gain, "h"), (freq[:, None], "h")],
+        kinds((doc_lengths, roster), "raw") + kinds((tokens, qkv_t, gain, jnp.asarray(freq)), "h"),
         [
             ((width, rows), BF16, "v"),
             ((2 * width, rows), BF16, "v"),
@@ -244,13 +262,10 @@
             ((HALF, rows), F32, "h"),
             ((HALF, rows), F32, "h"),
         ],
-        [
-            pltpu.VMEM((rows, model), BF16),
-            pltpu.VMEM(qkv_t.shape, BF16),
-            pltpu.VMEM((3 * width, rows), F32),
-        ]
+        [pltpu.VMEM((3 * width, rows), F32)]
         + doc_scratch(doc_lengths, roster)
-        + [pltpu.SemaphoreType.DMA((4,))],
+        + [pltpu.SemaphoreType.DMA((2,))],
+        lazy=True,
     )
 
 
@@ -343,19 +358,21 @@
     )
 
 
-def backward_kernel(index, heads, more, last, len_any, roster_any, *refs):
-    q_own, q_pair, g_own, g_pair, o_own, o_pair, t_own, t_pair, kv_ref = refs[:9]
-    refs = refs[9:]
+def backward_kernel(first, count, heads, more, last, len_any, roster_any, *refs):
+    q_own, q_pair, g_own, g_pair, o_own, o_pair, t_own, t_pair = refs[:8]
+    kv_refs, refs = refs[8 : 8 + count], refs[8 + count :]
     if more:
         dq_in, refs = refs[0], refs[1:]
-    outs = refs[: 3 if last else 2]
-    kv, q_aug, delta, dq, dkv, len_ref, roster_ref, sems = refs[len(outs) :]
+    outs, refs = refs[:count], refs[count:]
+    dq_outs, refs = (refs[:2], refs[2:]) if last else (refs[:1], refs[1:])
+    kv, q_aug, delta, dq, dkv, len_ref, roster_ref, sems = refs
     rows = q_own.shape[1]
     width = heads * HDIM
     me = lax.axis_index("seq")
-    copy = pltpu.make_async_copy(kv_ref, kv, sems.at[0])
-    copy.start()
-    fetch_docs(len_any, roster_any, len_ref, roster_ref, sems.at[1], sems.at[2])
+    copies = [pltpu.make_async_copy(kv_refs[j], kv.at[j], sems.at[j]) for j in range(count)]
+    for copy in copies:
+        copy.start()
+    fetch_docs(len_any, roster_any, len_ref, roster_ref, sems.at[count], sems.at[count + 1])
     ends = doc_bounds(len_ref)
     bases = (roster_ref[me] * rows, roster_ref[me ^ 1] * rows)
     for g, (q_ref, g_ref, o_ref) in enumerate(((q_own, g_own, o_own), (q_pair, g_pair, o_pair))):
@@ -372,41 +389,48 @@
         dq[...] = dq_in[...]
     else:
         dq[...] = jnp.zeros_like(dq)
-    dkv[...] = jnp.zeros_like(dkv)
-    key_base = roster_ref[key_row(index, me)] * rows
-    ban = ban_rows(ends, key_base, rows).astype(BF16)
-    copy.wait()
-
-    for g, (g_ref, t_ref) in enumerate(((g_own, t_own), (g_pair, t_pair))):
-
-        @pl.when(meet(ends, bases[g], key_base, rows))
-        def _():
-            for h in range(heads):
-                at = g * heads + h
-                part = slice(h * HDIM, (h + 1) * HDIM)
-                late = slice(width + h * HDIM, width + (h + 1) * HDIM)
-                keys = kv[part, :]
-                scores = mm(jnp.concatenate([keys, ban], axis=0), q_aug[at], TN)
-                probs = jnp.exp(scores - t_ref[h, 0:1, :])
-                prob_grads = mm(kv[late, :], g_ref[part, :], TN)
-                score_grad = (probs * (prob_grads - delta[at, 0:1, :])).astype(BF16)
-                dkv[late, :] += mm(g_ref[part, :], probs.astype(BF16), NT)
-                dkv[part, :] += mm(q_aug[at, :HDIM, :], score_grad, NT)
-                dq[at] += mm(keys, score_grad, NN)
-
-    outs[0][...] = dkv[...].astype(outs[0].dtype)
+    for copy in copies:
+        copy.wait()
+
+    def block(j, carry):
+        key_base = roster_ref[key_row(j + first, me)] * rows
+        ban = ban_rows(ends, key_base, rows).astype(BF16)
+        dkv[j] = jnp.zeros((2 * width, rows), F32)
+        for g, (g_ref, t_ref) in enumerate(((g_own, t_own), (g_pair, t_pair))):
+
+            @pl.when(meet(ends, bases[g], key_base, rows))
+            def _():
+                for h in range(heads):
+                    at = g * heads + h
+                    part = slice(h * HDIM, (h + 1) * HDIM)
+                    late = slice(width + h * HDIM, width + (h + 1) * HDIM)
+                    keys = kv[j, part, :]
+                    scores = mm(jnp.concatenate([keys, ban], axis=0), q_aug[at], TN)
+                    probs = jnp.exp(scores - t_ref[h, 0:1, :])
+                    prob_grads = mm(kv[j, late, :], g_ref[part, :], TN)
+                    score_grad = (probs * (prob_grads - delta[at, 0:1, :])).astype(BF16)
+                    dkv[j, late, :] += mm(g_ref[part, :], probs.astype(BF16), NT)
+                    dkv[j, part, :] += mm(q_aug[at, :HDIM, :], score_grad, NT)
+                    dq[at] += mm(keys, score_grad, NN)
+
+        return carry
+
+    lax.fori_loop(0, count, block, 0)
+    for j in range(count):
+        outs[j][...] = dkv[j].astype(outs[j].dtype)
     if last:
         for h in range(heads):
             part = slice(h * HDIM, (h + 1) * HDIM)
-            outs[1][part, :] = dq[h] * HDIM**-0.5
-            outs[2][part, :] = (dq[heads + h] * HDIM**-0.5).astype(BF16)
+            dq_outs[0][part, :] = dq[h] * HDIM**-0.5
+            dq_outs[1][part, :] = (dq[heads + h] * HDIM**-0.5).astype(BF16)
     else:
-        outs[1][...] = dq[...]
-
-
-def attention_backward(index, last, doc_lengths, roster, held, block, dq=None, after=()):
+        dq_outs[0][...] = dq[...]
+
+
+def attention_backward(first, last, doc_lengths, roster, held, blocks, dq=None, after=()):
     width, rows = held[0].shape
     heads = width // HDIM
+    count = len(blocks)
     given = [] if dq is None else [(dq, "v")]
     if last:
         queries = [((width, rows), F32, "v"), ((width, rows), BF16, "v")]
@@ -414,19 +438,19 @@
         queries = [((2 * heads, HDIM, rows), F32, "v")]
     return call(
         "attention_backward",
-        functools.partial(backward_kernel, index, heads, bool(given), last),
-        [(doc_lengths, "raw"), (roster, "raw")] + kinds(held, "v") + [(block, "free")] + given,
-        [((2 * width, rows), BF16 if index else F32, "v")] + queries,
+        functools.partial(backward_kernel, first, count, heads, bool(given), last),
+        kinds((doc_lengths, roster), "raw") + kinds(held, "v") + kinds(blocks, "free") + given,
+        [((2 * width, rows), BF16 if first else F32, "v")] * count + queries,
         [
-            pltpu.VMEM((2 * width, rows), BF16),
+            pltpu.VMEM((count, 2 * width, rows), BF16),
             pltpu.VMEM((2 * heads, AUG, rows), BF16),
             pltpu.VMEM((2 * heads, 8, rows), F32),
             pltpu.VMEM((2 * heads, HDIM, rows), F32),
-            pltpu.VMEM((2 * width, rows), F32),
+            pltpu.VMEM((count, 2 * width, rows), F32),
         ]
         + doc_scratch(doc_lengths, roster)
-        + [pltpu.SemaphoreType.DMA((3,))],
-        16,
+        + [pltpu.SemaphoreType.DMA((count + 2,))],
+        16 if count < 8 else 40,
         after,
     )
 
@@ -457,7 +481,7 @@
     )
 
 
-def feed_kernel(n_tp, x_ref, cot_ref, gain_ref, in_ref, down_ref, w_ref, *refs):
+def feed_kernel(n_tp, need, give, x_ref, cot_ref, gain_ref, in_ref, down_ref, w_ref, *refs):
     out_refs = refs[:n_tp]
     middle_out, h_out, mixed_out, gate_out, gain_out = refs[n_tp : n_tp + 5]
     part_refs = refs[n_tp + 5 : 2 * n_tp + 5]
@@ -470,8 +494,10 @@
     for k in range(n_tp):
         at = pl.ds(pl.multiple_of((tp ^ k) * width, width), width)
         outs[at, :] = out_refs[k][...]
+    need(5)
     middle_out[...] = mm(outs[...], w_ref[...], TN)
-    mixed_grad[...] = mm(down_ref[...], cot_ref[...], NT)
+    need(0, 2)
+    gain = gain_ref[...].reshape(1, -1)
 
     def strip(i, carry):
         at = pl.ds(i * STRIP, STRIP)
@@ -479,10 +505,14 @@
         middle_out[at, :] = middle
         held, unused = normed(middle)
         unit[at, :] = held
-        h_out[at, :] = (held * gain_ref[...]).astype(BF16)
+        h_out[at, :] = (held * gain).astype(BF16)
         return carry
 
     lax.fori_loop(0, rows // STRIP, strip, 0)
+    give(0, 1)
+    need(1, 4)
+    mixed_grad[...] = mm(down_ref[...], cot_ref[...], NT)
+    need(3)
     gate_up[...] = mm(in_ref[...], h_out[...], NT)
 
     def wave(i, carry):
@@ -500,7 +530,12 @@
         return carry
 
     lax.fori_loop(0, units // 32, wave, 0)
+    give(2, 3)
     grad[...] = mm(gate_out[...], in_ref[...], TN)
+    for k in range(n_tp):
+        at = pl.ds(pl.multiple_of((tp ^ k) * part, part), part)
+        part_refs[k][...] = grad[at, :].astype(part_refs[k].dtype)
+        give(5 + k)
 
     def gains(i, carry):
         at = pl.ds(i * STRIP, STRIP)
@@ -508,9 +543,6 @@
         return carry + jnp.sum(product.reshape(STRIP // 8, 8, -1), axis=0)
 
     gain_out[...] = lax.fori_loop(0, rows // STRIP, gains, jnp.zeros(gain_out.shape, F32))
-    for k in range(n_tp):
-        at = pl.ds(pl.multiple_of((tp ^ k) * part, part), part)
-        part_refs[k][...] = grad[at, :].astype(part_refs[k].dtype)
 
 
 def feed(tokens, cotangent, gain, in_t, w_down, w_full, outs):
@@ -539,22 +571,27 @@
             pltpu.VMEM((rows, model), F32),
         ],
         32,
-    )
-
-
-def branch_kernel(n_tp, middle_ref, cot_ref, gain_ref, w_ref, *refs):
+        lazy=True,
+    )
+
+
+def branch_kernel(n_tp, need, give, middle_ref, cot_ref, gain_ref, w_ref, *refs):
     arrived = refs[:n_tp]
     grad_out, branch_out = refs[n_tp : n_tp + 2]
     piece_refs = refs[n_tp + 2 :]
     width = piece_refs[0].shape[1]
     tp = lax.axis_index("tp")
+    need(0, 1, 2, 4)
     total = arrived[0][...]
     for ref in arrived[1:]:
         total = total + ref[...].astype(F32)
     unit, scale = normed(middle_ref[...])
-    value = cot_ref[...].astype(F32) + norm_back(unit, scale, total, gain_ref[...])
+    gain = gain_ref[...].reshape(1, -1)
+    value = cot_ref[...].astype(F32) + norm_back(unit, scale, total, gain)
     grad_out[...] = value
     branch_out[...] = value.astype(BF16)
+    give(0, 1)
+    need(3)
     for k in range(n_tp):
         at = pl.ds(pl.multiple_of((tp ^ k) * width, width), width)
         piece_refs[k][...] = mm(branch_out[...], w_ref[at, :], NT).astype(BF16)
@@ -573,6 +610,7 @@
         (),
         16,
         after,
+        True,
     )
 
 
@@ -631,7 +669,9 @@
         out_ref[spot + HALF : spot + HDIM, :] = (high * cos_table - low * sin_table).astype(BF16)
 
 
-def unproject_kernel(count, n_tp, x_ref, w_ref, cos_ref, sin_ref, two_ref, dq_ref, dq_back, *refs):
+def unproject_kernel(
+    count, n_tp, need, give, x_ref, w_ref, cos_ref, sin_ref, two_ref, dq_ref, dq_back, *refs
+):
     dkv_refs = refs[:count]
     proj_out = refs[count]
     part_refs = refs[count + 1 : count + 1 + n_tp]
@@ -640,6 +680,7 @@
     part = rows // n_tp
     width = dq_ref.shape[0]
     tp = lax.axis_index("tp")
+    need(2, 3)
     cos_table = cos_ref[...]
     sin_table = sin_ref[...]
     turn_back(proj_out, 0, dq_ref[...] + dq_back[...].astype(F32), cos_table, sin_table)
@@ -649,7 +690,9 @@
     dkv[...] = total
     turn_back(proj_out, width, dkv[:width, :], cos_table, sin_table)
     proj_out[2 * width :, :] = dkv[width:, :].astype(BF16)
+    need(1)
     grad[...] = mm(proj_out[...], w_ref[...], TN)
+    need(0, 4)
 
     def gains(i, carry):
         at = pl.ds(i * STRIP, STRIP)
@@ -681,6 +724,7 @@
         [pltpu.VMEM((rows, model), F32), pltpu.VMEM(dkvs[0].shape, F32)],
         16,
         after,
+        True,
     )
 
 
@@ -692,7 +736,8 @@
     for ref in arrived[1:]:
         total = total + ref[...].astype(F32)
     unit, scale = normed(x_ref[...].astype(F32))
-    value = grad_ref[...] + norm_back(unit, scale, total[:part], gain_ref[...])
+    gain = gain_ref[...].reshape(1, -1)
+    value = grad_ref[...] + norm_back(unit, scale, total[:part], gain)
     out_ref[...] = value.astype(BF16)
     gain_out[...] = total[part : part + 8]
 
@@ -724,34 +769,32 @@
         "early_grads",
         early_kernel,
         kinds((mixed, gate_grad, cotangent, h_two), "h"),
-        [((4 * mixed.shape[0], model), F32, "h")],
+        [((1104, model), F32, "h")],
     )
     return out
 
 
-def part_kernel(in_ref, *refs):
-    out_refs, sems = refs[:-1], refs[-1]
-    copies = []
+def part_kernel(in_any, *refs):
+    out_refs, held, sem = refs[:-2], refs[-2], refs[-1]
+    rows = held.shape[0]
+    copy = pltpu.make_async_copy(in_any.at[pl.ds(0, rows)], held, sem)
+    copy.start()
+    copy.wait()
     at = 0
-    for n, ref in enumerate(out_refs):
-        source = in_ref.at[pl.ds(at, ref.shape[0])]
-        copies.append(pltpu.make_async_copy(source, ref, sems.at[n]))
+    for ref in out_refs:
+        ref[...] = held[at : at + ref.shape[0], :]
         at += ref.shape[0]
-    for copy in copies:
-        copy.start()
-    for copy in copies:
-        copy.wait()
 
 
 def parted(value, sizes):
-    return pl.pallas_call(
+    model = value.shape[1]
+    return call(
+        "parted",
         part_kernel,
-        out_shape=tuple(shaped((size, value.shape[1]), value.dtype) for size in sizes),
-        in_specs=[HBM],
-        out_specs=(HBM,) * len(sizes),
-        scratch_shapes=[pltpu.SemaphoreType.DMA((len(sizes),))],
-        name="parted",
-    )(pin(value, "h"))
+        [(value, "raw")],
+        [((size, model), F32, "h") for size in sizes],
+        [pltpu.VMEM((sum(sizes), model), F32), pltpu.SemaphoreType.DMA],
+    )
 
 
 def late_kernel(n_tp, proj_ref, h_ref, out_ref, *refs):
@@ -771,7 +814,7 @@
         ref[wide:, :] = mm(out_ref[...], branch_full[:, columns], NN).astype(ref.dtype)
 
 
-def late_grads(proj_grad, h_one, out_b, branches):
+def late_grads(proj_grad, h_one, out_b, branches, after):
     rows, model = h_one.shape
     wide = proj_grad.shape[0] + out_b.shape[0]
     return call(
@@ -781,6 +824,8 @@
         + kinds(branches[1:], "v"),
         [((wide, model // 2), F32, "v"), ((wide, model // 2), BF16, "v")],
         [pltpu.VMEM((rows, model), BF16)],
+        16,
+        after,
     )
 
 
@@ -874,8 +919,8 @@
         out_ref[:, columns] = ref[wide : wide + tall, :].astype(F32)
     gains = own_ref[wide + tall :, :].astype(F32) + pair_ref[wide + tall :, :].astype(F32)
     for at, ref in ((0, one_ref), (2, two_ref)):
-        ref[:, :half] = gains[at : at + 1]
-        ref[:, half:] = gains[at + 1 : at + 2]
+        ref[pl.ds(0, half)] = gains[at]
+        ref[pl.ds(half, half)] = gains[at + 1]
 
 
 def finish(own, pair, wide, after=()):
@@ -889,8 +934,8 @@
         [
             ((wide, model), F32, "h"),
             ((tall, model), F32, "h"),
-            ((1, model), F32, "h"),
-            ((1, model), F32, "h"),
+            ((model,), F32, "h"),
+            ((model,), F32, "h"),
         ],
         (),
         16,
@@ -988,8 +1033,6 @@
     count = n_seq // 2
     qkv_t = w_qkv.transpose(1, 2, 0).reshape(3 * width, model)
     in_t = w_in.transpose(1, 2, 0).reshape(2 * units, model)
-    gain_one = gain_one[None]
-    gain_two = gain_two[None]
     over_tp = lambda x, k: swap(x, "tp", k, n_tp)
     over_chips = lambda x, k: swap(x, "seq", 2 * k, n_seq)
     over_cores = lambda x: swap(x, "seq", 1, n_seq)
@@ -1041,16 +1084,9 @@
     totals_all = by_steps(total)
 
     held = (queries, q_pair, out_grad, grad_pair, out_b, out_pair, totals, totals_pair)
-    dkvs = [None] * count
-    dq = None
-    after = [(own, "v")]
-    for j in range(count - 1, 0, -1):
-        terms, dq = attention_backward(j, False, *docs, held, blocks[j], dq, after)
-        after = ()
-        dkvs[j] = over_chips(terms, j)
-    dkv, dq_own, dq_pair = attention_backward(0, True, *docs, held, blocks[0], dq)
-    for j in range(count - 1, 1, -1):
-        dkv = total_of([dkv, dkvs[j]], F32)
+    *terms, dq = attention_backward(1, False, *docs, held, blocks[1:], None, [(own, "v")])
+    dkv, dq_own, dq_pair = attention_backward(0, True, *docs, held, blocks[:1], dq)
+    dkvs = [dkv] + [over_chips(terms[j - 1], j) for j in range(1, count)]
 
     proj_grad, *parts = unproject(
         n_tp,
@@ -1061,34 +1097,34 @@
         gain_two_part,
         dq_own,
         over_cores(dq_pair),
-        [dkv, dkvs[1]],
-        kinds([*branches[1:], totals_all[n_tp // 2]], "v"),
-    )
-    keep, send = late_grads(proj_grad, h_one, out_b, branches)
+        dkvs,
+        [(total, "v")],
+    )
+    layer_out = stack_parts(totals_all)
+    keep, send = late_grads(proj_grad, h_one, out_b, branches, [(totals_all[n_tp // 2], "v")])
     own, *others = spread(count, keep, over_cores(send))
     chip_sum = total_of([own] + [over_chips(others[k - 1], k) for k in range(1, count)], F32)
     input_part, gains = input_side(
         tokens, gain_one, middle_grad, everywhere(parts), [(own, "v")]
     )
     inputs_all = everywhere([input_part] * n_tp)
-    piece = sum_piece(gains, [chip_sum], ())
+    piece = sum_piece(gains, [chip_sum], [(layer_out, "h")])
     input_grad = stack_parts(inputs_all)
     collected = collect(
         [piece] + [over_chips(piece, k) for k in range(1, count)], [(input_grad, "h"), (grad_down, "h")]
     )
-    layer_out = stack_parts(totals_all, [(input_part, "v")])
     grad_qkv, grad_out, grad_one, grad_two = finish(
-        collected, over_cores(collected), 3 * width, [(layer_out, "h")]
+        collected, over_cores(collected), 3 * width
     )
 
     back = lambda x, n: x.reshape(-1, n, model).transpose(2, 0, 1)
     return (
         layer_out,
         input_grad,
-        grad_one[0],
+        grad_one,
         back(grad_qkv, width),
         grad_out,
-        grad_two[0],
+        grad_two,
         back(grad_in, units),
         grad_down,
     )

time: 297 us -> 198 us (0.67)
  Pallas kernels: 136 us -> 57.5 us
  waiting for transfers between devices: 85.4 us -> 67.2 us
  other arithmetic: 3.19 us -> 0 us
    pallas_call x1 -> x0, Pallas kernels: 81.5 us -> none  [parted(): pl.pallas_call(part_kernel, out_shape=tuple((shaped((size, value.shape[1]...]
    ppermute x43, waiting for transfers between devices: 84.6 us -> 66.5 us  [swap(): return lax.ppermute(x, axis, [(i, i ^ hop) for i in range(count)])]
    pallas_call x27 -> x24, Pallas kernels: 55 us -> 57.5 us  [call(): pl.pallas_call(run, out_shape=tuple((shaped(shape, dtype) if kind == 'v'...]
  transfers between devices with their start and end apart: 45 -> 45, of which waited for: 22 -> 18; matrix products, arithmetic and copies ran while one was open for 1% -> 0% of each run, Pallas kernels for 43% -> 24%
where the time goes in v5:
time: 198 us; the launch traced here: 196 us
  waiting for transfers between devices  67.2 us (34%)
  Pallas kernels  57.5 us (29%)
  starting transfers between devices  57.4 us (29%)
  between operations  14.4 us (7%)
    ppermute x43, waiting for transfers between devices, swap(): return lax.ppermute(x, axis, [(i, i ^ hop) for i in range(count)])  66.5 us
    pallas_call x24, Pallas kernels, call(): pl.pallas_call(run, out_shape=tuple((shaped(shape, dtype) if kind == 'v'...  57.5 us
    ppermute x43, starting transfers between devices, swap(): return lax.ppermute(x, axis, [(i, i ^ hop) for i in range(count)])  57.2 us
  transfers between devices with their start and end apart: 45, of which 18 were waited for; matrix products, arithmetic and copies ran while one was open for 0% of the time, Pallas kernels for 24%

profile of v5, /device:TPU:0, one launch (start us, length us, event | category | flops | bytes accessed | tf_op | source)
XLA Modules:
  0.0 196.5 jit_solution(432439538302600527)
XLA Ops:
  7.9 3.8 %project.1 = (bf16[192,448]{1,0:T(8,128)(2,1)S(1)}, bf16[384,448]{1,0:T(8,128)(2,1)S(1)}, bf16[448,768]{1,0:T(8,128)(2,1)}, f32[32,448]{1,0:T(8,128)}, f32[32,448]{1,0:T(8,128)}) custom-call(s32[4]{0:T(128)} %refs_0_.13, s32[8]{0:T(128)} %refs_1_.16, bf16[448,768]{1,0:T(8,128)(2,1)} %refs_0_.15, bf16[576,768]{1,0:T(8,128)(2,1)} %bitcast.12, f32[768]{0:T(1024)} %refs_1_.17, ...), custom_call_target="tpu_custom_call" | custom-call | tf_op jit(solution)/shard_map/project/pallas_call | solution.py:107
  11.7 3.0 %collective-permute-start.3 = (bf16[384,448]{1,0:T(8,128)(2,1)S(1)}, bf16[384,448]{1,0:T(8,128)(2,1)S(1)}, u32[]{:S(2)}, u32[]{:S(2)}) collective-permute-start(bf16[384,448]{1,0:T(8,128)(2,1)S(1)} %get-tuple-element.63.refs_4_.refs_10_), channel_id=1, source_target_pairs={{0,8},{4,12},{8,0},{12,4},{16,24},{20,28},{24,16},{28,20},{1,9},{5... | collective-permute-start | bytes 1032200 | tf_op jit(solution)/shard_map/ppermute | solution.py:125
  17.7 7.0 %collective-permute-done.3.refs_5_.refs_10_ = bf16[384,448]{1,0:T(8,128)(2,1)S(1)} collective-permute-done((bf16[384,448]{1,0:T(8,128)(2,1)S(1)}, bf16[384,448]{1,0:T(8,128)(2,1)S(1)}, u32[]{:S(2)}, u32[]{:S(2)}) %collective-permute-start.3) | collective-permute-done | bytes 344096 | tf_op jit(solution)/shard_map/ppermute | solution.py:125
  24.7 4.2 %attention_forward.2.refs_6_ = f32[6,80,448]{2,1,0:T(8,128)S(1)} custom-call(s32[4]{0:T(128)} %refs_0_.13, s32[8]{0:T(128)} %refs_1_.16, bf16[192,448]{1,0:T(8,128)(2,1)S(1)} %get-tuple-element.62.refs_2_, bf16[192,448]{1,0:T(8,128)(2,1)S(1)} %collective-permute-done.refs_3_, bf16[384,448]{1,0:T(8,128)(2,1)S(1)} %get-tuple-element.63.refs_4_.refs_10_, ...), custom_call_target="tpu_custom_call" | custom-call | tf_op jit(solution)/shard_map/attention_forward/pallas_call | solution.py:107
  28.9 4.8 %collective-permute-done.1.refs_4_.refs_11_ = bf16[384,448]{1,0:T(8,128)(2,1)S(1)} collective-permute-done((bf16[384,448]{1,0:T(8,128)(2,1)S(1)}, bf16[384,448]{1,0:T(8,128)(2,1)S(1)}, u32[]{:S(2)}, u32[]{:S(2)}) %collective-permute-start.1) | collective-permute-done | bytes 344096 | tf_op jit(solution)/shard_map/ppermute | solution.py:125
  33.7 4.2 %attention_forward.3 = (f32[3,80,448]{2,1,0:T(8,128)S(1)}, f32[3,80,448]{2,1,0:T(8,128)S(1)}) custom-call(s32[4]{0:T(128)} %refs_0_.13, s32[8]{0:T(128)} %refs_1_.16, bf16[192,448]{1,0:T(8,128)(2,1)S(1)} %get-tuple-element.62.refs_2_, bf16[192,448]{1,0:T(8,128)(2,1)S(1)} %collective-permute-done.refs_3_, ...), custom_call_target="tpu_custom_call" | custom-call | tf_op jit(solution)/shard_map/attention_forward/pallas_call | solution.py:107
  41.6 2.6 %collective-permute-start.6 = (bf16[192,448]{1,0:T(8,128)(2,1)S(1)}, bf16[192,448]{1,0:T(8,128)(2,1)S(1)}, u32[]{:S(2)}, u32[]{:S(2)}) collective-permute-start(bf16[192,448]{1,0:T(8,128)(2,1)S(1)} %get-tuple-element.66.refs_6_.refs_2_), channel_id=1, source_target_pairs={{0,2},{1,3},{2,0},{3,1},{4,6},{5,7},{6,4},{7,5},{8,10},{9,11},{10,... | collective-permute-start | bytes 516104 | tf_op jit(solution)/shard_map/ppermute | solution.py:125
  44.4 6.4 %collective-permute-done.5.refs_7_ = bf16[192,448]{1,0:T(8,128)(2,1)S(1)} collective-permute-done((bf16[192,448]{1,0:T(8,128)(2,1)S(1)}, bf16[192,448]{1,0:T(8,128)(2,1)S(1)}, u32[]{:S(2)}, u32[]{:S(2)}) %collective-permute-start.5) | collective-permute-done | bytes 172064 | tf_op jit(solution)/shard_map/ppermute | solution.py:125
  50.8 7.9 %collective-permute-done.6.refs_8_ = bf16[192,448]{1,0:T(8,128)(2,1)S(1)} collective-permute-done((bf16[192,448]{1,0:T(8,128)(2,1)S(1)}, bf16[192,448]{1,0:T(8,128)(2,1)S(1)}, u32[]{:S(2)}, u32[]{:S(2)}) %collective-permute-start.6) | collective-permute-done | bytes 172064 | tf_op jit(solution)/shard_map/ppermute | solution.py:125
  58.8 8.0 %feed.1 = (f32[448,768]{1,0:T(8,128)}, bf16[448,768]{1,0:T(8,128)(2,1)}, bf16[288,448]{1,0:T(8,128)(2,1)}, bf16[576,448]{1,0:T(8,128)(2,1)}, f32[8,768]{1,0:T(8,...) custom-call(bf16[448,768]{1,0:T(8,128)(2,1)} %refs_0_.15, ...), custom_call_target="tpu_custom_call" | custom-call | tf_op jit(solution)/shard_map/feed/pallas_call | solution.py:107
  66.7 3.9 %collective-permute-start.9 = (bf16[112,768]{1,0:T(8,128)(2,1)}, bf16[112,768]{1,0:T(8,128)(2,1)S(1)}, u32[]{:S(2)}, u32[]{:S(2)}) collective-permute-start(bf16[112,768]{1,0:T(8,128)(2,1)} %get-tuple-element.74), channel_id=1, source_target_pairs={{0,1},{1,0},{2,3},{3,2},{4,5},{5,4},{6,7},{7,6},{8,9},{9,8},{10,11... | collective-permute-start | bytes 516104 | tf_op jit(solution)/shard_map/ppermute | solution.py:125
  73.1 4.2 %early_grads.1.refs_3_ = f32[1104,768]{1,0:T(8,128)} custom-call(bf16[288,448]{1,0:T(8,128)(2,1)} %get-tuple-element.67.refs_0_, bf16[576,448]{1,0:T(8,128)(2,1)} %get-tuple-element.69.refs_1_, bf16[448,768]{1,0:T(8,128)(2,1)} %refs_1_.14, bf16[448,768]{1,0:T(8,128)(2,1)} %get-tuple-element.70.refs_3_), custom_call_target="tpu_custom_call" | custom-call | tf_op jit(solution)/shard_map/early_grads/pallas_call | solution.py:107
  77.3 3.2 %down.1 = (f32[224,768]{1,0:T(8,128)}, bf16[224,768]{1,0:T(8,128)(2,1)}) custom-call(bf16[288,448]{1,0:T(8,128)(2,1)} %get-tuple-element.67.refs_0_, bf16[288,768]{1,0:T(8,128)(2,1)} %refs_1_.13, f32[448,768]{1,0:T(8,128)} %get-tuple-element.68.refs_2_.refs_0_, f32[1104,768]{1,0:T(8,128)} %early_grads.1.refs_3_), custom_call_target="tpu_custom_call" | custom-call | tf_op jit(solution)/shard_map/down/pallas_call | solution.py:107
  81.9 4.2 %collective-permute-done.10.refs_6_ = bf16[112,768]{1,0:T(8,128)(2,1)S(1)} collective-permute-done((bf16[112,768]{1,0:T(8,128)(2,1)}, bf16[112,768]{1,0:T(8,128)(2,1)S(1)}, u32[]{:S(2)}, u32[]{:S(2)}) %collective-permute-start.10) | collective-permute-done | bytes 172064 | tf_op jit(solution)/shard_map/ppermute | solution.py:125
  86.2 2.7 %branch.1 = (f32[112,768]{1,0:T(8,128)}, bf16[112,768]{1,0:T(8,128)(2,1)}, bf16[112,192]{1,0:T(8,128)(2,1)S(1)}, bf16[112,192]{1,0:T(8,128)(2,1)S(1)}, bf16[112,...) custom-call(f32[448,768]{1,0:T(8,128)} %get-tuple-element.68.refs_2_.refs_0_, bf16[448,768]{1,0:T(8,128)(2,1)} %refs_1_.14, ...), custom_call_target="tpu_custom_call" | custom-call | tf_op jit(solution)/shard_map/branch/pallas_call | solution.py:107
  88.9 2.5 %collective-permute-start.12 = (bf16[112,192]{1,0:T(8,128)(2,1)S(1)}, bf16[112,192]{1,0:T(8,128)(2,1)S(1)}, u32[]{:S(2)}, u32[]{:S(2)}) collective-permute-start(bf16[112,192]{1,0:T(8,128)(2,1)S(1)} %get-tuple-element.78), channel_id=1, source_target_pairs={{0,1},{1,0},{2,3},{3,2},{4,5},{5,4},{6,7},{7,6},{8,9},{9,8},{10,11... | collective-permute-start | bytes 129032 | tf_op jit(solution)/shard_map/ppermute | solution.py:125
  94.4 3.0 %collective-permute-done.13.refs_2_ = bf16[112,192]{1,0:T(8,128)(2,1)S(1)} collective-permute-done((bf16[112,192]{1,0:T(8,128)(2,1)S(1)}, bf16[112,192]{1,0:T(8,128)(2,1)S(1)}, u32[]{:S(2)}, u32[]{:S(2)}) %collective-permute-start.13) | collective-permute-done | bytes 43040 | tf_op jit(solution)/shard_map/ppermute | solution.py:125
  101.6 5.5 %attention_backward.2 = (bf16[384,448]{1,0:T(8,128)(2,1)S(1)}, bf16[384,448]{1,0:T(8,128)(2,1)S(1)}, bf16[384,448]{1,0:T(8,128)(2,1)S(1)}, f32[6,64,448]{2,1,0:T(8,128)S(1)}) custom-call(s32[4]{0:T(128)} %refs_0_.13, s32[8]{0:T(128)} %refs_1_.16, bf16[192,448]{1,0:T(8,128)(2,1)S(1)} %get-tuple-element.62.refs_2_, ...), custom_call_target="tpu_custom_call" | custom-call | tf_op jit(solution)/shard_map/attention_backward/pallas_call | solution.py:107
  107.2 3.1 %collective-permute-start.24 = (bf16[384,448]{1,0:T(8,128)(2,1)S(1)}, bf16[384,448]{1,0:T(8,128)(2,1)S(1)}, u32[]{:S(2)}, u32[]{:S(2)}) collective-permute-start(bf16[384,448]{1,0:T(8,128)(2,1)S(1)} %get-tuple-element.93), channel_id=1, source_target_pairs={{0,16},{4,20},{8,24},{12,28},{16,0},{20,4},{24,8},{28,12},{1,17},{... | collective-permute-start | bytes 1032200 | tf_op jit(solution)/shard_map/ppermute | solution.py:125
  113.6 5.0 %attention_backward.3 = (f32[384,448]{1,0:T(8,128)S(1)}, f32[192,448]{1,0:T(8,128)S(1)}, bf16[192,448]{1,0:T(8,128)(2,1)S(1)}) custom-call(s32[4]{0:T(128)} %refs_0_.13, s32[8]{0:T(128)} %refs_1_.16, bf16[192,448]{1,0:T(8,128)(2,1)S(1)} %get-tuple-element.62.refs_2_, bf16[192,448]{1,0:T(8,128)(2,1)S(1)} %collective-permute-done.refs_3_, ...), custom_call_target="tpu_custom_call" | custom-call | tf_op jit(solution)/shard_map/attention_backward/pallas_call | solution.py:107
  118.6 3.1 %collective-permute-start.22 = (bf16[192,448]{1,0:T(8,128)(2,1)S(1)}, bf16[192,448]{1,0:T(8,128)(2,1)S(1)}, u32[]{:S(2)}, u32[]{:S(2)}) collective-permute-start(bf16[192,448]{1,0:T(8,128)(2,1)S(1)} %get-tuple-element.90), channel_id=1, source_target_pairs={{0,4},{4,0},{8,12},{12,8},{16,20},{20,16},{24,28},{28,24},{1,5},{5... | collective-permute-start | bytes 516104 | tf_op jit(solution)/shard_map/ppermute | solution.py:125
  123.0 2.1 %collective-permute-start.31 = (bf16[112,768]{1,0:T(8,128)(2,1)S(1)}, bf16[112,768]{1,0:T(8,128)(2,1)S(1)}, u32[]{:S(2)}, u32[]{:S(2)}) collective-permute-start(bf16[112,768]{1,0:T(8,128)(2,1)S(1)} %collective-permute-done.30.refs_5_), channel_id=1, source_target_pairs={{0,1},{1,0},{2,3},{3,2},{4,5},{5,4},{6,7},{7,6},{8,9},{9,8},{10,11... | collective-permute-start | bytes 516104 | tf_op jit(solution)/shard_map/ppermute | solution.py:125
  125.2 7.2 %collective-permute-done.24.refs_9_ = bf16[384,448]{1,0:T(8,128)(2,1)S(1)} collective-permute-done((bf16[384,448]{1,0:T(8,128)(2,1)S(1)}, bf16[384,448]{1,0:T(8,128)(2,1)S(1)}, u32[]{:S(2)}, u32[]{:S(2)}) %collective-permute-start.24) | collective-permute-done | bytes 344096 | tf_op jit(solution)/shard_map/ppermute | solution.py:125
  134.1 4.1 %unproject.1 = (bf16[576,448]{1,0:T(8,128)(2,1)S(1)}, f32[128,768]{1,0:T(8,128)S(1)}, bf16[128,768]{1,0:T(8,128)(2,1)S(1)}, bf16[128,768]{1,0:T(8,128)(2,1)S(1)}, bf16[128,768]{1,0:T(8,128)(2,1)S(1)}) custom-call(bf16[448,768]{1,0:T(8,128)(2,1)} %refs_0_.15, bf16[576,768]{1,0:T(8,128)(2,1)} %bitcast.13, f32[32,448]{1,0:T(8,128)} %get-tuple-element.84.refs_2_, ...), custom_call_target="tpu_custom_call" | custom-call | tf_op jit(solution)/shard_map/unproject/pallas_call | solution.py:107
  138.2 2.2 %late_grads.1 = (f32[768,384]{1,0:T(8,128)S(1)}, bf16[768,384]{1,0:T(8,128)(2,1)S(1)}) custom-call(bf16[576,448]{1,0:T(8,128)(2,1)S(1)} %get-tuple-element.99.refs_0_, bf16[448,768]{1,0:T(8,128)(2,1)} %get-tuple-element.100.refs_1_, bf16[192,448]{1,0:T(8,128)(2,1)S(1)} %get-tuple-element.66.refs_6_.refs_2_, bf16[112,768]{1,0:T(8,128)(2,1)} %get-tuple-element.101.refs_3_, ...), custom_call_target="tpu_custom_call" | custom-call | tf_op jit(solution)/shard_map/late_grads/pallas_call | solution.py:107
  147.5 4.7 %collective-permute-done.26.refs_4_ = bf16[128,768]{1,0:T(8,128)(2,1)S(1)} collective-permute-done((bf16[128,768]{1,0:T(8,128)(2,1)S(1)}, bf16[128,768]{1,0:T(8,128)(2,1)S(1)}, u32[]{:S(2)}, u32[]{:S(2)}) %collective-permute-start.26) | collective-permute-done | bytes 196640 | tf_op jit(solution)/shard_map/ppermute | solution.py:125
  152.2 7.0 %collective-permute-done.27.refs_5_ = bf16[128,768]{1,0:T(8,128)(2,1)S(1)} collective-permute-done((bf16[128,768]{1,0:T(8,128)(2,1)S(1)}, bf16[128,768]{1,0:T(8,128)(2,1)S(1)}, u32[]{:S(2)}, u32[]{:S(2)}) %collective-permute-start.27) | collective-permute-done | bytes 196640 | tf_op jit(solution)/shard_map/ppermute | solution.py:125
  160.7 3.7 %collective-permute-start.33 = (bf16[112,768]{1,0:T(8,128)(2,1)S(1)}, bf16[112,768]{1,0:T(8,128)(2,1)S(1)}, u32[]{:S(2)}, u32[]{:S(2)}) collective-permute-start(bf16[112,768]{1,0:T(8,128)(2,1)S(1)} %get-tuple-element.105.refs_0_), channel_id=1, source_target_pairs={{0,1},{1,0},{2,3},{3,2},{4,5},{5,4},{6,7},{7,6},{8,9},{9,8},{10,11... | collective-permute-start | bytes 516104 | tf_op jit(solution)/shard_map/ppermute | solution.py:125
  164.9 2.0 %collective-permute-start.37 = (bf16[192,384]{1,0:T(8,128)(2,1)S(1)}, bf16[192,384]{1,0:T(8,128)(2,1)S(1)}, u32[]{:S(2)}, u32[]{:S(2)}) collective-permute-start(bf16[192,384]{1,0:T(8,128)(2,1)S(1)} %get-tuple-element.108), channel_id=1, source_target_pairs={{0,16},{4,20},{8,24},{12,28},{16,0},{20,4},{24,8},{28,12},{1,17},{... | collective-permute-start | bytes 442376 | tf_op jit(solution)/shard_map/ppermute | solution.py:125
  168.9 3.3 %collective-permute-done.36.refs_1_ = bf16[192,384]{1,0:T(8,128)(2,1)S(1)} collective-permute-done((bf16[192,384]{1,0:T(8,128)(2,1)S(1)}, bf16[192,384]{1,0:T(8,128)(2,1)S(1)}, u32[]{:S(2)}, u32[]{:S(2)}) %collective-permute-start.36) | collective-permute-done | bytes 147488 | tf_op jit(solution)/shard_map/ppermute | solution.py:125
  172.3 3.3 %collective-permute-start.35 = (bf16[112,768]{1,0:T(8,128)(2,1)S(1)}, bf16[112,768]{1,0:T(8,128)(2,1)S(1)}, u32[]{:S(2)}, u32[]{:S(2)}) collective-permute-start(bf16[112,768]{1,0:T(8,128)(2,1)S(1)} %get-tuple-element.105.refs_0_), channel_id=1, source_target_pairs={{0,3},{1,2},{2,1},{3,0},{4,7},{5,6},{6,5},{7,4},{8,11},{9,10},{10,... | collective-permute-start | bytes 516104 | tf_op jit(solution)/shard_map/ppermute | solution.py:125
  182.4 3.3 %parted.1 = (f32[288,768]{1,0:T(8,128)}, f32[576,768]{1,0:T(8,128)}) custom-call(f32[1104,768]{1,0:T(8,128)} %all-reduce.2.cloned.1.call-done.refs_0_), custom_call_target="tpu_custom_call" | custom-call | tf_op jit(solution)/shard_map/parted/pallas_call | solution.py:107
  (86 shorter events, 46.7 us)
Async XLA Ops:
  7.2 51.6 %all-gather.2.cloned.1.call-start = ((), (), s32[]{:S(2)}) async-start(), calls=%async_computation | async-start | bytes 1474560 | tf_op jit(solution)/shard_map/all_gather | solution.py:1054
  11.7 12.9 %collective-permute-start.3 = (bf16[384,448]{1,0:T(8,128)(2,1)S(1)}, bf16[384,448]{1,0:T(8,128)(2,1)S(1)}, u32[]{:S(2)}, u32[]{:S(2)}) collective-permute-start(bf16[384,448]{1,0:T(8,128)(2,1)S(1)} %get-tuple-element.63.refs_4_.refs_10_), channel_id=1, source_target_pairs={{0,8},{4,12},{8,0},{12,4},{16,24},{20,28},{24,16},{28,20},{1,9},{5... | collective-permute-start | bytes 1032200 | tf_op jit(solution)/shard_map/ppermute | solution.py:125
  14.7 19.0 %collective-permute-start.1 = (bf16[384,448]{1,0:T(8,128)(2,1)S(1)}, bf16[384,448]{1,0:T(8,128)(2,1)S(1)}, u32[]{:S(2)}, u32[]{:S(2)}) collective-permute-start(bf16[384,448]{1,0:T(8,128)(2,1)S(1)} %get-tuple-element.63.refs_4_.refs_10_), channel_id=1, source_target_pairs={{0,16},{4,20},{8,24},{12,28},{16,0},{20,4},{24,8},{28,12},{1,17},{... | collective-permute-start | bytes 1032200 | tf_op jit(solution)/shard_map/ppermute | solution.py:125
  16.3 17.5 %collective-permute-start.2 = (bf16[384,448]{1,0:T(8,128)(2,1)S(1)}, bf16[384,448]{1,0:T(8,128)(2,1)S(1)}, u32[]{:S(2)}, u32[]{:S(2)}) collective-permute-start(bf16[384,448]{1,0:T(8,128)(2,1)S(1)} %get-tuple-element.63.refs_4_.refs_10_), channel_id=1, source_target_pairs={{0,24},{4,28},{8,16},{12,20},{16,8},{20,12},{24,0},{28,4},{1,25},{... | collective-permute-start | bytes 1032200 | tf_op jit(solution)/shard_map/ppermute | solution.py:125
  40.0 10.9 %collective-permute-start.5 = (bf16[192,448]{1,0:T(8,128)(2,1)S(1)}, bf16[192,448]{1,0:T(8,128)(2,1)S(1)}, u32[]{:S(2)}, u32[]{:S(2)}) collective-permute-start(bf16[192,448]{1,0:T(8,128)(2,1)S(1)} %get-tuple-element.66.refs_6_.refs_2_), channel_id=1, source_target_pairs={{0,1},{1,0},{2,3},{3,2},{4,5},{5,4},{6,7},{7,6},{8,9},{9,8},{10,11... | collective-permute-start | bytes 516104 | tf_op jit(solution)/shard_map/ppermute | solution.py:125
  41.6 17.1 %collective-permute-start.6 = (bf16[192,448]{1,0:T(8,128)(2,1)S(1)}, bf16[192,448]{1,0:T(8,128)(2,1)S(1)}, u32[]{:S(2)}, u32[]{:S(2)}) collective-permute-start(bf16[192,448]{1,0:T(8,128)(2,1)S(1)} %get-tuple-element.66.refs_6_.refs_2_), channel_id=1, source_target_pairs={{0,2},{1,3},{2,0},{3,1},{4,6},{5,7},{6,4},{7,5},{8,10},{9,11},{10,... | collective-permute-start | bytes 516104 | tf_op jit(solution)/shard_map/ppermute | solution.py:125
  44.2 14.6 %collective-permute-start.7 = (bf16[192,448]{1,0:T(8,128)(2,1)S(1)}, bf16[192,448]{1,0:T(8,128)(2,1)S(1)}, u32[]{:S(2)}, u32[]{:S(2)}) collective-permute-start(bf16[192,448]{1,0:T(8,128)(2,1)S(1)} %get-tuple-element.66.refs_6_.refs_2_), channel_id=1, source_target_pairs={{0,3},{1,2},{2,1},{3,0},{4,7},{5,6},{6,5},{7,4},{8,11},{9,10},{10,... | collective-permute-start | bytes 516104 | tf_op jit(solution)/shard_map/ppermute | solution.py:125
  66.7 15.2 %collective-permute-start.9 = (bf16[112,768]{1,0:T(8,128)(2,1)}, bf16[112,768]{1,0:T(8,128)(2,1)S(1)}, u32[]{:S(2)}, u32[]{:S(2)}) collective-permute-start(bf16[112,768]{1,0:T(8,128)(2,1)} %get-tuple-element.74), channel_id=1, source_target_pairs={{0,1},{1,0},{2,3},{3,2},{4,5},{5,4},{6,7},{7,6},{8,9},{9,8},{10,11... | collective-permute-start | bytes 516104 | tf_op jit(solution)/shard_map/ppermute | solution.py:125
  70.6 15.5 %collective-permute-start.10 = (bf16[112,768]{1,0:T(8,128)(2,1)}, bf16[112,768]{1,0:T(8,128)(2,1)S(1)}, u32[]{:S(2)}, u32[]{:S(2)}) collective-permute-start(bf16[112,768]{1,0:T(8,128)(2,1)} %get-tuple-element.75), channel_id=1, source_target_pairs={{0,2},{1,3},{2,0},{3,1},{4,6},{5,7},{6,4},{7,5},{8,10},{9,11},{10,... | collective-permute-start | bytes 516104 | tf_op jit(solution)/shard_map/ppermute | solution.py:125
  71.7 14.5 %collective-permute-start.11 = (bf16[112,768]{1,0:T(8,128)(2,1)}, bf16[112,768]{1,0:T(8,128)(2,1)S(1)}, u32[]{:S(2)}, u32[]{:S(2)}) collective-permute-start(bf16[112,768]{1,0:T(8,128)(2,1)} %get-tuple-element.76), channel_id=1, source_target_pairs={{0,3},{1,2},{2,1},{3,0},{4,7},{5,6},{6,5},{7,4},{8,11},{9,10},{10,... | collective-permute-start | bytes 516104 | tf_op jit(solution)/shard_map/ppermute | solution.py:125
  80.6 101.8 %all-reduce.2.cloned.1.call-start = ((), (), s32[]{:S(2)}) async-start(), calls=%async_computation.1 | async-start | bytes 6782976 | tf_op jit(solution)/shard_map/psum | solution.py:1074
  80.8 18.5 %collective-permute-start.8 = (bf16[224,768]{1,0:T(8,128)(2,1)}, bf16[224,768]{1,0:T(8,128)(2,1)S(1)}, u32[]{:S(2)}, u32[]{:S(2)}) collective-permute-start(bf16[224,768]{1,0:T(8,128)(2,1)} %get-tuple-element.72), channel_id=1, source_target_pairs={{0,1},{1,0},{2,3},{3,2},{4,5},{5,4},{6,7},{7,6},{8,9},{9,8},{10,11... | collective-permute-start | bytes 1032200 | tf_op jit(solution)/shard_map/ppermute | solution.py:125
  100.5 18.1 %collective-permute-start.15 = (bf16[112,768]{1,0:T(8,128)(2,1)S(1)}, bf16[112,768]{1,0:T(8,128)(2,1)S(1)}, u32[]{:S(2)}, u32[]{:S(2)}) collective-permute-start(bf16[112,768]{1,0:T(8,128)(2,1)S(1)} %get-tuple-element.82), channel_id=1, source_target_pairs={{0,2},{1,3},{2,0},{3,1},{4,6},{5,7},{6,4},{7,5},{8,10},{9,11},{10,... | collective-permute-start | bytes 516104 | tf_op jit(solution)/shard_map/ppermute | solution.py:125
  107.1 17.9 %collective-permute-start.23 = (bf16[384,448]{1,0:T(8,128)(2,1)S(1)}, bf16[384,448]{1,0:T(8,128)(2,1)S(1)}, u32[]{:S(2)}, u32[]{:S(2)}) collective-permute-start(bf16[384,448]{1,0:T(8,128)(2,1)S(1)} %get-tuple-element.92), channel_id=1, source_target_pairs={{0,8},{4,12},{8,0},{12,4},{16,24},{20,28},{24,16},{28,20},{1,9},{5... | collective-permute-start | bytes 1032200 | tf_op jit(solution)/shard_map/ppermute | solution.py:125
  107.2 25.2 %collective-permute-start.24 = (bf16[384,448]{1,0:T(8,128)(2,1)S(1)}, bf16[384,448]{1,0:T(8,128)(2,1)S(1)}, u32[]{:S(2)}, u32[]{:S(2)}) collective-permute-start(bf16[384,448]{1,0:T(8,128)(2,1)S(1)} %get-tuple-element.93), channel_id=1, source_target_pairs={{0,16},{4,20},{8,24},{12,28},{16,0},{20,4},{24,8},{28,12},{1,17},{... | collective-permute-start | bytes 1032200 | tf_op jit(solution)/shard_map/ppermute | solution.py:125
  110.3 23.8 %collective-permute-start.25 = (bf16[384,448]{1,0:T(8,128)(2,1)S(1)}, bf16[384,448]{1,0:T(8,128)(2,1)S(1)}, u32[]{:S(2)}, u32[]{:S(2)}) collective-permute-start(bf16[384,448]{1,0:T(8,128)(2,1)S(1)} %get-tuple-element.94), channel_id=1, source_target_pairs={{0,24},{4,28},{8,16},{12,20},{16,8},{20,12},{24,0},{28,4},{1,25},{... | collective-permute-start | bytes 1032200 | tf_op jit(solution)/shard_map/ppermute | solution.py:125
  111.7 11.3 %collective-permute-start.30 = (bf16[112,768]{1,0:T(8,128)(2,1)S(1)}, bf16[112,768]{1,0:T(8,128)(2,1)S(1)}, u32[]{:S(2)}, u32[]{:S(2)}) collective-permute-start(bf16[112,768]{1,0:T(8,128)(2,1)S(1)} %copy-done), channel_id=1, source_target_pairs={{0,2},{1,3},{2,0},{3,1},{4,6},{5,7},{6,4},{7,5},{8,10},{9,11},{10,... | collective-permute-start | bytes 516104 | tf_op jit(solution)/shard_map/ppermute | solution.py:125
  123.0 15.2 %collective-permute-start.29 = (bf16[112,768]{1,0:T(8,128)(2,1)S(1)}, bf16[112,768]{1,0:T(8,128)(2,1)S(1)}, u32[]{:S(2)}, u32[]{:S(2)}) collective-permute-start(bf16[112,768]{1,0:T(8,128)(2,1)S(1)} %copy-done), channel_id=1, source_target_pairs={{0,1},{1,0},{2,3},{3,2},{4,5},{5,4},{6,7},{7,6},{8,9},{9,8},{10,11... | collective-permute-start | bytes 516104 | tf_op jit(solution)/shard_map/ppermute | solution.py:125
  123.0 15.2 %collective-permute-start.31 = (bf16[112,768]{1,0:T(8,128)(2,1)S(1)}, bf16[112,768]{1,0:T(8,128)(2,1)S(1)}, u32[]{:S(2)}, u32[]{:S(2)}) collective-permute-start(bf16[112,768]{1,0:T(8,128)(2,1)S(1)} %collective-permute-done.30.refs_5_), channel_id=1, source_target_pairs={{0,1},{1,0},{2,3},{3,2},{4,5},{5,4},{6,7},{7,6},{8,9},{9,8},{10,11... | collective-permute-start | bytes 516104 | tf_op jit(solution)/shard_map/ppermute | solution.py:125
  125.1 13.1 %collective-permute-start.17 = (bf16[112,768]{1,0:T(8,128)(2,1)S(1)}, bf16[112,768]{1,0:T(8,128)(2,1)S(1)}, u32[]{:S(2)}, u32[]{:S(2)}) collective-permute-start(bf16[112,768]{1,0:T(8,128)(2,1)S(1)} %total_of.2.refs_0_.refs_11_), channel_id=1, source_target_pairs={{0,2},{1,3},{2,0},{3,1},{4,6},{5,7},{6,4},{7,5},{8,10},{9,11},{10,... | collective-permute-start | bytes 516104 | tf_op jit(solution)/shard_map/ppermute | solution.py:125
  140.8 11.3 %collective-permute-start.26 = (bf16[128,768]{1,0:T(8,128)(2,1)S(1)}, bf16[128,768]{1,0:T(8,128)(2,1)S(1)}, u32[]{:S(2)}, u32[]{:S(2)}) collective-permute-start(bf16[128,768]{1,0:T(8,128)(2,1)S(1)} %get-tuple-element.96), channel_id=1, source_target_pairs={{0,1},{1,0},{2,3},{3,2},{4,5},{5,4},{6,7},{7,6},{8,9},{9,8},{10,11... | collective-permute-start | bytes 589832 | tf_op jit(solution)/shard_map/ppermute | solution.py:125
  142.0 17.2 %collective-permute-start.27 = (bf16[128,768]{1,0:T(8,128)(2,1)S(1)}, bf16[128,768]{1,0:T(8,128)(2,1)S(1)}, u32[]{:S(2)}, u32[]{:S(2)}) collective-permute-start(bf16[128,768]{1,0:T(8,128)(2,1)S(1)} %get-tuple-element.97), channel_id=1, source_target_pairs={{0,2},{1,3},{2,0},{3,1},{4,6},{5,7},{6,4},{7,5},{8,10},{9,11},{10,... | collective-permute-start | bytes 589832 | tf_op jit(solution)/shard_map/ppermute | solution.py:125
  143.3 15.8 %collective-permute-start.28 = (bf16[128,768]{1,0:T(8,128)(2,1)S(1)}, bf16[128,768]{1,0:T(8,128)(2,1)S(1)}, u32[]{:S(2)}, u32[]{:S(2)}) collective-permute-start(bf16[128,768]{1,0:T(8,128)(2,1)S(1)} %get-tuple-element.98), channel_id=1, source_target_pairs={{0,3},{1,2},{2,1},{3,0},{4,7},{5,6},{6,5},{7,4},{8,11},{9,10},{10,... | collective-permute-start | bytes 589832 | tf_op jit(solution)/shard_map/ppermute | solution.py:125
  145.2 21.7 %collective-permute-start.16 = (bf16[112,768]{1,0:T(8,128)(2,1)S(1)}, bf16[112,768]{1,0:T(8,128)(2,1)S(1)}, u32[]{:S(2)}, u32[]{:S(2)}) collective-permute-start(bf16[112,768]{1,0:T(8,128)(2,1)S(1)} %total_of.2.refs_0_.refs_11_), channel_id=1, source_target_pairs={{0,1},{1,0},{2,3},{3,2},{4,5},{5,4},{6,7},{7,6},{8,9},{9,8},{10,11... | collective-permute-start | bytes 516104 | tf_op jit(solution)/shard_map/ppermute | solution.py:125
  145.5 22.4 %collective-permute-start.18 = (bf16[112,768]{1,0:T(8,128)(2,1)S(1)}, bf16[112,768]{1,0:T(8,128)(2,1)S(1)}, u32[]{:S(2)}, u32[]{:S(2)}) collective-permute-start(bf16[112,768]{1,0:T(8,128)(2,1)S(1)} %collective-permute-done.17.refs_2_.refs_7_), channel_id=1, source_target_pairs={{0,1},{1,0},{2,3},{3,2},{4,5},{5,4},{6,7},{7,6},{8,9},{9,8},{10,11... | collective-permute-start | bytes 516104 | tf_op jit(solution)/shard_map/ppermute | solution.py:125
  160.7 18.1 %collective-permute-start.33 = (bf16[112,768]{1,0:T(8,128)(2,1)S(1)}, bf16[112,768]{1,0:T(8,128)(2,1)S(1)}, u32[]{:S(2)}, u32[]{:S(2)}) collective-permute-start(bf16[112,768]{1,0:T(8,128)(2,1)S(1)} %get-tuple-element.105.refs_0_), channel_id=1, source_target_pairs={{0,1},{1,0},{2,3},{3,2},{4,5},{5,4},{6,7},{7,6},{8,9},{9,8},{10,11... | collective-permute-start | bytes 516104 | tf_op jit(solution)/shard_map/ppermute | solution.py:125
  164.9 11.6 %collective-permute-start.37 = (bf16[192,384]{1,0:T(8,128)(2,1)S(1)}, bf16[192,384]{1,0:T(8,128)(2,1)S(1)}, u32[]{:S(2)}, u32[]{:S(2)}) collective-permute-start(bf16[192,384]{1,0:T(8,128)(2,1)S(1)} %get-tuple-element.108), channel_id=1, source_target_pairs={{0,16},{4,20},{8,24},{12,28},{16,0},{20,4},{24,8},{28,12},{1,17},{... | collective-permute-start | bytes 442376 | tf_op jit(solution)/shard_map/ppermute | solution.py:125
  167.0 9.5 %collective-permute-start.38 = (bf16[192,384]{1,0:T(8,128)(2,1)S(1)}, bf16[192,384]{1,0:T(8,128)(2,1)S(1)}, u32[]{:S(2)}, u32[]{:S(2)}) collective-permute-start(bf16[192,384]{1,0:T(8,128)(2,1)S(1)} %get-tuple-element.109), channel_id=1, source_target_pairs={{0,24},{4,28},{8,16},{12,20},{16,8},{20,12},{24,0},{28,4},{1,25},{... | collective-permute-start | bytes 442376 | tf_op jit(solution)/shard_map/ppermute | solution.py:125
  167.9 13.5 %collective-permute-start.34 = (bf16[112,768]{1,0:T(8,128)(2,1)S(1)}, bf16[112,768]{1,0:T(8,128)(2,1)S(1)}, u32[]{:S(2)}, u32[]{:S(2)}) collective-permute-start(bf16[112,768]{1,0:T(8,128)(2,1)S(1)} %get-tuple-element.105.refs_0_), channel_id=1, source_target_pairs={{0,2},{1,3},{2,0},{3,1},{4,6},{5,7},{6,4},{7,5},{8,10},{9,11},{10,... | collective-permute-start | bytes 516104 | tf_op jit(solution)/shard_map/ppermute | solution.py:125
  172.3 9.2 %collective-permute-start.35 = (bf16[112,768]{1,0:T(8,128)(2,1)S(1)}, bf16[112,768]{1,0:T(8,128)(2,1)S(1)}, u32[]{:S(2)}, u32[]{:S(2)}) collective-permute-start(bf16[112,768]{1,0:T(8,128)(2,1)S(1)} %get-tuple-element.105.refs_0_), channel_id=1, source_target_pairs={{0,3},{1,2},{2,1},{3,0},{4,7},{5,6},{6,5},{7,4},{8,11},{9,10},{10,... | collective-permute-start | bytes 516104 | tf_op jit(solution)/shard_map/ppermute | solution.py:125
  176.6 9.1 %collective-permute-start.39 = (bf16[208,384]{1,0:T(8,128)(2,1)S(1)}, bf16[208,384]{1,0:T(8,128)(2,1)S(1)}, u32[]{:S(2)}, u32[]{:S(2)}) collective-permute-start(bf16[208,384]{1,0:T(8,128)(2,1)S(1)} %sum_piece.1.refs_0_), channel_id=1, source_target_pairs={{0,8},{4,12},{8,0},{12,4},{16,24},{20,28},{24,16},{28,20},{1,9},{5... | collective-permute-start | bytes 479240 | tf_op jit(solution)/shard_map/ppermute | solution.py:125
  177.3 8.4 %collective-permute-start.40 = (bf16[208,384]{1,0:T(8,128)(2,1)S(1)}, bf16[208,384]{1,0:T(8,128)(2,1)S(1)}, u32[]{:S(2)}, u32[]{:S(2)}) collective-permute-start(bf16[208,384]{1,0:T(8,128)(2,1)S(1)} %sum_piece.1.refs_0_), channel_id=1, source_target_pairs={{0,16},{4,20},{8,24},{12,28},{16,0},{20,4},{24,8},{28,12},{1,17},{... | collective-permute-start | bytes 479240 | tf_op jit(solution)/shard_map/ppermute | solution.py:125
  (14 other events, 73.7 us)
Sparse Core Ops, SparseCore 0:
  9.6 33.1 all-gather.1
  84.8 86.3 all-reduce.1

commit v6 on v5

--- a/solution.py
+++ b/solution.py
@@ -27,6 +27,10 @@
 
 def params(mib):
     return pltpu.CompilerParams(vmem_limit_bytes=mib * 2**20)
+
+
+def slot(tp, n_tp):
+    return tp % 2 * (n_tp // 2) + tp // 2
 
 
 def mm(a, b, dims):
@@ -67,7 +71,8 @@
             source = in_refs[i]
             if ins[i][1] != "h":
                 rows = ins[i][1]
-                at = pl.multiple_of(lax.axis_index("tp") * rows, rows)
+                n_tp = ins[i][0].shape[0] // rows
+                at = pl.multiple_of(slot(lax.axis_index("tp"), n_tp) * rows, rows)
                 source = source.at[pl.ds(at, rows)]
             copies.append(pltpu.make_async_copy(source, buffers[n], sems.at[n]))
             in_refs[i] = buffers[n]
@@ -333,7 +338,7 @@
         outs[0][...] = state[...]
 
 
-def attention_forward(first, last, doc_lengths, roster, q_own, q_pair, blocks, state=None):
+def attention_forward(first, last, doc_lengths, roster, q_own, q_pair, blocks, state=None, after=()):
     width, rows = q_own.shape
     heads = width // HDIM
     count = len(blocks)
@@ -355,6 +360,7 @@
         + doc_scratch(doc_lengths, roster)
         + [pltpu.SemaphoreType.DMA((count + 2,))],
         16 if count < 8 else 40,
+        after,
     )
 
 
@@ -455,7 +461,7 @@
     )
 
 
-def join_kernel(heads, own_ref, back_ref, out_ref, total_ref):
+def join_kernel(heads, own_ref, back_ref, out_ref, total_ref, mine_ref, other_ref):
     rows = own_ref.shape[2]
     for h in range(heads):
         top_own = own_ref[h, 72:73, :]
@@ -469,6 +475,13 @@
         value = own_ref[h, :HDIM, :] * share_own + back_ref[h, :HDIM, :] * share_back
         out_ref[h * HDIM : (h + 1) * HDIM, :] = value.astype(BF16)
         total_ref[h] = jnp.broadcast_to(top + jnp.log(total), (8, rows))
+    half = rows // 2
+    for bit in range(2):
+
+        @pl.when(lax.axis_index("tp") % 2 == bit)
+        def _():
+            mine_ref[...] = out_ref[:, bit * half : (bit + 1) * half]
+            other_ref[...] = out_ref[:, (1 - bit) * half : (2 - bit) * half]
 
 
 def join(own, back):
@@ -477,30 +490,87 @@
         "join",
         functools.partial(join_kernel, heads),
         [(own, "v"), (back, "v")],
-        [((heads * HDIM, rows), BF16, "v"), ((heads, 8, rows), F32, "v")],
-    )
-
-
-def feed_kernel(n_tp, need, give, x_ref, cot_ref, gain_ref, in_ref, down_ref, w_ref, *refs):
+        [
+            ((heads * HDIM, rows), BF16, "v"),
+            ((heads, 8, rows), F32, "v"),
+            ((heads * HDIM, rows // 2), BF16, "v"),
+            ((heads * HDIM, rows // 2), BF16, "v"),
+        ],
+    )
+
+
+def stage_kernel(x_any, cot_any, w_any, in_any, in_pair, down_any, down_pair, *refs):
+    x_ref, cot_ref, w_ref, in_ref, down_ref, sems = refs
+    half = x_ref.shape[0]
+    mine = pl.ds(pl.multiple_of(lax.axis_index("tp") % 2 * half, half), half)
+    moves = [(w_any, w_ref), (x_any.at[mine], x_ref), (cot_any.at[mine], cot_ref)]
+    for (own, pair), ref in (((down_any, down_pair), down_ref), ((in_any, in_pair), in_ref)):
+        rows = own.shape[0]
+        moves.append((own, ref.at[pl.ds(0, rows)]))
+        moves.append((pair, ref.at[pl.ds(rows, rows)]))
+    copies = [pltpu.make_async_copy(*move, sems.at[n]) for n, move in enumerate(moves)]
+    for copy in copies:
+        copy.start()
+    for copy in copies:
+        copy.wait()
+
+
+def stage(tokens, cotangent, w_full, in_t, in_pair, w_down, down_pair):
+    rows, model = tokens.shape
+    return call(
+        "stage",
+        stage_kernel,
+        kinds((tokens, cotangent, w_full, in_t, in_pair, w_down, down_pair), "raw"),
+        [
+            ((rows // 2, model), BF16, "v"),
+            ((rows // 2, model), BF16, "v"),
+            (w_full.shape, BF16, "v"),
+            ((2 * in_t.shape[0], model), BF16, "v"),
+            ((2 * w_down.shape[0], model), BF16, "v"),
+        ],
+        [pltpu.SemaphoreType.DMA((7,))],
+    )
+
+
+def gated(units, first, gate_up, mixed_grad, mixed_out, gate_out):
+    def wave(i, carry):
+        spot = pl.ds(first + i * 32, 32)
+        at = pl.ds(2 * first + i * 32, 32)
+        late = pl.ds(2 * first + units + i * 32, 32)
+        gate = gate_up[at, :]
+        up = gate_up[late, :]
+        back = mixed_grad[spot, :]
+        bell = 0.5 * (1.0 + lax.erf(gate * (2.0**-0.5)))
+        active = gate * bell
+        slope = bell + gate * jnp.exp(-0.5 * gate * gate) * ((2.0 * jnp.pi) ** -0.5)
+        mixed_out[spot, :] = (active * up).astype(BF16)
+        gate_out[at, :] = (back * up * slope).astype(BF16)
+        gate_out[late, :] = (back * active).astype(BF16)
+        return carry
+
+    lax.fori_loop(0, units // 32, wave, 0)
+
+
+def feed_kernel(n_tp, need, give, x_ref, cot_ref, w_ref, in_ref, down_ref, gain_ref, *refs):
     out_refs = refs[:n_tp]
-    middle_out, h_out, mixed_out, gate_out, gain_out = refs[n_tp : n_tp + 5]
-    part_refs = refs[n_tp + 5 : 2 * n_tp + 5]
-    outs, unit, gate_up, mixed_grad, grad = refs[2 * n_tp + 5 :]
+    middle_out, part_out, h_out, mixed_out, gate_out, gain_out = refs[n_tp : n_tp + 6]
+    keep_ref, *send_refs = refs[n_tp + 6 : n_tp + 6 + n_tp // 2]
+    outs, unit, gate_up, mixed_grad, grad = refs[n_tp + 6 + n_tp // 2 :]
     rows = x_ref.shape[0]
-    part = rows // n_tp
-    units = down_ref.shape[0]
+    part = keep_ref.shape[0]
+    units = down_ref.shape[0] // 2
     width = out_refs[0].shape[0]
     tp = lax.axis_index("tp")
     for k in range(n_tp):
         at = pl.ds(pl.multiple_of((tp ^ k) * width, width), width)
         outs[at, :] = out_refs[k][...]
+    mixed_grad[...] = mm(down_ref[...], cot_ref[...], NT)
+    middle_out[...] = mm(outs[...], w_ref[...], TN)
     need(5)
-    middle_out[...] = mm(outs[...], w_ref[...], TN)
-    need(0, 2)
     gain = gain_ref[...].reshape(1, -1)
 
     def strip(i, carry):
-        at = pl.ds(i * STRIP, STRIP)
+        at = pl.ds(i * 32, 32)
         middle = middle_out[at, :] + x_ref[at, :].astype(F32)
         middle_out[at, :] = middle
         held, unused = normed(middle)
@@ -508,61 +578,48 @@
         h_out[at, :] = (held * gain).astype(BF16)
         return carry
 
-    lax.fori_loop(0, rows // STRIP, strip, 0)
-    give(0, 1)
-    need(1, 4)
-    mixed_grad[...] = mm(down_ref[...], cot_ref[...], NT)
-    need(3)
+    lax.fori_loop(0, rows // 32, strip, 0)
+    give(0, 2)
     gate_up[...] = mm(in_ref[...], h_out[...], NT)
-
-    def wave(i, carry):
+    for first in (0, units):
+        gated(units, first, gate_up, mixed_grad, mixed_out, gate_out)
+    give(3, 4)
+    grad[...] = mm(gate_out[...], in_ref[...], TN)
+    for n, ref in enumerate((keep_ref, *send_refs)):
+        at = pl.ds(pl.multiple_of((tp ^ (2 * n)) // 2 * part, part), part)
+        ref[...] = grad[at, :].astype(ref.dtype)
+        give(6 + n)
+    own = pl.ds(pl.multiple_of(tp // 2 * part, part), part)
+    part_out[...] = middle_out[own, :]
+    give(1)
+
+    def gains(i, carry):
         at = pl.ds(i * 32, 32)
-        late = pl.ds(units + i * 32, 32)
-        gate = gate_up[at, :]
-        up = gate_up[late, :]
-        back = mixed_grad[at, :]
-        bell = 0.5 * (1.0 + lax.erf(gate * (2.0**-0.5)))
-        active = gate * bell
-        slope = bell + gate * jnp.exp(-0.5 * gate * gate) * ((2.0 * jnp.pi) ** -0.5)
-        mixed_out[at, :] = (active * up).astype(BF16)
-        gate_out[at, :] = (back * up * slope).astype(BF16)
-        gate_out[late, :] = (back * active).astype(BF16)
-        return carry
-
-    lax.fori_loop(0, units // 32, wave, 0)
-    give(2, 3)
-    grad[...] = mm(gate_out[...], in_ref[...], TN)
-    for k in range(n_tp):
-        at = pl.ds(pl.multiple_of((tp ^ k) * part, part), part)
-        part_refs[k][...] = grad[at, :].astype(part_refs[k].dtype)
-        give(5 + k)
-
-    def gains(i, carry):
-        at = pl.ds(i * STRIP, STRIP)
         product = grad[at, :] * unit[at, :]
-        return carry + jnp.sum(product.reshape(STRIP // 8, 8, -1), axis=0)
-
-    gain_out[...] = lax.fori_loop(0, rows // STRIP, gains, jnp.zeros(gain_out.shape, F32))
-
-
-def feed(tokens, cotangent, gain, in_t, w_down, w_full, outs):
-    rows, model = tokens.shape
+        return carry + jnp.sum(product.reshape(4, 8, -1), axis=0)
+
+    gain_out[...] = lax.fori_loop(0, rows // 32, gains, jnp.zeros(gain_out.shape, F32))
+
+
+def feed(gain, staged, outs):
+    rows, model = staged[0].shape
     n_tp = len(outs)
-    units = w_down.shape[0]
-    part = rows // n_tp
+    units = staged[4].shape[0]
+    part = 2 * rows // n_tp
     return call(
         "feed",
         functools.partial(feed_kernel, n_tp),
-        kinds((tokens, cotangent, gain, in_t, w_down, w_full), "h") + kinds(outs, "v"),
+        kinds(staged, "v") + [(gain, "h")] + kinds(outs, "v"),
         [
             ((rows, model), F32, "h"),
+            ((part, model), F32, "h"),
             ((rows, model), BF16, "h"),
             ((units, rows), BF16, "h"),
             ((2 * units, rows), BF16, "h"),
             ((8, model), F32, "h"),
             ((part, model), F32, "h"),
         ]
-        + [((part, model), BF16, "h")] * (n_tp - 1),
+        + [((part, model), BF16, "h")] * (n_tp // 2 - 1),
         [
             pltpu.VMEM((n_tp * outs[0].shape[0], rows), BF16),
             pltpu.VMEM((rows, model), F32),
@@ -570,15 +627,15 @@
             pltpu.VMEM((units, rows), F32),
             pltpu.VMEM((rows, model), F32),
         ],
-        32,
+        24,
         lazy=True,
     )
 
 
-def branch_kernel(n_tp, need, give, middle_ref, cot_ref, gain_ref, w_ref, *refs):
-    arrived = refs[:n_tp]
-    grad_out, branch_out = refs[n_tp : n_tp + 2]
-    piece_refs = refs[n_tp + 2 :]
+def branch_kernel(n_tp, count, need, give, middle_ref, cot_ref, gain_ref, w_ref, *refs):
+    arrived = refs[:count]
+    grad_out, branch_out = refs[count : count + 2]
+    piece_refs = refs[count + 2 :]
     width = piece_refs[0].shape[1]
     tp = lax.axis_index("tp")
     need(0, 1, 2, 4)
@@ -597,14 +654,15 @@
         piece_refs[k][...] = mm(branch_out[...], w_ref[at, :], NT).astype(BF16)
 
 
-def branch(middle, cotangent, gain, w_full, arrived, after):
+def branch(n_tp, middle_part, cotangent, gain, w_full, arrived, after):
     part, model = arrived[0].shape
-    n_tp = len(arrived)
     width = w_full.shape[0] // n_tp
     return call(
         "branch",
-        functools.partial(branch_kernel, n_tp),
-        [(middle, part), (cotangent, part)] + kinds((gain, w_full, arrived[0]), "h") + kinds(arrived[1:], "v"),
+        functools.partial(branch_kernel, n_tp, len(arrived)),
+        [(middle_part, "h"), (cotangent, part)]
+        + kinds((gain, w_full, arrived[0]), "h")
+        + kinds(arrived[1:], "v"),
         [((part, model), F32, "h"), ((part, model), BF16, "h")]
         + [((part, width), BF16, "v")] * n_tp,
         (),
@@ -619,12 +677,12 @@
     part = refs[0].shape[0]
     tp = lax.axis_index("tp")
     for k in range(n_tp):
-        at = pl.ds(pl.multiple_of((tp ^ k) * part, part), part)
+        at = pl.ds(pl.multiple_of(slot(tp ^ k, n_tp) * part, part), part)
         held[at, :] = refs[k][...].astype(F32)
     out_ref[...] = held[...].T.astype(BF16)
 
 
-def lay_turned(pieces):
+def lay_turned(pieces, after):
     part, width = pieces[0].shape
     rows = part * len(pieces)
     (out,) = call(
@@ -633,6 +691,8 @@
         kinds(pieces, "v"),
         [((width, rows), BF16, "v")],
         [pltpu.VMEM((rows, width), F32)],
+        16,
+        after,
     )
     return out
 
@@ -642,7 +702,7 @@
     part = refs[0].shape[0]
     tp = lax.axis_index("tp")
     for k in range(n_tp):
-        at = pl.ds(pl.multiple_of((tp ^ k) * part, part), part)
+        at = pl.ds(pl.multiple_of(slot(tp ^ k, n_tp) * part, part), part)
         out_ref[at, :] = refs[k][...]
 
 
@@ -706,7 +766,7 @@
     gain = jnp.sum(gain, axis=0, keepdims=True)
     gain = jnp.where(line == 0, gain, jnp.where(line == 1, gain_two, 0.0))
     for k in range(n_tp):
-        at = pl.ds(pl.multiple_of((tp ^ k) * part, part), part)
+        at = pl.ds(pl.multiple_of(slot(tp ^ k, n_tp) * part, part), part)
         part_refs[k][:part, :] = grad[at, :].astype(part_refs[k].dtype)
         part_refs[k][part:, :] = gain.astype(part_refs[k].dtype)
 
@@ -717,7 +777,7 @@
     return call(
         "unproject",
         functools.partial(unproject_kernel, len(dkvs), n_tp),
-        kinds((tokens, qkv_t, cos_table, sin_table, gain_two_part), "h")
+        kinds((tokens, qkv_t, cos_table, sin_table, gain_two_part), "v")
         + kinds((dq, dq_back, *dkvs), "v"),
         [((qkv_t.shape[0], rows), BF16, "v"), ((part + 16, model), F32, "v")]
         + [((part + 16, model), BF16, "v")] * (n_tp - 1),
@@ -747,7 +807,7 @@
     return call(
         "input_side",
         functools.partial(input_kernel, len(arrived)),
-        [(tokens, part), (gain, "h"), (middle_grad, "h")] + kinds(arrived, "v"),
+        [(tokens, part), (gain, "h"), (middle_grad, "v")] + kinds(arrived, "v"),
         [((part, model), BF16, "v"), ((8, model), F32, "v")],
         (),
         16,
@@ -755,21 +815,40 @@
     )
 
 
-def early_kernel(mixed_ref, gate_ref, cot_ref, h_ref, out_ref):
-    units = mixed_ref.shape[0]
-    out_ref[:units, :] = mm(mixed_ref[...], cot_ref[...], NN)
-    out_ref[units : 3 * units, :] = mm(gate_ref[...], h_ref[...], NN)
+def early_kernel(mixed_ref, gate_ref, cot_ref, h_ref, in_ref, down_ref, h_pair, out_ref, *refs):
+    gate_up, mixed_grad, mixed, gate = refs
+    units = down_ref.shape[0]
+    half = h_ref.shape[0]
+    bit = lax.axis_index("tp") % 2
+    mine = pl.ds(pl.multiple_of(bit * half, half), half)
+    other = pl.ds(pl.multiple_of((1 - bit) * half, half), half)
+    gate_up[...] = mm(in_ref[...], h_pair[...], NT)
+    mixed_grad[...] = mm(down_ref[...], cot_ref[other, :], NT)
+    gated(units, 0, gate_up, mixed_grad, mixed, gate)
+    out_ref[:units, :] = mm(mixed_ref[:units, :], cot_ref[mine, :], NN)
+    out_ref[:units, :] += mm(mixed[...], cot_ref[other, :], NN)
+    out_ref[units : 3 * units, :] = mm(gate_ref[: 2 * units, :], h_ref[...], NN)
+    out_ref[units : 3 * units, :] += mm(gate[...], h_pair[...], NN)
     if out_ref.shape[0] > 3 * units:
         out_ref[3 * units :, :] = jnp.zeros((out_ref.shape[0] - 3 * units, out_ref.shape[1]), F32)
 
 
-def early_grads(mixed, gate_grad, cotangent, h_two):
-    model = cotangent.shape[1]
+def early_grads(mixed, gate_grad, cotangent, h_two, in_t, w_down, h_pair, after):
+    units, model = w_down.shape
+    half = h_two.shape[0]
     (out,) = call(
         "early_grads",
         early_kernel,
-        kinds((mixed, gate_grad, cotangent, h_two), "h"),
-        [((1104, model), F32, "h")],
+        kinds((mixed, gate_grad, cotangent, h_two, in_t, w_down), "h") + [(h_pair, "v")],
+        [((7 * units // 2, model), F32, "h")],
+        [
+            pltpu.VMEM((2 * units, half), F32),
+            pltpu.VMEM((units, half), F32),
+            pltpu.VMEM((units, half), BF16),
+            pltpu.VMEM((2 * units, half), BF16),
+        ],
+        24,
+        after,
     )
     return out
 
@@ -806,7 +885,7 @@
     tp = lax.axis_index("tp")
     core = lax.axis_index("seq") % 2
     for k in range(n_tp):
-        at = pl.ds(pl.multiple_of((tp ^ k) * part, part), part)
+        at = pl.ds(pl.multiple_of(slot(tp ^ k, n_tp) * part, part), part)
         branch_full[at, :] = branch_refs[k][...]
     for ref, side in ((send_ref, 1 - core), (keep_ref, core)):
         columns = pl.ds(pl.multiple_of(side * half, half), half)
@@ -820,7 +899,7 @@
     return call(
         "late_grads",
         functools.partial(late_kernel, len(branches)),
-        [(proj_grad, "v"), (h_one, "h"), (out_b, "v"), (branches[0], "h")]
+        [(proj_grad, "v"), (h_one, "v"), (out_b, "v"), (branches[0], "v")]
         + kinds(branches[1:], "v"),
         [((wide, model // 2), F32, "v"), ((wide, model // 2), BF16, "v")],
         [pltpu.VMEM((rows, model), BF16)],
@@ -943,51 +1022,29 @@
     )
 
 
-def down_kernel(n_tp, mixed_ref, w_ref, middle_ref, keep_ref, send_ref, total):
-    part = keep_ref.shape[0] * 2 // n_tp
+def down_kernel(mixed_ref, w_ref, w_pair, middle_ref, keep_ref, *refs):
+    send_refs, total = refs[:-1], refs[-1]
+    part = keep_ref.shape[0]
+    units = w_ref.shape[0]
     tp = lax.axis_index("tp")
-    total[...] = mm(mixed_ref[...], w_ref[...], TN)
-    for k in range(n_tp):
-        at = pl.ds(pl.multiple_of((tp ^ k) * part, part), part)
-        spot = k // 2 * part
-        if k % 2:
-            send_ref[spot : spot + part, :] = total[at, :].astype(BF16)
-        else:
-            value = total[at, :] + middle_ref[at, :] if k == 0 else total[at, :]
-            keep_ref[spot : spot + part, :] = value
-
-
-def down(n_tp, mixed, w_down, middle, after):
+    total[...] = mm(mixed_ref[:units, :], w_ref[...], TN)
+    total[...] += mm(mixed_ref[units:, :], w_pair[...], TN)
+    own = pl.ds(pl.multiple_of(tp // 2 * part, part), part)
+    keep_ref[...] = total[own, :] + middle_ref[own, :]
+    for n, ref in enumerate(send_refs):
+        at = pl.ds(pl.multiple_of((tp ^ (2 * n + 2)) // 2 * part, part), part)
+        ref[...] = total[at, :].astype(ref.dtype)
+
+
+def down(n_tp, mixed, w_down, down_pair, middle, after):
     rows, model = middle.shape
+    part = 2 * rows // n_tp
     return call(
         "down",
-        functools.partial(down_kernel, n_tp),
-        kinds((mixed, w_down, middle), "h"),
-        [((rows // 2, model), F32, "h"), ((rows // 2, model), BF16, "h")],
+        down_kernel,
+        kinds((mixed, w_down, down_pair, middle), "h"),
+        [((part, model), F32, "h")] + [((part, model), BF16, "h")] * (n_tp // 2 - 1),
         [pltpu.VMEM((rows, model), F32)],
-        16,
-        after,
-    )
-
-
-def pair_kernel(keep_ref, back_ref, own_ref, *send_refs):
-    part = own_ref.shape[0]
-    own_ref[...] = keep_ref[:part, :] + back_ref[:part, :].astype(F32)
-    for k, ref in enumerate(send_refs):
-        at = (k + 1) * part
-        total = keep_ref[at : at + part, :] + back_ref[at : at + part, :].astype(F32)
-        ref[...] = total.astype(BF16)
-
-
-def pair_sum(n_tp, keep, back, after=()):
-    part = keep.shape[0] * 2 // n_tp
-    model = keep.shape[1]
-    return call(
-        "pair_sum",
-        pair_kernel,
-        [(keep, "h"), (back, "v")],
-        [((part, model), F32, "v")] + [((part, model), BF16, "v")] * (n_tp // 2 - 1),
-        (),
         16,
         after,
     )
@@ -1004,8 +1061,8 @@
     (out,) = call(
         "total_of",
         functools.partial(total_kernel, len(parts)),
-        kinds(parts, kind),
-        [(parts[0].shape, dtype, kind)],
+        [(parts[0], kind)] + kinds(parts[1:], "v"),
+        [(parts[0].shape, dtype, "v")],
         (),
         16,
         after,
@@ -1052,39 +1109,48 @@
     blocks = [kv] + [over_chips(kv, j) for j in range(1, count)]
     q_pair = over_cores(queries)
     w_full = lax.all_gather(w_out, "tp", axis=0, tiled=True)
+    in_pair = over_tp(in_t, 1)
+    down_pair = over_tp(w_down, 1)
 
     split = (count + 1) // 2
     (state,) = attention_forward(0, False, *docs, queries, q_pair, blocks[:split])
     state_own, state_pair = attention_forward(
-        split, True, *docs, queries, q_pair, blocks[split:], state
-    )
-    out_b, totals = join(state_own, over_cores(state_pair))
-    outs = everywhere([out_b] * n_tp)
+        split, True, *docs, queries, q_pair, blocks[split:], state, kinds((in_pair, down_pair), "h")
+    )
+    out_b, totals, out_mine, out_other = join(state_own, over_cores(state_pair))
+    outs = [out_mine] + [over_tp(out_other if k % 2 else out_mine, k) for k in range(1, n_tp)]
     out_pair = over_cores(out_b)
     totals_pair = over_cores(totals)
 
-    middle, h_two, mixed, gate_grad, gain_two_part, *parts = feed(
-        tokens, cotangent, gain_two, in_t, w_down, w_full, outs
-    )
-    early = early_grads(mixed, gate_grad, cotangent, h_two)
-    keep, send = down(n_tp, mixed, w_down, middle, [(early, "h")])
+    staged = stage(tokens, cotangent, w_full, in_t, in_pair, w_down, down_pair)
+    middle, middle_part, h_two, mixed, gate_grad, gain_two_part, own, *others = feed(
+        gain_two, staged, outs
+    )
+    arrived = [own] + [over_tp(others[n], 2 * n + 2) for n in range(n_tp // 2 - 1)]
+    own, *others = down(n_tp, mixed, w_down, down_pair, middle, ())
     middle_grad, branch_grad, *pieces = branch(
-        middle, cotangent, gain_two, w_full, everywhere(parts), [(keep, "h")]
-    )
-    early = lax.psum(early, "seq")
-    grad_down, grad_in = parted(early, (units, 2 * units))
-    out_grad = lay_turned(everywhere(pieces))
+        n_tp, middle_part, cotangent, gain_two, w_full, arrived, [(own, "h")]
+    )
+    h_pair = over_tp(h_two, 1)
+    early = early_grads(
+        mixed, gate_grad, cotangent, h_two, in_t, w_down, h_pair, [(branch_grad, "h")]
+    )
+    early_sum = lax.psum(early, "seq")
+    grad_down, grad_in = parted(early_sum, (units, 2 * units))
+    out_grad = lay_turned(everywhere(pieces), [(early, "h")])
     grad_pair = over_cores(out_grad)
     branches = by_steps(branch_grad)
 
-    own, *others = pair_sum(n_tp, keep, over_tp(send, 1), [(out_grad, "v")])
     total = total_of(
-        [own] + [over_tp(others[k], 2 * k + 2) for k in range(n_tp // 2 - 1)], BF16
+        [own] + [over_tp(others[n], 2 * n + 2) for n in range(n_tp // 2 - 1)],
+        BF16,
+        "h",
+        [(out_grad, "v")],
     )
     totals_all = by_steps(total)
 
     held = (queries, q_pair, out_grad, grad_pair, out_b, out_pair, totals, totals_pair)
-    *terms, dq = attention_backward(1, False, *docs, held, blocks[1:], None, [(own, "v")])
+    *terms, dq = attention_backward(1, False, *docs, held, blocks[1:], None, [(total, "v")])
     dkv, dq_own, dq_pair = attention_backward(0, True, *docs, held, blocks[:1], dq)
     dkvs = [dkv] + [over_chips(terms[j - 1], j) for j in range(1, count)]
 

time: 198 us -> 227 us (1.15)
  waiting for transfers between devices: 67.2 us -> 101 us
  Pallas kernels: 57.5 us -> 49.5 us
    ppermute x43, waiting for transfers between devices: 66.5 us -> 90.5 us  [swap(): return lax.ppermute(x, axis, [(i, i ^ hop) for i in range(count)])]
    psum x1, waiting for transfers between devices: 0.02 us -> 9.58 us  [body(): early_sum = lax.psum(early, 'seq')]
    pallas_call x24, Pallas kernels: 57.5 us -> 49.5 us  [call(): pl.pallas_call(run, out_shape=tuple((shaped(shape, dtype) if kind == 'v'...]
  transfers between devices with their start and end apart: 45 -> 45, of which waited for: 18 -> 16; matrix products, arithmetic and copies ran while one was open for 0% -> 0% of each run, Pallas kernels for 24% -> 18%
where the time goes in v6:
time: 227 us; the launch traced here: 225 us
  waiting for transfers between devices  101 us (44%)
  starting transfers between devices  57.9 us (26%)
  Pallas kernels  49.5 us (22%)
  between operations  14.5 us (6%)
    ppermute x43, waiting for transfers between devices, swap(): return lax.ppermute(x, axis, [(i, i ^ hop) for i in range(count)])  90.5 us
    ppermute x43, starting transfers between devices, swap(): return lax.ppermute(x, axis, [(i, i ^ hop) for i in range(count)])  57.6 us
    pallas_call x24, Pallas kernels, call(): pl.pallas_call(run, out_shape=tuple((shaped(shape, dtype) if kind == 'v'...  49.5 us
    psum x1, waiting for transfers between devices, body(): early_sum = lax.psum(early, 'seq')  9.58 us
  transfers between devices with their start and end apart: 45, of which 16 were waited for; matrix products, arithmetic and copies ran while one was open for 0% of the time, Pallas kernels for 18%

profile of v6, /device:TPU:0, one launch (start us, length us, event | category | flops | bytes accessed | tf_op | source)
XLA Modules:
  0.0 224.6 jit_solution(5444013309825812188)
XLA Ops:
  7.9 3.1 %collective-permute-start = (bf16[576,768]{1,0:T(8,128)(2,1)}, bf16[576,768]{1,0:T(8,128)(2,1)S(1)}, u32[]{:S(2)}, u32[]{:S(2)}) collective-permute-start(bf16[576,768]{1,0:T(8,128)(2,1)} %bitcast.14), channel_id=1, source_target_pairs={{0,1},{1,0},{2,3},{3,2},{4,5},{5,4},{6,7},{7,6},{8,9},{9,8},{10,11... | collective-permute-start | bytes 2654216 | tf_op jit(solution)/shard_map/ppermute | solution.py:130
  11.0 4.0 %project.1 = (bf16[192,448]{1,0:T(8,128)(2,1)S(1)}, bf16[384,448]{1,0:T(8,128)(2,1)S(1)}, bf16[448,768]{1,0:T(8,128)(2,1)}, f32[32,448]{1,0:T(8,128)}, f32[32,448]{1,0:T(8,128)}) custom-call(s32[4]{0:T(128)} %refs_0_.13, s32[8]{0:T(128)} %refs_1_.16, bf16[448,768]{1,0:T(8,128)(2,1)} %refs_0_.15, bf16[576,768]{1,0:T(8,128)(2,1)} %bitcast.12, f32[768]{0:T(1024)} %refs_1_.17, ...), custom_call_target="tpu_custom_call" | custom-call | tf_op jit(solution)/shard_map/project/pallas_call | solution.py:112
  18.9 8.2 %collective-permute-done.5.refs_5_.refs_10_ = bf16[384,448]{1,0:T(8,128)(2,1)S(1)} collective-permute-done((bf16[384,448]{1,0:T(8,128)(2,1)S(1)}, bf16[384,448]{1,0:T(8,128)(2,1)S(1)}, u32[]{:S(2)}, u32[]{:S(2)}) %collective-permute-start.5) | collective-permute-done | bytes 344096 | tf_op jit(solution)/shard_map/ppermute | solution.py:130
  27.2 4.2 %attention_forward.2.refs_6_ = f32[6,80,448]{2,1,0:T(8,128)S(1)} custom-call(s32[4]{0:T(128)} %refs_0_.13, s32[8]{0:T(128)} %refs_1_.16, bf16[192,448]{1,0:T(8,128)(2,1)S(1)} %get-tuple-element.71.refs_2_, bf16[192,448]{1,0:T(8,128)(2,1)S(1)} %collective-permute-done.2.refs_3_, bf16[384,448]{1,0:T(8,128)(2,1)S(1)} %get-tuple-element.72.refs_4_.refs_10_, ...), custom_call_target="tpu_custom_call" | custom-call | tf_op jit(solution)/shard_map/attention_forward/pallas_call | solution.py:112
  31.4 5.0 %collective-permute-done.3.refs_4_.refs_11_ = bf16[384,448]{1,0:T(8,128)(2,1)S(1)} collective-permute-done((bf16[384,448]{1,0:T(8,128)(2,1)S(1)}, bf16[384,448]{1,0:T(8,128)(2,1)S(1)}, u32[]{:S(2)}, u32[]{:S(2)}) %collective-permute-start.3) | collective-permute-done | bytes 344096 | tf_op jit(solution)/shard_map/ppermute | solution.py:130
  36.4 22.9 %collective-permute-done.1.refs_6_.refs_8_.refs_2_ = bf16[288,768]{1,0:T(8,128)(2,1)S(1)} collective-permute-done((bf16[288,768]{1,0:T(8,128)(2,1)S(1)}, bf16[288,768]{1,0:T(8,128)(2,1)S(1)}, u32[]{:S(2)}, u32[]{:S(2)}) %collective-permute-start.1) | collective-permute-done | bytes 442400 | tf_op jit(solution)/shard_map/ppermute | solution.py:130
  66.8 3.6 %collective-permute-start.8 = (bf16[192,224]{1,0:T(8,128)(2,1)S(1)}, bf16[192,224]{1,0:T(8,128)(2,1)S(1)}, u32[]{:S(2)}, u32[]{:S(2)}) collective-permute-start(bf16[192,224]{1,0:T(8,128)(2,1)S(1)} %get-tuple-element.75.refs_6_), channel_id=1, source_target_pairs={{0,2},{1,3},{2,0},{3,1},{4,6},{5,7},{6,4},{7,5},{8,10},{9,11},{10,... | collective-permute-start | bytes 258056 | tf_op jit(solution)/shard_map/ppermute | solution.py:130
  73.1 5.1 %collective-permute-done.8.refs_8_ = bf16[192,224]{1,0:T(8,128)(2,1)S(1)} collective-permute-done((bf16[192,224]{1,0:T(8,128)(2,1)S(1)}, bf16[192,224]{1,0:T(8,128)(2,1)S(1)}, u32[]{:S(2)}, u32[]{:S(2)}) %collective-permute-start.8) | collective-permute-done | bytes 86048 | tf_op jit(solution)/shard_map/ppermute | solution.py:130
  78.2 6.2 %feed.1 = (f32[224,768]{1,0:T(8,128)}, f32[112,768]{1,0:T(8,128)}, bf16[224,768]{1,0:T(8,128)(2,1)}, bf16[576,224]{1,0:T(8,128)(2,1)}, bf16[1152,224]{1,0:T(8,12...) custom-call(bf16[224,768]{1,0:T(8,128)(2,1)S(1)} %get-tuple-element.66.refs_0_, ...), custom_call_target="tpu_custom_call" | custom-call | tf_op jit(solution)/shard_map/feed/pallas_call | solution.py:112
  87.6 2.9 %down.1 = (f32[112,768]{1,0:T(8,128)}, bf16[112,768]{1,0:T(8,128)(2,1)}) custom-call(bf16[576,224]{1,0:T(8,128)(2,1)} %get-tuple-element.77.refs_0_, bf16[288,768]{1,0:T(8,128)(2,1)} %refs_5_.6, bf16[288,768]{1,0:T(8,128)(2,1)} %copy-done.8, f32[224,768]{1,0:T(8,128)} %get-tuple-element.78.refs_3_), custom_call_target="tpu_custom_call" | custom-call | tf_op jit(solution)/shard_map/down/pallas_call | solution.py:112
  90.5 7.1 %collective-permute-done.11.refs_5_ = bf16[112,768]{1,0:T(8,128)(2,1)S(1)} collective-permute-done((bf16[112,768]{1,0:T(8,128)(2,1)}, bf16[112,768]{1,0:T(8,128)(2,1)S(1)}, u32[]{:S(2)}, u32[]{:S(2)}) %collective-permute-start.11) | collective-permute-done | bytes 172064 | tf_op jit(solution)/shard_map/ppermute | solution.py:130
  97.6 2.7 %branch.1 = (f32[112,768]{1,0:T(8,128)}, bf16[112,768]{1,0:T(8,128)(2,1)}, bf16[112,192]{1,0:T(8,128)(2,1)S(1)}, bf16[112,192]{1,0:T(8,128)(2,1)S(1)}, bf16[112,...) custom-call(f32[112,768]{1,0:T(8,128)} %get-tuple-element.81.refs_0_, bf16[448,768]{1,0:T(8,128)(2,1)} %refs_2_.5, ...), custom_call_target="tpu_custom_call" | custom-call | tf_op jit(solution)/shard_map/branch/pallas_call | solution.py:112
  100.3 3.4 %collective-permute-start.12 = (bf16[112,192]{1,0:T(8,128)(2,1)S(1)}, bf16[112,192]{1,0:T(8,128)(2,1)S(1)}, u32[]{:S(2)}, u32[]{:S(2)}) collective-permute-start(bf16[112,192]{1,0:T(8,128)(2,1)S(1)} %get-tuple-element.85), channel_id=1, source_target_pairs={{0,1},{1,0},{2,3},{3,2},{4,5},{5,4},{6,7},{7,6},{8,9},{9,8},{10,11... | collective-permute-start | bytes 129032 | tf_op jit(solution)/shard_map/ppermute | solution.py:130
  103.7 2.4 %collective-permute-start.14 = (bf16[112,192]{1,0:T(8,128)(2,1)S(1)}, bf16[112,192]{1,0:T(8,128)(2,1)S(1)}, u32[]{:S(2)}, u32[]{:S(2)}) collective-permute-start(bf16[112,192]{1,0:T(8,128)(2,1)S(1)} %get-tuple-element.87), channel_id=1, source_target_pairs={{0,3},{1,2},{2,1},{3,0},{4,7},{5,6},{6,5},{7,4},{8,11},{9,10},{10,... | collective-permute-start | bytes 129032 | tf_op jit(solution)/shard_map/ppermute | solution.py:130
  107.2 5.3 %early_grads.1.refs_4_ = f32[1008,768]{1,0:T(8,128)} custom-call(bf16[576,224]{1,0:T(8,128)(2,1)} %get-tuple-element.77.refs_0_, bf16[1152,224]{1,0:T(8,128)(2,1)} %get-tuple-element.88.refs_1_, bf16[448,768]{1,0:T(8,128)(2,1)} %refs_2_.5, bf16[224,768]{1,0:T(8,128)(2,1)} %get-tuple-element.89.refs_3_, bf16[576,768]{1,0:T(8,128)(2,1)} %bitcast.16, ...), custom_call_target="tpu_custom_call" | custom-call | tf_op jit(solution)/shard_map/early_grads/pallas_call | solution.py:112
  113.8 3.8 %collective-permute-done.10.refs_1_ = bf16[112,768]{1,0:T(8,128)(2,1)S(1)} collective-permute-done((bf16[112,768]{1,0:T(8,128)(2,1)S(1)}, bf16[112,768]{1,0:T(8,128)(2,1)S(1)}, u32[]{:S(2)}, u32[]{:S(2)}) %collective-permute-start.10) | collective-permute-done | bytes 172064 | tf_op jit(solution)/shard_map/ppermute | solution.py:130
  120.7 3.4 %collective-permute-start.23 = (bf16[384,448]{1,0:T(8,128)(2,1)S(1)}, bf16[384,448]{1,0:T(8,128)(2,1)S(1)}, u32[]{:S(2)}, u32[]{:S(2)}) collective-permute-start(bf16[384,448]{1,0:T(8,128)(2,1)S(1)} %get-tuple-element.101), channel_id=1, source_target_pairs={{0,8},{4,12},{8,0},{12,4},{16,24},{20,28},{24,16},{28,20},{1,9},{5... | collective-permute-start | bytes 1032200 | tf_op jit(solution)/shard_map/ppermute | solution.py:130
  124.0 2.8 %collective-permute-start.24 = (bf16[384,448]{1,0:T(8,128)(2,1)S(1)}, bf16[384,448]{1,0:T(8,128)(2,1)S(1)}, u32[]{:S(2)}, u32[]{:S(2)}) collective-permute-start(bf16[384,448]{1,0:T(8,128)(2,1)S(1)} %get-tuple-element.102), channel_id=1, source_target_pairs={{0,16},{4,20},{8,24},{12,28},{16,0},{20,4},{24,8},{28,12},{1,17},{... | collective-permute-start | bytes 1032200 | tf_op jit(solution)/shard_map/ppermute | solution.py:130
  128.1 5.0 %attention_backward.3 = (f32[384,448]{1,0:T(8,128)S(1)}, f32[192,448]{1,0:T(8,128)S(1)}, bf16[192,448]{1,0:T(8,128)(2,1)S(1)}) custom-call(s32[4]{0:T(128)} %refs_0_.13, s32[8]{0:T(128)} %refs_1_.16, bf16[192,448]{1,0:T(8,128)(2,1)S(1)} %get-tuple-element.71.refs_2_, bf16[192,448]{1,0:T(8,128)(2,1)S(1)} %collective-permute-done.2.refs_3_, ...), custom_call_target="tpu_custom_call" | custom-call | tf_op jit(solution)/shard_map/attention_backward/pallas_call | solution.py:112
  135.4 3.6 %collective-permute-done.30.refs_5_ = bf16[112,768]{1,0:T(8,128)(2,1)S(1)} collective-permute-done((bf16[112,768]{1,0:T(8,128)(2,1)S(1)}, bf16[112,768]{1,0:T(8,128)(2,1)S(1)}, u32[]{:S(2)}, u32[]{:S(2)}) %collective-permute-start.30) | collective-permute-done | bytes 172064 | tf_op jit(solution)/shard_map/ppermute | solution.py:130
  141.3 3.5 %collective-permute-done.24.refs_9_ = bf16[384,448]{1,0:T(8,128)(2,1)S(1)} collective-permute-done((bf16[384,448]{1,0:T(8,128)(2,1)S(1)}, bf16[384,448]{1,0:T(8,128)(2,1)S(1)}, u32[]{:S(2)}, u32[]{:S(2)}) %collective-permute-start.24) | collective-permute-done | bytes 344096 | tf_op jit(solution)/shard_map/ppermute | solution.py:130
  144.8 10.1 %collective-permute-done.25.refs_10_ = bf16[384,448]{1,0:T(8,128)(2,1)S(1)} collective-permute-done((bf16[384,448]{1,0:T(8,128)(2,1)S(1)}, bf16[384,448]{1,0:T(8,128)(2,1)S(1)}, u32[]{:S(2)}, u32[]{:S(2)}) %collective-permute-start.25) | collective-permute-done | bytes 344096 | tf_op jit(solution)/shard_map/ppermute | solution.py:130
  154.9 2.5 %unproject.1 = (bf16[576,448]{1,0:T(8,128)(2,1)S(1)}, f32[128,768]{1,0:T(8,128)S(1)}, bf16[128,768]{1,0:T(8,128)(2,1)S(1)}, bf16[128,768]{1,0:T(8,128)(2,1)S(1)}, bf16[128,768]{1,0:T(8,128)(2,1)S(1)}) custom-call(bf16[448,768]{1,0:T(8,128)(2,1)S(1)} %copy-done, bf16[576,768]{1,0:T(8,128)(2,1)S(1)} %bitcast.13, f32[32,448]{1,0:T(8,128)S(1)} %copy-done.5, ...), custom_call_target="tpu_custom_call" | custom-call | tf_op jit(solution)/shard_map/unproject/pallas_call | solution.py:112
  160.1 2.4 %collective-permute-start.27 = (bf16[128,768]{1,0:T(8,128)(2,1)S(1)}, bf16[128,768]{1,0:T(8,128)(2,1)S(1)}, u32[]{:S(2)}, u32[]{:S(2)}) collective-permute-start(bf16[128,768]{1,0:T(8,128)(2,1)S(1)} %get-tuple-element.106), channel_id=1, source_target_pairs={{0,2},{1,3},{2,0},{3,1},{4,6},{5,7},{6,4},{7,5},{8,10},{9,11},{10,... | collective-permute-start | bytes 589832 | tf_op jit(solution)/shard_map/ppermute | solution.py:130
  165.3 4.8 %collective-permute-done.26.refs_4_ = bf16[128,768]{1,0:T(8,128)(2,1)S(1)} collective-permute-done((bf16[128,768]{1,0:T(8,128)(2,1)S(1)}, bf16[128,768]{1,0:T(8,128)(2,1)S(1)}, u32[]{:S(2)}, u32[]{:S(2)}) %collective-permute-start.26) | collective-permute-done | bytes 196640 | tf_op jit(solution)/shard_map/ppermute | solution.py:130
  170.0 7.2 %collective-permute-done.27.refs_5_ = bf16[128,768]{1,0:T(8,128)(2,1)S(1)} collective-permute-done((bf16[128,768]{1,0:T(8,128)(2,1)S(1)}, bf16[128,768]{1,0:T(8,128)(2,1)S(1)}, u32[]{:S(2)}, u32[]{:S(2)}) %collective-permute-start.27) | collective-permute-done | bytes 196640 | tf_op jit(solution)/shard_map/ppermute | solution.py:130
  178.6 4.1 %collective-permute-start.33 = (bf16[112,768]{1,0:T(8,128)(2,1)S(1)}, bf16[112,768]{1,0:T(8,128)(2,1)S(1)}, u32[]{:S(2)}, u32[]{:S(2)}) collective-permute-start(bf16[112,768]{1,0:T(8,128)(2,1)S(1)} %get-tuple-element.113.refs_0_), channel_id=1, source_target_pairs={{0,1},{1,0},{2,3},{3,2},{4,5},{5,4},{6,7},{7,6},{8,9},{9,8},{10,11... | collective-permute-start | bytes 516104 | tf_op jit(solution)/shard_map/ppermute | solution.py:130
  183.0 3.1 %collective-permute-start.38 = (bf16[192,384]{1,0:T(8,128)(2,1)S(1)}, bf16[192,384]{1,0:T(8,128)(2,1)S(1)}, u32[]{:S(2)}, u32[]{:S(2)}) collective-permute-start(bf16[192,384]{1,0:T(8,128)(2,1)S(1)} %get-tuple-element.117), channel_id=1, source_target_pairs={{0,24},{4,28},{8,16},{12,20},{16,8},{20,12},{24,0},{28,4},{1,25},{... | collective-permute-start | bytes 442376 | tf_op jit(solution)/shard_map/ppermute | solution.py:130
  189.1 2.4 %collective-permute-start.35 = (bf16[112,768]{1,0:T(8,128)(2,1)S(1)}, bf16[112,768]{1,0:T(8,128)(2,1)S(1)}, u32[]{:S(2)}, u32[]{:S(2)}) collective-permute-start(bf16[112,768]{1,0:T(8,128)(2,1)S(1)} %get-tuple-element.113.refs_0_), channel_id=1, source_target_pairs={{0,3},{1,2},{2,1},{3,0},{4,7},{5,6},{6,5},{7,4},{8,11},{9,10},{10,... | collective-permute-start | bytes 516104 | tf_op jit(solution)/shard_map/ppermute | solution.py:130
  196.2 3.8 %collective-permute-done.34.refs_2_ = bf16[112,768]{1,0:T(8,128)(2,1)S(1)} collective-permute-done((bf16[112,768]{1,0:T(8,128)(2,1)S(1)}, bf16[112,768]{1,0:T(8,128)(2,1)S(1)}, u32[]{:S(2)}, u32[]{:S(2)}) %collective-permute-start.34) | collective-permute-done | bytes 172064 | tf_op jit(solution)/shard_map/ppermute | solution.py:130
  200.9 9.6 %all-reduce.2.cloned.1.call-done.refs_0_ = f32[1008,768]{1,0:T(8,128)} async-done(((f32[1008,768]{1,0:T(8,128)}), f32[1008,768]{1,0:T(8,128)}) %all-reduce.2.cloned.1.call-update) | async-done | bytes 3096592 | tf_op jit(solution)/shard_map/psum | solution.py:1138
  210.5 3.3 %parted.1 = (f32[288,768]{1,0:T(8,128)}, f32[576,768]{1,0:T(8,128)}) custom-call(f32[1008,768]{1,0:T(8,128)} %all-reduce.2.cloned.1.call-done.refs_0_), custom_call_target="tpu_custom_call" | custom-call | tf_op jit(solution)/shard_map/parted/pallas_call | solution.py:112
  (108 shorter events, 48.6 us)
Async XLA Ops:
  7.2 63.6 %all-gather.2.cloned.1.call-start = ((), (), s32[]{:S(2)}) async-start(), calls=%async_computation | async-start | bytes 1474560 | tf_op jit(solution)/shard_map/all_gather | solution.py:1111
  7.9 51.4 %collective-permute-start = (bf16[576,768]{1,0:T(8,128)(2,1)}, bf16[576,768]{1,0:T(8,128)(2,1)S(1)}, u32[]{:S(2)}, u32[]{:S(2)}) collective-permute-start(bf16[576,768]{1,0:T(8,128)(2,1)} %bitcast.14), channel_id=1, source_target_pairs={{0,1},{1,0},{2,3},{3,2},{4,5},{5,4},{6,7},{7,6},{8,9},{9,8},{10,11... | collective-permute-start | bytes 2654216 | tf_op jit(solution)/shard_map/ppermute | solution.py:130
  15.1 44.2 %collective-permute-start.1 = (bf16[288,768]{1,0:T(8,128)(2,1)S(1)}, bf16[288,768]{1,0:T(8,128)(2,1)S(1)}, u32[]{:S(2)}, u32[]{:S(2)}) collective-permute-start(bf16[288,768]{1,0:T(8,128)(2,1)S(1)} %copy-done.9), channel_id=1, source_target_pairs={{0,1},{1,0},{2,3},{3,2},{4,5},{5,4},{6,7},{7,6},{8,9},{9,8},{10,11... | collective-permute-start | bytes 1327112 | tf_op jit(solution)/shard_map/ppermute | solution.py:130
  15.2 12.0 %collective-permute-start.5 = (bf16[384,448]{1,0:T(8,128)(2,1)S(1)}, bf16[384,448]{1,0:T(8,128)(2,1)S(1)}, u32[]{:S(2)}, u32[]{:S(2)}) collective-permute-start(bf16[384,448]{1,0:T(8,128)(2,1)S(1)} %get-tuple-element.72.refs_4_.refs_10_), channel_id=1, source_target_pairs={{0,8},{4,12},{8,0},{12,4},{16,24},{20,28},{24,16},{28,20},{1,9},{5... | collective-permute-start | bytes 1032200 | tf_op jit(solution)/shard_map/ppermute | solution.py:130
  17.1 19.3 %collective-permute-start.3 = (bf16[384,448]{1,0:T(8,128)(2,1)S(1)}, bf16[384,448]{1,0:T(8,128)(2,1)S(1)}, u32[]{:S(2)}, u32[]{:S(2)}) collective-permute-start(bf16[384,448]{1,0:T(8,128)(2,1)S(1)} %get-tuple-element.72.refs_4_.refs_10_), channel_id=1, source_target_pairs={{0,16},{4,20},{8,24},{12,28},{16,0},{20,4},{24,8},{28,12},{1,17},{... | collective-permute-start | bytes 1032200 | tf_op jit(solution)/shard_map/ppermute | solution.py:130
  18.6 17.8 %collective-permute-start.4 = (bf16[384,448]{1,0:T(8,128)(2,1)S(1)}, bf16[384,448]{1,0:T(8,128)(2,1)S(1)}, u32[]{:S(2)}, u32[]{:S(2)}) collective-permute-start(bf16[384,448]{1,0:T(8,128)(2,1)S(1)} %get-tuple-element.72.refs_4_.refs_10_), channel_id=1, source_target_pairs={{0,24},{4,28},{8,16},{12,20},{16,8},{20,12},{24,0},{28,4},{1,25},{... | collective-permute-start | bytes 1032200 | tf_op jit(solution)/shard_map/ppermute | solution.py:130
  66.8 11.5 %collective-permute-start.8 = (bf16[192,224]{1,0:T(8,128)(2,1)S(1)}, bf16[192,224]{1,0:T(8,128)(2,1)S(1)}, u32[]{:S(2)}, u32[]{:S(2)}) collective-permute-start(bf16[192,224]{1,0:T(8,128)(2,1)S(1)} %get-tuple-element.75.refs_6_), channel_id=1, source_target_pairs={{0,2},{1,3},{2,0},{3,1},{4,6},{5,7},{6,4},{7,5},{8,10},{9,11},{10,... | collective-permute-start | bytes 258056 | tf_op jit(solution)/shard_map/ppermute | solution.py:130
  84.4 21.8 %collective-permute-start.15 = (bf16[224,768]{1,0:T(8,128)(2,1)}, bf16[224,768]{1,0:T(8,128)(2,1)S(1)}, u32[]{:S(2)}, u32[]{:S(2)}) collective-permute-start(bf16[224,768]{1,0:T(8,128)(2,1)} %get-tuple-element.89.refs_3_), channel_id=1, source_target_pairs={{0,1},{1,0},{2,3},{3,2},{4,5},{5,4},{6,7},{7,6},{8,9},{9,8},{10,11... | collective-permute-start | bytes 1032200 | tf_op jit(solution)/shard_map/ppermute | solution.py:130
  86.6 11.0 %collective-permute-start.11 = (bf16[112,768]{1,0:T(8,128)(2,1)}, bf16[112,768]{1,0:T(8,128)(2,1)S(1)}, u32[]{:S(2)}, u32[]{:S(2)}) collective-permute-start(bf16[112,768]{1,0:T(8,128)(2,1)} %get-tuple-element.83), channel_id=1, source_target_pairs={{0,2},{1,3},{2,0},{3,1},{4,6},{5,7},{6,4},{7,5},{8,10},{9,11},{10,... | collective-permute-start | bytes 516104 | tf_op jit(solution)/shard_map/ppermute | solution.py:130
  100.3 12.3 %collective-permute-start.12 = (bf16[112,192]{1,0:T(8,128)(2,1)S(1)}, bf16[112,192]{1,0:T(8,128)(2,1)S(1)}, u32[]{:S(2)}, u32[]{:S(2)}) collective-permute-start(bf16[112,192]{1,0:T(8,128)(2,1)S(1)} %get-tuple-element.85), channel_id=1, source_target_pairs={{0,1},{1,0},{2,3},{3,2},{4,5},{5,4},{6,7},{7,6},{8,9},{9,8},{10,11... | collective-permute-start | bytes 129032 | tf_op jit(solution)/shard_map/ppermute | solution.py:130
  106.2 12.5 %collective-permute-start.20 = (bf16[192,448]{1,0:T(8,128)(2,1)S(1)}, bf16[192,448]{1,0:T(8,128)(2,1)S(1)}, u32[]{:S(2)}, u32[]{:S(2)}) collective-permute-start(bf16[192,448]{1,0:T(8,128)(2,1)S(1)} %get-tuple-element.95.refs_6_.refs_2_), channel_id=1, source_target_pairs={{0,4},{4,0},{8,12},{12,8},{16,20},{20,16},{24,28},{28,24},{1,5},{5... | collective-permute-start | bytes 516104 | tf_op jit(solution)/shard_map/ppermute | solution.py:130
  106.2 11.5 %collective-permute-start.10 = (bf16[112,768]{1,0:T(8,128)(2,1)S(1)}, bf16[112,768]{1,0:T(8,128)(2,1)S(1)}, u32[]{:S(2)}, u32[]{:S(2)}) collective-permute-start(bf16[112,768]{1,0:T(8,128)(2,1)S(1)} %copy-done.11), channel_id=1, source_target_pairs={{0,2},{1,3},{2,0},{3,1},{4,6},{5,7},{6,4},{7,5},{8,10},{9,11},{10,... | collective-permute-start | bytes 516104 | tf_op jit(solution)/shard_map/ppermute | solution.py:130
  112.8 97.6 %all-reduce.2.cloned.1.call-start = ((), (), s32[]{:S(2)}) async-start(), calls=%async_computation.1 | async-start | bytes 6193152 | tf_op jit(solution)/shard_map/psum | solution.py:1138
  120.7 20.7 %collective-permute-start.23 = (bf16[384,448]{1,0:T(8,128)(2,1)S(1)}, bf16[384,448]{1,0:T(8,128)(2,1)S(1)}, u32[]{:S(2)}, u32[]{:S(2)}) collective-permute-start(bf16[384,448]{1,0:T(8,128)(2,1)S(1)} %get-tuple-element.101), channel_id=1, source_target_pairs={{0,8},{4,12},{8,0},{12,4},{16,24},{20,28},{24,16},{28,20},{1,9},{5... | collective-permute-start | bytes 1032200 | tf_op jit(solution)/shard_map/ppermute | solution.py:130
  124.0 20.8 %collective-permute-start.24 = (bf16[384,448]{1,0:T(8,128)(2,1)S(1)}, bf16[384,448]{1,0:T(8,128)(2,1)S(1)}, u32[]{:S(2)}, u32[]{:S(2)}) collective-permute-start(bf16[384,448]{1,0:T(8,128)(2,1)S(1)} %get-tuple-element.102), channel_id=1, source_target_pairs={{0,16},{4,20},{8,24},{12,28},{16,0},{20,4},{24,8},{28,12},{1,17},{... | collective-permute-start | bytes 1032200 | tf_op jit(solution)/shard_map/ppermute | solution.py:130
  126.8 28.0 %collective-permute-start.25 = (bf16[384,448]{1,0:T(8,128)(2,1)S(1)}, bf16[384,448]{1,0:T(8,128)(2,1)S(1)}, u32[]{:S(2)}, u32[]{:S(2)}) collective-permute-start(bf16[384,448]{1,0:T(8,128)(2,1)S(1)} %get-tuple-element.103), channel_id=1, source_target_pairs={{0,24},{4,28},{8,16},{12,20},{16,8},{20,12},{24,0},{28,4},{1,25},{... | collective-permute-start | bytes 1032200 | tf_op jit(solution)/shard_map/ppermute | solution.py:130
  128.1 10.9 %collective-permute-start.30 = (bf16[112,768]{1,0:T(8,128)(2,1)S(1)}, bf16[112,768]{1,0:T(8,128)(2,1)S(1)}, u32[]{:S(2)}, u32[]{:S(2)}) collective-permute-start(bf16[112,768]{1,0:T(8,128)(2,1)S(1)} %copy-done.3), channel_id=1, source_target_pairs={{0,2},{1,3},{2,0},{3,1},{4,6},{5,7},{6,4},{7,5},{8,10},{9,11},{10,... | collective-permute-start | bytes 516104 | tf_op jit(solution)/shard_map/ppermute | solution.py:130
  139.0 18.4 %collective-permute-start.29 = (bf16[112,768]{1,0:T(8,128)(2,1)S(1)}, bf16[112,768]{1,0:T(8,128)(2,1)S(1)}, u32[]{:S(2)}, u32[]{:S(2)}) collective-permute-start(bf16[112,768]{1,0:T(8,128)(2,1)S(1)} %copy-done.3), channel_id=1, source_target_pairs={{0,1},{1,0},{2,3},{3,2},{4,5},{5,4},{6,7},{7,6},{8,9},{9,8},{10,11... | collective-permute-start | bytes 516104 | tf_op jit(solution)/shard_map/ppermute | solution.py:130
  139.0 18.4 %collective-permute-start.17 = (bf16[112,768]{1,0:T(8,128)(2,1)S(1)}, bf16[112,768]{1,0:T(8,128)(2,1)S(1)}, u32[]{:S(2)}, u32[]{:S(2)}) collective-permute-start(bf16[112,768]{1,0:T(8,128)(2,1)S(1)} %total_of.2.refs_0_.refs_13_.refs_11_), channel_id=1, source_target_pairs={{0,2},{1,3},{2,0},{3,1},{4,6},{5,7},{6,4},{7,5},{8,10},{9,11},{10,... | collective-permute-start | bytes 516104 | tf_op jit(solution)/shard_map/ppermute | solution.py:130
  141.3 16.1 %collective-permute-start.31 = (bf16[112,768]{1,0:T(8,128)(2,1)S(1)}, bf16[112,768]{1,0:T(8,128)(2,1)S(1)}, u32[]{:S(2)}, u32[]{:S(2)}) collective-permute-start(bf16[112,768]{1,0:T(8,128)(2,1)S(1)} %collective-permute-done.30.refs_5_), channel_id=1, source_target_pairs={{0,1},{1,0},{2,3},{3,2},{4,5},{5,4},{6,7},{7,6},{8,9},{9,8},{10,11... | collective-permute-start | bytes 516104 | tf_op jit(solution)/shard_map/ppermute | solution.py:130
  158.6 11.5 %collective-permute-start.26 = (bf16[128,768]{1,0:T(8,128)(2,1)S(1)}, bf16[128,768]{1,0:T(8,128)(2,1)S(1)}, u32[]{:S(2)}, u32[]{:S(2)}) collective-permute-start(bf16[128,768]{1,0:T(8,128)(2,1)S(1)} %get-tuple-element.105), channel_id=1, source_target_pairs={{0,1},{1,0},{2,3},{3,2},{4,5},{5,4},{6,7},{7,6},{8,9},{9,8},{10,11... | collective-permute-start | bytes 589832 | tf_op jit(solution)/shard_map/ppermute | solution.py:130
  160.1 17.2 %collective-permute-start.27 = (bf16[128,768]{1,0:T(8,128)(2,1)S(1)}, bf16[128,768]{1,0:T(8,128)(2,1)S(1)}, u32[]{:S(2)}, u32[]{:S(2)}) collective-permute-start(bf16[128,768]{1,0:T(8,128)(2,1)S(1)} %get-tuple-element.106), channel_id=1, source_target_pairs={{0,2},{1,3},{2,0},{3,1},{4,6},{5,7},{6,4},{7,5},{8,10},{9,11},{10,... | collective-permute-start | bytes 589832 | tf_op jit(solution)/shard_map/ppermute | solution.py:130
  162.5 14.7 %collective-permute-start.28 = (bf16[128,768]{1,0:T(8,128)(2,1)S(1)}, bf16[128,768]{1,0:T(8,128)(2,1)S(1)}, u32[]{:S(2)}, u32[]{:S(2)}) collective-permute-start(bf16[128,768]{1,0:T(8,128)(2,1)S(1)} %get-tuple-element.107), channel_id=1, source_target_pairs={{0,3},{1,2},{2,1},{3,0},{4,7},{5,6},{6,5},{7,4},{8,11},{9,10},{10,... | collective-permute-start | bytes 589832 | tf_op jit(solution)/shard_map/ppermute | solution.py:130
  163.0 20.0 %collective-permute-start.16 = (bf16[112,768]{1,0:T(8,128)(2,1)S(1)}, bf16[112,768]{1,0:T(8,128)(2,1)S(1)}, u32[]{:S(2)}, u32[]{:S(2)}) collective-permute-start(bf16[112,768]{1,0:T(8,128)(2,1)S(1)} %total_of.2.refs_0_.refs_13_.refs_11_), channel_id=1, source_target_pairs={{0,1},{1,0},{2,3},{3,2},{4,5},{5,4},{6,7},{7,6},{8,9},{9,8},{10,11... | collective-permute-start | bytes 516104 | tf_op jit(solution)/shard_map/ppermute | solution.py:130
  163.6 22.6 %collective-permute-start.18 = (bf16[112,768]{1,0:T(8,128)(2,1)S(1)}, bf16[112,768]{1,0:T(8,128)(2,1)S(1)}, u32[]{:S(2)}, u32[]{:S(2)}) collective-permute-start(bf16[112,768]{1,0:T(8,128)(2,1)S(1)} %collective-permute-done.17.refs_2_.refs_7_), channel_id=1, source_target_pairs={{0,1},{1,0},{2,3},{3,2},{4,5},{5,4},{6,7},{7,6},{8,9},{9,8},{10,11... | collective-permute-start | bytes 516104 | tf_op jit(solution)/shard_map/ppermute | solution.py:130
  178.6 16.2 %collective-permute-start.33 = (bf16[112,768]{1,0:T(8,128)(2,1)S(1)}, bf16[112,768]{1,0:T(8,128)(2,1)S(1)}, u32[]{:S(2)}, u32[]{:S(2)}) collective-permute-start(bf16[112,768]{1,0:T(8,128)(2,1)S(1)} %get-tuple-element.113.refs_0_), channel_id=1, source_target_pairs={{0,1},{1,0},{2,3},{3,2},{4,5},{5,4},{6,7},{7,6},{8,9},{9,8},{10,11... | collective-permute-start | bytes 516104 | tf_op jit(solution)/shard_map/ppermute | solution.py:130
  182.9 9.6 %collective-permute-start.37 = (bf16[192,384]{1,0:T(8,128)(2,1)S(1)}, bf16[192,384]{1,0:T(8,128)(2,1)S(1)}, u32[]{:S(2)}, u32[]{:S(2)}) collective-permute-start(bf16[192,384]{1,0:T(8,128)(2,1)S(1)} %get-tuple-element.116), channel_id=1, source_target_pairs={{0,16},{4,20},{8,24},{12,28},{16,0},{20,4},{24,8},{28,12},{1,17},{... | collective-permute-start | bytes 442376 | tf_op jit(solution)/shard_map/ppermute | solution.py:130
  186.1 13.8 %collective-permute-start.34 = (bf16[112,768]{1,0:T(8,128)(2,1)S(1)}, bf16[112,768]{1,0:T(8,128)(2,1)S(1)}, u32[]{:S(2)}, u32[]{:S(2)}) collective-permute-start(bf16[112,768]{1,0:T(8,128)(2,1)S(1)} %get-tuple-element.113.refs_0_), channel_id=1, source_target_pairs={{0,2},{1,3},{2,0},{3,1},{4,6},{5,7},{6,4},{7,5},{8,10},{9,11},{10,... | collective-permute-start | bytes 516104 | tf_op jit(solution)/shard_map/ppermute | solution.py:130
  189.1 10.8 %collective-permute-start.35 = (bf16[112,768]{1,0:T(8,128)(2,1)S(1)}, bf16[112,768]{1,0:T(8,128)(2,1)S(1)}, u32[]{:S(2)}, u32[]{:S(2)}) collective-permute-start(bf16[112,768]{1,0:T(8,128)(2,1)S(1)} %get-tuple-element.113.refs_0_), channel_id=1, source_target_pairs={{0,3},{1,2},{2,1},{3,0},{4,7},{5,6},{6,5},{7,4},{8,11},{9,10},{10,... | collective-permute-start | bytes 516104 | tf_op jit(solution)/shard_map/ppermute | solution.py:130
  192.6 21.2 %collective-permute-start.39 = (bf16[208,384]{1,0:T(8,128)(2,1)S(1)}, bf16[208,384]{1,0:T(8,128)(2,1)S(1)}, u32[]{:S(2)}, u32[]{:S(2)}) collective-permute-start(bf16[208,384]{1,0:T(8,128)(2,1)S(1)} %sum_piece.1.refs_0_), channel_id=1, source_target_pairs={{0,8},{4,12},{8,0},{12,4},{16,24},{20,28},{24,16},{28,20},{1,9},{5... | collective-permute-start | bytes 479240 | tf_op jit(solution)/shard_map/ppermute | solution.py:130
  194.2 19.6 %collective-permute-start.40 = (bf16[208,384]{1,0:T(8,128)(2,1)S(1)}, bf16[208,384]{1,0:T(8,128)(2,1)S(1)}, u32[]{:S(2)}, u32[]{:S(2)}) collective-permute-start(bf16[208,384]{1,0:T(8,128)(2,1)S(1)} %sum_piece.1.refs_0_), channel_id=1, source_target_pairs={{0,16},{4,20},{8,24},{12,28},{16,0},{20,4},{24,8},{28,12},{1,17},{... | collective-permute-start | bytes 479240 | tf_op jit(solution)/shard_map/ppermute | solution.py:130
  194.8 19.0 %collective-permute-start.41 = (bf16[208,384]{1,0:T(8,128)(2,1)S(1)}, bf16[208,384]{1,0:T(8,128)(2,1)S(1)}, u32[]{:S(2)}, u32[]{:S(2)}) collective-permute-start(bf16[208,384]{1,0:T(8,128)(2,1)S(1)} %sum_piece.1.refs_0_), channel_id=1, source_target_pairs={{0,24},{4,28},{8,16},{12,20},{16,8},{20,12},{24,0},{28,4},{1,25},{... | collective-permute-start | bytes 479240 | tf_op jit(solution)/shard_map/ppermute | solution.py:130
  (25 other events, 312.7 us)
Sparse Core Ops, SparseCore 0:
  9.6 48.4 all-gather.1
  117.0 93.4 all-reduce.1

commit v7 on v6

--- a/solution.py
+++ b/solution.py
@@ -49,7 +49,7 @@
     return array if kind in ("v", "free") else pltpu.with_memory_space_constraint(array, pltpu.HBM)
 
 
-def call(name, kernel, ins, outs, scratch=(), mib=16, after=(), lazy=False):
+def call(name, kernel, ins, outs, scratch=(), mib=16, after=(), lazy=False, flops=0):
     fetched = [i for i, given in enumerate(ins) if given[1] not in ("v", "raw", "free")]
     left = [i for i, out in enumerate(outs) if out[2] == "h"]
 
@@ -122,6 +122,9 @@
         + [pltpu.VMEM(outs[i][0], outs[i][1]) for i in left]
         + [pltpu.SemaphoreType.DMA((max(count, 1),))],
         name=name,
+        cost_estimate=pl.CostEstimate(flops=flops, bytes_accessed=0, transcendentals=0)
+        if flops
+        else None,
         compiler_params=params(mib),
     )(*[pin(*given) for given in ins], *[pin(*given) for given in after])
 
@@ -499,15 +502,48 @@
     )
 
 
-def stage_kernel(x_any, cot_any, w_any, in_any, in_pair, down_any, down_pair, *refs):
+def pick_kernel(in_any, down_any, out_ref, sems):
+    core = lax.axis_index("seq") % 2
+    at = 0
+    copies = []
+    for n, source in enumerate((in_any, down_any)):
+        rows = source.shape[0] // 2
+        mine = pl.ds(pl.multiple_of(core * rows, rows), rows)
+        copies.append(
+            pltpu.make_async_copy(source.at[mine], out_ref.at[pl.ds(at, rows)], sems.at[n])
+        )
+        at += rows
+    for copy in copies:
+        copy.start()
+    for copy in copies:
+        copy.wait()
+
+
+def pick(in_t, w_down):
+    (out,) = call(
+        "pick",
+        pick_kernel,
+        kinds((in_t, w_down), "raw"),
+        [(((in_t.shape[0] + w_down.shape[0]) // 2, in_t.shape[1]), BF16, "v")],
+        [pltpu.SemaphoreType.DMA((2,))],
+    )
+    return out
+
+
+def stage_kernel(x_any, cot_any, w_any, in_any, down_any, got_ref, rest_ref, *refs):
     x_ref, cot_ref, w_ref, in_ref, down_ref, sems = refs
     half = x_ref.shape[0]
+    core = lax.axis_index("seq") % 2
     mine = pl.ds(pl.multiple_of(lax.axis_index("tp") % 2 * half, half), half)
     moves = [(w_any, w_ref), (x_any.at[mine], x_ref), (cot_any.at[mine], cot_ref)]
-    for (own, pair), ref in (((down_any, down_pair), down_ref), ((in_any, in_pair), in_ref)):
-        rows = own.shape[0]
-        moves.append((own, ref.at[pl.ds(0, rows)]))
-        moves.append((pair, ref.at[pl.ds(rows, rows)]))
+    at = 0
+    for own, ref in ((in_any, in_ref), (down_any, down_ref)):
+        rows = own.shape[0] // 2
+        moves.append((own, ref.at[pl.ds(0, 2 * rows)]))
+        for source, side in ((got_ref, core), (rest_ref, 1 - core)):
+            spot = pl.multiple_of(2 * rows + side * rows, rows)
+            moves.append((source.at[pl.ds(at, rows)], ref.at[pl.ds(spot, rows)]))
+        at += rows
     copies = [pltpu.make_async_copy(*move, sems.at[n]) for n, move in enumerate(moves)]
     for copy in copies:
         copy.start()
@@ -515,12 +551,12 @@
         copy.wait()
 
 
-def stage(tokens, cotangent, w_full, in_t, in_pair, w_down, down_pair):
+def stage(tokens, cotangent, w_full, in_t, w_down, got, rest):
     rows, model = tokens.shape
     return call(
         "stage",
         stage_kernel,
-        kinds((tokens, cotangent, w_full, in_t, in_pair, w_down, down_pair), "raw"),
+        kinds((tokens, cotangent, w_full, in_t, w_down), "raw") + kinds((got, rest), "free"),
         [
             ((rows // 2, model), BF16, "v"),
             ((rows // 2, model), BF16, "v"),
@@ -528,7 +564,7 @@
             ((2 * in_t.shape[0], model), BF16, "v"),
             ((2 * w_down.shape[0], model), BF16, "v"),
         ],
-        [pltpu.SemaphoreType.DMA((7,))],
+        [pltpu.SemaphoreType.DMA((9,))],
     )
 
 
@@ -788,13 +824,9 @@
     )
 
 
-def input_kernel(n_tp, x_ref, gain_ref, grad_ref, *refs):
-    arrived = refs[:n_tp]
-    out_ref, gain_out = refs[n_tp:]
+def input_kernel(x_ref, gain_ref, grad_ref, sum_ref, out_ref, gain_out):
     part, model = grad_ref.shape
-    total = arrived[0][...]
-    for ref in arrived[1:]:
-        total = total + ref[...].astype(F32)
+    total = sum_ref[...]
     unit, scale = normed(x_ref[...].astype(F32))
     gain = gain_ref[...].reshape(1, -1)
     value = grad_ref[...] + norm_back(unit, scale, total[:part], gain)
@@ -802,12 +834,12 @@
     gain_out[...] = total[part : part + 8]
 
 
-def input_side(tokens, gain, middle_grad, arrived, after):
+def input_side(tokens, gain, middle_grad, summed, after):
     part, model = middle_grad.shape
     return call(
         "input_side",
-        functools.partial(input_kernel, len(arrived)),
-        [(tokens, part), (gain, "h"), (middle_grad, "v")] + kinds(arrived, "v"),
+        input_kernel,
+        [(tokens, part), (gain, "h"), (middle_grad, "v"), (summed, "v")],
         [((part, model), BF16, "v"), ((8, model), F32, "v")],
         (),
         16,
@@ -840,7 +872,7 @@
         "early_grads",
         early_kernel,
         kinds((mixed, gate_grad, cotangent, h_two, in_t, w_down), "h") + [(h_pair, "v")],
-        [((7 * units // 2, model), F32, "h")],
+        [((25 * units // 6, model), F32, "h")],
         [
             pltpu.VMEM((2 * units, half), F32),
             pltpu.VMEM((units, half), F32),
@@ -1022,13 +1054,11 @@
     )
 
 
-def down_kernel(mixed_ref, w_ref, w_pair, middle_ref, keep_ref, *refs):
+def down_kernel(mixed_ref, w_ref, middle_ref, keep_ref, *refs):
     send_refs, total = refs[:-1], refs[-1]
     part = keep_ref.shape[0]
-    units = w_ref.shape[0]
     tp = lax.axis_index("tp")
-    total[...] = mm(mixed_ref[:units, :], w_ref[...], TN)
-    total[...] += mm(mixed_ref[units:, :], w_pair[...], TN)
+    total[...] = mm(mixed_ref[...], w_ref[...], TN)
     own = pl.ds(pl.multiple_of(tp // 2 * part, part), part)
     keep_ref[...] = total[own, :] + middle_ref[own, :]
     for n, ref in enumerate(send_refs):
@@ -1036,13 +1066,13 @@
         ref[...] = total[at, :].astype(ref.dtype)
 
 
-def down(n_tp, mixed, w_down, down_pair, middle, after):
+def down(n_tp, mixed, w_both, middle, after):
     rows, model = middle.shape
     part = 2 * rows // n_tp
     return call(
         "down",
         down_kernel,
-        kinds((mixed, w_down, down_pair, middle), "h"),
+        [(mixed, "h"), (w_both, "v"), (middle, "h")],
         [((part, model), F32, "h")] + [((part, model), BF16, "h")] * (n_tp // 2 - 1),
         [pltpu.VMEM((rows, model), F32)],
         16,
@@ -1057,7 +1087,7 @@
     refs[count][...] = total.astype(refs[count].dtype)
 
 
-def total_of(parts, dtype=BF16, kind="v", after=()):
+def total_of(parts, dtype=BF16, kind="v", after=(), flops=0):
     (out,) = call(
         "total_of",
         functools.partial(total_kernel, len(parts)),
@@ -1066,6 +1096,7 @@
         (),
         16,
         after,
+        flops=flops,
     )
     return out
 
@@ -1109,48 +1140,46 @@
     blocks = [kv] + [over_chips(kv, j) for j in range(1, count)]
     q_pair = over_cores(queries)
     w_full = lax.all_gather(w_out, "tp", axis=0, tiled=True)
-    in_pair = over_tp(in_t, 1)
-    down_pair = over_tp(w_down, 1)
+    got = over_tp(pick(in_t, w_down), 1)
 
     split = (count + 1) // 2
     (state,) = attention_forward(0, False, *docs, queries, q_pair, blocks[:split])
     state_own, state_pair = attention_forward(
-        split, True, *docs, queries, q_pair, blocks[split:], state, kinds((in_pair, down_pair), "h")
+        split, True, *docs, queries, q_pair, blocks[split:], state
     )
     out_b, totals, out_mine, out_other = join(state_own, over_cores(state_pair))
     outs = [out_mine] + [over_tp(out_other if k % 2 else out_mine, k) for k in range(1, n_tp)]
     out_pair = over_cores(out_b)
     totals_pair = over_cores(totals)
 
-    staged = stage(tokens, cotangent, w_full, in_t, in_pair, w_down, down_pair)
+    staged = stage(tokens, cotangent, w_full, in_t, w_down, got, over_cores(got))
     middle, middle_part, h_two, mixed, gate_grad, gain_two_part, own, *others = feed(
         gain_two, staged, outs
     )
     arrived = [own] + [over_tp(others[n], 2 * n + 2) for n in range(n_tp // 2 - 1)]
-    own, *others = down(n_tp, mixed, w_down, down_pair, middle, ())
+    early = early_grads(
+        mixed, gate_grad, cotangent, h_two, in_t, w_down, over_tp(h_two, 1), ()
+    )
     middle_grad, branch_grad, *pieces = branch(
-        n_tp, middle_part, cotangent, gain_two, w_full, arrived, [(own, "h")]
-    )
-    h_pair = over_tp(h_two, 1)
-    early = early_grads(
-        mixed, gate_grad, cotangent, h_two, in_t, w_down, h_pair, [(branch_grad, "h")]
+        n_tp, middle_part, cotangent, gain_two, w_full, arrived, [(early, "h")]
     )
     early_sum = lax.psum(early, "seq")
+    own, *others = down(n_tp, mixed, staged[4], middle, [(branch_grad, "h")])
     grad_down, grad_in = parted(early_sum, (units, 2 * units))
-    out_grad = lay_turned(everywhere(pieces), [(early, "h")])
+    out_grad = lay_turned(everywhere(pieces), [(own, "h")])
     grad_pair = over_cores(out_grad)
     branches = by_steps(branch_grad)
 
+    held = (queries, q_pair, out_grad, grad_pair, out_b, out_pair, totals, totals_pair)
+    *terms, dq = attention_backward(1, False, *docs, held, blocks[1:], None)
     total = total_of(
         [own] + [over_tp(others[n], 2 * n + 2) for n in range(n_tp // 2 - 1)],
         BF16,
         "h",
-        [(out_grad, "v")],
+        [(dq, "v")],
     )
     totals_all = by_steps(total)
 
-    held = (queries, q_pair, out_grad, grad_pair, out_b, out_pair, totals, totals_pair)
-    *terms, dq = attention_backward(1, False, *docs, held, blocks[1:], None, [(total, "v")])
     dkv, dq_own, dq_pair = attention_backward(0, True, *docs, held, blocks[:1], dq)
     dkvs = [dkv] + [over_chips(terms[j - 1], j) for j in range(1, count)]
 
@@ -1169,15 +1198,17 @@
     layer_out = stack_parts(totals_all)
     keep, send = late_grads(proj_grad, h_one, out_b, branches, [(totals_all[n_tp // 2], "v")])
     own, *others = spread(count, keep, over_cores(send))
-    chip_sum = total_of([own] + [over_chips(others[k - 1], k) for k in range(1, count)], F32)
-    input_part, gains = input_side(
-        tokens, gain_one, middle_grad, everywhere(parts), [(own, "v")]
-    )
+    came = everywhere(parts)
+    summed = total_of(came[:2] + came[:1:-1], F32, flops=500_000_000)
+    chip_sum = total_of(
+        [own] + [over_chips(others[k - 1], k) for k in range(1, count)], F32, "v", [(summed, "v")]
+    )
+    input_part, gains = input_side(tokens, gain_one, middle_grad, summed, [(chip_sum, "v")])
     inputs_all = everywhere([input_part] * n_tp)
-    piece = sum_piece(gains, [chip_sum], [(layer_out, "h")])
+    piece = sum_piece(gains, [chip_sum], [])
     input_grad = stack_parts(inputs_all)
     collected = collect(
-        [piece] + [over_chips(piece, k) for k in range(1, count)], [(input_grad, "h"), (grad_down, "h")]
+        [piece] + [over_chips(piece, k) for k in range(1, count)], [(input_grad, "h"), (layer_out, "h"), (grad_down, "h")]
     )
     grad_qkv, grad_out, grad_one, grad_two = finish(
         collected, over_cores(collected), 3 * width

time: 227 us -> 210 us (0.925); the launches traced: 225 us -> 211 us
  waiting for transfers between devices: 101 us -> 77.1 us
  Pallas kernels: 49.5 us -> 64 us
  starting transfers between devices: 57.9 us -> 51.8 us
    ppermute x43, waiting for transfers between devices: 90.5 us -> 68.5 us  [swap(): return lax.ppermute(x, axis, [(i, i ^ hop) for i in range(count)])]
    pallas_call x24 -> x26, Pallas kernels: 49.5 us -> 64 us  [call(): pl.pallas_call(run, out_shape=tuple((shaped(shape, dtype) if kind == 'v'...]
    ppermute x43, starting transfers between devices: 57.6 us -> 51.6 us  [swap(): return lax.ppermute(x, axis, [(i, i ^ hop) for i in range(count)])]
  transfers between devices with their start and end apart: 45 -> 45, of which waited for: 16 -> 18; matrix products, arithmetic and copies ran while one was open for 0% -> 0% of each run, Pallas kernels for 18% -> 25%
where the time goes in v7:
time: 210 us; the launch traced here: 211 us
  waiting for transfers between devices  77.1 us (37%)
  Pallas kernels  64 us (30%)
  starting transfers between devices  51.8 us (25%)
  between operations  14.6 us (7%)
  local copies, waits for them, and re-layouts  3.06 us (1%)
    ppermute x43, waiting for transfers between devices, swap(): return lax.ppermute(x, axis, [(i, i ^ hop) for i in range(count)])  68.5 us
    pallas_call x26, Pallas kernels, call(): pl.pallas_call(run, out_shape=tuple((shaped(shape, dtype) if kind == 'v'...  64 us
    ppermute x43, starting transfers between devices, swap(): return lax.ppermute(x, axis, [(i, i ^ hop) for i in range(count)])  51.6 us
    psum x1, waiting for transfers between devices, body(): early_sum = lax.psum(early, 'seq')  7.42 us
  transfers between devices with their start and end apart: 45, of which 18 were waited for; matrix products, arithmetic and copies ran while one was open for 0% of the time, Pallas kernels for 25%

profile of v7, /device:TPU:0, one launch (start us, length us, event | category | flops | bytes accessed | tf_op | source)
XLA Modules:
  0.0 210.6 jit_solution(10903403624928660202)
XLA Ops:
  9.0 3.1 %collective-permute-start = (bf16[432,768]{1,0:T(8,128)(2,1)S(1)}, bf16[432,768]{1,0:T(8,128)(2,1)S(1)}, u32[]{:S(2)}, u32[]{:S(2)}) collective-permute-start(bf16[432,768]{1,0:T(8,128)(2,1)S(1)} %pick.1), channel_id=1, source_target_pairs={{0,1},{1,0},{2,3},{3,2},{4,5},{5,4},{6,7},{7,6},{8,9},{9,8},{10,11... | collective-permute-start | bytes 1990664 | tf_op jit(solution)/shard_map/ppermute | solution.py:133
  12.1 4.0 %project.1 = (bf16[192,448]{1,0:T(8,128)(2,1)S(1)}, bf16[384,448]{1,0:T(8,128)(2,1)S(1)}, bf16[448,768]{1,0:T(8,128)(2,1)}, f32[32,448]{1,0:T(8,128)}, f32[32,448]{1,0:T(8,128)}) custom-call(s32[4]{0:T(128)} %refs_0_.13, s32[8]{0:T(128)} %refs_1_.16, bf16[448,768]{1,0:T(8,128)(2,1)} %refs_0_.15, bf16[576,768]{1,0:T(8,128)(2,1)} %bitcast.12, f32[768]{0:T(1024)} %refs_1_.17, ...), custom_call_target="tpu_custom_call" | custom-call | tf_op jit(solution)/shard_map/project/pallas_call | solution.py:112
  19.7 18.1 %collective-permute-done.refs_5_ = bf16[432,768]{1,0:T(8,128)(2,1)S(1)} collective-permute-done((bf16[432,768]{1,0:T(8,128)(2,1)S(1)}, bf16[432,768]{1,0:T(8,128)(2,1)S(1)}, u32[]{:S(2)}, u32[]{:S(2)}) %collective-permute-start) | collective-permute-done | bytes 663584 | tf_op jit(solution)/shard_map/ppermute | solution.py:133
  37.8 4.3 %attention_forward.2.refs_6_ = f32[6,80,448]{2,1,0:T(8,128)S(1)} custom-call(s32[4]{0:T(128)} %refs_0_.13, s32[8]{0:T(128)} %refs_1_.16, bf16[192,448]{1,0:T(8,128)(2,1)S(1)} %get-tuple-element.71.refs_2_, bf16[192,448]{1,0:T(8,128)(2,1)S(1)} %collective-permute-done.2.refs_3_, bf16[384,448]{1,0:T(8,128)(2,1)S(1)} %get-tuple-element.72.refs_4_.refs_10_, ...), custom_call_target="tpu_custom_call" | custom-call | tf_op jit(solution)/shard_map/attention_forward/pallas_call | solution.py:112
  42.1 7.1 %attention_forward.3 = (f32[3,80,448]{2,1,0:T(8,128)S(1)}, f32[3,80,448]{2,1,0:T(8,128)S(1)}) custom-call(s32[4]{0:T(128)} %refs_0_.13, s32[8]{0:T(128)} %refs_1_.16, bf16[192,448]{1,0:T(8,128)(2,1)S(1)} %get-tuple-element.71.refs_2_, bf16[192,448]{1,0:T(8,128)(2,1)S(1)} %collective-permute-done.2.refs_3_, ...), custom_call_target="tpu_custom_call" | custom-call | tf_op jit(solution)/shard_map/attention_forward/pallas_call | solution.py:112
  52.1 9.9 %collective-permute-start.8 = (bf16[192,224]{1,0:T(8,128)(2,1)S(1)}, bf16[192,224]{1,0:T(8,128)(2,1)S(1)}, u32[]{:S(2)}, u32[]{:S(2)}) collective-permute-start(bf16[192,224]{1,0:T(8,128)(2,1)S(1)} %get-tuple-element.75.refs_6_), channel_id=1, source_target_pairs={{0,2},{1,3},{2,0},{3,1},{4,6},{5,7},{6,4},{7,5},{8,10},{9,11},{10,... | collective-permute-start | bytes 258056 | tf_op jit(solution)/shard_map/ppermute | solution.py:133
  65.0 2.1 stage.1
  67.1 2.6 %collective-permute-done.8.refs_8_ = bf16[192,224]{1,0:T(8,128)(2,1)S(1)} collective-permute-done((bf16[192,224]{1,0:T(8,128)(2,1)S(1)}, bf16[192,224]{1,0:T(8,128)(2,1)S(1)}, u32[]{:S(2)}, u32[]{:S(2)}) %collective-permute-start.8) | collective-permute-done | bytes 86048 | tf_op jit(solution)/shard_map/ppermute | solution.py:133
  69.7 6.2 %feed.1 = (f32[224,768]{1,0:T(8,128)}, f32[112,768]{1,0:T(8,128)}, bf16[224,768]{1,0:T(8,128)(2,1)}, bf16[576,224]{1,0:T(8,128)(2,1)}, bf16[1152,224]{1,0:T(8,12...) custom-call(bf16[224,768]{1,0:T(8,128)(2,1)S(1)} %get-tuple-element.66.refs_0_, ...), custom_call_target="tpu_custom_call" | custom-call | tf_op jit(solution)/shard_map/feed/pallas_call | solution.py:112
  75.9 2.0 collective-permute-start.11
  79.1 10.4 %collective-permute-done.11.refs_6_ = bf16[224,768]{1,0:T(8,128)(2,1)S(1)} collective-permute-done((bf16[224,768]{1,0:T(8,128)(2,1)}, bf16[224,768]{1,0:T(8,128)(2,1)S(1)}, u32[]{:S(2)}, u32[]{:S(2)}) %collective-permute-start.11) | collective-permute-done | bytes 344096 | tf_op jit(solution)/shard_map/ppermute | solution.py:133
  89.5 5.6 %early_grads.1.refs_6_ = f32[1200,768]{1,0:T(8,128)} custom-call(bf16[576,224]{1,0:T(8,128)(2,1)} %get-tuple-element.77.refs_0_, bf16[1152,224]{1,0:T(8,128)(2,1)} %get-tuple-element.82.refs_1_, bf16[448,768]{1,0:T(8,128)(2,1)} %refs_1_.14, bf16[224,768]{1,0:T(8,128)(2,1)} %get-tuple-element.83.refs_3_, bf16[576,768]{1,0:T(8,128)(2,1)} %bitcast.16, ...), custom_call_target="tpu_custom_call" | custom-call | tf_op jit(solution)/shard_map/early_grads/pallas_call | solution.py:112
  95.1 2.7 %branch.1 = (f32[112,768]{1,0:T(8,128)}, bf16[112,768]{1,0:T(8,128)(2,1)}, bf16[112,192]{1,0:T(8,128)(2,1)S(1)}, bf16[112,192]{1,0:T(8,128)(2,1)S(1)}, bf16[112,...) custom-call(f32[112,768]{1,0:T(8,128)} %get-tuple-element.79.refs_0_, bf16[448,768]{1,0:T(8,128)(2,1)} %refs_1_.14, ...), custom_call_target="tpu_custom_call" | custom-call | tf_op jit(solution)/shard_map/branch/pallas_call | solution.py:112
  98.6 2.9 %collective-permute-start.14 = (bf16[112,192]{1,0:T(8,128)(2,1)S(1)}, bf16[112,192]{1,0:T(8,128)(2,1)S(1)}, u32[]{:S(2)}, u32[]{:S(2)}) collective-permute-start(bf16[112,192]{1,0:T(8,128)(2,1)S(1)} %get-tuple-element.89), channel_id=1, source_target_pairs={{0,2},{1,3},{2,0},{3,1},{4,6},{5,7},{6,4},{7,5},{8,10},{9,11},{10,... | collective-permute-start | bytes 129032 | tf_op jit(solution)/shard_map/ppermute | solution.py:133
  103.0 2.5 %down.1 = (f32[112,768]{1,0:T(8,128)}, bf16[112,768]{1,0:T(8,128)(2,1)}) custom-call(bf16[576,224]{1,0:T(8,128)(2,1)} %get-tuple-element.77.refs_0_, bf16[576,768]{1,0:T(8,128)(2,1)S(1)} %get-tuple-element.70.refs_4_.refs_1_, f32[224,768]{1,0:T(8,128)} %get-tuple-element.78.refs_2_, bf16[112,768]{1,0:T(8,128)(2,1)} %get-tuple-element.84.refs_3_), custom_call_target="tpu_custom_call" | custom-call | tf_op jit(solution)/shard_map/down/pallas_call | solution.py:112
  109.3 9.0 %attention_backward.2 = (bf16[384,448]{1,0:T(8,128)(2,1)S(1)}, bf16[384,448]{1,0:T(8,128)(2,1)S(1)}, bf16[384,448]{1,0:T(8,128)(2,1)S(1)}, f32[6,64,448]{2,1,0:T(8,128)S(1)}) custom-call(s32[4]{0:T(128)} %refs_0_.13, s32[8]{0:T(128)} %refs_1_.16, bf16[192,448]{1,0:T(8,128)(2,1)S(1)} %get-tuple-element.71.refs_2_, ...), custom_call_target="tpu_custom_call" | custom-call | tf_op jit(solution)/shard_map/attention_backward/pallas_call | solution.py:112
  118.4 3.1 %collective-permute-start.24 = (bf16[384,448]{1,0:T(8,128)(2,1)S(1)}, bf16[384,448]{1,0:T(8,128)(2,1)S(1)}, u32[]{:S(2)}, u32[]{:S(2)}) collective-permute-start(bf16[384,448]{1,0:T(8,128)(2,1)S(1)} %get-tuple-element.102), channel_id=1, source_target_pairs={{0,16},{4,20},{8,24},{12,28},{16,0},{20,4},{24,8},{28,12},{1,17},{... | collective-permute-start | bytes 1032200 | tf_op jit(solution)/shard_map/ppermute | solution.py:133
  123.9 5.2 %attention_backward.3 = (f32[384,448]{1,0:T(8,128)S(1)}, f32[192,448]{1,0:T(8,128)S(1)}, bf16[192,448]{1,0:T(8,128)(2,1)S(1)}) custom-call(s32[4]{0:T(128)} %refs_0_.13, s32[8]{0:T(128)} %refs_1_.16, bf16[192,448]{1,0:T(8,128)(2,1)S(1)} %get-tuple-element.71.refs_2_, bf16[192,448]{1,0:T(8,128)(2,1)S(1)} %collective-permute-done.2.refs_3_, ...), custom_call_target="tpu_custom_call" | custom-call | tf_op jit(solution)/shard_map/attention_backward/pallas_call | solution.py:112
  133.8 2.6 %collective-permute-start.20 = (bf16[112,768]{1,0:T(8,128)(2,1)S(1)}, bf16[112,768]{1,0:T(8,128)(2,1)S(1)}, u32[]{:S(2)}, u32[]{:S(2)}) collective-permute-start(bf16[112,768]{1,0:T(8,128)(2,1)S(1)} %total_of.3.refs_0_.refs_11_), channel_id=1, source_target_pairs={{0,2},{1,3},{2,0},{3,1},{4,6},{5,7},{6,4},{7,5},{8,10},{9,11},{10,... | collective-permute-start | bytes 516104 | tf_op jit(solution)/shard_map/ppermute | solution.py:133
  136.4 7.0 %collective-permute-done.25.refs_10_ = bf16[384,448]{1,0:T(8,128)(2,1)S(1)} collective-permute-done((bf16[384,448]{1,0:T(8,128)(2,1)S(1)}, bf16[384,448]{1,0:T(8,128)(2,1)S(1)}, u32[]{:S(2)}, u32[]{:S(2)}) %collective-permute-start.25) | collective-permute-done | bytes 344096 | tf_op jit(solution)/shard_map/ppermute | solution.py:133
  143.4 2.5 %unproject.1 = (bf16[576,448]{1,0:T(8,128)(2,1)S(1)}, f32[128,768]{1,0:T(8,128)S(1)}, bf16[128,768]{1,0:T(8,128)(2,1)S(1)}, bf16[128,768]{1,0:T(8,128)(2,1)S(1)}, bf16[128,768]{1,0:T(8,128)(2,1)S(1)}) custom-call(bf16[448,768]{1,0:T(8,128)(2,1)S(1)} %copy-done, bf16[576,768]{1,0:T(8,128)(2,1)S(1)} %bitcast.13, f32[32,448]{1,0:T(8,128)S(1)} %copy-done.9, ...), custom_call_target="tpu_custom_call" | custom-call | tf_op jit(solution)/shard_map/unproject/pallas_call | solution.py:112
  148.6 2.4 %collective-permute-start.27 = (bf16[128,768]{1,0:T(8,128)(2,1)S(1)}, bf16[128,768]{1,0:T(8,128)(2,1)S(1)}, u32[]{:S(2)}, u32[]{:S(2)}) collective-permute-start(bf16[128,768]{1,0:T(8,128)(2,1)S(1)} %get-tuple-element.106), channel_id=1, source_target_pairs={{0,3},{1,2},{2,1},{3,0},{4,7},{5,6},{6,5},{7,4},{8,11},{9,10},{10,... | collective-permute-start | bytes 589832 | tf_op jit(solution)/shard_map/ppermute | solution.py:133
  155.4 5.7 %collective-permute-done.27.refs_2_ = bf16[128,768]{1,0:T(8,128)(2,1)S(1)} collective-permute-done((bf16[128,768]{1,0:T(8,128)(2,1)S(1)}, bf16[128,768]{1,0:T(8,128)(2,1)S(1)}, u32[]{:S(2)}, u32[]{:S(2)}) %collective-permute-start.27) | collective-permute-done | bytes 196640 | tf_op jit(solution)/shard_map/ppermute | solution.py:133
  161.0 4.7 %collective-permute-start.19 = (bf16[112,768]{1,0:T(8,128)(2,1)S(1)}, bf16[112,768]{1,0:T(8,128)(2,1)S(1)}, u32[]{:S(2)}, u32[]{:S(2)}) collective-permute-start(bf16[112,768]{1,0:T(8,128)(2,1)S(1)} %total_of.3.refs_0_.refs_11_), channel_id=1, source_target_pairs={{0,1},{1,0},{2,3},{3,2},{4,5},{5,4},{6,7},{7,6},{8,9},{9,8},{10,11... | collective-permute-start | bytes 516104 | tf_op jit(solution)/shard_map/ppermute | solution.py:133
  165.7 3.3 %collective-permute-done.28.refs_3_ = bf16[128,768]{1,0:T(8,128)(2,1)S(1)} collective-permute-done((bf16[128,768]{1,0:T(8,128)(2,1)S(1)}, bf16[128,768]{1,0:T(8,128)(2,1)S(1)}, u32[]{:S(2)}, u32[]{:S(2)}) %collective-permute-start.28) | collective-permute-done | bytes 196640 | tf_op jit(solution)/shard_map/ppermute | solution.py:133
  170.5 2.1 collective-permute-start.36
  175.7 3.2 %collective-permute-done.21.refs_3_ = bf16[112,768]{1,0:T(8,128)(2,1)S(1)} collective-permute-done((bf16[112,768]{1,0:T(8,128)(2,1)S(1)}, bf16[112,768]{1,0:T(8,128)(2,1)S(1)}, u32[]{:S(2)}, u32[]{:S(2)}) %collective-permute-start.21) | collective-permute-done | bytes 172064 | tf_op jit(solution)/shard_map/ppermute | solution.py:133
  179.4 2.1 %collective-permute-done.36.refs_1_ = bf16[112,768]{1,0:T(8,128)(2,1)S(1)} collective-permute-done((bf16[112,768]{1,0:T(8,128)(2,1)S(1)}, bf16[112,768]{1,0:T(8,128)(2,1)S(1)}, u32[]{:S(2)}, u32[]{:S(2)}) %collective-permute-start.36) | collective-permute-done | bytes 172064 | tf_op jit(solution)/shard_map/ppermute | solution.py:133
  182.5 5.5 %collective-permute-done.37.refs_2_ = bf16[112,768]{1,0:T(8,128)(2,1)S(1)} collective-permute-done((bf16[112,768]{1,0:T(8,128)(2,1)S(1)}, bf16[112,768]{1,0:T(8,128)(2,1)S(1)}, u32[]{:S(2)}, u32[]{:S(2)}) %collective-permute-start.37) | collective-permute-done | bytes 172064 | tf_op jit(solution)/shard_map/ppermute | solution.py:133
  189.0 7.4 %all-reduce.2.cloned.1.call-done.refs_0_ = f32[1200,768]{1,0:T(8,128)} async-done(((f32[1200,768]{1,0:T(8,128)}), f32[1200,768]{1,0:T(8,128)}) %all-reduce.2.cloned.1.call-update) | async-done | bytes 3686416 | tf_op jit(solution)/shard_map/psum | solution.py:1166
  196.4 3.3 %parted.1 = (f32[288,768]{1,0:T(8,128)}, f32[576,768]{1,0:T(8,128)}) custom-call(f32[1200,768]{1,0:T(8,128)} %all-reduce.2.cloned.1.call-done.refs_0_), custom_call_target="tpu_custom_call" | custom-call | tf_op jit(solution)/shard_map/parted/pallas_call | solution.py:112
  200.0 2.0 collective-permute-done.42.refs_1_
  (110 shorter events, 41.5 us)
Async XLA Ops:
  7.2 55.7 %all-gather.2.cloned.1.call-start = ((), (), s32[]{:S(2)}) async-start(), calls=%async_computation | async-start | bytes 1474560 | tf_op jit(solution)/shard_map/all_gather | solution.py:1142
  9.0 28.7 %collective-permute-start = (bf16[432,768]{1,0:T(8,128)(2,1)S(1)}, bf16[432,768]{1,0:T(8,128)(2,1)S(1)}, u32[]{:S(2)}, u32[]{:S(2)}) collective-permute-start(bf16[432,768]{1,0:T(8,128)(2,1)S(1)} %pick.1), channel_id=1, source_target_pairs={{0,1},{1,0},{2,3},{3,2},{4,5},{5,4},{6,7},{7,6},{8,9},{9,8},{10,11... | collective-permute-start | bytes 1990664 | tf_op jit(solution)/shard_map/ppermute | solution.py:133
  16.1 21.7 %collective-permute-start.5 = (bf16[384,448]{1,0:T(8,128)(2,1)S(1)}, bf16[384,448]{1,0:T(8,128)(2,1)S(1)}, u32[]{:S(2)}, u32[]{:S(2)}) collective-permute-start(bf16[384,448]{1,0:T(8,128)(2,1)S(1)} %get-tuple-element.72.refs_4_.refs_10_), channel_id=1, source_target_pairs={{0,8},{4,12},{8,0},{12,4},{16,24},{20,28},{24,16},{28,20},{1,9},{5... | collective-permute-start | bytes 1032200 | tf_op jit(solution)/shard_map/ppermute | solution.py:133
  17.7 24.4 %collective-permute-start.3 = (bf16[384,448]{1,0:T(8,128)(2,1)S(1)}, bf16[384,448]{1,0:T(8,128)(2,1)S(1)}, u32[]{:S(2)}, u32[]{:S(2)}) collective-permute-start(bf16[384,448]{1,0:T(8,128)(2,1)S(1)} %get-tuple-element.72.refs_4_.refs_10_), channel_id=1, source_target_pairs={{0,16},{4,20},{8,24},{12,28},{16,0},{20,4},{24,8},{28,12},{1,17},{... | collective-permute-start | bytes 1032200 | tf_op jit(solution)/shard_map/ppermute | solution.py:133
  19.2 22.9 %collective-permute-start.4 = (bf16[384,448]{1,0:T(8,128)(2,1)S(1)}, bf16[384,448]{1,0:T(8,128)(2,1)S(1)}, u32[]{:S(2)}, u32[]{:S(2)}) collective-permute-start(bf16[384,448]{1,0:T(8,128)(2,1)S(1)} %get-tuple-element.72.refs_4_.refs_10_), channel_id=1, source_target_pairs={{0,24},{4,28},{8,16},{12,20},{16,8},{20,12},{24,0},{28,4},{1,25},{... | collective-permute-start | bytes 1032200 | tf_op jit(solution)/shard_map/ppermute | solution.py:133
  19.7 18.1 %collective-permute-start.2 = (bf16[192,448]{1,0:T(8,128)(2,1)S(1)}, bf16[192,448]{1,0:T(8,128)(2,1)S(1)}, u32[]{:S(2)}, u32[]{:S(2)}) collective-permute-start(bf16[192,448]{1,0:T(8,128)(2,1)S(1)} %get-tuple-element.71.refs_2_), channel_id=1, source_target_pairs={{0,4},{4,0},{8,12},{12,8},{16,20},{20,16},{24,28},{28,24},{1,5},{5... | collective-permute-start | bytes 516104 | tf_op jit(solution)/shard_map/ppermute | solution.py:133
  37.8 24.3 %collective-permute-start.1 = (bf16[432,768]{1,0:T(8,128)(2,1)S(1)}, bf16[432,768]{1,0:T(8,128)(2,1)S(1)}, u32[]{:S(2)}, u32[]{:S(2)}) collective-permute-start(bf16[432,768]{1,0:T(8,128)(2,1)S(1)} %collective-permute-done.refs_5_), channel_id=1, source_target_pairs={{0,4},{4,0},{8,12},{12,8},{16,20},{20,16},{24,28},{28,24},{1,5},{5... | collective-permute-start | bytes 1990664 | tf_op jit(solution)/shard_map/ppermute | solution.py:133
  52.0 15.1 %collective-permute-start.7 = (bf16[192,224]{1,0:T(8,128)(2,1)}, bf16[192,224]{1,0:T(8,128)(2,1)S(1)}, u32[]{:S(2)}, u32[]{:S(2)}) collective-permute-start(bf16[192,224]{1,0:T(8,128)(2,1)} %get-tuple-element.76), channel_id=1, source_target_pairs={{0,1},{1,0},{2,3},{3,2},{4,5},{5,4},{6,7},{7,6},{8,9},{9,8},{10,11... | collective-permute-start | bytes 258056 | tf_op jit(solution)/shard_map/ppermute | solution.py:133
  52.1 17.7 %collective-permute-start.8 = (bf16[192,224]{1,0:T(8,128)(2,1)S(1)}, bf16[192,224]{1,0:T(8,128)(2,1)S(1)}, u32[]{:S(2)}, u32[]{:S(2)}) collective-permute-start(bf16[192,224]{1,0:T(8,128)(2,1)S(1)} %get-tuple-element.75.refs_6_), channel_id=1, source_target_pairs={{0,2},{1,3},{2,0},{3,1},{4,6},{5,7},{6,4},{7,5},{8,10},{9,11},{10,... | collective-permute-start | bytes 258056 | tf_op jit(solution)/shard_map/ppermute | solution.py:133
  75.9 13.6 %collective-permute-start.11 = (bf16[224,768]{1,0:T(8,128)(2,1)}, bf16[224,768]{1,0:T(8,128)(2,1)S(1)}, u32[]{:S(2)}, u32[]{:S(2)}) collective-permute-start(bf16[224,768]{1,0:T(8,128)(2,1)} %get-tuple-element.83.refs_3_), channel_id=1, source_target_pairs={{0,1},{1,0},{2,3},{3,2},{4,5},{5,4},{6,7},{7,6},{8,9},{9,8},{10,11... | collective-permute-start | bytes 1032200 | tf_op jit(solution)/shard_map/ppermute | solution.py:133
  78.0 17.1 %collective-permute-start.10 = (bf16[112,768]{1,0:T(8,128)(2,1)}, bf16[112,768]{1,0:T(8,128)(2,1)S(1)}, u32[]{:S(2)}, u32[]{:S(2)}) collective-permute-start(bf16[112,768]{1,0:T(8,128)(2,1)} %get-tuple-element.81), channel_id=1, source_target_pairs={{0,2},{1,3},{2,0},{3,1},{4,6},{5,7},{6,4},{7,5},{8,10},{9,11},{10,... | collective-permute-start | bytes 516104 | tf_op jit(solution)/shard_map/ppermute | solution.py:133
  97.8 98.6 %all-reduce.2.cloned.1.call-start = ((), (), s32[]{:S(2)}) async-start(), calls=%async_computation.1 | async-start | bytes 7372800 | tf_op jit(solution)/shard_map/psum | solution.py:1166
  108.3 20.8 %collective-permute-start.12 = (bf16[112,768]{1,0:T(8,128)(2,1)}, bf16[112,768]{1,0:T(8,128)(2,1)S(1)}, u32[]{:S(2)}, u32[]{:S(2)}) collective-permute-start(bf16[112,768]{1,0:T(8,128)(2,1)} %get-tuple-element.86), channel_id=1, source_target_pairs={{0,2},{1,3},{2,0},{3,1},{4,6},{5,7},{6,4},{7,5},{8,10},{9,11},{10,... | collective-permute-start | bytes 516104 | tf_op jit(solution)/shard_map/ppermute | solution.py:133
  118.4 15.4 %collective-permute-start.23 = (bf16[384,448]{1,0:T(8,128)(2,1)S(1)}, bf16[384,448]{1,0:T(8,128)(2,1)S(1)}, u32[]{:S(2)}, u32[]{:S(2)}) collective-permute-start(bf16[384,448]{1,0:T(8,128)(2,1)S(1)} %get-tuple-element.101), channel_id=1, source_target_pairs={{0,8},{4,12},{8,0},{12,4},{16,24},{20,28},{24,16},{28,20},{1,9},{5... | collective-permute-start | bytes 1032200 | tf_op jit(solution)/shard_map/ppermute | solution.py:133
  118.4 17.9 %collective-permute-start.24 = (bf16[384,448]{1,0:T(8,128)(2,1)S(1)}, bf16[384,448]{1,0:T(8,128)(2,1)S(1)}, u32[]{:S(2)}, u32[]{:S(2)}) collective-permute-start(bf16[384,448]{1,0:T(8,128)(2,1)S(1)} %get-tuple-element.102), channel_id=1, source_target_pairs={{0,16},{4,20},{8,24},{12,28},{16,0},{20,4},{24,8},{28,12},{1,17},{... | collective-permute-start | bytes 1032200 | tf_op jit(solution)/shard_map/ppermute | solution.py:133
  121.5 21.9 %collective-permute-start.25 = (bf16[384,448]{1,0:T(8,128)(2,1)S(1)}, bf16[384,448]{1,0:T(8,128)(2,1)S(1)}, u32[]{:S(2)}, u32[]{:S(2)}) collective-permute-start(bf16[384,448]{1,0:T(8,128)(2,1)S(1)} %get-tuple-element.103), channel_id=1, source_target_pairs={{0,24},{4,28},{8,16},{12,20},{16,8},{20,12},{24,0},{28,4},{1,25},{... | collective-permute-start | bytes 1032200 | tf_op jit(solution)/shard_map/ppermute | solution.py:133
  130.4 15.6 %collective-permute-start.29 = (bf16[112,768]{1,0:T(8,128)(2,1)S(1)}, bf16[112,768]{1,0:T(8,128)(2,1)S(1)}, u32[]{:S(2)}, u32[]{:S(2)}) collective-permute-start(bf16[112,768]{1,0:T(8,128)(2,1)S(1)} %copy-done.3), channel_id=1, source_target_pairs={{0,1},{1,0},{2,3},{3,2},{4,5},{5,4},{6,7},{7,6},{8,9},{9,8},{10,11... | collective-permute-start | bytes 516104 | tf_op jit(solution)/shard_map/ppermute | solution.py:133
  130.6 15.4 %collective-permute-start.31 = (bf16[112,768]{1,0:T(8,128)(2,1)S(1)}, bf16[112,768]{1,0:T(8,128)(2,1)S(1)}, u32[]{:S(2)}, u32[]{:S(2)}) collective-permute-start(bf16[112,768]{1,0:T(8,128)(2,1)S(1)} %collective-permute-done.30.refs_5_), channel_id=1, source_target_pairs={{0,1},{1,0},{2,3},{3,2},{4,5},{5,4},{6,7},{7,6},{8,9},{9,8},{10,11... | collective-permute-start | bytes 516104 | tf_op jit(solution)/shard_map/ppermute | solution.py:133
  133.8 12.2 %collective-permute-start.20 = (bf16[112,768]{1,0:T(8,128)(2,1)S(1)}, bf16[112,768]{1,0:T(8,128)(2,1)S(1)}, u32[]{:S(2)}, u32[]{:S(2)}) collective-permute-start(bf16[112,768]{1,0:T(8,128)(2,1)S(1)} %total_of.3.refs_0_.refs_11_), channel_id=1, source_target_pairs={{0,2},{1,3},{2,0},{3,1},{4,6},{5,7},{6,4},{7,5},{8,10},{9,11},{10,... | collective-permute-start | bytes 516104 | tf_op jit(solution)/shard_map/ppermute | solution.py:133
  148.6 12.4 %collective-permute-start.27 = (bf16[128,768]{1,0:T(8,128)(2,1)S(1)}, bf16[128,768]{1,0:T(8,128)(2,1)S(1)}, u32[]{:S(2)}, u32[]{:S(2)}) collective-permute-start(bf16[128,768]{1,0:T(8,128)(2,1)S(1)} %get-tuple-element.106), channel_id=1, source_target_pairs={{0,3},{1,2},{2,1},{3,0},{4,7},{5,6},{6,5},{7,4},{8,11},{9,10},{10,... | collective-permute-start | bytes 589832 | tf_op jit(solution)/shard_map/ppermute | solution.py:133
  151.0 18.0 %collective-permute-start.28 = (bf16[128,768]{1,0:T(8,128)(2,1)S(1)}, bf16[128,768]{1,0:T(8,128)(2,1)S(1)}, u32[]{:S(2)}, u32[]{:S(2)}) collective-permute-start(bf16[128,768]{1,0:T(8,128)(2,1)S(1)} %get-tuple-element.107), channel_id=1, source_target_pairs={{0,2},{1,3},{2,0},{3,1},{4,6},{5,7},{6,4},{7,5},{8,10},{9,11},{10,... | collective-permute-start | bytes 589832 | tf_op jit(solution)/shard_map/ppermute | solution.py:133
  151.3 17.8 %collective-permute-start.33 = (bf16[192,384]{1,0:T(8,128)(2,1)S(1)}, bf16[192,384]{1,0:T(8,128)(2,1)S(1)}, u32[]{:S(2)}, u32[]{:S(2)}) collective-permute-start(bf16[192,384]{1,0:T(8,128)(2,1)S(1)} %get-tuple-element.113), channel_id=1, source_target_pairs={{0,8},{4,12},{8,0},{12,4},{16,24},{20,28},{24,16},{28,20},{1,9},{5... | collective-permute-start | bytes 442376 | tf_op jit(solution)/shard_map/ppermute | solution.py:133
  151.7 17.4 %collective-permute-start.34 = (bf16[192,384]{1,0:T(8,128)(2,1)S(1)}, bf16[192,384]{1,0:T(8,128)(2,1)S(1)}, u32[]{:S(2)}, u32[]{:S(2)}) collective-permute-start(bf16[192,384]{1,0:T(8,128)(2,1)S(1)} %get-tuple-element.114), channel_id=1, source_target_pairs={{0,16},{4,20},{8,24},{12,28},{16,0},{20,4},{24,8},{28,12},{1,17},{... | collective-permute-start | bytes 442376 | tf_op jit(solution)/shard_map/ppermute | solution.py:133
  154.4 14.7 %collective-permute-start.35 = (bf16[192,384]{1,0:T(8,128)(2,1)S(1)}, bf16[192,384]{1,0:T(8,128)(2,1)S(1)}, u32[]{:S(2)}, u32[]{:S(2)}) collective-permute-start(bf16[192,384]{1,0:T(8,128)(2,1)S(1)} %get-tuple-element.115), channel_id=1, source_target_pairs={{0,24},{4,28},{8,16},{12,20},{16,8},{20,12},{24,0},{28,4},{1,25},{... | collective-permute-start | bytes 442376 | tf_op jit(solution)/shard_map/ppermute | solution.py:133
  161.0 14.3 %collective-permute-start.19 = (bf16[112,768]{1,0:T(8,128)(2,1)S(1)}, bf16[112,768]{1,0:T(8,128)(2,1)S(1)}, u32[]{:S(2)}, u32[]{:S(2)}) collective-permute-start(bf16[112,768]{1,0:T(8,128)(2,1)S(1)} %total_of.3.refs_0_.refs_11_), channel_id=1, source_target_pairs={{0,1},{1,0},{2,3},{3,2},{4,5},{5,4},{6,7},{7,6},{8,9},{9,8},{10,11... | collective-permute-start | bytes 516104 | tf_op jit(solution)/shard_map/ppermute | solution.py:133
  169.0 9.9 %collective-permute-start.21 = (bf16[112,768]{1,0:T(8,128)(2,1)S(1)}, bf16[112,768]{1,0:T(8,128)(2,1)S(1)}, u32[]{:S(2)}, u32[]{:S(2)}) collective-permute-start(bf16[112,768]{1,0:T(8,128)(2,1)S(1)} %collective-permute-done.20.refs_2_.refs_7_), channel_id=1, source_target_pairs={{0,1},{1,0},{2,3},{3,2},{4,5},{5,4},{6,7},{7,6},{8,9},{9,8},{10,11... | collective-permute-start | bytes 516104 | tf_op jit(solution)/shard_map/ppermute | solution.py:133
  170.5 11.0 %collective-permute-start.36 = (bf16[112,768]{1,0:T(8,128)(2,1)S(1)}, bf16[112,768]{1,0:T(8,128)(2,1)S(1)}, u32[]{:S(2)}, u32[]{:S(2)}) collective-permute-start(bf16[112,768]{1,0:T(8,128)(2,1)S(1)} %get-tuple-element.116.refs_0_), channel_id=1, source_target_pairs={{0,1},{1,0},{2,3},{3,2},{4,5},{5,4},{6,7},{7,6},{8,9},{9,8},{10,11... | collective-permute-start | bytes 516104 | tf_op jit(solution)/shard_map/ppermute | solution.py:133
  172.6 15.4 %collective-permute-start.37 = (bf16[112,768]{1,0:T(8,128)(2,1)S(1)}, bf16[112,768]{1,0:T(8,128)(2,1)S(1)}, u32[]{:S(2)}, u32[]{:S(2)}) collective-permute-start(bf16[112,768]{1,0:T(8,128)(2,1)S(1)} %get-tuple-element.116.refs_0_), channel_id=1, source_target_pairs={{0,2},{1,3},{2,0},{3,1},{4,6},{5,7},{6,4},{7,5},{8,10},{9,11},{10,... | collective-permute-start | bytes 516104 | tf_op jit(solution)/shard_map/ppermute | solution.py:133
  173.9 14.2 %collective-permute-start.38 = (bf16[112,768]{1,0:T(8,128)(2,1)S(1)}, bf16[112,768]{1,0:T(8,128)(2,1)S(1)}, u32[]{:S(2)}, u32[]{:S(2)}) collective-permute-start(bf16[112,768]{1,0:T(8,128)(2,1)S(1)} %get-tuple-element.116.refs_0_), channel_id=1, source_target_pairs={{0,3},{1,2},{2,1},{3,0},{4,7},{5,6},{6,5},{7,4},{8,11},{9,10},{10,... | collective-permute-start | bytes 516104 | tf_op jit(solution)/shard_map/ppermute | solution.py:133
  175.3 24.4 %collective-permute-start.39 = (bf16[208,384]{1,0:T(8,128)(2,1)S(1)}, bf16[208,384]{1,0:T(8,128)(2,1)S(1)}, u32[]{:S(2)}, u32[]{:S(2)}) collective-permute-start(bf16[208,384]{1,0:T(8,128)(2,1)S(1)} %sum_piece.1.refs_0_), channel_id=1, source_target_pairs={{0,8},{4,12},{8,0},{12,4},{16,24},{20,28},{24,16},{28,20},{1,9},{5... | collective-permute-start | bytes 479240 | tf_op jit(solution)/shard_map/ppermute | solution.py:133
  178.9 20.9 %collective-permute-start.40 = (bf16[208,384]{1,0:T(8,128)(2,1)S(1)}, bf16[208,384]{1,0:T(8,128)(2,1)S(1)}, u32[]{:S(2)}, u32[]{:S(2)}) collective-permute-start(bf16[208,384]{1,0:T(8,128)(2,1)S(1)} %sum_piece.1.refs_0_), channel_id=1, source_target_pairs={{0,16},{4,20},{8,24},{12,28},{16,0},{20,4},{24,8},{28,12},{1,17},{... | collective-permute-start | bytes 479240 | tf_op jit(solution)/shard_map/ppermute | solution.py:133
  181.6 18.2 %collective-permute-start.41 = (bf16[208,384]{1,0:T(8,128)(2,1)S(1)}, bf16[208,384]{1,0:T(8,128)(2,1)S(1)}, u32[]{:S(2)}, u32[]{:S(2)}) collective-permute-start(bf16[208,384]{1,0:T(8,128)(2,1)S(1)} %sum_piece.1.refs_0_), channel_id=1, source_target_pairs={{0,24},{4,28},{8,16},{12,20},{16,8},{20,12},{24,0},{28,4},{1,25},{... | collective-permute-start | bytes 479240 | tf_op jit(solution)/shard_map/ppermute | solution.py:133
  (25 other events, 211.5 us)
Sparse Core Ops, SparseCore 0:
  9.6 36.7 all-gather.1
  102.0 94.3 all-reduce.1

commit v8 on v7

--- a/solution.py
+++ b/solution.py
@@ -530,6 +530,15 @@
     return out
 
 
+def keep_kernel(in_ref, out_ref):
+    out_ref[...] = in_ref[...]
+
+
+def keep_until(value, after):
+    (out,) = call("keep", keep_kernel, [(value, "v")], [(value.shape, value.dtype, "v")], (), 16, after)
+    return out
+
+
 def stage_kernel(x_any, cot_any, w_any, in_any, down_any, got_ref, rest_ref, *refs):
     x_ref, cot_ref, w_ref, in_ref, down_ref, sems = refs
     half = x_ref.shape[0]
@@ -556,7 +565,7 @@
     return call(
         "stage",
         stage_kernel,
-        kinds((tokens, cotangent, w_full, in_t, w_down), "raw") + kinds((got, rest), "free"),
+        kinds((tokens, cotangent, w_full, in_t, w_down), "raw") + kinds((got, rest), "v"),
         [
             ((rows // 2, model), BF16, "v"),
             ((rows // 2, model), BF16, "v"),
@@ -697,7 +706,7 @@
         "branch",
         functools.partial(branch_kernel, n_tp, len(arrived)),
         [(middle_part, "h"), (cotangent, part)]
-        + kinds((gain, w_full, arrived[0]), "h")
+        + [(gain, "h"), (w_full, "v"), (arrived[0], "h")]
         + kinds(arrived[1:], "v"),
         [((part, model), F32, "h"), ((part, model), BF16, "h")]
         + [((part, width), BF16, "v")] * n_tp,
@@ -742,7 +751,7 @@
         out_ref[at, :] = refs[k][...]
 
 
-def stack_parts(pieces, after=()):
+def stack_parts(pieces, after=(), flops=0):
     part, model = pieces[0].shape
     (out,) = call(
         "stack_parts",
@@ -752,6 +761,7 @@
         (),
         16,
         after,
+        flops=flops,
     )
     return out
 
@@ -847,8 +857,8 @@
     )
 
 
-def early_kernel(mixed_ref, gate_ref, cot_ref, h_ref, in_ref, down_ref, h_pair, out_ref, *refs):
-    gate_up, mixed_grad, mixed, gate = refs
+def early_kernel(mixed_ref, gate_ref, cot_ref, h_ref, in_ref, down_ref, h_pair, *refs):
+    keep_ref, send_ref, gate_up, mixed_grad, mixed, gate = refs
     units = down_ref.shape[0]
     half = h_ref.shape[0]
     bit = lax.axis_index("tp") % 2
@@ -857,22 +867,26 @@
     gate_up[...] = mm(in_ref[...], h_pair[...], NT)
     mixed_grad[...] = mm(down_ref[...], cot_ref[other, :], NT)
     gated(units, 0, gate_up, mixed_grad, mixed, gate)
-    out_ref[:units, :] = mm(mixed_ref[:units, :], cot_ref[mine, :], NN)
-    out_ref[:units, :] += mm(mixed[...], cot_ref[other, :], NN)
-    out_ref[units : 3 * units, :] = mm(gate_ref[: 2 * units, :], h_ref[...], NN)
-    out_ref[units : 3 * units, :] += mm(gate[...], h_pair[...], NN)
-    if out_ref.shape[0] > 3 * units:
-        out_ref[3 * units :, :] = jnp.zeros((out_ref.shape[0] - 3 * units, out_ref.shape[1]), F32)
+    width = keep_ref.shape[1]
+    core = lax.axis_index("seq") % 2
+    for ref, side in ((send_ref, 1 - core), (keep_ref, core)):
+        columns = pl.ds(pl.multiple_of(side * width, width), width)
+        down = mm(mixed_ref[:units, :], cot_ref[mine, columns], NN)
+        down = down + mm(mixed[...], cot_ref[other, columns], NN)
+        ref[:units, :] = down.astype(ref.dtype)
+        both = mm(gate_ref[: 2 * units, :], h_ref[:, columns], NN)
+        both = both + mm(gate[...], h_pair[:, columns], NN)
+        ref[units:, :] = both.astype(ref.dtype)
 
 
 def early_grads(mixed, gate_grad, cotangent, h_two, in_t, w_down, h_pair, after):
     units, model = w_down.shape
     half = h_two.shape[0]
-    (out,) = call(
+    return call(
         "early_grads",
         early_kernel,
         kinds((mixed, gate_grad, cotangent, h_two, in_t, w_down), "h") + [(h_pair, "v")],
-        [((25 * units // 6, model), F32, "h")],
+        [((3 * units, model // 2), F32, "v"), ((3 * units, model // 2), BF16, "v")],
         [
             pltpu.VMEM((2 * units, half), F32),
             pltpu.VMEM((units, half), F32),
@@ -881,30 +895,6 @@
         ],
         24,
         after,
-    )
-    return out
-
-
-def part_kernel(in_any, *refs):
-    out_refs, held, sem = refs[:-2], refs[-2], refs[-1]
-    rows = held.shape[0]
-    copy = pltpu.make_async_copy(in_any.at[pl.ds(0, rows)], held, sem)
-    copy.start()
-    copy.wait()
-    at = 0
-    for ref in out_refs:
-        ref[...] = held[at : at + ref.shape[0], :]
-        at += ref.shape[0]
-
-
-def parted(value, sizes):
-    model = value.shape[1]
-    return call(
-        "parted",
-        part_kernel,
-        [(value, "raw")],
-        [((size, model), F32, "h") for size in sizes],
-        [pltpu.VMEM((sum(sizes), model), F32), pltpu.SemaphoreType.DMA],
     )
 
 
@@ -940,25 +930,32 @@
     )
 
 
-def spread_kernel(count, keep_ref, back_ref, *refs):
-    held = refs[count]
-    piece = refs[0].shape[0]
+def spread_kernel(count, *refs):
+    given, outs, held = refs[: -count - 1], refs[-count - 1 : -1], refs[-1]
+    piece = outs[0].shape[0]
     chip = lax.axis_index("seq") // 2
-    held[...] = keep_ref[...] + back_ref[...].astype(F32)
+    at = 0
+    for keep_ref, back_ref in zip(given[::2], given[1::2]):
+        rows = keep_ref.shape[0]
+        held[at : at + rows, :] = keep_ref[...] + back_ref[...].astype(F32)
+        at += rows
+    if at < held.shape[0]:
+        held[at:, :] = jnp.zeros((held.shape[0] - at, held.shape[1]), F32)
     for k in range(count):
         at = pl.ds(pl.multiple_of((chip ^ k) * piece, piece), piece)
-        refs[k][...] = held[at, :].astype(refs[k].dtype)
-
-
-def spread(count, keep, back):
-    wide, half = keep.shape
-    piece = wide // count
+        outs[k][...] = held[at, :].astype(outs[k].dtype)
+
+
+def spread(count, *pairs):
+    half = pairs[0][0].shape[1]
+    rows = sum(keep.shape[0] for keep, unused in pairs)
+    piece = -(-rows // (8 * count)) * 8
     return call(
         "spread",
         functools.partial(spread_kernel, count),
-        [(keep, "v"), (back, "v")],
+        [(array, "v") for pair in pairs for array in pair],
         [((piece, half), F32, "v")] + [((piece, half), BF16, "v")] * (count - 1),
-        [pltpu.VMEM((wide, half), F32)],
+        [pltpu.VMEM((count * piece, half), F32)],
     )
 
 
@@ -1020,37 +1017,32 @@
     return out
 
 
-def finish_kernel(own_ref, pair_ref, qkv_ref, out_ref, one_ref, two_ref):
+def finish_kernel(sizes, own_ref, pair_ref, *refs):
+    out_refs, gain_refs = refs[: len(sizes)], refs[len(sizes) :]
     half = own_ref.shape[1]
-    wide, tall = qkv_ref.shape[0], out_ref.shape[0]
     core = lax.axis_index("seq") % 2
     for ref, side in ((own_ref, core), (pair_ref, 1 - core)):
         columns = pl.ds(pl.multiple_of(side * half, half), half)
-        qkv_ref[:, columns] = ref[:wide, :].astype(F32)
-        out_ref[:, columns] = ref[wide : wide + tall, :].astype(F32)
-    gains = own_ref[wide + tall :, :].astype(F32) + pair_ref[wide + tall :, :].astype(F32)
-    for at, ref in ((0, one_ref), (2, two_ref)):
+        at = 0
+        for out_ref, size in zip(out_refs, sizes):
+            out_ref[:, columns] = ref[at : at + size, :].astype(F32)
+            at += size
+    first = own_ref.shape[0] - 16
+    gains = own_ref[first:, :].astype(F32) + pair_ref[first:, :].astype(F32)
+    for at, ref in zip((0, 2), gain_refs):
         ref[pl.ds(0, half)] = gains[at]
         ref[pl.ds(half, half)] = gains[at + 1]
 
 
-def finish(own, pair, wide, after=()):
-    half = own.shape[1]
-    tall = own.shape[0] - 16 - wide
-    model = 2 * half
+def finish(own, pair, sizes):
+    model = 2 * own.shape[1]
     return call(
         "finish",
-        finish_kernel,
+        functools.partial(finish_kernel, sizes),
         [(own, "v"), (pair, "v")],
-        [
-            ((wide, model), F32, "h"),
-            ((tall, model), F32, "h"),
-            ((model,), F32, "h"),
-            ((model,), F32, "h"),
-        ],
+        [((size, model), F32, "h") for size in sizes] + [((model,), F32, "h")] * 2,
         (),
-        16,
-        after,
+        24,
     )
 
 
@@ -1152,21 +1144,20 @@
     out_pair = over_cores(out_b)
     totals_pair = over_cores(totals)
 
+    got = keep_until(got, [(state_pair, "v")])
     staged = stage(tokens, cotangent, w_full, in_t, w_down, got, over_cores(got))
     middle, middle_part, h_two, mixed, gate_grad, gain_two_part, own, *others = feed(
         gain_two, staged, outs
     )
     arrived = [own] + [over_tp(others[n], 2 * n + 2) for n in range(n_tp // 2 - 1)]
-    early = early_grads(
-        mixed, gate_grad, cotangent, h_two, in_t, w_down, over_tp(h_two, 1), ()
-    )
+    own, *others = down(n_tp, mixed, staged[4], middle, ())
     middle_grad, branch_grad, *pieces = branch(
-        n_tp, middle_part, cotangent, gain_two, w_full, arrived, [(early, "h")]
-    )
-    early_sum = lax.psum(early, "seq")
-    own, *others = down(n_tp, mixed, staged[4], middle, [(branch_grad, "h")])
-    grad_down, grad_in = parted(early_sum, (units, 2 * units))
-    out_grad = lay_turned(everywhere(pieces), [(own, "h")])
+        n_tp, middle_part, cotangent, gain_two, staged[2], arrived, [(own, "h")]
+    )
+    early, early_send = early_grads(
+        mixed, gate_grad, cotangent, h_two, in_t, w_down, over_tp(h_two, 1), [(branch_grad, "h")]
+    )
+    out_grad = lay_turned(everywhere(pieces), [(early, "v")])
     grad_pair = over_cores(out_grad)
     branches = by_steps(branch_grad)
 
@@ -1197,21 +1188,21 @@
     )
     layer_out = stack_parts(totals_all)
     keep, send = late_grads(proj_grad, h_one, out_b, branches, [(totals_all[n_tp // 2], "v")])
-    own, *others = spread(count, keep, over_cores(send))
+    own, *others = spread(count, (keep, over_cores(send)), (early, over_cores(early_send)))
     came = everywhere(parts)
-    summed = total_of(came[:2] + came[:1:-1], F32, flops=500_000_000)
+    summed = total_of(came[:2] + came[:1:-1], F32, flops=2_000_000_000)
     chip_sum = total_of(
-        [own] + [over_chips(others[k - 1], k) for k in range(1, count)], F32, "v", [(summed, "v")]
-    )
-    input_part, gains = input_side(tokens, gain_one, middle_grad, summed, [(chip_sum, "v")])
+        [own] + [over_chips(others[k - 1], k) for k in range(1, count)], F32, "v", ()
+    )
+    input_part, gains = input_side(tokens, gain_one, middle_grad, summed, [(own, "v")])
     inputs_all = everywhere([input_part] * n_tp)
-    piece = sum_piece(gains, [chip_sum], [])
-    input_grad = stack_parts(inputs_all)
+    piece = sum_piece(gains, [chip_sum], ())
+    input_grad = stack_parts(inputs_all, (), 3_000_000_000)
     collected = collect(
-        [piece] + [over_chips(piece, k) for k in range(1, count)], [(input_grad, "h"), (layer_out, "h"), (grad_down, "h")]
-    )
-    grad_qkv, grad_out, grad_one, grad_two = finish(
-        collected, over_cores(collected), 3 * width
+        [piece] + [over_chips(piece, k) for k in range(1, count)], [(input_grad, "h"), (layer_out, "h")]
+    )
+    grad_qkv, grad_out, grad_down, grad_in, grad_one, grad_two = finish(
+        collected, over_cores(collected), (3 * width, width, units, 2 * units)
     )
 
     back = lambda x, n: x.reshape(-1, n, model).transpose(2, 0, 1)

time: 210 us -> 187 us (0.89); the launches traced: 211 us -> 185 us
  waiting for transfers between devices: 77.1 us -> 55.3 us
  Pallas kernels: 64 us -> 55.3 us
  starting transfers between devices: 51.8 us -> 59.3 us
  local copies, waits for them, and re-layouts: 3.06 us -> 0.91 us
    ppermute x43 -> x44, waiting for transfers between devices: 68.5 us -> 54.7 us  [swap(): return lax.ppermute(x, axis, [(i, i ^ hop) for i in range(count)])]
    pallas_call x26, Pallas kernels: 64 us -> 55.3 us  [call(): pl.pallas_call(run, out_shape=tuple((shaped(shape, dtype) if kind == 'v'...]
    ppermute x43 -> x44, starting transfers between devices: 51.6 us -> 59.3 us  [swap(): return lax.ppermute(x, axis, [(i, i ^ hop) for i in range(count)])]
    psum x1 -> x0, waiting for transfers between devices: 7.42 us -> none  [body(): early_sum = lax.psum(early, 'seq')]
    unnamed x24 -> x18, local copies, waits for them, and re-layouts: 3.06 us -> 0.91 us
  transfers between devices with their start and end apart: 45 -> 45, of which waited for: 18 -> 20; matrix products, arithmetic and copies ran while one was open for 0% -> 0% of each run, Pallas kernels for 25% -> 24%
where the time goes in v8:
time: 187 us; the launch traced here: 185 us
  starting transfers between devices  59.3 us (32%)
  waiting for transfers between devices  55.3 us (30%)
  Pallas kernels  55.3 us (30%)
  between operations  14.5 us (8%)
    ppermute x44, starting transfers between devices, swap(): return lax.ppermute(x, axis, [(i, i ^ hop) for i in range(count)])  59.3 us
    pallas_call x26, Pallas kernels, call(): pl.pallas_call(run, out_shape=tuple((shaped(shape, dtype) if kind == 'v'...  55.3 us
    ppermute x44, waiting for transfers between devices, swap(): return lax.ppermute(x, axis, [(i, i ^ hop) for i in range(count)])  54.7 us
  transfers between devices with their start and end apart: 45, of which 20 were waited for; matrix products, arithmetic and copies ran while one was open for 0% of the time, Pallas kernels for 24%

profile of v8, /device:TPU:0, one launch (start us, length us, event | category | flops | bytes accessed | tf_op | source)
XLA Modules:
  0.0 185.4 jit_solution(11923685637663651633)
XLA Ops:
  9.0 3.1 %collective-permute-start = (bf16[432,768]{1,0:T(8,128)(2,1)S(1)}, bf16[432,768]{1,0:T(8,128)(2,1)S(1)}, u32[]{:S(2)}, u32[]{:S(2)}) collective-permute-start(bf16[432,768]{1,0:T(8,128)(2,1)S(1)} %pick.1), channel_id=1, source_target_pairs={{0,1},{1,0},{2,3},{3,2},{4,5},{5,4},{6,7},{7,6},{8,9},{9,8},{10,11... | collective-permute-start | bytes 1990664 | tf_op jit(solution)/shard_map/ppermute | solution.py:133
  12.1 3.8 %project.1 = (bf16[192,448]{1,0:T(8,128)(2,1)S(1)}, bf16[384,448]{1,0:T(8,128)(2,1)S(1)}, bf16[448,768]{1,0:T(8,128)(2,1)}, f32[32,448]{1,0:T(8,128)}, f32[32,448]{1,0:T(8,128)}) custom-call(s32[4]{0:T(128)} %refs_0_.13, s32[8]{0:T(128)} %refs_1_.16, bf16[448,768]{1,0:T(8,128)(2,1)} %refs_0_.15, bf16[576,768]{1,0:T(8,128)(2,1)} %bitcast.12, f32[768]{0:T(1024)} %refs_1_.17, ...), custom_call_target="tpu_custom_call" | custom-call | tf_op jit(solution)/shard_map/project/pallas_call | solution.py:112
  20.9 7.1 %collective-permute-done.4.refs_5_.refs_10_ = bf16[384,448]{1,0:T(8,128)(2,1)S(1)} collective-permute-done((bf16[384,448]{1,0:T(8,128)(2,1)S(1)}, bf16[384,448]{1,0:T(8,128)(2,1)S(1)}, u32[]{:S(2)}, u32[]{:S(2)}) %collective-permute-start.4) | collective-permute-done | bytes 344096 | tf_op jit(solution)/shard_map/ppermute | solution.py:133
  28.0 7.1 %attention_forward.2.refs_6_ = f32[6,80,448]{2,1,0:T(8,128)S(1)} custom-call(s32[4]{0:T(128)} %refs_0_.13, s32[8]{0:T(128)} %refs_1_.16, bf16[192,448]{1,0:T(8,128)(2,1)S(1)} %get-tuple-element.68.refs_2_, bf16[192,448]{1,0:T(8,128)(2,1)S(1)} %collective-permute-done.1.refs_3_, bf16[384,448]{1,0:T(8,128)(2,1)S(1)} %get-tuple-element.69.refs_4_.refs_10_, ...), custom_call_target="tpu_custom_call" | custom-call | tf_op jit(solution)/shard_map/attention_forward/pallas_call | solution.py:112
  39.1 2.4 %collective-permute-done.6.refs_1_ = f32[3,80,448]{2,1,0:T(8,128)S(1)} collective-permute-done((f32[3,80,448]{2,1,0:T(8,128)S(1)}, f32[3,80,448]{2,1,0:T(8,128)S(1)}, u32[]{:S(2)}, u32[]{:S(2)}) %collective-permute-start.6) | collective-permute-done | bytes 430112 | tf_op jit(solution)/shard_map/ppermute | solution.py:133
  43.2 8.6 %collective-permute-start.8 = (bf16[192,224]{1,0:T(8,128)(2,1)}, bf16[192,224]{1,0:T(8,128)(2,1)}, u32[]{:S(2)}, u32[]{:S(2)}) collective-permute-start(bf16[192,224]{1,0:T(8,128)(2,1)} %get-tuple-element.77.refs_6_), channel_id=1, source_target_pairs={{0,2},{1,3},{2,0},{3,1},{4,6},{5,7},{6,4},{7,5},{8,10},{9,11},{10,... | collective-permute-start | bytes 258056 | tf_op jit(solution)/shard_map/ppermute | solution.py:133
  53.9 6.0 %collective-permute-done.8.refs_8_ = bf16[192,224]{1,0:T(8,128)(2,1)} collective-permute-done((bf16[192,224]{1,0:T(8,128)(2,1)}, bf16[192,224]{1,0:T(8,128)(2,1)}, u32[]{:S(2)}, u32[]{:S(2)}) %collective-permute-start.8) | collective-permute-done | bytes 86048 | tf_op jit(solution)/shard_map/ppermute | solution.py:133
  59.9 7.2 %feed.1 = (f32[224,768]{1,0:T(8,128)}, f32[112,768]{1,0:T(8,128)}, bf16[224,768]{1,0:T(8,128)(2,1)}, bf16[576,224]{1,0:T(8,128)(2,1)}, bf16[1152,224]{1,0:T(8,12...) custom-call(bf16[224,768]{1,0:T(8,128)(2,1)S(1)} %get-tuple-element.71.refs_0_, ...), custom_call_target="tpu_custom_call" | custom-call | tf_op jit(solution)/shard_map/feed/pallas_call | solution.py:112
  70.3 2.5 %down.1 = (f32[112,768]{1,0:T(8,128)}, bf16[112,768]{1,0:T(8,128)(2,1)}) custom-call(bf16[576,224]{1,0:T(8,128)(2,1)} %get-tuple-element.79.refs_0_, bf16[576,768]{1,0:T(8,128)(2,1)S(1)} %get-tuple-element.75.refs_4_.refs_1_, f32[224,768]{1,0:T(8,128)} %get-tuple-element.80.refs_2_), custom_call_target="tpu_custom_call" | custom-call | tf_op jit(solution)/shard_map/down/pallas_call | solution.py:112
  72.8 7.1 %collective-permute-done.11.refs_5_ = bf16[112,768]{1,0:T(8,128)(2,1)S(1)} collective-permute-done((bf16[112,768]{1,0:T(8,128)(2,1)}, bf16[112,768]{1,0:T(8,128)(2,1)S(1)}, u32[]{:S(2)}, u32[]{:S(2)}) %collective-permute-start.11) | collective-permute-done | bytes 172064 | tf_op jit(solution)/shard_map/ppermute | solution.py:133
  79.9 2.6 %branch.1 = (f32[112,768]{1,0:T(8,128)}, bf16[112,768]{1,0:T(8,128)(2,1)}, bf16[112,192]{1,0:T(8,128)(2,1)S(1)}, bf16[112,192]{1,0:T(8,128)(2,1)S(1)}, bf16[112,...) custom-call(f32[112,768]{1,0:T(8,128)} %get-tuple-element.83.refs_0_, bf16[448,768]{1,0:T(8,128)(2,1)} %refs_2_.5, ...), custom_call_target="tpu_custom_call" | custom-call | tf_op jit(solution)/shard_map/branch/pallas_call | solution.py:112
  82.5 3.5 %collective-permute-start.12 = (bf16[112,192]{1,0:T(8,128)(2,1)S(1)}, bf16[112,192]{1,0:T(8,128)(2,1)S(1)}, u32[]{:S(2)}, u32[]{:S(2)}) collective-permute-start(bf16[112,192]{1,0:T(8,128)(2,1)S(1)} %get-tuple-element.87), channel_id=1, source_target_pairs={{0,1},{1,0},{2,3},{3,2},{4,5},{5,4},{6,7},{7,6},{8,9},{9,8},{10,11... | collective-permute-start | bytes 129032 | tf_op jit(solution)/shard_map/ppermute | solution.py:133
  85.9 2.4 %collective-permute-start.14 = (bf16[112,192]{1,0:T(8,128)(2,1)S(1)}, bf16[112,192]{1,0:T(8,128)(2,1)S(1)}, u32[]{:S(2)}, u32[]{:S(2)}) collective-permute-start(bf16[112,192]{1,0:T(8,128)(2,1)S(1)} %get-tuple-element.89), channel_id=1, source_target_pairs={{0,3},{1,2},{2,1},{3,0},{4,7},{5,6},{6,5},{7,4},{8,11},{9,10},{10,... | collective-permute-start | bytes 129032 | tf_op jit(solution)/shard_map/ppermute | solution.py:133
  88.4 4.1 %early_grads.1 = (f32[864,384]{1,0:T(8,128)S(1)}, bf16[864,384]{1,0:T(8,128)(2,1)S(1)}) custom-call(bf16[576,224]{1,0:T(8,128)(2,1)} %get-tuple-element.79.refs_0_, bf16[1152,224]{1,0:T(8,128)(2,1)} %get-tuple-element.90.refs_1_, bf16[448,768]{1,0:T(8,128)(2,1)} %refs_2_.5, bf16[224,768]{1,0:T(8,128)(2,1)} %get-tuple-element.91.refs_3_, ...), custom_call_target="tpu_custom_call" | custom-call | tf_op jit(solution)/shard_map/early_grads/pallas_call | solution.py:112
  94.5 5.5 %attention_backward.2 = (bf16[384,448]{1,0:T(8,128)(2,1)S(1)}, bf16[384,448]{1,0:T(8,128)(2,1)S(1)}, bf16[384,448]{1,0:T(8,128)(2,1)S(1)}, f32[6,64,448]{2,1,0:T(8,128)S(1)}) custom-call(s32[4]{0:T(128)} %refs_0_.13, s32[8]{0:T(128)} %refs_1_.16, bf16[192,448]{1,0:T(8,128)(2,1)S(1)} %get-tuple-element.68.refs_2_, ...), custom_call_target="tpu_custom_call" | custom-call | tf_op jit(solution)/shard_map/attention_backward/pallas_call | solution.py:112
  100.0 3.4 %collective-permute-start.23 = (bf16[384,448]{1,0:T(8,128)(2,1)S(1)}, bf16[384,448]{1,0:T(8,128)(2,1)S(1)}, u32[]{:S(2)}, u32[]{:S(2)}) collective-permute-start(bf16[384,448]{1,0:T(8,128)(2,1)S(1)} %get-tuple-element.104), channel_id=1, source_target_pairs={{0,8},{4,12},{8,0},{12,4},{16,24},{20,28},{24,16},{28,20},{1,9},{5... | collective-permute-start | bytes 1032200 | tf_op jit(solution)/shard_map/ppermute | solution.py:133
  106.7 5.2 %attention_backward.3 = (f32[384,448]{1,0:T(8,128)S(1)}, f32[192,448]{1,0:T(8,128)S(1)}, bf16[192,448]{1,0:T(8,128)(2,1)S(1)}) custom-call(s32[4]{0:T(128)} %refs_0_.13, s32[8]{0:T(128)} %refs_1_.16, bf16[192,448]{1,0:T(8,128)(2,1)S(1)} %get-tuple-element.68.refs_2_, bf16[192,448]{1,0:T(8,128)(2,1)S(1)} %collective-permute-done.1.refs_3_, ...), custom_call_target="tpu_custom_call" | custom-call | tf_op jit(solution)/shard_map/attention_backward/pallas_call | solution.py:112
  116.7 4.3 %collective-permute-done.24.refs_9_ = bf16[384,448]{1,0:T(8,128)(2,1)S(1)} collective-permute-done((bf16[384,448]{1,0:T(8,128)(2,1)S(1)}, bf16[384,448]{1,0:T(8,128)(2,1)S(1)}, u32[]{:S(2)}, u32[]{:S(2)}) %collective-permute-start.24) | collective-permute-done | bytes 344096 | tf_op jit(solution)/shard_map/ppermute | solution.py:133
  121.1 2.5 %unproject.1 = (bf16[576,448]{1,0:T(8,128)(2,1)S(1)}, f32[128,768]{1,0:T(8,128)S(1)}, bf16[128,768]{1,0:T(8,128)(2,1)S(1)}, bf16[128,768]{1,0:T(8,128)(2,1)S(1)}, bf16[128,768]{1,0:T(8,128)(2,1)S(1)}) custom-call(bf16[448,768]{1,0:T(8,128)(2,1)S(1)} %copy-done, bf16[576,768]{1,0:T(8,128)(2,1)S(1)} %bitcast.13, f32[32,448]{1,0:T(8,128)S(1)} %copy-done.5, ...), custom_call_target="tpu_custom_call" | custom-call | tf_op jit(solution)/shard_map/unproject/pallas_call | solution.py:112
  124.8 2.5 %collective-permute-done.31.refs_6_ = bf16[112,768]{1,0:T(8,128)(2,1)S(1)} collective-permute-done((bf16[112,768]{1,0:T(8,128)(2,1)S(1)}, bf16[112,768]{1,0:T(8,128)(2,1)S(1)}, u32[]{:S(2)}, u32[]{:S(2)}) %collective-permute-start.31) | collective-permute-done | bytes 172064 | tf_op jit(solution)/shard_map/ppermute | solution.py:133
  129.6 2.3 %collective-permute-start.27 = (bf16[128,768]{1,0:T(8,128)(2,1)S(1)}, bf16[128,768]{1,0:T(8,128)(2,1)S(1)}, u32[]{:S(2)}, u32[]{:S(2)}) collective-permute-start(bf16[128,768]{1,0:T(8,128)(2,1)S(1)} %get-tuple-element.109), channel_id=1, source_target_pairs={{0,3},{1,2},{2,1},{3,0},{4,7},{5,6},{6,5},{7,4},{8,11},{9,10},{10,... | collective-permute-start | bytes 589832 | tf_op jit(solution)/shard_map/ppermute | solution.py:133
  132.6 2.6 %collective-permute-start.38 = (bf16[408,384]{1,0:T(8,128)(2,1)S(1)}, bf16[408,384]{1,0:T(8,128)(2,1)S(1)}, u32[]{:S(2)}, u32[]{:S(2)}) collective-permute-start(bf16[408,384]{1,0:T(8,128)(2,1)S(1)} %get-tuple-element.120), channel_id=1, source_target_pairs={{0,16},{4,20},{8,24},{12,28},{16,0},{20,4},{24,8},{28,12},{1,17},{... | collective-permute-start | bytes 940040 | tf_op jit(solution)/shard_map/ppermute | solution.py:133
  135.7 2.2 %collective-permute-start.39 = (bf16[408,384]{1,0:T(8,128)(2,1)S(1)}, bf16[408,384]{1,0:T(8,128)(2,1)S(1)}, u32[]{:S(2)}, u32[]{:S(2)}) collective-permute-start(bf16[408,384]{1,0:T(8,128)(2,1)S(1)} %get-tuple-element.121), channel_id=1, source_target_pairs={{0,24},{4,28},{8,16},{12,20},{16,8},{20,12},{24,0},{28,4},{1,25},{... | collective-permute-start | bytes 940040 | tf_op jit(solution)/shard_map/ppermute | solution.py:133
  137.9 3.9 %collective-permute-done.27.refs_2_ = bf16[128,768]{1,0:T(8,128)(2,1)S(1)} collective-permute-done((bf16[128,768]{1,0:T(8,128)(2,1)S(1)}, bf16[128,768]{1,0:T(8,128)(2,1)S(1)}, u32[]{:S(2)}, u32[]{:S(2)}) %collective-permute-start.27) | collective-permute-done | bytes 196640 | tf_op jit(solution)/shard_map/ppermute | solution.py:133
  141.9 4.8 %collective-permute-start.19 = (bf16[112,768]{1,0:T(8,128)(2,1)S(1)}, bf16[112,768]{1,0:T(8,128)(2,1)S(1)}, u32[]{:S(2)}, u32[]{:S(2)}) collective-permute-start(bf16[112,768]{1,0:T(8,128)(2,1)S(1)} %total_of.3.refs_0_.refs_11_), channel_id=1, source_target_pairs={{0,1},{1,0},{2,3},{3,2},{4,5},{5,4},{6,7},{7,6},{8,9},{9,8},{10,11... | collective-permute-start | bytes 516104 | tf_op jit(solution)/shard_map/ppermute | solution.py:133
  146.6 3.0 %collective-permute-done.28.refs_3_ = bf16[128,768]{1,0:T(8,128)(2,1)S(1)} collective-permute-done((bf16[128,768]{1,0:T(8,128)(2,1)S(1)}, bf16[128,768]{1,0:T(8,128)(2,1)S(1)}, u32[]{:S(2)}, u32[]{:S(2)}) %collective-permute-start.28) | collective-permute-done | bytes 196640 | tf_op jit(solution)/shard_map/ppermute | solution.py:133
  151.9 2.1 %collective-permute-start.34 = (bf16[112,768]{1,0:T(8,128)(2,1)S(1)}, bf16[112,768]{1,0:T(8,128)(2,1)S(1)}, u32[]{:S(2)}, u32[]{:S(2)}) collective-permute-start(bf16[112,768]{1,0:T(8,128)(2,1)S(1)} %get-tuple-element.117.refs_0_), channel_id=1, source_target_pairs={{0,1},{1,0},{2,3},{3,2},{4,5},{5,4},{6,7},{7,6},{8,9},{9,8},{10,11... | collective-permute-start | bytes 516104 | tf_op jit(solution)/shard_map/ppermute | solution.py:133
  161.5 2.1 %collective-permute-start.42 = (bf16[424,384]{1,0:T(8,128)(2,1)S(1)}, bf16[424,384]{1,0:T(8,128)(2,1)S(1)}, u32[]{:S(2)}, u32[]{:S(2)}) collective-permute-start(bf16[424,384]{1,0:T(8,128)(2,1)S(1)} %sum_piece.1.refs_0_), channel_id=1, source_target_pairs={{0,24},{4,28},{8,16},{12,20},{16,8},{20,12},{24,0},{28,4},{1,25},{... | collective-permute-start | bytes 976904 | tf_op jit(solution)/shard_map/ppermute | solution.py:133
  164.5 4.5 %collective-permute-done.35.refs_2_ = bf16[112,768]{1,0:T(8,128)(2,1)S(1)} collective-permute-done((bf16[112,768]{1,0:T(8,128)(2,1)S(1)}, bf16[112,768]{1,0:T(8,128)(2,1)S(1)}, u32[]{:S(2)}, u32[]{:S(2)}) %collective-permute-start.35) | collective-permute-done | bytes 172064 | tf_op jit(solution)/shard_map/ppermute | solution.py:133
  170.0 2.4 %collective-permute-done.41.refs_2_ = bf16[424,384]{1,0:T(8,128)(2,1)S(1)} collective-permute-done((bf16[424,384]{1,0:T(8,128)(2,1)S(1)}, bf16[424,384]{1,0:T(8,128)(2,1)S(1)}, u32[]{:S(2)}, u32[]{:S(2)}) %collective-permute-start.41) | collective-permute-done | bytes 325664 | tf_op jit(solution)/shard_map/ppermute | solution.py:133
  172.9 3.0 %collective-permute-done.43.refs_1_ = bf16[1648,384]{1,0:T(8,128)(2,1)S(1)} collective-permute-done((bf16[1648,384]{1,0:T(8,128)(2,1)S(1)}, bf16[1648,384]{1,0:T(8,128)(2,1)S(1)}, u32[]{:S(2)}, u32[]{:S(2)}) %collective-permute-start.43) | collective-permute-done | bytes 1265696 | tf_op jit(solution)/shard_map/ppermute | solution.py:133
  175.8 2.7 %finish.1 = (f32[576,768]{1,0:T(8,128)}, f32[192,768]{1,0:T(8,128)}, f32[288,768]{1,0:T(8,128)}, f32[576,768]{1,0:T(8,128)}, f32[768]{0:T(1024)}, /*index=5*/f32[768]{0:T(1024)}) custom-call(bf16[1648,384]{1,0:T(8,128)(2,1)S(1)} %collect.1.refs_0_, bf16[1648,384]{1,0:T(8,128)(2,1)S(1)} %collective-permute-done.43.refs_1_), custom_call_target="tpu_custom_call" | custom-call | tf_op jit(solution)/shard_map/finish/pallas_call | solution.py:112
  (103 shorter events, 44.5 us)
Async XLA Ops:
  7.2 44.6 %all-gather.2.cloned.1.call-start = ((), (), s32[]{:S(2)}) async-start(), calls=%async_computation | async-start | bytes 1474560 | tf_op jit(solution)/shard_map/all_gather | solution.py:1134
  9.0 28.7 %collective-permute-start = (bf16[432,768]{1,0:T(8,128)(2,1)S(1)}, bf16[432,768]{1,0:T(8,128)(2,1)S(1)}, u32[]{:S(2)}, u32[]{:S(2)}) collective-permute-start(bf16[432,768]{1,0:T(8,128)(2,1)S(1)} %pick.1), channel_id=1, source_target_pairs={{0,1},{1,0},{2,3},{3,2},{4,5},{5,4},{6,7},{7,6},{8,9},{9,8},{10,11... | collective-permute-start | bytes 1990664 | tf_op jit(solution)/shard_map/ppermute | solution.py:133
  15.9 12.1 %collective-permute-start.4 = (bf16[384,448]{1,0:T(8,128)(2,1)S(1)}, bf16[384,448]{1,0:T(8,128)(2,1)S(1)}, u32[]{:S(2)}, u32[]{:S(2)}) collective-permute-start(bf16[384,448]{1,0:T(8,128)(2,1)S(1)} %get-tuple-element.69.refs_4_.refs_10_), channel_id=1, source_target_pairs={{0,8},{4,12},{8,0},{12,4},{16,24},{20,28},{24,16},{28,20},{1,9},{5... | collective-permute-start | bytes 1032200 | tf_op jit(solution)/shard_map/ppermute | solution.py:133
  17.5 18.7 %collective-permute-start.2 = (bf16[384,448]{1,0:T(8,128)(2,1)S(1)}, bf16[384,448]{1,0:T(8,128)(2,1)S(1)}, u32[]{:S(2)}, u32[]{:S(2)}) collective-permute-start(bf16[384,448]{1,0:T(8,128)(2,1)S(1)} %get-tuple-element.69.refs_4_.refs_10_), channel_id=1, source_target_pairs={{0,16},{4,20},{8,24},{12,28},{16,0},{20,4},{24,8},{28,12},{1,17},{... | collective-permute-start | bytes 1032200 | tf_op jit(solution)/shard_map/ppermute | solution.py:133
  19.0 17.2 %collective-permute-start.3 = (bf16[384,448]{1,0:T(8,128)(2,1)S(1)}, bf16[384,448]{1,0:T(8,128)(2,1)S(1)}, u32[]{:S(2)}, u32[]{:S(2)}) collective-permute-start(bf16[384,448]{1,0:T(8,128)(2,1)S(1)} %get-tuple-element.69.refs_4_.refs_10_), channel_id=1, source_target_pairs={{0,24},{4,28},{8,16},{12,20},{16,8},{20,12},{24,0},{28,4},{1,25},{... | collective-permute-start | bytes 1032200 | tf_op jit(solution)/shard_map/ppermute | solution.py:133
  37.8 14.0 %collective-permute-start.5 = (bf16[432,768]{1,0:T(8,128)(2,1)S(1)}, bf16[432,768]{1,0:T(8,128)(2,1)S(1)}, u32[]{:S(2)}, u32[]{:S(2)}) collective-permute-start(bf16[432,768]{1,0:T(8,128)(2,1)S(1)} %keep.1.refs_5_), channel_id=1, source_target_pairs={{0,4},{4,0},{8,12},{12,8},{16,20},{20,16},{24,28},{28,24},{1,5},{5... | collective-permute-start | bytes 1990664 | tf_op jit(solution)/shard_map/ppermute | solution.py:133
  42.5 11.3 %collective-permute-start.7 = (bf16[192,224]{1,0:T(8,128)(2,1)}, bf16[192,224]{1,0:T(8,128)(2,1)}, u32[]{:S(2)}, u32[]{:S(2)}) collective-permute-start(bf16[192,224]{1,0:T(8,128)(2,1)} %get-tuple-element.78), channel_id=1, source_target_pairs={{0,1},{1,0},{2,3},{3,2},{4,5},{5,4},{6,7},{7,6},{8,9},{9,8},{10,11... | collective-permute-start | bytes 258056 | tf_op jit(solution)/shard_map/ppermute | solution.py:133
  43.2 16.8 %collective-permute-start.8 = (bf16[192,224]{1,0:T(8,128)(2,1)}, bf16[192,224]{1,0:T(8,128)(2,1)}, u32[]{:S(2)}, u32[]{:S(2)}) collective-permute-start(bf16[192,224]{1,0:T(8,128)(2,1)} %get-tuple-element.77.refs_6_), channel_id=1, source_target_pairs={{0,2},{1,3},{2,0},{3,1},{4,6},{5,7},{6,4},{7,5},{8,10},{9,11},{10,... | collective-permute-start | bytes 258056 | tf_op jit(solution)/shard_map/ppermute | solution.py:133
  67.1 21.2 %collective-permute-start.15 = (bf16[224,768]{1,0:T(8,128)(2,1)}, bf16[224,768]{1,0:T(8,128)(2,1)S(1)}, u32[]{:S(2)}, u32[]{:S(2)}) collective-permute-start(bf16[224,768]{1,0:T(8,128)(2,1)} %get-tuple-element.91.refs_3_), channel_id=1, source_target_pairs={{0,1},{1,0},{2,3},{3,2},{4,5},{5,4},{6,7},{7,6},{8,9},{9,8},{10,11... | collective-permute-start | bytes 1032200 | tf_op jit(solution)/shard_map/ppermute | solution.py:133
  69.1 10.8 %collective-permute-start.11 = (bf16[112,768]{1,0:T(8,128)(2,1)}, bf16[112,768]{1,0:T(8,128)(2,1)S(1)}, u32[]{:S(2)}, u32[]{:S(2)}) collective-permute-start(bf16[112,768]{1,0:T(8,128)(2,1)} %get-tuple-element.85), channel_id=1, source_target_pairs={{0,2},{1,3},{2,0},{3,1},{4,6},{5,7},{6,4},{7,5},{8,10},{9,11},{10,... | collective-permute-start | bytes 516104 | tf_op jit(solution)/shard_map/ppermute | solution.py:133
  82.5 10.0 %collective-permute-start.12 = (bf16[112,192]{1,0:T(8,128)(2,1)S(1)}, bf16[112,192]{1,0:T(8,128)(2,1)S(1)}, u32[]{:S(2)}, u32[]{:S(2)}) collective-permute-start(bf16[112,192]{1,0:T(8,128)(2,1)S(1)} %get-tuple-element.87), channel_id=1, source_target_pairs={{0,1},{1,0},{2,3},{3,2},{4,5},{5,4},{6,7},{7,6},{8,9},{9,8},{10,11... | collective-permute-start | bytes 129032 | tf_op jit(solution)/shard_map/ppermute | solution.py:133
  93.4 18.6 %collective-permute-start.10 = (bf16[112,768]{1,0:T(8,128)(2,1)S(1)}, bf16[112,768]{1,0:T(8,128)(2,1)S(1)}, u32[]{:S(2)}, u32[]{:S(2)}) collective-permute-start(bf16[112,768]{1,0:T(8,128)(2,1)S(1)} %copy-done.8), channel_id=1, source_target_pairs={{0,2},{1,3},{2,0},{3,1},{4,6},{5,7},{6,4},{7,5},{8,10},{9,11},{10,... | collective-permute-start | bytes 516104 | tf_op jit(solution)/shard_map/ppermute | solution.py:133
  100.0 15.9 %collective-permute-start.23 = (bf16[384,448]{1,0:T(8,128)(2,1)S(1)}, bf16[384,448]{1,0:T(8,128)(2,1)S(1)}, u32[]{:S(2)}, u32[]{:S(2)}) collective-permute-start(bf16[384,448]{1,0:T(8,128)(2,1)S(1)} %get-tuple-element.104), channel_id=1, source_target_pairs={{0,8},{4,12},{8,0},{12,4},{16,24},{20,28},{24,16},{28,20},{1,9},{5... | collective-permute-start | bytes 1032200 | tf_op jit(solution)/shard_map/ppermute | solution.py:133
  103.4 17.7 %collective-permute-start.24 = (bf16[384,448]{1,0:T(8,128)(2,1)S(1)}, bf16[384,448]{1,0:T(8,128)(2,1)S(1)}, u32[]{:S(2)}, u32[]{:S(2)}) collective-permute-start(bf16[384,448]{1,0:T(8,128)(2,1)S(1)} %get-tuple-element.105), channel_id=1, source_target_pairs={{0,16},{4,20},{8,24},{12,28},{16,0},{20,4},{24,8},{28,12},{1,17},{... | collective-permute-start | bytes 1032200 | tf_op jit(solution)/shard_map/ppermute | solution.py:133
  103.4 17.7 %collective-permute-start.25 = (bf16[384,448]{1,0:T(8,128)(2,1)S(1)}, bf16[384,448]{1,0:T(8,128)(2,1)S(1)}, u32[]{:S(2)}, u32[]{:S(2)}) collective-permute-start(bf16[384,448]{1,0:T(8,128)(2,1)S(1)} %get-tuple-element.106), channel_id=1, source_target_pairs={{0,24},{4,28},{8,16},{12,20},{16,8},{20,12},{24,0},{28,4},{1,25},{... | collective-permute-start | bytes 1032200 | tf_op jit(solution)/shard_map/ppermute | solution.py:133
  104.9 8.9 %collective-permute-start.30 = (bf16[112,768]{1,0:T(8,128)(2,1)S(1)}, bf16[112,768]{1,0:T(8,128)(2,1)S(1)}, u32[]{:S(2)}, u32[]{:S(2)}) collective-permute-start(bf16[112,768]{1,0:T(8,128)(2,1)S(1)} %copy-done.2), channel_id=1, source_target_pairs={{0,2},{1,3},{2,0},{3,1},{4,6},{5,7},{6,4},{7,5},{8,10},{9,11},{10,... | collective-permute-start | bytes 516104 | tf_op jit(solution)/shard_map/ppermute | solution.py:133
  113.9 11.0 %collective-permute-start.29 = (bf16[112,768]{1,0:T(8,128)(2,1)S(1)}, bf16[112,768]{1,0:T(8,128)(2,1)S(1)}, u32[]{:S(2)}, u32[]{:S(2)}) collective-permute-start(bf16[112,768]{1,0:T(8,128)(2,1)S(1)} %copy-done.2), channel_id=1, source_target_pairs={{0,1},{1,0},{2,3},{3,2},{4,5},{5,4},{6,7},{7,6},{8,9},{9,8},{10,11... | collective-permute-start | bytes 516104 | tf_op jit(solution)/shard_map/ppermute | solution.py:133
  114.3 13.0 %collective-permute-start.31 = (bf16[112,768]{1,0:T(8,128)(2,1)S(1)}, bf16[112,768]{1,0:T(8,128)(2,1)S(1)}, u32[]{:S(2)}, u32[]{:S(2)}) collective-permute-start(bf16[112,768]{1,0:T(8,128)(2,1)S(1)} %collective-permute-done.30.refs_5_), channel_id=1, source_target_pairs={{0,1},{1,0},{2,3},{3,2},{4,5},{5,4},{6,7},{7,6},{8,9},{9,8},{10,11... | collective-permute-start | bytes 516104 | tf_op jit(solution)/shard_map/ppermute | solution.py:133
  115.9 11.4 %collective-permute-start.20 = (bf16[112,768]{1,0:T(8,128)(2,1)S(1)}, bf16[112,768]{1,0:T(8,128)(2,1)S(1)}, u32[]{:S(2)}, u32[]{:S(2)}) collective-permute-start(bf16[112,768]{1,0:T(8,128)(2,1)S(1)} %total_of.3.refs_0_.refs_11_), channel_id=1, source_target_pairs={{0,2},{1,3},{2,0},{3,1},{4,6},{5,7},{6,4},{7,5},{8,10},{9,11},{10,... | collective-permute-start | bytes 516104 | tf_op jit(solution)/shard_map/ppermute | solution.py:133
  121.0 10.9 %collective-permute-start.33 = (bf16[864,384]{1,0:T(8,128)(2,1)S(1)}, bf16[864,384]{1,0:T(8,128)(2,1)S(1)}, u32[]{:S(2)}, u32[]{:S(2)}) collective-permute-start(bf16[864,384]{1,0:T(8,128)(2,1)S(1)} %get-tuple-element.115), channel_id=1, source_target_pairs={{0,4},{4,0},{8,12},{12,8},{16,20},{20,16},{24,28},{28,24},{1,5},{5... | collective-permute-start | bytes 1990664 | tf_op jit(solution)/shard_map/ppermute | solution.py:133
  129.6 12.3 %collective-permute-start.27 = (bf16[128,768]{1,0:T(8,128)(2,1)S(1)}, bf16[128,768]{1,0:T(8,128)(2,1)S(1)}, u32[]{:S(2)}, u32[]{:S(2)}) collective-permute-start(bf16[128,768]{1,0:T(8,128)(2,1)S(1)} %get-tuple-element.109), channel_id=1, source_target_pairs={{0,3},{1,2},{2,1},{3,0},{4,7},{5,6},{6,5},{7,4},{8,11},{9,10},{10,... | collective-permute-start | bytes 589832 | tf_op jit(solution)/shard_map/ppermute | solution.py:133
  131.9 17.8 %collective-permute-start.28 = (bf16[128,768]{1,0:T(8,128)(2,1)S(1)}, bf16[128,768]{1,0:T(8,128)(2,1)S(1)}, u32[]{:S(2)}, u32[]{:S(2)}) collective-permute-start(bf16[128,768]{1,0:T(8,128)(2,1)S(1)} %get-tuple-element.110), channel_id=1, source_target_pairs={{0,2},{1,3},{2,0},{3,1},{4,6},{5,7},{6,4},{7,5},{8,10},{9,11},{10,... | collective-permute-start | bytes 589832 | tf_op jit(solution)/shard_map/ppermute | solution.py:133
  132.4 19.5 %collective-permute-start.37 = (bf16[408,384]{1,0:T(8,128)(2,1)S(1)}, bf16[408,384]{1,0:T(8,128)(2,1)S(1)}, u32[]{:S(2)}, u32[]{:S(2)}) collective-permute-start(bf16[408,384]{1,0:T(8,128)(2,1)S(1)} %get-tuple-element.119), channel_id=1, source_target_pairs={{0,8},{4,12},{8,0},{12,4},{16,24},{20,28},{24,16},{28,20},{1,9},{5... | collective-permute-start | bytes 940040 | tf_op jit(solution)/shard_map/ppermute | solution.py:133
  132.6 21.3 %collective-permute-start.38 = (bf16[408,384]{1,0:T(8,128)(2,1)S(1)}, bf16[408,384]{1,0:T(8,128)(2,1)S(1)}, u32[]{:S(2)}, u32[]{:S(2)}) collective-permute-start(bf16[408,384]{1,0:T(8,128)(2,1)S(1)} %get-tuple-element.120), channel_id=1, source_target_pairs={{0,16},{4,20},{8,24},{12,28},{16,0},{20,4},{24,8},{28,12},{1,17},{... | collective-permute-start | bytes 940040 | tf_op jit(solution)/shard_map/ppermute | solution.py:133
  135.7 18.8 %collective-permute-start.39 = (bf16[408,384]{1,0:T(8,128)(2,1)S(1)}, bf16[408,384]{1,0:T(8,128)(2,1)S(1)}, u32[]{:S(2)}, u32[]{:S(2)}) collective-permute-start(bf16[408,384]{1,0:T(8,128)(2,1)S(1)} %get-tuple-element.121), channel_id=1, source_target_pairs={{0,24},{4,28},{8,16},{12,20},{16,8},{20,12},{24,0},{28,4},{1,25},{... | collective-permute-start | bytes 940040 | tf_op jit(solution)/shard_map/ppermute | solution.py:133
  141.9 14.8 %collective-permute-start.19 = (bf16[112,768]{1,0:T(8,128)(2,1)S(1)}, bf16[112,768]{1,0:T(8,128)(2,1)S(1)}, u32[]{:S(2)}, u32[]{:S(2)}) collective-permute-start(bf16[112,768]{1,0:T(8,128)(2,1)S(1)} %total_of.3.refs_0_.refs_11_), channel_id=1, source_target_pairs={{0,1},{1,0},{2,3},{3,2},{4,5},{5,4},{6,7},{7,6},{8,9},{9,8},{10,11... | collective-permute-start | bytes 516104 | tf_op jit(solution)/shard_map/ppermute | solution.py:133
  151.9 9.6 %collective-permute-start.34 = (bf16[112,768]{1,0:T(8,128)(2,1)S(1)}, bf16[112,768]{1,0:T(8,128)(2,1)S(1)}, u32[]{:S(2)}, u32[]{:S(2)}) collective-permute-start(bf16[112,768]{1,0:T(8,128)(2,1)S(1)} %get-tuple-element.117.refs_0_), channel_id=1, source_target_pairs={{0,1},{1,0},{2,3},{3,2},{4,5},{5,4},{6,7},{7,6},{8,9},{9,8},{10,11... | collective-permute-start | bytes 516104 | tf_op jit(solution)/shard_map/ppermute | solution.py:133
  154.0 15.1 %collective-permute-start.35 = (bf16[112,768]{1,0:T(8,128)(2,1)S(1)}, bf16[112,768]{1,0:T(8,128)(2,1)S(1)}, u32[]{:S(2)}, u32[]{:S(2)}) collective-permute-start(bf16[112,768]{1,0:T(8,128)(2,1)S(1)} %get-tuple-element.117.refs_0_), channel_id=1, source_target_pairs={{0,2},{1,3},{2,0},{3,1},{4,6},{5,7},{6,4},{7,5},{8,10},{9,11},{10,... | collective-permute-start | bytes 516104 | tf_op jit(solution)/shard_map/ppermute | solution.py:133
  154.5 14.6 %collective-permute-start.36 = (bf16[112,768]{1,0:T(8,128)(2,1)S(1)}, bf16[112,768]{1,0:T(8,128)(2,1)S(1)}, u32[]{:S(2)}, u32[]{:S(2)}) collective-permute-start(bf16[112,768]{1,0:T(8,128)(2,1)S(1)} %get-tuple-element.117.refs_0_), channel_id=1, source_target_pairs={{0,3},{1,2},{2,1},{3,0},{4,7},{5,6},{6,5},{7,4},{8,11},{9,10},{10,... | collective-permute-start | bytes 516104 | tf_op jit(solution)/shard_map/ppermute | solution.py:133
  156.7 13.3 %collective-permute-start.40 = (bf16[424,384]{1,0:T(8,128)(2,1)S(1)}, bf16[424,384]{1,0:T(8,128)(2,1)S(1)}, u32[]{:S(2)}, u32[]{:S(2)}) collective-permute-start(bf16[424,384]{1,0:T(8,128)(2,1)S(1)} %sum_piece.1.refs_0_), channel_id=1, source_target_pairs={{0,8},{4,12},{8,0},{12,4},{16,24},{20,28},{24,16},{28,20},{1,9},{5... | collective-permute-start | bytes 976904 | tf_op jit(solution)/shard_map/ppermute | solution.py:133
  158.2 14.3 %collective-permute-start.41 = (bf16[424,384]{1,0:T(8,128)(2,1)S(1)}, bf16[424,384]{1,0:T(8,128)(2,1)S(1)}, u32[]{:S(2)}, u32[]{:S(2)}) collective-permute-start(bf16[424,384]{1,0:T(8,128)(2,1)S(1)} %sum_piece.1.refs_0_), channel_id=1, source_target_pairs={{0,16},{4,20},{8,24},{12,28},{16,0},{20,4},{24,8},{28,12},{1,17},{... | collective-permute-start | bytes 976904 | tf_op jit(solution)/shard_map/ppermute | solution.py:133
  161.5 10.9 %collective-permute-start.42 = (bf16[424,384]{1,0:T(8,128)(2,1)S(1)}, bf16[424,384]{1,0:T(8,128)(2,1)S(1)}, u32[]{:S(2)}, u32[]{:S(2)}) collective-permute-start(bf16[424,384]{1,0:T(8,128)(2,1)S(1)} %sum_piece.1.refs_0_), channel_id=1, source_target_pairs={{0,24},{4,28},{8,16},{12,20},{16,8},{20,12},{24,0},{28,4},{1,25},{... | collective-permute-start | bytes 976904 | tf_op jit(solution)/shard_map/ppermute | solution.py:133
  (22 other events, 130.4 us)
Sparse Core Ops, SparseCore 0:
  9.6 36.9 all-gather.1

commit v9 on v8

--- a/solution.py
+++ b/solution.py
@@ -1,4 +1,5 @@
 import functools
+import math
 
 import jax
 import jax.numpy as jnp
@@ -31,6 +32,14 @@
 
 def slot(tp, n_tp):
     return tp % 2 * (n_tp // 2) + tp // 2
+
+
+def hop(n, count):
+    return (count - n) % count
+
+
+def came(count, send):
+    return [send(hop(n, count)) for n in range(1, count)]
 
 
 def mm(a, b, dims):
@@ -461,6 +470,7 @@
         + [pltpu.SemaphoreType.DMA((count + 2,))],
         16 if count < 8 else 40,
         after,
+        flops=0 if last else 0,
     )
 
 
@@ -578,10 +588,12 @@
 
 
 def gated(units, first, gate_up, mixed_grad, mixed_out, gate_out):
+    rows = math.gcd(units, 96)
+
     def wave(i, carry):
-        spot = pl.ds(first + i * 32, 32)
-        at = pl.ds(2 * first + i * 32, 32)
-        late = pl.ds(2 * first + units + i * 32, 32)
+        spot = pl.ds(first + i * rows, rows)
+        at = pl.ds(2 * first + i * rows, rows)
+        late = pl.ds(2 * first + units + i * rows, rows)
         gate = gate_up[at, :]
         up = gate_up[late, :]
         back = mixed_grad[spot, :]
@@ -593,7 +605,7 @@
         gate_out[late, :] = (back * active).astype(BF16)
         return carry
 
-    lax.fori_loop(0, units // 32, wave, 0)
+    lax.fori_loop(0, units // rows, wave, 0)
 
 
 def feed_kernel(n_tp, need, give, x_ref, cot_ref, w_ref, in_ref, down_ref, gain_ref, *refs):
@@ -607,7 +619,7 @@
     width = out_refs[0].shape[0]
     tp = lax.axis_index("tp")
     for k in range(n_tp):
-        at = pl.ds(pl.multiple_of((tp ^ k) * width, width), width)
+        at = pl.ds(pl.multiple_of((tp ^ hop(k, n_tp)) * width, width), width)
         outs[at, :] = out_refs[k][...]
     mixed_grad[...] = mm(down_ref[...], cot_ref[...], NT)
     middle_out[...] = mm(outs[...], w_ref[...], TN)
@@ -722,7 +734,7 @@
     part = refs[0].shape[0]
     tp = lax.axis_index("tp")
     for k in range(n_tp):
-        at = pl.ds(pl.multiple_of(slot(tp ^ k, n_tp) * part, part), part)
+        at = pl.ds(pl.multiple_of(slot(tp ^ hop(k, n_tp), n_tp) * part, part), part)
         held[at, :] = refs[k][...].astype(F32)
     out_ref[...] = held[...].T.astype(BF16)
 
@@ -747,7 +759,7 @@
     part = refs[0].shape[0]
     tp = lax.axis_index("tp")
     for k in range(n_tp):
-        at = pl.ds(pl.multiple_of(slot(tp ^ k, n_tp) * part, part), part)
+        at = pl.ds(pl.multiple_of(slot(tp ^ hop(k, n_tp), n_tp) * part, part), part)
         out_ref[at, :] = refs[k][...]
 
 
@@ -907,7 +919,7 @@
     tp = lax.axis_index("tp")
     core = lax.axis_index("seq") % 2
     for k in range(n_tp):
-        at = pl.ds(pl.multiple_of(slot(tp ^ k, n_tp) * part, part), part)
+        at = pl.ds(pl.multiple_of(slot(tp ^ hop(k, n_tp), n_tp) * part, part), part)
         branch_full[at, :] = branch_refs[k][...]
     for ref, side in ((send_ref, 1 - core), (keep_ref, core)):
         columns = pl.ds(pl.multiple_of(side * half, half), half)
@@ -994,7 +1006,7 @@
     chip = lax.axis_index("seq") // 2
     gains = jnp.zeros((16, out_ref.shape[1]), F32)
     for k in range(count):
-        at = pl.ds(pl.multiple_of((chip ^ k) * piece, piece), piece)
+        at = pl.ds(pl.multiple_of((chip ^ hop(k, count)) * piece, piece), piece)
         whole = refs[k][...].astype(F32)
         held[at, :] = whole[:piece]
         gains = gains + whole[piece:]
@@ -1017,16 +1029,17 @@
     return out
 
 
-def finish_kernel(sizes, own_ref, pair_ref, *refs):
+def finish_kernel(sizes, need, give, own_ref, pair_ref, *refs):
     out_refs, gain_refs = refs[: len(sizes)], refs[len(sizes) :]
     half = own_ref.shape[1]
     core = lax.axis_index("seq") % 2
-    for ref, side in ((own_ref, core), (pair_ref, 1 - core)):
-        columns = pl.ds(pl.multiple_of(side * half, half), half)
-        at = 0
-        for out_ref, size in zip(out_refs, sizes):
+    at = 0
+    for n, (out_ref, size) in enumerate(zip(out_refs, sizes)):
+        for ref, side in ((own_ref, core), (pair_ref, 1 - core)):
+            columns = pl.ds(pl.multiple_of(side * half, half), half)
             out_ref[:, columns] = ref[at : at + size, :].astype(F32)
-            at += size
+        give(n)
+        at += size
     first = own_ref.shape[0] - 16
     gains = own_ref[first:, :].astype(F32) + pair_ref[first:, :].astype(F32)
     for at, ref in zip((0, 2), gain_refs):
@@ -1043,6 +1056,7 @@
         [((size, model), F32, "h") for size in sizes] + [((model,), F32, "h")] * 2,
         (),
         24,
+        lazy=True,
     )
 
 
@@ -1116,15 +1130,15 @@
     over_tp = lambda x, k: swap(x, "tp", k, n_tp)
     over_chips = lambda x, k: swap(x, "seq", 2 * k, n_seq)
     over_cores = lambda x: swap(x, "seq", 1, n_seq)
-    everywhere = lambda xs: [xs[0]] + [over_tp(xs[k], k) for k in range(1, n_tp)]
+    everywhere = lambda xs: [xs[0]] + came(n_tp, lambda k: over_tp(xs[k], k))
 
     def by_steps(part):
         parts = {0: part}
-        hop = n_tp // 2
-        while hop:
-            parts.update({k ^ hop: over_tp(x, hop) for k, x in parts.items()})
-            hop //= 2
-        return [parts[k] for k in range(n_tp)]
+        step = n_tp // 2
+        while step:
+            parts.update({k ^ step: over_tp(x, step) for k, x in parts.items()})
+            step //= 2
+        return [parts[hop(n, n_tp)] for n in range(n_tp)]
 
     docs = (doc_lengths, roster)
 
@@ -1140,7 +1154,7 @@
         split, True, *docs, queries, q_pair, blocks[split:], state
     )
     out_b, totals, out_mine, out_other = join(state_own, over_cores(state_pair))
-    outs = [out_mine] + [over_tp(out_other if k % 2 else out_mine, k) for k in range(1, n_tp)]
+    outs = everywhere([out_other if k % 2 else out_mine for k in range(n_tp)])
     out_pair = over_cores(out_b)
     totals_pair = over_cores(totals)
 
@@ -1189,17 +1203,16 @@
     layer_out = stack_parts(totals_all)
     keep, send = late_grads(proj_grad, h_one, out_b, branches, [(totals_all[n_tp // 2], "v")])
     own, *others = spread(count, (keep, over_cores(send)), (early, over_cores(early_send)))
-    came = everywhere(parts)
-    summed = total_of(came[:2] + came[:1:-1], F32, flops=2_000_000_000)
+    summed = total_of(everywhere(parts), F32, flops=2_000_000_000)
     chip_sum = total_of(
-        [own] + [over_chips(others[k - 1], k) for k in range(1, count)], F32, "v", ()
+        [own] + came(count, lambda k: over_chips(others[k - 1], k)), F32, "v", ()
     )
     input_part, gains = input_side(tokens, gain_one, middle_grad, summed, [(own, "v")])
     inputs_all = everywhere([input_part] * n_tp)
     piece = sum_piece(gains, [chip_sum], ())
     input_grad = stack_parts(inputs_all, (), 3_000_000_000)
     collected = collect(
-        [piece] + [over_chips(piece, k) for k in range(1, count)], [(input_grad, "h"), (layer_out, "h")]
+        [piece] + came(count, lambda k: over_chips(piece, k)), [(input_grad, "h"), (layer_out, "h")]
     )
     grad_qkv, grad_out, grad_down, grad_in, grad_one, grad_two = finish(
         collected, over_cores(collected), (3 * width, width, units, 2 * units)

time: 187 us -> 188 us (level)
  waiting for transfers between devices: 55.3 us -> 65.2 us
  starting transfers between devices: 59.3 us -> 55.5 us
  Pallas kernels: 55.3 us -> 51.9 us
    ppermute x44, waiting for transfers between devices: 54.7 us -> 64.5 us  [swap(): return lax.ppermute(x, axis, [(i, i ^ hop) for i in range(count)])]
    ppermute x44, starting transfers between devices: 59.3 us -> 55.5 us  [swap(): return lax.ppermute(x, axis, [(i, i ^ hop) for i in range(count)])]
    pallas_call x26, Pallas kernels: 55.3 us -> 51.9 us  [call(): pl.pallas_call(run, out_shape=tuple((shaped(shape, dtype) if kind == 'v'...]
  transfers between devices with their start and end apart: 45 -> 45, of which waited for: 20 -> 18; matrix products, arithmetic and copies ran while one was open for 0% -> 0% of each run, Pallas kernels for 24% -> 22%
where the time goes in v9:
time: 188 us
  waiting for transfers between devices  65.2 us (35%)
  starting transfers between devices  55.5 us (30%)
  Pallas kernels  51.9 us (28%)
  between operations  14.5 us (8%)
    ppermute x44, waiting for transfers between devices, swap(): return lax.ppermute(x, axis, [(i, i ^ hop) for i in range(count)])  64.5 us
    ppermute x44, starting transfers between devices, swap(): return lax.ppermute(x, axis, [(i, i ^ hop) for i in range(count)])  55.5 us
    pallas_call x26, Pallas kernels, call(): pl.pallas_call(run, out_shape=tuple((shaped(shape, dtype) if kind == 'v'...  51.9 us
  transfers between devices with their start and end apart: 45, of which 18 were waited for; matrix products, arithmetic and copies ran while one was open for 0% of the time, Pallas kernels for 22%

profile of v9, /device:TPU:0, one launch (start us, length us, event | category | flops | bytes accessed | tf_op | source)
XLA Modules:
  0.0 188.0 jit_solution(7549794926836825558)
XLA Ops:
  9.0 3.1 %collective-permute-start = (bf16[432,768]{1,0:T(8,128)(2,1)S(1)}, bf16[432,768]{1,0:T(8,128)(2,1)S(1)}, u32[]{:S(2)}, u32[]{:S(2)}) collective-permute-start(bf16[432,768]{1,0:T(8,128)(2,1)S(1)} %pick.1), channel_id=1, source_target_pairs={{0,1},{1,0},{2,3},{3,2},{4,5},{5,4},{6,7},{7,6},{8,9},{9,8},{10,11... | collective-permute-start | bytes 1990664 | tf_op jit(solution)/shard_map/ppermute | solution.py:142
  12.1 3.8 %project.1 = (bf16[192,448]{1,0:T(8,128)(2,1)S(1)}, bf16[384,448]{1,0:T(8,128)(2,1)S(1)}, bf16[448,768]{1,0:T(8,128)(2,1)}, f32[32,448]{1,0:T(8,128)}, f32[32,448]{1,0:T(8,128)}) custom-call(s32[4]{0:T(128)} %refs_0_.13, s32[8]{0:T(128)} %refs_1_.16, bf16[448,768]{1,0:T(8,128)(2,1)} %refs_0_.15, bf16[576,768]{1,0:T(8,128)(2,1)} %bitcast.12, f32[768]{0:T(1024)} %refs_1_.17, ...), custom_call_target="tpu_custom_call" | custom-call | tf_op jit(solution)/shard_map/project/pallas_call | solution.py:121
  20.9 7.1 %collective-permute-done.4.refs_5_.refs_10_ = bf16[384,448]{1,0:T(8,128)(2,1)S(1)} collective-permute-done((bf16[384,448]{1,0:T(8,128)(2,1)S(1)}, bf16[384,448]{1,0:T(8,128)(2,1)S(1)}, u32[]{:S(2)}, u32[]{:S(2)}) %collective-permute-start.4) | collective-permute-done | bytes 344096 | tf_op jit(solution)/shard_map/ppermute | solution.py:142
  28.0 4.2 %attention_forward.2.refs_6_ = f32[6,80,448]{2,1,0:T(8,128)S(1)} custom-call(s32[4]{0:T(128)} %refs_0_.13, s32[8]{0:T(128)} %refs_1_.16, bf16[192,448]{1,0:T(8,128)(2,1)S(1)} %get-tuple-element.68.refs_2_, bf16[192,448]{1,0:T(8,128)(2,1)S(1)} %collective-permute-done.1.refs_3_, bf16[384,448]{1,0:T(8,128)(2,1)S(1)} %get-tuple-element.69.refs_4_.refs_10_, ...), custom_call_target="tpu_custom_call" | custom-call | tf_op jit(solution)/shard_map/attention_forward/pallas_call | solution.py:121
  32.3 3.9 %collective-permute-done.2.refs_4_.refs_11_ = bf16[384,448]{1,0:T(8,128)(2,1)S(1)} collective-permute-done((bf16[384,448]{1,0:T(8,128)(2,1)S(1)}, bf16[384,448]{1,0:T(8,128)(2,1)S(1)}, u32[]{:S(2)}, u32[]{:S(2)}) %collective-permute-start.2) | collective-permute-done | bytes 344096 | tf_op jit(solution)/shard_map/ppermute | solution.py:142
  36.2 2.8 %attention_forward.3 = (f32[3,80,448]{2,1,0:T(8,128)S(1)}, f32[3,80,448]{2,1,0:T(8,128)S(1)}) custom-call(s32[4]{0:T(128)} %refs_0_.13, s32[8]{0:T(128)} %refs_1_.16, bf16[192,448]{1,0:T(8,128)(2,1)S(1)} %get-tuple-element.68.refs_2_, bf16[192,448]{1,0:T(8,128)(2,1)S(1)} %collective-permute-done.1.refs_3_, ...), custom_call_target="tpu_custom_call" | custom-call | tf_op jit(solution)/shard_map/attention_forward/pallas_call | solution.py:121
  39.6 2.3 %collective-permute-done.6.refs_1_ = f32[3,80,448]{2,1,0:T(8,128)S(1)} collective-permute-done((f32[3,80,448]{2,1,0:T(8,128)S(1)}, f32[3,80,448]{2,1,0:T(8,128)S(1)}, u32[]{:S(2)}, u32[]{:S(2)}) %collective-permute-start.6) | collective-permute-done | bytes 430112 | tf_op jit(solution)/shard_map/ppermute | solution.py:142
  43.0 8.2 %collective-permute-start.7 = (bf16[192,224]{1,0:T(8,128)(2,1)}, bf16[192,224]{1,0:T(8,128)(2,1)}, u32[]{:S(2)}, u32[]{:S(2)}) collective-permute-start(bf16[192,224]{1,0:T(8,128)(2,1)} %get-tuple-element.78), channel_id=1, source_target_pairs={{0,3},{1,2},{2,1},{3,0},{4,7},{5,6},{6,5},{7,4},{8,11},{9,10},{10,... | collective-permute-start | bytes 258056 | tf_op jit(solution)/shard_map/ppermute | solution.py:142
  55.1 3.7 %collective-permute-done.8.refs_8_ = bf16[192,224]{1,0:T(8,128)(2,1)} collective-permute-done((bf16[192,224]{1,0:T(8,128)(2,1)}, bf16[192,224]{1,0:T(8,128)(2,1)}, u32[]{:S(2)}, u32[]{:S(2)}) %collective-permute-start.8) | collective-permute-done | bytes 86048 | tf_op jit(solution)/shard_map/ppermute | solution.py:142
  58.8 7.1 %feed.1 = (f32[224,768]{1,0:T(8,128)}, f32[112,768]{1,0:T(8,128)}, bf16[224,768]{1,0:T(8,128)(2,1)}, bf16[576,224]{1,0:T(8,128)(2,1)}, bf16[1152,224]{1,0:T(8,12...) custom-call(bf16[224,768]{1,0:T(8,128)(2,1)S(1)} %get-tuple-element.71.refs_0_, ...), custom_call_target="tpu_custom_call" | custom-call | tf_op jit(solution)/shard_map/feed/pallas_call | solution.py:121
  69.3 2.5 %down.1 = (f32[112,768]{1,0:T(8,128)}, bf16[112,768]{1,0:T(8,128)(2,1)}) custom-call(bf16[576,224]{1,0:T(8,128)(2,1)} %get-tuple-element.79.refs_0_, bf16[576,768]{1,0:T(8,128)(2,1)S(1)} %get-tuple-element.75.refs_4_.refs_1_, f32[224,768]{1,0:T(8,128)} %get-tuple-element.80.refs_2_), custom_call_target="tpu_custom_call" | custom-call | tf_op jit(solution)/shard_map/down/pallas_call | solution.py:121
  71.9 6.7 %collective-permute-done.11.refs_5_ = bf16[112,768]{1,0:T(8,128)(2,1)S(1)} collective-permute-done((bf16[112,768]{1,0:T(8,128)(2,1)}, bf16[112,768]{1,0:T(8,128)(2,1)S(1)}, u32[]{:S(2)}, u32[]{:S(2)}) %collective-permute-start.11) | collective-permute-done | bytes 172064 | tf_op jit(solution)/shard_map/ppermute | solution.py:142
  78.6 2.6 %branch.1 = (f32[112,768]{1,0:T(8,128)}, bf16[112,768]{1,0:T(8,128)(2,1)}, bf16[112,192]{1,0:T(8,128)(2,1)S(1)}, bf16[112,192]{1,0:T(8,128)(2,1)S(1)}, bf16[112,...) custom-call(f32[112,768]{1,0:T(8,128)} %get-tuple-element.83.refs_0_, bf16[448,768]{1,0:T(8,128)(2,1)} %refs_2_.5, ...), custom_call_target="tpu_custom_call" | custom-call | tf_op jit(solution)/shard_map/branch/pallas_call | solution.py:121
  82.7 2.4 %collective-permute-start.13 = (bf16[112,192]{1,0:T(8,128)(2,1)S(1)}, bf16[112,192]{1,0:T(8,128)(2,1)S(1)}, u32[]{:S(2)}, u32[]{:S(2)}) collective-permute-start(bf16[112,192]{1,0:T(8,128)(2,1)S(1)} %get-tuple-element.88), channel_id=1, source_target_pairs={{0,2},{1,3},{2,0},{3,1},{4,6},{5,7},{6,4},{7,5},{8,10},{9,11},{10,... | collective-permute-start | bytes 129032 | tf_op jit(solution)/shard_map/ppermute | solution.py:142
  85.7 4.0 %early_grads.1 = (f32[864,384]{1,0:T(8,128)S(1)}, bf16[864,384]{1,0:T(8,128)(2,1)S(1)}) custom-call(bf16[576,224]{1,0:T(8,128)(2,1)} %get-tuple-element.79.refs_0_, bf16[1152,224]{1,0:T(8,128)(2,1)} %get-tuple-element.90.refs_1_, bf16[448,768]{1,0:T(8,128)(2,1)} %refs_2_.5, bf16[224,768]{1,0:T(8,128)(2,1)} %get-tuple-element.91.refs_3_, ...), custom_call_target="tpu_custom_call" | custom-call | tf_op jit(solution)/shard_map/early_grads/pallas_call | solution.py:121
  90.6 2.4 %collective-permute-start.10 = (bf16[112,768]{1,0:T(8,128)(2,1)S(1)}, bf16[112,768]{1,0:T(8,128)(2,1)S(1)}, u32[]{:S(2)}, u32[]{:S(2)}) collective-permute-start(bf16[112,768]{1,0:T(8,128)(2,1)S(1)} %copy-done.8), channel_id=1, source_target_pairs={{0,2},{1,3},{2,0},{3,1},{4,6},{5,7},{6,4},{7,5},{8,10},{9,11},{10,... | collective-permute-start | bytes 516104 | tf_op jit(solution)/shard_map/ppermute | solution.py:142
  93.0 5.5 %attention_backward.2 = (bf16[384,448]{1,0:T(8,128)(2,1)S(1)}, bf16[384,448]{1,0:T(8,128)(2,1)S(1)}, bf16[384,448]{1,0:T(8,128)(2,1)S(1)}, f32[6,64,448]{2,1,0:T(8,128)S(1)}) custom-call(s32[4]{0:T(128)} %refs_0_.13, s32[8]{0:T(128)} %refs_1_.16, bf16[192,448]{1,0:T(8,128)(2,1)S(1)} %get-tuple-element.68.refs_2_, ...), custom_call_target="tpu_custom_call" | custom-call | tf_op jit(solution)/shard_map/attention_backward/pallas_call | solution.py:121
  100.1 3.3 %collective-permute-start.24 = (bf16[384,448]{1,0:T(8,128)(2,1)S(1)}, bf16[384,448]{1,0:T(8,128)(2,1)S(1)}, u32[]{:S(2)}, u32[]{:S(2)}) collective-permute-start(bf16[384,448]{1,0:T(8,128)(2,1)S(1)} %get-tuple-element.105), channel_id=1, source_target_pairs={{0,16},{4,20},{8,24},{12,28},{16,0},{20,4},{24,8},{28,12},{1,17},{... | collective-permute-start | bytes 1032200 | tf_op jit(solution)/shard_map/ppermute | solution.py:142
  104.6 3.4 %attention_backward.3 = (f32[384,448]{1,0:T(8,128)S(1)}, f32[192,448]{1,0:T(8,128)S(1)}, bf16[192,448]{1,0:T(8,128)(2,1)S(1)}) custom-call(s32[4]{0:T(128)} %refs_0_.13, s32[8]{0:T(128)} %refs_1_.16, bf16[192,448]{1,0:T(8,128)(2,1)S(1)} %get-tuple-element.68.refs_2_, bf16[192,448]{1,0:T(8,128)(2,1)S(1)} %collective-permute-done.1.refs_3_, ...), custom_call_target="tpu_custom_call" | custom-call | tf_op jit(solution)/shard_map/attention_backward/pallas_call | solution.py:121
  110.5 4.3 %collective-permute-done.29.refs_5_ = bf16[112,768]{1,0:T(8,128)(2,1)S(1)} collective-permute-done((bf16[112,768]{1,0:T(8,128)(2,1)S(1)}, bf16[112,768]{1,0:T(8,128)(2,1)S(1)}, u32[]{:S(2)}, u32[]{:S(2)}) %collective-permute-start.29) | collective-permute-done | bytes 172064 | tf_op jit(solution)/shard_map/ppermute | solution.py:142
  116.8 4.1 %collective-permute-done.24.refs_9_ = bf16[384,448]{1,0:T(8,128)(2,1)S(1)} collective-permute-done((bf16[384,448]{1,0:T(8,128)(2,1)S(1)}, bf16[384,448]{1,0:T(8,128)(2,1)S(1)}, u32[]{:S(2)}, u32[]{:S(2)}) %collective-permute-start.24) | collective-permute-done | bytes 344096 | tf_op jit(solution)/shard_map/ppermute | solution.py:142
  121.0 2.5 %unproject.1 = (bf16[576,448]{1,0:T(8,128)(2,1)S(1)}, f32[128,768]{1,0:T(8,128)S(1)}, bf16[128,768]{1,0:T(8,128)(2,1)S(1)}, bf16[128,768]{1,0:T(8,128)(2,1)S(1)}, bf16[128,768]{1,0:T(8,128)(2,1)S(1)}) custom-call(bf16[448,768]{1,0:T(8,128)(2,1)S(1)} %copy-done, bf16[576,768]{1,0:T(8,128)(2,1)S(1)} %bitcast.13, f32[32,448]{1,0:T(8,128)S(1)} %copy-done.5, ...), custom_call_target="tpu_custom_call" | custom-call | tf_op jit(solution)/shard_map/unproject/pallas_call | solution.py:121
  123.5 2.2 %collective-permute-done.31.refs_6_ = bf16[112,768]{1,0:T(8,128)(2,1)S(1)} collective-permute-done((bf16[112,768]{1,0:T(8,128)(2,1)S(1)}, bf16[112,768]{1,0:T(8,128)(2,1)S(1)}, u32[]{:S(2)}, u32[]{:S(2)}) %collective-permute-start.31) | collective-permute-done | bytes 172064 | tf_op jit(solution)/shard_map/ppermute | solution.py:142
  125.7 2.9 %collective-permute-done.30.refs_4_ = bf16[112,768]{1,0:T(8,128)(2,1)S(1)} collective-permute-done((bf16[112,768]{1,0:T(8,128)(2,1)S(1)}, bf16[112,768]{1,0:T(8,128)(2,1)S(1)}, u32[]{:S(2)}, u32[]{:S(2)}) %collective-permute-start.30) | collective-permute-done | bytes 172064 | tf_op jit(solution)/shard_map/ppermute | solution.py:142
  131.9 2.3 %collective-permute-start.28 = (bf16[128,768]{1,0:T(8,128)(2,1)S(1)}, bf16[128,768]{1,0:T(8,128)(2,1)S(1)}, u32[]{:S(2)}, u32[]{:S(2)}) collective-permute-start(bf16[128,768]{1,0:T(8,128)(2,1)S(1)} %get-tuple-element.110), channel_id=1, source_target_pairs={{0,1},{1,0},{2,3},{3,2},{4,5},{5,4},{6,7},{7,6},{8,9},{9,8},{10,11... | collective-permute-start | bytes 589832 | tf_op jit(solution)/shard_map/ppermute | solution.py:142
  140.9 8.8 %collective-permute-done.27.refs_2_ = bf16[128,768]{1,0:T(8,128)(2,1)S(1)} collective-permute-done((bf16[128,768]{1,0:T(8,128)(2,1)S(1)}, bf16[128,768]{1,0:T(8,128)(2,1)S(1)}, u32[]{:S(2)}, u32[]{:S(2)}) %collective-permute-start.27) | collective-permute-done | bytes 196640 | tf_op jit(solution)/shard_map/ppermute | solution.py:142
  156.1 2.4 %collective-permute-start.36 = (bf16[112,768]{1,0:T(8,128)(2,1)S(1)}, bf16[112,768]{1,0:T(8,128)(2,1)S(1)}, u32[]{:S(2)}, u32[]{:S(2)}) collective-permute-start(bf16[112,768]{1,0:T(8,128)(2,1)S(1)} %get-tuple-element.117.refs_0_), channel_id=1, source_target_pairs={{0,1},{1,0},{2,3},{3,2},{4,5},{5,4},{6,7},{7,6},{8,9},{9,8},{10,11... | collective-permute-start | bytes 516104 | tf_op jit(solution)/shard_map/ppermute | solution.py:142
  160.1 4.9 %collective-permute-done.20.refs_1_ = bf16[112,768]{1,0:T(8,128)(2,1)S(1)} collective-permute-done((bf16[112,768]{1,0:T(8,128)(2,1)S(1)}, bf16[112,768]{1,0:T(8,128)(2,1)S(1)}, u32[]{:S(2)}, u32[]{:S(2)}) %collective-permute-start.20) | collective-permute-done | bytes 172064 | tf_op jit(solution)/shard_map/ppermute | solution.py:142
  168.2 2.2 %collective-permute-done.35.refs_2_ = bf16[112,768]{1,0:T(8,128)(2,1)S(1)} collective-permute-done((bf16[112,768]{1,0:T(8,128)(2,1)S(1)}, bf16[112,768]{1,0:T(8,128)(2,1)S(1)}, u32[]{:S(2)}, u32[]{:S(2)}) %collective-permute-start.35) | collective-permute-done | bytes 172064 | tf_op jit(solution)/shard_map/ppermute | solution.py:142
  171.4 3.1 %collective-permute-done.41.refs_2_ = bf16[424,384]{1,0:T(8,128)(2,1)S(1)} collective-permute-done((bf16[424,384]{1,0:T(8,128)(2,1)S(1)}, bf16[424,384]{1,0:T(8,128)(2,1)S(1)}, u32[]{:S(2)}, u32[]{:S(2)}) %collective-permute-start.41) | collective-permute-done | bytes 325664 | tf_op jit(solution)/shard_map/ppermute | solution.py:142
  175.5 3.0 %collective-permute-done.43.refs_1_ = bf16[1648,384]{1,0:T(8,128)(2,1)S(1)} collective-permute-done((bf16[1648,384]{1,0:T(8,128)(2,1)S(1)}, bf16[1648,384]{1,0:T(8,128)(2,1)S(1)}, u32[]{:S(2)}, u32[]{:S(2)}) %collective-permute-start.43) | collective-permute-done | bytes 1265696 | tf_op jit(solution)/shard_map/ppermute | solution.py:142
  178.4 2.7 %finish.1 = (f32[576,768]{1,0:T(8,128)}, f32[192,768]{1,0:T(8,128)}, f32[288,768]{1,0:T(8,128)}, f32[576,768]{1,0:T(8,128)}, f32[768]{0:T(1024)}, /*index=5*/f32[768]{0:T(1024)}) custom-call(bf16[1648,384]{1,0:T(8,128)(2,1)S(1)} %collect.1.refs_0_, bf16[1648,384]{1,0:T(8,128)(2,1)S(1)} %collective-permute-done.43.refs_1_), custom_call_target="tpu_custom_call" | custom-call | tf_op jit(solution)/shard_map/finish/pallas_call | solution.py:121
  (103 shorter events, 48.9 us)
Async XLA Ops:
  7.2 44.7 %all-gather.2.cloned.1.call-start = ((), (), s32[]{:S(2)}) async-start(), calls=%async_computation | async-start | bytes 1474560 | tf_op jit(solution)/shard_map/all_gather | solution.py:1148
  9.0 30.0 %collective-permute-start = (bf16[432,768]{1,0:T(8,128)(2,1)S(1)}, bf16[432,768]{1,0:T(8,128)(2,1)S(1)}, u32[]{:S(2)}, u32[]{:S(2)}) collective-permute-start(bf16[432,768]{1,0:T(8,128)(2,1)S(1)} %pick.1), channel_id=1, source_target_pairs={{0,1},{1,0},{2,3},{3,2},{4,5},{5,4},{6,7},{7,6},{8,9},{9,8},{10,11... | collective-permute-start | bytes 1990664 | tf_op jit(solution)/shard_map/ppermute | solution.py:142
  15.9 12.1 %collective-permute-start.4 = (bf16[384,448]{1,0:T(8,128)(2,1)S(1)}, bf16[384,448]{1,0:T(8,128)(2,1)S(1)}, u32[]{:S(2)}, u32[]{:S(2)}) collective-permute-start(bf16[384,448]{1,0:T(8,128)(2,1)S(1)} %get-tuple-element.69.refs_4_.refs_10_), channel_id=1, source_target_pairs={{0,8},{4,12},{8,0},{12,4},{16,24},{20,28},{24,16},{28,20},{1,9},{5... | collective-permute-start | bytes 1032200 | tf_op jit(solution)/shard_map/ppermute | solution.py:142
  17.5 18.7 %collective-permute-start.2 = (bf16[384,448]{1,0:T(8,128)(2,1)S(1)}, bf16[384,448]{1,0:T(8,128)(2,1)S(1)}, u32[]{:S(2)}, u32[]{:S(2)}) collective-permute-start(bf16[384,448]{1,0:T(8,128)(2,1)S(1)} %get-tuple-element.69.refs_4_.refs_10_), channel_id=1, source_target_pairs={{0,16},{4,20},{8,24},{12,28},{16,0},{20,4},{24,8},{28,12},{1,17},{... | collective-permute-start | bytes 1032200 | tf_op jit(solution)/shard_map/ppermute | solution.py:142
  19.0 17.2 %collective-permute-start.3 = (bf16[384,448]{1,0:T(8,128)(2,1)S(1)}, bf16[384,448]{1,0:T(8,128)(2,1)S(1)}, u32[]{:S(2)}, u32[]{:S(2)}) collective-permute-start(bf16[384,448]{1,0:T(8,128)(2,1)S(1)} %get-tuple-element.69.refs_4_.refs_10_), channel_id=1, source_target_pairs={{0,24},{4,28},{8,16},{12,20},{16,8},{20,12},{24,0},{28,4},{1,25},{... | collective-permute-start | bytes 1032200 | tf_op jit(solution)/shard_map/ppermute | solution.py:142
  39.1 12.8 %collective-permute-start.5 = (bf16[432,768]{1,0:T(8,128)(2,1)S(1)}, bf16[432,768]{1,0:T(8,128)(2,1)S(1)}, u32[]{:S(2)}, u32[]{:S(2)}) collective-permute-start(bf16[432,768]{1,0:T(8,128)(2,1)S(1)} %keep.1.refs_5_), channel_id=1, source_target_pairs={{0,4},{4,0},{8,12},{12,8},{16,20},{20,16},{24,28},{28,24},{1,5},{5... | collective-permute-start | bytes 1990664 | tf_op jit(solution)/shard_map/ppermute | solution.py:142
  43.0 12.1 %collective-permute-start.7 = (bf16[192,224]{1,0:T(8,128)(2,1)}, bf16[192,224]{1,0:T(8,128)(2,1)}, u32[]{:S(2)}, u32[]{:S(2)}) collective-permute-start(bf16[192,224]{1,0:T(8,128)(2,1)} %get-tuple-element.78), channel_id=1, source_target_pairs={{0,3},{1,2},{2,1},{3,0},{4,7},{5,6},{6,5},{7,4},{8,11},{9,10},{10,... | collective-permute-start | bytes 258056 | tf_op jit(solution)/shard_map/ppermute | solution.py:142
  66.0 19.7 %collective-permute-start.15 = (bf16[224,768]{1,0:T(8,128)(2,1)}, bf16[224,768]{1,0:T(8,128)(2,1)S(1)}, u32[]{:S(2)}, u32[]{:S(2)}) collective-permute-start(bf16[224,768]{1,0:T(8,128)(2,1)} %get-tuple-element.91.refs_3_), channel_id=1, source_target_pairs={{0,1},{1,0},{2,3},{3,2},{4,5},{5,4},{6,7},{7,6},{8,9},{9,8},{10,11... | collective-permute-start | bytes 1032200 | tf_op jit(solution)/shard_map/ppermute | solution.py:142
  67.8 10.8 %collective-permute-start.11 = (bf16[112,768]{1,0:T(8,128)(2,1)}, bf16[112,768]{1,0:T(8,128)(2,1)S(1)}, u32[]{:S(2)}, u32[]{:S(2)}) collective-permute-start(bf16[112,768]{1,0:T(8,128)(2,1)} %get-tuple-element.85), channel_id=1, source_target_pairs={{0,2},{1,3},{2,0},{3,1},{4,6},{5,7},{6,4},{7,5},{8,10},{9,11},{10,... | collective-permute-start | bytes 516104 | tf_op jit(solution)/shard_map/ppermute | solution.py:142
  81.2 8.5 %collective-permute-start.12 = (bf16[112,192]{1,0:T(8,128)(2,1)S(1)}, bf16[112,192]{1,0:T(8,128)(2,1)S(1)}, u32[]{:S(2)}, u32[]{:S(2)}) collective-permute-start(bf16[112,192]{1,0:T(8,128)(2,1)S(1)} %get-tuple-element.87), channel_id=1, source_target_pairs={{0,3},{1,2},{2,1},{3,0},{4,7},{5,6},{6,5},{7,4},{8,11},{9,10},{10,... | collective-permute-start | bytes 129032 | tf_op jit(solution)/shard_map/ppermute | solution.py:142
  90.6 17.4 %collective-permute-start.10 = (bf16[112,768]{1,0:T(8,128)(2,1)S(1)}, bf16[112,768]{1,0:T(8,128)(2,1)S(1)}, u32[]{:S(2)}, u32[]{:S(2)}) collective-permute-start(bf16[112,768]{1,0:T(8,128)(2,1)S(1)} %copy-done.8), channel_id=1, source_target_pairs={{0,2},{1,3},{2,0},{3,1},{4,6},{5,7},{6,4},{7,5},{8,10},{9,11},{10,... | collective-permute-start | bytes 516104 | tf_op jit(solution)/shard_map/ppermute | solution.py:142
  98.5 18.3 %collective-permute-start.23 = (bf16[384,448]{1,0:T(8,128)(2,1)S(1)}, bf16[384,448]{1,0:T(8,128)(2,1)S(1)}, u32[]{:S(2)}, u32[]{:S(2)}) collective-permute-start(bf16[384,448]{1,0:T(8,128)(2,1)S(1)} %get-tuple-element.104), channel_id=1, source_target_pairs={{0,8},{4,12},{8,0},{12,4},{16,24},{20,28},{24,16},{28,20},{1,9},{5... | collective-permute-start | bytes 1032200 | tf_op jit(solution)/shard_map/ppermute | solution.py:142
  100.1 20.9 %collective-permute-start.24 = (bf16[384,448]{1,0:T(8,128)(2,1)S(1)}, bf16[384,448]{1,0:T(8,128)(2,1)S(1)}, u32[]{:S(2)}, u32[]{:S(2)}) collective-permute-start(bf16[384,448]{1,0:T(8,128)(2,1)S(1)} %get-tuple-element.105), channel_id=1, source_target_pairs={{0,16},{4,20},{8,24},{12,28},{16,0},{20,4},{24,8},{28,12},{1,17},{... | collective-permute-start | bytes 1032200 | tf_op jit(solution)/shard_map/ppermute | solution.py:142
  103.4 17.5 %collective-permute-start.25 = (bf16[384,448]{1,0:T(8,128)(2,1)S(1)}, bf16[384,448]{1,0:T(8,128)(2,1)S(1)}, u32[]{:S(2)}, u32[]{:S(2)}) collective-permute-start(bf16[384,448]{1,0:T(8,128)(2,1)S(1)} %get-tuple-element.106), channel_id=1, source_target_pairs={{0,24},{4,28},{8,16},{12,20},{16,8},{20,12},{24,0},{28,4},{1,25},{... | collective-permute-start | bytes 1032200 | tf_op jit(solution)/shard_map/ppermute | solution.py:142
  103.4 11.4 %collective-permute-start.29 = (bf16[112,768]{1,0:T(8,128)(2,1)S(1)}, bf16[112,768]{1,0:T(8,128)(2,1)S(1)}, u32[]{:S(2)}, u32[]{:S(2)}) collective-permute-start(bf16[112,768]{1,0:T(8,128)(2,1)S(1)} %copy-done.2), channel_id=1, source_target_pairs={{0,2},{1,3},{2,0},{3,1},{4,6},{5,7},{6,4},{7,5},{8,10},{9,11},{10,... | collective-permute-start | bytes 516104 | tf_op jit(solution)/shard_map/ppermute | solution.py:142
  114.8 10.9 %collective-permute-start.31 = (bf16[112,768]{1,0:T(8,128)(2,1)S(1)}, bf16[112,768]{1,0:T(8,128)(2,1)S(1)}, u32[]{:S(2)}, u32[]{:S(2)}) collective-permute-start(bf16[112,768]{1,0:T(8,128)(2,1)S(1)} %copy-done.2), channel_id=1, source_target_pairs={{0,1},{1,0},{2,3},{3,2},{4,5},{5,4},{6,7},{7,6},{8,9},{9,8},{10,11... | collective-permute-start | bytes 516104 | tf_op jit(solution)/shard_map/ppermute | solution.py:142
  114.8 13.8 %collective-permute-start.30 = (bf16[112,768]{1,0:T(8,128)(2,1)S(1)}, bf16[112,768]{1,0:T(8,128)(2,1)S(1)}, u32[]{:S(2)}, u32[]{:S(2)}) collective-permute-start(bf16[112,768]{1,0:T(8,128)(2,1)S(1)} %collective-permute-done.29.refs_5_), channel_id=1, source_target_pairs={{0,1},{1,0},{2,3},{3,2},{4,5},{5,4},{6,7},{7,6},{8,9},{9,8},{10,11... | collective-permute-start | bytes 516104 | tf_op jit(solution)/shard_map/ppermute | solution.py:142
  116.8 11.8 %collective-permute-start.19 = (bf16[112,768]{1,0:T(8,128)(2,1)S(1)}, bf16[112,768]{1,0:T(8,128)(2,1)S(1)}, u32[]{:S(2)}, u32[]{:S(2)}) collective-permute-start(bf16[112,768]{1,0:T(8,128)(2,1)S(1)} %total_of.3.refs_0_.refs_11_), channel_id=1, source_target_pairs={{0,2},{1,3},{2,0},{3,1},{4,6},{5,7},{6,4},{7,5},{8,10},{9,11},{10,... | collective-permute-start | bytes 516104 | tf_op jit(solution)/shard_map/ppermute | solution.py:142
  121.0 13.2 %collective-permute-start.33 = (bf16[864,384]{1,0:T(8,128)(2,1)S(1)}, bf16[864,384]{1,0:T(8,128)(2,1)S(1)}, u32[]{:S(2)}, u32[]{:S(2)}) collective-permute-start(bf16[864,384]{1,0:T(8,128)(2,1)S(1)} %get-tuple-element.115), channel_id=1, source_target_pairs={{0,4},{4,0},{8,12},{12,8},{16,20},{20,16},{24,28},{28,24},{1,5},{5... | collective-permute-start | bytes 1990664 | tf_op jit(solution)/shard_map/ppermute | solution.py:142
  129.7 9.7 %collective-permute-start.26 = (bf16[128,768]{1,0:T(8,128)(2,1)S(1)}, bf16[128,768]{1,0:T(8,128)(2,1)S(1)}, u32[]{:S(2)}, u32[]{:S(2)}) collective-permute-start(bf16[128,768]{1,0:T(8,128)(2,1)S(1)} %get-tuple-element.108), channel_id=1, source_target_pairs={{0,3},{1,2},{2,1},{3,0},{4,7},{5,6},{6,5},{7,4},{8,11},{9,10},{10,... | collective-permute-start | bytes 589832 | tf_op jit(solution)/shard_map/ppermute | solution.py:142
  131.6 18.1 %collective-permute-start.27 = (bf16[128,768]{1,0:T(8,128)(2,1)S(1)}, bf16[128,768]{1,0:T(8,128)(2,1)S(1)}, u32[]{:S(2)}, u32[]{:S(2)}) collective-permute-start(bf16[128,768]{1,0:T(8,128)(2,1)S(1)} %get-tuple-element.109), channel_id=1, source_target_pairs={{0,2},{1,3},{2,0},{3,1},{4,6},{5,7},{6,4},{7,5},{8,10},{9,11},{10,... | collective-permute-start | bytes 589832 | tf_op jit(solution)/shard_map/ppermute | solution.py:142
  131.9 17.9 %collective-permute-start.28 = (bf16[128,768]{1,0:T(8,128)(2,1)S(1)}, bf16[128,768]{1,0:T(8,128)(2,1)S(1)}, u32[]{:S(2)}, u32[]{:S(2)}) collective-permute-start(bf16[128,768]{1,0:T(8,128)(2,1)S(1)} %get-tuple-element.110), channel_id=1, source_target_pairs={{0,1},{1,0},{2,3},{3,2},{4,5},{5,4},{6,7},{7,6},{8,9},{9,8},{10,11... | collective-permute-start | bytes 589832 | tf_op jit(solution)/shard_map/ppermute | solution.py:142
  134.6 19.4 %collective-permute-start.37 = (bf16[408,384]{1,0:T(8,128)(2,1)S(1)}, bf16[408,384]{1,0:T(8,128)(2,1)S(1)}, u32[]{:S(2)}, u32[]{:S(2)}) collective-permute-start(bf16[408,384]{1,0:T(8,128)(2,1)S(1)} %get-tuple-element.119), channel_id=1, source_target_pairs={{0,24},{4,28},{8,16},{12,20},{16,8},{20,12},{24,0},{28,4},{1,25},{... | collective-permute-start | bytes 940040 | tf_op jit(solution)/shard_map/ppermute | solution.py:142
  136.7 19.5 %collective-permute-start.38 = (bf16[408,384]{1,0:T(8,128)(2,1)S(1)}, bf16[408,384]{1,0:T(8,128)(2,1)S(1)}, u32[]{:S(2)}, u32[]{:S(2)}) collective-permute-start(bf16[408,384]{1,0:T(8,128)(2,1)S(1)} %get-tuple-element.120), channel_id=1, source_target_pairs={{0,16},{4,20},{8,24},{12,28},{16,0},{20,4},{24,8},{28,12},{1,17},{... | collective-permute-start | bytes 940040 | tf_op jit(solution)/shard_map/ppermute | solution.py:142
  139.4 16.7 %collective-permute-start.39 = (bf16[408,384]{1,0:T(8,128)(2,1)S(1)}, bf16[408,384]{1,0:T(8,128)(2,1)S(1)}, u32[]{:S(2)}, u32[]{:S(2)}) collective-permute-start(bf16[408,384]{1,0:T(8,128)(2,1)S(1)} %get-tuple-element.121), channel_id=1, source_target_pairs={{0,8},{4,12},{8,0},{12,4},{16,24},{20,28},{24,16},{28,20},{1,9},{5... | collective-permute-start | bytes 940040 | tf_op jit(solution)/shard_map/ppermute | solution.py:142
  149.7 9.0 %collective-permute-start.21 = (bf16[112,768]{1,0:T(8,128)(2,1)S(1)}, bf16[112,768]{1,0:T(8,128)(2,1)S(1)}, u32[]{:S(2)}, u32[]{:S(2)}) collective-permute-start(bf16[112,768]{1,0:T(8,128)(2,1)S(1)} %total_of.3.refs_0_.refs_11_), channel_id=1, source_target_pairs={{0,1},{1,0},{2,3},{3,2},{4,5},{5,4},{6,7},{7,6},{8,9},{9,8},{10,11... | collective-permute-start | bytes 516104 | tf_op jit(solution)/shard_map/ppermute | solution.py:142
  149.7 15.3 %collective-permute-start.20 = (bf16[112,768]{1,0:T(8,128)(2,1)S(1)}, bf16[112,768]{1,0:T(8,128)(2,1)S(1)}, u32[]{:S(2)}, u32[]{:S(2)}) collective-permute-start(bf16[112,768]{1,0:T(8,128)(2,1)S(1)} %collective-permute-done.19.refs_2_.refs_7_), channel_id=1, source_target_pairs={{0,1},{1,0},{2,3},{3,2},{4,5},{5,4},{6,7},{7,6},{8,9},{9,8},{10,11... | collective-permute-start | bytes 516104 | tf_op jit(solution)/shard_map/ppermute | solution.py:142
  154.0 13.0 %collective-permute-start.34 = (bf16[112,768]{1,0:T(8,128)(2,1)S(1)}, bf16[112,768]{1,0:T(8,128)(2,1)S(1)}, u32[]{:S(2)}, u32[]{:S(2)}) collective-permute-start(bf16[112,768]{1,0:T(8,128)(2,1)S(1)} %get-tuple-element.117.refs_0_), channel_id=1, source_target_pairs={{0,3},{1,2},{2,1},{3,0},{4,7},{5,6},{6,5},{7,4},{8,11},{9,10},{10,... | collective-permute-start | bytes 516104 | tf_op jit(solution)/shard_map/ppermute | solution.py:142
  156.1 14.3 %collective-permute-start.35 = (bf16[112,768]{1,0:T(8,128)(2,1)S(1)}, bf16[112,768]{1,0:T(8,128)(2,1)S(1)}, u32[]{:S(2)}, u32[]{:S(2)}) collective-permute-start(bf16[112,768]{1,0:T(8,128)(2,1)S(1)} %get-tuple-element.117.refs_0_), channel_id=1, source_target_pairs={{0,2},{1,3},{2,0},{3,1},{4,6},{5,7},{6,4},{7,5},{8,10},{9,11},{10,... | collective-permute-start | bytes 516104 | tf_op jit(solution)/shard_map/ppermute | solution.py:142
  156.1 14.3 %collective-permute-start.36 = (bf16[112,768]{1,0:T(8,128)(2,1)S(1)}, bf16[112,768]{1,0:T(8,128)(2,1)S(1)}, u32[]{:S(2)}, u32[]{:S(2)}) collective-permute-start(bf16[112,768]{1,0:T(8,128)(2,1)S(1)} %get-tuple-element.117.refs_0_), channel_id=1, source_target_pairs={{0,1},{1,0},{2,3},{3,2},{4,5},{5,4},{6,7},{7,6},{8,9},{9,8},{10,11... | collective-permute-start | bytes 516104 | tf_op jit(solution)/shard_map/ppermute | solution.py:142
  158.7 12.6 %collective-permute-start.40 = (bf16[424,384]{1,0:T(8,128)(2,1)S(1)}, bf16[424,384]{1,0:T(8,128)(2,1)S(1)}, u32[]{:S(2)}, u32[]{:S(2)}) collective-permute-start(bf16[424,384]{1,0:T(8,128)(2,1)S(1)} %sum_piece.1.refs_0_), channel_id=1, source_target_pairs={{0,24},{4,28},{8,16},{12,20},{16,8},{20,12},{24,0},{28,4},{1,25},{... | collective-permute-start | bytes 976904 | tf_op jit(solution)/shard_map/ppermute | solution.py:142
  165.0 9.5 %collective-permute-start.41 = (bf16[424,384]{1,0:T(8,128)(2,1)S(1)}, bf16[424,384]{1,0:T(8,128)(2,1)S(1)}, u32[]{:S(2)}, u32[]{:S(2)}) collective-permute-start(bf16[424,384]{1,0:T(8,128)(2,1)S(1)} %sum_piece.1.refs_0_), channel_id=1, source_target_pairs={{0,16},{4,20},{8,24},{12,28},{16,0},{20,4},{24,8},{28,12},{1,17},{... | collective-permute-start | bytes 976904 | tf_op jit(solution)/shard_map/ppermute | solution.py:142
  (22 other events, 158.0 us)
Sparse Core Ops, SparseCore 0:
  9.6 36.7 all-gather.1

commit v10 on v9

--- a/solution.py
+++ b/solution.py
@@ -512,54 +512,80 @@
     )
 
 
-def pick_kernel(in_any, down_any, out_ref, sems):
+def pick_kernel(in_any, down_any, w_any, all_ref, w_ref, sems):
     core = lax.axis_index("seq") % 2
     at = 0
     copies = []
-    for n, source in enumerate((in_any, down_any)):
+    for source in (in_any, down_any, w_any):
         rows = source.shape[0] // 2
         mine = pl.ds(pl.multiple_of(core * rows, rows), rows)
-        copies.append(
-            pltpu.make_async_copy(source.at[mine], out_ref.at[pl.ds(at, rows)], sems.at[n])
-        )
+        copies.append((source.at[mine], all_ref.at[pl.ds(at, rows)]))
         at += rows
+    copies.append((w_any.at[mine], w_ref))
+    copies = [pltpu.make_async_copy(*move, sems.at[n]) for n, move in enumerate(copies)]
     for copy in copies:
         copy.start()
     for copy in copies:
         copy.wait()
 
 
-def pick(in_t, w_down):
-    (out,) = call(
+def pick(in_t, w_down, w_out):
+    rows = (in_t.shape[0] + w_down.shape[0] + w_out.shape[0]) // 2
+    model = w_out.shape[1]
+    return call(
         "pick",
         pick_kernel,
-        kinds((in_t, w_down), "raw"),
-        [(((in_t.shape[0] + w_down.shape[0]) // 2, in_t.shape[1]), BF16, "v")],
-        [pltpu.SemaphoreType.DMA((2,))],
+        kinds((in_t, w_down, w_out), "raw"),
+        [((rows, model), BF16, "v"), ((w_out.shape[0] // 2, model), BF16, "v")],
+        [pltpu.SemaphoreType.DMA((4,))],
+    )
+
+
+def pile_kernel(*refs):
+    out_ref = refs[-1]
+    at = 0
+    for ref in refs[:-1]:
+        out_ref[at : at + ref.shape[0], :] = ref[...]
+        at += ref.shape[0]
+
+
+def pile(values, after):
+    rows = sum(value.shape[0] for value in values)
+    (out,) = call(
+        "pile",
+        pile_kernel,
+        kinds(values, "v"),
+        [((rows, values[0].shape[1]), BF16, "v")],
+        (),
+        16,
+        after,
     )
     return out
 
 
-def keep_kernel(in_ref, out_ref):
-    out_ref[...] = in_ref[...]
-
-
-def keep_until(value, after):
-    (out,) = call("keep", keep_kernel, [(value, "v")], [(value.shape, value.dtype, "v")], (), 16, after)
-    return out
-
-
-def stage_kernel(x_any, cot_any, w_any, in_any, down_any, got_ref, rest_ref, *refs):
+def stage_kernel(x_any, cot_any, in_any, down_any, w_any, got_ref, rest_ref, *refs):
     x_ref, cot_ref, w_ref, in_ref, down_ref, sems = refs
     half = x_ref.shape[0]
     core = lax.axis_index("seq") % 2
-    mine = pl.ds(pl.multiple_of(lax.axis_index("tp") % 2 * half, half), half)
-    moves = [(w_any, w_ref), (x_any.at[mine], x_ref), (cot_any.at[mine], cot_ref)]
+    tp = lax.axis_index("tp")
+    n_tp = w_ref.shape[0] // w_any.shape[0]
+    mine = pl.ds(pl.multiple_of(tp % 2 * half, half), half)
+    width = w_any.shape[0]
+    rows = width // 2
+    own = pl.ds(pl.multiple_of(tp * width, width), width)
+    moves = [(w_any, w_ref.at[own]), (x_any.at[mine], x_ref), (cot_any.at[mine], cot_ref)]
+    sides = ((got_ref, core), (rest_ref, 1 - core))
+    first = got_ref.shape[0] - (n_tp - 1) * rows
+    for k in range(1, n_tp):
+        for source, side in sides:
+            spot = pl.multiple_of((tp ^ k) * width + side * rows, rows)
+            piece = source.at[pl.ds(first + (k - 1) * rows, rows)]
+            moves.append((piece, w_ref.at[pl.ds(spot, rows)]))
     at = 0
     for own, ref in ((in_any, in_ref), (down_any, down_ref)):
         rows = own.shape[0] // 2
         moves.append((own, ref.at[pl.ds(0, 2 * rows)]))
-        for source, side in ((got_ref, core), (rest_ref, 1 - core)):
+        for source, side in sides:
             spot = pl.multiple_of(2 * rows + side * rows, rows)
             moves.append((source.at[pl.ds(at, rows)], ref.at[pl.ds(spot, rows)]))
         at += rows
@@ -570,20 +596,20 @@
         copy.wait()
 
 
-def stage(tokens, cotangent, w_full, in_t, w_down, got, rest):
+def stage(n_tp, tokens, cotangent, in_t, w_down, w_out, got, rest):
     rows, model = tokens.shape
     return call(
         "stage",
         stage_kernel,
-        kinds((tokens, cotangent, w_full, in_t, w_down), "raw") + kinds((got, rest), "v"),
+        kinds((tokens, cotangent, in_t, w_down, w_out), "raw") + kinds((got, rest), "v"),
         [
             ((rows // 2, model), BF16, "v"),
             ((rows // 2, model), BF16, "v"),
-            (w_full.shape, BF16, "v"),
+            ((n_tp * w_out.shape[0], model), BF16, "v"),
             ((2 * in_t.shape[0], model), BF16, "v"),
             ((2 * w_down.shape[0], model), BF16, "v"),
         ],
-        [pltpu.SemaphoreType.DMA((9,))],
+        [pltpu.SemaphoreType.DMA((7 + 2 * n_tp,))],
     )
 
 
@@ -1145,21 +1171,21 @@
     queries, kv, h_one, cos_table, sin_table = project(*docs, tokens, gain_one, qkv_t)
     blocks = [kv] + [over_chips(kv, j) for j in range(1, count)]
     q_pair = over_cores(queries)
-    w_full = lax.all_gather(w_out, "tp", axis=0, tiled=True)
-    got = over_tp(pick(in_t, w_down), 1)
+    picked, w_half = pick(in_t, w_down, w_out)
+    got = [over_tp(picked, 1)] + [over_tp(w_half, k) for k in range(2, n_tp)]
 
     split = (count + 1) // 2
     (state,) = attention_forward(0, False, *docs, queries, q_pair, blocks[:split])
     state_own, state_pair = attention_forward(
-        split, True, *docs, queries, q_pair, blocks[split:], state
+        split, True, *docs, queries, q_pair, blocks[split:], state, kinds(got[1:], "v")
     )
     out_b, totals, out_mine, out_other = join(state_own, over_cores(state_pair))
     outs = everywhere([out_other if k % 2 else out_mine for k in range(n_tp)])
     out_pair = over_cores(out_b)
     totals_pair = over_cores(totals)
 
-    got = keep_until(got, [(state_pair, "v")])
-    staged = stage(tokens, cotangent, w_full, in_t, w_down, got, over_cores(got))
+    got = pile(got, [(state_pair, "v")])
+    staged = stage(n_tp, tokens, cotangent, in_t, w_down, w_out, got, over_cores(got))
     middle, middle_part, h_two, mixed, gate_grad, gain_two_part, own, *others = feed(
         gain_two, staged, outs
     )

time: 188 us -> 174 us (0.926)
  between operations: 14.5 us -> 1.26 us
  Pallas kernels: 51.9 us -> 58.1 us
  starting transfers between devices: 55.5 us -> 49.3 us
    pallas_call x26, Pallas kernels: 51.9 us -> 58.1 us  [call(): pl.pallas_call(run, out_shape=tuple((shaped(shape, dtype) if kind == 'v'...]
    ppermute x44 -> x46, starting transfers between devices: 55.5 us -> 49.3 us  [swap(): return lax.ppermute(x, axis, [(i, i ^ hop) for i in range(count)])]
    ppermute x44 -> x46, waiting for transfers between devices: 64.5 us -> 64.3 us  [swap(): return lax.ppermute(x, axis, [(i, i ^ hop) for i in range(count)])]
  transfers between devices with their start and end apart: 45 -> 46, of which waited for: 18 -> 17; matrix products, arithmetic and copies ran while one was open for 0% -> 0% of each run, Pallas kernels for 22% -> 27%
where the time goes in v10:
time: 174 us
  waiting for transfers between devices  64.3 us (37%)
  Pallas kernels  58.1 us (33%)
  starting transfers between devices  49.3 us (28%)
    ppermute x46, waiting for transfers between devices, swap(): return lax.ppermute(x, axis, [(i, i ^ hop) for i in range(count)])  64.3 us
    pallas_call x26, Pallas kernels, call(): pl.pallas_call(run, out_shape=tuple((shaped(shape, dtype) if kind == 'v'...  58.1 us
    ppermute x46, starting transfers between devices, swap(): return lax.ppermute(x, axis, [(i, i ^ hop) for i in range(count)])  49.3 us
  transfers between devices with their start and end apart: 46, of which 17 were waited for; matrix products, arithmetic and copies ran while one was open for 0% of the time, Pallas kernels for 27%

profile of v10, /device:TPU:0, one launch (start us, length us, event | category | flops | bytes accessed | tf_op | source)
XLA Modules:
  0.0 173.8 jit_solution(15015415703864888597)
XLA Ops:
  1.9 3.1 %collective-permute-start = (bf16[528,768]{1,0:T(8,128)(2,1)S(1)}, bf16[528,768]{1,0:T(8,128)(2,1)S(1)}, u32[]{:S(2)}, u32[]{:S(2)}) collective-permute-start(bf16[528,768]{1,0:T(8,128)(2,1)S(1)} %get-tuple-element.70), channel_id=1, source_target_pairs={{0,1},{1,0},{2,3},{3,2},{4,5},{5,4},{6,7},{7,6},{8,9},{9,8},{10,11... | collective-permute-start | bytes 2433032 | tf_op jit(solution)/shard_map/ppermute | solution.py:142
  5.0 4.0 %project.1 = (bf16[192,448]{1,0:T(8,128)(2,1)S(1)}, bf16[384,448]{1,0:T(8,128)(2,1)S(1)}, bf16[448,768]{1,0:T(8,128)(2,1)}, f32[32,448]{1,0:T(8,128)}, f32[32,448]{1,0:T(8,128)}) custom-call(s32[4]{0:T(128)} %refs_0_.13, s32[8]{0:T(128)} %refs_1_.16, bf16[448,768]{1,0:T(8,128)(2,1)} %refs_0_.15, bf16[576,768]{1,0:T(8,128)(2,1)} %bitcast.12, f32[768]{0:T(1024)} %refs_1_.17, ...), custom_call_target="tpu_custom_call" | custom-call | tf_op jit(solution)/shard_map/project/pallas_call | solution.py:121
  14.0 2.6 %collective-permute-start.1 = (bf16[96,768]{1,0:T(8,128)(2,1)S(1)}, bf16[96,768]{1,0:T(8,128)(2,1)S(1)}, u32[]{:S(2)}, u32[]{:S(2)}) collective-permute-start(bf16[96,768]{1,0:T(8,128)(2,1)S(1)} %get-tuple-element.71), channel_id=1, source_target_pairs={{0,2},{1,3},{2,0},{3,1},{4,6},{5,7},{6,4},{7,5},{8,10},{9,11},{10,... | collective-permute-start | bytes 442376 | tf_op jit(solution)/shard_map/ppermute | solution.py:142
  16.5 4.5 %collective-permute-done.6.refs_5_.refs_10_ = bf16[384,448]{1,0:T(8,128)(2,1)S(1)} collective-permute-done((bf16[384,448]{1,0:T(8,128)(2,1)S(1)}, bf16[384,448]{1,0:T(8,128)(2,1)S(1)}, u32[]{:S(2)}, u32[]{:S(2)}) %collective-permute-start.6) | collective-permute-done | bytes 344096 | tf_op jit(solution)/shard_map/ppermute | solution.py:142
  21.1 2.5 %collective-permute-start.2 = (bf16[96,768]{1,0:T(8,128)(2,1)S(1)}, bf16[96,768]{1,0:T(8,128)(2,1)S(1)}, u32[]{:S(2)}, u32[]{:S(2)}) collective-permute-start(bf16[96,768]{1,0:T(8,128)(2,1)S(1)} %get-tuple-element.71), channel_id=1, source_target_pairs={{0,3},{1,2},{2,1},{3,0},{4,7},{5,6},{6,5},{7,4},{8,11},{9,10},{10,... | collective-permute-start | bytes 442376 | tf_op jit(solution)/shard_map/ppermute | solution.py:142
  23.5 4.2 %attention_forward.2.refs_6_ = f32[6,80,448]{2,1,0:T(8,128)S(1)} custom-call(s32[4]{0:T(128)} %refs_0_.13, s32[8]{0:T(128)} %refs_1_.16, bf16[192,448]{1,0:T(8,128)(2,1)S(1)} %get-tuple-element.72.refs_2_, bf16[192,448]{1,0:T(8,128)(2,1)S(1)} %collective-permute-done.3.refs_3_, bf16[384,448]{1,0:T(8,128)(2,1)S(1)} %get-tuple-element.73.refs_4_.refs_10_, ...), custom_call_target="tpu_custom_call" | custom-call | tf_op jit(solution)/shard_map/attention_forward/pallas_call | solution.py:121
  27.8 3.9 %collective-permute-done.2.refs_8_.refs_2_ = bf16[96,768]{1,0:T(8,128)(2,1)S(1)} collective-permute-done((bf16[96,768]{1,0:T(8,128)(2,1)S(1)}, bf16[96,768]{1,0:T(8,128)(2,1)S(1)}, u32[]{:S(2)}, u32[]{:S(2)}) %collective-permute-start.2) | collective-permute-done | bytes 147488 | tf_op jit(solution)/shard_map/ppermute | solution.py:142
  31.7 5.7 %attention_forward.3 = (f32[3,80,448]{2,1,0:T(8,128)S(1)}, f32[3,80,448]{2,1,0:T(8,128)S(1)}) custom-call(s32[4]{0:T(128)} %refs_0_.13, s32[8]{0:T(128)} %refs_1_.16, bf16[192,448]{1,0:T(8,128)(2,1)S(1)} %get-tuple-element.72.refs_2_, bf16[192,448]{1,0:T(8,128)(2,1)S(1)} %collective-permute-done.3.refs_3_, ...), custom_call_target="tpu_custom_call" | custom-call | tf_op jit(solution)/shard_map/attention_forward/pallas_call | solution.py:121
  38.0 2.9 %collective-permute-done.8.refs_1_ = f32[3,80,448]{2,1,0:T(8,128)S(1)} collective-permute-done((f32[3,80,448]{2,1,0:T(8,128)S(1)}, f32[3,80,448]{2,1,0:T(8,128)S(1)}, u32[]{:S(2)}, u32[]{:S(2)}) %collective-permute-start.8) | collective-permute-done | bytes 430112 | tf_op jit(solution)/shard_map/ppermute | solution.py:142
  43.4 2.4 %collective-permute-start.9 = (bf16[192,224]{1,0:T(8,128)(2,1)S(1)}, bf16[192,224]{1,0:T(8,128)(2,1)S(1)}, u32[]{:S(2)}, u32[]{:S(2)}) collective-permute-start(bf16[192,224]{1,0:T(8,128)(2,1)S(1)} %get-tuple-element.82), channel_id=1, source_target_pairs={{0,3},{1,2},{2,1},{3,0},{4,7},{5,6},{6,5},{7,4},{8,11},{9,10},{10,... | collective-permute-start | bytes 258056 | tf_op jit(solution)/shard_map/ppermute | solution.py:142
  45.8 3.2 %stage.1 = (bf16[224,768]{1,0:T(8,128)(2,1)S(1)}, bf16[224,768]{1,0:T(8,128)(2,1)S(1)}, bf16[768,768]{1,0:T(8,128)(2,1)S(1)}, bf16[1152,768]{1,0:T(8,128)(2,1)S(1)}, bf16[576,768]{1,0:T(8,128)(2,1)S(1)}) custom-call(bf16[448,768]{1,0:T(8,128)(2,1)} %refs_0_.15, bf16[448,768]{1,0:T(8,128)(2,1)} %refs_2_.7, bf16[576,768]{1,0:T(8,128)(2,1)} %bitcast.15, ...), custom_call_target="tpu_custom_call" | custom-call | tf_op jit(solution)/shard_map/stage/pallas_call | solution.py:121
  52.4 6.1 %feed.1 = (f32[224,768]{1,0:T(8,128)}, f32[112,768]{1,0:T(8,128)}, bf16[224,768]{1,0:T(8,128)(2,1)}, bf16[576,224]{1,0:T(8,128)(2,1)}, bf16[1152,224]{1,0:T(8,12...) custom-call(bf16[224,768]{1,0:T(8,128)(2,1)S(1)} %get-tuple-element.75.refs_0_, ...), custom_call_target="tpu_custom_call" | custom-call | tf_op jit(solution)/shard_map/feed/pallas_call | solution.py:121
  61.1 2.5 %down.1 = (f32[112,768]{1,0:T(8,128)}, bf16[112,768]{1,0:T(8,128)(2,1)}) custom-call(bf16[576,224]{1,0:T(8,128)(2,1)} %get-tuple-element.83.refs_0_, bf16[576,768]{1,0:T(8,128)(2,1)S(1)} %get-tuple-element.79.refs_4_.refs_1_, f32[224,768]{1,0:T(8,128)} %get-tuple-element.84.refs_2_), custom_call_target="tpu_custom_call" | custom-call | tf_op jit(solution)/shard_map/down/pallas_call | solution.py:121
  63.6 7.4 %collective-permute-done.13.refs_5_ = bf16[112,768]{1,0:T(8,128)(2,1)S(1)} collective-permute-done((bf16[112,768]{1,0:T(8,128)(2,1)}, bf16[112,768]{1,0:T(8,128)(2,1)S(1)}, u32[]{:S(2)}, u32[]{:S(2)}) %collective-permute-start.13) | collective-permute-done | bytes 172064 | tf_op jit(solution)/shard_map/ppermute | solution.py:142
  71.0 2.6 %branch.1 = (f32[112,768]{1,0:T(8,128)}, bf16[112,768]{1,0:T(8,128)(2,1)}, bf16[112,192]{1,0:T(8,128)(2,1)S(1)}, bf16[112,192]{1,0:T(8,128)(2,1)S(1)}, bf16[112,...) custom-call(f32[112,768]{1,0:T(8,128)} %get-tuple-element.87.refs_0_, bf16[448,768]{1,0:T(8,128)(2,1)} %refs_2_.7, ...), custom_call_target="tpu_custom_call" | custom-call | tf_op jit(solution)/shard_map/branch/pallas_call | solution.py:121
  75.3 2.4 %collective-permute-start.15 = (bf16[112,192]{1,0:T(8,128)(2,1)S(1)}, bf16[112,192]{1,0:T(8,128)(2,1)S(1)}, u32[]{:S(2)}, u32[]{:S(2)}) collective-permute-start(bf16[112,192]{1,0:T(8,128)(2,1)S(1)} %get-tuple-element.92), channel_id=1, source_target_pairs={{0,2},{1,3},{2,0},{3,1},{4,6},{5,7},{6,4},{7,5},{8,10},{9,11},{10,... | collective-permute-start | bytes 129032 | tf_op jit(solution)/shard_map/ppermute | solution.py:142
  78.1 4.0 %early_grads.1 = (f32[864,384]{1,0:T(8,128)S(1)}, bf16[864,384]{1,0:T(8,128)(2,1)S(1)}) custom-call(bf16[576,224]{1,0:T(8,128)(2,1)} %get-tuple-element.83.refs_0_, bf16[1152,224]{1,0:T(8,128)(2,1)} %get-tuple-element.94.refs_1_, bf16[448,768]{1,0:T(8,128)(2,1)} %refs_2_.7, bf16[224,768]{1,0:T(8,128)(2,1)} %get-tuple-element.95.refs_3_, ...), custom_call_target="tpu_custom_call" | custom-call | tf_op jit(solution)/shard_map/early_grads/pallas_call | solution.py:121
  83.0 2.4 %collective-permute-start.12 = (bf16[112,768]{1,0:T(8,128)(2,1)S(1)}, bf16[112,768]{1,0:T(8,128)(2,1)S(1)}, u32[]{:S(2)}, u32[]{:S(2)}) collective-permute-start(bf16[112,768]{1,0:T(8,128)(2,1)S(1)} %copy-done.8), channel_id=1, source_target_pairs={{0,2},{1,3},{2,0},{3,1},{4,6},{5,7},{6,4},{7,5},{8,10},{9,11},{10,... | collective-permute-start | bytes 516104 | tf_op jit(solution)/shard_map/ppermute | solution.py:142
  85.4 7.2 %attention_backward.2 = (bf16[384,448]{1,0:T(8,128)(2,1)S(1)}, bf16[384,448]{1,0:T(8,128)(2,1)S(1)}, bf16[384,448]{1,0:T(8,128)(2,1)S(1)}, f32[6,64,448]{2,1,0:T(8,128)S(1)}) custom-call(s32[4]{0:T(128)} %refs_0_.13, s32[8]{0:T(128)} %refs_1_.16, bf16[192,448]{1,0:T(8,128)(2,1)S(1)} %get-tuple-element.72.refs_2_, ...), custom_call_target="tpu_custom_call" | custom-call | tf_op jit(solution)/shard_map/attention_backward/pallas_call | solution.py:121
  92.8 3.4 %collective-permute-start.27 = (bf16[384,448]{1,0:T(8,128)(2,1)S(1)}, bf16[384,448]{1,0:T(8,128)(2,1)S(1)}, u32[]{:S(2)}, u32[]{:S(2)}) collective-permute-start(bf16[384,448]{1,0:T(8,128)(2,1)S(1)} %get-tuple-element.110), channel_id=1, source_target_pairs={{0,24},{4,28},{8,16},{12,20},{16,8},{20,12},{24,0},{28,4},{1,25},{... | collective-permute-start | bytes 1032200 | tf_op jit(solution)/shard_map/ppermute | solution.py:142
  97.3 5.2 %attention_backward.3 = (f32[384,448]{1,0:T(8,128)S(1)}, f32[192,448]{1,0:T(8,128)S(1)}, bf16[192,448]{1,0:T(8,128)(2,1)S(1)}) custom-call(s32[4]{0:T(128)} %refs_0_.13, s32[8]{0:T(128)} %refs_1_.16, bf16[192,448]{1,0:T(8,128)(2,1)S(1)} %get-tuple-element.72.refs_2_, bf16[192,448]{1,0:T(8,128)(2,1)S(1)} %collective-permute-done.3.refs_3_, ...), custom_call_target="tpu_custom_call" | custom-call | tf_op jit(solution)/shard_map/attention_backward/pallas_call | solution.py:121
  104.6 3.3 %collective-permute-done.31.refs_5_ = bf16[112,768]{1,0:T(8,128)(2,1)S(1)} collective-permute-done((bf16[112,768]{1,0:T(8,128)(2,1)S(1)}, bf16[112,768]{1,0:T(8,128)(2,1)S(1)}, u32[]{:S(2)}, u32[]{:S(2)}) %collective-permute-start.31) | collective-permute-done | bytes 172064 | tf_op jit(solution)/shard_map/ppermute | solution.py:142
  113.4 2.5 %unproject.1 = (bf16[576,448]{1,0:T(8,128)(2,1)S(1)}, f32[128,768]{1,0:T(8,128)S(1)}, bf16[128,768]{1,0:T(8,128)(2,1)S(1)}, bf16[128,768]{1,0:T(8,128)(2,1)S(1)}, bf16[128,768]{1,0:T(8,128)(2,1)S(1)}) custom-call(bf16[448,768]{1,0:T(8,128)(2,1)S(1)} %copy-done, bf16[576,768]{1,0:T(8,128)(2,1)S(1)} %bitcast.13, f32[32,448]{1,0:T(8,128)S(1)} %copy-done.5, ...), custom_call_target="tpu_custom_call" | custom-call | tf_op jit(solution)/shard_map/unproject/pallas_call | solution.py:121
  115.9 2.9 %collective-permute-done.33.refs_6_ = bf16[112,768]{1,0:T(8,128)(2,1)S(1)} collective-permute-done((bf16[112,768]{1,0:T(8,128)(2,1)S(1)}, bf16[112,768]{1,0:T(8,128)(2,1)S(1)}, u32[]{:S(2)}, u32[]{:S(2)}) %collective-permute-start.33) | collective-permute-done | bytes 172064 | tf_op jit(solution)/shard_map/ppermute | solution.py:142
  118.8 2.9 %collective-permute-done.32.refs_4_ = bf16[112,768]{1,0:T(8,128)(2,1)S(1)} collective-permute-done((bf16[112,768]{1,0:T(8,128)(2,1)S(1)}, bf16[112,768]{1,0:T(8,128)(2,1)S(1)}, u32[]{:S(2)}, u32[]{:S(2)}) %collective-permute-start.32) | collective-permute-done | bytes 172064 | tf_op jit(solution)/shard_map/ppermute | solution.py:142
  129.3 3.2 %collective-permute-done.28.refs_1_ = bf16[128,768]{1,0:T(8,128)(2,1)S(1)} collective-permute-done((bf16[128,768]{1,0:T(8,128)(2,1)S(1)}, bf16[128,768]{1,0:T(8,128)(2,1)S(1)}, u32[]{:S(2)}, u32[]{:S(2)}) %collective-permute-start.28) | collective-permute-done | bytes 196640 | tf_op jit(solution)/shard_map/ppermute | solution.py:142
  132.6 10.2 %collective-permute-done.29.refs_2_ = bf16[128,768]{1,0:T(8,128)(2,1)S(1)} collective-permute-done((bf16[128,768]{1,0:T(8,128)(2,1)S(1)}, bf16[128,768]{1,0:T(8,128)(2,1)S(1)}, u32[]{:S(2)}, u32[]{:S(2)}) %collective-permute-start.29) | collective-permute-done | bytes 196640 | tf_op jit(solution)/shard_map/ppermute | solution.py:142
  151.9 6.2 %collective-permute-done.22.refs_1_ = bf16[112,768]{1,0:T(8,128)(2,1)S(1)} collective-permute-done((bf16[112,768]{1,0:T(8,128)(2,1)S(1)}, bf16[112,768]{1,0:T(8,128)(2,1)S(1)}, u32[]{:S(2)}, u32[]{:S(2)}) %collective-permute-start.22) | collective-permute-done | bytes 172064 | tf_op jit(solution)/shard_map/ppermute | solution.py:142
  159.6 3.8 %collective-permute-done.37.refs_2_ = bf16[112,768]{1,0:T(8,128)(2,1)S(1)} collective-permute-done((bf16[112,768]{1,0:T(8,128)(2,1)S(1)}, bf16[112,768]{1,0:T(8,128)(2,1)S(1)}, u32[]{:S(2)}, u32[]{:S(2)}) %collective-permute-start.37) | collective-permute-done | bytes 172064 | tf_op jit(solution)/shard_map/ppermute | solution.py:142
  164.4 3.1 %collective-permute-done.43.refs_2_ = bf16[424,384]{1,0:T(8,128)(2,1)S(1)} collective-permute-done((bf16[424,384]{1,0:T(8,128)(2,1)S(1)}, bf16[424,384]{1,0:T(8,128)(2,1)S(1)}, u32[]{:S(2)}, u32[]{:S(2)}) %collective-permute-start.43) | collective-permute-done | bytes 325664 | tf_op jit(solution)/shard_map/ppermute | solution.py:142
  168.0 3.0 %collective-permute-done.45.refs_1_ = bf16[1648,384]{1,0:T(8,128)(2,1)S(1)} collective-permute-done((bf16[1648,384]{1,0:T(8,128)(2,1)S(1)}, bf16[1648,384]{1,0:T(8,128)(2,1)S(1)}, u32[]{:S(2)}, u32[]{:S(2)}) %collective-permute-start.45) | collective-permute-done | bytes 1265696 | tf_op jit(solution)/shard_map/ppermute | solution.py:142
  170.9 2.7 %finish.1 = (f32[576,768]{1,0:T(8,128)}, f32[192,768]{1,0:T(8,128)}, f32[288,768]{1,0:T(8,128)}, f32[576,768]{1,0:T(8,128)}, f32[768]{0:T(1024)}, /*index=5*/f32[768]{0:T(1024)}) custom-call(bf16[1648,384]{1,0:T(8,128)(2,1)S(1)} %collect.1.refs_0_, bf16[1648,384]{1,0:T(8,128)(2,1)S(1)} %collective-permute-done.45.refs_1_), custom_call_target="tpu_custom_call" | custom-call | tf_op jit(solution)/shard_map/finish/pallas_call | solution.py:121
  (104 shorter events, 46.7 us)
Async XLA Ops:
  1.9 35.4 %collective-permute-start = (bf16[528,768]{1,0:T(8,128)(2,1)S(1)}, bf16[528,768]{1,0:T(8,128)(2,1)S(1)}, u32[]{:S(2)}, u32[]{:S(2)}) collective-permute-start(bf16[528,768]{1,0:T(8,128)(2,1)S(1)} %get-tuple-element.70), channel_id=1, source_target_pairs={{0,1},{1,0},{2,3},{3,2},{4,5},{5,4},{6,7},{7,6},{8,9},{9,8},{10,11... | collective-permute-start | bytes 2433032 | tf_op jit(solution)/shard_map/ppermute | solution.py:142
  9.0 12.1 %collective-permute-start.6 = (bf16[384,448]{1,0:T(8,128)(2,1)S(1)}, bf16[384,448]{1,0:T(8,128)(2,1)S(1)}, u32[]{:S(2)}, u32[]{:S(2)}) collective-permute-start(bf16[384,448]{1,0:T(8,128)(2,1)S(1)} %get-tuple-element.73.refs_4_.refs_10_), channel_id=1, source_target_pairs={{0,8},{4,12},{8,0},{12,4},{16,24},{20,28},{24,16},{28,20},{1,9},{5... | collective-permute-start | bytes 1032200 | tf_op jit(solution)/shard_map/ppermute | solution.py:142
  10.5 21.2 %collective-permute-start.4 = (bf16[384,448]{1,0:T(8,128)(2,1)S(1)}, bf16[384,448]{1,0:T(8,128)(2,1)S(1)}, u32[]{:S(2)}, u32[]{:S(2)}) collective-permute-start(bf16[384,448]{1,0:T(8,128)(2,1)S(1)} %get-tuple-element.73.refs_4_.refs_10_), channel_id=1, source_target_pairs={{0,16},{4,20},{8,24},{12,28},{16,0},{20,4},{24,8},{28,12},{1,17},{... | collective-permute-start | bytes 1032200 | tf_op jit(solution)/shard_map/ppermute | solution.py:142
  12.0 19.6 %collective-permute-start.5 = (bf16[384,448]{1,0:T(8,128)(2,1)S(1)}, bf16[384,448]{1,0:T(8,128)(2,1)S(1)}, u32[]{:S(2)}, u32[]{:S(2)}) collective-permute-start(bf16[384,448]{1,0:T(8,128)(2,1)S(1)} %get-tuple-element.73.refs_4_.refs_10_), channel_id=1, source_target_pairs={{0,24},{4,28},{8,16},{12,20},{16,8},{20,12},{24,0},{28,4},{1,25},{... | collective-permute-start | bytes 1032200 | tf_op jit(solution)/shard_map/ppermute | solution.py:142
  14.0 13.8 %collective-permute-start.1 = (bf16[96,768]{1,0:T(8,128)(2,1)S(1)}, bf16[96,768]{1,0:T(8,128)(2,1)S(1)}, u32[]{:S(2)}, u32[]{:S(2)}) collective-permute-start(bf16[96,768]{1,0:T(8,128)(2,1)S(1)} %get-tuple-element.71), channel_id=1, source_target_pairs={{0,2},{1,3},{2,0},{3,1},{4,6},{5,7},{6,4},{7,5},{8,10},{9,11},{10,... | collective-permute-start | bytes 442376 | tf_op jit(solution)/shard_map/ppermute | solution.py:142
  21.1 10.6 %collective-permute-start.2 = (bf16[96,768]{1,0:T(8,128)(2,1)S(1)}, bf16[96,768]{1,0:T(8,128)(2,1)S(1)}, u32[]{:S(2)}, u32[]{:S(2)}) collective-permute-start(bf16[96,768]{1,0:T(8,128)(2,1)S(1)} %get-tuple-element.71), channel_id=1, source_target_pairs={{0,3},{1,2},{2,1},{3,0},{4,7},{5,6},{6,5},{7,4},{8,11},{9,10},{10,... | collective-permute-start | bytes 442376 | tf_op jit(solution)/shard_map/ppermute | solution.py:142
  41.4 9.4 %collective-permute-start.10 = (bf16[192,224]{1,0:T(8,128)(2,1)S(1)}, bf16[192,224]{1,0:T(8,128)(2,1)S(1)}, u32[]{:S(2)}, u32[]{:S(2)}) collective-permute-start(bf16[192,224]{1,0:T(8,128)(2,1)S(1)} %get-tuple-element.81.refs_6_), channel_id=1, source_target_pairs={{0,2},{1,3},{2,0},{3,1},{4,6},{5,7},{6,4},{7,5},{8,10},{9,11},{10,... | collective-permute-start | bytes 258056 | tf_op jit(solution)/shard_map/ppermute | solution.py:142
  58.5 19.6 %collective-permute-start.17 = (bf16[224,768]{1,0:T(8,128)(2,1)}, bf16[224,768]{1,0:T(8,128)(2,1)S(1)}, u32[]{:S(2)}, u32[]{:S(2)}) collective-permute-start(bf16[224,768]{1,0:T(8,128)(2,1)} %get-tuple-element.95.refs_3_), channel_id=1, source_target_pairs={{0,1},{1,0},{2,3},{3,2},{4,5},{5,4},{6,7},{7,6},{8,9},{9,8},{10,11... | collective-permute-start | bytes 1032200 | tf_op jit(solution)/shard_map/ppermute | solution.py:142
  60.2 10.8 %collective-permute-start.13 = (bf16[112,768]{1,0:T(8,128)(2,1)}, bf16[112,768]{1,0:T(8,128)(2,1)S(1)}, u32[]{:S(2)}, u32[]{:S(2)}) collective-permute-start(bf16[112,768]{1,0:T(8,128)(2,1)} %get-tuple-element.89), channel_id=1, source_target_pairs={{0,2},{1,3},{2,0},{3,1},{4,6},{5,7},{6,4},{7,5},{8,10},{9,11},{10,... | collective-permute-start | bytes 516104 | tf_op jit(solution)/shard_map/ppermute | solution.py:142
  83.0 19.5 %collective-permute-start.12 = (bf16[112,768]{1,0:T(8,128)(2,1)S(1)}, bf16[112,768]{1,0:T(8,128)(2,1)S(1)}, u32[]{:S(2)}, u32[]{:S(2)}) collective-permute-start(bf16[112,768]{1,0:T(8,128)(2,1)S(1)} %copy-done.8), channel_id=1, source_target_pairs={{0,2},{1,3},{2,0},{3,1},{4,6},{5,7},{6,4},{7,5},{8,10},{9,11},{10,... | collective-permute-start | bytes 516104 | tf_op jit(solution)/shard_map/ppermute | solution.py:142
  92.7 17.3 %collective-permute-start.25 = (bf16[384,448]{1,0:T(8,128)(2,1)S(1)}, bf16[384,448]{1,0:T(8,128)(2,1)S(1)}, u32[]{:S(2)}, u32[]{:S(2)}) collective-permute-start(bf16[384,448]{1,0:T(8,128)(2,1)S(1)} %get-tuple-element.108), channel_id=1, source_target_pairs={{0,8},{4,12},{8,0},{12,4},{16,24},{20,28},{24,16},{28,20},{1,9},{5... | collective-permute-start | bytes 1032200 | tf_op jit(solution)/shard_map/ppermute | solution.py:142
  92.7 19.5 %collective-permute-start.26 = (bf16[384,448]{1,0:T(8,128)(2,1)S(1)}, bf16[384,448]{1,0:T(8,128)(2,1)S(1)}, u32[]{:S(2)}, u32[]{:S(2)}) collective-permute-start(bf16[384,448]{1,0:T(8,128)(2,1)S(1)} %get-tuple-element.109), channel_id=1, source_target_pairs={{0,16},{4,20},{8,24},{12,28},{16,0},{20,4},{24,8},{28,12},{1,17},{... | collective-permute-start | bytes 1032200 | tf_op jit(solution)/shard_map/ppermute | solution.py:142
  92.8 20.5 %collective-permute-start.27 = (bf16[384,448]{1,0:T(8,128)(2,1)S(1)}, bf16[384,448]{1,0:T(8,128)(2,1)S(1)}, u32[]{:S(2)}, u32[]{:S(2)}) collective-permute-start(bf16[384,448]{1,0:T(8,128)(2,1)S(1)} %get-tuple-element.110), channel_id=1, source_target_pairs={{0,24},{4,28},{8,16},{12,20},{16,8},{20,12},{24,0},{28,4},{1,25},{... | collective-permute-start | bytes 1032200 | tf_op jit(solution)/shard_map/ppermute | solution.py:142
  96.2 11.7 %collective-permute-start.31 = (bf16[112,768]{1,0:T(8,128)(2,1)S(1)}, bf16[112,768]{1,0:T(8,128)(2,1)S(1)}, u32[]{:S(2)}, u32[]{:S(2)}) collective-permute-start(bf16[112,768]{1,0:T(8,128)(2,1)S(1)} %copy-done.2), channel_id=1, source_target_pairs={{0,2},{1,3},{2,0},{3,1},{4,6},{5,7},{6,4},{7,5},{8,10},{9,11},{10,... | collective-permute-start | bytes 516104 | tf_op jit(solution)/shard_map/ppermute | solution.py:142
  107.9 10.9 %collective-permute-start.33 = (bf16[112,768]{1,0:T(8,128)(2,1)S(1)}, bf16[112,768]{1,0:T(8,128)(2,1)S(1)}, u32[]{:S(2)}, u32[]{:S(2)}) collective-permute-start(bf16[112,768]{1,0:T(8,128)(2,1)S(1)} %copy-done.2), channel_id=1, source_target_pairs={{0,1},{1,0},{2,3},{3,2},{4,5},{5,4},{6,7},{7,6},{8,9},{9,8},{10,11... | collective-permute-start | bytes 516104 | tf_op jit(solution)/shard_map/ppermute | solution.py:142
  107.9 13.8 %collective-permute-start.32 = (bf16[112,768]{1,0:T(8,128)(2,1)S(1)}, bf16[112,768]{1,0:T(8,128)(2,1)S(1)}, u32[]{:S(2)}, u32[]{:S(2)}) collective-permute-start(bf16[112,768]{1,0:T(8,128)(2,1)S(1)} %collective-permute-done.31.refs_5_), channel_id=1, source_target_pairs={{0,1},{1,0},{2,3},{3,2},{4,5},{5,4},{6,7},{7,6},{8,9},{9,8},{10,11... | collective-permute-start | bytes 516104 | tf_op jit(solution)/shard_map/ppermute | solution.py:142
  110.0 11.8 %collective-permute-start.21 = (bf16[112,768]{1,0:T(8,128)(2,1)S(1)}, bf16[112,768]{1,0:T(8,128)(2,1)S(1)}, u32[]{:S(2)}, u32[]{:S(2)}) collective-permute-start(bf16[112,768]{1,0:T(8,128)(2,1)S(1)} %total_of.3.refs_0_.refs_11_), channel_id=1, source_target_pairs={{0,2},{1,3},{2,0},{3,1},{4,6},{5,7},{6,4},{7,5},{8,10},{9,11},{10,... | collective-permute-start | bytes 516104 | tf_op jit(solution)/shard_map/ppermute | solution.py:142
  112.2 15.1 %collective-permute-start.35 = (bf16[864,384]{1,0:T(8,128)(2,1)S(1)}, bf16[864,384]{1,0:T(8,128)(2,1)S(1)}, u32[]{:S(2)}, u32[]{:S(2)}) collective-permute-start(bf16[864,384]{1,0:T(8,128)(2,1)S(1)} %get-tuple-element.119), channel_id=1, source_target_pairs={{0,4},{4,0},{8,12},{12,8},{16,20},{20,16},{24,28},{28,24},{1,5},{5... | collective-permute-start | bytes 1990664 | tf_op jit(solution)/shard_map/ppermute | solution.py:142
  122.8 9.7 %collective-permute-start.28 = (bf16[128,768]{1,0:T(8,128)(2,1)S(1)}, bf16[128,768]{1,0:T(8,128)(2,1)S(1)}, u32[]{:S(2)}, u32[]{:S(2)}) collective-permute-start(bf16[128,768]{1,0:T(8,128)(2,1)S(1)} %get-tuple-element.112), channel_id=1, source_target_pairs={{0,3},{1,2},{2,1},{3,0},{4,7},{5,6},{6,5},{7,4},{8,11},{9,10},{10,... | collective-permute-start | bytes 589832 | tf_op jit(solution)/shard_map/ppermute | solution.py:142
  124.7 18.1 %collective-permute-start.29 = (bf16[128,768]{1,0:T(8,128)(2,1)S(1)}, bf16[128,768]{1,0:T(8,128)(2,1)S(1)}, u32[]{:S(2)}, u32[]{:S(2)}) collective-permute-start(bf16[128,768]{1,0:T(8,128)(2,1)S(1)} %get-tuple-element.113), channel_id=1, source_target_pairs={{0,2},{1,3},{2,0},{3,1},{4,6},{5,7},{6,4},{7,5},{8,10},{9,11},{10,... | collective-permute-start | bytes 589832 | tf_op jit(solution)/shard_map/ppermute | solution.py:142
  124.9 17.9 %collective-permute-start.30 = (bf16[128,768]{1,0:T(8,128)(2,1)S(1)}, bf16[128,768]{1,0:T(8,128)(2,1)S(1)}, u32[]{:S(2)}, u32[]{:S(2)}) collective-permute-start(bf16[128,768]{1,0:T(8,128)(2,1)S(1)} %get-tuple-element.114), channel_id=1, source_target_pairs={{0,1},{1,0},{2,3},{3,2},{4,5},{5,4},{6,7},{7,6},{8,9},{9,8},{10,11... | collective-permute-start | bytes 589832 | tf_op jit(solution)/shard_map/ppermute | solution.py:142
  127.7 19.4 %collective-permute-start.39 = (bf16[408,384]{1,0:T(8,128)(2,1)S(1)}, bf16[408,384]{1,0:T(8,128)(2,1)S(1)}, u32[]{:S(2)}, u32[]{:S(2)}) collective-permute-start(bf16[408,384]{1,0:T(8,128)(2,1)S(1)} %get-tuple-element.123), channel_id=1, source_target_pairs={{0,24},{4,28},{8,16},{12,20},{16,8},{20,12},{24,0},{28,4},{1,25},{... | collective-permute-start | bytes 940040 | tf_op jit(solution)/shard_map/ppermute | solution.py:142
  127.8 21.4 %collective-permute-start.40 = (bf16[408,384]{1,0:T(8,128)(2,1)S(1)}, bf16[408,384]{1,0:T(8,128)(2,1)S(1)}, u32[]{:S(2)}, u32[]{:S(2)}) collective-permute-start(bf16[408,384]{1,0:T(8,128)(2,1)S(1)} %get-tuple-element.124), channel_id=1, source_target_pairs={{0,16},{4,20},{8,24},{12,28},{16,0},{20,4},{24,8},{28,12},{1,17},{... | collective-permute-start | bytes 940040 | tf_op jit(solution)/shard_map/ppermute | solution.py:142
  132.5 16.7 %collective-permute-start.41 = (bf16[408,384]{1,0:T(8,128)(2,1)S(1)}, bf16[408,384]{1,0:T(8,128)(2,1)S(1)}, u32[]{:S(2)}, u32[]{:S(2)}) collective-permute-start(bf16[408,384]{1,0:T(8,128)(2,1)S(1)} %get-tuple-element.125), channel_id=1, source_target_pairs={{0,8},{4,12},{8,0},{12,4},{16,24},{20,28},{24,16},{28,20},{1,9},{5... | collective-permute-start | bytes 940040 | tf_op jit(solution)/shard_map/ppermute | solution.py:142
  142.8 9.0 %collective-permute-start.23 = (bf16[112,768]{1,0:T(8,128)(2,1)S(1)}, bf16[112,768]{1,0:T(8,128)(2,1)S(1)}, u32[]{:S(2)}, u32[]{:S(2)}) collective-permute-start(bf16[112,768]{1,0:T(8,128)(2,1)S(1)} %total_of.3.refs_0_.refs_11_), channel_id=1, source_target_pairs={{0,1},{1,0},{2,3},{3,2},{4,5},{5,4},{6,7},{7,6},{8,9},{9,8},{10,11... | collective-permute-start | bytes 516104 | tf_op jit(solution)/shard_map/ppermute | solution.py:142
  142.8 15.3 %collective-permute-start.22 = (bf16[112,768]{1,0:T(8,128)(2,1)S(1)}, bf16[112,768]{1,0:T(8,128)(2,1)S(1)}, u32[]{:S(2)}, u32[]{:S(2)}) collective-permute-start(bf16[112,768]{1,0:T(8,128)(2,1)S(1)} %collective-permute-done.21.refs_2_.refs_7_), channel_id=1, source_target_pairs={{0,1},{1,0},{2,3},{3,2},{4,5},{5,4},{6,7},{7,6},{8,9},{9,8},{10,11... | collective-permute-start | bytes 516104 | tf_op jit(solution)/shard_map/ppermute | solution.py:142
  147.1 11.0 %collective-permute-start.36 = (bf16[112,768]{1,0:T(8,128)(2,1)S(1)}, bf16[112,768]{1,0:T(8,128)(2,1)S(1)}, u32[]{:S(2)}, u32[]{:S(2)}) collective-permute-start(bf16[112,768]{1,0:T(8,128)(2,1)S(1)} %get-tuple-element.121.refs_0_), channel_id=1, source_target_pairs={{0,3},{1,2},{2,1},{3,0},{4,7},{5,6},{6,5},{7,4},{8,11},{9,10},{10,... | collective-permute-start | bytes 516104 | tf_op jit(solution)/shard_map/ppermute | solution.py:142
  149.2 14.3 %collective-permute-start.37 = (bf16[112,768]{1,0:T(8,128)(2,1)S(1)}, bf16[112,768]{1,0:T(8,128)(2,1)S(1)}, u32[]{:S(2)}, u32[]{:S(2)}) collective-permute-start(bf16[112,768]{1,0:T(8,128)(2,1)S(1)} %get-tuple-element.121.refs_0_), channel_id=1, source_target_pairs={{0,2},{1,3},{2,0},{3,1},{4,6},{5,7},{6,4},{7,5},{8,10},{9,11},{10,... | collective-permute-start | bytes 516104 | tf_op jit(solution)/shard_map/ppermute | solution.py:142
  149.2 14.3 %collective-permute-start.38 = (bf16[112,768]{1,0:T(8,128)(2,1)S(1)}, bf16[112,768]{1,0:T(8,128)(2,1)S(1)}, u32[]{:S(2)}, u32[]{:S(2)}) collective-permute-start(bf16[112,768]{1,0:T(8,128)(2,1)S(1)} %get-tuple-element.121.refs_0_), channel_id=1, source_target_pairs={{0,1},{1,0},{2,3},{3,2},{4,5},{5,4},{6,7},{7,6},{8,9},{9,8},{10,11... | collective-permute-start | bytes 516104 | tf_op jit(solution)/shard_map/ppermute | solution.py:142
  151.8 12.6 %collective-permute-start.42 = (bf16[424,384]{1,0:T(8,128)(2,1)S(1)}, bf16[424,384]{1,0:T(8,128)(2,1)S(1)}, u32[]{:S(2)}, u32[]{:S(2)}) collective-permute-start(bf16[424,384]{1,0:T(8,128)(2,1)S(1)} %sum_piece.1.refs_0_), channel_id=1, source_target_pairs={{0,24},{4,28},{8,16},{12,20},{16,8},{20,12},{24,0},{28,4},{1,25},{... | collective-permute-start | bytes 976904 | tf_op jit(solution)/shard_map/ppermute | solution.py:142
  158.1 9.5 %collective-permute-start.43 = (bf16[424,384]{1,0:T(8,128)(2,1)S(1)}, bf16[424,384]{1,0:T(8,128)(2,1)S(1)}, u32[]{:S(2)}, u32[]{:S(2)}) collective-permute-start(bf16[424,384]{1,0:T(8,128)(2,1)S(1)} %sum_piece.1.refs_0_), channel_id=1, source_target_pairs={{0,16},{4,20},{8,24},{12,28},{16,0},{20,4},{24,8},{28,12},{1,17},{... | collective-permute-start | bytes 976904 | tf_op jit(solution)/shard_map/ppermute | solution.py:142
  158.1 9.5 %collective-permute-start.44 = (bf16[424,384]{1,0:T(8,128)(2,1)S(1)}, bf16[424,384]{1,0:T(8,128)(2,1)S(1)}, u32[]{:S(2)}, u32[]{:S(2)}) collective-permute-start(bf16[424,384]{1,0:T(8,128)(2,1)S(1)} %sum_piece.1.refs_0_), channel_id=1, source_target_pairs={{0,8},{4,12},{8,0},{12,4},{16,24},{20,28},{24,16},{28,20},{1,9},{5... | collective-permute-start | bytes 976904 | tf_op jit(solution)/shard_map/ppermute | solution.py:142
  (23 other events, 158.4 us)

commit v11 on v10

--- a/solution.py
+++ b/solution.py
@@ -275,9 +275,9 @@
         [
             ((width, rows), BF16, "v"),
             ((2 * width, rows), BF16, "v"),
-            ((rows, model), BF16, "h"),
-            ((HALF, rows), F32, "h"),
-            ((HALF, rows), F32, "h"),
+            ((rows, model), BF16, "v"),
+            ((HALF, rows), F32, "v"),
+            ((HALF, rows), F32, "v"),
         ],
         [pltpu.VMEM((3 * width, rows), F32)]
         + doc_scratch(doc_lengths, roster)
@@ -694,15 +694,15 @@
         functools.partial(feed_kernel, n_tp),
         kinds(staged, "v") + [(gain, "h")] + kinds(outs, "v"),
         [
-            ((rows, model), F32, "h"),
-            ((part, model), F32, "h"),
-            ((rows, model), BF16, "h"),
-            ((units, rows), BF16, "h"),
-            ((2 * units, rows), BF16, "h"),
-            ((8, model), F32, "h"),
-            ((part, model), F32, "h"),
+            ((rows, model), F32, "v"),
+            ((part, model), F32, "v"),
+            ((rows, model), BF16, "v"),
+            ((units, rows), BF16, "v"),
+            ((2 * units, rows), BF16, "v"),
+            ((8, model), F32, "v"),
+            ((part, model), F32, "v"),
         ]
-        + [((part, model), BF16, "h")] * (n_tp // 2 - 1),
+        + [((part, model), BF16, "v")] * (n_tp // 2 - 1),
         [
             pltpu.VMEM((n_tp * outs[0].shape[0], rows), BF16),
             pltpu.VMEM((rows, model), F32),
@@ -743,10 +743,10 @@
     return call(
         "branch",
         functools.partial(branch_kernel, n_tp, len(arrived)),
-        [(middle_part, "h"), (cotangent, part)]
-        + [(gain, "h"), (w_full, "v"), (arrived[0], "h")]
+        [(middle_part, "v"), (cotangent, part)]
+        + [(gain, "h"), (w_full, "v"), (arrived[0], "v")]
         + kinds(arrived[1:], "v"),
-        [((part, model), F32, "h"), ((part, model), BF16, "h")]
+        [((part, model), F32, "v"), ((part, model), BF16, "v")]
         + [((part, width), BF16, "v")] * n_tp,
         (),
         16,
@@ -923,7 +923,7 @@
     return call(
         "early_grads",
         early_kernel,
-        kinds((mixed, gate_grad, cotangent, h_two, in_t, w_down), "h") + [(h_pair, "v")],
+        kinds((mixed, gate_grad, cotangent, h_two, in_t, w_down, h_pair), "v"),
         [((3 * units, model // 2), F32, "v"), ((3 * units, model // 2), BF16, "v")],
         [
             pltpu.VMEM((2 * units, half), F32),
@@ -1104,8 +1104,8 @@
     return call(
         "down",
         down_kernel,
-        [(mixed, "h"), (w_both, "v"), (middle, "h")],
-        [((part, model), F32, "h")] + [((part, model), BF16, "h")] * (n_tp // 2 - 1),
+        kinds((mixed, w_both, middle), "v"),
+        [((part, model), F32, "v")] + [((part, model), BF16, "v")] * (n_tp // 2 - 1),
         [pltpu.VMEM((rows, model), F32)],
         16,
         after,
@@ -1177,7 +1177,7 @@
     split = (count + 1) // 2
     (state,) = attention_forward(0, False, *docs, queries, q_pair, blocks[:split])
     state_own, state_pair = attention_forward(
-        split, True, *docs, queries, q_pair, blocks[split:], state, kinds(got[1:], "v")
+        split, True, *docs, queries, q_pair, blocks[split:], state
     )
     out_b, totals, out_mine, out_other = join(state_own, over_cores(state_pair))
     outs = everywhere([out_other if k % 2 else out_mine for k in range(n_tp)])
@@ -1192,12 +1192,13 @@
     arrived = [own] + [over_tp(others[n], 2 * n + 2) for n in range(n_tp // 2 - 1)]
     own, *others = down(n_tp, mixed, staged[4], middle, ())
     middle_grad, branch_grad, *pieces = branch(
-        n_tp, middle_part, cotangent, gain_two, staged[2], arrived, [(own, "h")]
+        n_tp, middle_part, cotangent, gain_two, staged[2], arrived, [(own, "v")]
     )
     early, early_send = early_grads(
-        mixed, gate_grad, cotangent, h_two, in_t, w_down, over_tp(h_two, 1), [(branch_grad, "h")]
-    )
-    out_grad = lay_turned(everywhere(pieces), [(early, "v")])
+        mixed, gate_grad, cotangent, h_two, in_t, w_down, over_tp(h_two, 1), [(branch_grad, "v")]
+    )
+    early_back = over_cores(early_send)
+    out_grad = lay_turned(everywhere(pieces), ())
     grad_pair = over_cores(out_grad)
     branches = by_steps(branch_grad)
 
@@ -1206,12 +1207,14 @@
     total = total_of(
         [own] + [over_tp(others[n], 2 * n + 2) for n in range(n_tp // 2 - 1)],
         BF16,
-        "h",
+        "v",
         [(dq, "v")],
     )
     totals_all = by_steps(total)
 
-    dkv, dq_own, dq_pair = attention_backward(0, True, *docs, held, blocks[:1], dq)
+    dkv, dq_own, dq_pair = attention_backward(
+        0, True, *docs, held, blocks[:1], dq, ()
+    )
     dkvs = [dkv] + [over_chips(terms[j - 1], j) for j in range(1, count)]
 
     proj_grad, *parts = unproject(
@@ -1228,7 +1231,7 @@
     )
     layer_out = stack_parts(totals_all)
     keep, send = late_grads(proj_grad, h_one, out_b, branches, [(totals_all[n_tp // 2], "v")])
-    own, *others = spread(count, (keep, over_cores(send)), (early, over_cores(early_send)))
+    own, *others = spread(count, (keep, over_cores(send)), (early, early_back))
     summed = total_of(everywhere(parts), F32, flops=2_000_000_000)
     chip_sum = total_of(
         [own] + came(count, lambda k: over_chips(others[k - 1], k)), F32, "v", ()

time: 174 us -> 166 us (0.954); the launches traced: 174 us -> 168 us
  starting transfers between devices: 49.3 us -> 61.7 us
  Pallas kernels: 58.1 us -> 47.5 us
  waiting for transfers between devices: 64.3 us -> 57.3 us
    ppermute x46, starting transfers between devices: 49.3 us -> 61.7 us  [swap(): return lax.ppermute(x, axis, [(i, i ^ hop) for i in range(count)])]
    pallas_call x26, Pallas kernels: 58.1 us -> 47.5 us  [call(): pl.pallas_call(run, out_shape=tuple((shaped(shape, dtype) if kind == 'v'...]
    ppermute x46, waiting for transfers between devices: 64.3 us -> 57.3 us  [swap(): return lax.ppermute(x, axis, [(i, i ^ hop) for i in range(count)])]
  transfers between devices with their start and end apart: 46 -> 46, of which waited for: 17 -> 18; matrix products, arithmetic and copies ran while one was open for 0% -> 0% of each run, Pallas kernels for 27% -> 22%
where the time goes in v11:
time: 166 us; the launch traced here: 168 us
  starting transfers between devices  61.7 us (37%)
  waiting for transfers between devices  57.3 us (35%)
  Pallas kernels  47.5 us (29%)
    ppermute x46, starting transfers between devices, swap(): return lax.ppermute(x, axis, [(i, i ^ hop) for i in range(count)])  61.7 us
    ppermute x46, waiting for transfers between devices, swap(): return lax.ppermute(x, axis, [(i, i ^ hop) for i in range(count)])  57.3 us
    pallas_call x26, Pallas kernels, call(): pl.pallas_call(run, out_shape=tuple((shaped(shape, dtype) if kind == 'v'...  47.5 us
  transfers between devices with their start and end apart: 46, of which 18 were waited for; matrix products, arithmetic and copies ran while one was open for 0% of the time, Pallas kernels for 22%

profile of v11, /device:TPU:0, one launch (start us, length us, event | category | flops | bytes accessed | tf_op | source)
XLA Modules:
  0.0 167.8 jit_solution(14086140570425269445)
XLA Ops:
  1.9 3.1 %collective-permute-start = (bf16[528,768]{1,0:T(8,128)(2,1)S(1)}, bf16[528,768]{1,0:T(8,128)(2,1)S(1)}, u32[]{:S(2)}, u32[]{:S(2)}) collective-permute-start(bf16[528,768]{1,0:T(8,128)(2,1)S(1)} %get-tuple-element.70), channel_id=1, source_target_pairs={{0,1},{1,0},{2,3},{3,2},{4,5},{5,4},{6,7},{7,6},{8,9},{9,8},{10,11... | collective-permute-start | bytes 2433032 | tf_op jit(solution)/shard_map/ppermute | solution.py:142
  5.0 3.7 %project.1 = (bf16[192,448]{1,0:T(8,128)(2,1)S(1)}, bf16[384,448]{1,0:T(8,128)(2,1)S(1)}, bf16[448,768]{1,0:T(8,128)(2,1)S(1)}, f32[32,448]{1,0:T(8,128)S(1)}, f32[32,448]{1,0:T(8,128)S(1)}) custom-call(s32[4]{0:T(128)} %refs_0_.13, s32[8]{0:T(128)} %refs_1_.16, bf16[448,768]{1,0:T(8,128)(2,1)} %refs_0_.15, bf16[576,768]{1,0:T(8,128)(2,1)} %bitcast.15, ...), custom_call_target="tpu_custom_call" | custom-call | tf_op jit(solution)/shard_map/project/pallas_call | solution.py:121
  13.7 2.6 %collective-permute-start.1 = (bf16[96,768]{1,0:T(8,128)(2,1)S(1)}, bf16[96,768]{1,0:T(8,128)(2,1)S(1)}, u32[]{:S(2)}, u32[]{:S(2)}) collective-permute-start(bf16[96,768]{1,0:T(8,128)(2,1)S(1)} %get-tuple-element.71), channel_id=1, source_target_pairs={{0,2},{1,3},{2,0},{3,1},{4,6},{5,7},{6,4},{7,5},{8,10},{9,11},{10,... | collective-permute-start | bytes 442376 | tf_op jit(solution)/shard_map/ppermute | solution.py:142
  16.3 4.5 %collective-permute-done.6.refs_5_.refs_10_ = bf16[384,448]{1,0:T(8,128)(2,1)S(1)} collective-permute-done((bf16[384,448]{1,0:T(8,128)(2,1)S(1)}, bf16[384,448]{1,0:T(8,128)(2,1)S(1)}, u32[]{:S(2)}, u32[]{:S(2)}) %collective-permute-start.6) | collective-permute-done | bytes 344096 | tf_op jit(solution)/shard_map/ppermute | solution.py:142
  20.8 2.5 %collective-permute-start.2 = (bf16[96,768]{1,0:T(8,128)(2,1)S(1)}, bf16[96,768]{1,0:T(8,128)(2,1)S(1)}, u32[]{:S(2)}, u32[]{:S(2)}) collective-permute-start(bf16[96,768]{1,0:T(8,128)(2,1)S(1)} %get-tuple-element.71), channel_id=1, source_target_pairs={{0,3},{1,2},{2,1},{3,0},{4,7},{5,6},{6,5},{7,4},{8,11},{9,10},{10,... | collective-permute-start | bytes 442376 | tf_op jit(solution)/shard_map/ppermute | solution.py:142
  23.3 4.2 %attention_forward.2.refs_6_ = f32[6,80,448]{2,1,0:T(8,128)S(1)} custom-call(s32[4]{0:T(128)} %refs_0_.13, s32[8]{0:T(128)} %refs_1_.16, bf16[192,448]{1,0:T(8,128)(2,1)S(1)} %get-tuple-element.72.refs_2_, bf16[192,448]{1,0:T(8,128)(2,1)S(1)} %collective-permute-done.3.refs_3_, bf16[384,448]{1,0:T(8,128)(2,1)S(1)} %get-tuple-element.73.refs_4_.refs_10_, ...), custom_call_target="tpu_custom_call" | custom-call | tf_op jit(solution)/shard_map/attention_forward/pallas_call | solution.py:121
  29.0 4.2 %attention_forward.3 = (f32[3,80,448]{2,1,0:T(8,128)S(1)}, f32[3,80,448]{2,1,0:T(8,128)S(1)}) custom-call(s32[4]{0:T(128)} %refs_0_.13, s32[8]{0:T(128)} %refs_1_.16, bf16[192,448]{1,0:T(8,128)(2,1)S(1)} %get-tuple-element.72.refs_2_, bf16[192,448]{1,0:T(8,128)(2,1)S(1)} %collective-permute-done.3.refs_3_, ...), custom_call_target="tpu_custom_call" | custom-call | tf_op jit(solution)/shard_map/attention_forward/pallas_call | solution.py:121
  33.9 2.9 %collective-permute-done.8.refs_1_ = f32[3,80,448]{2,1,0:T(8,128)S(1)} collective-permute-done((f32[3,80,448]{2,1,0:T(8,128)S(1)}, f32[3,80,448]{2,1,0:T(8,128)S(1)}, u32[]{:S(2)}, u32[]{:S(2)}) %collective-permute-start.8) | collective-permute-done | bytes 430112 | tf_op jit(solution)/shard_map/ppermute | solution.py:142
  37.3 2.7 %collective-permute-start.10 = (bf16[192,224]{1,0:T(8,128)(2,1)S(1)}, bf16[192,224]{1,0:T(8,128)(2,1)S(1)}, u32[]{:S(2)}, u32[]{:S(2)}) collective-permute-start(bf16[192,224]{1,0:T(8,128)(2,1)S(1)} %get-tuple-element.81.refs_6_), channel_id=1, source_target_pairs={{0,2},{1,3},{2,0},{3,1},{4,6},{5,7},{6,4},{7,5},{8,10},{9,11},{10,... | collective-permute-start | bytes 258056 | tf_op jit(solution)/shard_map/ppermute | solution.py:142
  41.7 3.2 %stage.1 = (bf16[224,768]{1,0:T(8,128)(2,1)S(1)}, bf16[224,768]{1,0:T(8,128)(2,1)S(1)}, bf16[768,768]{1,0:T(8,128)(2,1)S(1)}, bf16[1152,768]{1,0:T(8,128)(2,1)S(1)}, bf16[576,768]{1,0:T(8,128)(2,1)S(1)}) custom-call(bf16[448,768]{1,0:T(8,128)(2,1)} %refs_0_.15, bf16[448,768]{1,0:T(8,128)(2,1)} %refs_2_.7, bf16[576,768]{1,0:T(8,128)(2,1)} %bitcast.13, ...), custom_call_target="tpu_custom_call" | custom-call | tf_op jit(solution)/shard_map/stage/pallas_call | solution.py:121
  44.9 2.4 %collective-permute-done.10.refs_8_ = bf16[192,224]{1,0:T(8,128)(2,1)S(1)} collective-permute-done((bf16[192,224]{1,0:T(8,128)(2,1)S(1)}, bf16[192,224]{1,0:T(8,128)(2,1)S(1)}, u32[]{:S(2)}, u32[]{:S(2)}) %collective-permute-start.10) | collective-permute-done | bytes 86048 | tf_op jit(solution)/shard_map/ppermute | solution.py:142
  48.6 4.7 %feed.1 = (f32[224,768]{1,0:T(8,128)S(1)}, f32[112,768]{1,0:T(8,128)S(1)}, bf16[224,768]{1,0:T(8,128)(2,1)S(1)}, bf16[576,224]{1,0:T(8,128)(2,1)S(1)}, bf16[1152...) custom-call(bf16[224,768]{1,0:T(8,128)(2,1)S(1)} %get-tuple-element.75.refs_, ...), custom_call_target="tpu_custom_call" | custom-call | tf_op jit(solution)/shard_map/feed/pallas_call | solution.py:121
  53.3 2.5 %collective-permute-start.13 = (bf16[112,768]{1,0:T(8,128)(2,1)S(1)}, bf16[112,768]{1,0:T(8,128)(2,1)S(1)}, u32[]{:S(2)}, u32[]{:S(2)}) collective-permute-start(bf16[112,768]{1,0:T(8,128)(2,1)S(1)} %get-tuple-element.89), channel_id=1, source_target_pairs={{0,2},{1,3},{2,0},{3,1},{4,6},{5,7},{6,4},{7,5},{8,10},{9,11},{10,... | collective-permute-start | bytes 516104 | tf_op jit(solution)/shard_map/ppermute | solution.py:142
  56.4 7.5 %collective-permute-done.13.refs_5_ = bf16[112,768]{1,0:T(8,128)(2,1)S(1)} collective-permute-done((bf16[112,768]{1,0:T(8,128)(2,1)S(1)}, bf16[112,768]{1,0:T(8,128)(2,1)S(1)}, u32[]{:S(2)}, u32[]{:S(2)}) %collective-permute-start.13) | collective-permute-done | bytes 172064 | tf_op jit(solution)/shard_map/ppermute | solution.py:142
  67.6 2.4 %collective-permute-start.16 = (bf16[112,192]{1,0:T(8,128)(2,1)S(1)}, bf16[112,192]{1,0:T(8,128)(2,1)S(1)}, u32[]{:S(2)}, u32[]{:S(2)}) collective-permute-start(bf16[112,192]{1,0:T(8,128)(2,1)S(1)} %get-tuple-element.93), channel_id=1, source_target_pairs={{0,1},{1,0},{2,3},{3,2},{4,5},{5,4},{6,7},{7,6},{8,9},{9,8},{10,11... | collective-permute-start | bytes 129032 | tf_op jit(solution)/shard_map/ppermute | solution.py:142
  76.1 7.3 %attention_backward.2 = (bf16[384,448]{1,0:T(8,128)(2,1)S(1)}, bf16[384,448]{1,0:T(8,128)(2,1)S(1)}, bf16[384,448]{1,0:T(8,128)(2,1)S(1)}, f32[6,64,448]{2,1,0:T(8,128)S(1)}) custom-call(s32[4]{0:T(128)} %refs_0_.13, s32[8]{0:T(128)} %refs_1_.16, bf16[192,448]{1,0:T(8,128)(2,1)S(1)} %get-tuple-element.72.refs_2_, ...), custom_call_target="tpu_custom_call" | custom-call | tf_op jit(solution)/shard_map/attention_backward/pallas_call | solution.py:121
  83.4 4.3 %collective-permute-start.24 = (bf16[384,448]{1,0:T(8,128)(2,1)S(1)}, bf16[384,448]{1,0:T(8,128)(2,1)S(1)}, u32[]{:S(2)}, u32[]{:S(2)}) collective-permute-start(bf16[384,448]{1,0:T(8,128)(2,1)S(1)} %get-tuple-element.104), channel_id=1, source_target_pairs={{0,8},{4,12},{8,0},{12,4},{16,24},{20,28},{24,16},{28,20},{1,9},{5... | collective-permute-start | bytes 1032200 | tf_op jit(solution)/shard_map/ppermute | solution.py:142
  87.6 2.5 %collective-permute-start.25 = (bf16[384,448]{1,0:T(8,128)(2,1)S(1)}, bf16[384,448]{1,0:T(8,128)(2,1)S(1)}, u32[]{:S(2)}, u32[]{:S(2)}) collective-permute-start(bf16[384,448]{1,0:T(8,128)(2,1)S(1)} %get-tuple-element.105), channel_id=1, source_target_pairs={{0,16},{4,20},{8,24},{12,28},{16,0},{20,4},{24,8},{28,12},{1,17},{... | collective-permute-start | bytes 1032200 | tf_op jit(solution)/shard_map/ppermute | solution.py:142
  90.2 3.4 %attention_backward.3 = (f32[384,448]{1,0:T(8,128)S(1)}, f32[192,448]{1,0:T(8,128)S(1)}, bf16[192,448]{1,0:T(8,128)(2,1)S(1)}) custom-call(s32[4]{0:T(128)} %refs_0_.13, s32[8]{0:T(128)} %refs_1_.16, bf16[192,448]{1,0:T(8,128)(2,1)S(1)} %get-tuple-element.72.refs_2_, bf16[192,448]{1,0:T(8,128)(2,1)S(1)} %collective-permute-done.3.refs_3_, ...), custom_call_target="tpu_custom_call" | custom-call | tf_op jit(solution)/shard_map/attention_backward/pallas_call | solution.py:121
  94.7 7.3 %collective-permute-done.30.refs_5_ = bf16[112,768]{1,0:T(8,128)(2,1)S(1)} collective-permute-done((bf16[112,768]{1,0:T(8,128)(2,1)S(1)}, bf16[112,768]{1,0:T(8,128)(2,1)S(1)}, u32[]{:S(2)}, u32[]{:S(2)}) %collective-permute-start.30) | collective-permute-done | bytes 172064 | tf_op jit(solution)/shard_map/ppermute | solution.py:142
  106.7 2.5 %unproject.1 = (bf16[576,448]{1,0:T(8,128)(2,1)S(1)}, f32[128,768]{1,0:T(8,128)S(1)}, bf16[128,768]{1,0:T(8,128)(2,1)S(1)}, bf16[128,768]{1,0:T(8,128)(2,1)S(1)}, bf16[128,768]{1,0:T(8,128)(2,1)S(1)}) custom-call(bf16[448,768]{1,0:T(8,128)(2,1)S(1)} %copy-done, bf16[576,768]{1,0:T(8,128)(2,1)S(1)} %bitcast.16, f32[32,448]{1,0:T(8,128)S(1)} %get-tuple-element.98.refs_2_, ...), custom_call_target="tpu_custom_call" | custom-call | tf_op jit(solution)/shard_map/unproject/pallas_call | solution.py:121
  109.2 3.0 %collective-permute-done.32.refs_6_ = bf16[112,768]{1,0:T(8,128)(2,1)S(1)} collective-permute-done((bf16[112,768]{1,0:T(8,128)(2,1)S(1)}, bf16[112,768]{1,0:T(8,128)(2,1)S(1)}, u32[]{:S(2)}, u32[]{:S(2)}) %collective-permute-start.32) | collective-permute-done | bytes 172064 | tf_op jit(solution)/shard_map/ppermute | solution.py:142
  120.0 3.5 %collective-permute-start.39 = (bf16[408,384]{1,0:T(8,128)(2,1)S(1)}, bf16[408,384]{1,0:T(8,128)(2,1)S(1)}, u32[]{:S(2)}, u32[]{:S(2)}) collective-permute-start(bf16[408,384]{1,0:T(8,128)(2,1)S(1)} %get-tuple-element.123), channel_id=1, source_target_pairs={{0,24},{4,28},{8,16},{12,20},{16,8},{20,12},{24,0},{28,4},{1,25},{... | collective-permute-start | bytes 940040 | tf_op jit(solution)/shard_map/ppermute | solution.py:142
  124.8 3.2 %collective-permute-start.41 = (bf16[408,384]{1,0:T(8,128)(2,1)S(1)}, bf16[408,384]{1,0:T(8,128)(2,1)S(1)}, u32[]{:S(2)}, u32[]{:S(2)}) collective-permute-start(bf16[408,384]{1,0:T(8,128)(2,1)S(1)} %get-tuple-element.125), channel_id=1, source_target_pairs={{0,8},{4,12},{8,0},{12,4},{16,24},{20,28},{24,16},{28,20},{1,9},{5... | collective-permute-start | bytes 940040 | tf_op jit(solution)/shard_map/ppermute | solution.py:142
  128.1 7.1 %collective-permute-done.28.refs_2_ = bf16[128,768]{1,0:T(8,128)(2,1)S(1)} collective-permute-done((bf16[128,768]{1,0:T(8,128)(2,1)S(1)}, bf16[128,768]{1,0:T(8,128)(2,1)S(1)}, u32[]{:S(2)}, u32[]{:S(2)}) %collective-permute-start.28) | collective-permute-done | bytes 196640 | tf_op jit(solution)/shard_map/ppermute | solution.py:142
  140.6 2.4 %collective-permute-start.38 = (bf16[112,768]{1,0:T(8,128)(2,1)S(1)}, bf16[112,768]{1,0:T(8,128)(2,1)S(1)}, u32[]{:S(2)}, u32[]{:S(2)}) collective-permute-start(bf16[112,768]{1,0:T(8,128)(2,1)S(1)} %get-tuple-element.121.refs_0_), channel_id=1, source_target_pairs={{0,1},{1,0},{2,3},{3,2},{4,5},{5,4},{6,7},{7,6},{8,9},{9,8},{10,11... | collective-permute-start | bytes 516104 | tf_op jit(solution)/shard_map/ppermute | solution.py:142
  143.3 2.7 %collective-permute-start.42 = (bf16[424,384]{1,0:T(8,128)(2,1)S(1)}, bf16[424,384]{1,0:T(8,128)(2,1)S(1)}, u32[]{:S(2)}, u32[]{:S(2)}) collective-permute-start(bf16[424,384]{1,0:T(8,128)(2,1)S(1)} %sum_piece.1.refs_0_), channel_id=1, source_target_pairs={{0,24},{4,28},{8,16},{12,20},{16,8},{20,12},{24,0},{28,4},{1,25},{... | collective-permute-start | bytes 976904 | tf_op jit(solution)/shard_map/ppermute | solution.py:142
  145.9 5.2 %collective-permute-done.21.refs_1_ = bf16[112,768]{1,0:T(8,128)(2,1)S(1)} collective-permute-done((bf16[112,768]{1,0:T(8,128)(2,1)S(1)}, bf16[112,768]{1,0:T(8,128)(2,1)S(1)}, u32[]{:S(2)}, u32[]{:S(2)}) %collective-permute-start.21) | collective-permute-done | bytes 172064 | tf_op jit(solution)/shard_map/ppermute | solution.py:142
  151.2 3.3 %collective-permute-start.43 = (bf16[424,384]{1,0:T(8,128)(2,1)S(1)}, bf16[424,384]{1,0:T(8,128)(2,1)S(1)}, u32[]{:S(2)}, u32[]{:S(2)}) collective-permute-start(bf16[424,384]{1,0:T(8,128)(2,1)S(1)} %sum_piece.1.refs_0_), channel_id=1, source_target_pairs={{0,16},{4,20},{8,24},{12,28},{16,0},{20,4},{24,8},{28,12},{1,17},{... | collective-permute-start | bytes 976904 | tf_op jit(solution)/shard_map/ppermute | solution.py:142
  156.8 3.1 %collective-permute-done.43.refs_2_ = bf16[424,384]{1,0:T(8,128)(2,1)S(1)} collective-permute-done((bf16[424,384]{1,0:T(8,128)(2,1)S(1)}, bf16[424,384]{1,0:T(8,128)(2,1)S(1)}, u32[]{:S(2)}, u32[]{:S(2)}) %collective-permute-start.43) | collective-permute-done | bytes 325664 | tf_op jit(solution)/shard_map/ppermute | solution.py:142
  161.9 3.0 %collective-permute-done.45.refs_1_ = bf16[1648,384]{1,0:T(8,128)(2,1)S(1)} collective-permute-done((bf16[1648,384]{1,0:T(8,128)(2,1)S(1)}, bf16[1648,384]{1,0:T(8,128)(2,1)S(1)}, u32[]{:S(2)}, u32[]{:S(2)}) %collective-permute-start.45) | collective-permute-done | bytes 1265696 | tf_op jit(solution)/shard_map/ppermute | solution.py:142
  164.9 2.7 %finish.1 = (f32[576,768]{1,0:T(8,128)}, f32[192,768]{1,0:T(8,128)}, f32[288,768]{1,0:T(8,128)}, f32[576,768]{1,0:T(8,128)}, f32[768]{0:T(1024)}, /*index=5*/f32[768]{0:T(1024)}) custom-call(bf16[1648,384]{1,0:T(8,128)(2,1)S(1)} %collect.1.refs_0_, bf16[1648,384]{1,0:T(8,128)(2,1)S(1)} %collective-permute-done.45.refs_1_), custom_call_target="tpu_custom_call" | custom-call | tf_op jit(solution)/shard_map/finish/pallas_call | solution.py:121
  (96 shorter events, 47.1 us)
Async XLA Ops:
  1.9 31.3 %collective-permute-start = (bf16[528,768]{1,0:T(8,128)(2,1)S(1)}, bf16[528,768]{1,0:T(8,128)(2,1)S(1)}, u32[]{:S(2)}, u32[]{:S(2)}) collective-permute-start(bf16[528,768]{1,0:T(8,128)(2,1)S(1)} %get-tuple-element.70), channel_id=1, source_target_pairs={{0,1},{1,0},{2,3},{3,2},{4,5},{5,4},{6,7},{7,6},{8,9},{9,8},{10,11... | collective-permute-start | bytes 2433032 | tf_op jit(solution)/shard_map/ppermute | solution.py:142
  8.7 12.1 %collective-permute-start.6 = (bf16[384,448]{1,0:T(8,128)(2,1)S(1)}, bf16[384,448]{1,0:T(8,128)(2,1)S(1)}, u32[]{:S(2)}, u32[]{:S(2)}) collective-permute-start(bf16[384,448]{1,0:T(8,128)(2,1)S(1)} %get-tuple-element.73.refs_4_.refs_10_), channel_id=1, source_target_pairs={{0,8},{4,12},{8,0},{12,4},{16,24},{20,28},{24,16},{28,20},{1,9},{5... | collective-permute-start | bytes 1032200 | tf_op jit(solution)/shard_map/ppermute | solution.py:142
  10.3 18.7 %collective-permute-start.4 = (bf16[384,448]{1,0:T(8,128)(2,1)S(1)}, bf16[384,448]{1,0:T(8,128)(2,1)S(1)}, u32[]{:S(2)}, u32[]{:S(2)}) collective-permute-start(bf16[384,448]{1,0:T(8,128)(2,1)S(1)} %get-tuple-element.73.refs_4_.refs_10_), channel_id=1, source_target_pairs={{0,16},{4,20},{8,24},{12,28},{16,0},{20,4},{24,8},{28,12},{1,17},{... | collective-permute-start | bytes 1032200 | tf_op jit(solution)/shard_map/ppermute | solution.py:142
  11.8 17.2 %collective-permute-start.5 = (bf16[384,448]{1,0:T(8,128)(2,1)S(1)}, bf16[384,448]{1,0:T(8,128)(2,1)S(1)}, u32[]{:S(2)}, u32[]{:S(2)}) collective-permute-start(bf16[384,448]{1,0:T(8,128)(2,1)S(1)} %get-tuple-element.73.refs_4_.refs_10_), channel_id=1, source_target_pairs={{0,24},{4,28},{8,16},{12,20},{16,8},{20,12},{24,0},{28,4},{1,25},{... | collective-permute-start | bytes 1032200 | tf_op jit(solution)/shard_map/ppermute | solution.py:142
  13.7 19.5 %collective-permute-start.1 = (bf16[96,768]{1,0:T(8,128)(2,1)S(1)}, bf16[96,768]{1,0:T(8,128)(2,1)S(1)}, u32[]{:S(2)}, u32[]{:S(2)}) collective-permute-start(bf16[96,768]{1,0:T(8,128)(2,1)S(1)} %get-tuple-element.71), channel_id=1, source_target_pairs={{0,2},{1,3},{2,0},{3,1},{4,6},{5,7},{6,4},{7,5},{8,10},{9,11},{10,... | collective-permute-start | bytes 442376 | tf_op jit(solution)/shard_map/ppermute | solution.py:142
  20.8 12.4 %collective-permute-start.2 = (bf16[96,768]{1,0:T(8,128)(2,1)S(1)}, bf16[96,768]{1,0:T(8,128)(2,1)S(1)}, u32[]{:S(2)}, u32[]{:S(2)}) collective-permute-start(bf16[96,768]{1,0:T(8,128)(2,1)S(1)} %get-tuple-element.71), channel_id=1, source_target_pairs={{0,3},{1,2},{2,1},{3,0},{4,7},{5,6},{6,5},{7,4},{8,11},{9,10},{10,... | collective-permute-start | bytes 442376 | tf_op jit(solution)/shard_map/ppermute | solution.py:142
  33.3 8.4 %collective-permute-start.7 = (bf16[720,768]{1,0:T(8,128)(2,1)S(1)}, bf16[720,768]{1,0:T(8,128)(2,1)S(1)}, u32[]{:S(2)}, u32[]{:S(2)}) collective-permute-start(bf16[720,768]{1,0:T(8,128)(2,1)S(1)} %pile.1.refs_5_), channel_id=1, source_target_pairs={{0,4},{4,0},{8,12},{12,8},{16,20},{20,16},{24,28},{28,24},{1,5},{5... | collective-permute-start | bytes 3317768 | tf_op jit(solution)/shard_map/ppermute | solution.py:142
  37.3 10.0 %collective-permute-start.10 = (bf16[192,224]{1,0:T(8,128)(2,1)S(1)}, bf16[192,224]{1,0:T(8,128)(2,1)S(1)}, u32[]{:S(2)}, u32[]{:S(2)}) collective-permute-start(bf16[192,224]{1,0:T(8,128)(2,1)S(1)} %get-tuple-element.81.refs_6_), channel_id=1, source_target_pairs={{0,2},{1,3},{2,0},{3,1},{4,6},{5,7},{6,4},{7,5},{8,10},{9,11},{10,... | collective-permute-start | bytes 258056 | tf_op jit(solution)/shard_map/ppermute | solution.py:142
  39.9 8.7 %collective-permute-start.11 = (bf16[192,224]{1,0:T(8,128)(2,1)S(1)}, bf16[192,224]{1,0:T(8,128)(2,1)S(1)}, u32[]{:S(2)}, u32[]{:S(2)}) collective-permute-start(bf16[192,224]{1,0:T(8,128)(2,1)S(1)} %get-tuple-element.82), channel_id=1, source_target_pairs={{0,1},{1,0},{2,3},{3,2},{4,5},{5,4},{6,7},{7,6},{8,9},{9,8},{10,11... | collective-permute-start | bytes 258056 | tf_op jit(solution)/shard_map/ppermute | solution.py:142
  53.3 10.5 %collective-permute-start.13 = (bf16[112,768]{1,0:T(8,128)(2,1)S(1)}, bf16[112,768]{1,0:T(8,128)(2,1)S(1)}, u32[]{:S(2)}, u32[]{:S(2)}) collective-permute-start(bf16[112,768]{1,0:T(8,128)(2,1)S(1)} %get-tuple-element.89), channel_id=1, source_target_pairs={{0,2},{1,3},{2,0},{3,1},{4,6},{5,7},{6,4},{7,5},{8,10},{9,11},{10,... | collective-permute-start | bytes 516104 | tf_op jit(solution)/shard_map/ppermute | solution.py:142
  70.0 24.7 %collective-permute-start.34 = (bf16[224,768]{1,0:T(8,128)(2,1)S(1)}, bf16[224,768]{1,0:T(8,128)(2,1)S(1)}, u32[]{:S(2)}, u32[]{:S(2)}) collective-permute-start(bf16[224,768]{1,0:T(8,128)(2,1)S(1)} %get-tuple-element.117.refs_3_), channel_id=1, source_target_pairs={{0,1},{1,0},{2,3},{3,2},{4,5},{5,4},{6,7},{7,6},{8,9},{9,8},{10,11... | collective-permute-start | bytes 1032200 | tf_op jit(solution)/shard_map/ppermute | solution.py:142
  74.1 19.5 %collective-permute-start.12 = (bf16[112,768]{1,0:T(8,128)(2,1)S(1)}, bf16[112,768]{1,0:T(8,128)(2,1)S(1)}, u32[]{:S(2)}, u32[]{:S(2)}) collective-permute-start(bf16[112,768]{1,0:T(8,128)(2,1)S(1)} %get-tuple-element.86), channel_id=1, source_target_pairs={{0,2},{1,3},{2,0},{3,1},{4,6},{5,7},{6,4},{7,5},{8,10},{9,11},{10,... | collective-permute-start | bytes 516104 | tf_op jit(solution)/shard_map/ppermute | solution.py:142
  83.4 20.6 %collective-permute-start.24 = (bf16[384,448]{1,0:T(8,128)(2,1)S(1)}, bf16[384,448]{1,0:T(8,128)(2,1)S(1)}, u32[]{:S(2)}, u32[]{:S(2)}) collective-permute-start(bf16[384,448]{1,0:T(8,128)(2,1)S(1)} %get-tuple-element.104), channel_id=1, source_target_pairs={{0,8},{4,12},{8,0},{12,4},{16,24},{20,28},{24,16},{28,20},{1,9},{5... | collective-permute-start | bytes 1032200 | tf_op jit(solution)/shard_map/ppermute | solution.py:142
  87.6 19.0 %collective-permute-start.25 = (bf16[384,448]{1,0:T(8,128)(2,1)S(1)}, bf16[384,448]{1,0:T(8,128)(2,1)S(1)}, u32[]{:S(2)}, u32[]{:S(2)}) collective-permute-start(bf16[384,448]{1,0:T(8,128)(2,1)S(1)} %get-tuple-element.105), channel_id=1, source_target_pairs={{0,16},{4,20},{8,24},{12,28},{16,0},{20,4},{24,8},{28,12},{1,17},{... | collective-permute-start | bytes 1032200 | tf_op jit(solution)/shard_map/ppermute | solution.py:142
  90.2 16.5 %collective-permute-start.26 = (bf16[384,448]{1,0:T(8,128)(2,1)S(1)}, bf16[384,448]{1,0:T(8,128)(2,1)S(1)}, u32[]{:S(2)}, u32[]{:S(2)}) collective-permute-start(bf16[384,448]{1,0:T(8,128)(2,1)S(1)} %get-tuple-element.106), channel_id=1, source_target_pairs={{0,24},{4,28},{8,16},{12,20},{16,8},{20,12},{24,0},{28,4},{1,25},{... | collective-permute-start | bytes 1032200 | tf_op jit(solution)/shard_map/ppermute | solution.py:142
  93.6 8.4 %collective-permute-start.30 = (bf16[112,768]{1,0:T(8,128)(2,1)S(1)}, bf16[112,768]{1,0:T(8,128)(2,1)S(1)}, u32[]{:S(2)}, u32[]{:S(2)}) collective-permute-start(bf16[112,768]{1,0:T(8,128)(2,1)S(1)} %get-tuple-element.113.refs_3_.refs_7_), channel_id=1, source_target_pairs={{0,2},{1,3},{2,0},{3,1},{4,6},{5,7},{6,4},{7,5},{8,10},{9,11},{10,... | collective-permute-start | bytes 516104 | tf_op jit(solution)/shard_map/ppermute | solution.py:142
  102.0 10.2 %collective-permute-start.32 = (bf16[112,768]{1,0:T(8,128)(2,1)S(1)}, bf16[112,768]{1,0:T(8,128)(2,1)S(1)}, u32[]{:S(2)}, u32[]{:S(2)}) collective-permute-start(bf16[112,768]{1,0:T(8,128)(2,1)S(1)} %get-tuple-element.113.refs_3_.refs_7_), channel_id=1, source_target_pairs={{0,1},{1,0},{2,3},{3,2},{4,5},{5,4},{6,7},{7,6},{8,9},{9,8},{10,11... | collective-permute-start | bytes 516104 | tf_op jit(solution)/shard_map/ppermute | solution.py:142
  102.0 12.0 %collective-permute-start.31 = (bf16[112,768]{1,0:T(8,128)(2,1)S(1)}, bf16[112,768]{1,0:T(8,128)(2,1)S(1)}, u32[]{:S(2)}, u32[]{:S(2)}) collective-permute-start(bf16[112,768]{1,0:T(8,128)(2,1)S(1)} %collective-permute-done.30.refs_5_), channel_id=1, source_target_pairs={{0,1},{1,0},{2,3},{3,2},{4,5},{5,4},{6,7},{7,6},{8,9},{9,8},{10,11... | collective-permute-start | bytes 516104 | tf_op jit(solution)/shard_map/ppermute | solution.py:142
  104.0 10.0 %collective-permute-start.20 = (bf16[112,768]{1,0:T(8,128)(2,1)S(1)}, bf16[112,768]{1,0:T(8,128)(2,1)S(1)}, u32[]{:S(2)}, u32[]{:S(2)}) collective-permute-start(bf16[112,768]{1,0:T(8,128)(2,1)S(1)} %total_of.3.refs_0_.refs_11_), channel_id=1, source_target_pairs={{0,2},{1,3},{2,0},{3,1},{4,6},{5,7},{6,4},{7,5},{8,10},{9,11},{10,... | collective-permute-start | bytes 516104 | tf_op jit(solution)/shard_map/ppermute | solution.py:142
  106.6 12.9 %collective-permute-start.35 = (bf16[864,384]{1,0:T(8,128)(2,1)S(1)}, bf16[864,384]{1,0:T(8,128)(2,1)S(1)}, u32[]{:S(2)}, u32[]{:S(2)}) collective-permute-start(bf16[864,384]{1,0:T(8,128)(2,1)S(1)} %get-tuple-element.119), channel_id=1, source_target_pairs={{0,4},{4,0},{8,12},{12,8},{16,20},{20,16},{24,28},{28,24},{1,5},{5... | collective-permute-start | bytes 1990664 | tf_op jit(solution)/shard_map/ppermute | solution.py:142
  115.1 9.7 %collective-permute-start.27 = (bf16[128,768]{1,0:T(8,128)(2,1)S(1)}, bf16[128,768]{1,0:T(8,128)(2,1)S(1)}, u32[]{:S(2)}, u32[]{:S(2)}) collective-permute-start(bf16[128,768]{1,0:T(8,128)(2,1)S(1)} %get-tuple-element.108), channel_id=1, source_target_pairs={{0,3},{1,2},{2,1},{3,0},{4,7},{5,6},{6,5},{7,4},{8,11},{9,10},{10,... | collective-permute-start | bytes 589832 | tf_op jit(solution)/shard_map/ppermute | solution.py:142
  117.0 18.1 %collective-permute-start.28 = (bf16[128,768]{1,0:T(8,128)(2,1)S(1)}, bf16[128,768]{1,0:T(8,128)(2,1)S(1)}, u32[]{:S(2)}, u32[]{:S(2)}) collective-permute-start(bf16[128,768]{1,0:T(8,128)(2,1)S(1)} %get-tuple-element.109), channel_id=1, source_target_pairs={{0,2},{1,3},{2,0},{3,1},{4,6},{5,7},{6,4},{7,5},{8,10},{9,11},{10,... | collective-permute-start | bytes 589832 | tf_op jit(solution)/shard_map/ppermute | solution.py:142
  117.3 17.9 %collective-permute-start.29 = (bf16[128,768]{1,0:T(8,128)(2,1)S(1)}, bf16[128,768]{1,0:T(8,128)(2,1)S(1)}, u32[]{:S(2)}, u32[]{:S(2)}) collective-permute-start(bf16[128,768]{1,0:T(8,128)(2,1)S(1)} %get-tuple-element.110), channel_id=1, source_target_pairs={{0,1},{1,0},{2,3},{3,2},{4,5},{5,4},{6,7},{7,6},{8,9},{9,8},{10,11... | collective-permute-start | bytes 589832 | tf_op jit(solution)/shard_map/ppermute | solution.py:142
  120.0 18.5 %collective-permute-start.39 = (bf16[408,384]{1,0:T(8,128)(2,1)S(1)}, bf16[408,384]{1,0:T(8,128)(2,1)S(1)}, u32[]{:S(2)}, u32[]{:S(2)}) collective-permute-start(bf16[408,384]{1,0:T(8,128)(2,1)S(1)} %get-tuple-element.123), channel_id=1, source_target_pairs={{0,24},{4,28},{8,16},{12,20},{16,8},{20,12},{24,0},{28,4},{1,25},{... | collective-permute-start | bytes 940040 | tf_op jit(solution)/shard_map/ppermute | solution.py:142
  123.6 17.1 %collective-permute-start.40 = (bf16[408,384]{1,0:T(8,128)(2,1)S(1)}, bf16[408,384]{1,0:T(8,128)(2,1)S(1)}, u32[]{:S(2)}, u32[]{:S(2)}) collective-permute-start(bf16[408,384]{1,0:T(8,128)(2,1)S(1)} %get-tuple-element.124), channel_id=1, source_target_pairs={{0,16},{4,20},{8,24},{12,28},{16,0},{20,4},{24,8},{28,12},{1,17},{... | collective-permute-start | bytes 940040 | tf_op jit(solution)/shard_map/ppermute | solution.py:142
  124.8 15.8 %collective-permute-start.41 = (bf16[408,384]{1,0:T(8,128)(2,1)S(1)}, bf16[408,384]{1,0:T(8,128)(2,1)S(1)}, u32[]{:S(2)}, u32[]{:S(2)}) collective-permute-start(bf16[408,384]{1,0:T(8,128)(2,1)S(1)} %get-tuple-element.125), channel_id=1, source_target_pairs={{0,8},{4,12},{8,0},{12,4},{16,24},{20,28},{24,16},{28,20},{1,9},{5... | collective-permute-start | bytes 940040 | tf_op jit(solution)/shard_map/ppermute | solution.py:142
  135.2 16.0 %collective-permute-start.21 = (bf16[112,768]{1,0:T(8,128)(2,1)S(1)}, bf16[112,768]{1,0:T(8,128)(2,1)S(1)}, u32[]{:S(2)}, u32[]{:S(2)}) collective-permute-start(bf16[112,768]{1,0:T(8,128)(2,1)S(1)} %collective-permute-done.20.refs_2_.refs_7_), channel_id=1, source_target_pairs={{0,1},{1,0},{2,3},{3,2},{4,5},{5,4},{6,7},{7,6},{8,9},{9,8},{10,11... | collective-permute-start | bytes 516104 | tf_op jit(solution)/shard_map/ppermute | solution.py:142
  138.6 15.9 %collective-permute-start.36 = (bf16[112,768]{1,0:T(8,128)(2,1)S(1)}, bf16[112,768]{1,0:T(8,128)(2,1)S(1)}, u32[]{:S(2)}, u32[]{:S(2)}) collective-permute-start(bf16[112,768]{1,0:T(8,128)(2,1)S(1)} %get-tuple-element.121.refs_0_), channel_id=1, source_target_pairs={{0,3},{1,2},{2,1},{3,0},{4,7},{5,6},{6,5},{7,4},{8,11},{9,10},{10,... | collective-permute-start | bytes 516104 | tf_op jit(solution)/shard_map/ppermute | solution.py:142
  140.6 14.8 %collective-permute-start.37 = (bf16[112,768]{1,0:T(8,128)(2,1)S(1)}, bf16[112,768]{1,0:T(8,128)(2,1)S(1)}, u32[]{:S(2)}, u32[]{:S(2)}) collective-permute-start(bf16[112,768]{1,0:T(8,128)(2,1)S(1)} %get-tuple-element.121.refs_0_), channel_id=1, source_target_pairs={{0,2},{1,3},{2,0},{3,1},{4,6},{5,7},{6,4},{7,5},{8,10},{9,11},{10,... | collective-permute-start | bytes 516104 | tf_op jit(solution)/shard_map/ppermute | solution.py:142
  140.6 15.2 %collective-permute-start.38 = (bf16[112,768]{1,0:T(8,128)(2,1)S(1)}, bf16[112,768]{1,0:T(8,128)(2,1)S(1)}, u32[]{:S(2)}, u32[]{:S(2)}) collective-permute-start(bf16[112,768]{1,0:T(8,128)(2,1)S(1)} %get-tuple-element.121.refs_0_), channel_id=1, source_target_pairs={{0,1},{1,0},{2,3},{3,2},{4,5},{5,4},{6,7},{7,6},{8,9},{9,8},{10,11... | collective-permute-start | bytes 516104 | tf_op jit(solution)/shard_map/ppermute | solution.py:142
  143.3 13.5 %collective-permute-start.42 = (bf16[424,384]{1,0:T(8,128)(2,1)S(1)}, bf16[424,384]{1,0:T(8,128)(2,1)S(1)}, u32[]{:S(2)}, u32[]{:S(2)}) collective-permute-start(bf16[424,384]{1,0:T(8,128)(2,1)S(1)} %sum_piece.1.refs_0_), channel_id=1, source_target_pairs={{0,24},{4,28},{8,16},{12,20},{16,8},{20,12},{24,0},{28,4},{1,25},{... | collective-permute-start | bytes 976904 | tf_op jit(solution)/shard_map/ppermute | solution.py:142
  151.2 8.7 %collective-permute-start.43 = (bf16[424,384]{1,0:T(8,128)(2,1)S(1)}, bf16[424,384]{1,0:T(8,128)(2,1)S(1)}, u32[]{:S(2)}, u32[]{:S(2)}) collective-permute-start(bf16[424,384]{1,0:T(8,128)(2,1)S(1)} %sum_piece.1.refs_0_), channel_id=1, source_target_pairs={{0,16},{4,20},{8,24},{12,28},{16,0},{20,4},{24,8},{28,12},{1,17},{... | collective-permute-start | bytes 976904 | tf_op jit(solution)/shard_map/ppermute | solution.py:142
  (19 other events, 112.9 us)

commit v12 on v11

--- a/solution.py
+++ b/solution.py
@@ -58,7 +58,7 @@
     return array if kind in ("v", "free") else pltpu.with_memory_space_constraint(array, pltpu.HBM)
 
 
-def call(name, kernel, ins, outs, scratch=(), mib=16, after=(), lazy=False, flops=0):
+def call(name, kernel, ins, outs, scratch=(), mib=16, after=(), lazy=False, flops=0, alias=None):
     fetched = [i for i, given in enumerate(ins) if given[1] not in ("v", "raw", "free")]
     left = [i for i, out in enumerate(outs) if out[2] == "h"]
 
@@ -131,6 +131,7 @@
         + [pltpu.VMEM(outs[i][0], outs[i][1]) for i in left]
         + [pltpu.SemaphoreType.DMA((max(count, 1),))],
         name=name,
+        input_output_aliases=alias or {},
         cost_estimate=pl.CostEstimate(flops=flops, bytes_accessed=0, transcendentals=0)
         if flops
         else None,
@@ -1055,34 +1056,56 @@
     return out
 
 
-def finish_kernel(sizes, need, give, own_ref, pair_ref, *refs):
-    out_refs, gain_refs = refs[: len(sizes)], refs[len(sizes) :]
+def write_half(sizes, source, side, out_refs, held, sems):
+    half = source.shape[1]
+    columns = pl.ds(pl.multiple_of(side * half, half), half)
+    at = 0
+    copies = []
+    for n, (ref, size) in enumerate(zip(out_refs, sizes)):
+        rows = pl.ds(at, size)
+        held[rows, :] = source[rows, :].astype(F32)
+        copies.append(pltpu.make_async_copy(held.at[rows], ref.at[:, columns], sems.at[n]))
+        copies[-1].start()
+        at += size
+    return copies
+
+
+def own_kernel(sizes, own_ref, *refs):
+    out_refs, held, sems = refs[:-2], refs[-2], refs[-1]
+    core = lax.axis_index("seq") % 2
+    for copy in write_half(sizes, own_ref, core, out_refs, held, sems):
+        copy.wait()
+
+
+def pair_kernel(sizes, own_ref, pair_ref, *refs):
+    refs = refs[len(sizes) :]
+    out_refs, gain_refs = refs[: len(sizes)], refs[len(sizes) : len(sizes) + 2]
+    held, sems = refs[-2:]
+    core = lax.axis_index("seq") % 2
+    copies = write_half(sizes, pair_ref, 1 - core, out_refs, held, sems)
     half = own_ref.shape[1]
-    core = lax.axis_index("seq") % 2
-    at = 0
-    for n, (out_ref, size) in enumerate(zip(out_refs, sizes)):
-        for ref, side in ((own_ref, core), (pair_ref, 1 - core)):
-            columns = pl.ds(pl.multiple_of(side * half, half), half)
-            out_ref[:, columns] = ref[at : at + size, :].astype(F32)
-        give(n)
-        at += size
     first = own_ref.shape[0] - 16
     gains = own_ref[first:, :].astype(F32) + pair_ref[first:, :].astype(F32)
     for at, ref in zip((0, 2), gain_refs):
         ref[pl.ds(0, half)] = gains[at]
         ref[pl.ds(half, half)] = gains[at + 1]
-
-
-def finish(own, pair, sizes):
-    model = 2 * own.shape[1]
-    return call(
-        "finish",
-        functools.partial(finish_kernel, sizes),
-        [(own, "v"), (pair, "v")],
-        [((size, model), F32, "h") for size in sizes] + [((model,), F32, "h")] * 2,
-        (),
-        24,
-        lazy=True,
+    for copy in copies:
+        copy.wait()
+
+
+def finish(own, over_cores, sizes):
+    half = own.shape[1]
+    shapes = [((size, 2 * half), F32, "raw") for size in sizes]
+    scratch = [pltpu.VMEM((sum(sizes), half), F32), pltpu.SemaphoreType.DMA((len(sizes),))]
+    pair = over_cores(own)
+    begun = call("own_half", functools.partial(own_kernel, sizes), [(own, "v")], shapes, scratch)
+    return call(
+        "pair_half",
+        functools.partial(pair_kernel, sizes),
+        [(own, "v"), (pair, "v")] + kinds(begun, "raw"),
+        shapes + [((2 * half,), F32, "h")] * 2,
+        scratch,
+        alias={2 + n: n for n in range(len(sizes))},
     )
 
 
@@ -1190,7 +1213,7 @@
         gain_two, staged, outs
     )
     arrived = [own] + [over_tp(others[n], 2 * n + 2) for n in range(n_tp // 2 - 1)]
-    own, *others = down(n_tp, mixed, staged[4], middle, ())
+    own, *others = down(n_tp, mixed, staged[4], middle, [(out_pair, "v"), (totals_pair, "v")])
     middle_grad, branch_grad, *pieces = branch(
         n_tp, middle_part, cotangent, gain_two, staged[2], arrived, [(own, "v")]
     )
@@ -1208,7 +1231,7 @@
         [own] + [over_tp(others[n], 2 * n + 2) for n in range(n_tp // 2 - 1)],
         BF16,
         "v",
-        [(dq, "v")],
+        [(dq, "v"), (branches[2], "v")],
     )
     totals_all = by_steps(total)
 
@@ -1244,7 +1267,7 @@
         [piece] + came(count, lambda k: over_chips(piece, k)), [(input_grad, "h"), (layer_out, "h")]
     )
     grad_qkv, grad_out, grad_down, grad_in, grad_one, grad_two = finish(
-        collected, over_cores(collected), (3 * width, width, units, 2 * units)
+        collected, over_cores, (3 * width, width, units, 2 * units)
     )
 
     back = lambda x, n: x.reshape(-1, n, model).transpose(2, 0, 1)

time: 166 us -> 167 us (level)
  starting transfers between devices: 61.7 us -> 49.2 us
  Pallas kernels: 47.5 us -> 54.8 us
  waiting for transfers between devices: 57.3 us -> 62.6 us
    ppermute x46, starting transfers between devices: 61.7 us -> 49.2 us  [swap(): return lax.ppermute(x, axis, [(i, i ^ hop) for i in range(count)])]
    pallas_call x26 -> x27, Pallas kernels: 47.5 us -> 54.8 us  [call(): pl.pallas_call(run, out_shape=tuple((shaped(shape, dtype) if kind == 'v'...]
    ppermute x46, waiting for transfers between devices: 57.3 us -> 62.6 us  [swap(): return lax.ppermute(x, axis, [(i, i ^ hop) for i in range(count)])]
  transfers between devices with their start and end apart: 46 -> 46, of which waited for: 18 -> 21; matrix products, arithmetic and copies ran while one was open for 0% -> 0% of each run, Pallas kernels for 22% -> 29%
where the time goes in v12:
time: 167 us; the launch traced here: 168 us
  waiting for transfers between devices  62.6 us (37%)
  Pallas kernels  54.8 us (33%)
  starting transfers between devices  49.2 us (29%)
    ppermute x46, waiting for transfers between devices, swap(): return lax.ppermute(x, axis, [(i, i ^ hop) for i in range(count)])  62.6 us
    pallas_call x27, Pallas kernels, call(): pl.pallas_call(run, out_shape=tuple((shaped(shape, dtype) if kind == 'v'...  54.8 us
    ppermute x46, starting transfers between devices, swap(): return lax.ppermute(x, axis, [(i, i ^ hop) for i in range(count)])  49.2 us
  transfers between devices with their start and end apart: 46, of which 21 were waited for; matrix products, arithmetic and copies ran while one was open for 0% of the time, Pallas kernels for 29%

profile of v12, /device:TPU:0, one launch (start us, length us, event | category | flops | bytes accessed | tf_op | source)
XLA Modules:
  0.0 168.0 jit_solution(5842082881967906340)
XLA Ops:
  1.9 3.1 %collective-permute-start = (bf16[528,768]{1,0:T(8,128)(2,1)S(1)}, bf16[528,768]{1,0:T(8,128)(2,1)S(1)}, u32[]{:S(2)}, u32[]{:S(2)}) collective-permute-start(bf16[528,768]{1,0:T(8,128)(2,1)S(1)} %get-tuple-element.74), channel_id=1, source_target_pairs={{0,1},{1,0},{2,3},{3,2},{4,5},{5,4},{6,7},{7,6},{8,9},{9,8},{10,11... | collective-permute-start | bytes 2433032 | tf_op jit(solution)/shard_map/ppermute | solution.py:143
  5.0 3.7 %project.1 = (bf16[192,448]{1,0:T(8,128)(2,1)S(1)}, bf16[384,448]{1,0:T(8,128)(2,1)S(1)}, bf16[448,768]{1,0:T(8,128)(2,1)S(1)}, f32[32,448]{1,0:T(8,128)S(1)}, f32[32,448]{1,0:T(8,128)S(1)}) custom-call(s32[4]{0:T(128)} %refs_0_.13, s32[8]{0:T(128)} %refs_1_.16, bf16[448,768]{1,0:T(8,128)(2,1)} %refs_0_.15, bf16[576,768]{1,0:T(8,128)(2,1)} %bitcast.15, ...), custom_call_target="tpu_custom_call" | custom-call | tf_op jit(solution)/shard_map/project/pallas_call | solution.py:121
  13.7 2.5 %collective-permute-start.2 = (bf16[96,768]{1,0:T(8,128)(2,1)S(1)}, bf16[96,768]{1,0:T(8,128)(2,1)S(1)}, u32[]{:S(2)}, u32[]{:S(2)}) collective-permute-start(bf16[96,768]{1,0:T(8,128)(2,1)S(1)} %get-tuple-element.75), channel_id=1, source_target_pairs={{0,3},{1,2},{2,1},{3,0},{4,7},{5,6},{6,5},{7,4},{8,11},{9,10},{10,... | collective-permute-start | bytes 442376 | tf_op jit(solution)/shard_map/ppermute | solution.py:143
  16.2 4.6 %collective-permute-done.6.refs_5_.refs_10_ = bf16[384,448]{1,0:T(8,128)(2,1)S(1)} collective-permute-done((bf16[384,448]{1,0:T(8,128)(2,1)S(1)}, bf16[384,448]{1,0:T(8,128)(2,1)S(1)}, u32[]{:S(2)}, u32[]{:S(2)}) %collective-permute-start.6) | collective-permute-done | bytes 344096 | tf_op jit(solution)/shard_map/ppermute | solution.py:143
  20.8 2.6 %collective-permute-start.1 = (bf16[96,768]{1,0:T(8,128)(2,1)S(1)}, bf16[96,768]{1,0:T(8,128)(2,1)S(1)}, u32[]{:S(2)}, u32[]{:S(2)}) collective-permute-start(bf16[96,768]{1,0:T(8,128)(2,1)S(1)} %get-tuple-element.75), channel_id=1, source_target_pairs={{0,2},{1,3},{2,0},{3,1},{4,6},{5,7},{6,4},{7,5},{8,10},{9,11},{10,... | collective-permute-start | bytes 442376 | tf_op jit(solution)/shard_map/ppermute | solution.py:143
  23.4 7.1 %attention_forward.2.refs_6_ = f32[6,80,448]{2,1,0:T(8,128)S(1)} custom-call(s32[4]{0:T(128)} %refs_0_.13, s32[8]{0:T(128)} %refs_1_.16, bf16[192,448]{1,0:T(8,128)(2,1)S(1)} %get-tuple-element.76.refs_2_, bf16[192,448]{1,0:T(8,128)(2,1)S(1)} %collective-permute-done.3.refs_3_, bf16[384,448]{1,0:T(8,128)(2,1)S(1)} %get-tuple-element.77.refs_4_.refs_10_, ...), custom_call_target="tpu_custom_call" | custom-call | tf_op jit(solution)/shard_map/attention_forward/pallas_call | solution.py:121
  30.6 4.2 %attention_forward.3 = (f32[3,80,448]{2,1,0:T(8,128)S(1)}, f32[3,80,448]{2,1,0:T(8,128)S(1)}) custom-call(s32[4]{0:T(128)} %refs_0_.13, s32[8]{0:T(128)} %refs_1_.16, bf16[192,448]{1,0:T(8,128)(2,1)S(1)} %get-tuple-element.76.refs_2_, bf16[192,448]{1,0:T(8,128)(2,1)S(1)} %collective-permute-done.3.refs_3_, ...), custom_call_target="tpu_custom_call" | custom-call | tf_op jit(solution)/shard_map/attention_forward/pallas_call | solution.py:121
  35.5 2.9 %collective-permute-done.8.refs_1_ = f32[3,80,448]{2,1,0:T(8,128)S(1)} collective-permute-done((f32[3,80,448]{2,1,0:T(8,128)S(1)}, f32[3,80,448]{2,1,0:T(8,128)S(1)}, u32[]{:S(2)}, u32[]{:S(2)}) %collective-permute-start.8) | collective-permute-done | bytes 430112 | tf_op jit(solution)/shard_map/ppermute | solution.py:143
  38.8 2.3 %collective-permute-start.10 = (bf16[192,224]{1,0:T(8,128)(2,1)S(1)}, bf16[192,224]{1,0:T(8,128)(2,1)S(1)}, u32[]{:S(2)}, u32[]{:S(2)}) collective-permute-start(bf16[192,224]{1,0:T(8,128)(2,1)S(1)} %get-tuple-element.85.refs_6_), channel_id=1, source_target_pairs={{0,2},{1,3},{2,0},{3,1},{4,6},{5,7},{6,4},{7,5},{8,10},{9,11},{10,... | collective-permute-start | bytes 258056 | tf_op jit(solution)/shard_map/ppermute | solution.py:143
  43.3 3.2 %stage.1 = (bf16[224,768]{1,0:T(8,128)(2,1)S(1)}, bf16[224,768]{1,0:T(8,128)(2,1)S(1)}, bf16[768,768]{1,0:T(8,128)(2,1)S(1)}, bf16[1152,768]{1,0:T(8,128)(2,1)S(1)}, bf16[576,768]{1,0:T(8,128)(2,1)S(1)}) custom-call(bf16[448,768]{1,0:T(8,128)(2,1)} %refs_0_.15, bf16[448,768]{1,0:T(8,128)(2,1)} %refs_2_.7, bf16[576,768]{1,0:T(8,128)(2,1)} %bitcast.13, ...), custom_call_target="tpu_custom_call" | custom-call | tf_op jit(solution)/shard_map/stage/pallas_call | solution.py:121
  46.5 2.4 %collective-permute-done.10.refs_8_ = bf16[192,224]{1,0:T(8,128)(2,1)S(1)} collective-permute-done((bf16[192,224]{1,0:T(8,128)(2,1)S(1)}, bf16[192,224]{1,0:T(8,128)(2,1)S(1)}, u32[]{:S(2)}, u32[]{:S(2)}) %collective-permute-start.10) | collective-permute-done | bytes 86048 | tf_op jit(solution)/shard_map/ppermute | solution.py:143
  49.8 4.8 %feed.1 = (f32[224,768]{1,0:T(8,128)S(1)}, f32[112,768]{1,0:T(8,128)S(1)}, bf16[224,768]{1,0:T(8,128)(2,1)S(1)}, bf16[576,224]{1,0:T(8,128)(2,1)S(1)}, bf16[1152...) custom-call(bf16[224,768]{1,0:T(8,128)(2,1)S(1)} %get-tuple-element.79.refs_, ...), custom_call_target="tpu_custom_call" | custom-call | tf_op jit(solution)/shard_map/feed/pallas_call | solution.py:121
  54.5 2.5 %collective-permute-start.15 = (bf16[112,768]{1,0:T(8,128)(2,1)S(1)}, bf16[112,768]{1,0:T(8,128)(2,1)S(1)}, u32[]{:S(2)}, u32[]{:S(2)}) collective-permute-start(bf16[112,768]{1,0:T(8,128)(2,1)S(1)} %get-tuple-element.95), channel_id=1, source_target_pairs={{0,2},{1,3},{2,0},{3,1},{4,6},{5,7},{6,4},{7,5},{8,10},{9,11},{10,... | collective-permute-start | bytes 516104 | tf_op jit(solution)/shard_map/ppermute | solution.py:143
  58.8 6.1 %collective-permute-done.15.refs_5_ = bf16[112,768]{1,0:T(8,128)(2,1)S(1)} collective-permute-done((bf16[112,768]{1,0:T(8,128)(2,1)S(1)}, bf16[112,768]{1,0:T(8,128)(2,1)S(1)}, u32[]{:S(2)}, u32[]{:S(2)}) %collective-permute-start.15) | collective-permute-done | bytes 172064 | tf_op jit(solution)/shard_map/ppermute | solution.py:143
  66.6 2.2 %collective-permute-start.16 = (bf16[112,192]{1,0:T(8,128)(2,1)S(1)}, bf16[112,192]{1,0:T(8,128)(2,1)S(1)}, u32[]{:S(2)}, u32[]{:S(2)}) collective-permute-start(bf16[112,192]{1,0:T(8,128)(2,1)S(1)} %get-tuple-element.97), channel_id=1, source_target_pairs={{0,3},{1,2},{2,1},{3,0},{4,7},{5,6},{6,5},{7,4},{8,11},{9,10},{10,... | collective-permute-start | bytes 129032 | tf_op jit(solution)/shard_map/ppermute | solution.py:143
  68.8 2.2 %collective-permute-start.18 = (bf16[112,192]{1,0:T(8,128)(2,1)S(1)}, bf16[112,192]{1,0:T(8,128)(2,1)S(1)}, u32[]{:S(2)}, u32[]{:S(2)}) collective-permute-start(bf16[112,192]{1,0:T(8,128)(2,1)S(1)} %get-tuple-element.99), channel_id=1, source_target_pairs={{0,1},{1,0},{2,3},{3,2},{4,5},{5,4},{6,7},{7,6},{8,9},{9,8},{10,11... | collective-permute-start | bytes 129032 | tf_op jit(solution)/shard_map/ppermute | solution.py:143
  71.0 2.1 %collective-permute-done.16.refs_1_ = bf16[112,192]{1,0:T(8,128)(2,1)S(1)} collective-permute-done((bf16[112,192]{1,0:T(8,128)(2,1)S(1)}, bf16[112,192]{1,0:T(8,128)(2,1)S(1)}, u32[]{:S(2)}, u32[]{:S(2)}) %collective-permute-start.16) | collective-permute-done | bytes 43040 | tf_op jit(solution)/shard_map/ppermute | solution.py:143
  78.5 9.0 %attention_backward.2 = (bf16[384,448]{1,0:T(8,128)(2,1)S(1)}, bf16[384,448]{1,0:T(8,128)(2,1)S(1)}, bf16[384,448]{1,0:T(8,128)(2,1)S(1)}, f32[6,64,448]{2,1,0:T(8,128)S(1)}) custom-call(s32[4]{0:T(128)} %refs_0_.13, s32[8]{0:T(128)} %refs_1_.16, bf16[192,448]{1,0:T(8,128)(2,1)S(1)} %get-tuple-element.76.refs_2_, ...), custom_call_target="tpu_custom_call" | custom-call | tf_op jit(solution)/shard_map/attention_backward/pallas_call | solution.py:121
  87.5 3.2 %collective-permute-start.25 = (bf16[384,448]{1,0:T(8,128)(2,1)S(1)}, bf16[384,448]{1,0:T(8,128)(2,1)S(1)}, u32[]{:S(2)}, u32[]{:S(2)}) collective-permute-start(bf16[384,448]{1,0:T(8,128)(2,1)S(1)} %get-tuple-element.109), channel_id=1, source_target_pairs={{0,8},{4,12},{8,0},{12,4},{16,24},{20,28},{24,16},{28,20},{1,9},{5... | collective-permute-start | bytes 1032200 | tf_op jit(solution)/shard_map/ppermute | solution.py:143
  92.3 5.0 %attention_backward.3 = (f32[384,448]{1,0:T(8,128)S(1)}, f32[192,448]{1,0:T(8,128)S(1)}, bf16[192,448]{1,0:T(8,128)(2,1)S(1)}) custom-call(s32[4]{0:T(128)} %refs_0_.13, s32[8]{0:T(128)} %refs_1_.16, bf16[192,448]{1,0:T(8,128)(2,1)S(1)} %get-tuple-element.76.refs_2_, bf16[192,448]{1,0:T(8,128)(2,1)S(1)} %collective-permute-done.3.refs_3_, ...), custom_call_target="tpu_custom_call" | custom-call | tf_op jit(solution)/shard_map/attention_backward/pallas_call | solution.py:121
  102.2 2.1 %early_grads.1 = (f32[864,384]{1,0:T(8,128)S(1)}, bf16[864,384]{1,0:T(8,128)(2,1)S(1)}) custom-call(bf16[576,224]{1,0:T(8,128)(2,1)S(1)} %get-tuple-element.87.refs_0_, bf16[1152,224]{1,0:T(8,128)(2,1)S(1)} %get-tuple-element.120.refs_1_, bf16[448,768]{1,0:T(8,128)(2,1)S(1)} %copy-done.2, bf16[224,768]{1,0:T(8,128)(2,1)S(1)} %get-tuple-element.121.refs_3_, ...), custom_call_target="tpu_custom_call" | custom-call | tf_op jit(solution)/shard_map/early_grads/pallas_call | solution.py:121
  104.3 3.4 %collective-permute-done.26.refs_9_ = bf16[384,448]{1,0:T(8,128)(2,1)S(1)} collective-permute-done((bf16[384,448]{1,0:T(8,128)(2,1)S(1)}, bf16[384,448]{1,0:T(8,128)(2,1)S(1)}, u32[]{:S(2)}, u32[]{:S(2)}) %collective-permute-start.26) | collective-permute-done | bytes 344096 | tf_op jit(solution)/shard_map/ppermute | solution.py:143
  107.7 2.5 %unproject.1 = (bf16[576,448]{1,0:T(8,128)(2,1)S(1)}, f32[128,768]{1,0:T(8,128)S(1)}, bf16[128,768]{1,0:T(8,128)(2,1)S(1)}, bf16[128,768]{1,0:T(8,128)(2,1)S(1)}, bf16[128,768]{1,0:T(8,128)(2,1)S(1)}) custom-call(bf16[448,768]{1,0:T(8,128)(2,1)S(1)} %copy-done, bf16[576,768]{1,0:T(8,128)(2,1)S(1)} %bitcast.16, f32[32,448]{1,0:T(8,128)S(1)} %get-tuple-element.103.refs_2_, ...), custom_call_target="tpu_custom_call" | custom-call | tf_op jit(solution)/shard_map/unproject/pallas_call | solution.py:121
  112.8 2.0 %collective-permute-start.28 = (bf16[128,768]{1,0:T(8,128)(2,1)S(1)}, bf16[128,768]{1,0:T(8,128)(2,1)S(1)}, u32[]{:S(2)}, u32[]{:S(2)}) collective-permute-start(bf16[128,768]{1,0:T(8,128)(2,1)S(1)} %get-tuple-element.113), channel_id=1, source_target_pairs={{0,3},{1,2},{2,1},{3,0},{4,7},{5,6},{6,5},{7,4},{8,11},{9,10},{10,... | collective-permute-start | bytes 589832 | tf_op jit(solution)/shard_map/ppermute | solution.py:143
  119.4 3.1 %collective-permute-done.28.refs_1_ = bf16[128,768]{1,0:T(8,128)(2,1)S(1)} collective-permute-done((bf16[128,768]{1,0:T(8,128)(2,1)S(1)}, bf16[128,768]{1,0:T(8,128)(2,1)S(1)}, u32[]{:S(2)}, u32[]{:S(2)}) %collective-permute-start.28) | collective-permute-done | bytes 196640 | tf_op jit(solution)/shard_map/ppermute | solution.py:143
  122.6 10.9 %collective-permute-done.29.refs_2_ = bf16[128,768]{1,0:T(8,128)(2,1)S(1)} collective-permute-done((bf16[128,768]{1,0:T(8,128)(2,1)S(1)}, bf16[128,768]{1,0:T(8,128)(2,1)S(1)}, u32[]{:S(2)}, u32[]{:S(2)}) %collective-permute-start.29) | collective-permute-done | bytes 196640 | tf_op jit(solution)/shard_map/ppermute | solution.py:143
  137.1 2.6 %collective-permute-start.37 = (bf16[112,768]{1,0:T(8,128)(2,1)S(1)}, bf16[112,768]{1,0:T(8,128)(2,1)S(1)}, u32[]{:S(2)}, u32[]{:S(2)}) collective-permute-start(bf16[112,768]{1,0:T(8,128)(2,1)S(1)} %get-tuple-element.125.refs_0_), channel_id=1, source_target_pairs={{0,2},{1,3},{2,0},{3,1},{4,6},{5,7},{6,4},{7,5},{8,10},{9,11},{10,... | collective-permute-start | bytes 516104 | tf_op jit(solution)/shard_map/ppermute | solution.py:143
  144.0 4.3 %collective-permute-done.22.refs_1_ = bf16[112,768]{1,0:T(8,128)(2,1)S(1)} collective-permute-done((bf16[112,768]{1,0:T(8,128)(2,1)S(1)}, bf16[112,768]{1,0:T(8,128)(2,1)S(1)}, u32[]{:S(2)}, u32[]{:S(2)}) %collective-permute-start.22) | collective-permute-done | bytes 172064 | tf_op jit(solution)/shard_map/ppermute | solution.py:143
  148.2 3.0 %collective-permute-done.38.refs_3_ = bf16[112,768]{1,0:T(8,128)(2,1)S(1)} collective-permute-done((bf16[112,768]{1,0:T(8,128)(2,1)S(1)}, bf16[112,768]{1,0:T(8,128)(2,1)S(1)}, u32[]{:S(2)}, u32[]{:S(2)}) %collective-permute-start.38) | collective-permute-done | bytes 172064 | tf_op jit(solution)/shard_map/ppermute | solution.py:143
  152.2 2.4 %collective-permute-done.36.refs_1_ = bf16[112,768]{1,0:T(8,128)(2,1)S(1)} collective-permute-done((bf16[112,768]{1,0:T(8,128)(2,1)S(1)}, bf16[112,768]{1,0:T(8,128)(2,1)S(1)}, u32[]{:S(2)}, u32[]{:S(2)}) %collective-permute-start.36) | collective-permute-done | bytes 172064 | tf_op jit(solution)/shard_map/ppermute | solution.py:143
  155.6 6.7 %collective-permute-done.43.refs_2_ = bf16[424,384]{1,0:T(8,128)(2,1)S(1)} collective-permute-done((bf16[424,384]{1,0:T(8,128)(2,1)S(1)}, bf16[424,384]{1,0:T(8,128)(2,1)S(1)}, u32[]{:S(2)}, u32[]{:S(2)}) %collective-permute-start.43) | collective-permute-done | bytes 325664 | tf_op jit(solution)/shard_map/ppermute | solution.py:143
  165.7 2.1 %pair_half.1 = (f32[576,768]{1,0:T(8,128)}, f32[192,768]{1,0:T(8,128)}, f32[288,768]{1,0:T(8,128)}, f32[576,768]{1,0:T(8,128)}, f32[768]{0:T(1024)}, /*index=5*/f32[768]{0:T(1024)}) custom-call(bf16[1648,384]{1,0:T(8,128)(2,1)S(1)} %collect.1.refs_0_, ...), custom_call_target="tpu_custom_call", output_to_operand_aliasing={{0}: (2, {}), {1}: (3, {}), {2}: (4, {}), {3}: (5, {})} | custom-call | tf_op jit(solution)/shard_map/pair_half/pallas_call | solution.py:121
  (97 shorter events, 45.8 us)
Async XLA Ops:
  1.9 32.9 %collective-permute-start = (bf16[528,768]{1,0:T(8,128)(2,1)S(1)}, bf16[528,768]{1,0:T(8,128)(2,1)S(1)}, u32[]{:S(2)}, u32[]{:S(2)}) collective-permute-start(bf16[528,768]{1,0:T(8,128)(2,1)S(1)} %get-tuple-element.74), channel_id=1, source_target_pairs={{0,1},{1,0},{2,3},{3,2},{4,5},{5,4},{6,7},{7,6},{8,9},{9,8},{10,11... | collective-permute-start | bytes 2433032 | tf_op jit(solution)/shard_map/ppermute | solution.py:143
  8.7 12.1 %collective-permute-start.6 = (bf16[384,448]{1,0:T(8,128)(2,1)S(1)}, bf16[384,448]{1,0:T(8,128)(2,1)S(1)}, u32[]{:S(2)}, u32[]{:S(2)}) collective-permute-start(bf16[384,448]{1,0:T(8,128)(2,1)S(1)} %get-tuple-element.77.refs_4_.refs_10_), channel_id=1, source_target_pairs={{0,8},{4,12},{8,0},{12,4},{16,24},{20,28},{24,16},{28,20},{1,9},{5... | collective-permute-start | bytes 1032200 | tf_op jit(solution)/shard_map/ppermute | solution.py:143
  10.3 20.3 %collective-permute-start.5 = (bf16[384,448]{1,0:T(8,128)(2,1)S(1)}, bf16[384,448]{1,0:T(8,128)(2,1)S(1)}, u32[]{:S(2)}, u32[]{:S(2)}) collective-permute-start(bf16[384,448]{1,0:T(8,128)(2,1)S(1)} %get-tuple-element.77.refs_4_.refs_10_), channel_id=1, source_target_pairs={{0,24},{4,28},{8,16},{12,20},{16,8},{20,12},{24,0},{28,4},{1,25},{... | collective-permute-start | bytes 1032200 | tf_op jit(solution)/shard_map/ppermute | solution.py:143
  11.8 18.8 %collective-permute-start.4 = (bf16[384,448]{1,0:T(8,128)(2,1)S(1)}, bf16[384,448]{1,0:T(8,128)(2,1)S(1)}, u32[]{:S(2)}, u32[]{:S(2)}) collective-permute-start(bf16[384,448]{1,0:T(8,128)(2,1)S(1)} %get-tuple-element.77.refs_4_.refs_10_), channel_id=1, source_target_pairs={{0,16},{4,20},{8,24},{12,28},{16,0},{20,4},{24,8},{28,12},{1,17},{... | collective-permute-start | bytes 1032200 | tf_op jit(solution)/shard_map/ppermute | solution.py:143
  13.7 21.1 %collective-permute-start.2 = (bf16[96,768]{1,0:T(8,128)(2,1)S(1)}, bf16[96,768]{1,0:T(8,128)(2,1)S(1)}, u32[]{:S(2)}, u32[]{:S(2)}) collective-permute-start(bf16[96,768]{1,0:T(8,128)(2,1)S(1)} %get-tuple-element.75), channel_id=1, source_target_pairs={{0,3},{1,2},{2,1},{3,0},{4,7},{5,6},{6,5},{7,4},{8,11},{9,10},{10,... | collective-permute-start | bytes 442376 | tf_op jit(solution)/shard_map/ppermute | solution.py:143
  20.8 14.0 %collective-permute-start.1 = (bf16[96,768]{1,0:T(8,128)(2,1)S(1)}, bf16[96,768]{1,0:T(8,128)(2,1)S(1)}, u32[]{:S(2)}, u32[]{:S(2)}) collective-permute-start(bf16[96,768]{1,0:T(8,128)(2,1)S(1)} %get-tuple-element.75), channel_id=1, source_target_pairs={{0,2},{1,3},{2,0},{3,1},{4,6},{5,7},{6,4},{7,5},{8,10},{9,11},{10,... | collective-permute-start | bytes 442376 | tf_op jit(solution)/shard_map/ppermute | solution.py:143
  38.8 10.0 %collective-permute-start.10 = (bf16[192,224]{1,0:T(8,128)(2,1)S(1)}, bf16[192,224]{1,0:T(8,128)(2,1)S(1)}, u32[]{:S(2)}, u32[]{:S(2)}) collective-permute-start(bf16[192,224]{1,0:T(8,128)(2,1)S(1)} %get-tuple-element.85.refs_6_), channel_id=1, source_target_pairs={{0,2},{1,3},{2,0},{3,1},{4,6},{5,7},{6,4},{7,5},{8,10},{9,11},{10,... | collective-permute-start | bytes 258056 | tf_op jit(solution)/shard_map/ppermute | solution.py:143
  43.3 15.0 %collective-permute-start.12 = (bf16[192,448]{1,0:T(8,128)(2,1)S(1)}, bf16[192,448]{1,0:T(8,128)(2,1)S(1)}, u32[]{:S(2)}, u32[]{:S(2)}) collective-permute-start(bf16[192,448]{1,0:T(8,128)(2,1)S(1)} %get-tuple-element.89.refs_6_.refs_2_), channel_id=1, source_target_pairs={{0,4},{4,0},{8,12},{12,8},{16,20},{20,16},{24,28},{28,24},{1,5},{5... | collective-permute-start | bytes 516104 | tf_op jit(solution)/shard_map/ppermute | solution.py:143
  54.5 10.3 %collective-permute-start.15 = (bf16[112,768]{1,0:T(8,128)(2,1)S(1)}, bf16[112,768]{1,0:T(8,128)(2,1)S(1)}, u32[]{:S(2)}, u32[]{:S(2)}) collective-permute-start(bf16[112,768]{1,0:T(8,128)(2,1)S(1)} %get-tuple-element.95), channel_id=1, source_target_pairs={{0,2},{1,3},{2,0},{3,1},{4,6},{5,7},{6,4},{7,5},{8,10},{9,11},{10,... | collective-permute-start | bytes 516104 | tf_op jit(solution)/shard_map/ppermute | solution.py:143
  74.7 16.0 %collective-permute-start.14 = (bf16[112,768]{1,0:T(8,128)(2,1)S(1)}, bf16[112,768]{1,0:T(8,128)(2,1)S(1)}, u32[]{:S(2)}, u32[]{:S(2)}) collective-permute-start(bf16[112,768]{1,0:T(8,128)(2,1)S(1)} %get-tuple-element.92), channel_id=1, source_target_pairs={{0,2},{1,3},{2,0},{3,1},{4,6},{5,7},{6,4},{7,5},{8,10},{9,11},{10,... | collective-permute-start | bytes 516104 | tf_op jit(solution)/shard_map/ppermute | solution.py:143
  76.3 21.2 %collective-permute-start.34 = (bf16[224,768]{1,0:T(8,128)(2,1)S(1)}, bf16[224,768]{1,0:T(8,128)(2,1)S(1)}, u32[]{:S(2)}, u32[]{:S(2)}) collective-permute-start(bf16[224,768]{1,0:T(8,128)(2,1)S(1)} %get-tuple-element.121.refs_3_), channel_id=1, source_target_pairs={{0,1},{1,0},{2,3},{3,2},{4,5},{5,4},{6,7},{7,6},{8,9},{9,8},{10,11... | collective-permute-start | bytes 1032200 | tf_op jit(solution)/shard_map/ppermute | solution.py:143
  76.9 20.4 %collective-permute-start.20 = (bf16[112,768]{1,0:T(8,128)(2,1)S(1)}, bf16[112,768]{1,0:T(8,128)(2,1)S(1)}, u32[]{:S(2)}, u32[]{:S(2)}) collective-permute-start(bf16[112,768]{1,0:T(8,128)(2,1)S(1)} %get-tuple-element.101.refs_3_.refs_7_), channel_id=1, source_target_pairs={{0,2},{1,3},{2,0},{3,1},{4,6},{5,7},{6,4},{7,5},{8,10},{9,11},{10,... | collective-permute-start | bytes 516104 | tf_op jit(solution)/shard_map/ppermute | solution.py:143
  87.5 13.2 %collective-permute-start.25 = (bf16[384,448]{1,0:T(8,128)(2,1)S(1)}, bf16[384,448]{1,0:T(8,128)(2,1)S(1)}, u32[]{:S(2)}, u32[]{:S(2)}) collective-permute-start(bf16[384,448]{1,0:T(8,128)(2,1)S(1)} %get-tuple-element.109), channel_id=1, source_target_pairs={{0,8},{4,12},{8,0},{12,4},{16,24},{20,28},{24,16},{28,20},{1,9},{5... | collective-permute-start | bytes 1032200 | tf_op jit(solution)/shard_map/ppermute | solution.py:143
  90.7 17.0 %collective-permute-start.26 = (bf16[384,448]{1,0:T(8,128)(2,1)S(1)}, bf16[384,448]{1,0:T(8,128)(2,1)S(1)}, u32[]{:S(2)}, u32[]{:S(2)}) collective-permute-start(bf16[384,448]{1,0:T(8,128)(2,1)S(1)} %get-tuple-element.110), channel_id=1, source_target_pairs={{0,16},{4,20},{8,24},{12,28},{16,0},{20,4},{24,8},{28,12},{1,17},{... | collective-permute-start | bytes 1032200 | tf_op jit(solution)/shard_map/ppermute | solution.py:143
  90.7 17.0 %collective-permute-start.27 = (bf16[384,448]{1,0:T(8,128)(2,1)S(1)}, bf16[384,448]{1,0:T(8,128)(2,1)S(1)}, u32[]{:S(2)}, u32[]{:S(2)}) collective-permute-start(bf16[384,448]{1,0:T(8,128)(2,1)S(1)} %get-tuple-element.111), channel_id=1, source_target_pairs={{0,24},{4,28},{8,16},{12,20},{16,8},{20,12},{24,0},{28,4},{1,25},{... | collective-permute-start | bytes 1032200 | tf_op jit(solution)/shard_map/ppermute | solution.py:143
  97.5 12.7 %collective-permute-start.32 = (bf16[112,768]{1,0:T(8,128)(2,1)S(1)}, bf16[112,768]{1,0:T(8,128)(2,1)S(1)}, u32[]{:S(2)}, u32[]{:S(2)}) collective-permute-start(bf16[112,768]{1,0:T(8,128)(2,1)S(1)} %get-tuple-element.101.refs_3_.refs_7_), channel_id=1, source_target_pairs={{0,1},{1,0},{2,3},{3,2},{4,5},{5,4},{6,7},{7,6},{8,9},{9,8},{10,11... | collective-permute-start | bytes 516104 | tf_op jit(solution)/shard_map/ppermute | solution.py:143
  98.8 12.8 %collective-permute-start.31 = (bf16[112,768]{1,0:T(8,128)(2,1)S(1)}, bf16[112,768]{1,0:T(8,128)(2,1)S(1)}, u32[]{:S(2)}, u32[]{:S(2)}) collective-permute-start(bf16[112,768]{1,0:T(8,128)(2,1)S(1)} %collective-permute-done.20.refs_3_.refs_5_), channel_id=1, source_target_pairs={{0,1},{1,0},{2,3},{3,2},{4,5},{5,4},{6,7},{7,6},{8,9},{9,8},{10,11... | collective-permute-start | bytes 516104 | tf_op jit(solution)/shard_map/ppermute | solution.py:143
  100.7 10.9 %collective-permute-start.21 = (bf16[112,768]{1,0:T(8,128)(2,1)S(1)}, bf16[112,768]{1,0:T(8,128)(2,1)S(1)}, u32[]{:S(2)}, u32[]{:S(2)}) collective-permute-start(bf16[112,768]{1,0:T(8,128)(2,1)S(1)} %total_of.3.refs_0_.refs_11_), channel_id=1, source_target_pairs={{0,2},{1,3},{2,0},{3,1},{4,6},{5,7},{6,4},{7,5},{8,10},{9,11},{10,... | collective-permute-start | bytes 516104 | tf_op jit(solution)/shard_map/ppermute | solution.py:143
  112.8 9.7 %collective-permute-start.28 = (bf16[128,768]{1,0:T(8,128)(2,1)S(1)}, bf16[128,768]{1,0:T(8,128)(2,1)S(1)}, u32[]{:S(2)}, u32[]{:S(2)}) collective-permute-start(bf16[128,768]{1,0:T(8,128)(2,1)S(1)} %get-tuple-element.113), channel_id=1, source_target_pairs={{0,3},{1,2},{2,1},{3,0},{4,7},{5,6},{6,5},{7,4},{8,11},{9,10},{10,... | collective-permute-start | bytes 589832 | tf_op jit(solution)/shard_map/ppermute | solution.py:143
  114.8 18.8 %collective-permute-start.29 = (bf16[128,768]{1,0:T(8,128)(2,1)S(1)}, bf16[128,768]{1,0:T(8,128)(2,1)S(1)}, u32[]{:S(2)}, u32[]{:S(2)}) collective-permute-start(bf16[128,768]{1,0:T(8,128)(2,1)S(1)} %get-tuple-element.114), channel_id=1, source_target_pairs={{0,2},{1,3},{2,0},{3,1},{4,6},{5,7},{6,4},{7,5},{8,10},{9,11},{10,... | collective-permute-start | bytes 589832 | tf_op jit(solution)/shard_map/ppermute | solution.py:143
  115.7 17.9 %collective-permute-start.30 = (bf16[128,768]{1,0:T(8,128)(2,1)S(1)}, bf16[128,768]{1,0:T(8,128)(2,1)S(1)}, u32[]{:S(2)}, u32[]{:S(2)}) collective-permute-start(bf16[128,768]{1,0:T(8,128)(2,1)S(1)} %get-tuple-element.115), channel_id=1, source_target_pairs={{0,1},{1,0},{2,3},{3,2},{4,5},{5,4},{6,7},{7,6},{8,9},{9,8},{10,11... | collective-permute-start | bytes 589832 | tf_op jit(solution)/shard_map/ppermute | solution.py:143
  117.7 19.3 %collective-permute-start.39 = (bf16[408,384]{1,0:T(8,128)(2,1)S(1)}, bf16[408,384]{1,0:T(8,128)(2,1)S(1)}, u32[]{:S(2)}, u32[]{:S(2)}) collective-permute-start(bf16[408,384]{1,0:T(8,128)(2,1)S(1)} %get-tuple-element.127), channel_id=1, source_target_pairs={{0,24},{4,28},{8,16},{12,20},{16,8},{20,12},{24,0},{28,4},{1,25},{... | collective-permute-start | bytes 940040 | tf_op jit(solution)/shard_map/ppermute | solution.py:143
  117.8 19.3 %collective-permute-start.40 = (bf16[408,384]{1,0:T(8,128)(2,1)S(1)}, bf16[408,384]{1,0:T(8,128)(2,1)S(1)}, u32[]{:S(2)}, u32[]{:S(2)}) collective-permute-start(bf16[408,384]{1,0:T(8,128)(2,1)S(1)} %get-tuple-element.128), channel_id=1, source_target_pairs={{0,16},{4,20},{8,24},{12,28},{16,0},{20,4},{24,8},{28,12},{1,17},{... | collective-permute-start | bytes 940040 | tf_op jit(solution)/shard_map/ppermute | solution.py:143
  122.5 17.3 %collective-permute-start.41 = (bf16[408,384]{1,0:T(8,128)(2,1)S(1)}, bf16[408,384]{1,0:T(8,128)(2,1)S(1)}, u32[]{:S(2)}, u32[]{:S(2)}) collective-permute-start(bf16[408,384]{1,0:T(8,128)(2,1)S(1)} %get-tuple-element.129), channel_id=1, source_target_pairs={{0,8},{4,12},{8,0},{12,4},{16,24},{20,28},{24,16},{28,20},{1,9},{5... | collective-permute-start | bytes 940040 | tf_op jit(solution)/shard_map/ppermute | solution.py:143
  133.6 10.1 %collective-permute-start.23 = (bf16[112,768]{1,0:T(8,128)(2,1)S(1)}, bf16[112,768]{1,0:T(8,128)(2,1)S(1)}, u32[]{:S(2)}, u32[]{:S(2)}) collective-permute-start(bf16[112,768]{1,0:T(8,128)(2,1)S(1)} %total_of.3.refs_0_.refs_11_), channel_id=1, source_target_pairs={{0,1},{1,0},{2,3},{3,2},{4,5},{5,4},{6,7},{7,6},{8,9},{9,8},{10,11... | collective-permute-start | bytes 516104 | tf_op jit(solution)/shard_map/ppermute | solution.py:143
  133.6 14.7 %collective-permute-start.22 = (bf16[112,768]{1,0:T(8,128)(2,1)S(1)}, bf16[112,768]{1,0:T(8,128)(2,1)S(1)}, u32[]{:S(2)}, u32[]{:S(2)}) collective-permute-start(bf16[112,768]{1,0:T(8,128)(2,1)S(1)} %collective-permute-done.21.refs_2_.refs_7_), channel_id=1, source_target_pairs={{0,1},{1,0},{2,3},{3,2},{4,5},{5,4},{6,7},{7,6},{8,9},{9,8},{10,11... | collective-permute-start | bytes 516104 | tf_op jit(solution)/shard_map/ppermute | solution.py:143
  137.0 14.2 %collective-permute-start.38 = (bf16[112,768]{1,0:T(8,128)(2,1)S(1)}, bf16[112,768]{1,0:T(8,128)(2,1)S(1)}, u32[]{:S(2)}, u32[]{:S(2)}) collective-permute-start(bf16[112,768]{1,0:T(8,128)(2,1)S(1)} %get-tuple-element.125.refs_0_), channel_id=1, source_target_pairs={{0,1},{1,0},{2,3},{3,2},{4,5},{5,4},{6,7},{7,6},{8,9},{9,8},{10,11... | collective-permute-start | bytes 516104 | tf_op jit(solution)/shard_map/ppermute | solution.py:143
  137.1 15.1 %collective-permute-start.37 = (bf16[112,768]{1,0:T(8,128)(2,1)S(1)}, bf16[112,768]{1,0:T(8,128)(2,1)S(1)}, u32[]{:S(2)}, u32[]{:S(2)}) collective-permute-start(bf16[112,768]{1,0:T(8,128)(2,1)S(1)} %get-tuple-element.125.refs_0_), channel_id=1, source_target_pairs={{0,2},{1,3},{2,0},{3,1},{4,6},{5,7},{6,4},{7,5},{8,10},{9,11},{10,... | collective-permute-start | bytes 516104 | tf_op jit(solution)/shard_map/ppermute | solution.py:143
  139.7 14.9 %collective-permute-start.36 = (bf16[112,768]{1,0:T(8,128)(2,1)S(1)}, bf16[112,768]{1,0:T(8,128)(2,1)S(1)}, u32[]{:S(2)}, u32[]{:S(2)}) collective-permute-start(bf16[112,768]{1,0:T(8,128)(2,1)S(1)} %get-tuple-element.125.refs_0_), channel_id=1, source_target_pairs={{0,3},{1,2},{2,1},{3,0},{4,7},{5,6},{6,5},{7,4},{8,11},{9,10},{10,... | collective-permute-start | bytes 516104 | tf_op jit(solution)/shard_map/ppermute | solution.py:143
  143.7 11.8 %collective-permute-start.44 = (bf16[424,384]{1,0:T(8,128)(2,1)S(1)}, bf16[424,384]{1,0:T(8,128)(2,1)S(1)}, u32[]{:S(2)}, u32[]{:S(2)}) collective-permute-start(bf16[424,384]{1,0:T(8,128)(2,1)S(1)} %sum_piece.1.refs_0_), channel_id=1, source_target_pairs={{0,8},{4,12},{8,0},{12,4},{16,24},{20,28},{24,16},{28,20},{1,9},{5... | collective-permute-start | bytes 976904 | tf_op jit(solution)/shard_map/ppermute | solution.py:143
  148.2 14.0 %collective-permute-start.43 = (bf16[424,384]{1,0:T(8,128)(2,1)S(1)}, bf16[424,384]{1,0:T(8,128)(2,1)S(1)}, u32[]{:S(2)}, u32[]{:S(2)}) collective-permute-start(bf16[424,384]{1,0:T(8,128)(2,1)S(1)} %sum_piece.1.refs_0_), channel_id=1, source_target_pairs={{0,16},{4,20},{8,24},{12,28},{16,0},{20,4},{24,8},{28,12},{1,17},{... | collective-permute-start | bytes 976904 | tf_op jit(solution)/shard_map/ppermute | solution.py:143
  151.3 11.0 %collective-permute-start.42 = (bf16[424,384]{1,0:T(8,128)(2,1)S(1)}, bf16[424,384]{1,0:T(8,128)(2,1)S(1)}, u32[]{:S(2)}, u32[]{:S(2)}) collective-permute-start(bf16[424,384]{1,0:T(8,128)(2,1)S(1)} %sum_piece.1.refs_0_), channel_id=1, source_target_pairs={{0,24},{4,28},{8,16},{12,20},{16,8},{20,12},{24,0},{28,4},{1,25},{... | collective-permute-start | bytes 976904 | tf_op jit(solution)/shard_map/ppermute | solution.py:143
  (19 other events, 102.4 us)

commit v13 on v12

--- a/solution.py
+++ b/solution.py
@@ -1093,18 +1093,29 @@
         copy.wait()
 
 
-def finish(own, over_cores, sizes):
+def half_scratch(sizes, half):
+    return [pltpu.VMEM((sum(sizes), half), F32), pltpu.SemaphoreType.DMA((len(sizes),))]
+
+
+def begin(own, sizes):
     half = own.shape[1]
-    shapes = [((size, 2 * half), F32, "raw") for size in sizes]
-    scratch = [pltpu.VMEM((sum(sizes), half), F32), pltpu.SemaphoreType.DMA((len(sizes),))]
-    pair = over_cores(own)
-    begun = call("own_half", functools.partial(own_kernel, sizes), [(own, "v")], shapes, scratch)
+    return call(
+        "own_half",
+        functools.partial(own_kernel, sizes),
+        [(own, "v")],
+        [((size, 2 * half), F32, "raw") for size in sizes],
+        half_scratch(sizes, half),
+    )
+
+
+def finish(begun, own, pair, sizes):
+    half = own.shape[1]
     return call(
         "pair_half",
         functools.partial(pair_kernel, sizes),
         [(own, "v"), (pair, "v")] + kinds(begun, "raw"),
-        shapes + [((2 * half,), F32, "h")] * 2,
-        scratch,
+        [((size, 2 * half), F32, "raw") for size in sizes] + [((2 * half,), F32, "h")] * 2,
+        half_scratch(sizes, half),
         alias={2 + n: n for n in range(len(sizes))},
     )
 
@@ -1252,7 +1263,6 @@
         dkvs,
         [(total, "v")],
     )
-    layer_out = stack_parts(totals_all)
     keep, send = late_grads(proj_grad, h_one, out_b, branches, [(totals_all[n_tp // 2], "v")])
     own, *others = spread(count, (keep, over_cores(send)), (early, early_back))
     summed = total_of(everywhere(parts), F32, flops=2_000_000_000)
@@ -1264,10 +1274,14 @@
     piece = sum_piece(gains, [chip_sum], ())
     input_grad = stack_parts(inputs_all, (), 3_000_000_000)
     collected = collect(
-        [piece] + came(count, lambda k: over_chips(piece, k)), [(input_grad, "h"), (layer_out, "h")]
-    )
+        [piece] + came(count, lambda k: over_chips(piece, k)), [(input_grad, "h")]
+    )
+    sizes = (3 * width, width, units, 2 * units)
+    pair = over_cores(collected)
+    begun = begin(collected, sizes)
+    layer_out = stack_parts(totals_all, [(begun[0], "h")])
     grad_qkv, grad_out, grad_down, grad_in, grad_one, grad_two = finish(
-        collected, over_cores, (3 * width, width, units, 2 * units)
+        begun, collected, pair, sizes
     )
 
     back = lambda x, n: x.reshape(-1, n, model).transpose(2, 0, 1)

time: 167 us -> 169 us (1.012); the launches traced: 168 us -> 167 us
  Pallas kernels: 54.8 us -> 48.4 us
  starting transfers between devices: 49.2 us -> 55.1 us
    pallas_call x27, Pallas kernels: 54.8 us -> 48.4 us  [call(): pl.pallas_call(run, out_shape=tuple((shaped(shape, dtype) if kind == 'v'...]
    ppermute x46, starting transfers between devices: 49.2 us -> 55.1 us  [swap(): return lax.ppermute(x, axis, [(i, i ^ hop) for i in range(count)])]
  transfers between devices with their start and end apart: 46 -> 46, of which waited for: 21 -> 21; matrix products, arithmetic and copies ran while one was open for 0% -> 0% of each run, Pallas kernels for 29% -> 26%
where the time goes in v13:
time: 169 us; the launch traced here: 167 us
  waiting for transfers between devices  62.1 us (37%)
  starting transfers between devices  55.1 us (33%)
  Pallas kernels  48.4 us (29%)
    ppermute x46, waiting for transfers between devices, swap(): return lax.ppermute(x, axis, [(i, i ^ hop) for i in range(count)])  62.1 us
    ppermute x46, starting transfers between devices, swap(): return lax.ppermute(x, axis, [(i, i ^ hop) for i in range(count)])  55.1 us
    pallas_call x27, Pallas kernels, call(): pl.pallas_call(run, out_shape=tuple((shaped(shape, dtype) if kind == 'v'...  48.4 us
  transfers between devices with their start and end apart: 46, of which 21 were waited for; matrix products, arithmetic and copies ran while one was open for 0% of the time, Pallas kernels for 26%

profile of v13, /device:TPU:0, one launch (start us, length us, event | category | flops | bytes accessed | tf_op | source)
XLA Modules:
  0.0 166.9 jit_solution(144933597649501316)
XLA Ops:
  1.9 3.1 %collective-permute-start = (bf16[528,768]{1,0:T(8,128)(2,1)S(1)}, bf16[528,768]{1,0:T(8,128)(2,1)S(1)}, u32[]{:S(2)}, u32[]{:S(2)}) collective-permute-start(bf16[528,768]{1,0:T(8,128)(2,1)S(1)} %get-tuple-element.74), channel_id=1, source_target_pairs={{0,1},{1,0},{2,3},{3,2},{4,5},{5,4},{6,7},{7,6},{8,9},{9,8},{10,11... | collective-permute-start | bytes 2433032 | tf_op jit(solution)/shard_map/ppermute | solution.py:143
  5.0 3.7 %project.1 = (bf16[192,448]{1,0:T(8,128)(2,1)S(1)}, bf16[384,448]{1,0:T(8,128)(2,1)S(1)}, bf16[448,768]{1,0:T(8,128)(2,1)S(1)}, f32[32,448]{1,0:T(8,128)S(1)}, f32[32,448]{1,0:T(8,128)S(1)}) custom-call(s32[4]{0:T(128)} %refs_0_.13, s32[8]{0:T(128)} %refs_1_.16, bf16[448,768]{1,0:T(8,128)(2,1)} %refs_0_.15, bf16[576,768]{1,0:T(8,128)(2,1)} %bitcast.15, ...), custom_call_target="tpu_custom_call" | custom-call | tf_op jit(solution)/shard_map/project/pallas_call | solution.py:121
  13.7 2.5 %collective-permute-start.2 = (bf16[96,768]{1,0:T(8,128)(2,1)S(1)}, bf16[96,768]{1,0:T(8,128)(2,1)S(1)}, u32[]{:S(2)}, u32[]{:S(2)}) collective-permute-start(bf16[96,768]{1,0:T(8,128)(2,1)S(1)} %get-tuple-element.75), channel_id=1, source_target_pairs={{0,3},{1,2},{2,1},{3,0},{4,7},{5,6},{6,5},{7,4},{8,11},{9,10},{10,... | collective-permute-start | bytes 442376 | tf_op jit(solution)/shard_map/ppermute | solution.py:143
  16.2 4.6 %collective-permute-done.6.refs_5_.refs_10_ = bf16[384,448]{1,0:T(8,128)(2,1)S(1)} collective-permute-done((bf16[384,448]{1,0:T(8,128)(2,1)S(1)}, bf16[384,448]{1,0:T(8,128)(2,1)S(1)}, u32[]{:S(2)}, u32[]{:S(2)}) %collective-permute-start.6) | collective-permute-done | bytes 344096 | tf_op jit(solution)/shard_map/ppermute | solution.py:143
  20.8 2.6 %collective-permute-start.1 = (bf16[96,768]{1,0:T(8,128)(2,1)S(1)}, bf16[96,768]{1,0:T(8,128)(2,1)S(1)}, u32[]{:S(2)}, u32[]{:S(2)}) collective-permute-start(bf16[96,768]{1,0:T(8,128)(2,1)S(1)} %get-tuple-element.75), channel_id=1, source_target_pairs={{0,2},{1,3},{2,0},{3,1},{4,6},{5,7},{6,4},{7,5},{8,10},{9,11},{10,... | collective-permute-start | bytes 442376 | tf_op jit(solution)/shard_map/ppermute | solution.py:143
  23.4 7.1 %attention_forward.2.refs_6_ = f32[6,80,448]{2,1,0:T(8,128)S(1)} custom-call(s32[4]{0:T(128)} %refs_0_.13, s32[8]{0:T(128)} %refs_1_.16, bf16[192,448]{1,0:T(8,128)(2,1)S(1)} %get-tuple-element.76.refs_2_, bf16[192,448]{1,0:T(8,128)(2,1)S(1)} %collective-permute-done.3.refs_3_, bf16[384,448]{1,0:T(8,128)(2,1)S(1)} %get-tuple-element.77.refs_4_.refs_10_, ...), custom_call_target="tpu_custom_call" | custom-call | tf_op jit(solution)/shard_map/attention_forward/pallas_call | solution.py:121
  33.3 2.9 %collective-permute-done.8.refs_1_ = f32[3,80,448]{2,1,0:T(8,128)S(1)} collective-permute-done((f32[3,80,448]{2,1,0:T(8,128)S(1)}, f32[3,80,448]{2,1,0:T(8,128)S(1)}, u32[]{:S(2)}, u32[]{:S(2)}) %collective-permute-start.8) | collective-permute-done | bytes 430112 | tf_op jit(solution)/shard_map/ppermute | solution.py:143
  39.1 1.9 %collective-permute-start.9 = (bf16[192,224]{1,0:T(8,128)(2,1)S(1)}, bf16[192,224]{1,0:T(8,128)(2,1)S(1)}, u32[]{:S(2)}, u32[]{:S(2)}) collective-permute-start(bf16[192,224]{1,0:T(8,128)(2,1)S(1)} %get-tuple-element.86), channel_id=1, source_target_pairs={{0,3},{1,2},{2,1},{3,0},{4,7},{5,6},{6,5},{7,4},{8,11},{9,10},{10,... | collective-permute-start | bytes 258056 | tf_op jit(solution)/shard_map/ppermute | solution.py:143
  41.1 3.2 %stage.1 = (bf16[224,768]{1,0:T(8,128)(2,1)S(1)}, bf16[224,768]{1,0:T(8,128)(2,1)S(1)}, bf16[768,768]{1,0:T(8,128)(2,1)S(1)}, bf16[1152,768]{1,0:T(8,128)(2,1)S(1)}, bf16[576,768]{1,0:T(8,128)(2,1)S(1)}) custom-call(bf16[448,768]{1,0:T(8,128)(2,1)} %refs_0_.15, bf16[448,768]{1,0:T(8,128)(2,1)} %refs_2_.7, bf16[576,768]{1,0:T(8,128)(2,1)} %bitcast.13, ...), custom_call_target="tpu_custom_call" | custom-call | tf_op jit(solution)/shard_map/stage/pallas_call | solution.py:121
  47.0 4.8 %feed.1 = (f32[224,768]{1,0:T(8,128)S(1)}, f32[112,768]{1,0:T(8,128)S(1)}, bf16[224,768]{1,0:T(8,128)(2,1)S(1)}, bf16[576,224]{1,0:T(8,128)(2,1)S(1)}, bf16[1152...) custom-call(bf16[224,768]{1,0:T(8,128)(2,1)S(1)} %get-tuple-element.79.refs_, ...), custom_call_target="tpu_custom_call" | custom-call | tf_op jit(solution)/shard_map/feed/pallas_call | solution.py:121
  51.7 2.8 %collective-permute-start.15 = (bf16[112,768]{1,0:T(8,128)(2,1)S(1)}, bf16[112,768]{1,0:T(8,128)(2,1)S(1)}, u32[]{:S(2)}, u32[]{:S(2)}) collective-permute-start(bf16[112,768]{1,0:T(8,128)(2,1)S(1)} %get-tuple-element.95), channel_id=1, source_target_pairs={{0,2},{1,3},{2,0},{3,1},{4,6},{5,7},{6,4},{7,5},{8,10},{9,11},{10,... | collective-permute-start | bytes 516104 | tf_op jit(solution)/shard_map/ppermute | solution.py:143
  56.3 5.9 %collective-permute-done.15.refs_5_ = bf16[112,768]{1,0:T(8,128)(2,1)S(1)} collective-permute-done((bf16[112,768]{1,0:T(8,128)(2,1)S(1)}, bf16[112,768]{1,0:T(8,128)(2,1)S(1)}, u32[]{:S(2)}, u32[]{:S(2)}) %collective-permute-start.15) | collective-permute-done | bytes 172064 | tf_op jit(solution)/shard_map/ppermute | solution.py:143
  64.0 2.0 %collective-permute-start.16 = (bf16[112,192]{1,0:T(8,128)(2,1)S(1)}, bf16[112,192]{1,0:T(8,128)(2,1)S(1)}, u32[]{:S(2)}, u32[]{:S(2)}) collective-permute-start(bf16[112,192]{1,0:T(8,128)(2,1)S(1)} %get-tuple-element.97), channel_id=1, source_target_pairs={{0,3},{1,2},{2,1},{3,0},{4,7},{5,6},{6,5},{7,4},{8,11},{9,10},{10,... | collective-permute-start | bytes 129032 | tf_op jit(solution)/shard_map/ppermute | solution.py:143
  65.9 2.5 %collective-permute-start.18 = (bf16[112,192]{1,0:T(8,128)(2,1)S(1)}, bf16[112,192]{1,0:T(8,128)(2,1)S(1)}, u32[]{:S(2)}, u32[]{:S(2)}) collective-permute-start(bf16[112,192]{1,0:T(8,128)(2,1)S(1)} %get-tuple-element.99), channel_id=1, source_target_pairs={{0,1},{1,0},{2,3},{3,2},{4,5},{5,4},{6,7},{7,6},{8,9},{9,8},{10,11... | collective-permute-start | bytes 129032 | tf_op jit(solution)/shard_map/ppermute | solution.py:143
  71.5 1.8 %collective-permute-start.14 = (bf16[112,768]{1,0:T(8,128)(2,1)S(1)}, bf16[112,768]{1,0:T(8,128)(2,1)S(1)}, u32[]{:S(2)}, u32[]{:S(2)}) collective-permute-start(bf16[112,768]{1,0:T(8,128)(2,1)S(1)} %get-tuple-element.92), channel_id=1, source_target_pairs={{0,2},{1,3},{2,0},{3,1},{4,6},{5,7},{6,4},{7,5},{8,10},{9,11},{10,... | collective-permute-start | bytes 516104 | tf_op jit(solution)/shard_map/ppermute | solution.py:143
  75.9 5.4 %attention_backward.2 = (bf16[384,448]{1,0:T(8,128)(2,1)S(1)}, bf16[384,448]{1,0:T(8,128)(2,1)S(1)}, bf16[384,448]{1,0:T(8,128)(2,1)S(1)}, f32[6,64,448]{2,1,0:T(8,128)S(1)}) custom-call(s32[4]{0:T(128)} %refs_0_.13, s32[8]{0:T(128)} %refs_1_.16, bf16[192,448]{1,0:T(8,128)(2,1)S(1)} %get-tuple-element.76.refs_2_, ...), custom_call_target="tpu_custom_call" | custom-call | tf_op jit(solution)/shard_map/attention_backward/pallas_call | solution.py:121
  81.4 6.1 %collective-permute-start.25 = (bf16[384,448]{1,0:T(8,128)(2,1)S(1)}, bf16[384,448]{1,0:T(8,128)(2,1)S(1)}, u32[]{:S(2)}, u32[]{:S(2)}) collective-permute-start(bf16[384,448]{1,0:T(8,128)(2,1)S(1)} %get-tuple-element.109), channel_id=1, source_target_pairs={{0,8},{4,12},{8,0},{12,4},{16,24},{20,28},{24,16},{28,20},{1,9},{5... | collective-permute-start | bytes 1032200 | tf_op jit(solution)/shard_map/ppermute | solution.py:143
  89.0 5.0 %attention_backward.3 = (f32[384,448]{1,0:T(8,128)S(1)}, f32[192,448]{1,0:T(8,128)S(1)}, bf16[192,448]{1,0:T(8,128)(2,1)S(1)}) custom-call(s32[4]{0:T(128)} %refs_0_.13, s32[8]{0:T(128)} %refs_1_.16, bf16[192,448]{1,0:T(8,128)(2,1)S(1)} %get-tuple-element.76.refs_2_, bf16[192,448]{1,0:T(8,128)(2,1)S(1)} %collective-permute-done.3.refs_3_, ...), custom_call_target="tpu_custom_call" | custom-call | tf_op jit(solution)/shard_map/attention_backward/pallas_call | solution.py:121
  99.0 2.1 %early_grads.1 = (f32[864,384]{1,0:T(8,128)S(1)}, bf16[864,384]{1,0:T(8,128)(2,1)S(1)}) custom-call(bf16[576,224]{1,0:T(8,128)(2,1)S(1)} %get-tuple-element.87.refs_0_, bf16[1152,224]{1,0:T(8,128)(2,1)S(1)} %get-tuple-element.120.refs_1_, bf16[448,768]{1,0:T(8,128)(2,1)S(1)} %copy-done.2, bf16[224,768]{1,0:T(8,128)(2,1)S(1)} %get-tuple-element.121.refs_3_, ...), custom_call_target="tpu_custom_call" | custom-call | tf_op jit(solution)/shard_map/early_grads/pallas_call | solution.py:121
  101.1 3.9 %collective-permute-done.26.refs_9_ = bf16[384,448]{1,0:T(8,128)(2,1)S(1)} collective-permute-done((bf16[384,448]{1,0:T(8,128)(2,1)S(1)}, bf16[384,448]{1,0:T(8,128)(2,1)S(1)}, u32[]{:S(2)}, u32[]{:S(2)}) %collective-permute-start.26) | collective-permute-done | bytes 344096 | tf_op jit(solution)/shard_map/ppermute | solution.py:143
  105.0 2.5 %unproject.1 = (bf16[576,448]{1,0:T(8,128)(2,1)S(1)}, f32[128,768]{1,0:T(8,128)S(1)}, bf16[128,768]{1,0:T(8,128)(2,1)S(1)}, bf16[128,768]{1,0:T(8,128)(2,1)S(1)}, bf16[128,768]{1,0:T(8,128)(2,1)S(1)}) custom-call(bf16[448,768]{1,0:T(8,128)(2,1)S(1)} %copy-done, bf16[576,768]{1,0:T(8,128)(2,1)S(1)} %bitcast.16, f32[32,448]{1,0:T(8,128)S(1)} %get-tuple-element.103.refs_2_, ...), custom_call_target="tpu_custom_call" | custom-call | tf_op jit(solution)/shard_map/unproject/pallas_call | solution.py:121
  109.5 2.0 %collective-permute-start.28 = (bf16[128,768]{1,0:T(8,128)(2,1)S(1)}, bf16[128,768]{1,0:T(8,128)(2,1)S(1)}, u32[]{:S(2)}, u32[]{:S(2)}) collective-permute-start(bf16[128,768]{1,0:T(8,128)(2,1)S(1)} %get-tuple-element.113), channel_id=1, source_target_pairs={{0,3},{1,2},{2,1},{3,0},{4,7},{5,6},{6,5},{7,4},{8,11},{9,10},{10,... | collective-permute-start | bytes 589832 | tf_op jit(solution)/shard_map/ppermute | solution.py:143
  116.2 3.1 %collective-permute-done.28.refs_1_ = bf16[128,768]{1,0:T(8,128)(2,1)S(1)} collective-permute-done((bf16[128,768]{1,0:T(8,128)(2,1)S(1)}, bf16[128,768]{1,0:T(8,128)(2,1)S(1)}, u32[]{:S(2)}, u32[]{:S(2)}) %collective-permute-start.28) | collective-permute-done | bytes 196640 | tf_op jit(solution)/shard_map/ppermute | solution.py:143
  119.4 10.9 %collective-permute-done.29.refs_2_ = bf16[128,768]{1,0:T(8,128)(2,1)S(1)} collective-permute-done((bf16[128,768]{1,0:T(8,128)(2,1)S(1)}, bf16[128,768]{1,0:T(8,128)(2,1)S(1)}, u32[]{:S(2)}, u32[]{:S(2)}) %collective-permute-start.29) | collective-permute-done | bytes 196640 | tf_op jit(solution)/shard_map/ppermute | solution.py:143
  131.8 2.6 %collective-permute-start.43 = (bf16[112,768]{1,0:T(8,128)(2,1)S(1)}, bf16[112,768]{1,0:T(8,128)(2,1)S(1)}, u32[]{:S(2)}, u32[]{:S(2)}) collective-permute-start(bf16[112,768]{1,0:T(8,128)(2,1)S(1)} %get-tuple-element.129.refs_0_), channel_id=1, source_target_pairs={{0,2},{1,3},{2,0},{3,1},{4,6},{5,7},{6,4},{7,5},{8,10},{9,11},{10,... | collective-permute-start | bytes 516104 | tf_op jit(solution)/shard_map/ppermute | solution.py:143
  137.9 2.6 %collective-permute-done.44.refs_3_ = bf16[112,768]{1,0:T(8,128)(2,1)S(1)} collective-permute-done((bf16[112,768]{1,0:T(8,128)(2,1)S(1)}, bf16[112,768]{1,0:T(8,128)(2,1)S(1)}, u32[]{:S(2)}, u32[]{:S(2)}) %collective-permute-start.44) | collective-permute-done | bytes 172064 | tf_op jit(solution)/shard_map/ppermute | solution.py:143
  141.2 6.2 %collective-permute-done.43.refs_2_ = bf16[112,768]{1,0:T(8,128)(2,1)S(1)} collective-permute-done((bf16[112,768]{1,0:T(8,128)(2,1)S(1)}, bf16[112,768]{1,0:T(8,128)(2,1)S(1)}, u32[]{:S(2)}, u32[]{:S(2)}) %collective-permute-start.43) | collective-permute-done | bytes 172064 | tf_op jit(solution)/shard_map/ppermute | solution.py:143
  148.4 4.3 %collective-permute-done.40.refs_2_ = bf16[424,384]{1,0:T(8,128)(2,1)S(1)} collective-permute-done((bf16[424,384]{1,0:T(8,128)(2,1)S(1)}, bf16[424,384]{1,0:T(8,128)(2,1)S(1)}, u32[]{:S(2)}, u32[]{:S(2)}) %collective-permute-start.40) | collective-permute-done | bytes 325664 | tf_op jit(solution)/shard_map/ppermute | solution.py:143
  153.2 2.0 %collective-permute-start.22 = (bf16[112,768]{1,0:T(8,128)(2,1)S(1)}, bf16[112,768]{1,0:T(8,128)(2,1)S(1)}, u32[]{:S(2)}, u32[]{:S(2)}) collective-permute-start(bf16[112,768]{1,0:T(8,128)(2,1)S(1)} %collective-permute-done.21.refs_7_.refs_2_), channel_id=1, source_target_pairs={{0,1},{1,0},{2,3},{3,2},{4,5},{5,4},{6,7},{7,6},{8,9},{9,8},{10,11... | collective-permute-start | bytes 516104 | tf_op jit(solution)/shard_map/ppermute | solution.py:143
  156.7 3.6 %collective-permute-done.23.refs_3_ = bf16[112,768]{1,0:T(8,128)(2,1)S(1)} collective-permute-done((bf16[112,768]{1,0:T(8,128)(2,1)S(1)}, bf16[112,768]{1,0:T(8,128)(2,1)S(1)}, u32[]{:S(2)}, u32[]{:S(2)}) %collective-permute-start.23) | collective-permute-done | bytes 172064 | tf_op jit(solution)/shard_map/ppermute | solution.py:143
  160.3 3.2 %collective-permute-done.22.refs_1_ = bf16[112,768]{1,0:T(8,128)(2,1)S(1)} collective-permute-done((bf16[112,768]{1,0:T(8,128)(2,1)S(1)}, bf16[112,768]{1,0:T(8,128)(2,1)S(1)}, u32[]{:S(2)}, u32[]{:S(2)}) %collective-permute-start.22) | collective-permute-done | bytes 172064 | tf_op jit(solution)/shard_map/ppermute | solution.py:143
  164.5 2.1 %pair_half.1 = (f32[576,768]{1,0:T(8,128)}, f32[192,768]{1,0:T(8,128)}, f32[288,768]{1,0:T(8,128)}, f32[576,768]{1,0:T(8,128)}, f32[768]{0:T(1024)}, /*index=5*/f32[768]{0:T(1024)}) custom-call(bf16[1648,384]{1,0:T(8,128)(2,1)S(1)} %collect.1.refs_0_, ...), custom_call_target="tpu_custom_call", output_to_operand_aliasing={{0}: (2, {}), {1}: (3, {}), {2}: (4, {}), {3}: (5, {})} | custom-call | tf_op jit(solution)/shard_map/pair_half/pallas_call | solution.py:121
  (97 shorter events, 46.3 us)
Async XLA Ops:
  1.9 30.7 %collective-permute-start = (bf16[528,768]{1,0:T(8,128)(2,1)S(1)}, bf16[528,768]{1,0:T(8,128)(2,1)S(1)}, u32[]{:S(2)}, u32[]{:S(2)}) collective-permute-start(bf16[528,768]{1,0:T(8,128)(2,1)S(1)} %get-tuple-element.74), channel_id=1, source_target_pairs={{0,1},{1,0},{2,3},{3,2},{4,5},{5,4},{6,7},{7,6},{8,9},{9,8},{10,11... | collective-permute-start | bytes 2433032 | tf_op jit(solution)/shard_map/ppermute | solution.py:143
  8.7 12.1 %collective-permute-start.6 = (bf16[384,448]{1,0:T(8,128)(2,1)S(1)}, bf16[384,448]{1,0:T(8,128)(2,1)S(1)}, u32[]{:S(2)}, u32[]{:S(2)}) collective-permute-start(bf16[384,448]{1,0:T(8,128)(2,1)S(1)} %get-tuple-element.77.refs_4_.refs_10_), channel_id=1, source_target_pairs={{0,8},{4,12},{8,0},{12,4},{16,24},{20,28},{24,16},{28,20},{1,9},{5... | collective-permute-start | bytes 1032200 | tf_op jit(solution)/shard_map/ppermute | solution.py:143
  10.3 20.3 %collective-permute-start.5 = (bf16[384,448]{1,0:T(8,128)(2,1)S(1)}, bf16[384,448]{1,0:T(8,128)(2,1)S(1)}, u32[]{:S(2)}, u32[]{:S(2)}) collective-permute-start(bf16[384,448]{1,0:T(8,128)(2,1)S(1)} %get-tuple-element.77.refs_4_.refs_10_), channel_id=1, source_target_pairs={{0,24},{4,28},{8,16},{12,20},{16,8},{20,12},{24,0},{28,4},{1,25},{... | collective-permute-start | bytes 1032200 | tf_op jit(solution)/shard_map/ppermute | solution.py:143
  11.8 18.8 %collective-permute-start.4 = (bf16[384,448]{1,0:T(8,128)(2,1)S(1)}, bf16[384,448]{1,0:T(8,128)(2,1)S(1)}, u32[]{:S(2)}, u32[]{:S(2)}) collective-permute-start(bf16[384,448]{1,0:T(8,128)(2,1)S(1)} %get-tuple-element.77.refs_4_.refs_10_), channel_id=1, source_target_pairs={{0,16},{4,20},{8,24},{12,28},{16,0},{20,4},{24,8},{28,12},{1,17},{... | collective-permute-start | bytes 1032200 | tf_op jit(solution)/shard_map/ppermute | solution.py:143
  13.7 18.2 %collective-permute-start.2 = (bf16[96,768]{1,0:T(8,128)(2,1)S(1)}, bf16[96,768]{1,0:T(8,128)(2,1)S(1)}, u32[]{:S(2)}, u32[]{:S(2)}) collective-permute-start(bf16[96,768]{1,0:T(8,128)(2,1)S(1)} %get-tuple-element.75), channel_id=1, source_target_pairs={{0,3},{1,2},{2,1},{3,0},{4,7},{5,6},{6,5},{7,4},{8,11},{9,10},{10,... | collective-permute-start | bytes 442376 | tf_op jit(solution)/shard_map/ppermute | solution.py:143
  20.8 11.8 %collective-permute-start.1 = (bf16[96,768]{1,0:T(8,128)(2,1)S(1)}, bf16[96,768]{1,0:T(8,128)(2,1)S(1)}, u32[]{:S(2)}, u32[]{:S(2)}) collective-permute-start(bf16[96,768]{1,0:T(8,128)(2,1)S(1)} %get-tuple-element.75), channel_id=1, source_target_pairs={{0,2},{1,3},{2,0},{3,1},{4,6},{5,7},{6,4},{7,5},{8,10},{9,11},{10,... | collective-permute-start | bytes 442376 | tf_op jit(solution)/shard_map/ppermute | solution.py:143
  36.6 9.4 %collective-permute-start.10 = (bf16[192,224]{1,0:T(8,128)(2,1)S(1)}, bf16[192,224]{1,0:T(8,128)(2,1)S(1)}, u32[]{:S(2)}, u32[]{:S(2)}) collective-permute-start(bf16[192,224]{1,0:T(8,128)(2,1)S(1)} %get-tuple-element.85.refs_6_), channel_id=1, source_target_pairs={{0,2},{1,3},{2,0},{3,1},{4,6},{5,7},{6,4},{7,5},{8,10},{9,11},{10,... | collective-permute-start | bytes 258056 | tf_op jit(solution)/shard_map/ppermute | solution.py:143
  41.1 14.7 %collective-permute-start.12 = (bf16[192,448]{1,0:T(8,128)(2,1)S(1)}, bf16[192,448]{1,0:T(8,128)(2,1)S(1)}, u32[]{:S(2)}, u32[]{:S(2)}) collective-permute-start(bf16[192,448]{1,0:T(8,128)(2,1)S(1)} %get-tuple-element.89.refs_6_.refs_2_), channel_id=1, source_target_pairs={{0,4},{4,0},{8,12},{12,8},{16,20},{20,16},{24,28},{28,24},{1,5},{5... | collective-permute-start | bytes 516104 | tf_op jit(solution)/shard_map/ppermute | solution.py:143
  51.7 10.5 %collective-permute-start.15 = (bf16[112,768]{1,0:T(8,128)(2,1)S(1)}, bf16[112,768]{1,0:T(8,128)(2,1)S(1)}, u32[]{:S(2)}, u32[]{:S(2)}) collective-permute-start(bf16[112,768]{1,0:T(8,128)(2,1)S(1)} %get-tuple-element.95), channel_id=1, source_target_pairs={{0,2},{1,3},{2,0},{3,1},{4,6},{5,7},{6,4},{7,5},{8,10},{9,11},{10,... | collective-permute-start | bytes 516104 | tf_op jit(solution)/shard_map/ppermute | solution.py:143
  71.5 15.9 %collective-permute-start.14 = (bf16[112,768]{1,0:T(8,128)(2,1)S(1)}, bf16[112,768]{1,0:T(8,128)(2,1)S(1)}, u32[]{:S(2)}, u32[]{:S(2)}) collective-permute-start(bf16[112,768]{1,0:T(8,128)(2,1)S(1)} %get-tuple-element.92), channel_id=1, source_target_pairs={{0,2},{1,3},{2,0},{3,1},{4,6},{5,7},{6,4},{7,5},{8,10},{9,11},{10,... | collective-permute-start | bytes 516104 | tf_op jit(solution)/shard_map/ppermute | solution.py:143
  73.4 20.8 %collective-permute-start.34 = (bf16[224,768]{1,0:T(8,128)(2,1)S(1)}, bf16[224,768]{1,0:T(8,128)(2,1)S(1)}, u32[]{:S(2)}, u32[]{:S(2)}) collective-permute-start(bf16[224,768]{1,0:T(8,128)(2,1)S(1)} %get-tuple-element.121.refs_3_), channel_id=1, source_target_pairs={{0,1},{1,0},{2,3},{3,2},{4,5},{5,4},{6,7},{7,6},{8,9},{9,8},{10,11... | collective-permute-start | bytes 1032200 | tf_op jit(solution)/shard_map/ppermute | solution.py:143
  74.3 19.8 %collective-permute-start.20 = (bf16[112,768]{1,0:T(8,128)(2,1)S(1)}, bf16[112,768]{1,0:T(8,128)(2,1)S(1)}, u32[]{:S(2)}, u32[]{:S(2)}) collective-permute-start(bf16[112,768]{1,0:T(8,128)(2,1)S(1)} %get-tuple-element.101.refs_3_.refs_7_), channel_id=1, source_target_pairs={{0,2},{1,3},{2,0},{3,1},{4,6},{5,7},{6,4},{7,5},{8,10},{9,11},{10,... | collective-permute-start | bytes 516104 | tf_op jit(solution)/shard_map/ppermute | solution.py:143
  81.4 16.2 %collective-permute-start.25 = (bf16[384,448]{1,0:T(8,128)(2,1)S(1)}, bf16[384,448]{1,0:T(8,128)(2,1)S(1)}, u32[]{:S(2)}, u32[]{:S(2)}) collective-permute-start(bf16[384,448]{1,0:T(8,128)(2,1)S(1)} %get-tuple-element.109), channel_id=1, source_target_pairs={{0,8},{4,12},{8,0},{12,4},{16,24},{20,28},{24,16},{28,20},{1,9},{5... | collective-permute-start | bytes 1032200 | tf_op jit(solution)/shard_map/ppermute | solution.py:143
  87.5 17.5 %collective-permute-start.26 = (bf16[384,448]{1,0:T(8,128)(2,1)S(1)}, bf16[384,448]{1,0:T(8,128)(2,1)S(1)}, u32[]{:S(2)}, u32[]{:S(2)}) collective-permute-start(bf16[384,448]{1,0:T(8,128)(2,1)S(1)} %get-tuple-element.110), channel_id=1, source_target_pairs={{0,16},{4,20},{8,24},{12,28},{16,0},{20,4},{24,8},{28,12},{1,17},{... | collective-permute-start | bytes 1032200 | tf_op jit(solution)/shard_map/ppermute | solution.py:143
  87.5 17.5 %collective-permute-start.27 = (bf16[384,448]{1,0:T(8,128)(2,1)S(1)}, bf16[384,448]{1,0:T(8,128)(2,1)S(1)}, u32[]{:S(2)}, u32[]{:S(2)}) collective-permute-start(bf16[384,448]{1,0:T(8,128)(2,1)S(1)} %get-tuple-element.111), channel_id=1, source_target_pairs={{0,24},{4,28},{8,16},{12,20},{16,8},{20,12},{24,0},{28,4},{1,25},{... | collective-permute-start | bytes 1032200 | tf_op jit(solution)/shard_map/ppermute | solution.py:143
  94.2 13.3 %collective-permute-start.32 = (bf16[112,768]{1,0:T(8,128)(2,1)S(1)}, bf16[112,768]{1,0:T(8,128)(2,1)S(1)}, u32[]{:S(2)}, u32[]{:S(2)}) collective-permute-start(bf16[112,768]{1,0:T(8,128)(2,1)S(1)} %get-tuple-element.101.refs_3_.refs_7_), channel_id=1, source_target_pairs={{0,1},{1,0},{2,3},{3,2},{4,5},{5,4},{6,7},{7,6},{8,9},{9,8},{10,11... | collective-permute-start | bytes 516104 | tf_op jit(solution)/shard_map/ppermute | solution.py:143
  95.6 12.8 %collective-permute-start.31 = (bf16[112,768]{1,0:T(8,128)(2,1)S(1)}, bf16[112,768]{1,0:T(8,128)(2,1)S(1)}, u32[]{:S(2)}, u32[]{:S(2)}) collective-permute-start(bf16[112,768]{1,0:T(8,128)(2,1)S(1)} %collective-permute-done.20.refs_3_.refs_5_), channel_id=1, source_target_pairs={{0,1},{1,0},{2,3},{3,2},{4,5},{5,4},{6,7},{7,6},{8,9},{9,8},{10,11... | collective-permute-start | bytes 516104 | tf_op jit(solution)/shard_map/ppermute | solution.py:143
  97.5 10.9 %collective-permute-start.21 = (bf16[112,768]{1,0:T(8,128)(2,1)S(1)}, bf16[112,768]{1,0:T(8,128)(2,1)S(1)}, u32[]{:S(2)}, u32[]{:S(2)}) collective-permute-start(bf16[112,768]{1,0:T(8,128)(2,1)S(1)} %total_of.3.refs_11_.refs_0_), channel_id=1, source_target_pairs={{0,2},{1,3},{2,0},{3,1},{4,6},{5,7},{6,4},{7,5},{8,10},{9,11},{10,... | collective-permute-start | bytes 516104 | tf_op jit(solution)/shard_map/ppermute | solution.py:143
  105.0 9.0 %collective-permute-start.35 = (bf16[864,384]{1,0:T(8,128)(2,1)S(1)}, bf16[864,384]{1,0:T(8,128)(2,1)S(1)}, u32[]{:S(2)}, u32[]{:S(2)}) collective-permute-start(bf16[864,384]{1,0:T(8,128)(2,1)S(1)} %get-tuple-element.123), channel_id=1, source_target_pairs={{0,4},{4,0},{8,12},{12,8},{16,20},{20,16},{24,28},{28,24},{1,5},{5... | collective-permute-start | bytes 1990664 | tf_op jit(solution)/shard_map/ppermute | solution.py:143
  109.5 9.7 %collective-permute-start.28 = (bf16[128,768]{1,0:T(8,128)(2,1)S(1)}, bf16[128,768]{1,0:T(8,128)(2,1)S(1)}, u32[]{:S(2)}, u32[]{:S(2)}) collective-permute-start(bf16[128,768]{1,0:T(8,128)(2,1)S(1)} %get-tuple-element.113), channel_id=1, source_target_pairs={{0,3},{1,2},{2,1},{3,0},{4,7},{5,6},{6,5},{7,4},{8,11},{9,10},{10,... | collective-permute-start | bytes 589832 | tf_op jit(solution)/shard_map/ppermute | solution.py:143
  111.6 18.8 %collective-permute-start.29 = (bf16[128,768]{1,0:T(8,128)(2,1)S(1)}, bf16[128,768]{1,0:T(8,128)(2,1)S(1)}, u32[]{:S(2)}, u32[]{:S(2)}) collective-permute-start(bf16[128,768]{1,0:T(8,128)(2,1)S(1)} %get-tuple-element.114), channel_id=1, source_target_pairs={{0,2},{1,3},{2,0},{3,1},{4,6},{5,7},{6,4},{7,5},{8,10},{9,11},{10,... | collective-permute-start | bytes 589832 | tf_op jit(solution)/shard_map/ppermute | solution.py:143
  112.5 17.9 %collective-permute-start.30 = (bf16[128,768]{1,0:T(8,128)(2,1)S(1)}, bf16[128,768]{1,0:T(8,128)(2,1)S(1)}, u32[]{:S(2)}, u32[]{:S(2)}) collective-permute-start(bf16[128,768]{1,0:T(8,128)(2,1)S(1)} %get-tuple-element.115), channel_id=1, source_target_pairs={{0,1},{1,0},{2,3},{3,2},{4,5},{5,4},{6,7},{7,6},{8,9},{9,8},{10,11... | collective-permute-start | bytes 589832 | tf_op jit(solution)/shard_map/ppermute | solution.py:143
  114.5 20.0 %collective-permute-start.36 = (bf16[408,384]{1,0:T(8,128)(2,1)S(1)}, bf16[408,384]{1,0:T(8,128)(2,1)S(1)}, u32[]{:S(2)}, u32[]{:S(2)}) collective-permute-start(bf16[408,384]{1,0:T(8,128)(2,1)S(1)} %get-tuple-element.126), channel_id=1, source_target_pairs={{0,24},{4,28},{8,16},{12,20},{16,8},{20,12},{24,0},{28,4},{1,25},{... | collective-permute-start | bytes 940040 | tf_op jit(solution)/shard_map/ppermute | solution.py:143
  115.6 20.6 %collective-permute-start.37 = (bf16[408,384]{1,0:T(8,128)(2,1)S(1)}, bf16[408,384]{1,0:T(8,128)(2,1)S(1)}, u32[]{:S(2)}, u32[]{:S(2)}) collective-permute-start(bf16[408,384]{1,0:T(8,128)(2,1)S(1)} %get-tuple-element.127), channel_id=1, source_target_pairs={{0,16},{4,20},{8,24},{12,28},{16,0},{20,4},{24,8},{28,12},{1,17},{... | collective-permute-start | bytes 940040 | tf_op jit(solution)/shard_map/ppermute | solution.py:143
  119.2 17.0 %collective-permute-start.38 = (bf16[408,384]{1,0:T(8,128)(2,1)S(1)}, bf16[408,384]{1,0:T(8,128)(2,1)S(1)}, u32[]{:S(2)}, u32[]{:S(2)}) collective-permute-start(bf16[408,384]{1,0:T(8,128)(2,1)S(1)} %get-tuple-element.128), channel_id=1, source_target_pairs={{0,8},{4,12},{8,0},{12,4},{16,24},{20,28},{24,16},{28,20},{1,9},{5... | collective-permute-start | bytes 940040 | tf_op jit(solution)/shard_map/ppermute | solution.py:143
  131.8 15.6 %collective-permute-start.43 = (bf16[112,768]{1,0:T(8,128)(2,1)S(1)}, bf16[112,768]{1,0:T(8,128)(2,1)S(1)}, u32[]{:S(2)}, u32[]{:S(2)}) collective-permute-start(bf16[112,768]{1,0:T(8,128)(2,1)S(1)} %get-tuple-element.129.refs_0_), channel_id=1, source_target_pairs={{0,2},{1,3},{2,0},{3,1},{4,6},{5,7},{6,4},{7,5},{8,10},{9,11},{10,... | collective-permute-start | bytes 516104 | tf_op jit(solution)/shard_map/ppermute | solution.py:143
  134.5 13.0 %collective-permute-start.42 = (bf16[112,768]{1,0:T(8,128)(2,1)S(1)}, bf16[112,768]{1,0:T(8,128)(2,1)S(1)}, u32[]{:S(2)}, u32[]{:S(2)}) collective-permute-start(bf16[112,768]{1,0:T(8,128)(2,1)S(1)} %get-tuple-element.129.refs_0_), channel_id=1, source_target_pairs={{0,3},{1,2},{2,1},{3,0},{4,7},{5,6},{6,5},{7,4},{8,11},{9,10},{10,... | collective-permute-start | bytes 516104 | tf_op jit(solution)/shard_map/ppermute | solution.py:143
  136.4 11.9 %collective-permute-start.41 = (bf16[424,384]{1,0:T(8,128)(2,1)S(1)}, bf16[424,384]{1,0:T(8,128)(2,1)S(1)}, u32[]{:S(2)}, u32[]{:S(2)}) collective-permute-start(bf16[424,384]{1,0:T(8,128)(2,1)S(1)} %sum_piece.1.refs_0_), channel_id=1, source_target_pairs={{0,8},{4,12},{8,0},{12,4},{16,24},{20,28},{24,16},{28,20},{1,9},{5... | collective-permute-start | bytes 976904 | tf_op jit(solution)/shard_map/ppermute | solution.py:143
  137.4 15.3 %collective-permute-start.40 = (bf16[424,384]{1,0:T(8,128)(2,1)S(1)}, bf16[424,384]{1,0:T(8,128)(2,1)S(1)}, u32[]{:S(2)}, u32[]{:S(2)}) collective-permute-start(bf16[424,384]{1,0:T(8,128)(2,1)S(1)} %sum_piece.1.refs_0_), channel_id=1, source_target_pairs={{0,16},{4,20},{8,24},{12,28},{16,0},{20,4},{24,8},{28,12},{1,17},{... | collective-permute-start | bytes 976904 | tf_op jit(solution)/shard_map/ppermute | solution.py:143
  140.5 12.2 %collective-permute-start.39 = (bf16[424,384]{1,0:T(8,128)(2,1)S(1)}, bf16[424,384]{1,0:T(8,128)(2,1)S(1)}, u32[]{:S(2)}, u32[]{:S(2)}) collective-permute-start(bf16[424,384]{1,0:T(8,128)(2,1)S(1)} %sum_piece.1.refs_0_), channel_id=1, source_target_pairs={{0,24},{4,28},{8,16},{12,20},{16,8},{20,12},{24,0},{28,4},{1,25},{... | collective-permute-start | bytes 976904 | tf_op jit(solution)/shard_map/ppermute | solution.py:143
  153.0 11.5 %collective-permute-start.45 = (bf16[1648,384]{1,0:T(8,128)(2,1)S(1)}, bf16[1648,384]{1,0:T(8,128)(2,1)S(1)}, u32[]{:S(2)}, u32[]{:S(2)}) collective-permute-start(bf16[1648,384]{1,0:T(8,128)(2,1)S(1)} %collect.1.refs_0_), channel_id=1, source_target_pairs={{0,4},{4,0},{8,12},{12,8},{16,20},{20,16},{24,28},{28,24},{1,5},{5... | collective-permute-start | bytes 3797000 | tf_op jit(solution)/shard_map/ppermute | solution.py:143
  153.2 10.4 %collective-permute-start.22 = (bf16[112,768]{1,0:T(8,128)(2,1)S(1)}, bf16[112,768]{1,0:T(8,128)(2,1)S(1)}, u32[]{:S(2)}, u32[]{:S(2)}) collective-permute-start(bf16[112,768]{1,0:T(8,128)(2,1)S(1)} %collective-permute-done.21.refs_7_.refs_2_), channel_id=1, source_target_pairs={{0,1},{1,0},{2,3},{3,2},{4,5},{5,4},{6,7},{7,6},{8,9},{9,8},{10,11... | collective-permute-start | bytes 516104 | tf_op jit(solution)/shard_map/ppermute | solution.py:143
  (19 other events, 106.0 us)

commit v14 on v13

--- a/solution.py
+++ b/solution.py
@@ -1263,7 +1263,8 @@
         dkvs,
         [(total, "v")],
     )
-    keep, send = late_grads(proj_grad, h_one, out_b, branches, [(totals_all[n_tp // 2], "v")])
+    layer_out = stack_parts(totals_all, [(proj_grad, "v"), (branches[1], "v"), (branches[3], "v")])
+    keep, send = late_grads(proj_grad, h_one, out_b, branches, [(layer_out, "h")])
     own, *others = spread(count, (keep, over_cores(send)), (early, early_back))
     summed = total_of(everywhere(parts), F32, flops=2_000_000_000)
     chip_sum = total_of(
@@ -1279,7 +1280,6 @@
     sizes = (3 * width, width, units, 2 * units)
     pair = over_cores(collected)
     begun = begin(collected, sizes)
-    layer_out = stack_parts(totals_all, [(begun[0], "h")])
     grad_qkv, grad_out, grad_down, grad_in, grad_one, grad_two = finish(
         begun, collected, pair, sizes
     )

time: 169 us -> 171 us (1.012); the launches traced: 167 us -> 171 us
  waiting for transfers between devices: 62.1 us -> 76.6 us
  starting transfers between devices: 55.1 us -> 47.6 us
  Pallas kernels: 48.4 us -> 45.3 us
    ppermute x46, waiting for transfers between devices: 62.1 us -> 76.6 us  [swap(): return lax.ppermute(x, axis, [(i, i ^ hop) for i in range(count)])]
    ppermute x46, starting transfers between devices: 55.1 us -> 47.6 us  [swap(): return lax.ppermute(x, axis, [(i, i ^ hop) for i in range(count)])]
    pallas_call x27, Pallas kernels: 48.4 us -> 45.3 us  [call(): pl.pallas_call(run, out_shape=tuple((shaped(shape, dtype) if kind == 'v'...]
  transfers between devices with their start and end apart: 46 -> 46, of which waited for: 21 -> 24; matrix products, arithmetic and copies ran while one was open for 0% -> 0% of each run, Pallas kernels for 26% -> 23%
where the time goes in v14:
time: 171 us
  waiting for transfers between devices  76.6 us (45%)
  starting transfers between devices  47.6 us (28%)
  Pallas kernels  45.3 us (26%)
    ppermute x46, waiting for transfers between devices, swap(): return lax.ppermute(x, axis, [(i, i ^ hop) for i in range(count)])  76.6 us
    ppermute x46, starting transfers between devices, swap(): return lax.ppermute(x, axis, [(i, i ^ hop) for i in range(count)])  47.6 us
    pallas_call x27, Pallas kernels, call(): pl.pallas_call(run, out_shape=tuple((shaped(shape, dtype) if kind == 'v'...  45.3 us
  transfers between devices with their start and end apart: 46, of which 24 were waited for; matrix products, arithmetic and copies ran while one was open for 0% of the time, Pallas kernels for 23%

profile of v14, /device:TPU:0, one launch (start us, length us, event | category | flops | bytes accessed | tf_op | source)
XLA Modules:
  0.0 170.7 jit_solution(16294401976539288273)
XLA Ops:
  1.9 3.1 %collective-permute-start = (bf16[528,768]{1,0:T(8,128)(2,1)S(1)}, bf16[528,768]{1,0:T(8,128)(2,1)S(1)}, u32[]{:S(2)}, u32[]{:S(2)}) collective-permute-start(bf16[528,768]{1,0:T(8,128)(2,1)S(1)} %get-tuple-element.74), channel_id=1, source_target_pairs={{0,1},{1,0},{2,3},{3,2},{4,5},{5,4},{6,7},{7,6},{8,9},{9,8},{10,11... | collective-permute-start | bytes 2433032 | tf_op jit(solution)/shard_map/ppermute | solution.py:143
  5.0 3.7 %project.1 = (bf16[192,448]{1,0:T(8,128)(2,1)S(1)}, bf16[384,448]{1,0:T(8,128)(2,1)S(1)}, bf16[448,768]{1,0:T(8,128)(2,1)S(1)}, f32[32,448]{1,0:T(8,128)S(1)}, f32[32,448]{1,0:T(8,128)S(1)}) custom-call(s32[4]{0:T(128)} %refs_0_.13, s32[8]{0:T(128)} %refs_1_.16, bf16[448,768]{1,0:T(8,128)(2,1)} %refs_0_.15, bf16[576,768]{1,0:T(8,128)(2,1)} %bitcast.15, ...), custom_call_target="tpu_custom_call" | custom-call | tf_op jit(solution)/shard_map/project/pallas_call | solution.py:121
  13.7 2.5 %collective-permute-start.2 = (bf16[96,768]{1,0:T(8,128)(2,1)S(1)}, bf16[96,768]{1,0:T(8,128)(2,1)S(1)}, u32[]{:S(2)}, u32[]{:S(2)}) collective-permute-start(bf16[96,768]{1,0:T(8,128)(2,1)S(1)} %get-tuple-element.75), channel_id=1, source_target_pairs={{0,3},{1,2},{2,1},{3,0},{4,7},{5,6},{6,5},{7,4},{8,11},{9,10},{10,... | collective-permute-start | bytes 442376 | tf_op jit(solution)/shard_map/ppermute | solution.py:143
  16.2 4.6 %collective-permute-done.6.refs_5_.refs_10_ = bf16[384,448]{1,0:T(8,128)(2,1)S(1)} collective-permute-done((bf16[384,448]{1,0:T(8,128)(2,1)S(1)}, bf16[384,448]{1,0:T(8,128)(2,1)S(1)}, u32[]{:S(2)}, u32[]{:S(2)}) %collective-permute-start.6) | collective-permute-done | bytes 344096 | tf_op jit(solution)/shard_map/ppermute | solution.py:143
  20.8 2.6 %collective-permute-start.1 = (bf16[96,768]{1,0:T(8,128)(2,1)S(1)}, bf16[96,768]{1,0:T(8,128)(2,1)S(1)}, u32[]{:S(2)}, u32[]{:S(2)}) collective-permute-start(bf16[96,768]{1,0:T(8,128)(2,1)S(1)} %get-tuple-element.75), channel_id=1, source_target_pairs={{0,2},{1,3},{2,0},{3,1},{4,6},{5,7},{6,4},{7,5},{8,10},{9,11},{10,... | collective-permute-start | bytes 442376 | tf_op jit(solution)/shard_map/ppermute | solution.py:143
  23.4 5.7 %attention_forward.2.refs_6_ = f32[6,80,448]{2,1,0:T(8,128)S(1)} custom-call(s32[4]{0:T(128)} %refs_0_.13, s32[8]{0:T(128)} %refs_1_.16, bf16[192,448]{1,0:T(8,128)(2,1)S(1)} %get-tuple-element.76.refs_2_, bf16[192,448]{1,0:T(8,128)(2,1)S(1)} %collective-permute-done.3.refs_3_, bf16[384,448]{1,0:T(8,128)(2,1)S(1)} %get-tuple-element.77.refs_4_.refs_10_, ...), custom_call_target="tpu_custom_call" | custom-call | tf_op jit(solution)/shard_map/attention_forward/pallas_call | solution.py:121
  34.9 3.0 %collective-permute-done.8.refs_1_ = f32[3,80,448]{2,1,0:T(8,128)S(1)} collective-permute-done((f32[3,80,448]{2,1,0:T(8,128)S(1)}, f32[3,80,448]{2,1,0:T(8,128)S(1)}, u32[]{:S(2)}, u32[]{:S(2)}) %collective-permute-start.8) | collective-permute-done | bytes 430112 | tf_op jit(solution)/shard_map/ppermute | solution.py:143
  38.3 2.6 %collective-permute-start.10 = (bf16[192,224]{1,0:T(8,128)(2,1)S(1)}, bf16[192,224]{1,0:T(8,128)(2,1)S(1)}, u32[]{:S(2)}, u32[]{:S(2)}) collective-permute-start(bf16[192,224]{1,0:T(8,128)(2,1)S(1)} %get-tuple-element.85.refs_6_), channel_id=1, source_target_pairs={{0,2},{1,3},{2,0},{3,1},{4,6},{5,7},{6,4},{7,5},{8,10},{9,11},{10,... | collective-permute-start | bytes 258056 | tf_op jit(solution)/shard_map/ppermute | solution.py:143
  42.7 3.2 %stage.1 = (bf16[224,768]{1,0:T(8,128)(2,1)S(1)}, bf16[224,768]{1,0:T(8,128)(2,1)S(1)}, bf16[768,768]{1,0:T(8,128)(2,1)S(1)}, bf16[1152,768]{1,0:T(8,128)(2,1)S(1)}, bf16[576,768]{1,0:T(8,128)(2,1)S(1)}) custom-call(bf16[448,768]{1,0:T(8,128)(2,1)} %refs_0_.15, bf16[448,768]{1,0:T(8,128)(2,1)} %refs_2_.7, bf16[576,768]{1,0:T(8,128)(2,1)} %bitcast.13, ...), custom_call_target="tpu_custom_call" | custom-call | tf_op jit(solution)/shard_map/stage/pallas_call | solution.py:121
  46.0 2.6 %collective-permute-done.10.refs_8_ = bf16[192,224]{1,0:T(8,128)(2,1)S(1)} collective-permute-done((bf16[192,224]{1,0:T(8,128)(2,1)S(1)}, bf16[192,224]{1,0:T(8,128)(2,1)S(1)}, u32[]{:S(2)}, u32[]{:S(2)}) %collective-permute-start.10) | collective-permute-done | bytes 86048 | tf_op jit(solution)/shard_map/ppermute | solution.py:143
  49.8 4.8 %feed.1 = (f32[224,768]{1,0:T(8,128)S(1)}, f32[112,768]{1,0:T(8,128)S(1)}, bf16[224,768]{1,0:T(8,128)(2,1)S(1)}, bf16[576,224]{1,0:T(8,128)(2,1)S(1)}, bf16[1152...) custom-call(bf16[224,768]{1,0:T(8,128)(2,1)S(1)} %get-tuple-element.79.refs_, ...), custom_call_target="tpu_custom_call" | custom-call | tf_op jit(solution)/shard_map/feed/pallas_call | solution.py:121
  54.5 2.5 %collective-permute-start.15 = (bf16[112,768]{1,0:T(8,128)(2,1)S(1)}, bf16[112,768]{1,0:T(8,128)(2,1)S(1)}, u32[]{:S(2)}, u32[]{:S(2)}) collective-permute-start(bf16[112,768]{1,0:T(8,128)(2,1)S(1)} %get-tuple-element.95), channel_id=1, source_target_pairs={{0,2},{1,3},{2,0},{3,1},{4,6},{5,7},{6,4},{7,5},{8,10},{9,11},{10,... | collective-permute-start | bytes 516104 | tf_op jit(solution)/shard_map/ppermute | solution.py:143
  58.8 6.2 %collective-permute-done.15.refs_5_ = bf16[112,768]{1,0:T(8,128)(2,1)S(1)} collective-permute-done((bf16[112,768]{1,0:T(8,128)(2,1)S(1)}, bf16[112,768]{1,0:T(8,128)(2,1)S(1)}, u32[]{:S(2)}, u32[]{:S(2)}) %collective-permute-start.15) | collective-permute-done | bytes 172064 | tf_op jit(solution)/shard_map/ppermute | solution.py:143
  66.7 2.3 %collective-permute-start.16 = (bf16[112,192]{1,0:T(8,128)(2,1)S(1)}, bf16[112,192]{1,0:T(8,128)(2,1)S(1)}, u32[]{:S(2)}, u32[]{:S(2)}) collective-permute-start(bf16[112,192]{1,0:T(8,128)(2,1)S(1)} %get-tuple-element.97), channel_id=1, source_target_pairs={{0,3},{1,2},{2,1},{3,0},{4,7},{5,6},{6,5},{7,4},{8,11},{9,10},{10,... | collective-permute-start | bytes 129032 | tf_op jit(solution)/shard_map/ppermute | solution.py:143
  69.1 2.1 %collective-permute-start.18 = (bf16[112,192]{1,0:T(8,128)(2,1)S(1)}, bf16[112,192]{1,0:T(8,128)(2,1)S(1)}, u32[]{:S(2)}, u32[]{:S(2)}) collective-permute-start(bf16[112,192]{1,0:T(8,128)(2,1)S(1)} %get-tuple-element.99), channel_id=1, source_target_pairs={{0,1},{1,0},{2,3},{3,2},{4,5},{5,4},{6,7},{7,6},{8,9},{9,8},{10,11... | collective-permute-start | bytes 129032 | tf_op jit(solution)/shard_map/ppermute | solution.py:143
  78.1 3.7 %attention_backward.2 = (bf16[384,448]{1,0:T(8,128)(2,1)S(1)}, bf16[384,448]{1,0:T(8,128)(2,1)S(1)}, bf16[384,448]{1,0:T(8,128)(2,1)S(1)}, f32[6,64,448]{2,1,0:T(8,128)S(1)}) custom-call(s32[4]{0:T(128)} %refs_0_.13, s32[8]{0:T(128)} %refs_1_.16, bf16[192,448]{1,0:T(8,128)(2,1)S(1)} %get-tuple-element.76.refs_2_, ...), custom_call_target="tpu_custom_call" | custom-call | tf_op jit(solution)/shard_map/attention_backward/pallas_call | solution.py:121
  81.9 2.7 %collective-permute-start.26 = (bf16[384,448]{1,0:T(8,128)(2,1)S(1)}, bf16[384,448]{1,0:T(8,128)(2,1)S(1)}, u32[]{:S(2)}, u32[]{:S(2)}) collective-permute-start(bf16[384,448]{1,0:T(8,128)(2,1)S(1)} %get-tuple-element.109), channel_id=1, source_target_pairs={{0,16},{4,20},{8,24},{12,28},{16,0},{20,4},{24,8},{28,12},{1,17},{... | collective-permute-start | bytes 1032200 | tf_op jit(solution)/shard_map/ppermute | solution.py:143
  84.6 6.1 %collective-permute-done.14.refs_1_ = bf16[112,768]{1,0:T(8,128)(2,1)S(1)} collective-permute-done((bf16[112,768]{1,0:T(8,128)(2,1)S(1)}, bf16[112,768]{1,0:T(8,128)(2,1)S(1)}, u32[]{:S(2)}, u32[]{:S(2)}) %collective-permute-start.14) | collective-permute-done | bytes 172064 | tf_op jit(solution)/shard_map/ppermute | solution.py:143
  90.7 3.2 %collective-permute-done.20.refs_3_.refs_5_ = bf16[112,768]{1,0:T(8,128)(2,1)S(1)} collective-permute-done((bf16[112,768]{1,0:T(8,128)(2,1)S(1)}, bf16[112,768]{1,0:T(8,128)(2,1)S(1)}, u32[]{:S(2)}, u32[]{:S(2)}) %collective-permute-start.20) | collective-permute-done | bytes 172064 | tf_op jit(solution)/shard_map/ppermute | solution.py:143
  94.1 5.2 %attention_backward.3 = (f32[384,448]{1,0:T(8,128)S(1)}, f32[192,448]{1,0:T(8,128)S(1)}, bf16[192,448]{1,0:T(8,128)(2,1)S(1)}) custom-call(s32[4]{0:T(128)} %refs_0_.13, s32[8]{0:T(128)} %refs_1_.16, bf16[192,448]{1,0:T(8,128)(2,1)S(1)} %get-tuple-element.76.refs_2_, bf16[192,448]{1,0:T(8,128)(2,1)S(1)} %collective-permute-done.3.refs_3_, ...), custom_call_target="tpu_custom_call" | custom-call | tf_op jit(solution)/shard_map/attention_backward/pallas_call | solution.py:121
  100.4 4.2 %collective-permute-done.21.refs_2_ = bf16[112,768]{1,0:T(8,128)(2,1)S(1)} collective-permute-done((bf16[112,768]{1,0:T(8,128)(2,1)S(1)}, bf16[112,768]{1,0:T(8,128)(2,1)S(1)}, u32[]{:S(2)}, u32[]{:S(2)}) %collective-permute-start.21) | collective-permute-done | bytes 172064 | tf_op jit(solution)/shard_map/ppermute | solution.py:143
  110.9 2.5 %unproject.1 = (bf16[576,448]{1,0:T(8,128)(2,1)S(1)}, f32[128,768]{1,0:T(8,128)S(1)}, bf16[128,768]{1,0:T(8,128)(2,1)S(1)}, bf16[128,768]{1,0:T(8,128)(2,1)S(1)}, bf16[128,768]{1,0:T(8,128)(2,1)S(1)}) custom-call(bf16[448,768]{1,0:T(8,128)(2,1)S(1)} %copy-done, bf16[576,768]{1,0:T(8,128)(2,1)S(1)} %bitcast.16, f32[32,448]{1,0:T(8,128)S(1)} %get-tuple-element.102.refs_2_, ...), custom_call_target="tpu_custom_call" | custom-call | tf_op jit(solution)/shard_map/unproject/pallas_call | solution.py:121
  113.4 2.2 %collective-permute-done.28.refs_5_.refs_4_ = bf16[112,768]{1,0:T(8,128)(2,1)S(1)} collective-permute-done((bf16[112,768]{1,0:T(8,128)(2,1)S(1)}, bf16[112,768]{1,0:T(8,128)(2,1)S(1)}, u32[]{:S(2)}, u32[]{:S(2)}) %collective-permute-start.28) | collective-permute-done | bytes 172064 | tf_op jit(solution)/shard_map/ppermute | solution.py:143
  115.6 3.7 %collective-permute-done.23.refs_3_ = bf16[112,768]{1,0:T(8,128)(2,1)S(1)} collective-permute-done((bf16[112,768]{1,0:T(8,128)(2,1)S(1)}, bf16[112,768]{1,0:T(8,128)(2,1)S(1)}, u32[]{:S(2)}, u32[]{:S(2)}) %collective-permute-start.23) | collective-permute-done | bytes 172064 | tf_op jit(solution)/shard_map/ppermute | solution.py:143
  123.3 3.0 %collective-permute-start.30 = (bf16[128,768]{1,0:T(8,128)(2,1)S(1)}, bf16[128,768]{1,0:T(8,128)(2,1)S(1)}, u32[]{:S(2)}, u32[]{:S(2)}) collective-permute-start(bf16[128,768]{1,0:T(8,128)(2,1)S(1)} %get-tuple-element.114), channel_id=1, source_target_pairs={{0,3},{1,2},{2,1},{3,0},{4,7},{5,6},{6,5},{7,4},{8,11},{9,10},{10,... | collective-permute-start | bytes 589832 | tf_op jit(solution)/shard_map/ppermute | solution.py:143
  129.6 3.4 %collective-permute-done.30.refs_1_ = bf16[128,768]{1,0:T(8,128)(2,1)S(1)} collective-permute-done((bf16[128,768]{1,0:T(8,128)(2,1)S(1)}, bf16[128,768]{1,0:T(8,128)(2,1)S(1)}, u32[]{:S(2)}, u32[]{:S(2)}) %collective-permute-start.30) | collective-permute-done | bytes 196640 | tf_op jit(solution)/shard_map/ppermute | solution.py:143
  133.0 10.2 %collective-permute-done.31.refs_2_ = bf16[128,768]{1,0:T(8,128)(2,1)S(1)} collective-permute-done((bf16[128,768]{1,0:T(8,128)(2,1)S(1)}, bf16[128,768]{1,0:T(8,128)(2,1)S(1)}, u32[]{:S(2)}, u32[]{:S(2)}) %collective-permute-start.31) | collective-permute-done | bytes 196640 | tf_op jit(solution)/shard_map/ppermute | solution.py:143
  144.7 3.2 %collective-permute-start.37 = (bf16[112,768]{1,0:T(8,128)(2,1)S(1)}, bf16[112,768]{1,0:T(8,128)(2,1)S(1)}, u32[]{:S(2)}, u32[]{:S(2)}) collective-permute-start(bf16[112,768]{1,0:T(8,128)(2,1)S(1)} %get-tuple-element.125.refs_0_), channel_id=1, source_target_pairs={{0,2},{1,3},{2,0},{3,1},{4,6},{5,7},{6,4},{7,5},{8,10},{9,11},{10,... | collective-permute-start | bytes 516104 | tf_op jit(solution)/shard_map/ppermute | solution.py:143
  150.0 3.7 %collective-permute-done.38.refs_3_ = bf16[112,768]{1,0:T(8,128)(2,1)S(1)} collective-permute-done((bf16[112,768]{1,0:T(8,128)(2,1)S(1)}, bf16[112,768]{1,0:T(8,128)(2,1)S(1)}, u32[]{:S(2)}, u32[]{:S(2)}) %collective-permute-start.38) | collective-permute-done | bytes 172064 | tf_op jit(solution)/shard_map/ppermute | solution.py:143
  153.8 6.8 %collective-permute-done.37.refs_2_ = bf16[112,768]{1,0:T(8,128)(2,1)S(1)} collective-permute-done((bf16[112,768]{1,0:T(8,128)(2,1)S(1)}, bf16[112,768]{1,0:T(8,128)(2,1)S(1)}, u32[]{:S(2)}, u32[]{:S(2)}) %collective-permute-start.37) | collective-permute-done | bytes 172064 | tf_op jit(solution)/shard_map/ppermute | solution.py:143
  161.5 3.5 %collective-permute-done.43.refs_2_ = bf16[424,384]{1,0:T(8,128)(2,1)S(1)} collective-permute-done((bf16[424,384]{1,0:T(8,128)(2,1)S(1)}, bf16[424,384]{1,0:T(8,128)(2,1)S(1)}, u32[]{:S(2)}, u32[]{:S(2)}) %collective-permute-start.43) | collective-permute-done | bytes 325664 | tf_op jit(solution)/shard_map/ppermute | solution.py:143
  168.4 2.1 %pair_half.1 = (f32[576,768]{1,0:T(8,128)}, f32[192,768]{1,0:T(8,128)}, f32[288,768]{1,0:T(8,128)}, f32[576,768]{1,0:T(8,128)}, f32[768]{0:T(1024)}, /*index=5*/f32[768]{0:T(1024)}) custom-call(bf16[1648,384]{1,0:T(8,128)(2,1)S(1)} %collect.1.refs_0_, ...), custom_call_target="tpu_custom_call", output_to_operand_aliasing={{0}: (2, {}), {1}: (3, {}), {2}: (4, {}), {3}: (5, {})} | custom-call | tf_op jit(solution)/shard_map/pair_half/pallas_call | solution.py:121
  (97 shorter events, 48.6 us)
Async XLA Ops:
  1.9 30.7 %collective-permute-start = (bf16[528,768]{1,0:T(8,128)(2,1)S(1)}, bf16[528,768]{1,0:T(8,128)(2,1)S(1)}, u32[]{:S(2)}, u32[]{:S(2)}) collective-permute-start(bf16[528,768]{1,0:T(8,128)(2,1)S(1)} %get-tuple-element.74), channel_id=1, source_target_pairs={{0,1},{1,0},{2,3},{3,2},{4,5},{5,4},{6,7},{7,6},{8,9},{9,8},{10,11... | collective-permute-start | bytes 2433032 | tf_op jit(solution)/shard_map/ppermute | solution.py:143
  8.7 12.1 %collective-permute-start.6 = (bf16[384,448]{1,0:T(8,128)(2,1)S(1)}, bf16[384,448]{1,0:T(8,128)(2,1)S(1)}, u32[]{:S(2)}, u32[]{:S(2)}) collective-permute-start(bf16[384,448]{1,0:T(8,128)(2,1)S(1)} %get-tuple-element.77.refs_4_.refs_10_), channel_id=1, source_target_pairs={{0,8},{4,12},{8,0},{12,4},{16,24},{20,28},{24,16},{28,20},{1,9},{5... | collective-permute-start | bytes 1032200 | tf_op jit(solution)/shard_map/ppermute | solution.py:143
  10.3 18.8 %collective-permute-start.5 = (bf16[384,448]{1,0:T(8,128)(2,1)S(1)}, bf16[384,448]{1,0:T(8,128)(2,1)S(1)}, u32[]{:S(2)}, u32[]{:S(2)}) collective-permute-start(bf16[384,448]{1,0:T(8,128)(2,1)S(1)} %get-tuple-element.77.refs_4_.refs_10_), channel_id=1, source_target_pairs={{0,24},{4,28},{8,16},{12,20},{16,8},{20,12},{24,0},{28,4},{1,25},{... | collective-permute-start | bytes 1032200 | tf_op jit(solution)/shard_map/ppermute | solution.py:143
  11.8 18.4 %collective-permute-start.4 = (bf16[384,448]{1,0:T(8,128)(2,1)S(1)}, bf16[384,448]{1,0:T(8,128)(2,1)S(1)}, u32[]{:S(2)}, u32[]{:S(2)}) collective-permute-start(bf16[384,448]{1,0:T(8,128)(2,1)S(1)} %get-tuple-element.77.refs_4_.refs_10_), channel_id=1, source_target_pairs={{0,16},{4,20},{8,24},{12,28},{16,0},{20,4},{24,8},{28,12},{1,17},{... | collective-permute-start | bytes 1032200 | tf_op jit(solution)/shard_map/ppermute | solution.py:143
  13.7 17.8 %collective-permute-start.2 = (bf16[96,768]{1,0:T(8,128)(2,1)S(1)}, bf16[96,768]{1,0:T(8,128)(2,1)S(1)}, u32[]{:S(2)}, u32[]{:S(2)}) collective-permute-start(bf16[96,768]{1,0:T(8,128)(2,1)S(1)} %get-tuple-element.75), channel_id=1, source_target_pairs={{0,3},{1,2},{2,1},{3,0},{4,7},{5,6},{6,5},{7,4},{8,11},{9,10},{10,... | collective-permute-start | bytes 442376 | tf_op jit(solution)/shard_map/ppermute | solution.py:143
  20.8 11.8 %collective-permute-start.1 = (bf16[96,768]{1,0:T(8,128)(2,1)S(1)}, bf16[96,768]{1,0:T(8,128)(2,1)S(1)}, u32[]{:S(2)}, u32[]{:S(2)}) collective-permute-start(bf16[96,768]{1,0:T(8,128)(2,1)S(1)} %get-tuple-element.75), channel_id=1, source_target_pairs={{0,2},{1,3},{2,0},{3,1},{4,6},{5,7},{6,4},{7,5},{8,10},{9,11},{10,... | collective-permute-start | bytes 442376 | tf_op jit(solution)/shard_map/ppermute | solution.py:143
  32.7 10.1 %collective-permute-start.7 = (bf16[720,768]{1,0:T(8,128)(2,1)S(1)}, bf16[720,768]{1,0:T(8,128)(2,1)S(1)}, u32[]{:S(2)}, u32[]{:S(2)}) collective-permute-start(bf16[720,768]{1,0:T(8,128)(2,1)S(1)} %pile.1.refs_5_), channel_id=1, source_target_pairs={{0,4},{4,0},{8,12},{12,8},{16,20},{20,16},{24,28},{28,24},{1,5},{5... | collective-permute-start | bytes 3317768 | tf_op jit(solution)/shard_map/ppermute | solution.py:143
  38.3 10.2 %collective-permute-start.10 = (bf16[192,224]{1,0:T(8,128)(2,1)S(1)}, bf16[192,224]{1,0:T(8,128)(2,1)S(1)}, u32[]{:S(2)}, u32[]{:S(2)}) collective-permute-start(bf16[192,224]{1,0:T(8,128)(2,1)S(1)} %get-tuple-element.85.refs_6_), channel_id=1, source_target_pairs={{0,2},{1,3},{2,0},{3,1},{4,6},{5,7},{6,4},{7,5},{8,10},{9,11},{10,... | collective-permute-start | bytes 258056 | tf_op jit(solution)/shard_map/ppermute | solution.py:143
  42.7 15.5 %collective-permute-start.12 = (bf16[192,448]{1,0:T(8,128)(2,1)S(1)}, bf16[192,448]{1,0:T(8,128)(2,1)S(1)}, u32[]{:S(2)}, u32[]{:S(2)}) collective-permute-start(bf16[192,448]{1,0:T(8,128)(2,1)S(1)} %get-tuple-element.89.refs_6_.refs_2_), channel_id=1, source_target_pairs={{0,4},{4,0},{8,12},{12,8},{16,20},{20,16},{24,28},{28,24},{1,5},{5... | collective-permute-start | bytes 516104 | tf_op jit(solution)/shard_map/ppermute | solution.py:143
  54.5 10.5 %collective-permute-start.15 = (bf16[112,768]{1,0:T(8,128)(2,1)S(1)}, bf16[112,768]{1,0:T(8,128)(2,1)S(1)}, u32[]{:S(2)}, u32[]{:S(2)}) collective-permute-start(bf16[112,768]{1,0:T(8,128)(2,1)S(1)} %get-tuple-element.95), channel_id=1, source_target_pairs={{0,2},{1,3},{2,0},{3,1},{4,6},{5,7},{6,4},{7,5},{8,10},{9,11},{10,... | collective-permute-start | bytes 516104 | tf_op jit(solution)/shard_map/ppermute | solution.py:143
  71.2 28.1 %collective-permute-start.34 = (bf16[224,768]{1,0:T(8,128)(2,1)S(1)}, bf16[224,768]{1,0:T(8,128)(2,1)S(1)}, u32[]{:S(2)}, u32[]{:S(2)}) collective-permute-start(bf16[224,768]{1,0:T(8,128)(2,1)S(1)} %get-tuple-element.121.refs_3_), channel_id=1, source_target_pairs={{0,1},{1,0},{2,3},{3,2},{4,5},{5,4},{6,7},{7,6},{8,9},{9,8},{10,11... | collective-permute-start | bytes 1032200 | tf_op jit(solution)/shard_map/ppermute | solution.py:143
  75.1 15.6 %collective-permute-start.14 = (bf16[112,768]{1,0:T(8,128)(2,1)S(1)}, bf16[112,768]{1,0:T(8,128)(2,1)S(1)}, u32[]{:S(2)}, u32[]{:S(2)}) collective-permute-start(bf16[112,768]{1,0:T(8,128)(2,1)S(1)} %get-tuple-element.92), channel_id=1, source_target_pairs={{0,2},{1,3},{2,0},{3,1},{4,6},{5,7},{6,4},{7,5},{8,10},{9,11},{10,... | collective-permute-start | bytes 516104 | tf_op jit(solution)/shard_map/ppermute | solution.py:143
  77.2 16.7 %collective-permute-start.20 = (bf16[112,768]{1,0:T(8,128)(2,1)S(1)}, bf16[112,768]{1,0:T(8,128)(2,1)S(1)}, u32[]{:S(2)}, u32[]{:S(2)}) collective-permute-start(bf16[112,768]{1,0:T(8,128)(2,1)S(1)} %get-tuple-element.101.refs_3_.refs_7_), channel_id=1, source_target_pairs={{0,2},{1,3},{2,0},{3,1},{4,6},{5,7},{6,4},{7,5},{8,10},{9,11},{10,... | collective-permute-start | bytes 516104 | tf_op jit(solution)/shard_map/ppermute | solution.py:143
  81.8 24.9 %collective-permute-start.25 = (bf16[384,448]{1,0:T(8,128)(2,1)S(1)}, bf16[384,448]{1,0:T(8,128)(2,1)S(1)}, u32[]{:S(2)}, u32[]{:S(2)}) collective-permute-start(bf16[384,448]{1,0:T(8,128)(2,1)S(1)} %get-tuple-element.108), channel_id=1, source_target_pairs={{0,8},{4,12},{8,0},{12,4},{16,24},{20,28},{24,16},{28,20},{1,9},{5... | collective-permute-start | bytes 1032200 | tf_op jit(solution)/shard_map/ppermute | solution.py:143
  81.9 24.8 %collective-permute-start.26 = (bf16[384,448]{1,0:T(8,128)(2,1)S(1)}, bf16[384,448]{1,0:T(8,128)(2,1)S(1)}, u32[]{:S(2)}, u32[]{:S(2)}) collective-permute-start(bf16[384,448]{1,0:T(8,128)(2,1)S(1)} %get-tuple-element.109), channel_id=1, source_target_pairs={{0,16},{4,20},{8,24},{12,28},{16,0},{20,4},{24,8},{28,12},{1,17},{... | collective-permute-start | bytes 1032200 | tf_op jit(solution)/shard_map/ppermute | solution.py:143
  90.7 20.1 %collective-permute-start.27 = (bf16[384,448]{1,0:T(8,128)(2,1)S(1)}, bf16[384,448]{1,0:T(8,128)(2,1)S(1)}, u32[]{:S(2)}, u32[]{:S(2)}) collective-permute-start(bf16[384,448]{1,0:T(8,128)(2,1)S(1)} %get-tuple-element.110), channel_id=1, source_target_pairs={{0,24},{4,28},{8,16},{12,20},{16,8},{20,12},{24,0},{28,4},{1,25},{... | collective-permute-start | bytes 1032200 | tf_op jit(solution)/shard_map/ppermute | solution.py:143
  94.0 10.6 %collective-permute-start.21 = (bf16[112,768]{1,0:T(8,128)(2,1)S(1)}, bf16[112,768]{1,0:T(8,128)(2,1)S(1)}, u32[]{:S(2)}, u32[]{:S(2)}) collective-permute-start(bf16[112,768]{1,0:T(8,128)(2,1)S(1)} %total_of.3.refs_11_.refs_0_), channel_id=1, source_target_pairs={{0,2},{1,3},{2,0},{3,1},{4,6},{5,7},{6,4},{7,5},{8,10},{9,11},{10,... | collective-permute-start | bytes 516104 | tf_op jit(solution)/shard_map/ppermute | solution.py:143
  104.6 11.0 %collective-permute-start.28 = (bf16[112,768]{1,0:T(8,128)(2,1)S(1)}, bf16[112,768]{1,0:T(8,128)(2,1)S(1)}, u32[]{:S(2)}, u32[]{:S(2)}) collective-permute-start(bf16[112,768]{1,0:T(8,128)(2,1)S(1)} %collective-permute-done.20.refs_3_.refs_5_), channel_id=1, source_target_pairs={{0,1},{1,0},{2,3},{3,2},{4,5},{5,4},{6,7},{7,6},{8,9},{9,8},{10,11... | collective-permute-start | bytes 516104 | tf_op jit(solution)/shard_map/ppermute | solution.py:143
  106.6 12.7 %collective-permute-start.23 = (bf16[112,768]{1,0:T(8,128)(2,1)S(1)}, bf16[112,768]{1,0:T(8,128)(2,1)S(1)}, u32[]{:S(2)}, u32[]{:S(2)}) collective-permute-start(bf16[112,768]{1,0:T(8,128)(2,1)S(1)} %total_of.3.refs_11_.refs_0_), channel_id=1, source_target_pairs={{0,1},{1,0},{2,3},{3,2},{4,5},{5,4},{6,7},{7,6},{8,9},{9,8},{10,11... | collective-permute-start | bytes 516104 | tf_op jit(solution)/shard_map/ppermute | solution.py:143
  106.7 14.5 %collective-permute-start.22 = (bf16[112,768]{1,0:T(8,128)(2,1)S(1)}, bf16[112,768]{1,0:T(8,128)(2,1)S(1)}, u32[]{:S(2)}, u32[]{:S(2)}) collective-permute-start(bf16[112,768]{1,0:T(8,128)(2,1)S(1)} %collective-permute-done.21.refs_2_), channel_id=1, source_target_pairs={{0,1},{1,0},{2,3},{3,2},{4,5},{5,4},{6,7},{7,6},{8,9},{9,8},{10,11... | collective-permute-start | bytes 516104 | tf_op jit(solution)/shard_map/ppermute | solution.py:143
  110.8 16.9 %collective-permute-start.35 = (bf16[864,384]{1,0:T(8,128)(2,1)S(1)}, bf16[864,384]{1,0:T(8,128)(2,1)S(1)}, u32[]{:S(2)}, u32[]{:S(2)}) collective-permute-start(bf16[864,384]{1,0:T(8,128)(2,1)S(1)} %get-tuple-element.123), channel_id=1, source_target_pairs={{0,4},{4,0},{8,12},{12,8},{16,20},{20,16},{24,28},{28,24},{1,5},{5... | collective-permute-start | bytes 1990664 | tf_op jit(solution)/shard_map/ppermute | solution.py:143
  123.3 9.7 %collective-permute-start.30 = (bf16[128,768]{1,0:T(8,128)(2,1)S(1)}, bf16[128,768]{1,0:T(8,128)(2,1)S(1)}, u32[]{:S(2)}, u32[]{:S(2)}) collective-permute-start(bf16[128,768]{1,0:T(8,128)(2,1)S(1)} %get-tuple-element.114), channel_id=1, source_target_pairs={{0,3},{1,2},{2,1},{3,0},{4,7},{5,6},{6,5},{7,4},{8,11},{9,10},{10,... | collective-permute-start | bytes 589832 | tf_op jit(solution)/shard_map/ppermute | solution.py:143
  126.3 17.0 %collective-permute-start.31 = (bf16[128,768]{1,0:T(8,128)(2,1)S(1)}, bf16[128,768]{1,0:T(8,128)(2,1)S(1)}, u32[]{:S(2)}, u32[]{:S(2)}) collective-permute-start(bf16[128,768]{1,0:T(8,128)(2,1)S(1)} %get-tuple-element.115), channel_id=1, source_target_pairs={{0,2},{1,3},{2,0},{3,1},{4,6},{5,7},{6,4},{7,5},{8,10},{9,11},{10,... | collective-permute-start | bytes 589832 | tf_op jit(solution)/shard_map/ppermute | solution.py:143
  126.3 17.0 %collective-permute-start.32 = (bf16[128,768]{1,0:T(8,128)(2,1)S(1)}, bf16[128,768]{1,0:T(8,128)(2,1)S(1)}, u32[]{:S(2)}, u32[]{:S(2)}) collective-permute-start(bf16[128,768]{1,0:T(8,128)(2,1)S(1)} %get-tuple-element.116), channel_id=1, source_target_pairs={{0,1},{1,0},{2,3},{3,2},{4,5},{5,4},{6,7},{7,6},{8,9},{9,8},{10,11... | collective-permute-start | bytes 589832 | tf_op jit(solution)/shard_map/ppermute | solution.py:143
  128.2 19.7 %collective-permute-start.39 = (bf16[408,384]{1,0:T(8,128)(2,1)S(1)}, bf16[408,384]{1,0:T(8,128)(2,1)S(1)}, u32[]{:S(2)}, u32[]{:S(2)}) collective-permute-start(bf16[408,384]{1,0:T(8,128)(2,1)S(1)} %get-tuple-element.127), channel_id=1, source_target_pairs={{0,24},{4,28},{8,16},{12,20},{16,8},{20,12},{24,0},{28,4},{1,25},{... | collective-permute-start | bytes 940040 | tf_op jit(solution)/shard_map/ppermute | solution.py:143
  128.7 20.4 %collective-permute-start.40 = (bf16[408,384]{1,0:T(8,128)(2,1)S(1)}, bf16[408,384]{1,0:T(8,128)(2,1)S(1)}, u32[]{:S(2)}, u32[]{:S(2)}) collective-permute-start(bf16[408,384]{1,0:T(8,128)(2,1)S(1)} %get-tuple-element.128), channel_id=1, source_target_pairs={{0,16},{4,20},{8,24},{12,28},{16,0},{20,4},{24,8},{28,12},{1,17},{... | collective-permute-start | bytes 940040 | tf_op jit(solution)/shard_map/ppermute | solution.py:143
  133.0 16.1 %collective-permute-start.41 = (bf16[408,384]{1,0:T(8,128)(2,1)S(1)}, bf16[408,384]{1,0:T(8,128)(2,1)S(1)}, u32[]{:S(2)}, u32[]{:S(2)}) collective-permute-start(bf16[408,384]{1,0:T(8,128)(2,1)S(1)} %get-tuple-element.129), channel_id=1, source_target_pairs={{0,8},{4,12},{8,0},{12,4},{16,24},{20,28},{24,16},{28,20},{1,9},{5... | collective-permute-start | bytes 940040 | tf_op jit(solution)/shard_map/ppermute | solution.py:143
  144.7 15.8 %collective-permute-start.37 = (bf16[112,768]{1,0:T(8,128)(2,1)S(1)}, bf16[112,768]{1,0:T(8,128)(2,1)S(1)}, u32[]{:S(2)}, u32[]{:S(2)}) collective-permute-start(bf16[112,768]{1,0:T(8,128)(2,1)S(1)} %get-tuple-element.125.refs_0_), channel_id=1, source_target_pairs={{0,2},{1,3},{2,0},{3,1},{4,6},{5,7},{6,4},{7,5},{8,10},{9,11},{10,... | collective-permute-start | bytes 516104 | tf_op jit(solution)/shard_map/ppermute | solution.py:143
  147.9 12.6 %collective-permute-start.36 = (bf16[112,768]{1,0:T(8,128)(2,1)S(1)}, bf16[112,768]{1,0:T(8,128)(2,1)S(1)}, u32[]{:S(2)}, u32[]{:S(2)}) collective-permute-start(bf16[112,768]{1,0:T(8,128)(2,1)S(1)} %get-tuple-element.125.refs_0_), channel_id=1, source_target_pairs={{0,3},{1,2},{2,1},{3,0},{4,7},{5,6},{6,5},{7,4},{8,11},{9,10},{10,... | collective-permute-start | bytes 516104 | tf_op jit(solution)/shard_map/ppermute | solution.py:143
  149.3 12.2 %collective-permute-start.44 = (bf16[424,384]{1,0:T(8,128)(2,1)S(1)}, bf16[424,384]{1,0:T(8,128)(2,1)S(1)}, u32[]{:S(2)}, u32[]{:S(2)}) collective-permute-start(bf16[424,384]{1,0:T(8,128)(2,1)S(1)} %sum_piece.1.refs_0_), channel_id=1, source_target_pairs={{0,8},{4,12},{8,0},{12,4},{16,24},{20,28},{24,16},{28,20},{1,9},{5... | collective-permute-start | bytes 976904 | tf_op jit(solution)/shard_map/ppermute | solution.py:143
  149.4 15.6 %collective-permute-start.43 = (bf16[424,384]{1,0:T(8,128)(2,1)S(1)}, bf16[424,384]{1,0:T(8,128)(2,1)S(1)}, u32[]{:S(2)}, u32[]{:S(2)}) collective-permute-start(bf16[424,384]{1,0:T(8,128)(2,1)S(1)} %sum_piece.1.refs_0_), channel_id=1, source_target_pairs={{0,16},{4,20},{8,24},{12,28},{16,0},{20,4},{24,8},{28,12},{1,17},{... | collective-permute-start | bytes 976904 | tf_op jit(solution)/shard_map/ppermute | solution.py:143
  153.7 11.3 %collective-permute-start.42 = (bf16[424,384]{1,0:T(8,128)(2,1)S(1)}, bf16[424,384]{1,0:T(8,128)(2,1)S(1)}, u32[]{:S(2)}, u32[]{:S(2)}) collective-permute-start(bf16[424,384]{1,0:T(8,128)(2,1)S(1)} %sum_piece.1.refs_0_), channel_id=1, source_target_pairs={{0,24},{4,28},{8,16},{12,20},{16,8},{20,12},{24,0},{28,4},{1,25},{... | collective-permute-start | bytes 976904 | tf_op jit(solution)/shard_map/ppermute | solution.py:143
  (19 other events, 123.2 us)

commit v15 on v12

--- a/solution.py
+++ b/solution.py
@@ -781,22 +781,26 @@
     return out
 
 
-def stack_kernel(n_tp, *refs):
-    out_ref = refs[n_tp]
-    part = refs[0].shape[0]
+def lay_rows(out_ref, n_tp, places, refs):
+    part = out_ref.shape[0] // n_tp
     tp = lax.axis_index("tp")
-    for k in range(n_tp):
-        at = pl.ds(pl.multiple_of(slot(tp ^ hop(k, n_tp), n_tp) * part, part), part)
-        out_ref[at, :] = refs[k][...]
-
-
-def stack_parts(pieces, after=(), flops=0):
+    for ks, ref in zip(places, refs):
+        for n, k in enumerate(ks):
+            at = pl.ds(pl.multiple_of(slot(tp ^ k, n_tp) * part, part), part)
+            out_ref[at, :] = ref[n * part : (n + 1) * part, :]
+
+
+def stack_kernel(n_tp, places, *refs):
+    lay_rows(refs[-1], n_tp, places, refs[:-1])
+
+
+def stack_parts(n_tp, pieces, places, after=(), flops=0):
     part, model = pieces[0].shape
     (out,) = call(
         "stack_parts",
-        functools.partial(stack_kernel, len(pieces)),
+        functools.partial(stack_kernel, n_tp, places),
         kinds(pieces, "v"),
-        [((part * len(pieces), model), pieces[0].dtype, "h")],
+        [((part * n_tp, model), pieces[0].dtype, "h")],
         (),
         16,
         after,
@@ -937,29 +941,25 @@
     )
 
 
-def late_kernel(n_tp, proj_ref, h_ref, out_ref, *refs):
-    branch_refs = refs[:n_tp]
-    keep_ref, send_ref, branch_full = refs[n_tp:]
-    part = branch_refs[0].shape[0]
+def late_kernel(n_tp, places, proj_ref, h_ref, out_ref, *refs):
+    branch_refs = refs[: len(places)]
+    keep_ref, send_ref, branch_full = refs[len(places) :]
     half = keep_ref.shape[1]
     wide = proj_ref.shape[0]
-    tp = lax.axis_index("tp")
     core = lax.axis_index("seq") % 2
-    for k in range(n_tp):
-        at = pl.ds(pl.multiple_of(slot(tp ^ hop(k, n_tp), n_tp) * part, part), part)
-        branch_full[at, :] = branch_refs[k][...]
+    lay_rows(branch_full, n_tp, places, branch_refs)
     for ref, side in ((send_ref, 1 - core), (keep_ref, core)):
         columns = pl.ds(pl.multiple_of(side * half, half), half)
         ref[:wide, :] = mm(proj_ref[...], h_ref[:, columns], NN).astype(ref.dtype)
         ref[wide:, :] = mm(out_ref[...], branch_full[:, columns], NN).astype(ref.dtype)
 
 
-def late_grads(proj_grad, h_one, out_b, branches, after):
+def late_grads(n_tp, proj_grad, h_one, out_b, branches, places, after):
     rows, model = h_one.shape
     wide = proj_grad.shape[0] + out_b.shape[0]
     return call(
         "late_grads",
-        functools.partial(late_kernel, len(branches)),
+        functools.partial(late_kernel, n_tp, places),
         [(proj_grad, "v"), (h_one, "v"), (out_b, "v"), (branches[0], "v")]
         + kinds(branches[1:], "v"),
         [((wide, model // 2), F32, "v"), ((wide, model // 2), BF16, "v")],
@@ -1182,13 +1182,14 @@
     everywhere = lambda xs: [xs[0]] + came(n_tp, lambda k: over_tp(xs[k], k))
 
     def by_steps(part):
-        parts = {0: part}
-        step = n_tp // 2
+        held, places, step = [part], [(0,)], n_tp // 2
         while step:
-            parts.update({k ^ step: over_tp(x, step) for k, x in parts.items()})
-            step //= 2
-        return [parts[hop(n, n_tp)] for n in range(n_tp)]
-
+            joined = pile(held, ()) if len(held) > 1 else part
+            ks = tuple(k ^ step for group in places for k in group)
+            held, places, step = held + [over_tp(joined, step)], places + [ks], step // 2
+        return held, tuple(places)
+
+    singly = tuple((hop(n, n_tp),) for n in range(n_tp))
     docs = (doc_lengths, roster)
 
     queries, kv, h_one, cos_table, sin_table = project(*docs, tokens, gain_one, qkv_t)
@@ -1223,7 +1224,7 @@
     early_back = over_cores(early_send)
     out_grad = lay_turned(everywhere(pieces), ())
     grad_pair = over_cores(out_grad)
-    branches = by_steps(branch_grad)
+    branches, branch_places = by_steps(branch_grad)
 
     held = (queries, q_pair, out_grad, grad_pair, out_b, out_pair, totals, totals_pair)
     *terms, dq = attention_backward(1, False, *docs, held, blocks[1:], None)
@@ -1231,9 +1232,9 @@
         [own] + [over_tp(others[n], 2 * n + 2) for n in range(n_tp // 2 - 1)],
         BF16,
         "v",
-        [(dq, "v"), (branches[2], "v")],
-    )
-    totals_all = by_steps(total)
+        [(dq, "v"), (branches[1], "v")],
+    )
+    totals_all, total_places = by_steps(total)
 
     dkv, dq_own, dq_pair = attention_backward(
         0, True, *docs, held, blocks[:1], dq, ()
@@ -1252,17 +1253,20 @@
         dkvs,
         [(total, "v")],
     )
-    layer_out = stack_parts(totals_all)
-    keep, send = late_grads(proj_grad, h_one, out_b, branches, [(totals_all[n_tp // 2], "v")])
+    layer_out = stack_parts(n_tp, totals_all, total_places)
+    keep, send = late_grads(
+        n_tp, proj_grad, h_one, out_b, branches, branch_places, [(totals_all[1], "v")]
+    )
     own, *others = spread(count, (keep, over_cores(send)), (early, early_back))
-    summed = total_of(everywhere(parts), F32, flops=2_000_000_000)
+    ways = everywhere(parts)
+    summed = total_of([ways[0]] + [ways[i] for i in (1, 3, 2)], F32, flops=2_000_000_000)
     chip_sum = total_of(
         [own] + came(count, lambda k: over_chips(others[k - 1], k)), F32, "v", ()
     )
     input_part, gains = input_side(tokens, gain_one, middle_grad, summed, [(own, "v")])
     inputs_all = everywhere([input_part] * n_tp)
     piece = sum_piece(gains, [chip_sum], ())
-    input_grad = stack_parts(inputs_all, (), 3_000_000_000)
+    input_grad = stack_parts(n_tp, inputs_all, singly, (), 3_000_000_000)
     collected = collect(
         [piece] + came(count, lambda k: over_chips(piece, k)), [(input_grad, "h"), (layer_out, "h")]
     )

time: 167 us -> 161 us (0.964)
  waiting for transfers between devices: 62.6 us -> 56.9 us
    ppermute x46 -> x44, waiting for transfers between devices: 62.6 us -> 56.9 us  [swap(): return lax.ppermute(x, axis, [(i, i ^ hop) for i in range(count)])]
    ppermute x46 -> x44, starting transfers between devices: 49.2 us -> 47.8 us  [swap(): return lax.ppermute(x, axis, [(i, i ^ hop) for i in range(count)])]
    pallas_call x27 -> x29, Pallas kernels: 54.8 us -> 54.9 us  [call(): pl.pallas_call(run, out_shape=tuple((shaped(shape, dtype) if kind == 'v'...]
  transfers between devices with their start and end apart: 46 -> 44, of which waited for: 21 -> 20; matrix products, arithmetic and copies ran while one was open for 0% -> 0% of each run, Pallas kernels for 29% -> 32%
where the time goes in v15:
time: 161 us
  waiting for transfers between devices  56.9 us (35%)
  Pallas kernels  54.9 us (34%)
  starting transfers between devices  47.8 us (30%)
    ppermute x44, waiting for transfers between devices, swap(): return lax.ppermute(x, axis, [(i, i ^ hop) for i in range(count)])  56.9 us
    pallas_call x29, Pallas kernels, call(): pl.pallas_call(run, out_shape=tuple((shaped(shape, dtype) if kind == 'v'...  54.9 us
    ppermute x44, starting transfers between devices, swap(): return lax.ppermute(x, axis, [(i, i ^ hop) for i in range(count)])  47.8 us
  transfers between devices with their start and end apart: 44, of which 20 were waited for; matrix products, arithmetic and copies ran while one was open for 0% of the time, Pallas kernels for 32%

profile of v15, /device:TPU:0, one launch (start us, length us, event | category | flops | bytes accessed | tf_op | source)
XLA Modules:
  0.0 161.0 jit_solution(4923341039579206060)
XLA Ops:
  1.9 3.1 %collective-permute-start = (bf16[528,768]{1,0:T(8,128)(2,1)S(1)}, bf16[528,768]{1,0:T(8,128)(2,1)S(1)}, u32[]{:S(2)}, u32[]{:S(2)}) collective-permute-start(bf16[528,768]{1,0:T(8,128)(2,1)S(1)} %get-tuple-element.74), channel_id=1, source_target_pairs={{0,1},{1,0},{2,3},{3,2},{4,5},{5,4},{6,7},{7,6},{8,9},{9,8},{10,11... | collective-permute-start | bytes 2433032 | tf_op jit(solution)/shard_map/ppermute | solution.py:143
  5.0 3.7 %project.1 = (bf16[192,448]{1,0:T(8,128)(2,1)S(1)}, bf16[384,448]{1,0:T(8,128)(2,1)S(1)}, bf16[448,768]{1,0:T(8,128)(2,1)S(1)}, f32[32,448]{1,0:T(8,128)S(1)}, f32[32,448]{1,0:T(8,128)S(1)}) custom-call(s32[4]{0:T(128)} %refs_0_.13, s32[8]{0:T(128)} %refs_1_.16, bf16[448,768]{1,0:T(8,128)(2,1)} %refs_0_.15, bf16[576,768]{1,0:T(8,128)(2,1)} %bitcast.15, ...), custom_call_target="tpu_custom_call" | custom-call | tf_op jit(solution)/shard_map/project/pallas_call | solution.py:121
  13.7 2.5 %collective-permute-start.2 = (bf16[96,768]{1,0:T(8,128)(2,1)S(1)}, bf16[96,768]{1,0:T(8,128)(2,1)S(1)}, u32[]{:S(2)}, u32[]{:S(2)}) collective-permute-start(bf16[96,768]{1,0:T(8,128)(2,1)S(1)} %get-tuple-element.75), channel_id=1, source_target_pairs={{0,3},{1,2},{2,1},{3,0},{4,7},{5,6},{6,5},{7,4},{8,11},{9,10},{10,... | collective-permute-start | bytes 442376 | tf_op jit(solution)/shard_map/ppermute | solution.py:143
  16.2 4.6 %collective-permute-done.6.refs_5_.refs_10_ = bf16[384,448]{1,0:T(8,128)(2,1)S(1)} collective-permute-done((bf16[384,448]{1,0:T(8,128)(2,1)S(1)}, bf16[384,448]{1,0:T(8,128)(2,1)S(1)}, u32[]{:S(2)}, u32[]{:S(2)}) %collective-permute-start.6) | collective-permute-done | bytes 344096 | tf_op jit(solution)/shard_map/ppermute | solution.py:143
  20.8 2.6 %collective-permute-start.1 = (bf16[96,768]{1,0:T(8,128)(2,1)S(1)}, bf16[96,768]{1,0:T(8,128)(2,1)S(1)}, u32[]{:S(2)}, u32[]{:S(2)}) collective-permute-start(bf16[96,768]{1,0:T(8,128)(2,1)S(1)} %get-tuple-element.75), channel_id=1, source_target_pairs={{0,2},{1,3},{2,0},{3,1},{4,6},{5,7},{6,4},{7,5},{8,10},{9,11},{10,... | collective-permute-start | bytes 442376 | tf_op jit(solution)/shard_map/ppermute | solution.py:143
  23.4 7.1 %attention_forward.2.refs_6_ = f32[6,80,448]{2,1,0:T(8,128)S(1)} custom-call(s32[4]{0:T(128)} %refs_0_.13, s32[8]{0:T(128)} %refs_1_.16, bf16[192,448]{1,0:T(8,128)(2,1)S(1)} %get-tuple-element.76.refs_2_, bf16[192,448]{1,0:T(8,128)(2,1)S(1)} %collective-permute-done.3.refs_3_, bf16[384,448]{1,0:T(8,128)(2,1)S(1)} %get-tuple-element.77.refs_4_.refs_10_, ...), custom_call_target="tpu_custom_call" | custom-call | tf_op jit(solution)/shard_map/attention_forward/pallas_call | solution.py:121
  30.6 4.2 %attention_forward.3 = (f32[3,80,448]{2,1,0:T(8,128)S(1)}, f32[3,80,448]{2,1,0:T(8,128)S(1)}) custom-call(s32[4]{0:T(128)} %refs_0_.13, s32[8]{0:T(128)} %refs_1_.16, bf16[192,448]{1,0:T(8,128)(2,1)S(1)} %get-tuple-element.76.refs_2_, bf16[192,448]{1,0:T(8,128)(2,1)S(1)} %collective-permute-done.3.refs_3_, ...), custom_call_target="tpu_custom_call" | custom-call | tf_op jit(solution)/shard_map/attention_forward/pallas_call | solution.py:121
  35.5 2.9 %collective-permute-done.8.refs_1_ = f32[3,80,448]{2,1,0:T(8,128)S(1)} collective-permute-done((f32[3,80,448]{2,1,0:T(8,128)S(1)}, f32[3,80,448]{2,1,0:T(8,128)S(1)}, u32[]{:S(2)}, u32[]{:S(2)}) %collective-permute-start.8) | collective-permute-done | bytes 430112 | tf_op jit(solution)/shard_map/ppermute | solution.py:143
  38.8 2.3 %collective-permute-start.10 = (bf16[192,224]{1,0:T(8,128)(2,1)S(1)}, bf16[192,224]{1,0:T(8,128)(2,1)S(1)}, u32[]{:S(2)}, u32[]{:S(2)}) collective-permute-start(bf16[192,224]{1,0:T(8,128)(2,1)S(1)} %get-tuple-element.85.refs_6_), channel_id=1, source_target_pairs={{0,2},{1,3},{2,0},{3,1},{4,6},{5,7},{6,4},{7,5},{8,10},{9,11},{10,... | collective-permute-start | bytes 258056 | tf_op jit(solution)/shard_map/ppermute | solution.py:143
  43.3 3.2 %stage.1 = (bf16[224,768]{1,0:T(8,128)(2,1)S(1)}, bf16[224,768]{1,0:T(8,128)(2,1)S(1)}, bf16[768,768]{1,0:T(8,128)(2,1)S(1)}, bf16[1152,768]{1,0:T(8,128)(2,1)S(1)}, bf16[576,768]{1,0:T(8,128)(2,1)S(1)}) custom-call(bf16[448,768]{1,0:T(8,128)(2,1)} %refs_0_.15, bf16[448,768]{1,0:T(8,128)(2,1)} %refs_2_.7, bf16[576,768]{1,0:T(8,128)(2,1)} %bitcast.13, ...), custom_call_target="tpu_custom_call" | custom-call | tf_op jit(solution)/shard_map/stage/pallas_call | solution.py:121
  46.5 2.4 %collective-permute-done.10.refs_8_ = bf16[192,224]{1,0:T(8,128)(2,1)S(1)} collective-permute-done((bf16[192,224]{1,0:T(8,128)(2,1)S(1)}, bf16[192,224]{1,0:T(8,128)(2,1)S(1)}, u32[]{:S(2)}, u32[]{:S(2)}) %collective-permute-start.10) | collective-permute-done | bytes 86048 | tf_op jit(solution)/shard_map/ppermute | solution.py:143
  49.8 4.7 %feed.1 = (f32[224,768]{1,0:T(8,128)S(1)}, f32[112,768]{1,0:T(8,128)S(1)}, bf16[224,768]{1,0:T(8,128)(2,1)S(1)}, bf16[576,224]{1,0:T(8,128)(2,1)S(1)}, bf16[1152...) custom-call(bf16[224,768]{1,0:T(8,128)(2,1)S(1)} %get-tuple-element.79.refs_, ...), custom_call_target="tpu_custom_call" | custom-call | tf_op jit(solution)/shard_map/feed/pallas_call | solution.py:121
  54.5 2.5 %collective-permute-start.15 = (bf16[112,768]{1,0:T(8,128)(2,1)S(1)}, bf16[112,768]{1,0:T(8,128)(2,1)S(1)}, u32[]{:S(2)}, u32[]{:S(2)}) collective-permute-start(bf16[112,768]{1,0:T(8,128)(2,1)S(1)} %get-tuple-element.95), channel_id=1, source_target_pairs={{0,2},{1,3},{2,0},{3,1},{4,6},{5,7},{6,4},{7,5},{8,10},{9,11},{10,... | collective-permute-start | bytes 516104 | tf_op jit(solution)/shard_map/ppermute | solution.py:143
  59.3 5.7 %collective-permute-done.15.refs_5_ = bf16[112,768]{1,0:T(8,128)(2,1)S(1)} collective-permute-done((bf16[112,768]{1,0:T(8,128)(2,1)S(1)}, bf16[112,768]{1,0:T(8,128)(2,1)S(1)}, u32[]{:S(2)}, u32[]{:S(2)}) %collective-permute-start.15) | collective-permute-done | bytes 172064 | tf_op jit(solution)/shard_map/ppermute | solution.py:143
  66.7 2.2 %collective-permute-start.16 = (bf16[112,192]{1,0:T(8,128)(2,1)S(1)}, bf16[112,192]{1,0:T(8,128)(2,1)S(1)}, u32[]{:S(2)}, u32[]{:S(2)}) collective-permute-start(bf16[112,192]{1,0:T(8,128)(2,1)S(1)} %get-tuple-element.97), channel_id=1, source_target_pairs={{0,3},{1,2},{2,1},{3,0},{4,7},{5,6},{6,5},{7,4},{8,11},{9,10},{10,... | collective-permute-start | bytes 129032 | tf_op jit(solution)/shard_map/ppermute | solution.py:143
  68.9 2.2 %collective-permute-start.18 = (bf16[112,192]{1,0:T(8,128)(2,1)S(1)}, bf16[112,192]{1,0:T(8,128)(2,1)S(1)}, u32[]{:S(2)}, u32[]{:S(2)}) collective-permute-start(bf16[112,192]{1,0:T(8,128)(2,1)S(1)} %get-tuple-element.99), channel_id=1, source_target_pairs={{0,1},{1,0},{2,3},{3,2},{4,5},{5,4},{6,7},{7,6},{8,9},{9,8},{10,11... | collective-permute-start | bytes 129032 | tf_op jit(solution)/shard_map/ppermute | solution.py:143
  77.4 9.0 %attention_backward.2 = (bf16[384,448]{1,0:T(8,128)(2,1)S(1)}, bf16[384,448]{1,0:T(8,128)(2,1)S(1)}, bf16[384,448]{1,0:T(8,128)(2,1)S(1)}, f32[6,64,448]{2,1,0:T(8,128)S(1)}) custom-call(s32[4]{0:T(128)} %refs_0_.13, s32[8]{0:T(128)} %refs_1_.16, bf16[192,448]{1,0:T(8,128)(2,1)S(1)} %get-tuple-element.76.refs_2_, ...), custom_call_target="tpu_custom_call" | custom-call | tf_op jit(solution)/shard_map/attention_backward/pallas_call | solution.py:121
  86.4 3.0 %collective-permute-start.24 = (bf16[384,448]{1,0:T(8,128)(2,1)S(1)}, bf16[384,448]{1,0:T(8,128)(2,1)S(1)}, u32[]{:S(2)}, u32[]{:S(2)}) collective-permute-start(bf16[384,448]{1,0:T(8,128)(2,1)S(1)} %get-tuple-element.109), channel_id=1, source_target_pairs={{0,8},{4,12},{8,0},{12,4},{16,24},{20,28},{24,16},{28,20},{1,9},{5... | collective-permute-start | bytes 1032200 | tf_op jit(solution)/shard_map/ppermute | solution.py:143
  89.9 2.9 %collective-permute-start.26 = (bf16[384,448]{1,0:T(8,128)(2,1)S(1)}, bf16[384,448]{1,0:T(8,128)(2,1)S(1)}, u32[]{:S(2)}, u32[]{:S(2)}) collective-permute-start(bf16[384,448]{1,0:T(8,128)(2,1)S(1)} %get-tuple-element.111), channel_id=1, source_target_pairs={{0,24},{4,28},{8,16},{12,20},{16,8},{20,12},{24,0},{28,4},{1,25},{... | collective-permute-start | bytes 1032200 | tf_op jit(solution)/shard_map/ppermute | solution.py:143
  92.9 5.0 %attention_backward.3 = (f32[384,448]{1,0:T(8,128)S(1)}, f32[192,448]{1,0:T(8,128)S(1)}, bf16[192,448]{1,0:T(8,128)(2,1)S(1)}) custom-call(s32[4]{0:T(128)} %refs_0_.13, s32[8]{0:T(128)} %refs_1_.16, bf16[192,448]{1,0:T(8,128)(2,1)S(1)} %get-tuple-element.76.refs_2_, bf16[192,448]{1,0:T(8,128)(2,1)S(1)} %collective-permute-done.3.refs_3_, ...), custom_call_target="tpu_custom_call" | custom-call | tf_op jit(solution)/shard_map/attention_backward/pallas_call | solution.py:121
  103.2 2.5 %collective-permute-done.25.refs_9_ = bf16[384,448]{1,0:T(8,128)(2,1)S(1)} collective-permute-done((bf16[384,448]{1,0:T(8,128)(2,1)S(1)}, bf16[384,448]{1,0:T(8,128)(2,1)S(1)}, u32[]{:S(2)}, u32[]{:S(2)}) %collective-permute-start.25) | collective-permute-done | bytes 344096 | tf_op jit(solution)/shard_map/ppermute | solution.py:143
  105.6 2.5 %unproject.1 = (bf16[576,448]{1,0:T(8,128)(2,1)S(1)}, f32[128,768]{1,0:T(8,128)S(1)}, bf16[128,768]{1,0:T(8,128)(2,1)S(1)}, bf16[128,768]{1,0:T(8,128)(2,1)S(1)}, bf16[128,768]{1,0:T(8,128)(2,1)S(1)}) custom-call(bf16[448,768]{1,0:T(8,128)(2,1)S(1)} %copy-done, bf16[576,768]{1,0:T(8,128)(2,1)S(1)} %bitcast.16, f32[32,448]{1,0:T(8,128)S(1)} %get-tuple-element.103.refs_2_, ...), custom_call_target="tpu_custom_call" | custom-call | tf_op jit(solution)/shard_map/unproject/pallas_call | solution.py:121
  110.0 2.2 %collective-permute-done.30.refs_5_ = bf16[224,768]{1,0:T(8,128)(2,1)S(1)} collective-permute-done((bf16[224,768]{1,0:T(8,128)(2,1)S(1)}, bf16[224,768]{1,0:T(8,128)(2,1)S(1)}, u32[]{:S(2)}, u32[]{:S(2)}) %collective-permute-start.30) | collective-permute-done | bytes 344096 | tf_op jit(solution)/shard_map/ppermute | solution.py:143
  115.5 2.3 %collective-permute-start.29 = (bf16[128,768]{1,0:T(8,128)(2,1)S(1)}, bf16[128,768]{1,0:T(8,128)(2,1)S(1)}, u32[]{:S(2)}, u32[]{:S(2)}) collective-permute-start(bf16[128,768]{1,0:T(8,128)(2,1)S(1)} %get-tuple-element.115), channel_id=1, source_target_pairs={{0,2},{1,3},{2,0},{3,1},{4,6},{5,7},{6,4},{7,5},{8,10},{9,11},{10,... | collective-permute-start | bytes 589832 | tf_op jit(solution)/shard_map/ppermute | solution.py:143
  118.4 4.5 %collective-permute-done.27.refs_1_ = bf16[128,768]{1,0:T(8,128)(2,1)S(1)} collective-permute-done((bf16[128,768]{1,0:T(8,128)(2,1)S(1)}, bf16[128,768]{1,0:T(8,128)(2,1)S(1)}, u32[]{:S(2)}, u32[]{:S(2)}) %collective-permute-start.27) | collective-permute-done | bytes 196640 | tf_op jit(solution)/shard_map/ppermute | solution.py:143
  122.9 3.3 %collective-permute-start.22 = (bf16[224,768]{1,0:T(8,128)(2,1)S(1)}, bf16[224,768]{1,0:T(8,128)(2,1)S(1)}, u32[]{:S(2)}, u32[]{:S(2)}) collective-permute-start(bf16[224,768]{1,0:T(8,128)(2,1)S(1)} %pile.4), channel_id=1, source_target_pairs={{0,1},{1,0},{2,3},{3,2},{4,5},{5,4},{6,7},{7,6},{8,9},{9,8},{10,11... | collective-permute-start | bytes 1032200 | tf_op jit(solution)/shard_map/ppermute | solution.py:143
  126.2 2.2 %collective-permute-done.28.refs_2_ = bf16[128,768]{1,0:T(8,128)(2,1)S(1)} collective-permute-done((bf16[128,768]{1,0:T(8,128)(2,1)S(1)}, bf16[128,768]{1,0:T(8,128)(2,1)S(1)}, u32[]{:S(2)}, u32[]{:S(2)}) %collective-permute-start.28) | collective-permute-done | bytes 196640 | tf_op jit(solution)/shard_map/ppermute | solution.py:143
  128.4 5.3 %collective-permute-done.29.refs_3_ = bf16[128,768]{1,0:T(8,128)(2,1)S(1)} collective-permute-done((bf16[128,768]{1,0:T(8,128)(2,1)S(1)}, bf16[128,768]{1,0:T(8,128)(2,1)S(1)}, u32[]{:S(2)}, u32[]{:S(2)}) %collective-permute-start.29) | collective-permute-done | bytes 196640 | tf_op jit(solution)/shard_map/ppermute | solution.py:143
  135.2 2.3 %collective-permute-start.35 = (bf16[112,768]{1,0:T(8,128)(2,1)S(1)}, bf16[112,768]{1,0:T(8,128)(2,1)S(1)}, u32[]{:S(2)}, u32[]{:S(2)}) collective-permute-start(bf16[112,768]{1,0:T(8,128)(2,1)S(1)} %get-tuple-element.125.refs_0_), channel_id=1, source_target_pairs={{0,2},{1,3},{2,0},{3,1},{4,6},{5,7},{6,4},{7,5},{8,10},{9,11},{10,... | collective-permute-start | bytes 516104 | tf_op jit(solution)/shard_map/ppermute | solution.py:143
  140.0 5.0 %collective-permute-done.36.refs_3_ = bf16[112,768]{1,0:T(8,128)(2,1)S(1)} collective-permute-done((bf16[112,768]{1,0:T(8,128)(2,1)S(1)}, bf16[112,768]{1,0:T(8,128)(2,1)S(1)}, u32[]{:S(2)}, u32[]{:S(2)}) %collective-permute-start.36) | collective-permute-done | bytes 172064 | tf_op jit(solution)/shard_map/ppermute | solution.py:143
  145.9 5.0 %collective-permute-done.35.refs_2_ = bf16[112,768]{1,0:T(8,128)(2,1)S(1)} collective-permute-done((bf16[112,768]{1,0:T(8,128)(2,1)S(1)}, bf16[112,768]{1,0:T(8,128)(2,1)S(1)}, u32[]{:S(2)}, u32[]{:S(2)}) %collective-permute-start.35) | collective-permute-done | bytes 172064 | tf_op jit(solution)/shard_map/ppermute | solution.py:143
  151.8 3.5 %collective-permute-done.40.refs_1_ = bf16[424,384]{1,0:T(8,128)(2,1)S(1)} collective-permute-done((bf16[424,384]{1,0:T(8,128)(2,1)S(1)}, bf16[424,384]{1,0:T(8,128)(2,1)S(1)}, u32[]{:S(2)}, u32[]{:S(2)}) %collective-permute-start.40) | collective-permute-done | bytes 325664 | tf_op jit(solution)/shard_map/ppermute | solution.py:143
  (95 shorter events, 43.4 us)
Async XLA Ops:
  1.9 32.9 %collective-permute-start = (bf16[528,768]{1,0:T(8,128)(2,1)S(1)}, bf16[528,768]{1,0:T(8,128)(2,1)S(1)}, u32[]{:S(2)}, u32[]{:S(2)}) collective-permute-start(bf16[528,768]{1,0:T(8,128)(2,1)S(1)} %get-tuple-element.74), channel_id=1, source_target_pairs={{0,1},{1,0},{2,3},{3,2},{4,5},{5,4},{6,7},{7,6},{8,9},{9,8},{10,11... | collective-permute-start | bytes 2433032 | tf_op jit(solution)/shard_map/ppermute | solution.py:143
  8.7 12.1 %collective-permute-start.6 = (bf16[384,448]{1,0:T(8,128)(2,1)S(1)}, bf16[384,448]{1,0:T(8,128)(2,1)S(1)}, u32[]{:S(2)}, u32[]{:S(2)}) collective-permute-start(bf16[384,448]{1,0:T(8,128)(2,1)S(1)} %get-tuple-element.77.refs_4_.refs_10_), channel_id=1, source_target_pairs={{0,8},{4,12},{8,0},{12,4},{16,24},{20,28},{24,16},{28,20},{1,9},{5... | collective-permute-start | bytes 1032200 | tf_op jit(solution)/shard_map/ppermute | solution.py:143
  10.3 20.3 %collective-permute-start.5 = (bf16[384,448]{1,0:T(8,128)(2,1)S(1)}, bf16[384,448]{1,0:T(8,128)(2,1)S(1)}, u32[]{:S(2)}, u32[]{:S(2)}) collective-permute-start(bf16[384,448]{1,0:T(8,128)(2,1)S(1)} %get-tuple-element.77.refs_4_.refs_10_), channel_id=1, source_target_pairs={{0,24},{4,28},{8,16},{12,20},{16,8},{20,12},{24,0},{28,4},{1,25},{... | collective-permute-start | bytes 1032200 | tf_op jit(solution)/shard_map/ppermute | solution.py:143
  11.8 18.8 %collective-permute-start.4 = (bf16[384,448]{1,0:T(8,128)(2,1)S(1)}, bf16[384,448]{1,0:T(8,128)(2,1)S(1)}, u32[]{:S(2)}, u32[]{:S(2)}) collective-permute-start(bf16[384,448]{1,0:T(8,128)(2,1)S(1)} %get-tuple-element.77.refs_4_.refs_10_), channel_id=1, source_target_pairs={{0,16},{4,20},{8,24},{12,28},{16,0},{20,4},{24,8},{28,12},{1,17},{... | collective-permute-start | bytes 1032200 | tf_op jit(solution)/shard_map/ppermute | solution.py:143
  13.7 21.1 %collective-permute-start.2 = (bf16[96,768]{1,0:T(8,128)(2,1)S(1)}, bf16[96,768]{1,0:T(8,128)(2,1)S(1)}, u32[]{:S(2)}, u32[]{:S(2)}) collective-permute-start(bf16[96,768]{1,0:T(8,128)(2,1)S(1)} %get-tuple-element.75), channel_id=1, source_target_pairs={{0,3},{1,2},{2,1},{3,0},{4,7},{5,6},{6,5},{7,4},{8,11},{9,10},{10,... | collective-permute-start | bytes 442376 | tf_op jit(solution)/shard_map/ppermute | solution.py:143
  20.8 14.0 %collective-permute-start.1 = (bf16[96,768]{1,0:T(8,128)(2,1)S(1)}, bf16[96,768]{1,0:T(8,128)(2,1)S(1)}, u32[]{:S(2)}, u32[]{:S(2)}) collective-permute-start(bf16[96,768]{1,0:T(8,128)(2,1)S(1)} %get-tuple-element.75), channel_id=1, source_target_pairs={{0,2},{1,3},{2,0},{3,1},{4,6},{5,7},{6,4},{7,5},{8,10},{9,11},{10,... | collective-permute-start | bytes 442376 | tf_op jit(solution)/shard_map/ppermute | solution.py:143
  38.8 10.0 %collective-permute-start.10 = (bf16[192,224]{1,0:T(8,128)(2,1)S(1)}, bf16[192,224]{1,0:T(8,128)(2,1)S(1)}, u32[]{:S(2)}, u32[]{:S(2)}) collective-permute-start(bf16[192,224]{1,0:T(8,128)(2,1)S(1)} %get-tuple-element.85.refs_6_), channel_id=1, source_target_pairs={{0,2},{1,3},{2,0},{3,1},{4,6},{5,7},{6,4},{7,5},{8,10},{9,11},{10,... | collective-permute-start | bytes 258056 | tf_op jit(solution)/shard_map/ppermute | solution.py:143
  41.1 8.7 %collective-permute-start.11 = (bf16[192,224]{1,0:T(8,128)(2,1)S(1)}, bf16[192,224]{1,0:T(8,128)(2,1)S(1)}, u32[]{:S(2)}, u32[]{:S(2)}) collective-permute-start(bf16[192,224]{1,0:T(8,128)(2,1)S(1)} %get-tuple-element.86), channel_id=1, source_target_pairs={{0,1},{1,0},{2,3},{3,2},{4,5},{5,4},{6,7},{7,6},{8,9},{9,8},{10,11... | collective-permute-start | bytes 258056 | tf_op jit(solution)/shard_map/ppermute | solution.py:143
  43.3 15.4 %collective-permute-start.12 = (bf16[192,448]{1,0:T(8,128)(2,1)S(1)}, bf16[192,448]{1,0:T(8,128)(2,1)S(1)}, u32[]{:S(2)}, u32[]{:S(2)}) collective-permute-start(bf16[192,448]{1,0:T(8,128)(2,1)S(1)} %get-tuple-element.89.refs_6_.refs_2_), channel_id=1, source_target_pairs={{0,4},{4,0},{8,12},{12,8},{16,20},{20,16},{24,28},{28,24},{1,5},{5... | collective-permute-start | bytes 516104 | tf_op jit(solution)/shard_map/ppermute | solution.py:143
  54.5 10.4 %collective-permute-start.15 = (bf16[112,768]{1,0:T(8,128)(2,1)S(1)}, bf16[112,768]{1,0:T(8,128)(2,1)S(1)}, u32[]{:S(2)}, u32[]{:S(2)}) collective-permute-start(bf16[112,768]{1,0:T(8,128)(2,1)S(1)} %get-tuple-element.95), channel_id=1, source_target_pairs={{0,2},{1,3},{2,0},{3,1},{4,6},{5,7},{6,4},{7,5},{8,10},{9,11},{10,... | collective-permute-start | bytes 516104 | tf_op jit(solution)/shard_map/ppermute | solution.py:143
  57.0 41.0 %collective-permute-start.32 = (bf16[224,768]{1,0:T(8,128)(2,1)S(1)}, bf16[224,768]{1,0:T(8,128)(2,1)S(1)}, u32[]{:S(2)}, u32[]{:S(2)}) collective-permute-start(bf16[224,768]{1,0:T(8,128)(2,1)S(1)} %get-tuple-element.121.refs_3_), channel_id=1, source_target_pairs={{0,1},{1,0},{2,3},{3,2},{4,5},{5,4},{6,7},{7,6},{8,9},{9,8},{10,11... | collective-permute-start | bytes 1032200 | tf_op jit(solution)/shard_map/ppermute | solution.py:143
  74.4 15.5 %collective-permute-start.20 = (bf16[112,768]{1,0:T(8,128)(2,1)S(1)}, bf16[112,768]{1,0:T(8,128)(2,1)S(1)}, u32[]{:S(2)}, u32[]{:S(2)}) collective-permute-start(bf16[112,768]{1,0:T(8,128)(2,1)S(1)} %get-tuple-element.101.refs_0_.refs_3_.refs_7_), channel_id=1, source_target_pairs={{0,2},{1,3},{2,0},{3,1},{4,6},{5,7},{6,4},{7,5},{8,10},{9,11},{10,... | collective-permute-start | bytes 516104 | tf_op jit(solution)/shard_map/ppermute | solution.py:143
  76.4 21.6 %collective-permute-start.14 = (bf16[112,768]{1,0:T(8,128)(2,1)S(1)}, bf16[112,768]{1,0:T(8,128)(2,1)S(1)}, u32[]{:S(2)}, u32[]{:S(2)}) collective-permute-start(bf16[112,768]{1,0:T(8,128)(2,1)S(1)} %get-tuple-element.92), channel_id=1, source_target_pairs={{0,2},{1,3},{2,0},{3,1},{4,6},{5,7},{6,4},{7,5},{8,10},{9,11},{10,... | collective-permute-start | bytes 516104 | tf_op jit(solution)/shard_map/ppermute | solution.py:143
  86.4 16.6 %collective-permute-start.24 = (bf16[384,448]{1,0:T(8,128)(2,1)S(1)}, bf16[384,448]{1,0:T(8,128)(2,1)S(1)}, u32[]{:S(2)}, u32[]{:S(2)}) collective-permute-start(bf16[384,448]{1,0:T(8,128)(2,1)S(1)} %get-tuple-element.109), channel_id=1, source_target_pairs={{0,8},{4,12},{8,0},{12,4},{16,24},{20,28},{24,16},{28,20},{1,9},{5... | collective-permute-start | bytes 1032200 | tf_op jit(solution)/shard_map/ppermute | solution.py:143
  89.5 16.2 %collective-permute-start.25 = (bf16[384,448]{1,0:T(8,128)(2,1)S(1)}, bf16[384,448]{1,0:T(8,128)(2,1)S(1)}, u32[]{:S(2)}, u32[]{:S(2)}) collective-permute-start(bf16[384,448]{1,0:T(8,128)(2,1)S(1)} %get-tuple-element.110), channel_id=1, source_target_pairs={{0,16},{4,20},{8,24},{12,28},{16,0},{20,4},{24,8},{28,12},{1,17},{... | collective-permute-start | bytes 1032200 | tf_op jit(solution)/shard_map/ppermute | solution.py:143
  89.9 15.7 %collective-permute-start.26 = (bf16[384,448]{1,0:T(8,128)(2,1)S(1)}, bf16[384,448]{1,0:T(8,128)(2,1)S(1)}, u32[]{:S(2)}, u32[]{:S(2)}) collective-permute-start(bf16[384,448]{1,0:T(8,128)(2,1)S(1)} %get-tuple-element.111), channel_id=1, source_target_pairs={{0,24},{4,28},{8,16},{12,20},{16,8},{20,12},{24,0},{28,4},{1,25},{... | collective-permute-start | bytes 1032200 | tf_op jit(solution)/shard_map/ppermute | solution.py:143
  98.0 14.2 %collective-permute-start.30 = (bf16[224,768]{1,0:T(8,128)(2,1)S(1)}, bf16[224,768]{1,0:T(8,128)(2,1)S(1)}, u32[]{:S(2)}, u32[]{:S(2)}) collective-permute-start(bf16[224,768]{1,0:T(8,128)(2,1)S(1)} %pile.5), channel_id=1, source_target_pairs={{0,1},{1,0},{2,3},{3,2},{4,5},{5,4},{6,7},{7,6},{8,9},{9,8},{10,11... | collective-permute-start | bytes 1032200 | tf_op jit(solution)/shard_map/ppermute | solution.py:143
  99.5 10.5 %collective-permute-start.21 = (bf16[112,768]{1,0:T(8,128)(2,1)S(1)}, bf16[112,768]{1,0:T(8,128)(2,1)S(1)}, u32[]{:S(2)}, u32[]{:S(2)}) collective-permute-start(bf16[112,768]{1,0:T(8,128)(2,1)S(1)} %total_of.3.refs_0_.refs_11_), channel_id=1, source_target_pairs={{0,2},{1,3},{2,0},{3,1},{4,6},{5,7},{6,4},{7,5},{8,10},{9,11},{10,... | collective-permute-start | bytes 516104 | tf_op jit(solution)/shard_map/ppermute | solution.py:143
  103.1 14.7 %collective-permute-start.33 = (bf16[864,384]{1,0:T(8,128)(2,1)S(1)}, bf16[864,384]{1,0:T(8,128)(2,1)S(1)}, u32[]{:S(2)}, u32[]{:S(2)}) collective-permute-start(bf16[864,384]{1,0:T(8,128)(2,1)S(1)} %get-tuple-element.123), channel_id=1, source_target_pairs={{0,4},{4,0},{8,12},{12,8},{16,20},{20,16},{24,28},{28,24},{1,5},{5... | collective-permute-start | bytes 1990664 | tf_op jit(solution)/shard_map/ppermute | solution.py:143
  113.3 9.7 %collective-permute-start.27 = (bf16[128,768]{1,0:T(8,128)(2,1)S(1)}, bf16[128,768]{1,0:T(8,128)(2,1)S(1)}, u32[]{:S(2)}, u32[]{:S(2)}) collective-permute-start(bf16[128,768]{1,0:T(8,128)(2,1)S(1)} %get-tuple-element.113), channel_id=1, source_target_pairs={{0,3},{1,2},{2,1},{3,0},{4,7},{5,6},{6,5},{7,4},{8,11},{9,10},{10,... | collective-permute-start | bytes 589832 | tf_op jit(solution)/shard_map/ppermute | solution.py:143
  115.5 13.0 %collective-permute-start.28 = (bf16[128,768]{1,0:T(8,128)(2,1)S(1)}, bf16[128,768]{1,0:T(8,128)(2,1)S(1)}, u32[]{:S(2)}, u32[]{:S(2)}) collective-permute-start(bf16[128,768]{1,0:T(8,128)(2,1)S(1)} %get-tuple-element.114), channel_id=1, source_target_pairs={{0,1},{1,0},{2,3},{3,2},{4,5},{5,4},{6,7},{7,6},{8,9},{9,8},{10,11... | collective-permute-start | bytes 589832 | tf_op jit(solution)/shard_map/ppermute | solution.py:143
  115.5 18.2 %collective-permute-start.29 = (bf16[128,768]{1,0:T(8,128)(2,1)S(1)}, bf16[128,768]{1,0:T(8,128)(2,1)S(1)}, u32[]{:S(2)}, u32[]{:S(2)}) collective-permute-start(bf16[128,768]{1,0:T(8,128)(2,1)S(1)} %get-tuple-element.115), channel_id=1, source_target_pairs={{0,2},{1,3},{2,0},{3,1},{4,6},{5,7},{6,4},{7,5},{8,10},{9,11},{10,... | collective-permute-start | bytes 589832 | tf_op jit(solution)/shard_map/ppermute | solution.py:143
  118.2 17.0 %collective-permute-start.37 = (bf16[408,384]{1,0:T(8,128)(2,1)S(1)}, bf16[408,384]{1,0:T(8,128)(2,1)S(1)}, u32[]{:S(2)}, u32[]{:S(2)}) collective-permute-start(bf16[408,384]{1,0:T(8,128)(2,1)S(1)} %get-tuple-element.127), channel_id=1, source_target_pairs={{0,24},{4,28},{8,16},{12,20},{16,8},{20,12},{24,0},{28,4},{1,25},{... | collective-permute-start | bytes 940040 | tf_op jit(solution)/shard_map/ppermute | solution.py:143
  118.3 19.2 %collective-permute-start.38 = (bf16[408,384]{1,0:T(8,128)(2,1)S(1)}, bf16[408,384]{1,0:T(8,128)(2,1)S(1)}, u32[]{:S(2)}, u32[]{:S(2)}) collective-permute-start(bf16[408,384]{1,0:T(8,128)(2,1)S(1)} %get-tuple-element.128), channel_id=1, source_target_pairs={{0,16},{4,20},{8,24},{12,28},{16,0},{20,4},{24,8},{28,12},{1,17},{... | collective-permute-start | bytes 940040 | tf_op jit(solution)/shard_map/ppermute | solution.py:143
  122.9 16.9 %collective-permute-start.22 = (bf16[224,768]{1,0:T(8,128)(2,1)S(1)}, bf16[224,768]{1,0:T(8,128)(2,1)S(1)}, u32[]{:S(2)}, u32[]{:S(2)}) collective-permute-start(bf16[224,768]{1,0:T(8,128)(2,1)S(1)} %pile.4), channel_id=1, source_target_pairs={{0,1},{1,0},{2,3},{3,2},{4,5},{5,4},{6,7},{7,6},{8,9},{9,8},{10,11... | collective-permute-start | bytes 1032200 | tf_op jit(solution)/shard_map/ppermute | solution.py:143
  128.4 11.1 %collective-permute-start.39 = (bf16[408,384]{1,0:T(8,128)(2,1)S(1)}, bf16[408,384]{1,0:T(8,128)(2,1)S(1)}, u32[]{:S(2)}, u32[]{:S(2)}) collective-permute-start(bf16[408,384]{1,0:T(8,128)(2,1)S(1)} %get-tuple-element.129), channel_id=1, source_target_pairs={{0,8},{4,12},{8,0},{12,4},{16,24},{20,28},{24,16},{28,20},{1,9},{5... | collective-permute-start | bytes 940040 | tf_op jit(solution)/shard_map/ppermute | solution.py:143
  135.1 9.8 %collective-permute-start.36 = (bf16[112,768]{1,0:T(8,128)(2,1)S(1)}, bf16[112,768]{1,0:T(8,128)(2,1)S(1)}, u32[]{:S(2)}, u32[]{:S(2)}) collective-permute-start(bf16[112,768]{1,0:T(8,128)(2,1)S(1)} %get-tuple-element.125.refs_0_), channel_id=1, source_target_pairs={{0,1},{1,0},{2,3},{3,2},{4,5},{5,4},{6,7},{7,6},{8,9},{9,8},{10,11... | collective-permute-start | bytes 516104 | tf_op jit(solution)/shard_map/ppermute | solution.py:143
  135.2 15.6 %collective-permute-start.35 = (bf16[112,768]{1,0:T(8,128)(2,1)S(1)}, bf16[112,768]{1,0:T(8,128)(2,1)S(1)}, u32[]{:S(2)}, u32[]{:S(2)}) collective-permute-start(bf16[112,768]{1,0:T(8,128)(2,1)S(1)} %get-tuple-element.125.refs_0_), channel_id=1, source_target_pairs={{0,2},{1,3},{2,0},{3,1},{4,6},{5,7},{6,4},{7,5},{8,10},{9,11},{10,... | collective-permute-start | bytes 516104 | tf_op jit(solution)/shard_map/ppermute | solution.py:143
  137.5 13.4 %collective-permute-start.34 = (bf16[112,768]{1,0:T(8,128)(2,1)S(1)}, bf16[112,768]{1,0:T(8,128)(2,1)S(1)}, u32[]{:S(2)}, u32[]{:S(2)}) collective-permute-start(bf16[112,768]{1,0:T(8,128)(2,1)S(1)} %get-tuple-element.125.refs_0_), channel_id=1, source_target_pairs={{0,3},{1,2},{2,1},{3,0},{4,7},{5,6},{6,5},{7,4},{8,11},{9,10},{10,... | collective-permute-start | bytes 516104 | tf_op jit(solution)/shard_map/ppermute | solution.py:143
  139.8 12.0 %collective-permute-start.42 = (bf16[424,384]{1,0:T(8,128)(2,1)S(1)}, bf16[424,384]{1,0:T(8,128)(2,1)S(1)}, u32[]{:S(2)}, u32[]{:S(2)}) collective-permute-start(bf16[424,384]{1,0:T(8,128)(2,1)S(1)} %sum_piece.1.refs_0_), channel_id=1, source_target_pairs={{0,8},{4,12},{8,0},{12,4},{16,24},{20,28},{24,16},{28,20},{1,9},{5... | collective-permute-start | bytes 976904 | tf_op jit(solution)/shard_map/ppermute | solution.py:143
  139.9 11.9 %collective-permute-start.41 = (bf16[424,384]{1,0:T(8,128)(2,1)S(1)}, bf16[424,384]{1,0:T(8,128)(2,1)S(1)}, u32[]{:S(2)}, u32[]{:S(2)}) collective-permute-start(bf16[424,384]{1,0:T(8,128)(2,1)S(1)} %sum_piece.1.refs_0_), channel_id=1, source_target_pairs={{0,16},{4,20},{8,24},{12,28},{16,0},{20,4},{24,8},{28,12},{1,17},{... | collective-permute-start | bytes 976904 | tf_op jit(solution)/shard_map/ppermute | solution.py:143
  144.9 10.3 %collective-permute-start.40 = (bf16[424,384]{1,0:T(8,128)(2,1)S(1)}, bf16[424,384]{1,0:T(8,128)(2,1)S(1)}, u32[]{:S(2)}, u32[]{:S(2)}) collective-permute-start(bf16[424,384]{1,0:T(8,128)(2,1)S(1)} %sum_piece.1.refs_0_), channel_id=1, source_target_pairs={{0,24},{4,28},{8,16},{12,20},{16,8},{20,12},{24,0},{28,4},{1,25},{... | collective-permute-start | bytes 976904 | tf_op jit(solution)/shard_map/ppermute | solution.py:143
  (17 other events, 75.0 us)

commit v16 on v15

--- a/solution.py
+++ b/solution.py
@@ -225,8 +225,8 @@
 def project_kernel(
     width, need, give, len_any, roster_any, x_ref, w_ref, gain_ref, freq_ref, *refs
 ):
-    q_out, kv_out, h_out, cos_out, sin_out = refs[:5]
-    proj, len_ref, roster_ref, sems = refs[5:]
+    q_out, kv_out, h_out, cos_out, sin_out, unit_out = refs[:6]
+    proj, len_ref, roster_ref, sems = refs[6:]
     rows = x_ref.shape[0]
     fetch_docs(len_any, roster_any, len_ref, roster_ref, sems.at[0], sems.at[1])
     need(5)
@@ -244,6 +244,7 @@
     def strip(i, carry):
         at = pl.ds(i * STRIP, STRIP)
         unit, unused = normed(x_ref[at, :].astype(F32))
+        unit_out[at, :] = unit
         h_out[at, :] = (unit * gain).astype(BF16)
         return carry
 
@@ -279,6 +280,7 @@
             ((rows, model), BF16, "v"),
             ((HALF, rows), F32, "v"),
             ((HALF, rows), F32, "v"),
+            ((rows, model), F32, "v"),
         ],
         [pltpu.VMEM((3 * width, rows), F32)]
         + doc_scratch(doc_lengths, roster)
@@ -530,7 +532,7 @@
         copy.wait()
 
 
-def pick(in_t, w_down, w_out):
+def pick(in_t, w_down, w_out, after=()):
     rows = (in_t.shape[0] + w_down.shape[0] + w_out.shape[0]) // 2
     model = w_out.shape[1]
     return call(
@@ -539,6 +541,8 @@
         kinds((in_t, w_down, w_out), "raw"),
         [((rows, model), BF16, "v"), ((w_out.shape[0] // 2, model), BF16, "v")],
         [pltpu.SemaphoreType.DMA((4,))],
+        16,
+        after,
     )
 
 
@@ -564,8 +568,10 @@
     return out
 
 
-def stage_kernel(x_any, cot_any, in_any, down_any, w_any, got_ref, rest_ref, *refs):
-    x_ref, cot_ref, w_ref, in_ref, down_ref, sems = refs
+def stage_kernel(
+    x_any, cot_any, in_any, down_any, w_any, one_any, two_any, got_ref, rest_ref, *refs
+):
+    x_ref, cot_ref, w_ref, in_ref, down_ref, x_part, cot_part, one_ref, two_ref, sems = refs
     half = x_ref.shape[0]
     core = lax.axis_index("seq") % 2
     tp = lax.axis_index("tp")
@@ -574,7 +580,11 @@
     width = w_any.shape[0]
     rows = width // 2
     own = pl.ds(pl.multiple_of(tp * width, width), width)
+    part = x_part.shape[0]
+    kept = pl.ds(pl.multiple_of(slot(tp, n_tp) * part, part), part)
     moves = [(w_any, w_ref.at[own]), (x_any.at[mine], x_ref), (cot_any.at[mine], cot_ref)]
+    moves += [(x_any.at[kept], x_part), (cot_any.at[kept], cot_part)]
+    moves += [(one_any, one_ref), (two_any, two_ref)]
     sides = ((got_ref, core), (rest_ref, 1 - core))
     first = got_ref.shape[0] - (n_tp - 1) * rows
     for k in range(1, n_tp):
@@ -597,20 +607,25 @@
         copy.wait()
 
 
-def stage(n_tp, tokens, cotangent, in_t, w_down, w_out, got, rest):
+def stage(n_tp, tokens, cotangent, in_t, w_down, w_out, gain_one, gain_two, got, rest):
     rows, model = tokens.shape
     return call(
         "stage",
         stage_kernel,
-        kinds((tokens, cotangent, in_t, w_down, w_out), "raw") + kinds((got, rest), "v"),
+        kinds((tokens, cotangent, in_t, w_down, w_out, gain_one, gain_two), "raw")
+        + kinds((got, rest), "v"),
         [
             ((rows // 2, model), BF16, "v"),
             ((rows // 2, model), BF16, "v"),
             ((n_tp * w_out.shape[0], model), BF16, "v"),
             ((2 * in_t.shape[0], model), BF16, "v"),
             ((2 * w_down.shape[0], model), BF16, "v"),
+            ((rows // n_tp, model), BF16, "v"),
+            ((rows // n_tp, model), BF16, "v"),
+            ((model,), F32, "v"),
+            ((model,), F32, "v"),
         ],
-        [pltpu.SemaphoreType.DMA((7 + 2 * n_tp,))],
+        [pltpu.SemaphoreType.DMA((11 + 2 * n_tp,))],
     )
 
 
@@ -693,7 +708,7 @@
     return call(
         "feed",
         functools.partial(feed_kernel, n_tp),
-        kinds(staged, "v") + [(gain, "h")] + kinds(outs, "v"),
+        kinds((*staged, gain, *outs), "v"),
         [
             ((rows, model), F32, "v"),
             ((part, model), F32, "v"),
@@ -744,8 +759,8 @@
     return call(
         "branch",
         functools.partial(branch_kernel, n_tp, len(arrived)),
-        [(middle_part, "v"), (cotangent, part)]
-        + [(gain, "h"), (w_full, "v"), (arrived[0], "v")]
+        [(middle_part, "v"), (cotangent, "v")]
+        + [(gain, "v"), (w_full, "v"), (arrived[0], "v")]
         + kinds(arrived[1:], "v"),
         [((part, model), F32, "v"), ((part, model), BF16, "v")]
         + [((part, width), BF16, "v")] * n_tp,
@@ -845,8 +860,7 @@
 
     def gains(i, carry):
         at = pl.ds(i * STRIP, STRIP)
-        unit, unused = normed(x_ref[at, :].astype(F32))
-        product = grad[at, :] * unit
+        product = grad[at, :] * x_ref[at, :]
         return carry + jnp.sum(product.reshape(STRIP // 8, 8, -1), axis=0)
 
     gain = lax.fori_loop(0, rows // STRIP, gains, jnp.zeros((8, model), F32))
@@ -892,7 +906,7 @@
     return call(
         "input_side",
         input_kernel,
-        [(tokens, part), (gain, "h"), (middle_grad, "v"), (summed, "v")],
+        kinds((tokens, gain, middle_grad, summed), "v"),
         [((part, model), BF16, "v"), ((8, model), F32, "v")],
         (),
         16,
@@ -1064,8 +1078,11 @@
     for n, (ref, size) in enumerate(zip(out_refs, sizes)):
         rows = pl.ds(at, size)
         held[rows, :] = source[rows, :].astype(F32)
-        copies.append(pltpu.make_async_copy(held.at[rows], ref.at[:, columns], sems.at[n]))
-        copies[-1].start()
+        for part in range(2):
+            some = pl.ds(at + part * (size // 2), size // 2)
+            target = ref.at[pl.ds(part * (size // 2), size // 2), columns]
+            copies.append(pltpu.make_async_copy(held.at[some], target, sems.at[2 * n + part]))
+            copies[-1].start()
         at += size
     return copies
 
@@ -1096,7 +1113,7 @@
 def finish(own, over_cores, sizes):
     half = own.shape[1]
     shapes = [((size, 2 * half), F32, "raw") for size in sizes]
-    scratch = [pltpu.VMEM((sum(sizes), half), F32), pltpu.SemaphoreType.DMA((len(sizes),))]
+    scratch = [pltpu.VMEM((sum(sizes), half), F32), pltpu.SemaphoreType.DMA((2 * len(sizes),))]
     pair = over_cores(own)
     begun = call("own_half", functools.partial(own_kernel, sizes), [(own, "v")], shapes, scratch)
     return call(
@@ -1181,10 +1198,10 @@
     over_cores = lambda x: swap(x, "seq", 1, n_seq)
     everywhere = lambda xs: [xs[0]] + came(n_tp, lambda k: over_tp(xs[k], k))
 
-    def by_steps(part):
+    def by_steps(part, after=()):
         held, places, step = [part], [(0,)], n_tp // 2
         while step:
-            joined = pile(held, ()) if len(held) > 1 else part
+            joined = pile(held, after) if len(held) > 1 else part
             ks = tuple(k ^ step for group in places for k in group)
             held, places, step = held + [over_tp(joined, step)], places + [ks], step // 2
         return held, tuple(places)
@@ -1192,12 +1209,12 @@
     singly = tuple((hop(n, n_tp),) for n in range(n_tp))
     docs = (doc_lengths, roster)
 
-    queries, kv, h_one, cos_table, sin_table = project(*docs, tokens, gain_one, qkv_t)
+    queries, kv, h_one, cos_table, sin_table, unit_one = project(*docs, tokens, gain_one, qkv_t)
     blocks = [kv] + [over_chips(kv, j) for j in range(1, count)]
     q_pair = over_cores(queries)
-    picked, w_half = pick(in_t, w_down, w_out)
+
+    picked, w_half = pick(in_t, w_down, w_out, ())
     got = [over_tp(picked, 1)] + [over_tp(w_half, k) for k in range(2, n_tp)]
-
     split = (count + 1) // 2
     (state,) = attention_forward(0, False, *docs, queries, q_pair, blocks[:split])
     state_own, state_pair = attention_forward(
@@ -1209,14 +1226,16 @@
     totals_pair = over_cores(totals)
 
     got = pile(got, [(state_pair, "v")])
-    staged = stage(n_tp, tokens, cotangent, in_t, w_down, w_out, got, over_cores(got))
+    *staged, x_part, cot_part, gain_one, gain_two = stage(
+        n_tp, tokens, cotangent, in_t, w_down, w_out, gain_one, gain_two, got, over_cores(got)
+    )
     middle, middle_part, h_two, mixed, gate_grad, gain_two_part, own, *others = feed(
         gain_two, staged, outs
     )
     arrived = [own] + [over_tp(others[n], 2 * n + 2) for n in range(n_tp // 2 - 1)]
     own, *others = down(n_tp, mixed, staged[4], middle, [(out_pair, "v"), (totals_pair, "v")])
     middle_grad, branch_grad, *pieces = branch(
-        n_tp, middle_part, cotangent, gain_two, staged[2], arrived, [(own, "v")]
+        n_tp, middle_part, cot_part, gain_two, staged[2], arrived, [(own, "v")]
     )
     early, early_send = early_grads(
         mixed, gate_grad, cotangent, h_two, in_t, w_down, over_tp(h_two, 1), [(branch_grad, "v")]
@@ -1234,16 +1253,15 @@
         "v",
         [(dq, "v"), (branches[1], "v")],
     )
-    totals_all, total_places = by_steps(total)
 
     dkv, dq_own, dq_pair = attention_backward(
         0, True, *docs, held, blocks[:1], dq, ()
     )
-    dkvs = [dkv] + [over_chips(terms[j - 1], j) for j in range(1, count)]
+    dkvs = [dkv] + [over_chips(terms[j - 1], j) for j in range(count - 1, 0, -1)]
 
     proj_grad, *parts = unproject(
         n_tp,
-        tokens,
+        unit_one,
         qkv_t,
         cos_table,
         sin_table,
@@ -1253,17 +1271,18 @@
         dkvs,
         [(total, "v")],
     )
-    layer_out = stack_parts(n_tp, totals_all, total_places)
+    ways = everywhere(parts)
+    totals_all, total_places = by_steps(total, ())
     keep, send = late_grads(
         n_tp, proj_grad, h_one, out_b, branches, branch_places, [(totals_all[1], "v")]
     )
     own, *others = spread(count, (keep, over_cores(send)), (early, early_back))
-    ways = everywhere(parts)
     summed = total_of([ways[0]] + [ways[i] for i in (1, 3, 2)], F32, flops=2_000_000_000)
     chip_sum = total_of(
         [own] + came(count, lambda k: over_chips(others[k - 1], k)), F32, "v", ()
     )
-    input_part, gains = input_side(tokens, gain_one, middle_grad, summed, [(own, "v")])
+    layer_out = stack_parts(n_tp, totals_all, total_places)
+    input_part, gains = input_side(x_part, gain_one, middle_grad, summed, [(own, "v")])
     inputs_all = everywhere([input_part] * n_tp)
     piece = sum_piece(gains, [chip_sum], ())
     input_grad = stack_parts(n_tp, inputs_all, singly, (), 3_000_000_000)

time: 161 us -> 162 us (level)
  starting transfers between devices: 47.8 us -> 56.2 us
  waiting for transfers between devices: 56.9 us -> 52.4 us
  Pallas kernels: 54.9 us -> 52.1 us
    ppermute x44, starting transfers between devices: 47.8 us -> 56.2 us  [swap(): return lax.ppermute(x, axis, [(i, i ^ hop) for i in range(count)])]
    ppermute x44, waiting for transfers between devices: 56.9 us -> 52.4 us  [swap(): return lax.ppermute(x, axis, [(i, i ^ hop) for i in range(count)])]
    pallas_call x29, Pallas kernels: 54.9 us -> 52.1 us  [call(): pl.pallas_call(run, out_shape=tuple((shaped(shape, dtype) if kind == 'v'...]
  transfers between devices with their start and end apart: 44 -> 44, of which waited for: 20 -> 21; matrix products, arithmetic and copies ran while one was open for 0% -> 0% of each run, Pallas kernels for 32% -> 30%
where the time goes in v16:
time: 162 us
  starting transfers between devices  56.2 us (35%)
  waiting for transfers between devices  52.4 us (32%)
  Pallas kernels  52.1 us (32%)
    ppermute x44, starting transfers between devices, swap(): return lax.ppermute(x, axis, [(i, i ^ hop) for i in range(count)])  56.2 us
    ppermute x44, waiting for transfers between devices, swap(): return lax.ppermute(x, axis, [(i, i ^ hop) for i in range(count)])  52.4 us
    pallas_call x29, Pallas kernels, call(): pl.pallas_call(run, out_shape=tuple((shaped(shape, dtype) if kind == 'v'...  52.1 us
  transfers between devices with their start and end apart: 44, of which 21 were waited for; matrix products, arithmetic and copies ran while one was open for 0% of the time, Pallas kernels for 30%

profile of v16, /device:TPU:0, one launch (start us, length us, event | category | flops | bytes accessed | tf_op | source)
XLA Modules:
  0.0 161.9 jit_solution(15143757511499400826)
XLA Ops:
  1.9 3.1 %collective-permute-start = (bf16[528,768]{1,0:T(8,128)(2,1)S(1)}, bf16[528,768]{1,0:T(8,128)(2,1)S(1)}, u32[]{:S(2)}, u32[]{:S(2)}) collective-permute-start(bf16[528,768]{1,0:T(8,128)(2,1)S(1)} %get-tuple-element.79), channel_id=1, source_target_pairs={{0,1},{1,0},{2,3},{3,2},{4,5},{5,4},{6,7},{7,6},{8,9},{9,8},{10,11... | collective-permute-start | bytes 2433032 | tf_op jit(solution)/shard_map/ppermute | solution.py:143
  5.0 3.7 %project.1 = (bf16[192,448]{1,0:T(8,128)(2,1)S(1)}, bf16[384,448]{1,0:T(8,128)(2,1)S(1)}, bf16[448,768]{1,0:T(8,128)(2,1)S(1)}, f32[32,448]{1,0:T(8,128)S(1)}, f...) custom-call(s32[4]{0:T(128)} %refs_0_.11, s32[8]{0:T(128)} %refs_1_.13, bf16[448,768]{1,0:T(8,128)(2,1)} %refs_0_.9, ...), custom_call_target="tpu_custom_call" | custom-call | tf_op jit(solution)/shard_map/project/pallas_call | solution.py:121
  13.7 2.5 %collective-permute-start.2 = (bf16[96,768]{1,0:T(8,128)(2,1)S(1)}, bf16[96,768]{1,0:T(8,128)(2,1)S(1)}, u32[]{:S(2)}, u32[]{:S(2)}) collective-permute-start(bf16[96,768]{1,0:T(8,128)(2,1)S(1)} %get-tuple-element.80), channel_id=1, source_target_pairs={{0,3},{1,2},{2,1},{3,0},{4,7},{5,6},{6,5},{7,4},{8,11},{9,10},{10,... | collective-permute-start | bytes 442376 | tf_op jit(solution)/shard_map/ppermute | solution.py:143
  16.2 4.6 %collective-permute-done.6.refs_5_.refs_10_ = bf16[384,448]{1,0:T(8,128)(2,1)S(1)} collective-permute-done((bf16[384,448]{1,0:T(8,128)(2,1)S(1)}, bf16[384,448]{1,0:T(8,128)(2,1)S(1)}, u32[]{:S(2)}, u32[]{:S(2)}) %collective-permute-start.6) | collective-permute-done | bytes 344096 | tf_op jit(solution)/shard_map/ppermute | solution.py:143
  20.8 2.6 %collective-permute-start.1 = (bf16[96,768]{1,0:T(8,128)(2,1)S(1)}, bf16[96,768]{1,0:T(8,128)(2,1)S(1)}, u32[]{:S(2)}, u32[]{:S(2)}) collective-permute-start(bf16[96,768]{1,0:T(8,128)(2,1)S(1)} %get-tuple-element.80), channel_id=1, source_target_pairs={{0,2},{1,3},{2,0},{3,1},{4,6},{5,7},{6,4},{7,5},{8,10},{9,11},{10,... | collective-permute-start | bytes 442376 | tf_op jit(solution)/shard_map/ppermute | solution.py:143
  23.4 7.1 %attention_forward.2.refs_6_ = f32[6,80,448]{2,1,0:T(8,128)S(1)} custom-call(s32[4]{0:T(128)} %refs_0_.11, s32[8]{0:T(128)} %refs_1_.13, bf16[192,448]{1,0:T(8,128)(2,1)S(1)} %get-tuple-element.81.refs_2_, bf16[192,448]{1,0:T(8,128)(2,1)S(1)} %collective-permute-done.3.refs_3_, bf16[384,448]{1,0:T(8,128)(2,1)S(1)} %get-tuple-element.82.refs_4_.refs_10_, ...), custom_call_target="tpu_custom_call" | custom-call | tf_op jit(solution)/shard_map/attention_forward/pallas_call | solution.py:121
  30.6 4.2 %attention_forward.3 = (f32[3,80,448]{2,1,0:T(8,128)S(1)}, f32[3,80,448]{2,1,0:T(8,128)S(1)}) custom-call(s32[4]{0:T(128)} %refs_0_.11, s32[8]{0:T(128)} %refs_1_.13, bf16[192,448]{1,0:T(8,128)(2,1)S(1)} %get-tuple-element.81.refs_2_, bf16[192,448]{1,0:T(8,128)(2,1)S(1)} %collective-permute-done.3.refs_3_, ...), custom_call_target="tpu_custom_call" | custom-call | tf_op jit(solution)/shard_map/attention_forward/pallas_call | solution.py:121
  35.5 2.9 %collective-permute-done.8.refs_1_ = f32[3,80,448]{2,1,0:T(8,128)S(1)} collective-permute-done((f32[3,80,448]{2,1,0:T(8,128)S(1)}, f32[3,80,448]{2,1,0:T(8,128)S(1)}, u32[]{:S(2)}, u32[]{:S(2)}) %collective-permute-start.8) | collective-permute-done | bytes 430112 | tf_op jit(solution)/shard_map/ppermute | solution.py:143
  38.9 2.3 %collective-permute-start.10 = (bf16[192,224]{1,0:T(8,128)(2,1)S(1)}, bf16[192,224]{1,0:T(8,128)(2,1)S(1)}, u32[]{:S(2)}, u32[]{:S(2)}) collective-permute-start(bf16[192,224]{1,0:T(8,128)(2,1)S(1)} %get-tuple-element.91.refs_6_), channel_id=1, source_target_pairs={{0,2},{1,3},{2,0},{3,1},{4,6},{5,7},{6,4},{7,5},{8,10},{9,11},{10,... | collective-permute-start | bytes 258056 | tf_op jit(solution)/shard_map/ppermute | solution.py:143
  43.3 3.3 %stage.1 = (bf16[224,768]{1,0:T(8,128)(2,1)S(1)}, bf16[224,768]{1,0:T(8,128)(2,1)S(1)}, bf16[768,768]{1,0:T(8,128)(2,1)S(1)}, bf16[1152,768]{1,0:T(8,128)(2,1)S(...) custom-call(bf16[448,768]{1,0:T(8,128)(2,1)} %refs_0_.9, ...), custom_call_target="tpu_custom_call" | custom-call | tf_op jit(solution)/shard_map/stage/pallas_call | solution.py:121
  46.6 2.3 %collective-permute-done.10.refs_8_ = bf16[192,224]{1,0:T(8,128)(2,1)S(1)} collective-permute-done((bf16[192,224]{1,0:T(8,128)(2,1)S(1)}, bf16[192,224]{1,0:T(8,128)(2,1)S(1)}, u32[]{:S(2)}, u32[]{:S(2)}) %collective-permute-start.10) | collective-permute-done | bytes 86048 | tf_op jit(solution)/shard_map/ppermute | solution.py:143
  49.8 4.8 %feed.1 = (f32[224,768]{1,0:T(8,128)S(1)}, f32[112,768]{1,0:T(8,128)S(1)}, bf16[224,768]{1,0:T(8,128)(2,1)S(1)}, bf16[576,224]{1,0:T(8,128)(2,1)S(1)}, bf16[1152...) custom-call(bf16[224,768]{1,0:T(8,128)(2,1)S(1)} %get-tuple-element.84.refs_, ...), custom_call_target="tpu_custom_call" | custom-call | tf_op jit(solution)/shard_map/feed/pallas_call | solution.py:121
  54.6 2.5 %collective-permute-start.15 = (bf16[112,768]{1,0:T(8,128)(2,1)S(1)}, bf16[112,768]{1,0:T(8,128)(2,1)S(1)}, u32[]{:S(2)}, u32[]{:S(2)}) collective-permute-start(bf16[112,768]{1,0:T(8,128)(2,1)S(1)} %get-tuple-element.102), channel_id=1, source_target_pairs={{0,2},{1,3},{2,0},{3,1},{4,6},{5,7},{6,4},{7,5},{8,10},{9,11},{10,... | collective-permute-start | bytes 516104 | tf_op jit(solution)/shard_map/ppermute | solution.py:143
  59.3 5.7 %collective-permute-done.15.refs_5_ = bf16[112,768]{1,0:T(8,128)(2,1)S(1)} collective-permute-done((bf16[112,768]{1,0:T(8,128)(2,1)S(1)}, bf16[112,768]{1,0:T(8,128)(2,1)S(1)}, u32[]{:S(2)}, u32[]{:S(2)}) %collective-permute-start.15) | collective-permute-done | bytes 172064 | tf_op jit(solution)/shard_map/ppermute | solution.py:143
  65.8 2.3 %collective-permute-start.16 = (bf16[112,192]{1,0:T(8,128)(2,1)S(1)}, bf16[112,192]{1,0:T(8,128)(2,1)S(1)}, u32[]{:S(2)}, u32[]{:S(2)}) collective-permute-start(bf16[112,192]{1,0:T(8,128)(2,1)S(1)} %get-tuple-element.104), channel_id=1, source_target_pairs={{0,3},{1,2},{2,1},{3,0},{4,7},{5,6},{6,5},{7,4},{8,11},{9,10},{10,... | collective-permute-start | bytes 129032 | tf_op jit(solution)/shard_map/ppermute | solution.py:143
  68.1 2.2 %collective-permute-start.18 = (bf16[112,192]{1,0:T(8,128)(2,1)S(1)}, bf16[112,192]{1,0:T(8,128)(2,1)S(1)}, u32[]{:S(2)}, u32[]{:S(2)}) collective-permute-start(bf16[112,192]{1,0:T(8,128)(2,1)S(1)} %get-tuple-element.106), channel_id=1, source_target_pairs={{0,1},{1,0},{2,3},{3,2},{4,5},{5,4},{6,7},{7,6},{8,9},{9,8},{10,11... | collective-permute-start | bytes 129032 | tf_op jit(solution)/shard_map/ppermute | solution.py:143
  70.2 2.4 %collective-permute-done.16.refs_1_ = bf16[112,192]{1,0:T(8,128)(2,1)S(1)} collective-permute-done((bf16[112,192]{1,0:T(8,128)(2,1)S(1)}, bf16[112,192]{1,0:T(8,128)(2,1)S(1)}, u32[]{:S(2)}, u32[]{:S(2)}) %collective-permute-start.16) | collective-permute-done | bytes 43040 | tf_op jit(solution)/shard_map/ppermute | solution.py:143
  77.1 9.0 %attention_backward.2 = (bf16[384,448]{1,0:T(8,128)(2,1)S(1)}, bf16[384,448]{1,0:T(8,128)(2,1)S(1)}, bf16[384,448]{1,0:T(8,128)(2,1)S(1)}, f32[6,64,448]{2,1,0:T(8,128)S(1)}) custom-call(s32[4]{0:T(128)} %refs_0_.11, s32[8]{0:T(128)} %refs_1_.13, bf16[192,448]{1,0:T(8,128)(2,1)S(1)} %get-tuple-element.81.refs_2_, ...), custom_call_target="tpu_custom_call" | custom-call | tf_op jit(solution)/shard_map/attention_backward/pallas_call | solution.py:121
  86.1 6.1 %collective-permute-start.24 = (bf16[384,448]{1,0:T(8,128)(2,1)S(1)}, bf16[384,448]{1,0:T(8,128)(2,1)S(1)}, u32[]{:S(2)}, u32[]{:S(2)}) collective-permute-start(bf16[384,448]{1,0:T(8,128)(2,1)S(1)} %get-tuple-element.119), channel_id=1, source_target_pairs={{0,24},{4,28},{8,16},{12,20},{16,8},{20,12},{24,0},{28,4},{1,25},{... | collective-permute-start | bytes 1032200 | tf_op jit(solution)/shard_map/ppermute | solution.py:143
  92.9 5.1 %attention_backward.3 = (f32[384,448]{1,0:T(8,128)S(1)}, f32[192,448]{1,0:T(8,128)S(1)}, bf16[192,448]{1,0:T(8,128)(2,1)S(1)}) custom-call(s32[4]{0:T(128)} %refs_0_.11, s32[8]{0:T(128)} %refs_1_.13, bf16[192,448]{1,0:T(8,128)(2,1)S(1)} %get-tuple-element.81.refs_2_, bf16[192,448]{1,0:T(8,128)(2,1)S(1)} %collective-permute-done.3.refs_3_, ...), custom_call_target="tpu_custom_call" | custom-call | tf_op jit(solution)/shard_map/attention_backward/pallas_call | solution.py:121
  100.9 2.1 %early_grads.1 = (f32[864,384]{1,0:T(8,128)S(1)}, bf16[864,384]{1,0:T(8,128)(2,1)S(1)}) custom-call(bf16[576,224]{1,0:T(8,128)(2,1)S(1)} %get-tuple-element.93.refs_0_, bf16[1152,224]{1,0:T(8,128)(2,1)S(1)} %get-tuple-element.130.refs_1_, bf16[448,768]{1,0:T(8,128)(2,1)S(1)} %copy-done.3, bf16[224,768]{1,0:T(8,128)(2,1)S(1)} %get-tuple-element.131.refs_3_, ...), custom_call_target="tpu_custom_call" | custom-call | tf_op jit(solution)/shard_map/early_grads/pallas_call | solution.py:121
  105.7 4.9 %collective-permute-done.21.refs_1_.refs_6_ = bf16[112,768]{1,0:T(8,128)(2,1)S(1)} collective-permute-done((bf16[112,768]{1,0:T(8,128)(2,1)S(1)}, bf16[112,768]{1,0:T(8,128)(2,1)S(1)}, u32[]{:S(2)}, u32[]{:S(2)}) %collective-permute-start.21) | collective-permute-done | bytes 172064 | tf_op jit(solution)/shard_map/ppermute | solution.py:143
  115.8 2.0 %collective-permute-start.29 = (bf16[128,768]{1,0:T(8,128)(2,1)S(1)}, bf16[128,768]{1,0:T(8,128)(2,1)S(1)}, u32[]{:S(2)}, u32[]{:S(2)}) collective-permute-start(bf16[128,768]{1,0:T(8,128)(2,1)S(1)} %get-tuple-element.125), channel_id=1, source_target_pairs={{0,2},{1,3},{2,0},{3,1},{4,6},{5,7},{6,4},{7,5},{8,10},{9,11},{10,... | collective-permute-start | bytes 589832 | tf_op jit(solution)/shard_map/ppermute | solution.py:143
  118.3 2.9 %collective-permute-start.37 = (bf16[408,384]{1,0:T(8,128)(2,1)S(1)}, bf16[408,384]{1,0:T(8,128)(2,1)S(1)}, u32[]{:S(2)}, u32[]{:S(2)}) collective-permute-start(bf16[408,384]{1,0:T(8,128)(2,1)S(1)} %get-tuple-element.137), channel_id=1, source_target_pairs={{0,24},{4,28},{8,16},{12,20},{16,8},{20,12},{24,0},{28,4},{1,25},{... | collective-permute-start | bytes 940040 | tf_op jit(solution)/shard_map/ppermute | solution.py:143
  123.0 3.8 %collective-permute-start.22 = (bf16[224,768]{1,0:T(8,128)(2,1)S(1)}, bf16[224,768]{1,0:T(8,128)(2,1)S(1)}, u32[]{:S(2)}, u32[]{:S(2)}) collective-permute-start(bf16[224,768]{1,0:T(8,128)(2,1)S(1)} %pile.4), channel_id=1, source_target_pairs={{0,1},{1,0},{2,3},{3,2},{4,5},{5,4},{6,7},{7,6},{8,9},{9,8},{10,11... | collective-permute-start | bytes 1032200 | tf_op jit(solution)/shard_map/ppermute | solution.py:143
  127.9 6.4 %collective-permute-done.29.refs_3_ = bf16[128,768]{1,0:T(8,128)(2,1)S(1)} collective-permute-done((bf16[128,768]{1,0:T(8,128)(2,1)S(1)}, bf16[128,768]{1,0:T(8,128)(2,1)S(1)}, u32[]{:S(2)}, u32[]{:S(2)}) %collective-permute-start.29) | collective-permute-done | bytes 196640 | tf_op jit(solution)/shard_map/ppermute | solution.py:143
  134.8 2.4 %collective-permute-start.35 = (bf16[112,768]{1,0:T(8,128)(2,1)S(1)}, bf16[112,768]{1,0:T(8,128)(2,1)S(1)}, u32[]{:S(2)}, u32[]{:S(2)}) collective-permute-start(bf16[112,768]{1,0:T(8,128)(2,1)S(1)} %get-tuple-element.135.refs_0_), channel_id=1, source_target_pairs={{0,2},{1,3},{2,0},{3,1},{4,6},{5,7},{6,4},{7,5},{8,10},{9,11},{10,... | collective-permute-start | bytes 516104 | tf_op jit(solution)/shard_map/ppermute | solution.py:143
  139.5 2.3 %collective-permute-done.22.refs_2_ = bf16[224,768]{1,0:T(8,128)(2,1)S(1)} collective-permute-done((bf16[224,768]{1,0:T(8,128)(2,1)S(1)}, bf16[224,768]{1,0:T(8,128)(2,1)S(1)}, u32[]{:S(2)}, u32[]{:S(2)}) %collective-permute-start.22) | collective-permute-done | bytes 344096 | tf_op jit(solution)/shard_map/ppermute | solution.py:143
  142.9 2.0 %collective-permute-done.36.refs_3_ = bf16[112,768]{1,0:T(8,128)(2,1)S(1)} collective-permute-done((bf16[112,768]{1,0:T(8,128)(2,1)S(1)}, bf16[112,768]{1,0:T(8,128)(2,1)S(1)}, u32[]{:S(2)}, u32[]{:S(2)}) %collective-permute-start.36) | collective-permute-done | bytes 172064 | tf_op jit(solution)/shard_map/ppermute | solution.py:143
  144.9 2.8 %collective-permute-start.40 = (bf16[424,384]{1,0:T(8,128)(2,1)S(1)}, bf16[424,384]{1,0:T(8,128)(2,1)S(1)}, u32[]{:S(2)}, u32[]{:S(2)}) collective-permute-start(bf16[424,384]{1,0:T(8,128)(2,1)S(1)} %sum_piece.1.refs_0_), channel_id=1, source_target_pairs={{0,24},{4,28},{8,16},{12,20},{16,8},{20,12},{24,0},{28,4},{1,25},{... | collective-permute-start | bytes 976904 | tf_op jit(solution)/shard_map/ppermute | solution.py:143
  151.4 4.8 %collective-permute-done.41.refs_2_ = bf16[424,384]{1,0:T(8,128)(2,1)S(1)} collective-permute-done((bf16[424,384]{1,0:T(8,128)(2,1)S(1)}, bf16[424,384]{1,0:T(8,128)(2,1)S(1)}, u32[]{:S(2)}, u32[]{:S(2)}) %collective-permute-start.41) | collective-permute-done | bytes 325664 | tf_op jit(solution)/shard_map/ppermute | solution.py:143
  159.6 2.2 %pair_half.1 = (f32[576,768]{1,0:T(8,128)}, f32[192,768]{1,0:T(8,128)}, f32[288,768]{1,0:T(8,128)}, f32[576,768]{1,0:T(8,128)}, f32[768]{0:T(1024)}, /*index=5*/f32[768]{0:T(1024)}) custom-call(bf16[1648,384]{1,0:T(8,128)(2,1)S(1)} %collect.1.refs_0_, ...), custom_call_target="tpu_custom_call", output_to_operand_aliasing={{0}: (2, {}), {1}: (3, {}), {2}: (4, {}), {3}: (5, {})} | custom-call | tf_op jit(solution)/shard_map/pair_half/pallas_call | solution.py:121
  (93 shorter events, 43.4 us)
Async XLA Ops:
  1.9 33.0 %collective-permute-start = (bf16[528,768]{1,0:T(8,128)(2,1)S(1)}, bf16[528,768]{1,0:T(8,128)(2,1)S(1)}, u32[]{:S(2)}, u32[]{:S(2)}) collective-permute-start(bf16[528,768]{1,0:T(8,128)(2,1)S(1)} %get-tuple-element.79), channel_id=1, source_target_pairs={{0,1},{1,0},{2,3},{3,2},{4,5},{5,4},{6,7},{7,6},{8,9},{9,8},{10,11... | collective-permute-start | bytes 2433032 | tf_op jit(solution)/shard_map/ppermute | solution.py:143
  8.7 12.1 %collective-permute-start.6 = (bf16[384,448]{1,0:T(8,128)(2,1)S(1)}, bf16[384,448]{1,0:T(8,128)(2,1)S(1)}, u32[]{:S(2)}, u32[]{:S(2)}) collective-permute-start(bf16[384,448]{1,0:T(8,128)(2,1)S(1)} %get-tuple-element.82.refs_4_.refs_10_), channel_id=1, source_target_pairs={{0,8},{4,12},{8,0},{12,4},{16,24},{20,28},{24,16},{28,20},{1,9},{5... | collective-permute-start | bytes 1032200 | tf_op jit(solution)/shard_map/ppermute | solution.py:143
  10.3 20.3 %collective-permute-start.5 = (bf16[384,448]{1,0:T(8,128)(2,1)S(1)}, bf16[384,448]{1,0:T(8,128)(2,1)S(1)}, u32[]{:S(2)}, u32[]{:S(2)}) collective-permute-start(bf16[384,448]{1,0:T(8,128)(2,1)S(1)} %get-tuple-element.82.refs_4_.refs_10_), channel_id=1, source_target_pairs={{0,24},{4,28},{8,16},{12,20},{16,8},{20,12},{24,0},{28,4},{1,25},{... | collective-permute-start | bytes 1032200 | tf_op jit(solution)/shard_map/ppermute | solution.py:143
  11.8 18.8 %collective-permute-start.4 = (bf16[384,448]{1,0:T(8,128)(2,1)S(1)}, bf16[384,448]{1,0:T(8,128)(2,1)S(1)}, u32[]{:S(2)}, u32[]{:S(2)}) collective-permute-start(bf16[384,448]{1,0:T(8,128)(2,1)S(1)} %get-tuple-element.82.refs_4_.refs_10_), channel_id=1, source_target_pairs={{0,16},{4,20},{8,24},{12,28},{16,0},{20,4},{24,8},{28,12},{1,17},{... | collective-permute-start | bytes 1032200 | tf_op jit(solution)/shard_map/ppermute | solution.py:143
  13.7 21.1 %collective-permute-start.2 = (bf16[96,768]{1,0:T(8,128)(2,1)S(1)}, bf16[96,768]{1,0:T(8,128)(2,1)S(1)}, u32[]{:S(2)}, u32[]{:S(2)}) collective-permute-start(bf16[96,768]{1,0:T(8,128)(2,1)S(1)} %get-tuple-element.80), channel_id=1, source_target_pairs={{0,3},{1,2},{2,1},{3,0},{4,7},{5,6},{6,5},{7,4},{8,11},{9,10},{10,... | collective-permute-start | bytes 442376 | tf_op jit(solution)/shard_map/ppermute | solution.py:143
  20.8 14.0 %collective-permute-start.1 = (bf16[96,768]{1,0:T(8,128)(2,1)S(1)}, bf16[96,768]{1,0:T(8,128)(2,1)S(1)}, u32[]{:S(2)}, u32[]{:S(2)}) collective-permute-start(bf16[96,768]{1,0:T(8,128)(2,1)S(1)} %get-tuple-element.80), channel_id=1, source_target_pairs={{0,2},{1,3},{2,0},{3,1},{4,6},{5,7},{6,4},{7,5},{8,10},{9,11},{10,... | collective-permute-start | bytes 442376 | tf_op jit(solution)/shard_map/ppermute | solution.py:143
  38.9 10.0 %collective-permute-start.10 = (bf16[192,224]{1,0:T(8,128)(2,1)S(1)}, bf16[192,224]{1,0:T(8,128)(2,1)S(1)}, u32[]{:S(2)}, u32[]{:S(2)}) collective-permute-start(bf16[192,224]{1,0:T(8,128)(2,1)S(1)} %get-tuple-element.91.refs_6_), channel_id=1, source_target_pairs={{0,2},{1,3},{2,0},{3,1},{4,6},{5,7},{6,4},{7,5},{8,10},{9,11},{10,... | collective-permute-start | bytes 258056 | tf_op jit(solution)/shard_map/ppermute | solution.py:143
  41.1 8.7 %collective-permute-start.11 = (bf16[192,224]{1,0:T(8,128)(2,1)S(1)}, bf16[192,224]{1,0:T(8,128)(2,1)S(1)}, u32[]{:S(2)}, u32[]{:S(2)}) collective-permute-start(bf16[192,224]{1,0:T(8,128)(2,1)S(1)} %get-tuple-element.92), channel_id=1, source_target_pairs={{0,1},{1,0},{2,3},{3,2},{4,5},{5,4},{6,7},{7,6},{8,9},{9,8},{10,11... | collective-permute-start | bytes 258056 | tf_op jit(solution)/shard_map/ppermute | solution.py:143
  43.3 15.5 %collective-permute-start.12 = (bf16[192,448]{1,0:T(8,128)(2,1)S(1)}, bf16[192,448]{1,0:T(8,128)(2,1)S(1)}, u32[]{:S(2)}, u32[]{:S(2)}) collective-permute-start(bf16[192,448]{1,0:T(8,128)(2,1)S(1)} %get-tuple-element.95.refs_6_.refs_2_), channel_id=1, source_target_pairs={{0,4},{4,0},{8,12},{12,8},{16,20},{20,16},{24,28},{28,24},{1,5},{5... | collective-permute-start | bytes 516104 | tf_op jit(solution)/shard_map/ppermute | solution.py:143
  54.6 10.4 %collective-permute-start.15 = (bf16[112,768]{1,0:T(8,128)(2,1)S(1)}, bf16[112,768]{1,0:T(8,128)(2,1)S(1)}, u32[]{:S(2)}, u32[]{:S(2)}) collective-permute-start(bf16[112,768]{1,0:T(8,128)(2,1)S(1)} %get-tuple-element.102), channel_id=1, source_target_pairs={{0,2},{1,3},{2,0},{3,1},{4,6},{5,7},{6,4},{7,5},{8,10},{9,11},{10,... | collective-permute-start | bytes 516104 | tf_op jit(solution)/shard_map/ppermute | solution.py:143
  57.1 41.0 %collective-permute-start.32 = (bf16[224,768]{1,0:T(8,128)(2,1)S(1)}, bf16[224,768]{1,0:T(8,128)(2,1)S(1)}, u32[]{:S(2)}, u32[]{:S(2)}) collective-permute-start(bf16[224,768]{1,0:T(8,128)(2,1)S(1)} %get-tuple-element.131.refs_3_), channel_id=1, source_target_pairs={{0,1},{1,0},{2,3},{3,2},{4,5},{5,4},{6,7},{7,6},{8,9},{9,8},{10,11... | collective-permute-start | bytes 1032200 | tf_op jit(solution)/shard_map/ppermute | solution.py:143
  74.1 18.1 %collective-permute-start.20 = (bf16[112,768]{1,0:T(8,128)(2,1)S(1)}, bf16[112,768]{1,0:T(8,128)(2,1)S(1)}, u32[]{:S(2)}, u32[]{:S(2)}) collective-permute-start(bf16[112,768]{1,0:T(8,128)(2,1)S(1)} %get-tuple-element.108.refs_0_.refs_3_.refs_7_), channel_id=1, source_target_pairs={{0,2},{1,3},{2,0},{3,1},{4,6},{5,7},{6,4},{7,5},{8,10},{9,11},{10,... | collective-permute-start | bytes 516104 | tf_op jit(solution)/shard_map/ppermute | solution.py:143
  75.5 22.5 %collective-permute-start.14 = (bf16[112,768]{1,0:T(8,128)(2,1)S(1)}, bf16[112,768]{1,0:T(8,128)(2,1)S(1)}, u32[]{:S(2)}, u32[]{:S(2)}) collective-permute-start(bf16[112,768]{1,0:T(8,128)(2,1)S(1)} %get-tuple-element.98), channel_id=1, source_target_pairs={{0,2},{1,3},{2,0},{3,1},{4,6},{5,7},{6,4},{7,5},{8,10},{9,11},{10,... | collective-permute-start | bytes 516104 | tf_op jit(solution)/shard_map/ppermute | solution.py:143
  86.1 17.0 %collective-permute-start.24 = (bf16[384,448]{1,0:T(8,128)(2,1)S(1)}, bf16[384,448]{1,0:T(8,128)(2,1)S(1)}, u32[]{:S(2)}, u32[]{:S(2)}) collective-permute-start(bf16[384,448]{1,0:T(8,128)(2,1)S(1)} %get-tuple-element.119), channel_id=1, source_target_pairs={{0,24},{4,28},{8,16},{12,20},{16,8},{20,12},{24,0},{28,4},{1,25},{... | collective-permute-start | bytes 1032200 | tf_op jit(solution)/shard_map/ppermute | solution.py:143
  92.2 12.2 %collective-permute-start.25 = (bf16[384,448]{1,0:T(8,128)(2,1)S(1)}, bf16[384,448]{1,0:T(8,128)(2,1)S(1)}, u32[]{:S(2)}, u32[]{:S(2)}) collective-permute-start(bf16[384,448]{1,0:T(8,128)(2,1)S(1)} %get-tuple-element.120), channel_id=1, source_target_pairs={{0,16},{4,20},{8,24},{12,28},{16,0},{20,4},{24,8},{28,12},{1,17},{... | collective-permute-start | bytes 1032200 | tf_op jit(solution)/shard_map/ppermute | solution.py:143
  92.2 12.2 %collective-permute-start.26 = (bf16[384,448]{1,0:T(8,128)(2,1)S(1)}, bf16[384,448]{1,0:T(8,128)(2,1)S(1)}, u32[]{:S(2)}, u32[]{:S(2)}) collective-permute-start(bf16[384,448]{1,0:T(8,128)(2,1)S(1)} %get-tuple-element.121), channel_id=1, source_target_pairs={{0,8},{4,12},{8,0},{12,4},{16,24},{20,28},{24,16},{28,20},{1,9},{5... | collective-permute-start | bytes 1032200 | tf_op jit(solution)/shard_map/ppermute | solution.py:143
  98.1 14.2 %collective-permute-start.30 = (bf16[224,768]{1,0:T(8,128)(2,1)S(1)}, bf16[224,768]{1,0:T(8,128)(2,1)S(1)}, u32[]{:S(2)}, u32[]{:S(2)}) collective-permute-start(bf16[224,768]{1,0:T(8,128)(2,1)S(1)} %pile.5), channel_id=1, source_target_pairs={{0,1},{1,0},{2,3},{3,2},{4,5},{5,4},{6,7},{7,6},{8,9},{9,8},{10,11... | collective-permute-start | bytes 1032200 | tf_op jit(solution)/shard_map/ppermute | solution.py:143
  99.5 11.1 %collective-permute-start.21 = (bf16[112,768]{1,0:T(8,128)(2,1)S(1)}, bf16[112,768]{1,0:T(8,128)(2,1)S(1)}, u32[]{:S(2)}, u32[]{:S(2)}) collective-permute-start(bf16[112,768]{1,0:T(8,128)(2,1)S(1)} %total_of.3.refs_0_.refs_11_), channel_id=1, source_target_pairs={{0,2},{1,3},{2,0},{3,1},{4,6},{5,7},{6,4},{7,5},{8,10},{9,11},{10,... | collective-permute-start | bytes 516104 | tf_op jit(solution)/shard_map/ppermute | solution.py:143
  103.1 14.7 %collective-permute-start.33 = (bf16[864,384]{1,0:T(8,128)(2,1)S(1)}, bf16[864,384]{1,0:T(8,128)(2,1)S(1)}, u32[]{:S(2)}, u32[]{:S(2)}) collective-permute-start(bf16[864,384]{1,0:T(8,128)(2,1)S(1)} %get-tuple-element.133), channel_id=1, source_target_pairs={{0,4},{4,0},{8,12},{12,8},{16,20},{20,16},{24,28},{28,24},{1,5},{5... | collective-permute-start | bytes 1990664 | tf_op jit(solution)/shard_map/ppermute | solution.py:143
  113.3 9.6 %collective-permute-start.27 = (bf16[128,768]{1,0:T(8,128)(2,1)S(1)}, bf16[128,768]{1,0:T(8,128)(2,1)S(1)}, u32[]{:S(2)}, u32[]{:S(2)}) collective-permute-start(bf16[128,768]{1,0:T(8,128)(2,1)S(1)} %get-tuple-element.123), channel_id=1, source_target_pairs={{0,3},{1,2},{2,1},{3,0},{4,7},{5,6},{6,5},{7,4},{8,11},{9,10},{10,... | collective-permute-start | bytes 589832 | tf_op jit(solution)/shard_map/ppermute | solution.py:143
  115.3 12.6 %collective-permute-start.28 = (bf16[128,768]{1,0:T(8,128)(2,1)S(1)}, bf16[128,768]{1,0:T(8,128)(2,1)S(1)}, u32[]{:S(2)}, u32[]{:S(2)}) collective-permute-start(bf16[128,768]{1,0:T(8,128)(2,1)S(1)} %get-tuple-element.124), channel_id=1, source_target_pairs={{0,1},{1,0},{2,3},{3,2},{4,5},{5,4},{6,7},{7,6},{8,9},{9,8},{10,11... | collective-permute-start | bytes 589832 | tf_op jit(solution)/shard_map/ppermute | solution.py:143
  115.8 18.5 %collective-permute-start.29 = (bf16[128,768]{1,0:T(8,128)(2,1)S(1)}, bf16[128,768]{1,0:T(8,128)(2,1)S(1)}, u32[]{:S(2)}, u32[]{:S(2)}) collective-permute-start(bf16[128,768]{1,0:T(8,128)(2,1)S(1)} %get-tuple-element.125), channel_id=1, source_target_pairs={{0,2},{1,3},{2,0},{3,1},{4,6},{5,7},{6,4},{7,5},{8,10},{9,11},{10,... | collective-permute-start | bytes 589832 | tf_op jit(solution)/shard_map/ppermute | solution.py:143
  118.3 16.5 %collective-permute-start.37 = (bf16[408,384]{1,0:T(8,128)(2,1)S(1)}, bf16[408,384]{1,0:T(8,128)(2,1)S(1)}, u32[]{:S(2)}, u32[]{:S(2)}) collective-permute-start(bf16[408,384]{1,0:T(8,128)(2,1)S(1)} %get-tuple-element.137), channel_id=1, source_target_pairs={{0,24},{4,28},{8,16},{12,20},{16,8},{20,12},{24,0},{28,4},{1,25},{... | collective-permute-start | bytes 940040 | tf_op jit(solution)/shard_map/ppermute | solution.py:143
  121.2 16.0 %collective-permute-start.38 = (bf16[408,384]{1,0:T(8,128)(2,1)S(1)}, bf16[408,384]{1,0:T(8,128)(2,1)S(1)}, u32[]{:S(2)}, u32[]{:S(2)}) collective-permute-start(bf16[408,384]{1,0:T(8,128)(2,1)S(1)} %get-tuple-element.138), channel_id=1, source_target_pairs={{0,16},{4,20},{8,24},{12,28},{16,0},{20,4},{24,8},{28,12},{1,17},{... | collective-permute-start | bytes 940040 | tf_op jit(solution)/shard_map/ppermute | solution.py:143
  123.0 18.9 %collective-permute-start.22 = (bf16[224,768]{1,0:T(8,128)(2,1)S(1)}, bf16[224,768]{1,0:T(8,128)(2,1)S(1)}, u32[]{:S(2)}, u32[]{:S(2)}) collective-permute-start(bf16[224,768]{1,0:T(8,128)(2,1)S(1)} %pile.4), channel_id=1, source_target_pairs={{0,1},{1,0},{2,3},{3,2},{4,5},{5,4},{6,7},{7,6},{8,9},{9,8},{10,11... | collective-permute-start | bytes 1032200 | tf_op jit(solution)/shard_map/ppermute | solution.py:143
  127.9 11.3 %collective-permute-start.39 = (bf16[408,384]{1,0:T(8,128)(2,1)S(1)}, bf16[408,384]{1,0:T(8,128)(2,1)S(1)}, u32[]{:S(2)}, u32[]{:S(2)}) collective-permute-start(bf16[408,384]{1,0:T(8,128)(2,1)S(1)} %get-tuple-element.139), channel_id=1, source_target_pairs={{0,8},{4,12},{8,0},{12,4},{16,24},{20,28},{24,16},{28,20},{1,9},{5... | collective-permute-start | bytes 940040 | tf_op jit(solution)/shard_map/ppermute | solution.py:143
  134.7 10.2 %collective-permute-start.36 = (bf16[112,768]{1,0:T(8,128)(2,1)S(1)}, bf16[112,768]{1,0:T(8,128)(2,1)S(1)}, u32[]{:S(2)}, u32[]{:S(2)}) collective-permute-start(bf16[112,768]{1,0:T(8,128)(2,1)S(1)} %get-tuple-element.135.refs_0_), channel_id=1, source_target_pairs={{0,1},{1,0},{2,3},{3,2},{4,5},{5,4},{6,7},{7,6},{8,9},{9,8},{10,11... | collective-permute-start | bytes 516104 | tf_op jit(solution)/shard_map/ppermute | solution.py:143
  134.8 15.6 %collective-permute-start.35 = (bf16[112,768]{1,0:T(8,128)(2,1)S(1)}, bf16[112,768]{1,0:T(8,128)(2,1)S(1)}, u32[]{:S(2)}, u32[]{:S(2)}) collective-permute-start(bf16[112,768]{1,0:T(8,128)(2,1)S(1)} %get-tuple-element.135.refs_0_), channel_id=1, source_target_pairs={{0,2},{1,3},{2,0},{3,1},{4,6},{5,7},{6,4},{7,5},{8,10},{9,11},{10,... | collective-permute-start | bytes 516104 | tf_op jit(solution)/shard_map/ppermute | solution.py:143
  137.2 13.3 %collective-permute-start.34 = (bf16[112,768]{1,0:T(8,128)(2,1)S(1)}, bf16[112,768]{1,0:T(8,128)(2,1)S(1)}, u32[]{:S(2)}, u32[]{:S(2)}) collective-permute-start(bf16[112,768]{1,0:T(8,128)(2,1)S(1)} %get-tuple-element.135.refs_0_), channel_id=1, source_target_pairs={{0,3},{1,2},{2,1},{3,0},{4,7},{5,6},{6,5},{7,4},{8,11},{9,10},{10,... | collective-permute-start | bytes 516104 | tf_op jit(solution)/shard_map/ppermute | solution.py:143
  139.4 12.0 %collective-permute-start.42 = (bf16[424,384]{1,0:T(8,128)(2,1)S(1)}, bf16[424,384]{1,0:T(8,128)(2,1)S(1)}, u32[]{:S(2)}, u32[]{:S(2)}) collective-permute-start(bf16[424,384]{1,0:T(8,128)(2,1)S(1)} %sum_piece.1.refs_0_), channel_id=1, source_target_pairs={{0,8},{4,12},{8,0},{12,4},{16,24},{20,28},{24,16},{28,20},{1,9},{5... | collective-permute-start | bytes 976904 | tf_op jit(solution)/shard_map/ppermute | solution.py:143
  141.8 14.4 %collective-permute-start.41 = (bf16[424,384]{1,0:T(8,128)(2,1)S(1)}, bf16[424,384]{1,0:T(8,128)(2,1)S(1)}, u32[]{:S(2)}, u32[]{:S(2)}) collective-permute-start(bf16[424,384]{1,0:T(8,128)(2,1)S(1)} %sum_piece.1.refs_0_), channel_id=1, source_target_pairs={{0,16},{4,20},{8,24},{12,28},{16,0},{20,4},{24,8},{28,12},{1,17},{... | collective-permute-start | bytes 976904 | tf_op jit(solution)/shard_map/ppermute | solution.py:143
  144.9 11.2 %collective-permute-start.40 = (bf16[424,384]{1,0:T(8,128)(2,1)S(1)}, bf16[424,384]{1,0:T(8,128)(2,1)S(1)}, u32[]{:S(2)}, u32[]{:S(2)}) collective-permute-start(bf16[424,384]{1,0:T(8,128)(2,1)S(1)} %sum_piece.1.refs_0_), channel_id=1, source_target_pairs={{0,24},{4,28},{8,16},{12,20},{16,8},{20,12},{24,0},{28,4},{1,25},{... | collective-permute-start | bytes 976904 | tf_op jit(solution)/shard_map/ppermute | solution.py:143
  (16 other events, 70.6 us)

commit v17 on v16

--- a/solution.py
+++ b/solution.py
@@ -1272,12 +1272,12 @@
         [(total, "v")],
     )
     ways = everywhere(parts)
-    totals_all, total_places = by_steps(total, ())
+    totals_all, total_places = by_steps(total, [(ways[3], "v")])
     keep, send = late_grads(
         n_tp, proj_grad, h_one, out_b, branches, branch_places, [(totals_all[1], "v")]
     )
     own, *others = spread(count, (keep, over_cores(send)), (early, early_back))
-    summed = total_of([ways[0]] + [ways[i] for i in (1, 3, 2)], F32, flops=2_000_000_000)
+    summed = total_of([ways[0]] + [ways[i] for i in (3, 2, 1)], F32, flops=2_000_000_000)
     chip_sum = total_of(
         [own] + came(count, lambda k: over_chips(others[k - 1], k)), F32, "v", ()
     )

time: 162 us -> 158 us (0.975)
  Pallas kernels: 52.1 us -> 42.3 us
  waiting for transfers between devices: 52.4 us -> 58.8 us
    pallas_call x29, Pallas kernels: 52.1 us -> 42.3 us  [call(): pl.pallas_call(run, out_shape=tuple((shaped(shape, dtype) if kind == 'v'...]
    ppermute x44, waiting for transfers between devices: 52.4 us -> 58.8 us  [swap(): return lax.ppermute(x, axis, [(i, i ^ hop) for i in range(count)])]
  transfers between devices with their start and end apart: 44 -> 44, of which waited for: 21 -> 22; matrix products, arithmetic and copies ran while one was open for 0% -> 0% of each run, Pallas kernels for 30% -> 24%
where the time goes in v17:
time: 158 us
  waiting for transfers between devices  58.8 us (37%)
  starting transfers between devices  55.6 us (35%)
  Pallas kernels  42.3 us (27%)
    ppermute x44, waiting for transfers between devices, swap(): return lax.ppermute(x, axis, [(i, i ^ hop) for i in range(count)])  58.8 us
    ppermute x44, starting transfers between devices, swap(): return lax.ppermute(x, axis, [(i, i ^ hop) for i in range(count)])  55.6 us
    pallas_call x29, Pallas kernels, call(): pl.pallas_call(run, out_shape=tuple((shaped(shape, dtype) if kind == 'v'...  42.3 us
  transfers between devices with their start and end apart: 44, of which 22 were waited for; matrix products, arithmetic and copies ran while one was open for 0% of the time, Pallas kernels for 24%

profile of v17, /device:TPU:0, one launch (start us, length us, event | category | flops | bytes accessed | tf_op | source)
XLA Modules:
  0.0 158.0 jit_solution(7014878477837793852)
XLA Ops:
  1.9 3.1 %collective-permute-start = (bf16[528,768]{1,0:T(8,128)(2,1)S(1)}, bf16[528,768]{1,0:T(8,128)(2,1)S(1)}, u32[]{:S(2)}, u32[]{:S(2)}) collective-permute-start(bf16[528,768]{1,0:T(8,128)(2,1)S(1)} %get-tuple-element.79), channel_id=1, source_target_pairs={{0,1},{1,0},{2,3},{3,2},{4,5},{5,4},{6,7},{7,6},{8,9},{9,8},{10,11... | collective-permute-start | bytes 2433032 | tf_op jit(solution)/shard_map/ppermute | solution.py:143
  5.0 3.7 %project.1 = (bf16[192,448]{1,0:T(8,128)(2,1)S(1)}, bf16[384,448]{1,0:T(8,128)(2,1)S(1)}, bf16[448,768]{1,0:T(8,128)(2,1)S(1)}, f32[32,448]{1,0:T(8,128)S(1)}, f...) custom-call(s32[4]{0:T(128)} %refs_0_.11, s32[8]{0:T(128)} %refs_1_.13, bf16[448,768]{1,0:T(8,128)(2,1)} %refs_0_.9, ...), custom_call_target="tpu_custom_call" | custom-call | tf_op jit(solution)/shard_map/project/pallas_call | solution.py:121
  13.7 2.5 %collective-permute-start.2 = (bf16[96,768]{1,0:T(8,128)(2,1)S(1)}, bf16[96,768]{1,0:T(8,128)(2,1)S(1)}, u32[]{:S(2)}, u32[]{:S(2)}) collective-permute-start(bf16[96,768]{1,0:T(8,128)(2,1)S(1)} %get-tuple-element.80), channel_id=1, source_target_pairs={{0,3},{1,2},{2,1},{3,0},{4,7},{5,6},{6,5},{7,4},{8,11},{9,10},{10,... | collective-permute-start | bytes 442376 | tf_op jit(solution)/shard_map/ppermute | solution.py:143
  16.2 4.6 %collective-permute-done.6.refs_5_.refs_10_ = bf16[384,448]{1,0:T(8,128)(2,1)S(1)} collective-permute-done((bf16[384,448]{1,0:T(8,128)(2,1)S(1)}, bf16[384,448]{1,0:T(8,128)(2,1)S(1)}, u32[]{:S(2)}, u32[]{:S(2)}) %collective-permute-start.6) | collective-permute-done | bytes 344096 | tf_op jit(solution)/shard_map/ppermute | solution.py:143
  20.8 2.6 %collective-permute-start.1 = (bf16[96,768]{1,0:T(8,128)(2,1)S(1)}, bf16[96,768]{1,0:T(8,128)(2,1)S(1)}, u32[]{:S(2)}, u32[]{:S(2)}) collective-permute-start(bf16[96,768]{1,0:T(8,128)(2,1)S(1)} %get-tuple-element.80), channel_id=1, source_target_pairs={{0,2},{1,3},{2,0},{3,1},{4,6},{5,7},{6,4},{7,5},{8,10},{9,11},{10,... | collective-permute-start | bytes 442376 | tf_op jit(solution)/shard_map/ppermute | solution.py:143
  23.4 2.8 %attention_forward.2.refs_6_ = f32[6,80,448]{2,1,0:T(8,128)S(1)} custom-call(s32[4]{0:T(128)} %refs_0_.11, s32[8]{0:T(128)} %refs_1_.13, bf16[192,448]{1,0:T(8,128)(2,1)S(1)} %get-tuple-element.81.refs_2_, bf16[192,448]{1,0:T(8,128)(2,1)S(1)} %collective-permute-done.3.refs_3_, bf16[384,448]{1,0:T(8,128)(2,1)S(1)} %get-tuple-element.82.refs_4_.refs_10_, ...), custom_call_target="tpu_custom_call" | custom-call | tf_op jit(solution)/shard_map/attention_forward/pallas_call | solution.py:121
  26.2 2.6 %collective-permute-done.5.refs_5_.refs_12_ = bf16[384,448]{1,0:T(8,128)(2,1)S(1)} collective-permute-done((bf16[384,448]{1,0:T(8,128)(2,1)S(1)}, bf16[384,448]{1,0:T(8,128)(2,1)S(1)}, u32[]{:S(2)}, u32[]{:S(2)}) %collective-permute-start.5) | collective-permute-done | bytes 344096 | tf_op jit(solution)/shard_map/ppermute | solution.py:143
  30.2 4.2 %attention_forward.3 = (f32[3,80,448]{2,1,0:T(8,128)S(1)}, f32[3,80,448]{2,1,0:T(8,128)S(1)}) custom-call(s32[4]{0:T(128)} %refs_0_.11, s32[8]{0:T(128)} %refs_1_.13, bf16[192,448]{1,0:T(8,128)(2,1)S(1)} %get-tuple-element.81.refs_2_, bf16[192,448]{1,0:T(8,128)(2,1)S(1)} %collective-permute-done.3.refs_3_, ...), custom_call_target="tpu_custom_call" | custom-call | tf_op jit(solution)/shard_map/attention_forward/pallas_call | solution.py:121
  35.1 2.9 %collective-permute-done.8.refs_1_ = f32[3,80,448]{2,1,0:T(8,128)S(1)} collective-permute-done((f32[3,80,448]{2,1,0:T(8,128)S(1)}, f32[3,80,448]{2,1,0:T(8,128)S(1)}, u32[]{:S(2)}, u32[]{:S(2)}) %collective-permute-start.8) | collective-permute-done | bytes 430112 | tf_op jit(solution)/shard_map/ppermute | solution.py:143
  38.5 2.7 %collective-permute-start.10 = (bf16[192,224]{1,0:T(8,128)(2,1)S(1)}, bf16[192,224]{1,0:T(8,128)(2,1)S(1)}, u32[]{:S(2)}, u32[]{:S(2)}) collective-permute-start(bf16[192,224]{1,0:T(8,128)(2,1)S(1)} %get-tuple-element.91.refs_6_), channel_id=1, source_target_pairs={{0,2},{1,3},{2,0},{3,1},{4,6},{5,7},{6,4},{7,5},{8,10},{9,11},{10,... | collective-permute-start | bytes 258056 | tf_op jit(solution)/shard_map/ppermute | solution.py:143
  42.9 3.3 %stage.1 = (bf16[224,768]{1,0:T(8,128)(2,1)S(1)}, bf16[224,768]{1,0:T(8,128)(2,1)S(1)}, bf16[768,768]{1,0:T(8,128)(2,1)S(1)}, bf16[1152,768]{1,0:T(8,128)(2,1)S(...) custom-call(bf16[448,768]{1,0:T(8,128)(2,1)} %refs_0_.9, ...), custom_call_target="tpu_custom_call" | custom-call | tf_op jit(solution)/shard_map/stage/pallas_call | solution.py:121
  46.2 2.3 %collective-permute-done.10.refs_8_ = bf16[192,224]{1,0:T(8,128)(2,1)S(1)} collective-permute-done((bf16[192,224]{1,0:T(8,128)(2,1)S(1)}, bf16[192,224]{1,0:T(8,128)(2,1)S(1)}, u32[]{:S(2)}, u32[]{:S(2)}) %collective-permute-start.10) | collective-permute-done | bytes 86048 | tf_op jit(solution)/shard_map/ppermute | solution.py:143
  49.8 4.8 %feed.1 = (f32[224,768]{1,0:T(8,128)S(1)}, f32[112,768]{1,0:T(8,128)S(1)}, bf16[224,768]{1,0:T(8,128)(2,1)S(1)}, bf16[576,224]{1,0:T(8,128)(2,1)S(1)}, bf16[1152...) custom-call(bf16[224,768]{1,0:T(8,128)(2,1)S(1)} %get-tuple-element.84.refs_, ...), custom_call_target="tpu_custom_call" | custom-call | tf_op jit(solution)/shard_map/feed/pallas_call | solution.py:121
  54.6 2.5 %collective-permute-start.15 = (bf16[112,768]{1,0:T(8,128)(2,1)S(1)}, bf16[112,768]{1,0:T(8,128)(2,1)S(1)}, u32[]{:S(2)}, u32[]{:S(2)}) collective-permute-start(bf16[112,768]{1,0:T(8,128)(2,1)S(1)} %get-tuple-element.102), channel_id=1, source_target_pairs={{0,2},{1,3},{2,0},{3,1},{4,6},{5,7},{6,4},{7,5},{8,10},{9,11},{10,... | collective-permute-start | bytes 516104 | tf_op jit(solution)/shard_map/ppermute | solution.py:143
  59.3 5.9 %collective-permute-done.15.refs_5_ = bf16[112,768]{1,0:T(8,128)(2,1)S(1)} collective-permute-done((bf16[112,768]{1,0:T(8,128)(2,1)S(1)}, bf16[112,768]{1,0:T(8,128)(2,1)S(1)}, u32[]{:S(2)}, u32[]{:S(2)}) %collective-permute-start.15) | collective-permute-done | bytes 172064 | tf_op jit(solution)/shard_map/ppermute | solution.py:143
  66.0 2.0 %collective-permute-start.16 = (bf16[112,192]{1,0:T(8,128)(2,1)S(1)}, bf16[112,192]{1,0:T(8,128)(2,1)S(1)}, u32[]{:S(2)}, u32[]{:S(2)}) collective-permute-start(bf16[112,192]{1,0:T(8,128)(2,1)S(1)} %get-tuple-element.104), channel_id=1, source_target_pairs={{0,3},{1,2},{2,1},{3,0},{4,7},{5,6},{6,5},{7,4},{8,11},{9,10},{10,... | collective-permute-start | bytes 129032 | tf_op jit(solution)/shard_map/ppermute | solution.py:143
  68.0 2.4 %collective-permute-start.18 = (bf16[112,192]{1,0:T(8,128)(2,1)S(1)}, bf16[112,192]{1,0:T(8,128)(2,1)S(1)}, u32[]{:S(2)}, u32[]{:S(2)}) collective-permute-start(bf16[112,192]{1,0:T(8,128)(2,1)S(1)} %get-tuple-element.106), channel_id=1, source_target_pairs={{0,1},{1,0},{2,3},{3,2},{4,5},{5,4},{6,7},{7,6},{8,9},{9,8},{10,11... | collective-permute-start | bytes 129032 | tf_op jit(solution)/shard_map/ppermute | solution.py:143
  70.4 2.2 %collective-permute-done.16.refs_1_ = bf16[112,192]{1,0:T(8,128)(2,1)S(1)} collective-permute-done((bf16[112,192]{1,0:T(8,128)(2,1)S(1)}, bf16[112,192]{1,0:T(8,128)(2,1)S(1)}, u32[]{:S(2)}, u32[]{:S(2)}) %collective-permute-start.16) | collective-permute-done | bytes 43040 | tf_op jit(solution)/shard_map/ppermute | solution.py:143
  77.0 5.5 %attention_backward.2 = (bf16[384,448]{1,0:T(8,128)(2,1)S(1)}, bf16[384,448]{1,0:T(8,128)(2,1)S(1)}, bf16[384,448]{1,0:T(8,128)(2,1)S(1)}, f32[6,64,448]{2,1,0:T(8,128)S(1)}) custom-call(s32[4]{0:T(128)} %refs_0_.11, s32[8]{0:T(128)} %refs_1_.13, bf16[192,448]{1,0:T(8,128)(2,1)S(1)} %get-tuple-element.81.refs_2_, ...), custom_call_target="tpu_custom_call" | custom-call | tf_op jit(solution)/shard_map/attention_backward/pallas_call | solution.py:121
  84.8 4.6 %collective-permute-done.20.refs_3_.refs_1_.refs_4_ = bf16[112,768]{1,0:T(8,128)(2,1)S(1)} collective-permute-done((bf16[112,768]{1,0:T(8,128)(2,1)S(1)}, bf16[112,768]{1,0:T(8,128)(2,1)S(1)}, u32[]{:S(2)}, u32[]{:S(2)}) %collective-permute-start.20) | collective-permute-done | bytes 172064 | tf_op jit(solution)/shard_map/ppermute | solution.py:143
  89.5 3.3 %attention_backward.3 = (f32[384,448]{1,0:T(8,128)S(1)}, f32[192,448]{1,0:T(8,128)S(1)}, bf16[192,448]{1,0:T(8,128)(2,1)S(1)}) custom-call(s32[4]{0:T(128)} %refs_0_.11, s32[8]{0:T(128)} %refs_1_.13, bf16[192,448]{1,0:T(8,128)(2,1)S(1)} %get-tuple-element.81.refs_2_, bf16[192,448]{1,0:T(8,128)(2,1)S(1)} %collective-permute-done.3.refs_3_, ...), custom_call_target="tpu_custom_call" | custom-call | tf_op jit(solution)/shard_map/attention_backward/pallas_call | solution.py:121
  95.6 2.1 %early_grads.1 = (f32[864,384]{1,0:T(8,128)S(1)}, bf16[864,384]{1,0:T(8,128)(2,1)S(1)}) custom-call(bf16[576,224]{1,0:T(8,128)(2,1)S(1)} %get-tuple-element.93.refs_0_, bf16[1152,224]{1,0:T(8,128)(2,1)S(1)} %get-tuple-element.130.refs_1_, bf16[448,768]{1,0:T(8,128)(2,1)S(1)} %copy-done.3, bf16[224,768]{1,0:T(8,128)(2,1)S(1)} %get-tuple-element.131.refs_3_, ...), custom_call_target="tpu_custom_call" | custom-call | tf_op jit(solution)/shard_map/early_grads/pallas_call | solution.py:121
  97.9 4.9 %collective-permute-done.24.refs_9_ = bf16[384,448]{1,0:T(8,128)(2,1)S(1)} collective-permute-done((bf16[384,448]{1,0:T(8,128)(2,1)S(1)}, bf16[384,448]{1,0:T(8,128)(2,1)S(1)}, u32[]{:S(2)}, u32[]{:S(2)}) %collective-permute-start.24) | collective-permute-done | bytes 344096 | tf_op jit(solution)/shard_map/ppermute | solution.py:143
  104.9 2.2 %collective-permute-done.30.refs_5_ = bf16[224,768]{1,0:T(8,128)(2,1)S(1)} collective-permute-done((bf16[224,768]{1,0:T(8,128)(2,1)S(1)}, bf16[224,768]{1,0:T(8,128)(2,1)S(1)}, u32[]{:S(2)}, u32[]{:S(2)}) %collective-permute-start.30) | collective-permute-done | bytes 344096 | tf_op jit(solution)/shard_map/ppermute | solution.py:143
  113.1 3.7 %collective-permute-start.37 = (bf16[408,384]{1,0:T(8,128)(2,1)S(1)}, bf16[408,384]{1,0:T(8,128)(2,1)S(1)}, u32[]{:S(2)}, u32[]{:S(2)}) collective-permute-start(bf16[408,384]{1,0:T(8,128)(2,1)S(1)} %get-tuple-element.137), channel_id=1, source_target_pairs={{0,24},{4,28},{8,16},{12,20},{16,8},{20,12},{24,0},{28,4},{1,25},{... | collective-permute-start | bytes 940040 | tf_op jit(solution)/shard_map/ppermute | solution.py:143
  119.1 7.1 %collective-permute-done.28.refs_2_ = bf16[128,768]{1,0:T(8,128)(2,1)S(1)} collective-permute-done((bf16[128,768]{1,0:T(8,128)(2,1)S(1)}, bf16[128,768]{1,0:T(8,128)(2,1)S(1)}, u32[]{:S(2)}, u32[]{:S(2)}) %collective-permute-start.28) | collective-permute-done | bytes 196640 | tf_op jit(solution)/shard_map/ppermute | solution.py:143
  126.2 3.8 %collective-permute-start.39 = (bf16[408,384]{1,0:T(8,128)(2,1)S(1)}, bf16[408,384]{1,0:T(8,128)(2,1)S(1)}, u32[]{:S(2)}, u32[]{:S(2)}) collective-permute-start(bf16[408,384]{1,0:T(8,128)(2,1)S(1)} %get-tuple-element.139), channel_id=1, source_target_pairs={{0,8},{4,12},{8,0},{12,4},{16,24},{20,28},{24,16},{28,20},{1,9},{5... | collective-permute-start | bytes 940040 | tf_op jit(solution)/shard_map/ppermute | solution.py:143
  130.7 2.2 %collective-permute-start.35 = (bf16[112,768]{1,0:T(8,128)(2,1)S(1)}, bf16[112,768]{1,0:T(8,128)(2,1)S(1)}, u32[]{:S(2)}, u32[]{:S(2)}) collective-permute-start(bf16[112,768]{1,0:T(8,128)(2,1)S(1)} %get-tuple-element.135.refs_0_), channel_id=1, source_target_pairs={{0,2},{1,3},{2,0},{3,1},{4,6},{5,7},{6,4},{7,5},{8,10},{9,11},{10,... | collective-permute-start | bytes 516104 | tf_op jit(solution)/shard_map/ppermute | solution.py:143
  135.1 2.1 %collective-permute-start.42 = (bf16[424,384]{1,0:T(8,128)(2,1)S(1)}, bf16[424,384]{1,0:T(8,128)(2,1)S(1)}, u32[]{:S(2)}, u32[]{:S(2)}) collective-permute-start(bf16[424,384]{1,0:T(8,128)(2,1)S(1)} %sum_piece.1.refs_0_), channel_id=1, source_target_pairs={{0,8},{4,12},{8,0},{12,4},{16,24},{20,28},{24,16},{28,20},{1,9},{5... | collective-permute-start | bytes 976904 | tf_op jit(solution)/shard_map/ppermute | solution.py:143
  139.7 3.7 %collective-permute-start.40 = (bf16[424,384]{1,0:T(8,128)(2,1)S(1)}, bf16[424,384]{1,0:T(8,128)(2,1)S(1)}, u32[]{:S(2)}, u32[]{:S(2)}) collective-permute-start(bf16[424,384]{1,0:T(8,128)(2,1)S(1)} %sum_piece.1.refs_0_), channel_id=1, source_target_pairs={{0,24},{4,28},{8,16},{12,20},{16,8},{20,12},{24,0},{28,4},{1,25},{... | collective-permute-start | bytes 976904 | tf_op jit(solution)/shard_map/ppermute | solution.py:143
  146.9 5.4 %collective-permute-done.41.refs_2_ = bf16[424,384]{1,0:T(8,128)(2,1)S(1)} collective-permute-done((bf16[424,384]{1,0:T(8,128)(2,1)S(1)}, bf16[424,384]{1,0:T(8,128)(2,1)S(1)}, u32[]{:S(2)}, u32[]{:S(2)}) %collective-permute-start.41) | collective-permute-done | bytes 325664 | tf_op jit(solution)/shard_map/ppermute | solution.py:143
  155.6 2.2 %pair_half.1 = (f32[576,768]{1,0:T(8,128)}, f32[192,768]{1,0:T(8,128)}, f32[288,768]{1,0:T(8,128)}, f32[576,768]{1,0:T(8,128)}, f32[768]{0:T(1024)}, /*index=5*/f32[768]{0:T(1024)}) custom-call(bf16[1648,384]{1,0:T(8,128)(2,1)S(1)} %collect.1.refs_0_, ...), custom_call_target="tpu_custom_call", output_to_operand_aliasing={{0}: (2, {}), {1}: (3, {}), {2}: (4, {}), {3}: (5, {})} | custom-call | tf_op jit(solution)/shard_map/pair_half/pallas_call | solution.py:121
  (93 shorter events, 47.1 us)
Async XLA Ops:
  1.9 32.6 %collective-permute-start = (bf16[528,768]{1,0:T(8,128)(2,1)S(1)}, bf16[528,768]{1,0:T(8,128)(2,1)S(1)}, u32[]{:S(2)}, u32[]{:S(2)}) collective-permute-start(bf16[528,768]{1,0:T(8,128)(2,1)S(1)} %get-tuple-element.79), channel_id=1, source_target_pairs={{0,1},{1,0},{2,3},{3,2},{4,5},{5,4},{6,7},{7,6},{8,9},{9,8},{10,11... | collective-permute-start | bytes 2433032 | tf_op jit(solution)/shard_map/ppermute | solution.py:143
  8.7 12.1 %collective-permute-start.6 = (bf16[384,448]{1,0:T(8,128)(2,1)S(1)}, bf16[384,448]{1,0:T(8,128)(2,1)S(1)}, u32[]{:S(2)}, u32[]{:S(2)}) collective-permute-start(bf16[384,448]{1,0:T(8,128)(2,1)S(1)} %get-tuple-element.82.refs_4_.refs_10_), channel_id=1, source_target_pairs={{0,8},{4,12},{8,0},{12,4},{16,24},{20,28},{24,16},{28,20},{1,9},{5... | collective-permute-start | bytes 1032200 | tf_op jit(solution)/shard_map/ppermute | solution.py:143
  10.3 18.6 %collective-permute-start.5 = (bf16[384,448]{1,0:T(8,128)(2,1)S(1)}, bf16[384,448]{1,0:T(8,128)(2,1)S(1)}, u32[]{:S(2)}, u32[]{:S(2)}) collective-permute-start(bf16[384,448]{1,0:T(8,128)(2,1)S(1)} %get-tuple-element.82.refs_4_.refs_10_), channel_id=1, source_target_pairs={{0,24},{4,28},{8,16},{12,20},{16,8},{20,12},{24,0},{28,4},{1,25},{... | collective-permute-start | bytes 1032200 | tf_op jit(solution)/shard_map/ppermute | solution.py:143
  11.8 18.4 %collective-permute-start.4 = (bf16[384,448]{1,0:T(8,128)(2,1)S(1)}, bf16[384,448]{1,0:T(8,128)(2,1)S(1)}, u32[]{:S(2)}, u32[]{:S(2)}) collective-permute-start(bf16[384,448]{1,0:T(8,128)(2,1)S(1)} %get-tuple-element.82.refs_4_.refs_10_), channel_id=1, source_target_pairs={{0,16},{4,20},{8,24},{12,28},{16,0},{20,4},{24,8},{28,12},{1,17},{... | collective-permute-start | bytes 1032200 | tf_op jit(solution)/shard_map/ppermute | solution.py:143
  13.7 20.7 %collective-permute-start.2 = (bf16[96,768]{1,0:T(8,128)(2,1)S(1)}, bf16[96,768]{1,0:T(8,128)(2,1)S(1)}, u32[]{:S(2)}, u32[]{:S(2)}) collective-permute-start(bf16[96,768]{1,0:T(8,128)(2,1)S(1)} %get-tuple-element.80), channel_id=1, source_target_pairs={{0,3},{1,2},{2,1},{3,0},{4,7},{5,6},{6,5},{7,4},{8,11},{9,10},{10,... | collective-permute-start | bytes 442376 | tf_op jit(solution)/shard_map/ppermute | solution.py:143
  20.8 13.6 %collective-permute-start.1 = (bf16[96,768]{1,0:T(8,128)(2,1)S(1)}, bf16[96,768]{1,0:T(8,128)(2,1)S(1)}, u32[]{:S(2)}, u32[]{:S(2)}) collective-permute-start(bf16[96,768]{1,0:T(8,128)(2,1)S(1)} %get-tuple-element.80), channel_id=1, source_target_pairs={{0,2},{1,3},{2,0},{3,1},{4,6},{5,7},{6,4},{7,5},{8,10},{9,11},{10,... | collective-permute-start | bytes 442376 | tf_op jit(solution)/shard_map/ppermute | solution.py:143
  38.5 10.0 %collective-permute-start.10 = (bf16[192,224]{1,0:T(8,128)(2,1)S(1)}, bf16[192,224]{1,0:T(8,128)(2,1)S(1)}, u32[]{:S(2)}, u32[]{:S(2)}) collective-permute-start(bf16[192,224]{1,0:T(8,128)(2,1)S(1)} %get-tuple-element.91.refs_6_), channel_id=1, source_target_pairs={{0,2},{1,3},{2,0},{3,1},{4,6},{5,7},{6,4},{7,5},{8,10},{9,11},{10,... | collective-permute-start | bytes 258056 | tf_op jit(solution)/shard_map/ppermute | solution.py:143
  41.1 8.7 %collective-permute-start.11 = (bf16[192,224]{1,0:T(8,128)(2,1)S(1)}, bf16[192,224]{1,0:T(8,128)(2,1)S(1)}, u32[]{:S(2)}, u32[]{:S(2)}) collective-permute-start(bf16[192,224]{1,0:T(8,128)(2,1)S(1)} %get-tuple-element.92), channel_id=1, source_target_pairs={{0,1},{1,0},{2,3},{3,2},{4,5},{5,4},{6,7},{7,6},{8,9},{9,8},{10,11... | collective-permute-start | bytes 258056 | tf_op jit(solution)/shard_map/ppermute | solution.py:143
  42.9 15.8 %collective-permute-start.12 = (bf16[192,448]{1,0:T(8,128)(2,1)S(1)}, bf16[192,448]{1,0:T(8,128)(2,1)S(1)}, u32[]{:S(2)}, u32[]{:S(2)}) collective-permute-start(bf16[192,448]{1,0:T(8,128)(2,1)S(1)} %get-tuple-element.95.refs_6_.refs_2_), channel_id=1, source_target_pairs={{0,4},{4,0},{8,12},{12,8},{16,20},{20,16},{24,28},{28,24},{1,5},{5... | collective-permute-start | bytes 516104 | tf_op jit(solution)/shard_map/ppermute | solution.py:143
  54.6 10.6 %collective-permute-start.15 = (bf16[112,768]{1,0:T(8,128)(2,1)S(1)}, bf16[112,768]{1,0:T(8,128)(2,1)S(1)}, u32[]{:S(2)}, u32[]{:S(2)}) collective-permute-start(bf16[112,768]{1,0:T(8,128)(2,1)S(1)} %get-tuple-element.102), channel_id=1, source_target_pairs={{0,2},{1,3},{2,0},{3,1},{4,6},{5,7},{6,4},{7,5},{8,10},{9,11},{10,... | collective-permute-start | bytes 516104 | tf_op jit(solution)/shard_map/ppermute | solution.py:143
  57.1 35.9 %collective-permute-start.32 = (bf16[224,768]{1,0:T(8,128)(2,1)S(1)}, bf16[224,768]{1,0:T(8,128)(2,1)S(1)}, u32[]{:S(2)}, u32[]{:S(2)}) collective-permute-start(bf16[224,768]{1,0:T(8,128)(2,1)S(1)} %get-tuple-element.131.refs_3_), channel_id=1, source_target_pairs={{0,1},{1,0},{2,3},{3,2},{4,5},{5,4},{6,7},{7,6},{8,9},{9,8},{10,11... | collective-permute-start | bytes 1032200 | tf_op jit(solution)/shard_map/ppermute | solution.py:143
  74.0 15.4 %collective-permute-start.20 = (bf16[112,768]{1,0:T(8,128)(2,1)S(1)}, bf16[112,768]{1,0:T(8,128)(2,1)S(1)}, u32[]{:S(2)}, u32[]{:S(2)}) collective-permute-start(bf16[112,768]{1,0:T(8,128)(2,1)S(1)} %get-tuple-element.108.refs_0_.refs_3_.refs_7_), channel_id=1, source_target_pairs={{0,2},{1,3},{2,0},{3,1},{4,6},{5,7},{6,4},{7,5},{8,10},{9,11},{10,... | collective-permute-start | bytes 516104 | tf_op jit(solution)/shard_map/ppermute | solution.py:143
  75.5 17.4 %collective-permute-start.14 = (bf16[112,768]{1,0:T(8,128)(2,1)S(1)}, bf16[112,768]{1,0:T(8,128)(2,1)S(1)}, u32[]{:S(2)}, u32[]{:S(2)}) collective-permute-start(bf16[112,768]{1,0:T(8,128)(2,1)S(1)} %get-tuple-element.98), channel_id=1, source_target_pairs={{0,2},{1,3},{2,0},{3,1},{4,6},{5,7},{6,4},{7,5},{8,10},{9,11},{10,... | collective-permute-start | bytes 516104 | tf_op jit(solution)/shard_map/ppermute | solution.py:143
  82.5 15.3 %collective-permute-start.23 = (bf16[384,448]{1,0:T(8,128)(2,1)S(1)}, bf16[384,448]{1,0:T(8,128)(2,1)S(1)}, u32[]{:S(2)}, u32[]{:S(2)}) collective-permute-start(bf16[384,448]{1,0:T(8,128)(2,1)S(1)} %get-tuple-element.116), channel_id=1, source_target_pairs={{0,24},{4,28},{8,16},{12,20},{16,8},{20,12},{24,0},{28,4},{1,25},{... | collective-permute-start | bytes 1032200 | tf_op jit(solution)/shard_map/ppermute | solution.py:143
  84.0 18.8 %collective-permute-start.24 = (bf16[384,448]{1,0:T(8,128)(2,1)S(1)}, bf16[384,448]{1,0:T(8,128)(2,1)S(1)}, u32[]{:S(2)}, u32[]{:S(2)}) collective-permute-start(bf16[384,448]{1,0:T(8,128)(2,1)S(1)} %get-tuple-element.117), channel_id=1, source_target_pairs={{0,16},{4,20},{8,24},{12,28},{16,0},{20,4},{24,8},{28,12},{1,17},{... | collective-permute-start | bytes 1032200 | tf_op jit(solution)/shard_map/ppermute | solution.py:143
  89.4 13.3 %collective-permute-start.25 = (bf16[384,448]{1,0:T(8,128)(2,1)S(1)}, bf16[384,448]{1,0:T(8,128)(2,1)S(1)}, u32[]{:S(2)}, u32[]{:S(2)}) collective-permute-start(bf16[384,448]{1,0:T(8,128)(2,1)S(1)} %get-tuple-element.118), channel_id=1, source_target_pairs={{0,8},{4,12},{8,0},{12,4},{16,24},{20,28},{24,16},{28,20},{1,9},{5... | collective-permute-start | bytes 1032200 | tf_op jit(solution)/shard_map/ppermute | solution.py:143
  92.9 14.2 %collective-permute-start.30 = (bf16[224,768]{1,0:T(8,128)(2,1)S(1)}, bf16[224,768]{1,0:T(8,128)(2,1)S(1)}, u32[]{:S(2)}, u32[]{:S(2)}) collective-permute-start(bf16[224,768]{1,0:T(8,128)(2,1)S(1)} %pile.5), channel_id=1, source_target_pairs={{0,1},{1,0},{2,3},{3,2},{4,5},{5,4},{6,7},{7,6},{8,9},{9,8},{10,11... | collective-permute-start | bytes 1032200 | tf_op jit(solution)/shard_map/ppermute | solution.py:143
  94.3 10.5 %collective-permute-start.21 = (bf16[112,768]{1,0:T(8,128)(2,1)S(1)}, bf16[112,768]{1,0:T(8,128)(2,1)S(1)}, u32[]{:S(2)}, u32[]{:S(2)}) collective-permute-start(bf16[112,768]{1,0:T(8,128)(2,1)S(1)} %total_of.3.refs_11_.refs_0_), channel_id=1, source_target_pairs={{0,2},{1,3},{2,0},{3,1},{4,6},{5,7},{6,4},{7,5},{8,10},{9,11},{10,... | collective-permute-start | bytes 516104 | tf_op jit(solution)/shard_map/ppermute | solution.py:143
  97.8 14.8 %collective-permute-start.33 = (bf16[864,384]{1,0:T(8,128)(2,1)S(1)}, bf16[864,384]{1,0:T(8,128)(2,1)S(1)}, u32[]{:S(2)}, u32[]{:S(2)}) collective-permute-start(bf16[864,384]{1,0:T(8,128)(2,1)S(1)} %get-tuple-element.133), channel_id=1, source_target_pairs={{0,4},{4,0},{8,12},{12,8},{16,20},{20,16},{24,28},{28,24},{1,5},{5... | collective-permute-start | bytes 1990664 | tf_op jit(solution)/shard_map/ppermute | solution.py:143
  108.2 10.8 %collective-permute-start.26 = (bf16[128,768]{1,0:T(8,128)(2,1)S(1)}, bf16[128,768]{1,0:T(8,128)(2,1)S(1)}, u32[]{:S(2)}, u32[]{:S(2)}) collective-permute-start(bf16[128,768]{1,0:T(8,128)(2,1)S(1)} %get-tuple-element.119), channel_id=1, source_target_pairs={{0,1},{1,0},{2,3},{3,2},{4,5},{5,4},{6,7},{7,6},{8,9},{9,8},{10,11... | collective-permute-start | bytes 589832 | tf_op jit(solution)/shard_map/ppermute | solution.py:143
  109.0 17.2 %collective-permute-start.28 = (bf16[128,768]{1,0:T(8,128)(2,1)S(1)}, bf16[128,768]{1,0:T(8,128)(2,1)S(1)}, u32[]{:S(2)}, u32[]{:S(2)}) collective-permute-start(bf16[128,768]{1,0:T(8,128)(2,1)S(1)} %get-tuple-element.124), channel_id=1, source_target_pairs={{0,2},{1,3},{2,0},{3,1},{4,6},{5,7},{6,4},{7,5},{8,10},{9,11},{10,... | collective-permute-start | bytes 589832 | tf_op jit(solution)/shard_map/ppermute | solution.py:143
  110.8 19.2 %collective-permute-start.29 = (bf16[128,768]{1,0:T(8,128)(2,1)S(1)}, bf16[128,768]{1,0:T(8,128)(2,1)S(1)}, u32[]{:S(2)}, u32[]{:S(2)}) collective-permute-start(bf16[128,768]{1,0:T(8,128)(2,1)S(1)} %get-tuple-element.125), channel_id=1, source_target_pairs={{0,3},{1,2},{2,1},{3,0},{4,7},{5,6},{6,5},{7,4},{8,11},{9,10},{10,... | collective-permute-start | bytes 589832 | tf_op jit(solution)/shard_map/ppermute | solution.py:143
  113.1 17.6 %collective-permute-start.37 = (bf16[408,384]{1,0:T(8,128)(2,1)S(1)}, bf16[408,384]{1,0:T(8,128)(2,1)S(1)}, u32[]{:S(2)}, u32[]{:S(2)}) collective-permute-start(bf16[408,384]{1,0:T(8,128)(2,1)S(1)} %get-tuple-element.137), channel_id=1, source_target_pairs={{0,24},{4,28},{8,16},{12,20},{16,8},{20,12},{24,0},{28,4},{1,25},{... | collective-permute-start | bytes 940040 | tf_op jit(solution)/shard_map/ppermute | solution.py:143
  116.9 16.0 %collective-permute-start.38 = (bf16[408,384]{1,0:T(8,128)(2,1)S(1)}, bf16[408,384]{1,0:T(8,128)(2,1)S(1)}, u32[]{:S(2)}, u32[]{:S(2)}) collective-permute-start(bf16[408,384]{1,0:T(8,128)(2,1)S(1)} %get-tuple-element.138), channel_id=1, source_target_pairs={{0,16},{4,20},{8,24},{12,28},{16,0},{20,4},{24,8},{28,12},{1,17},{... | collective-permute-start | bytes 940040 | tf_op jit(solution)/shard_map/ppermute | solution.py:143
  119.0 18.2 %collective-permute-start.27 = (bf16[224,768]{1,0:T(8,128)(2,1)S(1)}, bf16[224,768]{1,0:T(8,128)(2,1)S(1)}, u32[]{:S(2)}, u32[]{:S(2)}) collective-permute-start(bf16[224,768]{1,0:T(8,128)(2,1)S(1)} %pile.4), channel_id=1, source_target_pairs={{0,1},{1,0},{2,3},{3,2},{4,5},{5,4},{6,7},{7,6},{8,9},{9,8},{10,11... | collective-permute-start | bytes 1032200 | tf_op jit(solution)/shard_map/ppermute | solution.py:143
  126.2 8.7 %collective-permute-start.39 = (bf16[408,384]{1,0:T(8,128)(2,1)S(1)}, bf16[408,384]{1,0:T(8,128)(2,1)S(1)}, u32[]{:S(2)}, u32[]{:S(2)}) collective-permute-start(bf16[408,384]{1,0:T(8,128)(2,1)S(1)} %get-tuple-element.139), channel_id=1, source_target_pairs={{0,8},{4,12},{8,0},{12,4},{16,24},{20,28},{24,16},{28,20},{1,9},{5... | collective-permute-start | bytes 940040 | tf_op jit(solution)/shard_map/ppermute | solution.py:143
  130.4 9.3 %collective-permute-start.36 = (bf16[112,768]{1,0:T(8,128)(2,1)S(1)}, bf16[112,768]{1,0:T(8,128)(2,1)S(1)}, u32[]{:S(2)}, u32[]{:S(2)}) collective-permute-start(bf16[112,768]{1,0:T(8,128)(2,1)S(1)} %get-tuple-element.135.refs_0_), channel_id=1, source_target_pairs={{0,1},{1,0},{2,3},{3,2},{4,5},{5,4},{6,7},{7,6},{8,9},{9,8},{10,11... | collective-permute-start | bytes 516104 | tf_op jit(solution)/shard_map/ppermute | solution.py:143
  130.7 15.2 %collective-permute-start.35 = (bf16[112,768]{1,0:T(8,128)(2,1)S(1)}, bf16[112,768]{1,0:T(8,128)(2,1)S(1)}, u32[]{:S(2)}, u32[]{:S(2)}) collective-permute-start(bf16[112,768]{1,0:T(8,128)(2,1)S(1)} %get-tuple-element.135.refs_0_), channel_id=1, source_target_pairs={{0,2},{1,3},{2,0},{3,1},{4,6},{5,7},{6,4},{7,5},{8,10},{9,11},{10,... | collective-permute-start | bytes 516104 | tf_op jit(solution)/shard_map/ppermute | solution.py:143
  132.9 13.0 %collective-permute-start.34 = (bf16[112,768]{1,0:T(8,128)(2,1)S(1)}, bf16[112,768]{1,0:T(8,128)(2,1)S(1)}, u32[]{:S(2)}, u32[]{:S(2)}) collective-permute-start(bf16[112,768]{1,0:T(8,128)(2,1)S(1)} %get-tuple-element.135.refs_0_), channel_id=1, source_target_pairs={{0,3},{1,2},{2,1},{3,0},{4,7},{5,6},{6,5},{7,4},{8,11},{9,10},{10,... | collective-permute-start | bytes 516104 | tf_op jit(solution)/shard_map/ppermute | solution.py:143
  135.1 11.8 %collective-permute-start.42 = (bf16[424,384]{1,0:T(8,128)(2,1)S(1)}, bf16[424,384]{1,0:T(8,128)(2,1)S(1)}, u32[]{:S(2)}, u32[]{:S(2)}) collective-permute-start(bf16[424,384]{1,0:T(8,128)(2,1)S(1)} %sum_piece.1.refs_0_), channel_id=1, source_target_pairs={{0,8},{4,12},{8,0},{12,4},{16,24},{20,28},{24,16},{28,20},{1,9},{5... | collective-permute-start | bytes 976904 | tf_op jit(solution)/shard_map/ppermute | solution.py:143
  137.2 15.0 %collective-permute-start.41 = (bf16[424,384]{1,0:T(8,128)(2,1)S(1)}, bf16[424,384]{1,0:T(8,128)(2,1)S(1)}, u32[]{:S(2)}, u32[]{:S(2)}) collective-permute-start(bf16[424,384]{1,0:T(8,128)(2,1)S(1)} %sum_piece.1.refs_0_), channel_id=1, source_target_pairs={{0,16},{4,20},{8,24},{12,28},{16,0},{20,4},{24,8},{28,12},{1,17},{... | collective-permute-start | bytes 976904 | tf_op jit(solution)/shard_map/ppermute | solution.py:143
  139.7 12.6 %collective-permute-start.40 = (bf16[424,384]{1,0:T(8,128)(2,1)S(1)}, bf16[424,384]{1,0:T(8,128)(2,1)S(1)}, u32[]{:S(2)}, u32[]{:S(2)}) collective-permute-start(bf16[424,384]{1,0:T(8,128)(2,1)S(1)} %sum_piece.1.refs_0_), channel_id=1, source_target_pairs={{0,24},{4,28},{8,16},{12,20},{16,8},{20,12},{24,0},{28,4},{1,25},{... | collective-permute-start | bytes 976904 | tf_op jit(solution)/shard_map/ppermute | solution.py:143
  (16 other events, 71.8 us)
